TPU v7x, 256 devices: a whole 4x4x8 slice. The times are simulated.
256 devices in a mesh: img: 8 (over z_lo, core), txt: 32 (over z_hi, y, x).
Axes of the slice: x: 4, y: 4, z: 8 (z_hi: 2, z_lo: 4; z = z_hi * 4 + z_lo), core: 2. Of those that a mesh axis runs over, the one named last changes fastest.
Arguments:
- image_emb: bfloat16 [16384, 1280], P(('img', 'txt')), may hold values from -1 to 1
- text_emb: bfloat16 [16384, 1280], P(('txt', 'img')), may hold values from -1 to 1
- logit_scale: float32 [1], replicated, may hold values from 15 to 30
Outputs:
- mean_loss: float32 [1], replicated
- image_grad: bfloat16 [16384, 1280], P(('img', 'txt'))
- text_grad: bfloat16 [16384, 1280], P(('txt', 'img'))
All inputs are finite; a program needn't handle non-finite values.
Results may differ from a plain program's by a relative error of at most 0.023.
Values may be sent and summed in bfloat16 or wider, within the bound.
No kernel may reach another device: no remote copies, remote signals or barrier semaphores. Data moves between devices by JAX's collectives and lax.ppermute only.
A program may use at most 64 MiB of HBM per device.

v0:
```python
import jax
import jax.numpy as jnp
from jax import lax
from jax.sharding import PartitionSpec as P


def local(image_emb, text_emb, logit_scale):
    multiplier = logit_scale[0]
    own_rows = image_emb.shape[0]
    text_block = lax.all_gather(text_emb, "img", axis=0, tiled=True)
    image_block = lax.all_gather(image_emb, "txt", axis=0, tiled=True)
    row_count = image_block.shape[0]
    col_count = text_block.shape[0]
    grand_total = own_rows * lax.axis_size("img") * lax.axis_size("txt")
    row_first = lax.axis_index("img") * row_count
    col_first = lax.axis_index("txt") * col_count
    logits = multiplier * lax.dot_general(
        image_block, text_block, (((1,), (1,)), ((), ())), preferred_element_type=jnp.float32
    )
    row_top = lax.pmax(jnp.max(logits, axis=1), "txt")
    col_top = lax.pmax(jnp.max(logits, axis=0), "img")
    row_total = lax.psum(jnp.sum(jnp.exp(logits - row_top[:, None]), axis=1), "txt")
    col_total = lax.psum(jnp.sum(jnp.exp(logits - col_top[None, :]), axis=0), "img")
    row_lse = row_top + jnp.log(row_total)
    col_lse = col_top + jnp.log(col_total)
    col_ids = col_first + jnp.arange(col_count, dtype=jnp.int32)
    all_rows = row_first + jnp.arange(row_count, dtype=jnp.int32)
    matches = all_rows[:, None] == col_ids[None, :]
    local_loss = jnp.sum(
        jnp.where(matches, row_lse[:, None] + col_lse[None, :] - 2.0 * logits, 0.0)
    ) / (2.0 * grand_total)
    mean_loss = lax.psum(local_loss, ("img", "txt")).reshape(1)
    row_ids = row_first + jnp.arange(logits.shape[0], dtype=jnp.int32)
    labels = (row_ids[:, None] == col_ids[None, :]).astype(jnp.float32)
    weights = (
        0.5 * jnp.exp(logits - row_lse[:, None]) + 0.5 * jnp.exp(logits - col_lse[None, :]) - labels
    ).astype(jnp.bfloat16)
    image_grad = lax.psum_scatter(
        (multiplier * jnp.dot(weights, text_block, preferred_element_type=jnp.float32)).astype(
            jnp.bfloat16
        ),
        "txt",
        scatter_dimension=0,
        tiled=True,
    )
    text_grad = lax.psum_scatter(
        (
            multiplier
            * lax.dot_general(
                weights, image_block, (((0,), (0,)), ((), ())), preferred_element_type=jnp.float32
            )
        ).astype(jnp.bfloat16),
        "img",
        scatter_dimension=0,
        tiled=True,
    )
    return (mean_loss, image_grad, text_grad)


def solution(mesh):
    return jax.shard_map(
        local,
        mesh=mesh,
        in_specs=(P(("img", "txt"), None), P(("txt", "img"), None), P()),
        out_specs=(P(), P(("img", "txt"), None), P(("txt", "img"), None)),
        check_vma=False,
    )
```

profile of v0, /device:TPU:32, one launch (start us, length us, event | category | flops | bytes accessed | tf_op | source)
XLA Modules:
  0.0 725.2 jit_solution(8122168581603303964)
XLA Ops:
  7.2 0.0 all-gather.5.cloned.1.call-start
  7.2 0.7 all-gather.5.cloned.1.call-update
  7.9 0.0 all-gather.3.cloned.1.call-start
  7.9 0.7 all-gather.3.cloned.1.call-update
  8.6 0.0 reduce-scatter.5.cloned.1.call-start
  9.4 37.4 %all-gather.5.cloned.1.call-done = bf16[512,1280]{1,0:T(8,128)(2,1)} async-done(((bf16[64,1280]{1,0:T(8,128)(2,1)}), bf16[512,1280]{1,0:T(8,128)(2,1)}) %all-gather.5.cloned.1.call-update) | async-done | bytes 1310736 | tf_op jit(solution)/shard_map/all_gather | solution.py:10
  46.8 126.9 %all-gather.3.cloned.1.call-done = bf16[2048,1280]{1,0:T(8,128)(2,1)} async-done(((bf16[64,1280]{1,0:T(8,128)(2,1)}), bf16[2048,1280]{1,0:T(8,128)(2,1)}) %all-gather.3.cloned.1.call-update) | async-done | bytes 5242896 | tf_op jit(solution)/shard_map/all_gather | solution.py:11
  173.7 7.9 %fusion.6 = (f32[2048]{0:T(1024)S(1)}, f32[512]{0:T(512)S(1)}, f32[2048,512]{1,0:T(8,128)}) fusion(bf16[2048,1280]{1,0:T(8,128)(2,1)} %all-gather.3.cloned.1.call-done, bf16[512,1280]{1,0:T(8,128)(2,1)} %all-gather.5.cloned.1.call-done, f32[]{:T(128)} %bitcast.6), kind=kOutput, calls=%fused_computation.15 | convolution fusion | flops 2687497728 | bytes 10758148 | tf_op jit(solution)/shard_map/dot_general | solution.py:17
  181.6 112.5 %pmax.14 = f32[2048]{0:T(1024)S(1)} all-reduce(f32[2048]{0:T(1024)S(1)} %get-tuple-element.5), channel_id=1, replica_groups=mesh['img'=8,'txt'=32] {'txt'}, use_global_device_ids=true, to_apply=%region_1.0 | all-reduce | flops 2048 | bytes 16384 | tf_op jit(solution)/shard_map/pmax | solution.py:20
  294.1 10.2 %pmax.15 = f32[512]{0:T(512)S(1)} all-reduce(f32[512]{0:T(512)S(1)} %get-tuple-element.6), channel_id=1, replica_groups=mesh['img'=8,'txt'=32] {'img'}, use_global_device_ids=true, to_apply=%region_5.0 | all-reduce | flops 512 | bytes 4096 | tf_op jit(solution)/shard_map/pmax | solution.py:21
  304.3 3.2 exponential_reduce_fusion.1
  307.4 109.3 %psum.21 = f32[2048]{0:T(1024)S(1)} all-reduce(f32[2048]{0:T(1024)S(1)} %get-tuple-element.3), channel_id=1, replica_groups=mesh['img'=8,'txt'=32] {'txt'}, use_global_device_ids=true, to_apply=%region_3.0 | all-reduce | flops 2048 | bytes 16384 | tf_op jit(solution)/shard_map/psum | solution.py:22
  416.8 13.0 %psum.22 = f32[512]{0:T(512)S(1)} all-reduce(f32[512]{0:T(512)S(1)} %get-tuple-element.4), channel_id=1, replica_groups=mesh['img'=8,'txt'=32] {'img'}, use_global_device_ids=true, to_apply=%region_7.0 | all-reduce | flops 512 | bytes 4096 | tf_op jit(solution)/shard_map/psum | solution.py:23
  429.8 0.0 copy-start
  429.8 8.5 %fusion.3 = bf16[512,1280]{1,0:T(8,128)(2,1)} fusion(bf16[2048,1280]{1,0:T(8,128)(2,1)} %all-gather.3.cloned.1.call-done, f32[]{:T(128)} %bitcast.8, f32[2048,512]{1,0:T(8,128)} %get-tuple-element.7, f32[512]{0:T(512)S(1)} %log_add_fusion.1, f32[2048]{0:T(1024)S(1)} %log_add_fusion, s32[512]{0:T(512)S(1)} %iota_add_fusion.1, s32[2048]{0:T(1024)S(1)} %iota_add_fusion), kind=kOutput, calls=%fused_computation.10 | convolution fusion | flops 2694053888 | bytes 10768388 | tf_op jit(solution)/shard_map/dot_general | solution.py:49
  438.2 0.0 reduce-scatter.5.cloned.1.call-update
  438.3 0.0 reduce-scatter.3.cloned.1.call-start
  438.3 0.0 copy-done
  438.3 7.4 %multiply_convert_fusion = bf16[2048,1280]{1,0:T(8,128)(2,1)} fusion(bf16[512,1280]{1,0:T(8,128)(2,1)S(1)} %copy-done, f32[]{:T(128)} %bitcast.7, f32[2048,512]{1,0:T(8,128)} %get-tuple-element.7, f32[512]{0:T(512)S(1)} %log_add_fusion.1, f32[2048]{0:T(1024)S(1)} %log_add_fusion, s32[512]{0:T(512)S(1)} %iota_add_fusion.1, s32[2048]{0:T(1024)S(1)} %iota_add_fusion), kind=kOutput, calls=%fused_computation | convolution fusion | flops 2697986048 | bytes 10768388 | tf_op jit(solution)/shard_map/dot_general | solution.py:39
  445.8 0.0 reduce-scatter.3.cloned.1.call-update
  445.8 3.9 fusion
  450.3 80.3 %psum.23 = f32[1]{0:T(128)} all-reduce(f32[1]{0:T(128)} %bitcast.1), channel_id=1, replica_groups=mesh['img'=8,'txt'=32] {'img','txt'}, use_global_device_ids=true, to_apply=%region_9.10 | all-reduce | flops 1 | bytes 8 | tf_op jit(solution)/shard_map/psum | solution.py:32
  530.6 0.0 reduce-scatter.5.cloned.1.call-done
  530.6 188.2 %reduce-scatter.3.cloned.1.call-done = bf16[64,1280]{1,0:T(8,128)(2,1)} async-done(((bf16[2048,1280]{1,0:T(8,128)(2,1)}), bf16[64,1280]{1,0:T(8,128)(2,1)}) %reduce-scatter.3.cloned.1.call-update) | async-done | bytes 163856 | tf_op jit(solution)/shard_map/reduce_scatter | solution.py:38
  (4 shorter events, 0.0 us)
Async XLA Ops:
  7.2 39.6 %all-gather.5.cloned.1.call-start = ((), (), s32[]{:S(2)}) async-start(), calls=%async_computation.3 | async-start | bytes 1474560 | tf_op jit(solution)/shard_map/all_gather | solution.py:10
  7.9 165.8 %all-gather.3.cloned.1.call-start = ((), (), s32[]{:S(2)}) async-start(), calls=%async_computation.2 | async-start | bytes 5406720 | tf_op jit(solution)/shard_map/all_gather | solution.py:11
  8.6 521.9 %reduce-scatter.5.cloned.1.call-start = ((), (), s32[]{:S(2)}) async-start(), calls=%async_computation.5 | async-start | bytes 1474560 | tf_op jit(solution)/shard_map/reduce_scatter | solution.py:46
  429.8 8.5 %copy-start = (bf16[512,1280]{1,0:T(8,128)(2,1)S(1)}, bf16[512,1280]{1,0:T(8,128)(2,1)}, u32[]{:S(2)}) copy-start(bf16[512,1280]{1,0:T(8,128)(2,1)} %all-gather.5.cloned.1.call-done) | copy-start | bytes 3932164
  438.3 280.5 %reduce-scatter.3.cloned.1.call-start = ((), (), s32[]{:S(2)}) async-start(), calls=%async_computation.4 | async-start | bytes 5406720 | tf_op jit(solution)/shard_map/reduce_scatter | solution.py:38
Sparse Core Ops, SparseCore 0:
  9.8 36.9 all-gather.4
  50.2 123.4 all-gather.2
  438.4 36.5 reduce-scatter.4
  478.0 240.6 reduce-scatter.2
where the time goes:
time: 733 us; the launch traced here: 725 us
  waiting for transfers between devices  354 us (48%)
  blocking collectives  325 us (44%)
  matrix products  23.8 us (3%)
  between operations  15.1 us (2%)
    reduce_scatter x1, waiting for transfers between devices, local(): lax.psum_scatter((multiplier * jnp.dot(weights, text_block, preferred_ele...  188 us
    all_gather x1, waiting for transfers between devices, local(): image_block = lax.all_gather(image_emb, 'txt', axis=0, tiled=True)  127 us
    pmax x1, blocking collectives, local(): row_top = lax.pmax(jnp.max(logits, axis=1), 'txt')  112 us
    psum x1, blocking collectives, local(): lax.psum(jnp.sum(jnp.exp(logits - row_top[:, None]), axis=1), 'txt')  109 us
    psum x1, blocking collectives, local(): mean_loss = lax.psum(local_loss, ('img', 'txt')).reshape(1)  80.3 us
    all_gather x1, waiting for transfers between devices, local(): text_block = lax.all_gather(text_emb, 'img', axis=0, tiled=True)  37.4 us
  transfers between devices with their start and end apart: 4, of which 3 were waited for; matrix products, arithmetic and copies ran while one was open for 2% of the time, Pallas kernels for 0%

commit v1 on v0

v1 whole, which is shorter than its diff:
```python
import jax
import jax.numpy as jnp
from jax import lax
from jax.experimental import pallas as pl
from jax.experimental.pallas import tpu as pltpu
from jax.sharding import Mesh, PartitionSpec as P

AXES = ("zl", "core", "zh", "y", "x")
NX, NY, NZ = 4, 4, 8
ROWS, EMBED = 64, 1280
CHUNK = 4 * ROWS
BLOCK = 16 * ROWS
BF16, F32 = jnp.bfloat16, jnp.float32
VMEM = pl.BlockSpec(memory_space=pltpu.VMEM)
SMEM = pl.BlockSpec(memory_space=pltpu.SMEM)
PARAMS = pltpu.CompilerParams(vmem_limit_bytes=36 * 1024 * 1024)


def plane_shift(v, k, primary):
    pairs = []
    for c in range(2):
        for h in range(2):
            for y in range(NY):
                for x in range(NX):
                    if (c == 0) == primary:
                        to = (y, (x + k) % NX)
                    else:
                        to = ((y + k) % NY, x)
                    base = (c * 2 + h) * NY
                    pairs.append(((base + y) * NX + x, (base + to[0]) * NX + to[1]))
    return lax.ppermute(v, ("core", "zh", "y", "x"), pairs)


def z_index(z):
    return (z % 4) * 2 + z // 4


def z_shift(v, k):
    pairs = []
    for c in range(2):
        for z in range(NZ):
            to = (z + (k if c == 0 else -k)) % NZ
            pairs.append((((z % 4) * 2 + c) * 2 + z // 4, ((to % 4) * 2 + c) * 2 + to // 4))
    return lax.ppermute(v, ("zl", "core", "zh"), pairs)


def core_swap(v):
    return lax.ppermute(v, "core", [(0, 1), (1, 0)])


def flip(v, axis, bit):
    if axis == "z":
        return lax.ppermute(v, ("zl", "zh"), [(z_index(i), z_index(i ^ bit)) for i in range(NZ)])
    return lax.ppermute(v, axis, [(i, i ^ bit) for i in range(lax.axis_size(axis))])


def lse2(a, b):
    top = jnp.maximum(a, b)
    return top + jnp.log(jnp.exp(a - top) + jnp.exp(b - top))


def row_place(where, a, b):
    zl, c, zh, y, x = where
    p, s = jnp.where(c == 0, b, a), jnp.where(c == 0, a, b)
    n = ((y - s) & 3) * 4 + ((x - p) & 3)
    return n, ((zl * 2 + c) * 2 + zh) * 16 + n


def col_place(where, j, i):
    zl, c, zh, y, x = where
    core = c if j < 2 else 1 - c
    sign = 1 - 2 * core
    off = sign * ((0, 0, 2, 2)[i] + j % 2) + (0, 4, 0, 4)[i]
    z = (zh * 4 + zl + off) & 7
    return z * 2 + core, ((z >> 2) * 16 + y * 4 + x) * 8 + (z & 3) * 2 + core


def row_ids(where, a):
    span = lax.broadcasted_iota(jnp.int32, (ROWS, 128), 0)
    return [row_place(where, a, b)[1] * ROWS + span for b in range(4)]


def col_ids(where):
    lane = lax.broadcasted_iota(jnp.int32, (8, 128), 1)
    out = []
    for t in range(8):
        lo = col_place(where, t // 2, (t % 2) * 2)[1] * ROWS
        hi = col_place(where, t // 2, (t % 2) * 2 + 1)[1] * ROWS - ROWS
        out.append(lane + jnp.where(lane < ROWS, lo, hi))
    return out


def pack_body(n, *refs):
    at = 0
    for r in refs[:n]:
        refs[n][at : at + r.shape[0], :] = r[...]
        at += r.shape[0]


def pack(*parts):
    rows = sum(p.shape[0] for p in parts)
    return pl.pallas_call(
        lambda *refs: pack_body(len(parts), *refs),
        out_shape=jax.ShapeDtypeStruct((rows, EMBED), BF16),
        in_specs=[VMEM] * len(parts),
        out_specs=VMEM,
        compiler_params=PARAMS,
    )(*parts)


def logits_body(place, scale, *refs):
    images, texts = refs[:4], refs[4:8]
    logits, row_out, col_out, match_out = refs[8:12]
    row_wide = refs[12]
    where = [place[i] for i in range(5)]
    multiplier = scale[0]
    for a in range(4):
        for j in range(4):
            logits[a * CHUNK : (a + 1) * CHUNK, j * CHUNK : (j + 1) * CHUNK] = (
                multiplier
                * lax.dot_general(
                    images[a][...],
                    texts[j][...],
                    (((1,), (1,)), ((), ())),
                    preferred_element_type=F32,
                )
            )
    cols = col_ids(where)
    step = 32
    matched = jnp.zeros((8, 128), F32)
    col_top = [jnp.full((8, 128), -jnp.inf, F32) for _ in range(8)]
    for a in range(4):
        ids = row_ids(where, a)
        for b in range(4):
            for half in range(ROWS // step):
                at = a * CHUNK + b * ROWS + half * step
                tiles = [logits[at : at + step, t * 128 : (t + 1) * 128] for t in range(8)]
                top = tiles[0]
                for t in range(1, 8):
                    top = jnp.maximum(top, tiles[t])
                top = jnp.max(top, axis=1, keepdims=True)
                mine = ids[b][half * step : (half + 1) * step]
                total = jnp.zeros((step, 128), F32)
                for t in range(8):
                    total += jnp.exp(tiles[t] - top)
                    folded = tiles[t].reshape(step // 8, 8, 128)
                    col_top[t] = jnp.maximum(col_top[t], jnp.max(folded, axis=0))
                    hit = jnp.where(mine == cols[t][0:1], tiles[t], 0.0)
                    matched += jnp.sum(hit.reshape(step // 8, 8, 128), axis=0)
                part = top + jnp.log(jnp.sum(total, axis=1, keepdims=True))
                row_wide[at : at + step, :] = jnp.broadcast_to(part, (step, 128))
    match_out[...] = jnp.broadcast_to(jnp.sum(matched, keepdims=True), (8, 128))
    col_out[...] = jnp.zeros((16, 128), F32)
    row_out[...] = jnp.zeros((16, 128), F32)
    for t in range(8):
        top = jnp.max(col_top[t], axis=0, keepdims=True)

        def cols_pass(i, total, t=t, top=top):
            tile = logits[pl.ds(pl.multiple_of(i * 128, 128), 128), t * 128 : (t + 1) * 128]
            return total + jnp.sum(jnp.exp(tile - top).reshape(16, 8, 128), axis=0)

        total = lax.fori_loop(0, 8, cols_pass, jnp.zeros((8, 128), F32), unroll=True)
        part = top + jnp.log(jnp.sum(total, axis=0, keepdims=True))
        j, i = t // 2, (t % 2) * 2
        col_out[pl.ds(col_place(where, j, i)[0], 1), :] = part
        col_out[pl.ds(col_place(where, j, i + 1)[0], 1), :] = pltpu.roll(part, 64, 1)
        line = jnp.transpose(row_wide[t * 128 : (t + 1) * 128, :])[0:1]
        row_out[pl.ds(row_place(where, j, i)[0], 1), :] = line
        row_out[pl.ds(row_place(where, j, i + 1)[0], 1), :] = pltpu.roll(line, 64, 1)


def logits_call(place, scale, images, texts):
    return pl.pallas_call(
        logits_body,
        out_shape=(
            jax.ShapeDtypeStruct((BLOCK, BLOCK), F32),
            jax.ShapeDtypeStruct((16, 128), F32),
            jax.ShapeDtypeStruct((16, 128), F32),
            jax.ShapeDtypeStruct((8, 128), F32),
        ),
        in_specs=[SMEM, SMEM] + [VMEM] * 8,
        out_specs=(VMEM,) * 4,
        scratch_shapes=[pltpu.VMEM((BLOCK, 128), F32)],
        compiler_params=PARAMS,
    )(place, scale, *images, *texts)


def text_body(place, scale, logits, row_lse, col_lse, *refs):
    images = refs[:4]
    weights = refs[4]
    outs = refs[5:9]
    row_wide = refs[9]
    where = [place[i] for i in range(5)]
    multiplier = scale[0]
    lane = lax.broadcasted_iota(jnp.int32, (1, 128), 1)
    cols = col_ids(where)
    col_line = []
    for t in range(8):
        j, i = t // 2, (t % 2) * 2
        lo = col_lse[pl.ds(col_place(where, j, i)[0], 1), :]
        hi = col_lse[pl.ds(col_place(where, j, i + 1)[0], 1), :]
        col_line.append(jnp.where(lane < ROWS, lo, pltpu.roll(hi, 64, 1)))
        lo = row_lse[pl.ds(row_place(where, j, i)[0], 1), :]
        hi = row_lse[pl.ds(row_place(where, j, i + 1)[0], 1), :]
        line = jnp.where(lane < ROWS, lo, pltpu.roll(hi, 64, 1))
        row_wide[t * 128 : (t + 1) * 128, :] = jnp.transpose(jnp.broadcast_to(line, (128, 128)))
    for a in range(4):
        ids = row_ids(where, a)
        for b in range(4):
            at = a * CHUNK + b * ROWS
            wide = row_wide[at : at + ROWS, :]
            for t in range(8):
                tile = logits[at : at + ROWS, t * 128 : (t + 1) * 128]
                both = 0.5 * jnp.exp(tile - wide) + 0.5 * jnp.exp(tile - col_line[t])
                both = both - jnp.where(ids[b] == cols[t][0:1], 1.0, 0.0)
                weights[at : at + ROWS, t * 128 : (t + 1) * 128] = both.astype(BF16)
    for j in (3, 2, 1, 0):
        for e in range(5):
            acc = None
            for a in range(4):
                term = lax.dot_general(
                    weights[a * CHUNK : (a + 1) * CHUNK, j * CHUNK : (j + 1) * CHUNK],
                    images[a][:, e * 256 : (e + 1) * 256],
                    (((0,), (0,)), ((), ())),
                    preferred_element_type=F32,
                )
                acc = term if acc is None else acc + term
            outs[j][:, e * 256 : (e + 1) * 256] = (multiplier * acc).astype(BF16)


def text_call(place, scale, logits, row_lse, col_lse, images):
    part = jax.ShapeDtypeStruct((CHUNK, EMBED), BF16)
    return pl.pallas_call(
        text_body,
        out_shape=(jax.ShapeDtypeStruct((BLOCK, BLOCK), BF16), part, part, part, part),
        in_specs=[SMEM, SMEM] + [VMEM] * 7,
        out_specs=(VMEM,) * 5,
        scratch_shapes=[pltpu.VMEM((BLOCK, 128), F32)],
        compiler_params=PARAMS,
    )(place, scale, logits, row_lse, col_lse, *images)


def image_body(scale, weights, *refs):
    texts, outs = refs[:4], refs[4:]
    multiplier = scale[0]
    for a in (2, 1, 3, 0):
        for e in range(5):
            acc = None
            for j in range(4):
                term = jnp.dot(
                    weights[a * CHUNK : (a + 1) * CHUNK, j * CHUNK : (j + 1) * CHUNK],
                    texts[j][:, e * 256 : (e + 1) * 256],
                    preferred_element_type=F32,
                )
                acc = term if acc is None else acc + term
            outs[a][:, e * 256 : (e + 1) * 256] = (multiplier * acc).astype(BF16)


def image_call(scale, weights, texts):
    part = jax.ShapeDtypeStruct((CHUNK, EMBED), BF16)
    return pl.pallas_call(
        image_body,
        out_shape=(part,) * 4,
        in_specs=[SMEM] + [VMEM] * 5,
        out_specs=(VMEM,) * 4,
        compiler_params=PARAMS,
    )(scale, weights, *texts)


def add_body(n, *refs):
    outs = refs[n:]
    rows = outs[0].shape[0]
    for o, out in enumerate(outs):
        for at in range(0, rows, 16):
            total = refs[0][o * rows + at : o * rows + at + 16, :].astype(F32)
            for r in refs[1:n]:
                total += r[o * rows + at : o * rows + at + 16, :].astype(F32)
            out[at : at + 16, :] = total.astype(out.dtype)


def add(parts, pieces=1):
    rows = parts[0].shape[0] // pieces
    out = pl.pallas_call(
        lambda *refs: add_body(len(parts), *refs),
        out_shape=(jax.ShapeDtypeStruct((rows, EMBED), BF16),) * pieces,
        in_specs=[VMEM] * len(parts),
        out_specs=(VMEM,) * pieces,
        compiler_params=PARAMS,
    )(*parts)
    return out if pieces > 1 else out[0]


def local(image_emb, text_emb, logit_scale):
    place = jnp.stack([lax.axis_index(n) for n in AXES]).astype(jnp.int32)

    far = z_shift(text_emb, 4)
    near = [plane_shift(image_emb, k, True) for k in (1, 2, 3)]
    pair = pack(text_emb, far)
    own = pack(image_emb, *near)
    text_0 = pack(pair, z_shift(pair, -2))
    images = [own] + [plane_shift(own, k, False) for k in (1, 2, 3)]
    text_1 = z_shift(text_0, -1)
    texts = [text_0, text_1, core_swap(text_0), core_swap(text_1)]

    logits, row_part, col_part, matched = logits_call(place, logit_scale, images, texts)

    row_lse, col_lse = row_part, col_part
    for axis, bit, col_axis, col_bit in (
        ("x", 2, "z", 4),
        ("x", 1, "z", 2),
        ("y", 2, "z", 1),
        ("y", 1, "core", 1),
    ):
        row_lse = lse2(row_lse, flip(row_lse, axis, bit))
        col_lse = lse2(col_lse, flip(col_lse, col_axis, col_bit))

    weights, *text_parts = text_call(place, logit_scale, logits, row_lse, col_lse, images)
    back_1, back_0 = core_swap(text_parts[3]), core_swap(text_parts[2])
    image_parts = image_call(logit_scale, weights, texts)

    back = [plane_shift(image_parts[k], -k, False) for k in (2, 1, 3)]
    t = z_shift(add([text_parts[1], back_1]), 1)
    t_near, t_far = add([text_parts[0], back_0, t], pieces=2)
    pieces = add([image_parts[0]] + back, pieces=4)
    t_near, t_far = add([t_near, z_shift(t_far, 2)], pieces=2)
    image_grad = add([pieces[0]] + [plane_shift(pieces[k], -k, True) for k in (2, 1, 3)])
    text_grad = add([t_near, z_shift(t_far, 4)])

    real = lax.broadcasted_iota(jnp.int32, (16, 128), 1) < ROWS
    lses = jnp.sum(jnp.where(real, row_lse + col_lse, 0.0)) / 16.0
    s = jnp.broadcast_to(lses - 2.0 * matched[0, 0], (8, 128))
    for axis, bit in (("x", 2), ("x", 1), ("y", 2), ("y", 1), ("z", 4), ("z", 2), ("z", 1), ("core", 1)):
        s = s + flip(s, axis, bit)
    mean_loss = s[0, :1] / (2.0 * ROWS * 256)
    return mean_loss, image_grad, text_grad


def solution(mesh):
    fine = Mesh(mesh.devices.reshape(4, 2, 2, 4, 4), AXES)
    return jax.shard_map(
        local,
        mesh=fine,
        in_specs=(P(AXES, None), P(("zh", "y", "x", "zl", "core"), None), P()),
        out_specs=(P(), P(AXES, None), P(("zh", "y", "x", "zl", "core"), None)),
        check_vma=False,
    )
```

time: 733 us -> 165 us (0.23)
  blocking collectives: 325 us -> 0 us
  waiting for transfers between devices: 354 us -> 66.7 us
  starting transfers between devices: 0.16 us -> 67.7 us
  matrix products: 23.8 us -> 0 us
  Pallas kernels: 0 us -> 19.2 us
  between operations: 15.1 us -> 4.5 us
    psum x3 -> x0, blocking collectives: 203 us -> none  [the longest x1 109 us: local(): lax.psum(jnp.sum(jnp.exp(logits - row_top[:, None]), axis=1), 'txt')]
    reduce_scatter x2 -> x0, waiting for transfers between devices: 188 us -> none  [the longest x1 188 us: local(): lax.psum_scatter((multiplier * jnp.dot(weights, text_block, preferred_ele...]
    all_gather x2 -> x0, waiting for transfers between devices: 164 us -> none  [the longest x1 127 us: local(): image_block = lax.all_gather(image_emb, 'txt', axis=0, tiled=True)]
    pmax x2 -> x0, blocking collectives: 123 us -> none  [the longest x1 112 us: local(): row_top = lax.pmax(jnp.max(logits, axis=1), 'txt')]
    ppermute x0 -> x38, starting transfers between devices: none -> 67.7 us  [the longest x6 20 us: z_shift(): return lax.ppermute(v, ('zl', 'core', 'zh'), pairs)]
    ppermute x0 -> x38, waiting for transfers between devices: none -> 66.7 us  [the longest x12 21.5 us: plane_shift(): return lax.ppermute(v, ('core', 'zh', 'y', 'x'), pairs)]
    dot_general x3 -> x0, matrix products: 23.8 us -> none  [the longest x1 8.45 us: local(): lax.dot_general(weights, image_block, (((0,), (0,)), ((), ())), preferred...]
    pallas_call x0 -> x12, Pallas kernels: none -> 19.2 us  [the longest x1 7.09 us: text_call(): pl.pallas_call(text_body, out_shape=(jax.ShapeDtypeStruct((BLOCK, BLOCK),...]
  transfers between devices with their start and end apart: 4 -> 38, of which waited for: 3 -> 21; matrix products, arithmetic and copies ran while one was open for 2% -> 1% of each run, Pallas kernels for 0% -> 3%
where the time goes in v1:
time: 165 us; the launch traced here: 162 us
  starting transfers between devices  67.7 us (41%)
  waiting for transfers between devices  66.7 us (40%)
  Pallas kernels  19.2 us (12%)
  between operations  4.5 us (3%)
  local copies, waits for them, and re-layouts  2.95 us (2%)
    ppermute x12, waiting for transfers between devices, plane_shift(): return lax.ppermute(v, ('core', 'zh', 'y', 'x'), pairs)  21.5 us
    ppermute x6, starting transfers between devices, z_shift(): return lax.ppermute(v, ('zl', 'core', 'zh'), pairs)  20 us
    ppermute x12, starting transfers between devices, plane_shift(): return lax.ppermute(v, ('core', 'zh', 'y', 'x'), pairs)  19 us
    ppermute x6, waiting for transfers between devices, z_shift(): return lax.ppermute(v, ('zl', 'core', 'zh'), pairs)  17.5 us
    ppermute x6, starting transfers between devices, flip(): lax.ppermute(v, ('zl', 'zh'), [(z_index(i), z_index(i ^ bit)) for i in ra...  14.3 us
    ppermute x10, waiting for transfers between devices, flip(): lax.ppermute(v, axis, [(i, i ^ bit) for i in range(lax.axis_size(axis))])  14 us
    ppermute x10, starting transfers between devices, flip(): lax.ppermute(v, axis, [(i, i ^ bit) for i in range(lax.axis_size(axis))])  13.3 us
    ppermute x6, waiting for transfers between devices, flip(): lax.ppermute(v, ('zl', 'zh'), [(z_index(i), z_index(i ^ bit)) for i in ra...  12.1 us
  transfers between devices with their start and end apart: 38, of which 21 were waited for; matrix products, arithmetic and copies ran while one was open for 1% of the time, Pallas kernels for 3%

profile of v1, /device:TPU:32, one launch (start us, length us, event | category | flops | bytes accessed | tf_op | source)
XLA Modules:
  0.0 161.8 jit_solution(124524926931902156)
XLA Ops:
  0.6 6.4 %collective-permute-start.6 = (bf16[64,1280]{1,0:T(8,128)(2,1)}, bf16[64,1280]{1,0:T(8,128)(2,1)S(1)}, u32[]{:S(2)}, u32[]{:S(2)}) collective-permute-start(bf16[64,1280]{1,0:T(8,128)(2,1)} %refs_0_.3), channel_id=1, source_target_pairs={{0,16},{64,80},{128,144},{192,208},{16,0},{80,64},{144,128},{208,1... | collective-permute-start | bytes 491528 | tf_op jit(solution)/shard_map/ppermute | solution.py:44
  7.0 7.7 %collective-permute-done.6.refs_1_ = bf16[64,1280]{1,0:T(8,128)(2,1)S(1)} collective-permute-done((bf16[64,1280]{1,0:T(8,128)(2,1)}, bf16[64,1280]{1,0:T(8,128)(2,1)S(1)}, u32[]{:S(2)}, u32[]{:S(2)}) %collective-permute-start.6) | collective-permute-done | bytes 163872 | tf_op jit(solution)/shard_map/ppermute | solution.py:44
  14.7 0.9 copy-done
  15.6 4.0 %collective-permute-start.7 = (bf16[128,1280]{1,0:T(8,128)(2,1)S(1)}, bf16[128,1280]{1,0:T(8,128)(2,1)S(1)}, u32[]{:S(2)}, u32[]{:S(2)}) collective-permute-start(bf16[128,1280]{1,0:T(8,128)(2,1)S(1)} %shard_map.59.refs_0_), channel_id=1, source_target_pairs={{0,144},{64,208},{128,0},{192,64},{16,128},{80,192},{144,16},{208,... | collective-permute-start | bytes 983048 | tf_op jit(solution)/shard_map/ppermute | solution.py:44
  19.7 6.8 %collective-permute-done.7.refs_1_ = bf16[128,1280]{1,0:T(8,128)(2,1)S(1)} collective-permute-done((bf16[128,1280]{1,0:T(8,128)(2,1)S(1)}, bf16[128,1280]{1,0:T(8,128)(2,1)S(1)}, u32[]{:S(2)}, u32[]{:S(2)}) %collective-permute-start.7) | collective-permute-done | bytes 327712 | tf_op jit(solution)/shard_map/ppermute | solution.py:44
  26.5 2.9 %collective-permute-start.8 = (bf16[256,1280]{1,0:T(8,128)(2,1)S(1)}, bf16[256,1280]{1,0:T(8,128)(2,1)S(1)}, u32[]{:S(2)}, u32[]{:S(2)}) collective-permute-start(bf16[256,1280]{1,0:T(8,128)(2,1)S(1)} %shard_map.60.refs_4_.refs_0_), channel_id=1, source_target_pairs={{0,208},{64,0},{128,64},{192,128},{16,192},{80,16},{144,80},{208,1... | collective-permute-start | bytes 1966088 | tf_op jit(solution)/shard_map/ppermute | solution.py:44
  29.4 3.0 %collective-permute-start.1 = (bf16[64,1280]{1,0:T(8,128)(2,1)}, bf16[64,1280]{1,0:T(8,128)(2,1)S(1)}, u32[]{:S(2)}, u32[]{:S(2)}) collective-permute-start(bf16[64,1280]{1,0:T(8,128)(2,1)} %refs_0_.2), channel_id=1, source_target_pairs={{0,2},{1,3},{2,0},{3,1},{4,6},{5,7},{6,4},{7,5},{8,10},{9,11},{10,... | collective-permute-start | bytes 491528 | tf_op jit(solution)/shard_map/ppermute | solution.py:31
  32.4 0.6 collective-permute-start
  33.0 2.6 %collective-permute-start.2 = (bf16[64,1280]{1,0:T(8,128)(2,1)}, bf16[64,1280]{1,0:T(8,128)(2,1)S(1)}, u32[]{:S(2)}, u32[]{:S(2)}) collective-permute-start(bf16[64,1280]{1,0:T(8,128)(2,1)} %refs_0_.2), channel_id=1, source_target_pairs={{0,3},{1,0},{2,1},{3,2},{4,7},{5,4},{6,5},{7,6},{8,11},{9,8},{10,9... | collective-permute-start | bytes 491528 | tf_op jit(solution)/shard_map/ppermute | solution.py:31
  35.6 0.8 collective-permute-done.1.refs_2_
  36.4 2.7 %collective-permute-done.refs_1_ = bf16[64,1280]{1,0:T(8,128)(2,1)S(1)} collective-permute-done((bf16[64,1280]{1,0:T(8,128)(2,1)}, bf16[64,1280]{1,0:T(8,128)(2,1)S(1)}, u32[]{:S(2)}, u32[]{:S(2)}) %collective-permute-start) | collective-permute-done | bytes 163872 | tf_op jit(solution)/shard_map/ppermute | solution.py:31
  39.1 0.9 copy-done.1
  40.1 3.1 %collective-permute-start.5 = (bf16[256,1280]{1,0:T(8,128)(2,1)S(1)}, bf16[256,1280]{1,0:T(8,128)(2,1)}, u32[]{:S(2)}, u32[]{:S(2)}) collective-permute-start(bf16[256,1280]{1,0:T(8,128)(2,1)S(1)} %shard_map.58.refs_0_), channel_id=1, source_target_pairs={{0,12},{1,13},{2,14},{3,15},{4,0},{5,1},{6,2},{7,3},{8,4},{9,5},{1... | collective-permute-start | bytes 1966088 | tf_op jit(solution)/shard_map/ppermute | solution.py:31
  43.2 0.6 collective-permute-start.4
  43.8 1.0 collective-permute-start.3
  44.8 0.5 collective-permute-start.10
  46.0 12.3 %collective-permute-done.5.refs_3_ = bf16[256,1280]{1,0:T(8,128)(2,1)} collective-permute-done((bf16[256,1280]{1,0:T(8,128)(2,1)S(1)}, bf16[256,1280]{1,0:T(8,128)(2,1)}, u32[]{:S(2)}, u32[]{:S(2)}) %collective-permute-start.5) | collective-permute-done | bytes 655392 | tf_op jit(solution)/shard_map/ppermute | solution.py:31
  58.3 4.1 %collective-permute-done.3.refs_1_ = bf16[256,1280]{1,0:T(8,128)(2,1)} collective-permute-done((bf16[256,1280]{1,0:T(8,128)(2,1)S(1)}, bf16[256,1280]{1,0:T(8,128)(2,1)}, u32[]{:S(2)}, u32[]{:S(2)}) %collective-permute-start.3) | collective-permute-done | bytes 655392 | tf_op jit(solution)/shard_map/ppermute | solution.py:31
  62.4 5.9 %shard_map.61 = (f32[1024,1024]{1,0:T(8,128)S(1)}, f32[16,128]{1,0:T(8,128)S(1)}, f32[16,128]{1,0:T(8,128)S(1)}, f32[8,128]{1,0:T(8,128)S(1)}) custom-call(s32[5]{0:T(128)S(1)} %stack.23.place, f32[1]{0:T(128)S(6)} %copy.6.scale, bf16[256,1280]{1,0:T(8,128)(2,1)S(1)} %shard_map.58.refs_0_, bf16[256,1280]{1,0:T(8,128)(2,1)} %collective-permute-done.3.refs_1_, ...), custom_call_target="tpu_custom_call" | custom-call | tf_op jit(solution)/shard_map/pallas_call | solution.py:173
  68.3 1.5 collective-permute-start.11
  69.8 3.9 %collective-permute-start.15 = (f32[16,128]{1,0:T(8,128)S(1)}, f32[16,128]{1,0:T(8,128)S(1)}, u32[]{:S(2)}, u32[]{:S(2)}) collective-permute-start(f32[16,128]{1,0:T(8,128)S(1)} %get-tuple-element.25), channel_id=1, source_target_pairs={{0,16},{64,80},{128,144},{192,208},{16,0},{80,64},{144,128},{208,1... | collective-permute-start | bytes 24584 | tf_op jit(solution)/shard_map/ppermute | solution.py:53
  73.7 2.7 %collective-permute-start.12 = (f32[16,128]{1,0:T(8,128)S(1)}, f32[16,128]{1,0:T(8,128)S(1)}, u32[]{:S(2)}, u32[]{:S(2)}) collective-permute-start(f32[16,128]{1,0:T(8,128)S(1)} %log_add_fusion.7), channel_id=1, source_target_pairs={{0,1},{1,0},{2,3},{3,2},{4,5},{5,4},{6,7},{7,6},{8,9},{9,8},{10,11... | collective-permute-start | bytes 24584 | tf_op jit(solution)/shard_map/ppermute | solution.py:54
  76.4 1.0 collective-permute-done.15
  77.4 2.4 %collective-permute-start.16 = (f32[16,128]{1,0:T(8,128)S(1)}, f32[16,128]{1,0:T(8,128)S(1)}, u32[]{:S(2)}, u32[]{:S(2)}) collective-permute-start(f32[16,128]{1,0:T(8,128)S(1)} %log_add_fusion.3), channel_id=1, source_target_pairs={{0,128},{64,192},{128,0},{192,64},{16,144},{80,208},{144,16},{208,... | collective-permute-start | bytes 24584 | tf_op jit(solution)/shard_map/ppermute | solution.py:53
  79.8 1.9 %collective-permute-start.13 = (f32[16,128]{1,0:T(8,128)S(1)}, f32[16,128]{1,0:T(8,128)S(1)}, u32[]{:S(2)}, u32[]{:S(2)}) collective-permute-start(f32[16,128]{1,0:T(8,128)S(1)} %log_add_fusion.6), channel_id=1, source_target_pairs={{0,8},{4,12},{8,0},{12,4},{1,9},{5,13},{9,1},{13,5},{2,10},{6,14},... | collective-permute-start | bytes 24584 | tf_op jit(solution)/shard_map/ppermute | solution.py:54
  82.0 2.5 %collective-permute-start.17 = (f32[16,128]{1,0:T(8,128)S(1)}, f32[16,128]{1,0:T(8,128)S(1)}, u32[]{:S(2)}, u32[]{:S(2)}) collective-permute-start(f32[16,128]{1,0:T(8,128)S(1)} %log_add_fusion.2), channel_id=1, source_target_pairs={{0,64},{64,0},{128,192},{192,128},{16,80},{80,16},{144,208},{208,1... | collective-permute-start | bytes 24584 | tf_op jit(solution)/shard_map/ppermute | solution.py:53
  84.5 0.5 collective-permute-done.13
  85.1 0.5 collective-permute-start.14
  85.5 0.7 collective-permute-done.17
  86.3 2.5 %collective-permute-done.14 = f32[16,128]{1,0:T(8,128)S(1)} collective-permute-done((f32[16,128]{1,0:T(8,128)S(1)}, f32[16,128]{1,0:T(8,128)S(1)}, u32[]{:S(2)}, u32[]{:S(2)}) %collective-permute-start.14) | collective-permute-done | bytes 8224 | tf_op jit(solution)/shard_map/ppermute | solution.py:54
  88.8 0.6 select_reduce_fusion
  89.4 7.1 %shard_map.62 = (bf16[1024,1024]{1,0:T(8,128)(2,1)S(1)}, bf16[256,1280]{1,0:T(8,128)(2,1)S(1)}, bf16[256,1280]{1,0:T(8,128)(2,1)S(1)}, bf16[256,1280]{1,0:T(8,128)(2,1)S(1)}, bf16[256,1280]{1,0:T(8,128)(2,1)S(1)}) custom-call(s32[5]{0:T(128)S(1)} %stack.23.place, f32[1]{0:T(128)S(6)} %copy.6.scale, f32[1024,1024]{1,0:T(8,128)S(1)} %get-tuple-element.27.logits, ...), custom_call_target="tpu_custom_call" | custom-call | tf_op jit(solution)/shard_map/pallas_call | solution.py:233
  96.6 0.5 collective-permute-start.33
  97.1 1.6 collective-permute-done.34.refs_1_
  98.9 1.9 %collective-permute-start.35 = (bf16[256,1280]{1,0:T(8,128)(2,1)S(1)}, bf16[256,1280]{1,0:T(8,128)(2,1)S(1)}, u32[]{:S(2)}, u32[]{:S(2)}) collective-permute-start(bf16[256,1280]{1,0:T(8,128)(2,1)S(1)} %shard_map.66), channel_id=1, source_target_pairs={{0,64},{64,128},{128,192},{192,16},{16,80},{80,144},{144,208},{208... | collective-permute-start | bytes 1966088 | tf_op jit(solution)/shard_map/ppermute | solution.py:44
  100.7 3.2 %shard_map.63 = (bf16[256,1280]{1,0:T(8,128)(2,1)S(1)}, bf16[256,1280]{1,0:T(8,128)(2,1)}, bf16[256,1280]{1,0:T(8,128)(2,1)}, bf16[256,1280]{1,0:T(8,128)(2,1)}) custom-call(f32[1]{0:T(128)S(6)} %copy.6.scale, bf16[1024,1024]{1,0:T(8,128)(2,1)S(1)} %get-tuple-element.28.weights, bf16[256,1280]{1,0:T(8,128)(2,1)S(1)} %shard_map.60.refs_4_.refs_0_, ...), custom_call_target="tpu_custom_call" | custom-call | tf_op jit(solution)/shard_map/pallas_call | solution.py:261
  104.0 0.6 collective-permute-start.27
  104.6 2.0 %collective-permute-start.28 = (bf16[256,1280]{1,0:T(8,128)(2,1)}, bf16[256,1280]{1,0:T(8,128)(2,1)S(1)}, u32[]{:S(2)}, u32[]{:S(2)}) collective-permute-start(bf16[256,1280]{1,0:T(8,128)(2,1)} %get-tuple-element.31), channel_id=1, source_target_pairs={{0,12},{1,13},{2,14},{3,15},{4,0},{5,1},{6,2},{7,3},{8,4},{9,5},{1... | collective-permute-start | bytes 1966088 | tf_op jit(solution)/shard_map/ppermute | solution.py:31
  106.7 3.1 %collective-permute-done.35.refs_2_ = bf16[256,1280]{1,0:T(8,128)(2,1)S(1)} collective-permute-done((bf16[256,1280]{1,0:T(8,128)(2,1)S(1)}, bf16[256,1280]{1,0:T(8,128)(2,1)S(1)}, u32[]{:S(2)}, u32[]{:S(2)}) %collective-permute-start.35) | collective-permute-done | bytes 655392 | tf_op jit(solution)/shard_map/ppermute | solution.py:44
  109.7 0.9 shard_map.67
  110.6 1.5 collective-permute-start.36
  112.1 0.5 slice.6
  114.0 2.0 %collective-permute-start.19 = (f32[8,128]{1,0:T(8,128)S(1)}, f32[8,128]{1,0:T(8,128)S(1)}, u32[]{:S(2)}, u32[]{:S(2)}) collective-permute-start(f32[8,128]{1,0:T(8,128)S(1)} %broadcast_in_dim.8), channel_id=1, source_target_pairs={{0,2},{1,3},{2,0},{3,1},{4,6},{5,7},{6,4},{7,5},{8,10},{9,11},{10,... | collective-permute-start | bytes 12296 | tf_op jit(solution)/shard_map/ppermute | solution.py:54
  115.9 3.3 %collective-permute-done.19 = f32[8,128]{1,0:T(8,128)S(1)} collective-permute-done((f32[8,128]{1,0:T(8,128)S(1)}, f32[8,128]{1,0:T(8,128)S(1)}, u32[]{:S(2)}, u32[]{:S(2)}) %collective-permute-start.19) | collective-permute-done | bytes 4128 | tf_op jit(solution)/shard_map/ppermute | solution.py:54
  119.3 2.4 %collective-permute-start.20 = (f32[8,128]{1,0:T(8,128)S(1)}, f32[8,128]{1,0:T(8,128)S(1)}, u32[]{:S(2)}, u32[]{:S(2)}) collective-permute-start(f32[8,128]{1,0:T(8,128)S(1)} %broadcast_add_fusion), channel_id=1, source_target_pairs={{0,1},{1,0},{2,3},{3,2},{4,5},{5,4},{6,7},{7,6},{8,9},{9,8},{10,11... | collective-permute-start | bytes 12296 | tf_op jit(solution)/shard_map/ppermute | solution.py:54
  121.7 1.6 collective-permute-done.29.refs_3_
  123.3 0.3 shard_map.64
  123.6 2.1 %collective-permute-start.30 = (bf16[64,1280]{1,0:T(8,128)(2,1)S(1)}, bf16[64,1280]{1,0:T(8,128)(2,1)S(1)}, u32[]{:S(2)}, u32[]{:S(2)}) collective-permute-start(bf16[64,1280]{1,0:T(8,128)(2,1)S(1)} %get-tuple-element.34), channel_id=1, source_target_pairs={{0,2},{1,3},{2,0},{3,1},{4,6},{5,7},{6,4},{7,5},{8,10},{9,11},{10,... | collective-permute-start | bytes 491528 | tf_op jit(solution)/shard_map/ppermute | solution.py:31
  125.7 3.2 %collective-permute-start.31 = (bf16[64,1280]{1,0:T(8,128)(2,1)S(1)}, bf16[64,1280]{1,0:T(8,128)(2,1)S(1)}, u32[]{:S(2)}, u32[]{:S(2)}) collective-permute-start(bf16[64,1280]{1,0:T(8,128)(2,1)S(1)} %get-tuple-element.35), channel_id=1, source_target_pairs={{0,3},{1,0},{2,1},{3,2},{4,7},{5,4},{6,5},{7,6},{8,11},{9,8},{10,9... | collective-permute-start | bytes 491528 | tf_op jit(solution)/shard_map/ppermute | solution.py:31
  129.1 3.4 %collective-permute-start.37 = (bf16[64,1280]{1,0:T(8,128)(2,1)S(1)}, bf16[64,1280]{1,0:T(8,128)(2,1)S(1)}, u32[]{:S(2)}, u32[]{:S(2)}) collective-permute-start(bf16[64,1280]{1,0:T(8,128)(2,1)S(1)} %get-tuple-element.44), channel_id=1, source_target_pairs={{0,16},{64,80},{128,144},{192,208},{16,0},{80,64},{144,128},{208,1... | collective-permute-start | bytes 491528 | tf_op jit(solution)/shard_map/ppermute | solution.py:44
  132.4 1.8 %collective-permute-start.21 = (f32[8,128]{1,0:T(8,128)S(1)}, f32[8,128]{1,0:T(8,128)S(1)}, u32[]{:S(2)}, u32[]{:S(2)}) collective-permute-start(f32[8,128]{1,0:T(8,128)S(1)} %fusion.8), channel_id=1, source_target_pairs={{0,8},{4,12},{8,0},{12,4},{1,9},{5,13},{9,1},{13,5},{2,10},{6,14},... | collective-permute-start | bytes 12296 | tf_op jit(solution)/shard_map/ppermute | solution.py:54
  134.3 3.3 %collective-permute-done.21 = f32[8,128]{1,0:T(8,128)S(1)} collective-permute-done((f32[8,128]{1,0:T(8,128)S(1)}, f32[8,128]{1,0:T(8,128)S(1)}, u32[]{:S(2)}, u32[]{:S(2)}) %collective-permute-start.21) | collective-permute-done | bytes 4128 | tf_op jit(solution)/shard_map/ppermute | solution.py:54
  137.6 0.4 collective-permute-start.22
  137.9 3.2 %collective-permute-done.22 = f32[8,128]{1,0:T(8,128)S(1)} collective-permute-done((f32[8,128]{1,0:T(8,128)S(1)}, f32[8,128]{1,0:T(8,128)S(1)}, u32[]{:S(2)}, u32[]{:S(2)}) %collective-permute-start.22) | collective-permute-done | bytes 4128 | tf_op jit(solution)/shard_map/ppermute | solution.py:54
  141.2 2.7 %collective-permute-start.23 = (f32[8,128]{1,0:T(8,128)S(1)}, f32[8,128]{1,0:T(8,128)S(1)}, u32[]{:S(2)}, u32[]{:S(2)}) collective-permute-start(f32[8,128]{1,0:T(8,128)S(1)} %add.95), channel_id=1, source_target_pairs={{0,16},{64,80},{128,144},{192,208},{16,0},{80,64},{144,128},{208,1... | collective-permute-start | bytes 12296 | tf_op jit(solution)/shard_map/ppermute | solution.py:53
  143.8 4.9 %collective-permute-done.23 = f32[8,128]{1,0:T(8,128)S(1)} collective-permute-done((f32[8,128]{1,0:T(8,128)S(1)}, f32[8,128]{1,0:T(8,128)S(1)}, u32[]{:S(2)}, u32[]{:S(2)}) %collective-permute-start.23) | collective-permute-done | bytes 4128 | tf_op jit(solution)/shard_map/ppermute | solution.py:53
  148.7 0.9 collective-permute-start.24
  149.5 3.6 %collective-permute-done.24 = f32[8,128]{1,0:T(8,128)S(1)} collective-permute-done((f32[8,128]{1,0:T(8,128)S(1)}, f32[8,128]{1,0:T(8,128)S(1)}, u32[]{:S(2)}, u32[]{:S(2)}) %collective-permute-start.24) | collective-permute-done | bytes 4128 | tf_op jit(solution)/shard_map/ppermute | solution.py:53
  153.2 2.0 %collective-permute-start.25 = (f32[8,128]{1,0:T(8,128)S(1)}, f32[8,128]{1,0:T(8,128)S(1)}, u32[]{:S(2)}, u32[]{:S(2)}) collective-permute-start(f32[8,128]{1,0:T(8,128)S(1)} %add.97), channel_id=1, source_target_pairs={{0,64},{64,0},{128,192},{192,128},{16,80},{80,16},{144,208},{208,1... | collective-permute-start | bytes 12296 | tf_op jit(solution)/shard_map/ppermute | solution.py:53
  155.2 1.6 collective-permute-done.25
  156.8 1.2 collective-permute-done.26
  158.0 0.5 slice.7
  159.2 0.8 shard_map.65
  159.9 0.7 shard_map.69
  (48 shorter events, 1.1 us)
Async XLA Ops:
  0.6 14.1 %collective-permute-start.6 = (bf16[64,1280]{1,0:T(8,128)(2,1)}, bf16[64,1280]{1,0:T(8,128)(2,1)S(1)}, u32[]{:S(2)}, u32[]{:S(2)}) collective-permute-start(bf16[64,1280]{1,0:T(8,128)(2,1)} %refs_0_.3), channel_id=1, source_target_pairs={{0,16},{64,80},{128,144},{192,208},{16,0},{80,64},{144,128},{208,1... | collective-permute-start | bytes 491528 | tf_op jit(solution)/shard_map/ppermute | solution.py:44
  14.7 0.9 copy-start
  15.6 10.8 %collective-permute-start.7 = (bf16[128,1280]{1,0:T(8,128)(2,1)S(1)}, bf16[128,1280]{1,0:T(8,128)(2,1)S(1)}, u32[]{:S(2)}, u32[]{:S(2)}) collective-permute-start(bf16[128,1280]{1,0:T(8,128)(2,1)S(1)} %shard_map.59.refs_0_), channel_id=1, source_target_pairs={{0,144},{64,208},{128,0},{192,64},{16,128},{80,192},{144,16},{208,... | collective-permute-start | bytes 983048 | tf_op jit(solution)/shard_map/ppermute | solution.py:44
  26.5 18.3 %collective-permute-start.8 = (bf16[256,1280]{1,0:T(8,128)(2,1)S(1)}, bf16[256,1280]{1,0:T(8,128)(2,1)S(1)}, u32[]{:S(2)}, u32[]{:S(2)}) collective-permute-start(bf16[256,1280]{1,0:T(8,128)(2,1)S(1)} %shard_map.60.refs_4_.refs_0_), channel_id=1, source_target_pairs={{0,208},{64,0},{128,64},{192,128},{16,192},{80,16},{144,80},{208,1... | collective-permute-start | bytes 1966088 | tf_op jit(solution)/shard_map/ppermute | solution.py:44
  29.4 7.0 %collective-permute-start.1 = (bf16[64,1280]{1,0:T(8,128)(2,1)}, bf16[64,1280]{1,0:T(8,128)(2,1)S(1)}, u32[]{:S(2)}, u32[]{:S(2)}) collective-permute-start(bf16[64,1280]{1,0:T(8,128)(2,1)} %refs_0_.2), channel_id=1, source_target_pairs={{0,2},{1,3},{2,0},{3,1},{4,6},{5,7},{6,4},{7,5},{8,10},{9,11},{10,... | collective-permute-start | bytes 491528 | tf_op jit(solution)/shard_map/ppermute | solution.py:31
  32.4 6.7 %collective-permute-start = (bf16[64,1280]{1,0:T(8,128)(2,1)}, bf16[64,1280]{1,0:T(8,128)(2,1)S(1)}, u32[]{:S(2)}, u32[]{:S(2)}) collective-permute-start(bf16[64,1280]{1,0:T(8,128)(2,1)} %refs_0_.2), channel_id=1, source_target_pairs={{0,1},{1,2},{2,3},{3,0},{4,5},{5,6},{6,7},{7,4},{8,9},{9,10},{10,1... | collective-permute-start | bytes 491528 | tf_op jit(solution)/shard_map/ppermute | solution.py:31
  33.0 6.2 %collective-permute-start.2 = (bf16[64,1280]{1,0:T(8,128)(2,1)}, bf16[64,1280]{1,0:T(8,128)(2,1)S(1)}, u32[]{:S(2)}, u32[]{:S(2)}) collective-permute-start(bf16[64,1280]{1,0:T(8,128)(2,1)} %refs_0_.2), channel_id=1, source_target_pairs={{0,3},{1,0},{2,1},{3,2},{4,7},{5,4},{6,5},{7,6},{8,11},{9,8},{10,9... | collective-permute-start | bytes 491528 | tf_op jit(solution)/shard_map/ppermute | solution.py:31
  39.1 0.9 copy-start.1
  40.1 18.2 %collective-permute-start.5 = (bf16[256,1280]{1,0:T(8,128)(2,1)S(1)}, bf16[256,1280]{1,0:T(8,128)(2,1)}, u32[]{:S(2)}, u32[]{:S(2)}) collective-permute-start(bf16[256,1280]{1,0:T(8,128)(2,1)S(1)} %shard_map.58.refs_0_), channel_id=1, source_target_pairs={{0,12},{1,13},{2,14},{3,15},{4,0},{5,1},{6,2},{7,3},{8,4},{9,5},{1... | collective-permute-start | bytes 1966088 | tf_op jit(solution)/shard_map/ppermute | solution.py:31
  43.2 15.1 %collective-permute-start.4 = (bf16[256,1280]{1,0:T(8,128)(2,1)S(1)}, bf16[256,1280]{1,0:T(8,128)(2,1)}, u32[]{:S(2)}, u32[]{:S(2)}) collective-permute-start(bf16[256,1280]{1,0:T(8,128)(2,1)S(1)} %shard_map.58.refs_0_), channel_id=1, source_target_pairs={{0,8},{1,9},{2,10},{3,11},{4,12},{5,13},{6,14},{7,15},{8,0},{9,1},... | collective-permute-start | bytes 1966088 | tf_op jit(solution)/shard_map/ppermute | solution.py:31
  43.8 18.6 %collective-permute-start.3 = (bf16[256,1280]{1,0:T(8,128)(2,1)S(1)}, bf16[256,1280]{1,0:T(8,128)(2,1)}, u32[]{:S(2)}, u32[]{:S(2)}) collective-permute-start(bf16[256,1280]{1,0:T(8,128)(2,1)S(1)} %shard_map.58.refs_0_), channel_id=1, source_target_pairs={{0,4},{1,5},{2,6},{3,7},{4,8},{5,9},{6,10},{7,11},{8,12},{9,13},{1... | collective-permute-start | bytes 1966088 | tf_op jit(solution)/shard_map/ppermute | solution.py:31
  44.8 17.6 %collective-permute-start.9 = (bf16[256,1280]{1,0:T(8,128)(2,1)S(1)}, bf16[256,1280]{1,0:T(8,128)(2,1)S(1)}, u32[]{:S(2)}, u32[]{:S(2)}) collective-permute-start(bf16[256,1280]{1,0:T(8,128)(2,1)S(1)} %shard_map.60.refs_4_.refs_0_), channel_id=1, source_target_pairs={{0,32},{32,0},{1,33},{33,1},{2,34},{34,2},{3,35},{35,3},{4,36},{36... | collective-permute-start | bytes 1966088 | tf_op jit(solution)/shard_map/ppermute | solution.py:48
  44.8 17.6 %collective-permute-start.10 = (bf16[256,1280]{1,0:T(8,128)(2,1)S(1)}, bf16[256,1280]{1,0:T(8,128)(2,1)S(1)}, u32[]{:S(2)}, u32[]{:S(2)}) collective-permute-start(bf16[256,1280]{1,0:T(8,128)(2,1)S(1)} %collective-permute-done.8.refs_5_.refs_1_), channel_id=1, source_target_pairs={{0,32},{32,0},{1,33},{33,1},{2,34},{34,2},{3,35},{35,3},{4,36},{36... | collective-permute-start | bytes 1966088 | tf_op jit(solution)/shard_map/ppermute | solution.py:48
  68.3 5.4 %collective-permute-start.11 = (f32[16,128]{1,0:T(8,128)S(1)}, f32[16,128]{1,0:T(8,128)S(1)}, u32[]{:S(2)}, u32[]{:S(2)}) collective-permute-start(f32[16,128]{1,0:T(8,128)S(1)} %get-tuple-element.24), channel_id=1, source_target_pairs={{0,2},{1,3},{2,0},{3,1},{4,6},{5,7},{6,4},{7,5},{8,10},{9,11},{10,... | collective-permute-start | bytes 24584 | tf_op jit(solution)/shard_map/ppermute | solution.py:54
  69.8 7.6 %collective-permute-start.15 = (f32[16,128]{1,0:T(8,128)S(1)}, f32[16,128]{1,0:T(8,128)S(1)}, u32[]{:S(2)}, u32[]{:S(2)}) collective-permute-start(f32[16,128]{1,0:T(8,128)S(1)} %get-tuple-element.25), channel_id=1, source_target_pairs={{0,16},{64,80},{128,144},{192,208},{16,0},{80,64},{144,128},{208,1... | collective-permute-start | bytes 24584 | tf_op jit(solution)/shard_map/ppermute | solution.py:53
  73.7 6.1 %collective-permute-start.12 = (f32[16,128]{1,0:T(8,128)S(1)}, f32[16,128]{1,0:T(8,128)S(1)}, u32[]{:S(2)}, u32[]{:S(2)}) collective-permute-start(f32[16,128]{1,0:T(8,128)S(1)} %log_add_fusion.7), channel_id=1, source_target_pairs={{0,1},{1,0},{2,3},{3,2},{4,5},{5,4},{6,7},{7,6},{8,9},{9,8},{10,11... | collective-permute-start | bytes 24584 | tf_op jit(solution)/shard_map/ppermute | solution.py:54
  77.4 4.6 %collective-permute-start.16 = (f32[16,128]{1,0:T(8,128)S(1)}, f32[16,128]{1,0:T(8,128)S(1)}, u32[]{:S(2)}, u32[]{:S(2)}) collective-permute-start(f32[16,128]{1,0:T(8,128)S(1)} %log_add_fusion.3), channel_id=1, source_target_pairs={{0,128},{64,192},{128,0},{192,64},{16,144},{80,208},{144,16},{208,... | collective-permute-start | bytes 24584 | tf_op jit(solution)/shard_map/ppermute | solution.py:53
  79.8 5.2 %collective-permute-start.13 = (f32[16,128]{1,0:T(8,128)S(1)}, f32[16,128]{1,0:T(8,128)S(1)}, u32[]{:S(2)}, u32[]{:S(2)}) collective-permute-start(f32[16,128]{1,0:T(8,128)S(1)} %log_add_fusion.6), channel_id=1, source_target_pairs={{0,8},{4,12},{8,0},{12,4},{1,9},{5,13},{9,1},{13,5},{2,10},{6,14},... | collective-permute-start | bytes 24584 | tf_op jit(solution)/shard_map/ppermute | solution.py:54
  82.0 4.1 %collective-permute-start.17 = (f32[16,128]{1,0:T(8,128)S(1)}, f32[16,128]{1,0:T(8,128)S(1)}, u32[]{:S(2)}, u32[]{:S(2)}) collective-permute-start(f32[16,128]{1,0:T(8,128)S(1)} %log_add_fusion.2), channel_id=1, source_target_pairs={{0,64},{64,0},{128,192},{192,128},{16,80},{80,16},{144,208},{208,1... | collective-permute-start | bytes 24584 | tf_op jit(solution)/shard_map/ppermute | solution.py:53
  85.1 3.7 %collective-permute-start.14 = (f32[16,128]{1,0:T(8,128)S(1)}, f32[16,128]{1,0:T(8,128)S(1)}, u32[]{:S(2)}, u32[]{:S(2)}) collective-permute-start(f32[16,128]{1,0:T(8,128)S(1)} %log_add_fusion.5), channel_id=1, source_target_pairs={{0,4},{4,0},{8,12},{12,8},{1,5},{5,1},{9,13},{13,9},{2,6},{6,2},{1... | collective-permute-start | bytes 24584 | tf_op jit(solution)/shard_map/ppermute | solution.py:54
  86.2 2.6 %collective-permute-start.18 = (f32[16,128]{1,0:T(8,128)S(1)}, f32[16,128]{1,0:T(8,128)S(1)}, u32[]{:S(2)}, u32[]{:S(2)}) collective-permute-start(f32[16,128]{1,0:T(8,128)S(1)} %log_add_fusion.1), channel_id=1, source_target_pairs={{0,32},{32,0},{1,33},{33,1},{2,34},{34,2},{3,35},{35,3},{4,36},{36... | collective-permute-start | bytes 24584 | tf_op jit(solution)/shard_map/ppermute | solution.py:54
  96.5 2.2 %collective-permute-start.34 = (bf16[256,1280]{1,0:T(8,128)(2,1)S(1)}, bf16[256,1280]{1,0:T(8,128)(2,1)S(1)}, u32[]{:S(2)}, u32[]{:S(2)}) collective-permute-start(bf16[256,1280]{1,0:T(8,128)(2,1)S(1)} %get-tuple-element.40), channel_id=1, source_target_pairs={{0,32},{32,0},{1,33},{33,1},{2,34},{34,2},{3,35},{35,3},{4,36},{36... | collective-permute-start | bytes 1966088 | tf_op jit(solution)/shard_map/ppermute | solution.py:48
  96.6 10.1 %collective-permute-start.33 = (bf16[256,1280]{1,0:T(8,128)(2,1)S(1)}, bf16[256,1280]{1,0:T(8,128)(2,1)S(1)}, u32[]{:S(2)}, u32[]{:S(2)}) collective-permute-start(bf16[256,1280]{1,0:T(8,128)(2,1)S(1)} %get-tuple-element.38), channel_id=1, source_target_pairs={{0,32},{32,0},{1,33},{33,1},{2,34},{34,2},{3,35},{35,3},{4,36},{36... | collective-permute-start | bytes 1966088 | tf_op jit(solution)/shard_map/ppermute | solution.py:48
  98.9 10.9 %collective-permute-start.35 = (bf16[256,1280]{1,0:T(8,128)(2,1)S(1)}, bf16[256,1280]{1,0:T(8,128)(2,1)S(1)}, u32[]{:S(2)}, u32[]{:S(2)}) collective-permute-start(bf16[256,1280]{1,0:T(8,128)(2,1)S(1)} %shard_map.66), channel_id=1, source_target_pairs={{0,64},{64,128},{128,192},{192,16},{16,80},{80,144},{144,208},{208... | collective-permute-start | bytes 1966088 | tf_op jit(solution)/shard_map/ppermute | solution.py:44
  104.0 17.7 %collective-permute-start.27 = (bf16[256,1280]{1,0:T(8,128)(2,1)}, bf16[256,1280]{1,0:T(8,128)(2,1)S(1)}, u32[]{:S(2)}, u32[]{:S(2)}) collective-permute-start(bf16[256,1280]{1,0:T(8,128)(2,1)} %get-tuple-element.30), channel_id=1, source_target_pairs={{0,8},{1,9},{2,10},{3,11},{4,12},{5,13},{6,14},{7,15},{8,0},{9,1},... | collective-permute-start | bytes 1966088 | tf_op jit(solution)/shard_map/ppermute | solution.py:31
  104.6 17.1 %collective-permute-start.28 = (bf16[256,1280]{1,0:T(8,128)(2,1)}, bf16[256,1280]{1,0:T(8,128)(2,1)S(1)}, u32[]{:S(2)}, u32[]{:S(2)}) collective-permute-start(bf16[256,1280]{1,0:T(8,128)(2,1)} %get-tuple-element.31), channel_id=1, source_target_pairs={{0,12},{1,13},{2,14},{3,15},{4,0},{5,1},{6,2},{7,3},{8,4},{9,5},{1... | collective-permute-start | bytes 1966088 | tf_op jit(solution)/shard_map/ppermute | solution.py:31
  106.7 16.6 %collective-permute-start.29 = (bf16[256,1280]{1,0:T(8,128)(2,1)}, bf16[256,1280]{1,0:T(8,128)(2,1)S(1)}, u32[]{:S(2)}, u32[]{:S(2)}) collective-permute-start(bf16[256,1280]{1,0:T(8,128)(2,1)} %get-tuple-element.32), channel_id=1, source_target_pairs={{0,4},{1,5},{2,6},{3,7},{4,8},{5,9},{6,10},{7,11},{8,12},{9,13},{1... | collective-permute-start | bytes 1966088 | tf_op jit(solution)/shard_map/ppermute | solution.py:31
  110.6 18.4 %collective-permute-start.36 = (bf16[128,1280]{1,0:T(8,128)(2,1)}, bf16[128,1280]{1,0:T(8,128)(2,1)S(1)}, u32[]{:S(2)}, u32[]{:S(2)}) collective-permute-start(bf16[128,1280]{1,0:T(8,128)(2,1)} %get-tuple-element.42), channel_id=1, source_target_pairs={{0,128},{64,192},{128,16},{192,80},{16,144},{80,208},{144,0},{208,... | collective-permute-start | bytes 983048 | tf_op jit(solution)/shard_map/ppermute | solution.py:44
  114.0 5.3 %collective-permute-start.19 = (f32[8,128]{1,0:T(8,128)S(1)}, f32[8,128]{1,0:T(8,128)S(1)}, u32[]{:S(2)}, u32[]{:S(2)}) collective-permute-start(f32[8,128]{1,0:T(8,128)S(1)} %broadcast_in_dim.8), channel_id=1, source_target_pairs={{0,2},{1,3},{2,0},{3,1},{4,6},{5,7},{6,4},{7,5},{8,10},{9,11},{10,... | collective-permute-start | bytes 12296 | tf_op jit(solution)/shard_map/ppermute | solution.py:54
  119.3 13.2 %collective-permute-start.20 = (f32[8,128]{1,0:T(8,128)S(1)}, f32[8,128]{1,0:T(8,128)S(1)}, u32[]{:S(2)}, u32[]{:S(2)}) collective-permute-start(f32[8,128]{1,0:T(8,128)S(1)} %broadcast_add_fusion), channel_id=1, source_target_pairs={{0,1},{1,0},{2,3},{3,2},{4,5},{5,4},{6,7},{7,6},{8,9},{9,8},{10,11... | collective-permute-start | bytes 12296 | tf_op jit(solution)/shard_map/ppermute | solution.py:54
  123.6 35.5 %collective-permute-start.30 = (bf16[64,1280]{1,0:T(8,128)(2,1)S(1)}, bf16[64,1280]{1,0:T(8,128)(2,1)S(1)}, u32[]{:S(2)}, u32[]{:S(2)}) collective-permute-start(bf16[64,1280]{1,0:T(8,128)(2,1)S(1)} %get-tuple-element.34), channel_id=1, source_target_pairs={{0,2},{1,3},{2,0},{3,1},{4,6},{5,7},{6,4},{7,5},{8,10},{9,11},{10,... | collective-permute-start | bytes 491528 | tf_op jit(solution)/shard_map/ppermute | solution.py:31
  125.7 33.4 %collective-permute-start.31 = (bf16[64,1280]{1,0:T(8,128)(2,1)S(1)}, bf16[64,1280]{1,0:T(8,128)(2,1)S(1)}, u32[]{:S(2)}, u32[]{:S(2)}) collective-permute-start(bf16[64,1280]{1,0:T(8,128)(2,1)S(1)} %get-tuple-element.35), channel_id=1, source_target_pairs={{0,3},{1,0},{2,1},{3,2},{4,7},{5,4},{6,5},{7,6},{8,11},{9,8},{10,9... | collective-permute-start | bytes 491528 | tf_op jit(solution)/shard_map/ppermute | solution.py:31
  129.0 30.2 %collective-permute-start.32 = (bf16[64,1280]{1,0:T(8,128)(2,1)S(1)}, bf16[64,1280]{1,0:T(8,128)(2,1)S(1)}, u32[]{:S(2)}, u32[]{:S(2)}) collective-permute-start(bf16[64,1280]{1,0:T(8,128)(2,1)S(1)} %get-tuple-element.36), channel_id=1, source_target_pairs={{0,1},{1,2},{2,3},{3,0},{4,5},{5,6},{6,7},{7,4},{8,9},{9,10},{10,1... | collective-permute-start | bytes 491528 | tf_op jit(solution)/shard_map/ppermute | solution.py:31
  129.1 30.9 %collective-permute-start.37 = (bf16[64,1280]{1,0:T(8,128)(2,1)S(1)}, bf16[64,1280]{1,0:T(8,128)(2,1)S(1)}, u32[]{:S(2)}, u32[]{:S(2)}) collective-permute-start(bf16[64,1280]{1,0:T(8,128)(2,1)S(1)} %get-tuple-element.44), channel_id=1, source_target_pairs={{0,16},{64,80},{128,144},{192,208},{16,0},{80,64},{144,128},{208,1... | collective-permute-start | bytes 491528 | tf_op jit(solution)/shard_map/ppermute | solution.py:44
  132.4 5.1 %collective-permute-start.21 = (f32[8,128]{1,0:T(8,128)S(1)}, f32[8,128]{1,0:T(8,128)S(1)}, u32[]{:S(2)}, u32[]{:S(2)}) collective-permute-start(f32[8,128]{1,0:T(8,128)S(1)} %fusion.8), channel_id=1, source_target_pairs={{0,8},{4,12},{8,0},{12,4},{1,9},{5,13},{9,1},{13,5},{2,10},{6,14},... | collective-permute-start | bytes 12296 | tf_op jit(solution)/shard_map/ppermute | solution.py:54
  137.6 3.6 %collective-permute-start.22 = (f32[8,128]{1,0:T(8,128)S(1)}, f32[8,128]{1,0:T(8,128)S(1)}, u32[]{:S(2)}, u32[]{:S(2)}) collective-permute-start(f32[8,128]{1,0:T(8,128)S(1)} %add.94), channel_id=1, source_target_pairs={{0,4},{4,0},{8,12},{12,8},{1,5},{5,1},{9,13},{13,9},{2,6},{6,2},{1... | collective-permute-start | bytes 12296 | tf_op jit(solution)/shard_map/ppermute | solution.py:54
  141.2 7.5 %collective-permute-start.23 = (f32[8,128]{1,0:T(8,128)S(1)}, f32[8,128]{1,0:T(8,128)S(1)}, u32[]{:S(2)}, u32[]{:S(2)}) collective-permute-start(f32[8,128]{1,0:T(8,128)S(1)} %add.95), channel_id=1, source_target_pairs={{0,16},{64,80},{128,144},{192,208},{16,0},{80,64},{144,128},{208,1... | collective-permute-start | bytes 12296 | tf_op jit(solution)/shard_map/ppermute | solution.py:53
  148.7 4.5 %collective-permute-start.24 = (f32[8,128]{1,0:T(8,128)S(1)}, f32[8,128]{1,0:T(8,128)S(1)}, u32[]{:S(2)}, u32[]{:S(2)}) collective-permute-start(f32[8,128]{1,0:T(8,128)S(1)} %add.96), channel_id=1, source_target_pairs={{0,128},{64,192},{128,0},{192,64},{16,144},{80,208},{144,16},{208,... | collective-permute-start | bytes 12296 | tf_op jit(solution)/shard_map/ppermute | solution.py:53
  153.2 3.6 %collective-permute-start.25 = (f32[8,128]{1,0:T(8,128)S(1)}, f32[8,128]{1,0:T(8,128)S(1)}, u32[]{:S(2)}, u32[]{:S(2)}) collective-permute-start(f32[8,128]{1,0:T(8,128)S(1)} %add.97), channel_id=1, source_target_pairs={{0,64},{64,0},{128,192},{192,128},{16,80},{80,16},{144,208},{208,1... | collective-permute-start | bytes 12296 | tf_op jit(solution)/shard_map/ppermute | solution.py:53
  156.8 1.2 collective-permute-start.26

commit v2 on v1

--- a/solution.py
+++ b/solution.py
@@ -31,10 +31,6 @@
     return lax.ppermute(v, ("core", "zh", "y", "x"), pairs)
 
 
-def z_index(z):
-    return (z % 4) * 2 + z // 4
-
-
 def z_shift(v, k):
     pairs = []
     for c in range(2):
@@ -48,15 +44,39 @@
     return lax.ppermute(v, "core", [(0, 1), (1, 0)])
 
 
-def flip(v, axis, bit):
-    if axis == "z":
-        return lax.ppermute(v, ("zl", "zh"), [(z_index(i), z_index(i ^ bit)) for i in range(NZ)])
-    return lax.ppermute(v, axis, [(i, i ^ bit) for i in range(lax.axis_size(axis))])
-
-
-def lse2(a, b):
-    top = jnp.maximum(a, b)
-    return top + jnp.log(jnp.exp(a - top) + jnp.exp(b - top))
+def split_move(v, to_0, to_1):
+    pairs = []
+    for c, to in ((0, to_0), (1, to_1)):
+        if to is None:
+            continue
+        for z in range(NZ):
+            for y in range(NY):
+                for x in range(NX):
+                    ty, tx, tz = to(y, x, z)
+                    pairs.append((device(c, y, x, z), device(c, ty % NY, tx % NX, tz % NZ)))
+    return lax.ppermute(v, AXES, pairs)
+
+
+def device(c, y, x, z):
+    return ((((z % 4) * 2 + c) * 2 + z // 4) * NY + y) * NX + x
+
+
+def lse(parts):
+    top = parts[0]
+    for p in parts[1:]:
+        top = jnp.maximum(top, p)
+    return top + jnp.log(sum(jnp.exp(p - top) for p in parts))
+
+
+def in_order(parts, at):
+    out = []
+    for i in range(4):
+        k = (at - i) & 3
+        v = parts[3]
+        for n in (2, 1, 0):
+            v = jnp.where(k == n, parts[n], v)
+        out.append(v)
+    return out
 
 
 def row_place(where, a, b):
@@ -90,20 +110,24 @@
     return out
 
 
-def pack_body(n, *refs):
+def pack_body(counts, *refs):
     at = 0
-    for r in refs[:n]:
-        refs[n][at : at + r.shape[0], :] = r[...]
-        at += r.shape[0]
-
-
-def pack(*parts):
-    rows = sum(p.shape[0] for p in parts)
+    for n, out in zip(counts, refs[sum(counts) :]):
+        row = 0
+        for r in refs[at : at + n]:
+            out[row : row + r.shape[0], :] = r[...]
+            row += r.shape[0]
+        at += n
+
+
+def pack(*groups):
+    parts = [p for g in groups for p in g]
+    shapes = [jax.ShapeDtypeStruct((sum(p.shape[0] for p in g), EMBED), BF16) for g in groups]
     return pl.pallas_call(
-        lambda *refs: pack_body(len(parts), *refs),
-        out_shape=jax.ShapeDtypeStruct((rows, EMBED), BF16),
+        lambda *refs: pack_body([len(g) for g in groups], *refs),
+        out_shape=tuple(shapes),
         in_specs=[VMEM] * len(parts),
-        out_specs=VMEM,
+        out_specs=(VMEM,) * len(groups),
         compiler_params=PARAMS,
     )(*parts)
 
@@ -185,11 +209,11 @@
     )(place, scale, *images, *texts)
 
 
-def text_body(place, scale, logits, row_lse, col_lse, *refs):
+def weights_body(place, scale, logits, row_lse, col_lse, *refs):
     images = refs[:4]
     weights = refs[4]
-    outs = refs[5:9]
-    row_wide = refs[9]
+    outs = refs[5:7]
+    row_wide = refs[7]
     where = [place[i] for i in range(5)]
     multiplier = scale[0]
     lane = lax.broadcasted_iota(jnp.int32, (1, 128), 1)
@@ -214,7 +238,11 @@
                 both = 0.5 * jnp.exp(tile - wide) + 0.5 * jnp.exp(tile - col_line[t])
                 both = both - jnp.where(ids[b] == cols[t][0:1], 1.0, 0.0)
                 weights[at : at + ROWS, t * 128 : (t + 1) * 128] = both.astype(BF16)
-    for j in (3, 2, 1, 0):
+    text_terms(multiplier, weights, images, {1: outs[0], 3: outs[1]})
+
+
+def text_terms(multiplier, weights, images, outs):
+    for j, out in outs.items():
         for e in range(5):
             acc = None
             for a in range(4):
@@ -225,25 +253,11 @@
                     preferred_element_type=F32,
                 )
                 acc = term if acc is None else acc + term
-            outs[j][:, e * 256 : (e + 1) * 256] = (multiplier * acc).astype(BF16)
-
-
-def text_call(place, scale, logits, row_lse, col_lse, images):
-    part = jax.ShapeDtypeStruct((CHUNK, EMBED), BF16)
-    return pl.pallas_call(
-        text_body,
-        out_shape=(jax.ShapeDtypeStruct((BLOCK, BLOCK), BF16), part, part, part, part),
-        in_specs=[SMEM, SMEM] + [VMEM] * 7,
-        out_specs=(VMEM,) * 5,
-        scratch_shapes=[pltpu.VMEM((BLOCK, 128), F32)],
-        compiler_params=PARAMS,
-    )(place, scale, logits, row_lse, col_lse, *images)
-
-
-def image_body(scale, weights, *refs):
-    texts, outs = refs[:4], refs[4:]
-    multiplier = scale[0]
-    for a in (2, 1, 3, 0):
+            out[:, e * 256 : (e + 1) * 256] = (multiplier * acc).astype(BF16)
+
+
+def image_terms(multiplier, weights, texts, outs):
+    for a, out in outs.items():
         for e in range(5):
             acc = None
             for j in range(4):
@@ -253,18 +267,51 @@
                     preferred_element_type=F32,
                 )
                 acc = term if acc is None else acc + term
-            outs[a][:, e * 256 : (e + 1) * 256] = (multiplier * acc).astype(BF16)
+            out[:, e * 256 : (e + 1) * 256] = (multiplier * acc).astype(BF16)
+
+
+PART = jax.ShapeDtypeStruct((CHUNK, EMBED), BF16)
+
+
+def weights_call(place, scale, logits, row_lse, col_lse, images):
+    return pl.pallas_call(
+        weights_body,
+        out_shape=(jax.ShapeDtypeStruct((BLOCK, BLOCK), BF16), PART, PART),
+        in_specs=[SMEM, SMEM] + [VMEM] * 7,
+        out_specs=(VMEM,) * 3,
+        scratch_shapes=[pltpu.VMEM((BLOCK, 128), F32)],
+        compiler_params=PARAMS,
+    )(place, scale, logits, row_lse, col_lse, *images)
+
+
+def image_body(scale, weights, *refs):
+    image_terms(scale[0], weights, refs[:4], dict(zip((2, 1, 3), refs[4:])))
 
 
 def image_call(scale, weights, texts):
-    part = jax.ShapeDtypeStruct((CHUNK, EMBED), BF16)
     return pl.pallas_call(
         image_body,
-        out_shape=(part,) * 4,
+        out_shape=(PART,) * 3,
         in_specs=[SMEM] + [VMEM] * 5,
-        out_specs=(VMEM,) * 4,
+        out_specs=(VMEM,) * 3,
         compiler_params=PARAMS,
     )(scale, weights, *texts)
+
+
+def rest_body(scale, weights, *refs):
+    images, texts, outs = refs[:4], refs[4:8], refs[8:]
+    text_terms(scale[0], weights, images, {2: outs[1], 0: outs[0]})
+    image_terms(scale[0], weights, texts, {0: outs[2]})
+
+
+def rest_call(scale, weights, images, texts):
+    return pl.pallas_call(
+        rest_body,
+        out_shape=(PART,) * 3,
+        in_specs=[SMEM] + [VMEM] * 9,
+        out_specs=(VMEM,) * 3,
+        compiler_params=PARAMS,
+    )(scale, weights, *images, *texts)
 
 
 def add_body(n, *refs):
@@ -295,42 +342,70 @@
 
     far = z_shift(text_emb, 4)
     near = [plane_shift(image_emb, k, True) for k in (1, 2, 3)]
-    pair = pack(text_emb, far)
-    own = pack(image_emb, *near)
-    text_0 = pack(pair, z_shift(pair, -2))
+    pair, own = pack([text_emb, far], [image_emb] + near)
+    (text_0,) = pack([pair, z_shift(pair, -2)])
     images = [own] + [plane_shift(own, k, False) for k in (1, 2, 3)]
     text_1 = z_shift(text_0, -1)
     texts = [text_0, text_1, core_swap(text_0), core_swap(text_1)]
 
     logits, row_part, col_part, matched = logits_call(place, logit_scale, images, texts)
 
-    row_lse, col_lse = row_part, col_part
-    for axis, bit, col_axis, col_bit in (
-        ("x", 2, "z", 4),
-        ("x", 1, "z", 2),
-        ("y", 2, "z", 1),
-        ("y", 1, "core", 1),
-    ):
-        row_lse = lse2(row_lse, flip(row_lse, axis, bit))
-        col_lse = lse2(col_lse, flip(col_lse, col_axis, col_bit))
-
-    weights, *text_parts = text_call(place, logit_scale, logits, row_lse, col_lse, images)
-    back_1, back_0 = core_swap(text_parts[3]), core_swap(text_parts[2])
-    image_parts = image_call(logit_scale, weights, texts)
-
-    back = [plane_shift(image_parts[k], -k, False) for k in (2, 1, 3)]
-    t = z_shift(add([text_parts[1], back_1]), 1)
-    t_near, t_far = add([text_parts[0], back_0, t], pieces=2)
-    pieces = add([image_parts[0]] + back, pieces=4)
+    first = place[1] == 0
+    got = core_swap(jnp.concatenate([jnp.where(first, col_part, row_part), matched]))
+    rows_first = jnp.concatenate([row_part, got[:16]])
+    cols_first = jnp.concatenate([lse([col_part, got[:16]])] * 2)
+    state = jnp.where(first, rows_first, cols_first)
+    hits = matched + got[16:]
+
+    def join(parts, at):
+        parts = in_order(parts, at)
+        kept = lse([p[:32] for p in parts])
+        return jnp.concatenate([kept, parts[0][32:] + parts[1][32:] + (parts[2][32:] + parts[3][32:])])
+
+    state = jnp.concatenate([state, hits])
+    z = place[2] * 4 + place[0]
+    state = join(
+        [state]
+        + [
+            split_move(state, lambda y, x, z: (y, x + k, z), lambda y, x, z: (y, x, z + 2 * k))
+            for k in (1, 2, 3)
+        ],
+        jnp.where(first, place[4], z >> 1),
+    )
+    moved = [
+        split_move(
+            state, lambda y, x, z: (y + k, x, z), (lambda y, x, z: (y, x, z ^ 1)) if k == 1 else None
+        )
+        for k in (1, 2, 3)
+    ]
+    state = jnp.where(first, join([state] + moved, place[3]), jnp.concatenate([lse([state[:32], moved[0][:32]]), hits]))
+    got = core_swap(jnp.where(first, state[16:32], state[:16]))
+    row_lse = jnp.where(first, state[:16], got)
+    col_lse = jnp.where(first, got, state[:16])
+
+    weights, text_1_term, text_3_term = weights_call(place, logit_scale, logits, row_lse, col_lse, images)
+    back_1 = core_swap(text_3_term)
+    image_terms_far = image_call(logit_scale, weights, texts)
+    text_0_term, text_2_term, image_0_term = rest_call(logit_scale, weights, images, texts)
+    back_0 = core_swap(text_2_term)
+
+    back = [plane_shift(v, -k, False) for v, k in zip(image_terms_far, (2, 1, 3))]
+    t = z_shift(add([text_1_term, back_1]), 1)
+    t_near, t_far = add([text_0_term, back_0, t], pieces=2)
+    pieces = add([image_0_term] + back, pieces=4)
     t_near, t_far = add([t_near, z_shift(t_far, 2)], pieces=2)
     image_grad = add([pieces[0]] + [plane_shift(pieces[k], -k, True) for k in (2, 1, 3)])
     text_grad = add([t_near, z_shift(t_far, 4)])
 
     real = lax.broadcasted_iota(jnp.int32, (16, 128), 1) < ROWS
-    lses = jnp.sum(jnp.where(real, row_lse + col_lse, 0.0)) / 16.0
-    s = jnp.broadcast_to(lses - 2.0 * matched[0, 0], (8, 128))
-    for axis, bit in (("x", 2), ("x", 1), ("y", 2), ("y", 1), ("z", 4), ("z", 2), ("z", 1), ("core", 1)):
-        s = s + flip(s, axis, bit)
+    half = [jnp.sum(jnp.where(real, v, 0.0)) for v in (state[:16], state[16:32])]
+    share = jnp.where(first, half[0] + half[1] - 2.0 * state[32, 0], half[0])
+    s = jnp.broadcast_to(share, (8, 128))
+    s = s + split_move(s, lambda y, x, z: (y, x, z ^ 4), lambda y, x, z: (y, x ^ 2, z))
+    s = s + split_move(s, lambda y, x, z: (y, x, z ^ 2), lambda y, x, z: (y, x ^ 1, z))
+    s = s + split_move(s, lambda y, x, z: (y, x, z ^ 1), lambda y, x, z: (y ^ 2, x, z))
+    s = s + split_move(s, None, lambda y, x, z: (y ^ 1, x, z))
+    s = s + core_swap(s)
     mean_loss = s[0, :1] / (2.0 * ROWS * 256)
     return mean_loss, image_grad, text_grad
 

time: 165 us -> 146 us (0.88); the launches traced: 162 us -> 145 us
  waiting for transfers between devices: 66.7 us -> 52.4 us
  starting transfers between devices: 67.7 us -> 56.7 us
  local copies, waits for them, and re-layouts: 2.95 us -> 7.95 us
  Pallas kernels: 19.2 us -> 21.5 us
    ppermute x16 -> x10, waiting for transfers between devices: 26.1 us -> 17.8 us  [split_move(): return lax.ppermute(v, AXES, pairs)]
    ppermute x16 -> x10, starting transfers between devices: 27.6 us -> 19.6 us  [split_move(): return lax.ppermute(v, AXES, pairs)]
    ppermute x12, waiting for transfers between devices: 21.5 us -> 14.1 us  [plane_shift(): return lax.ppermute(v, ('core', 'zh', 'y', 'x'), pairs)]
    unnamed x4 -> x12, local copies, waits for them, and re-layouts: 1.83 us -> 6.83 us
    pallas_call x5, Pallas kernels: 10.4 us -> 12.8 us  [the longest x1 5.51 us: weights_call(): pl.pallas_call(weights_body, out_shape=(jax.ShapeDtypeStruct((BLOCK, BLOC...]
    ppermute x6, starting transfers between devices: 20 us -> 17.9 us  [z_shift(): return lax.ppermute(v, ('zl', 'core', 'zh'), pairs)]
    ppermute x4 -> x7, waiting for transfers between devices: 1.59 us -> 3.48 us  [core_swap(): return lax.ppermute(v, 'core', [(0, 1), (1, 0)])]
  transfers between devices with their start and end apart: 38 -> 35, of which waited for: 21 -> 16; matrix products, arithmetic and copies ran while one was open for 1% -> 1% of each run, Pallas kernels for 3% -> 6%
where the time goes in v2:
time: 146 us; the launch traced here: 145 us
  starting transfers between devices  56.7 us (39%)
  waiting for transfers between devices  52.4 us (36%)
  Pallas kernels  21.5 us (15%)
  local copies, waits for them, and re-layouts  7.95 us (5%)
  between operations  5.95 us (4%)
    ppermute x10, starting transfers between devices, split_move(): return lax.ppermute(v, AXES, pairs)  19.6 us
    ppermute x12, starting transfers between devices, plane_shift(): return lax.ppermute(v, ('core', 'zh', 'y', 'x'), pairs)  18.4 us
    ppermute x6, starting transfers between devices, z_shift(): return lax.ppermute(v, ('zl', 'core', 'zh'), pairs)  17.9 us
    ppermute x10, waiting for transfers between devices, split_move(): return lax.ppermute(v, AXES, pairs)  17.8 us
    ppermute x6, waiting for transfers between devices, z_shift(): return lax.ppermute(v, ('zl', 'core', 'zh'), pairs)  17 us
    ppermute x12, waiting for transfers between devices, plane_shift(): return lax.ppermute(v, ('core', 'zh', 'y', 'x'), pairs)  14.1 us
    unnamed x12, local copies, waits for them, and re-layouts  6.83 us
    pallas_call x1, Pallas kernels, logits_call(): pl.pallas_call(logits_body, out_shape=(jax.ShapeDtypeStruct((BLOCK, BLOCK...  5.85 us
  transfers between devices with their start and end apart: 35, of which 16 were waited for; matrix products, arithmetic and copies ran while one was open for 1% of the time, Pallas kernels for 6%

profile of v2, /device:TPU:32, one launch (start us, length us, event | category | flops | bytes accessed | tf_op | source)
XLA Modules:
  0.0 145.4 jit_solution(14911198859337389630)
XLA Ops:
  0.6 6.4 %collective-permute-start = (bf16[64,1280]{1,0:T(8,128)(2,1)}, bf16[64,1280]{1,0:T(8,128)(2,1)S(1)}, u32[]{:S(2)}, u32[]{:S(2)}) collective-permute-start(bf16[64,1280]{1,0:T(8,128)(2,1)} %refs_0_.1), channel_id=1, source_target_pairs={{0,16},{64,80},{128,144},{192,208},{16,0},{80,64},{144,128},{208,1... | collective-permute-start | bytes 491528 | tf_op jit(solution)/shard_map/ppermute | solution.py:40
  7.0 3.0 %collective-permute-start.2 = (bf16[64,1280]{1,0:T(8,128)(2,1)}, bf16[64,1280]{1,0:T(8,128)(2,1)S(1)}, u32[]{:S(2)}, u32[]{:S(2)}) collective-permute-start(bf16[64,1280]{1,0:T(8,128)(2,1)} %refs_2_.1), channel_id=1, source_target_pairs={{0,2},{1,3},{2,0},{3,1},{4,6},{5,7},{6,4},{7,5},{8,10},{9,11},{10,... | collective-permute-start | bytes 491528 | tf_op jit(solution)/shard_map/ppermute | solution.py:31
  10.0 0.6 collective-permute-start.1
  10.6 2.6 %collective-permute-start.3 = (bf16[64,1280]{1,0:T(8,128)(2,1)}, bf16[64,1280]{1,0:T(8,128)(2,1)S(1)}, u32[]{:S(2)}, u32[]{:S(2)}) collective-permute-start(bf16[64,1280]{1,0:T(8,128)(2,1)} %refs_2_.1), channel_id=1, source_target_pairs={{0,3},{1,0},{2,1},{3,2},{4,7},{5,4},{6,5},{7,6},{8,11},{9,8},{10,9... | collective-permute-start | bytes 491528 | tf_op jit(solution)/shard_map/ppermute | solution.py:31
  13.3 1.4 collective-permute-done.refs_1_
  14.7 2.1 %collective-permute-done.1.refs_3_ = bf16[64,1280]{1,0:T(8,128)(2,1)S(1)} collective-permute-done((bf16[64,1280]{1,0:T(8,128)(2,1)}, bf16[64,1280]{1,0:T(8,128)(2,1)S(1)}, u32[]{:S(2)}, u32[]{:S(2)}) %collective-permute-start.1) | collective-permute-done | bytes 163872 | tf_op jit(solution)/shard_map/ppermute | solution.py:31
  16.8 0.9 copy-done.4
  17.7 0.9 copy-done.5
  18.7 2.0 %collective-permute-start.7 = (bf16[128,1280]{1,0:T(8,128)(2,1)S(1)}, bf16[128,1280]{1,0:T(8,128)(2,1)S(1)}, u32[]{:S(2)}, u32[]{:S(2)}) collective-permute-start(bf16[128,1280]{1,0:T(8,128)(2,1)S(1)} %get-tuple-element.27.refs_0_), channel_id=1, source_target_pairs={{0,144},{64,208},{128,0},{192,64},{16,128},{80,192},{144,16},{208,... | collective-permute-start | bytes 983048 | tf_op jit(solution)/shard_map/ppermute | solution.py:40
  20.6 8.1 %collective-permute-done.7.refs_1_ = bf16[128,1280]{1,0:T(8,128)(2,1)S(1)} collective-permute-done((bf16[128,1280]{1,0:T(8,128)(2,1)S(1)}, bf16[128,1280]{1,0:T(8,128)(2,1)S(1)}, u32[]{:S(2)}, u32[]{:S(2)}) %collective-permute-start.7) | collective-permute-done | bytes 327712 | tf_op jit(solution)/shard_map/ppermute | solution.py:40
  28.8 2.7 %collective-permute-start.8 = (bf16[256,1280]{1,0:T(8,128)(2,1)S(1)}, bf16[256,1280]{1,0:T(8,128)(2,1)S(1)}, u32[]{:S(2)}, u32[]{:S(2)}) collective-permute-start(bf16[256,1280]{1,0:T(8,128)(2,1)S(1)} %shard_map.59.refs_4_.refs_0_), channel_id=1, source_target_pairs={{0,208},{64,0},{128,64},{192,128},{16,192},{80,16},{144,80},{208,1... | collective-permute-start | bytes 1966088 | tf_op jit(solution)/shard_map/ppermute | solution.py:40
  31.4 3.0 %collective-permute-start.6 = (bf16[256,1280]{1,0:T(8,128)(2,1)S(1)}, bf16[256,1280]{1,0:T(8,128)(2,1)}, u32[]{:S(2)}, u32[]{:S(2)}) collective-permute-start(bf16[256,1280]{1,0:T(8,128)(2,1)S(1)} %get-tuple-element.26.refs_0_), channel_id=1, source_target_pairs={{0,12},{1,13},{2,14},{3,15},{4,0},{5,1},{6,2},{7,3},{8,4},{9,5},{1... | collective-permute-start | bytes 1966088 | tf_op jit(solution)/shard_map/ppermute | solution.py:31
  34.4 0.6 collective-permute-start.5
  35.1 1.0 collective-permute-start.4
  36.0 4.9 %collective-permute-done.8.refs_5_.refs_1_ = bf16[256,1280]{1,0:T(8,128)(2,1)S(1)} collective-permute-done((bf16[256,1280]{1,0:T(8,128)(2,1)S(1)}, bf16[256,1280]{1,0:T(8,128)(2,1)S(1)}, u32[]{:S(2)}, u32[]{:S(2)}) %collective-permute-start.8) | collective-permute-done | bytes 655392 | tf_op jit(solution)/shard_map/ppermute | solution.py:40
  41.6 0.1 stack.23.place
  41.7 7.9 %collective-permute-done.6.refs_3_ = bf16[256,1280]{1,0:T(8,128)(2,1)} collective-permute-done((bf16[256,1280]{1,0:T(8,128)(2,1)S(1)}, bf16[256,1280]{1,0:T(8,128)(2,1)}, u32[]{:S(2)}, u32[]{:S(2)}) %collective-permute-start.6) | collective-permute-done | bytes 655392 | tf_op jit(solution)/shard_map/ppermute | solution.py:31
  49.6 4.1 %collective-permute-done.4.refs_1_ = bf16[256,1280]{1,0:T(8,128)(2,1)} collective-permute-done((bf16[256,1280]{1,0:T(8,128)(2,1)S(1)}, bf16[256,1280]{1,0:T(8,128)(2,1)}, u32[]{:S(2)}, u32[]{:S(2)}) %collective-permute-start.4) | collective-permute-done | bytes 655392 | tf_op jit(solution)/shard_map/ppermute | solution.py:31
  53.7 5.8 %shard_map.60 = (f32[1024,1024]{1,0:T(8,128)S(1)}, f32[16,128]{1,0:T(8,128)S(1)}, f32[16,128]{1,0:T(8,128)S(1)}, f32[8,128]{1,0:T(8,128)S(1)}) custom-call(s32[5]{0:T(128)S(1)} %stack.23.place, f32[1]{0:T(128)S(6)} %copy.6.scale, bf16[256,1280]{1,0:T(8,128)(2,1)S(1)} %get-tuple-element.26.refs_0_, bf16[256,1280]{1,0:T(8,128)(2,1)} %collective-permute-done.4.refs_1_, ...), custom_call_target="tpu_custom_call" | custom-call | tf_op jit(solution)/shard_map/pallas_call | solution.py:197
  59.5 2.0 %copy-done = f32[1024,1024]{1,0:T(8,128)} copy-done((f32[1024,1024]{1,0:T(8,128)}, f32[1024,1024]{1,0:T(8,128)S(1)}, u32[]{:S(2)}) %copy-start) | copy-done | bytes 4194328
  61.5 1.2 collective-permute-done.11
  62.7 3.5 %collective-permute-start.14 = (f32[40,128]{1,0:T(8,128)S(1)}, f32[40,128]{1,0:T(8,128)S(1)}, u32[]{:S(2)}, u32[]{:S(2)}) collective-permute-start(f32[40,128]{1,0:T(8,128)S(1)} %pad_maximum_fusion.1), channel_id=1, source_target_pairs={{0,3},{1,0},{2,1},{3,2},{4,7},{5,4},{6,5},{7,6},{8,11},{9,8},{10,9... | collective-permute-start | bytes 61448 | tf_op jit(solution)/shard_map/ppermute | solution.py:57
  66.2 1.0 collective-permute-start.12
  67.2 0.5 collective-permute-done.14
  67.7 3.8 %collective-permute-done.13 = f32[40,128]{1,0:T(8,128)S(1)} collective-permute-done((f32[40,128]{1,0:T(8,128)S(1)}, f32[40,128]{1,0:T(8,128)S(1)}, u32[]{:S(2)}, u32[]{:S(2)}) %collective-permute-start.13) | collective-permute-done | bytes 20512 | tf_op jit(solution)/shard_map/ppermute | solution.py:57
  71.6 2.5 %collective-permute-start.17 = (f32[40,128]{1,0:T(8,128)S(1)}, f32[40,128]{1,0:T(8,128)S(1)}, u32[]{:S(2)}, u32[]{:S(2)}) collective-permute-start(f32[40,128]{1,0:T(8,128)S(1)} %pad_maximum_fusion.2), channel_id=1, source_target_pairs={{0,12},{1,13},{2,14},{3,15},{4,0},{5,1},{6,2},{7,3},{8,4},{9,5},{1... | collective-permute-start | bytes 61448 | tf_op jit(solution)/shard_map/ppermute | solution.py:57
  74.1 2.5 %collective-permute-start.16 = (f32[40,128]{1,0:T(8,128)S(1)}, f32[40,128]{1,0:T(8,128)S(1)}, u32[]{:S(2)}, u32[]{:S(2)}) collective-permute-start(f32[40,128]{1,0:T(8,128)S(1)} %pad_maximum_fusion.2), channel_id=1, source_target_pairs={{0,8},{1,9},{2,10},{3,11},{4,12},{5,13},{6,14},{7,15},{8,0},{9,1},... | collective-permute-start | bytes 61448 | tf_op jit(solution)/shard_map/ppermute | solution.py:57
  76.7 0.9 collective-permute-start.15
  77.6 3.7 %collective-permute-done.16 = f32[40,128]{1,0:T(8,128)S(1)} collective-permute-done((f32[40,128]{1,0:T(8,128)S(1)}, f32[40,128]{1,0:T(8,128)S(1)}, u32[]{:S(2)}, u32[]{:S(2)}) %collective-permute-start.16) | collective-permute-done | bytes 20512 | tf_op jit(solution)/shard_map/ppermute | solution.py:57
  81.3 0.7 collective-permute-done.15
  82.1 0.1 collective-permute-start.23
  82.2 1.1 collective-permute-done.23
  83.4 0.6 slice_select_fusion.1
  84.0 2.2 %copy-done.1 = f32[1024,1024]{1,0:T(8,128)S(1)} copy-done((f32[1024,1024]{1,0:T(8,128)S(1)}, f32[1024,1024]{1,0:T(8,128)}, u32[]{:S(2)}) %copy-start.1) | copy-done | bytes 4194328
  86.2 5.5 %shard_map.61 = (bf16[1024,1024]{1,0:T(8,128)(2,1)S(1)}, bf16[256,1280]{1,0:T(8,128)(2,1)S(1)}, bf16[256,1280]{1,0:T(8,128)(2,1)S(1)}) custom-call(s32[5]{0:T(128)S(1)} %stack.23.place, f32[1]{0:T(128)S(6)} %copy.6.scale, f32[1024,1024]{1,0:T(8,128)S(1)} %copy-done.1, f32[16,128]{1,0:T(8,128)S(1)} %get-tuple-element.58.row_lse, ...), custom_call_target="tpu_custom_call" | custom-call | tf_op jit(solution)/shard_map/pallas_call | solution.py:277
  91.7 0.3 collective-permute-start.31
  91.9 3.8 %shard_map.62 = (bf16[256,1280]{1,0:T(8,128)(2,1)S(1)}, bf16[256,1280]{1,0:T(8,128)(2,1)S(1)}, bf16[256,1280]{1,0:T(8,128)(2,1)S(1)}) custom-call(f32[1]{0:T(128)S(6)} %copy.6.scale, bf16[1024,1024]{1,0:T(8,128)(2,1)S(1)} %get-tuple-element.32.weights, bf16[256,1280]{1,0:T(8,128)(2,1)S(1)} %get-tuple-element.26.refs_0_, ...), custom_call_target="tpu_custom_call" | custom-call | tf_op jit(solution)/shard_map/pallas_call | solution.py:308
  95.8 0.8 copy-done.2
  96.6 0.3 collective-permute-start.30
  96.9 0.2 shard_map.66
  97.1 1.6 %collective-permute-start.32 = (bf16[256,1280]{1,0:T(8,128)(2,1)S(1)}, bf16[256,1280]{1,0:T(8,128)(2,1)S(1)}, u32[]{:S(2)}, u32[]{:S(2)}) collective-permute-start(bf16[256,1280]{1,0:T(8,128)(2,1)S(1)} %shard_map.66), channel_id=1, source_target_pairs={{0,64},{64,128},{128,192},{192,16},{16,80},{80,144},{144,208},{208... | collective-permute-start | bytes 1966088 | tf_op jit(solution)/shard_map/ppermute | solution.py:40
  98.6 3.4 %shard_map.63 = (bf16[256,1280]{1,0:T(8,128)(2,1)}, bf16[256,1280]{1,0:T(8,128)(2,1)}, bf16[256,1280]{1,0:T(8,128)(2,1)}) custom-call(f32[1]{0:T(128)S(6)} %copy.6.scale, bf16[1024,1024]{1,0:T(8,128)(2,1)S(1)} %get-tuple-element.32.weights, bf16[256,1280]{1,0:T(8,128)(2,1)S(1)} %shard_map.59.refs_4_.refs_0_, ...), custom_call_target="tpu_custom_call" | custom-call | tf_op jit(solution)/shard_map/pallas_call | solution.py:292
  102.0 1.5 %collective-permute-start.24 = (bf16[256,1280]{1,0:T(8,128)(2,1)}, bf16[256,1280]{1,0:T(8,128)(2,1)S(1)}, u32[]{:S(2)}, u32[]{:S(2)}) collective-permute-start(bf16[256,1280]{1,0:T(8,128)(2,1)} %get-tuple-element.34), channel_id=1, source_target_pairs={{0,8},{1,9},{2,10},{3,11},{4,12},{5,13},{6,14},{7,15},{8,0},{9,1},... | collective-permute-start | bytes 1966088 | tf_op jit(solution)/shard_map/ppermute | solution.py:31
  103.5 2.0 %collective-permute-start.25 = (bf16[256,1280]{1,0:T(8,128)(2,1)}, bf16[256,1280]{1,0:T(8,128)(2,1)S(1)}, u32[]{:S(2)}, u32[]{:S(2)}) collective-permute-start(bf16[256,1280]{1,0:T(8,128)(2,1)} %get-tuple-element.35), channel_id=1, source_target_pairs={{0,12},{1,13},{2,14},{3,15},{4,0},{5,1},{6,2},{7,3},{8,4},{9,5},{1... | collective-permute-start | bytes 1966088 | tf_op jit(solution)/shard_map/ppermute | solution.py:31
  105.5 2.6 %collective-permute-done.32.refs_2_ = bf16[256,1280]{1,0:T(8,128)(2,1)S(1)} collective-permute-done((bf16[256,1280]{1,0:T(8,128)(2,1)S(1)}, bf16[256,1280]{1,0:T(8,128)(2,1)S(1)}, u32[]{:S(2)}, u32[]{:S(2)}) %collective-permute-start.32) | collective-permute-done | bytes 655392 | tf_op jit(solution)/shard_map/ppermute | solution.py:40
  108.1 0.9 shard_map.67
  109.0 2.5 %collective-permute-start.33 = (bf16[128,1280]{1,0:T(8,128)(2,1)}, bf16[128,1280]{1,0:T(8,128)(2,1)S(1)}, u32[]{:S(2)}, u32[]{:S(2)}) collective-permute-start(bf16[128,1280]{1,0:T(8,128)(2,1)} %get-tuple-element.46), channel_id=1, source_target_pairs={{0,128},{64,192},{128,16},{192,80},{16,144},{80,208},{144,0},{208,... | collective-permute-start | bytes 983048 | tf_op jit(solution)/shard_map/ppermute | solution.py:40
  111.5 0.5 slice.118
  114.6 3.3 %collective-permute-start.18 = (f32[8,128]{1,0:T(8,128)S(1)}, f32[8,128]{1,0:T(8,128)S(1)}, u32[]{:S(2)}, u32[]{:S(2)}) collective-permute-start(f32[8,128]{1,0:T(8,128)S(1)} %broadcast_in_dim.9), channel_id=1, source_target_pairs={{0,16},{1,17},{2,18},{3,19},{4,20},{5,21},{6,22},{7,23},{8,24},{9,... | collective-permute-start | bytes 12296 | tf_op jit(solution)/shard_map/ppermute | solution.py:57
  117.9 4.4 %collective-permute-done.18 = f32[8,128]{1,0:T(8,128)S(1)} collective-permute-done((f32[8,128]{1,0:T(8,128)S(1)}, f32[8,128]{1,0:T(8,128)S(1)}, u32[]{:S(2)}, u32[]{:S(2)}) %collective-permute-start.18) | collective-permute-done | bytes 4128 | tf_op jit(solution)/shard_map/ppermute | solution.py:57
  122.3 1.1 collective-permute-start.19
  123.4 0.3 shard_map.64
  123.7 2.0 %collective-permute-start.27 = (bf16[64,1280]{1,0:T(8,128)(2,1)S(1)}, bf16[64,1280]{1,0:T(8,128)(2,1)S(1)}, u32[]{:S(2)}, u32[]{:S(2)}) collective-permute-start(bf16[64,1280]{1,0:T(8,128)(2,1)S(1)} %get-tuple-element.38), channel_id=1, source_target_pairs={{0,2},{1,3},{2,0},{3,1},{4,6},{5,7},{6,4},{7,5},{8,10},{9,11},{10,... | collective-permute-start | bytes 491528 | tf_op jit(solution)/shard_map/ppermute | solution.py:31
  125.7 0.4 collective-permute-start.28
  126.2 1.6 %collective-permute-start.29 = (bf16[64,1280]{1,0:T(8,128)(2,1)S(1)}, bf16[64,1280]{1,0:T(8,128)(2,1)S(1)}, u32[]{:S(2)}, u32[]{:S(2)}) collective-permute-start(bf16[64,1280]{1,0:T(8,128)(2,1)S(1)} %get-tuple-element.40), channel_id=1, source_target_pairs={{0,1},{1,2},{2,3},{3,0},{4,5},{5,6},{6,7},{7,4},{8,9},{9,10},{10,1... | collective-permute-start | bytes 491528 | tf_op jit(solution)/shard_map/ppermute | solution.py:31
  127.8 2.9 %collective-permute-start.34 = (bf16[64,1280]{1,0:T(8,128)(2,1)S(1)}, bf16[64,1280]{1,0:T(8,128)(2,1)S(1)}, u32[]{:S(2)}, u32[]{:S(2)}) collective-permute-start(bf16[64,1280]{1,0:T(8,128)(2,1)S(1)} %get-tuple-element.48), channel_id=1, source_target_pairs={{0,16},{64,80},{128,144},{192,208},{16,0},{80,64},{144,128},{208,1... | collective-permute-start | bytes 491528 | tf_op jit(solution)/shard_map/ppermute | solution.py:40
  130.7 4.2 %collective-permute-start.20 = (f32[8,128]{1,0:T(8,128)S(1)}, f32[8,128]{1,0:T(8,128)S(1)}, u32[]{:S(2)}, u32[]{:S(2)}) collective-permute-start(f32[8,128]{1,0:T(8,128)S(1)} %fusion.5), channel_id=1, source_target_pairs={{0,64},{1,65},{2,66},{3,67},{4,68},{5,69},{6,70},{7,71},{8,72},{9,... | collective-permute-start | bytes 12296 | tf_op jit(solution)/shard_map/ppermute | solution.py:57
  134.9 4.7 %collective-permute-done.20 = f32[8,128]{1,0:T(8,128)S(1)} collective-permute-done((f32[8,128]{1,0:T(8,128)S(1)}, f32[8,128]{1,0:T(8,128)S(1)}, u32[]{:S(2)}, u32[]{:S(2)}) %collective-permute-start.20) | collective-permute-done | bytes 4128 | tf_op jit(solution)/shard_map/ppermute | solution.py:57
  139.6 0.7 collective-permute-start.21
  140.3 0.1 collective-permute-start.22
  140.4 1.2 collective-permute-done.22
  141.6 0.5 slice.96
  142.8 0.8 shard_map.65
  143.5 0.7 shard_map.69
  (59 shorter events, 0.5 us)
Async XLA Ops:
  0.6 14.1 %collective-permute-start = (bf16[64,1280]{1,0:T(8,128)(2,1)}, bf16[64,1280]{1,0:T(8,128)(2,1)S(1)}, u32[]{:S(2)}, u32[]{:S(2)}) collective-permute-start(bf16[64,1280]{1,0:T(8,128)(2,1)} %refs_0_.1), channel_id=1, source_target_pairs={{0,16},{64,80},{128,144},{192,208},{16,0},{80,64},{144,128},{208,1... | collective-permute-start | bytes 491528 | tf_op jit(solution)/shard_map/ppermute | solution.py:40
  7.0 7.7 %collective-permute-start.2 = (bf16[64,1280]{1,0:T(8,128)(2,1)}, bf16[64,1280]{1,0:T(8,128)(2,1)S(1)}, u32[]{:S(2)}, u32[]{:S(2)}) collective-permute-start(bf16[64,1280]{1,0:T(8,128)(2,1)} %refs_2_.1), channel_id=1, source_target_pairs={{0,2},{1,3},{2,0},{3,1},{4,6},{5,7},{6,4},{7,5},{8,10},{9,11},{10,... | collective-permute-start | bytes 491528 | tf_op jit(solution)/shard_map/ppermute | solution.py:31
  10.0 6.7 %collective-permute-start.1 = (bf16[64,1280]{1,0:T(8,128)(2,1)}, bf16[64,1280]{1,0:T(8,128)(2,1)S(1)}, u32[]{:S(2)}, u32[]{:S(2)}) collective-permute-start(bf16[64,1280]{1,0:T(8,128)(2,1)} %refs_2_.1), channel_id=1, source_target_pairs={{0,1},{1,2},{2,3},{3,0},{4,5},{5,6},{6,7},{7,4},{8,9},{9,10},{10,1... | collective-permute-start | bytes 491528 | tf_op jit(solution)/shard_map/ppermute | solution.py:31
  10.6 6.2 %collective-permute-start.3 = (bf16[64,1280]{1,0:T(8,128)(2,1)}, bf16[64,1280]{1,0:T(8,128)(2,1)S(1)}, u32[]{:S(2)}, u32[]{:S(2)}) collective-permute-start(bf16[64,1280]{1,0:T(8,128)(2,1)} %refs_2_.1), channel_id=1, source_target_pairs={{0,3},{1,0},{2,1},{3,2},{4,7},{5,4},{6,5},{7,6},{8,11},{9,8},{10,9... | collective-permute-start | bytes 491528 | tf_op jit(solution)/shard_map/ppermute | solution.py:31
  16.8 0.9 copy-start.4
  17.7 0.9 copy-start.5
  18.7 10.0 %collective-permute-start.7 = (bf16[128,1280]{1,0:T(8,128)(2,1)S(1)}, bf16[128,1280]{1,0:T(8,128)(2,1)S(1)}, u32[]{:S(2)}, u32[]{:S(2)}) collective-permute-start(bf16[128,1280]{1,0:T(8,128)(2,1)S(1)} %get-tuple-element.27.refs_0_), channel_id=1, source_target_pairs={{0,144},{64,208},{128,0},{192,64},{16,128},{80,192},{144,16},{208,... | collective-permute-start | bytes 983048 | tf_op jit(solution)/shard_map/ppermute | solution.py:40
  28.8 12.2 %collective-permute-start.8 = (bf16[256,1280]{1,0:T(8,128)(2,1)S(1)}, bf16[256,1280]{1,0:T(8,128)(2,1)S(1)}, u32[]{:S(2)}, u32[]{:S(2)}) collective-permute-start(bf16[256,1280]{1,0:T(8,128)(2,1)S(1)} %shard_map.59.refs_4_.refs_0_), channel_id=1, source_target_pairs={{0,208},{64,0},{128,64},{192,128},{16,192},{80,16},{144,80},{208,1... | collective-permute-start | bytes 1966088 | tf_op jit(solution)/shard_map/ppermute | solution.py:40
  31.4 18.1 %collective-permute-start.6 = (bf16[256,1280]{1,0:T(8,128)(2,1)S(1)}, bf16[256,1280]{1,0:T(8,128)(2,1)}, u32[]{:S(2)}, u32[]{:S(2)}) collective-permute-start(bf16[256,1280]{1,0:T(8,128)(2,1)S(1)} %get-tuple-element.26.refs_0_), channel_id=1, source_target_pairs={{0,12},{1,13},{2,14},{3,15},{4,0},{5,1},{6,2},{7,3},{8,4},{9,5},{1... | collective-permute-start | bytes 1966088 | tf_op jit(solution)/shard_map/ppermute | solution.py:31
  34.4 15.1 %collective-permute-start.5 = (bf16[256,1280]{1,0:T(8,128)(2,1)S(1)}, bf16[256,1280]{1,0:T(8,128)(2,1)}, u32[]{:S(2)}, u32[]{:S(2)}) collective-permute-start(bf16[256,1280]{1,0:T(8,128)(2,1)S(1)} %get-tuple-element.26.refs_0_), channel_id=1, source_target_pairs={{0,8},{1,9},{2,10},{3,11},{4,12},{5,13},{6,14},{7,15},{8,0},{9,1},... | collective-permute-start | bytes 1966088 | tf_op jit(solution)/shard_map/ppermute | solution.py:31
  35.1 18.6 %collective-permute-start.4 = (bf16[256,1280]{1,0:T(8,128)(2,1)S(1)}, bf16[256,1280]{1,0:T(8,128)(2,1)}, u32[]{:S(2)}, u32[]{:S(2)}) collective-permute-start(bf16[256,1280]{1,0:T(8,128)(2,1)S(1)} %get-tuple-element.26.refs_0_), channel_id=1, source_target_pairs={{0,4},{1,5},{2,6},{3,7},{4,8},{5,9},{6,10},{7,11},{8,12},{9,13},{1... | collective-permute-start | bytes 1966088 | tf_op jit(solution)/shard_map/ppermute | solution.py:31
  36.0 17.6 %collective-permute-start.9 = (bf16[256,1280]{1,0:T(8,128)(2,1)S(1)}, bf16[256,1280]{1,0:T(8,128)(2,1)S(1)}, u32[]{:S(2)}, u32[]{:S(2)}) collective-permute-start(bf16[256,1280]{1,0:T(8,128)(2,1)S(1)} %shard_map.59.refs_4_.refs_0_), channel_id=1, source_target_pairs={{0,32},{32,0},{1,33},{33,1},{2,34},{34,2},{3,35},{35,3},{4,36},{36... | collective-permute-start | bytes 1966088 | tf_op jit(solution)/shard_map/ppermute | solution.py:44
  40.9 12.7 %collective-permute-start.10 = (bf16[256,1280]{1,0:T(8,128)(2,1)S(1)}, bf16[256,1280]{1,0:T(8,128)(2,1)S(1)}, u32[]{:S(2)}, u32[]{:S(2)}) collective-permute-start(bf16[256,1280]{1,0:T(8,128)(2,1)S(1)} %collective-permute-done.8.refs_5_.refs_1_), channel_id=1, source_target_pairs={{0,32},{32,0},{1,33},{33,1},{2,34},{34,2},{3,35},{35,3},{4,36},{36... | collective-permute-start | bytes 1966088 | tf_op jit(solution)/shard_map/ppermute | solution.py:44
  59.5 2.0 %copy-start = (f32[1024,1024]{1,0:T(8,128)}, f32[1024,1024]{1,0:T(8,128)S(1)}, u32[]{:S(2)}) copy-start(f32[1024,1024]{1,0:T(8,128)S(1)} %get-tuple-element.31.logits) | copy-start | bytes 12582916
  61.5 1.2 collective-permute-start.11
  62.7 5.0 %collective-permute-start.14 = (f32[40,128]{1,0:T(8,128)S(1)}, f32[40,128]{1,0:T(8,128)S(1)}, u32[]{:S(2)}, u32[]{:S(2)}) collective-permute-start(f32[40,128]{1,0:T(8,128)S(1)} %pad_maximum_fusion.1), channel_id=1, source_target_pairs={{0,3},{1,0},{2,1},{3,2},{4,7},{5,4},{6,5},{7,6},{8,11},{9,8},{10,9... | collective-permute-start | bytes 61448 | tf_op jit(solution)/shard_map/ppermute | solution.py:57
  66.2 5.3 %collective-permute-start.13 = (f32[40,128]{1,0:T(8,128)S(1)}, f32[40,128]{1,0:T(8,128)S(1)}, u32[]{:S(2)}, u32[]{:S(2)}) collective-permute-start(f32[40,128]{1,0:T(8,128)S(1)} %pad_maximum_fusion.1), channel_id=1, source_target_pairs={{0,2},{1,3},{2,0},{3,1},{4,6},{5,7},{6,4},{7,5},{8,10},{9,11},{10,... | collective-permute-start | bytes 61448 | tf_op jit(solution)/shard_map/ppermute | solution.py:57
  66.2 5.3 %collective-permute-start.12 = (f32[40,128]{1,0:T(8,128)S(1)}, f32[40,128]{1,0:T(8,128)S(1)}, u32[]{:S(2)}, u32[]{:S(2)}) collective-permute-start(f32[40,128]{1,0:T(8,128)S(1)} %pad_maximum_fusion.1), channel_id=1, source_target_pairs={{0,1},{1,2},{2,3},{3,0},{4,5},{5,6},{6,7},{7,4},{8,9},{9,10},{10,1... | collective-permute-start | bytes 61448 | tf_op jit(solution)/shard_map/ppermute | solution.py:57
  71.6 6.0 %collective-permute-start.17 = (f32[40,128]{1,0:T(8,128)S(1)}, f32[40,128]{1,0:T(8,128)S(1)}, u32[]{:S(2)}, u32[]{:S(2)}) collective-permute-start(f32[40,128]{1,0:T(8,128)S(1)} %pad_maximum_fusion.2), channel_id=1, source_target_pairs={{0,12},{1,13},{2,14},{3,15},{4,0},{5,1},{6,2},{7,3},{8,4},{9,5},{1... | collective-permute-start | bytes 61448 | tf_op jit(solution)/shard_map/ppermute | solution.py:57
  74.1 7.2 %collective-permute-start.16 = (f32[40,128]{1,0:T(8,128)S(1)}, f32[40,128]{1,0:T(8,128)S(1)}, u32[]{:S(2)}, u32[]{:S(2)}) collective-permute-start(f32[40,128]{1,0:T(8,128)S(1)} %pad_maximum_fusion.2), channel_id=1, source_target_pairs={{0,8},{1,9},{2,10},{3,11},{4,12},{5,13},{6,14},{7,15},{8,0},{9,1},... | collective-permute-start | bytes 61448 | tf_op jit(solution)/shard_map/ppermute | solution.py:57
  76.7 5.3 %collective-permute-start.15 = (f32[40,128]{1,0:T(8,128)S(1)}, f32[40,128]{1,0:T(8,128)S(1)}, u32[]{:S(2)}, u32[]{:S(2)}) collective-permute-start(f32[40,128]{1,0:T(8,128)S(1)} %pad_maximum_fusion.2), channel_id=1, source_target_pairs={{0,4},{1,5},{2,6},{3,7},{4,8},{5,9},{6,10},{7,11},{8,12},{9,13},{1... | collective-permute-start | bytes 61448 | tf_op jit(solution)/shard_map/ppermute | solution.py:57
  82.1 1.3 collective-permute-start.23
  84.0 2.2 %copy-start.1 = (f32[1024,1024]{1,0:T(8,128)S(1)}, f32[1024,1024]{1,0:T(8,128)}, u32[]{:S(2)}) copy-start(f32[1024,1024]{1,0:T(8,128)} %copy-done) | copy-start | bytes 12582916
  91.7 5.2 %collective-permute-start.31 = (bf16[256,1280]{1,0:T(8,128)(2,1)S(1)}, bf16[256,1280]{1,0:T(8,128)(2,1)S(1)}, u32[]{:S(2)}, u32[]{:S(2)}) collective-permute-start(bf16[256,1280]{1,0:T(8,128)(2,1)S(1)} %get-tuple-element.44), channel_id=1, source_target_pairs={{0,32},{32,0},{1,33},{33,1},{2,34},{34,2},{3,35},{35,3},{4,36},{36... | collective-permute-start | bytes 1966088 | tf_op jit(solution)/shard_map/ppermute | solution.py:44
  95.7 0.8 copy-start.2
  96.6 8.9 %collective-permute-start.30 = (bf16[256,1280]{1,0:T(8,128)(2,1)S(1)}, bf16[256,1280]{1,0:T(8,128)(2,1)S(1)}, u32[]{:S(2)}, u32[]{:S(2)}) collective-permute-start(bf16[256,1280]{1,0:T(8,128)(2,1)S(1)} %get-tuple-element.42), channel_id=1, source_target_pairs={{0,32},{32,0},{1,33},{33,1},{2,34},{34,2},{3,35},{35,3},{4,36},{36... | collective-permute-start | bytes 1966088 | tf_op jit(solution)/shard_map/ppermute | solution.py:44
  96.9 26.5 %copy-start.3 = (bf16[256,1280]{1,0:T(8,128)(2,1)S(1)}, bf16[256,1280]{1,0:T(8,128)(2,1)}, u32[]{:S(2)}) copy-start(bf16[256,1280]{1,0:T(8,128)(2,1)} %copy-done.2) | copy-start | bytes 1966084
  97.1 11.0 %collective-permute-start.32 = (bf16[256,1280]{1,0:T(8,128)(2,1)S(1)}, bf16[256,1280]{1,0:T(8,128)(2,1)S(1)}, u32[]{:S(2)}, u32[]{:S(2)}) collective-permute-start(bf16[256,1280]{1,0:T(8,128)(2,1)S(1)} %shard_map.66), channel_id=1, source_target_pairs={{0,64},{64,128},{128,192},{192,16},{16,80},{80,144},{144,208},{208... | collective-permute-start | bytes 1966088 | tf_op jit(solution)/shard_map/ppermute | solution.py:40
  102.0 21.4 %collective-permute-start.24 = (bf16[256,1280]{1,0:T(8,128)(2,1)}, bf16[256,1280]{1,0:T(8,128)(2,1)S(1)}, u32[]{:S(2)}, u32[]{:S(2)}) collective-permute-start(bf16[256,1280]{1,0:T(8,128)(2,1)} %get-tuple-element.34), channel_id=1, source_target_pairs={{0,8},{1,9},{2,10},{3,11},{4,12},{5,13},{6,14},{7,15},{8,0},{9,1},... | collective-permute-start | bytes 1966088 | tf_op jit(solution)/shard_map/ppermute | solution.py:31
  103.5 19.9 %collective-permute-start.25 = (bf16[256,1280]{1,0:T(8,128)(2,1)}, bf16[256,1280]{1,0:T(8,128)(2,1)S(1)}, u32[]{:S(2)}, u32[]{:S(2)}) collective-permute-start(bf16[256,1280]{1,0:T(8,128)(2,1)} %get-tuple-element.35), channel_id=1, source_target_pairs={{0,12},{1,13},{2,14},{3,15},{4,0},{5,1},{6,2},{7,3},{8,4},{9,5},{1... | collective-permute-start | bytes 1966088 | tf_op jit(solution)/shard_map/ppermute | solution.py:31
  105.4 18.0 %collective-permute-start.26 = (bf16[256,1280]{1,0:T(8,128)(2,1)}, bf16[256,1280]{1,0:T(8,128)(2,1)S(1)}, u32[]{:S(2)}, u32[]{:S(2)}) collective-permute-start(bf16[256,1280]{1,0:T(8,128)(2,1)} %get-tuple-element.36), channel_id=1, source_target_pairs={{0,4},{1,5},{2,6},{3,7},{4,8},{5,9},{6,10},{7,11},{8,12},{9,13},{1... | collective-permute-start | bytes 1966088 | tf_op jit(solution)/shard_map/ppermute | solution.py:31
  109.0 18.8 %collective-permute-start.33 = (bf16[128,1280]{1,0:T(8,128)(2,1)}, bf16[128,1280]{1,0:T(8,128)(2,1)S(1)}, u32[]{:S(2)}, u32[]{:S(2)}) collective-permute-start(bf16[128,1280]{1,0:T(8,128)(2,1)} %get-tuple-element.46), channel_id=1, source_target_pairs={{0,128},{64,192},{128,16},{192,80},{16,144},{80,208},{144,0},{208,... | collective-permute-start | bytes 983048 | tf_op jit(solution)/shard_map/ppermute | solution.py:40
  114.6 7.7 %collective-permute-start.18 = (f32[8,128]{1,0:T(8,128)S(1)}, f32[8,128]{1,0:T(8,128)S(1)}, u32[]{:S(2)}, u32[]{:S(2)}) collective-permute-start(f32[8,128]{1,0:T(8,128)S(1)} %broadcast_in_dim.9), channel_id=1, source_target_pairs={{0,16},{1,17},{2,18},{3,19},{4,20},{5,21},{6,22},{7,23},{8,24},{9,... | collective-permute-start | bytes 12296 | tf_op jit(solution)/shard_map/ppermute | solution.py:57
  122.3 8.4 %collective-permute-start.19 = (f32[8,128]{1,0:T(8,128)S(1)}, f32[8,128]{1,0:T(8,128)S(1)}, u32[]{:S(2)}, u32[]{:S(2)}) collective-permute-start(f32[8,128]{1,0:T(8,128)S(1)} %broadcast_add_fusion), channel_id=1, source_target_pairs={{0,128},{1,129},{2,130},{3,131},{4,132},{5,133},{6,134},{7,135},{8... | collective-permute-start | bytes 12296 | tf_op jit(solution)/shard_map/ppermute | solution.py:57
  123.7 19.0 %collective-permute-start.27 = (bf16[64,1280]{1,0:T(8,128)(2,1)S(1)}, bf16[64,1280]{1,0:T(8,128)(2,1)S(1)}, u32[]{:S(2)}, u32[]{:S(2)}) collective-permute-start(bf16[64,1280]{1,0:T(8,128)(2,1)S(1)} %get-tuple-element.38), channel_id=1, source_target_pairs={{0,2},{1,3},{2,0},{3,1},{4,6},{5,7},{6,4},{7,5},{8,10},{9,11},{10,... | collective-permute-start | bytes 491528 | tf_op jit(solution)/shard_map/ppermute | solution.py:31
  125.7 17.0 %collective-permute-start.28 = (bf16[64,1280]{1,0:T(8,128)(2,1)S(1)}, bf16[64,1280]{1,0:T(8,128)(2,1)S(1)}, u32[]{:S(2)}, u32[]{:S(2)}) collective-permute-start(bf16[64,1280]{1,0:T(8,128)(2,1)S(1)} %get-tuple-element.39), channel_id=1, source_target_pairs={{0,3},{1,0},{2,1},{3,2},{4,7},{5,4},{6,5},{7,6},{8,11},{9,8},{10,9... | collective-permute-start | bytes 491528 | tf_op jit(solution)/shard_map/ppermute | solution.py:31
  126.2 16.6 %collective-permute-start.29 = (bf16[64,1280]{1,0:T(8,128)(2,1)S(1)}, bf16[64,1280]{1,0:T(8,128)(2,1)S(1)}, u32[]{:S(2)}, u32[]{:S(2)}) collective-permute-start(bf16[64,1280]{1,0:T(8,128)(2,1)S(1)} %get-tuple-element.40), channel_id=1, source_target_pairs={{0,1},{1,2},{2,3},{3,0},{4,5},{5,6},{6,7},{7,4},{8,9},{9,10},{10,1... | collective-permute-start | bytes 491528 | tf_op jit(solution)/shard_map/ppermute | solution.py:31
  127.8 15.7 %collective-permute-start.34 = (bf16[64,1280]{1,0:T(8,128)(2,1)S(1)}, bf16[64,1280]{1,0:T(8,128)(2,1)S(1)}, u32[]{:S(2)}, u32[]{:S(2)}) collective-permute-start(bf16[64,1280]{1,0:T(8,128)(2,1)S(1)} %get-tuple-element.48), channel_id=1, source_target_pairs={{0,16},{64,80},{128,144},{192,208},{16,0},{80,64},{144,128},{208,1... | collective-permute-start | bytes 491528 | tf_op jit(solution)/shard_map/ppermute | solution.py:40
  130.7 8.9 %collective-permute-start.20 = (f32[8,128]{1,0:T(8,128)S(1)}, f32[8,128]{1,0:T(8,128)S(1)}, u32[]{:S(2)}, u32[]{:S(2)}) collective-permute-start(f32[8,128]{1,0:T(8,128)S(1)} %fusion.5), channel_id=1, source_target_pairs={{0,64},{1,65},{2,66},{3,67},{4,68},{5,69},{6,70},{7,71},{8,72},{9,... | collective-permute-start | bytes 12296 | tf_op jit(solution)/shard_map/ppermute | solution.py:57
  139.6 0.7 collective-permute-start.21
  140.3 1.3 collective-permute-start.22

commit v3 on v2

--- a/solution.py
+++ b/solution.py
@@ -13,7 +13,8 @@
 BF16, F32 = jnp.bfloat16, jnp.float32
 VMEM = pl.BlockSpec(memory_space=pltpu.VMEM)
 SMEM = pl.BlockSpec(memory_space=pltpu.SMEM)
-PARAMS = pltpu.CompilerParams(vmem_limit_bytes=36 * 1024 * 1024)
+ANY = pl.BlockSpec(memory_space=pl.ANY)
+PARAMS = pltpu.CompilerParams(vmem_limit_bytes=12 * 1024 * 1024)
 
 
 def plane_shift(v, k, primary):
@@ -61,22 +62,9 @@
     return ((((z % 4) * 2 + c) * 2 + z // 4) * NY + y) * NX + x
 
 
-def lse(parts):
-    top = parts[0]
-    for p in parts[1:]:
-        top = jnp.maximum(top, p)
-    return top + jnp.log(sum(jnp.exp(p - top) for p in parts))
-
-
-def in_order(parts, at):
-    out = []
-    for i in range(4):
-        k = (at - i) & 3
-        v = parts[3]
-        for n in (2, 1, 0):
-            v = jnp.where(k == n, parts[n], v)
-        out.append(v)
-    return out
+def lse2(a, b):
+    top = jnp.maximum(a, b)
+    return top + jnp.log(jnp.exp(a - top) + jnp.exp(b - top))
 
 
 def row_place(where, a, b):
@@ -88,9 +76,9 @@
 
 def col_place(where, j, i):
     zl, c, zh, y, x = where
-    core = c if j < 2 else 1 - c
-    sign = 1 - 2 * core
-    off = sign * ((0, 0, 2, 2)[i] + j % 2) + (0, 4, 0, 4)[i]
+    core = c if (i < 2) == (j != 2) else 1 - c
+    sign = 1 - 2 * c
+    off = sign * ((0, 1, -1, 2 if i < 2 else -2)[j]) + 4 * (i % 2)
     z = (zh * 4 + zl + off) & 7
     return z * 2 + core, ((z >> 2) * 16 + y * 4 + x) * 8 + (z & 3) * 2 + core
 
@@ -111,13 +99,22 @@
 
 
 def pack_body(counts, *refs):
+    n = sum(counts)
+    outs, sem = refs[n:-1], refs[-1]
     at = 0
-    for n, out in zip(counts, refs[sum(counts) :]):
+    local_copy = None
+    for count, out in zip(counts, outs):
         row = 0
-        for r in refs[at : at + n]:
-            out[row : row + r.shape[0], :] = r[...]
+        for r in refs[at : at + count]:
+            rows = out.at[row : row + r.shape[0], :]
+            if at == 0 and row == 0:
+                local_copy = pltpu.make_async_copy(r, rows, sem)
+                local_copy.start()
+            else:
+                rows[...] = r[...]
             row += r.shape[0]
-        at += n
+        at += count
+    local_copy.wait()
 
 
 def pack(*groups):
@@ -126,8 +123,9 @@
     return pl.pallas_call(
         lambda *refs: pack_body([len(g) for g in groups], *refs),
         out_shape=tuple(shapes),
-        in_specs=[VMEM] * len(parts),
+        in_specs=[ANY] + [VMEM] * (len(parts) - 1),
         out_specs=(VMEM,) * len(groups),
+        scratch_shapes=[pltpu.SemaphoreType.DMA],
         compiler_params=PARAMS,
     )(*parts)
 
@@ -212,8 +210,8 @@
 def weights_body(place, scale, logits, row_lse, col_lse, *refs):
     images = refs[:4]
     weights = refs[4]
-    outs = refs[5:7]
-    row_wide = refs[7]
+    outs = refs[5:9]
+    row_wide = refs[9]
     where = [place[i] for i in range(5)]
     multiplier = scale[0]
     lane = lax.broadcasted_iota(jnp.int32, (1, 128), 1)
@@ -238,16 +236,17 @@
                 both = 0.5 * jnp.exp(tile - wide) + 0.5 * jnp.exp(tile - col_line[t])
                 both = both - jnp.where(ids[b] == cols[t][0:1], 1.0, 0.0)
                 weights[at : at + ROWS, t * 128 : (t + 1) * 128] = both.astype(BF16)
-    text_terms(multiplier, weights, images, {1: outs[0], 3: outs[1]})
+    text_terms(multiplier, weights, images, ((2, 0, outs[0]), (3, 128, outs[1]), (3, 0, outs[2]), (1, 0, outs[3])))
 
 
 def text_terms(multiplier, weights, images, outs):
-    for j, out in outs.items():
+    for j, skip, out in outs:
+        at = j * CHUNK + skip
         for e in range(5):
             acc = None
             for a in range(4):
                 term = lax.dot_general(
-                    weights[a * CHUNK : (a + 1) * CHUNK, j * CHUNK : (j + 1) * CHUNK],
+                    weights[a * CHUNK : (a + 1) * CHUNK, at : at + out.shape[0]],
                     images[a][:, e * 256 : (e + 1) * 256],
                     (((0,), (0,)), ((), ())),
                     preferred_element_type=F32,
@@ -273,68 +272,103 @@
 PART = jax.ShapeDtypeStruct((CHUNK, EMBED), BF16)
 
 
+HALF = jax.ShapeDtypeStruct((CHUNK // 2, EMBED), BF16)
+
+
 def weights_call(place, scale, logits, row_lse, col_lse, images):
     return pl.pallas_call(
         weights_body,
-        out_shape=(jax.ShapeDtypeStruct((BLOCK, BLOCK), BF16), PART, PART),
+        out_shape=(jax.ShapeDtypeStruct((BLOCK, BLOCK), BF16), PART, HALF, HALF, PART),
         in_specs=[SMEM, SMEM] + [VMEM] * 7,
-        out_specs=(VMEM,) * 3,
+        out_specs=(VMEM,) * 5,
         scratch_shapes=[pltpu.VMEM((BLOCK, 128), F32)],
         compiler_params=PARAMS,
     )(place, scale, logits, row_lse, col_lse, *images)
 
 
-def image_body(scale, weights, *refs):
+def image_body(scale, after, weights, *refs):
     image_terms(scale[0], weights, refs[:4], dict(zip((2, 1, 3), refs[4:])))
 
 
-def image_call(scale, weights, texts):
+def image_call(scale, after, weights, texts):
     return pl.pallas_call(
         image_body,
         out_shape=(PART,) * 3,
-        in_specs=[SMEM] + [VMEM] * 5,
+        in_specs=[SMEM] + [VMEM] * 6,
         out_specs=(VMEM,) * 3,
         compiler_params=PARAMS,
-    )(scale, weights, *texts)
+    )(scale, after, weights, *texts)
 
 
 def rest_body(scale, weights, *refs):
     images, texts, outs = refs[:4], refs[4:8], refs[8:]
-    text_terms(scale[0], weights, images, {2: outs[1], 0: outs[0]})
-    image_terms(scale[0], weights, texts, {0: outs[2]})
+    text_terms(scale[0], weights, images, ((0, 0, outs[0]),))
+    image_terms(scale[0], weights, texts, {0: outs[1]})
 
 
 def rest_call(scale, weights, images, texts):
     return pl.pallas_call(
         rest_body,
-        out_shape=(PART,) * 3,
+        out_shape=(PART,) * 2,
         in_specs=[SMEM] + [VMEM] * 9,
-        out_specs=(VMEM,) * 3,
+        out_specs=(VMEM,) * 2,
         compiler_params=PARAMS,
     )(scale, weights, *images, *texts)
 
 
-def add_body(n, *refs):
-    outs = refs[n:]
-    rows = outs[0].shape[0]
-    for o, out in enumerate(outs):
+def sums_body(n, plan, *refs):
+    for (rows, terms), out in zip(plan, refs[n:]):
         for at in range(0, rows, 16):
-            total = refs[0][o * rows + at : o * rows + at + 16, :].astype(F32)
-            for r in refs[1:n]:
-                total += r[o * rows + at : o * rows + at + 16, :].astype(F32)
+            total = None
+            for i, skip in terms:
+                v = refs[i][skip + at : skip + at + 16, :].astype(F32)
+                total = v if total is None else total + v
             out[at : at + 16, :] = total.astype(out.dtype)
 
 
-def add(parts, pieces=1):
-    rows = parts[0].shape[0] // pieces
+def sums(arrays, *plan):
     out = pl.pallas_call(
-        lambda *refs: add_body(len(parts), *refs),
-        out_shape=(jax.ShapeDtypeStruct((rows, EMBED), BF16),) * pieces,
-        in_specs=[VMEM] * len(parts),
-        out_specs=(VMEM,) * pieces,
-        compiler_params=PARAMS,
-    )(*parts)
-    return out if pieces > 1 else out[0]
+        lambda *refs: sums_body(len(arrays), plan, *refs),
+        out_shape=tuple(jax.ShapeDtypeStruct((rows, EMBED), BF16) for rows, _ in plan),
+        in_specs=[VMEM] * len(arrays),
+        out_specs=(VMEM,) * len(plan),
+        compiler_params=PARAMS,
+    )(*arrays)
+    return out if len(plan) > 1 else out[0]
+
+
+def share_body(place, state, out):
+    real = lax.broadcasted_iota(jnp.int32, (16, 128), 1) < ROWS
+    both = jnp.where(real, state[:16, :], 0.0)
+    more = jnp.where(real, state[16:32, :], 0.0)
+    first = place[1] == 0
+    both = both + jnp.where(first, more, 0.0)
+    total = jnp.sum(both, keepdims=True) - jnp.where(first, 2.0, 0.0) * state[32:33, 0:1]
+    out[...] = jnp.broadcast_to(total, (8, 128))
+
+
+def share_call(place, state):
+    return pl.pallas_call(
+        share_body,
+        out_shape=jax.ShapeDtypeStruct((8, 128), F32),
+        in_specs=[SMEM, VMEM],
+        out_specs=VMEM,
+        compiler_params=PARAMS,
+    )(place, state)
+
+
+def mean_body(a, b, out):
+    out[...] = (a[0:1, 0:1] + b[0:1, 0:1]) * (1.0 / (2.0 * ROWS * 256))
+
+
+def mean_call(a, b):
+    return pl.pallas_call(
+        mean_body,
+        out_shape=jax.ShapeDtypeStruct((1, 1), F32),
+        in_specs=[VMEM] * 2,
+        out_specs=VMEM,
+        compiler_params=PARAMS,
+    )(a, b)
 
 
 def local(image_emb, text_emb, logit_scale):
@@ -342,71 +376,58 @@
 
     far = z_shift(text_emb, 4)
     near = [plane_shift(image_emb, k, True) for k in (1, 2, 3)]
-    pair, own = pack([text_emb, far], [image_emb] + near)
-    (text_0,) = pack([pair, z_shift(pair, -2)])
+    (pair,) = pack([text_emb, far])
+    own, text_0 = pack([image_emb] + near, [pair, core_swap(pair)])
+    text_1 = z_shift(text_0, -1)
+    text_3 = z_shift(pair, -2)
     images = [own] + [plane_shift(own, k, False) for k in (1, 2, 3)]
-    text_1 = z_shift(text_0, -1)
-    texts = [text_0, text_1, core_swap(text_0), core_swap(text_1)]
+    (text_3,) = pack([text_3, core_swap(text_3)])
+    texts = [text_0, text_1, core_swap(text_1), text_3]
 
     logits, row_part, col_part, matched = logits_call(place, logit_scale, images, texts)
 
     first = place[1] == 0
     got = core_swap(jnp.concatenate([jnp.where(first, col_part, row_part), matched]))
     rows_first = jnp.concatenate([row_part, got[:16]])
-    cols_first = jnp.concatenate([lse([col_part, got[:16]])] * 2)
-    state = jnp.where(first, rows_first, cols_first)
-    hits = matched + got[16:]
-
-    def join(parts, at):
-        parts = in_order(parts, at)
-        kept = lse([p[:32] for p in parts])
-        return jnp.concatenate([kept, parts[0][32:] + parts[1][32:] + (parts[2][32:] + parts[3][32:])])
-
-    state = jnp.concatenate([state, hits])
-    z = place[2] * 4 + place[0]
-    state = join(
-        [state]
-        + [
-            split_move(state, lambda y, x, z: (y, x + k, z), lambda y, x, z: (y, x, z + 2 * k))
-            for k in (1, 2, 3)
-        ],
-        jnp.where(first, place[4], z >> 1),
-    )
-    moved = [
-        split_move(
-            state, lambda y, x, z: (y + k, x, z), (lambda y, x, z: (y, x, z ^ 1)) if k == 1 else None
-        )
-        for k in (1, 2, 3)
-    ]
-    state = jnp.where(first, join([state] + moved, place[3]), jnp.concatenate([lse([state[:32], moved[0][:32]]), hits]))
+    cols_first = jnp.concatenate([lse2(col_part, got[:16])] * 2)
+    state = jnp.concatenate([jnp.where(first, rows_first, cols_first), matched + got[16:]])
+    for to_0, to_1 in (
+        (lambda y, x, z: (y, x ^ 2, z), lambda y, x, z: (y, x, z ^ 4)),
+        (lambda y, x, z: (y, x ^ 1, z), lambda y, x, z: (y, x, z ^ 2)),
+        (lambda y, x, z: (y ^ 2, x, z), lambda y, x, z: (y, x, z ^ 1)),
+        (lambda y, x, z: (y ^ 1, x, z), None),
+    ):
+        other = split_move(state, to_0, to_1)
+        joined = jnp.concatenate([lse2(state[:32], other[:32]), state[32:] + other[32:]])
+        state = joined if to_1 is not None else jnp.where(first, joined, state)
     got = core_swap(jnp.where(first, state[16:32], state[:16]))
     row_lse = jnp.where(first, state[:16], got)
     col_lse = jnp.where(first, got, state[:16])
 
-    weights, text_1_term, text_3_term = weights_call(place, logit_scale, logits, row_lse, col_lse, images)
-    back_1 = core_swap(text_3_term)
-    image_terms_far = image_call(logit_scale, weights, texts)
-    text_0_term, text_2_term, image_0_term = rest_call(logit_scale, weights, images, texts)
-    back_0 = core_swap(text_2_term)
-
-    back = [plane_shift(v, -k, False) for v, k in zip(image_terms_far, (2, 1, 3))]
-    t = z_shift(add([text_1_term, back_1]), 1)
-    t_near, t_far = add([text_0_term, back_0, t], pieces=2)
-    pieces = add([image_0_term] + back, pieces=4)
-    t_near, t_far = add([t_near, z_shift(t_far, 2)], pieces=2)
-    image_grad = add([pieces[0]] + [plane_shift(pieces[k], -k, True) for k in (2, 1, 3)])
-    text_grad = add([t_near, z_shift(t_far, 4)])
-
-    real = lax.broadcasted_iota(jnp.int32, (16, 128), 1) < ROWS
-    half = [jnp.sum(jnp.where(real, v, 0.0)) for v in (state[:16], state[16:32])]
-    share = jnp.where(first, half[0] + half[1] - 2.0 * state[32, 0], half[0])
-    s = jnp.broadcast_to(share, (8, 128))
-    s = s + split_move(s, lambda y, x, z: (y, x, z ^ 4), lambda y, x, z: (y, x ^ 2, z))
-    s = s + split_move(s, lambda y, x, z: (y, x, z ^ 2), lambda y, x, z: (y, x ^ 1, z))
-    s = s + split_move(s, lambda y, x, z: (y, x, z ^ 1), lambda y, x, z: (y ^ 2, x, z))
+    s = share_call(place, state)
+    s_1 = s + split_move(s, lambda y, x, z: (y, x, z ^ 4), lambda y, x, z: (y, x ^ 2, z))
+    s_2 = s_1 + split_move(s_1, lambda y, x, z: (y, x, z ^ 2), lambda y, x, z: (y, x ^ 1, z))
+    s = s_2 + split_move(s_2, lambda y, x, z: (y, x, z ^ 1), lambda y, x, z: (y ^ 2, x, z))
     s = s + split_move(s, None, lambda y, x, z: (y ^ 1, x, z))
-    s = s + core_swap(s)
-    mean_loss = s[0, :1] / (2.0 * ROWS * 256)
+    mean_loss = mean_call(s, core_swap(s)).reshape(1)
+
+    weights, text_2, text_3b, text_3a, text_1 = weights_call(
+        place, logit_scale, logits, row_lse, col_lse, images
+    )
+    near, far = core_swap(text_2), core_swap(text_3b)
+    image_parts = image_call(logit_scale, s_1, weights, texts)
+    near, far = sums([text_1, near, text_3a, far, s_2], (256, ((0, 0), (1, 0))), (128, ((2, 0), (3, 0))))
+    near, far = z_shift(near, 1), z_shift(far, 2)
+    back = [plane_shift(v, -k, False) for v, k in zip(image_parts, (2, 1, 3))]
+    text_0, image_0 = rest_call(logit_scale, weights, images, texts)
+    mine, other = sums(
+        [text_0, near, far], (128, ((0, 0), (1, 0), (2, 0))), (128, ((0, 128), (1, 128)))
+    )
+    mine, far = sums([mine, core_swap(other)], (64, ((0, 0), (1, 0))), (64, ((0, 64), (1, 64))))
+    pieces = sums([image_0] + back, *[(64, [(i, 64 * k) for i in range(4)]) for k in range(4)])
+    shards = [pieces[0]] + [plane_shift(pieces[k], -k, True) for k in (2, 1, 3)]
+    image_grad = sums(shards, (64, [(i, 0) for i in range(4)]))
+    text_grad = sums([mine, z_shift(far, 4)], (64, ((0, 0), (1, 0))))
     return mean_loss, image_grad, text_grad
 
 

time: 146 us -> 147 us (level)
  the two profiles are of different devices: /device:TPU:32 before, /device:TPU:65 now
where the time goes in v3:
time: 147 us
  starting transfers between devices  70.2 us (48%)
  waiting for transfers between devices  48.8 us (33%)
  Pallas kernels  24.1 us (16%)
  local copies, waits for them, and re-layouts  1.92 us (1%)
  between operations  1.53 us (1%)
    ppermute x9, starting transfers between devices, core_swap(): return lax.ppermute(v, 'core', [(0, 1), (1, 0)])  24.7 us
    ppermute x6, waiting for transfers between devices, z_shift(): return lax.ppermute(v, ('zl', 'core', 'zh'), pairs)  23.1 us
    ppermute x6, starting transfers between devices, z_shift(): return lax.ppermute(v, ('zl', 'core', 'zh'), pairs)  16.6 us
    ppermute x12, starting transfers between devices, plane_shift(): return lax.ppermute(v, ('core', 'zh', 'y', 'x'), pairs)  16.5 us
    ppermute x8, waiting for transfers between devices, split_move(): return lax.ppermute(v, AXES, pairs)  16.3 us
    ppermute x8, starting transfers between devices, split_move(): return lax.ppermute(v, AXES, pairs)  12.4 us
    pallas_call x1, Pallas kernels, weights_call(): pl.pallas_call(weights_body, out_shape=(jax.ShapeDtypeStruct((BLOCK, BLOC...  6.4 us
    ppermute x12, waiting for transfers between devices, plane_shift(): return lax.ppermute(v, ('core', 'zh', 'y', 'x'), pairs)  6.06 us
  transfers between devices with their start and end apart: 35, of which 19 were waited for; matrix products, arithmetic and copies ran while one was open for 0% of the time, Pallas kernels for 7%

profile of v3, /device:TPU:65, one launch (start us, length us, event | category | flops | bytes accessed | tf_op | source)
XLA Modules:
  0.0 146.8 jit_solution(10528630961045602358)
XLA Ops:
  0.6 5.2 %collective-permute-start.3 = (bf16[64,1280]{1,0:T(8,128)(2,1)}, bf16[64,1280]{1,0:T(8,128)(2,1)S(1)}, u32[]{:S(2)}, u32[]{:S(2)}) collective-permute-start(bf16[64,1280]{1,0:T(8,128)(2,1)} %refs_0_.2), channel_id=1, source_target_pairs={{0,16},{64,80},{128,144},{192,208},{16,0},{80,64},{144,128},{208,1... | collective-permute-start | bytes 491528 | tf_op jit(solution)/shard_map/ppermute | solution.py:41
  5.8 8.0 %collective-permute-done.3.refs_1_ = bf16[64,1280]{1,0:T(8,128)(2,1)S(1)} collective-permute-done((bf16[64,1280]{1,0:T(8,128)(2,1)}, bf16[64,1280]{1,0:T(8,128)(2,1)S(1)}, u32[]{:S(2)}, u32[]{:S(2)}) %collective-permute-start.3) | collective-permute-done | bytes 163872 | tf_op jit(solution)/shard_map/ppermute | solution.py:41
  13.8 0.9 copy-done
  14.9 1.4 collective-permute-start.4
  16.3 2.9 %collective-permute-start.1 = (bf16[64,1280]{1,0:T(8,128)(2,1)}, bf16[64,1280]{1,0:T(8,128)(2,1)S(1)}, u32[]{:S(2)}, u32[]{:S(2)}) collective-permute-start(bf16[64,1280]{1,0:T(8,128)(2,1)} %refs_0_.3), channel_id=1, source_target_pairs={{0,2},{1,3},{2,0},{3,1},{4,6},{5,7},{6,4},{7,5},{8,10},{9,11},{10,... | collective-permute-start | bytes 491528 | tf_op jit(solution)/shard_map/ppermute | solution.py:32
  19.2 0.4 collective-permute-start
  19.6 2.3 %collective-permute-start.2 = (bf16[64,1280]{1,0:T(8,128)(2,1)}, bf16[64,1280]{1,0:T(8,128)(2,1)S(1)}, u32[]{:S(2)}, u32[]{:S(2)}) collective-permute-start(bf16[64,1280]{1,0:T(8,128)(2,1)} %refs_0_.3), channel_id=1, source_target_pairs={{0,3},{1,0},{2,1},{3,2},{4,7},{5,4},{6,5},{7,6},{8,11},{9,8},{10,9... | collective-permute-start | bytes 491528 | tf_op jit(solution)/shard_map/ppermute | solution.py:32
  21.9 0.6 collective-permute-done.1.refs_2_
  22.5 2.6 %collective-permute-done.refs_1_ = bf16[64,1280]{1,0:T(8,128)(2,1)S(1)} collective-permute-done((bf16[64,1280]{1,0:T(8,128)(2,1)}, bf16[64,1280]{1,0:T(8,128)(2,1)S(1)}, u32[]{:S(2)}, u32[]{:S(2)}) %collective-permute-start) | collective-permute-done | bytes 163872 | tf_op jit(solution)/shard_map/ppermute | solution.py:32
  25.1 0.9 copy-done.1
  26.0 0.3 shard_map.59
  26.4 4.8 %collective-permute-start.10 = (bf16[128,1280]{1,0:T(8,128)(2,1)S(1)}, bf16[128,1280]{1,0:T(8,128)(2,1)}, u32[]{:S(2)}, u32[]{:S(2)}) collective-permute-start(bf16[128,1280]{1,0:T(8,128)(2,1)S(1)} %shard_map.58.refs_4_), channel_id=1, source_target_pairs={{0,144},{64,208},{128,0},{192,64},{16,128},{80,192},{144,16},{208,... | collective-permute-start | bytes 983048 | tf_op jit(solution)/shard_map/ppermute | solution.py:41
  31.2 2.5 %collective-permute-start.7 = (bf16[256,1280]{1,0:T(8,128)(2,1)S(1)}, bf16[256,1280]{1,0:T(8,128)(2,1)S(1)}, u32[]{:S(2)}, u32[]{:S(2)}) collective-permute-start(bf16[256,1280]{1,0:T(8,128)(2,1)S(1)} %get-tuple-element.29.refs_0_), channel_id=1, source_target_pairs={{0,12},{1,13},{2,14},{3,15},{4,0},{5,1},{6,2},{7,3},{8,4},{9,5},{1... | collective-permute-start | bytes 1966088 | tf_op jit(solution)/shard_map/ppermute | solution.py:32
  33.9 0.6 collective-permute-start.5
  34.5 3.9 %collective-permute-done.8.refs_5_.refs_1_ = bf16[256,1280]{1,0:T(8,128)(2,1)S(1)} collective-permute-done((bf16[256,1280]{1,0:T(8,128)(2,1)S(1)}, bf16[256,1280]{1,0:T(8,128)(2,1)S(1)}, u32[]{:S(2)}, u32[]{:S(2)}) %collective-permute-start.8) | collective-permute-done | bytes 655392 | tf_op jit(solution)/shard_map/ppermute | solution.py:41
  38.4 3.3 %collective-permute-done.10.refs_0_ = bf16[128,1280]{1,0:T(8,128)(2,1)} collective-permute-done((bf16[128,1280]{1,0:T(8,128)(2,1)S(1)}, bf16[128,1280]{1,0:T(8,128)(2,1)}, u32[]{:S(2)}, u32[]{:S(2)}) %collective-permute-start.10) | collective-permute-done | bytes 327712 | tf_op jit(solution)/shard_map/ppermute | solution.py:41
  41.7 5.1 %collective-permute-start.11 = (bf16[128,1280]{1,0:T(8,128)(2,1)}, bf16[128,1280]{1,0:T(8,128)(2,1)}, u32[]{:S(2)}, u32[]{:S(2)}) collective-permute-start(bf16[128,1280]{1,0:T(8,128)(2,1)} %collective-permute-done.10.refs_0_), channel_id=1, source_target_pairs={{0,32},{32,0},{1,33},{33,1},{2,34},{34,2},{3,35},{35,3},{4,36},{36... | collective-permute-start | bytes 983048 | tf_op jit(solution)/shard_map/ppermute | solution.py:45
  47.5 0.9 collective-permute-done.11.refs_1_
  48.4 2.0 %shard_map.60.refs_7_.refs_3_ = bf16[256,1280]{1,0:T(8,128)(2,1)S(1)} custom-call(bf16[128,1280]{1,0:T(8,128)(2,1)} %collective-permute-done.10.refs_0_, bf16[128,1280]{1,0:T(8,128)(2,1)} %collective-permute-done.11.refs_1_), custom_call_target="tpu_custom_call" | custom-call | tf_op jit(solution)/shard_map/pallas_call | solution.py:123
  50.4 1.6 %collective-permute-done.5.refs_1_ = bf16[256,1280]{1,0:T(8,128)(2,1)} collective-permute-done((bf16[256,1280]{1,0:T(8,128)(2,1)S(1)}, bf16[256,1280]{1,0:T(8,128)(2,1)}, u32[]{:S(2)}, u32[]{:S(2)}) %collective-permute-start.5) | collective-permute-done | bytes 655392 | tf_op jit(solution)/shard_map/ppermute | solution.py:32
  52.0 5.7 %shard_map.61 = (f32[1024,1024]{1,0:T(8,128)S(1)}, f32[16,128]{1,0:T(8,128)S(1)}, f32[16,128]{1,0:T(8,128)S(1)}, f32[8,128]{1,0:T(8,128)S(1)}) custom-call(s32[5]{0:T(128)S(1)} %stack.23.place, f32[1]{0:T(128)S(6)} %copy.6.scale, bf16[256,1280]{1,0:T(8,128)(2,1)S(1)} %get-tuple-element.29.refs_0_, bf16[256,1280]{1,0:T(8,128)(2,1)} %collective-permute-done.5.refs_1_, ...), custom_call_target="tpu_custom_call" | custom-call | tf_op jit(solution)/shard_map/pallas_call | solution.py:195
  57.6 2.3 %collective-permute-start.12 = (f32[24,128]{1,0:T(8,128)S(1)}, f32[24,128]{1,0:T(8,128)S(1)}, u32[]{:S(2)}, u32[]{:S(2)}) collective-permute-start(f32[24,128]{1,0:T(8,128)S(1)} %pad_maximum_fusion.4), channel_id=1, source_target_pairs={{0,32},{32,0},{1,33},{33,1},{2,34},{34,2},{3,35},{35,3},{4,36},{36... | collective-permute-start | bytes 36872 | tf_op jit(solution)/shard_map/ppermute | solution.py:45
  59.9 0.8 collective-permute-done.12
  60.8 1.7 %collective-permute-start.13 = (f32[40,128]{1,0:T(8,128)S(1)}, f32[40,128]{1,0:T(8,128)S(1)}, u32[]{:S(2)}, u32[]{:S(2)}) collective-permute-start(f32[40,128]{1,0:T(8,128)S(1)} %pad_maximum_fusion), channel_id=1, source_target_pairs={{0,2},{1,3},{2,0},{3,1},{4,6},{5,7},{6,4},{7,5},{8,10},{9,11},{10,... | collective-permute-start | bytes 61448 | tf_op jit(solution)/shard_map/ppermute | solution.py:58
  62.6 4.9 %collective-permute-done.13 = f32[40,128]{1,0:T(8,128)S(1)} collective-permute-done((f32[40,128]{1,0:T(8,128)S(1)}, f32[40,128]{1,0:T(8,128)S(1)}, u32[]{:S(2)}, u32[]{:S(2)}) %collective-permute-start.13) | collective-permute-done | bytes 20512 | tf_op jit(solution)/shard_map/ppermute | solution.py:58
  67.5 2.3 %collective-permute-start.14 = (f32[40,128]{1,0:T(8,128)S(1)}, f32[40,128]{1,0:T(8,128)S(1)}, u32[]{:S(2)}, u32[]{:S(2)}) collective-permute-start(f32[40,128]{1,0:T(8,128)S(1)} %pad_maximum_fusion.1), channel_id=1, source_target_pairs={{0,1},{1,0},{2,3},{3,2},{4,5},{5,4},{6,7},{7,6},{8,9},{9,8},{10,11... | collective-permute-start | bytes 61448 | tf_op jit(solution)/shard_map/ppermute | solution.py:58
  69.8 1.3 collective-permute-done.14
  71.2 0.6 collective-permute-start.15
  71.8 2.1 %collective-permute-done.15 = f32[40,128]{1,0:T(8,128)S(1)} collective-permute-done((f32[40,128]{1,0:T(8,128)S(1)}, f32[40,128]{1,0:T(8,128)S(1)}, u32[]{:S(2)}, u32[]{:S(2)}) %collective-permute-start.15) | collective-permute-done | bytes 20512 | tf_op jit(solution)/shard_map/ppermute | solution.py:58
  73.9 0.7 collective-permute-start.16
  74.7 7.1 %collective-permute-start.22 = (f32[16,128]{1,0:T(8,128)S(1)}, f32[16,128]{1,0:T(8,128)S(1)}, u32[]{:S(2)}, u32[]{:S(2)}) collective-permute-start(f32[16,128]{1,0:T(8,128)S(1)} %slice_select_fusion), channel_id=1, source_target_pairs={{0,32},{32,0},{1,33},{33,1},{2,34},{34,2},{3,35},{35,3},{4,36},{36... | collective-permute-start | bytes 24584 | tf_op jit(solution)/shard_map/ppermute | solution.py:45
  81.7 0.8 collective-permute-done.22
  82.6 6.4 %shard_map.64 = (bf16[1024,1024]{1,0:T(8,128)(2,1)S(1)}, bf16[256,1280]{1,0:T(8,128)(2,1)S(1)}, bf16[128,1280]{1,0:T(8,128)(2,1)S(1)}, bf16[128,1280]{1,0:T(8,128)(2,1)S(1)}, bf16[256,1280]{1,0:T(8,128)(2,1)S(1)}) custom-call(s32[5]{0:T(128)S(1)} %stack.23.place, f32[1]{0:T(128)S(6)} %copy.6.scale, f32[1024,1024]{1,0:T(8,128)S(1)} %get-tuple-element.34.logits, ...), custom_call_target="tpu_custom_call" | custom-call | tf_op jit(solution)/shard_map/pallas_call | solution.py:279
  89.0 0.4 collective-permute-start.29
  89.6 0.7 shard_map.62
  90.3 2.5 %collective-permute-start.17 = (f32[8,128]{1,0:T(8,128)S(1)}, f32[8,128]{1,0:T(8,128)S(1)}, u32[]{:S(2)}, u32[]{:S(2)}) collective-permute-start(f32[8,128]{1,0:T(8,128)S(1)} %shard_map.62), channel_id=1, source_target_pairs={{0,16},{1,17},{2,18},{3,19},{4,20},{5,21},{6,22},{7,23},{8,24},{9,... | collective-permute-start | bytes 12296 | tf_op jit(solution)/shard_map/ppermute | solution.py:58
  92.7 1.6 %collective-permute-done.17 = f32[8,128]{1,0:T(8,128)S(1)} collective-permute-done((f32[8,128]{1,0:T(8,128)S(1)}, f32[8,128]{1,0:T(8,128)S(1)}, u32[]{:S(2)}, u32[]{:S(2)}) %collective-permute-start.17) | collective-permute-done | bytes 4128 | tf_op jit(solution)/shard_map/ppermute | solution.py:58
  94.3 0.6 collective-permute-start.18
  94.9 2.2 %collective-permute-done.18 = f32[8,128]{1,0:T(8,128)S(1)} collective-permute-done((f32[8,128]{1,0:T(8,128)S(1)}, f32[8,128]{1,0:T(8,128)S(1)}, u32[]{:S(2)}, u32[]{:S(2)}) %collective-permute-start.18) | collective-permute-done | bytes 4128 | tf_op jit(solution)/shard_map/ppermute | solution.py:58
  97.1 0.2 shard_map.69
  97.3 2.0 %collective-permute-start.31 = (bf16[256,1280]{1,0:T(8,128)(2,1)S(1)}, bf16[256,1280]{1,0:T(8,128)(2,1)S(1)}, u32[]{:S(2)}, u32[]{:S(2)}) collective-permute-start(bf16[256,1280]{1,0:T(8,128)(2,1)S(1)} %get-tuple-element.49), channel_id=1, source_target_pairs={{0,64},{64,128},{128,192},{192,16},{16,80},{80,144},{144,208},{208... | collective-permute-start | bytes 1966088 | tf_op jit(solution)/shard_map/ppermute | solution.py:41
  99.3 3.3 %shard_map.66 = (bf16[256,1280]{1,0:T(8,128)(2,1)S(1)}, bf16[256,1280]{1,0:T(8,128)(2,1)S(1)}, bf16[256,1280]{1,0:T(8,128)(2,1)S(1)}) custom-call(f32[1]{0:T(128)S(6)} %copy.6.scale, f32[8,128]{1,0:T(8,128)S(1)} %add.72.after, bf16[1024,1024]{1,0:T(8,128)(2,1)S(1)} %get-tuple-element.35.weights, bf16[256,1280]{1,0:T(8,128)(2,1)S(1)} %get-tuple-element.30.refs_4_.refs_0_, ...), custom_call_target="tpu_custom_call" | custom-call | tf_op jit(solution)/shard_map/pallas_call | solution.py:294
  102.7 2.7 %collective-permute-start.23 = (bf16[256,1280]{1,0:T(8,128)(2,1)S(1)}, bf16[256,1280]{1,0:T(8,128)(2,1)S(1)}, u32[]{:S(2)}, u32[]{:S(2)}) collective-permute-start(bf16[256,1280]{1,0:T(8,128)(2,1)S(1)} %get-tuple-element.37), channel_id=1, source_target_pairs={{0,8},{1,9},{2,10},{3,11},{4,12},{5,13},{6,14},{7,15},{8,0},{9,1},... | collective-permute-start | bytes 1966088 | tf_op jit(solution)/shard_map/ppermute | solution.py:32
  105.4 0.4 collective-permute-start.24
  105.8 1.1 collective-permute-start.25
  106.9 0.6 collective-permute-start.32
  107.4 2.9 %shard_map.65 = (bf16[256,1280]{1,0:T(8,128)(2,1)S(1)}, bf16[256,1280]{1,0:T(8,128)(2,1)S(1)}) custom-call(f32[1]{0:T(128)S(6)} %copy.6.scale, bf16[1024,1024]{1,0:T(8,128)(2,1)S(1)} %get-tuple-element.35.weights, bf16[256,1280]{1,0:T(8,128)(2,1)S(1)} %get-tuple-element.29.refs_0_, bf16[256,1280]{1,0:T(8,128)(2,1)} %collective-permute-done.5.refs_1_, ...), custom_call_target="tpu_custom_call" | custom-call | tf_op jit(solution)/shard_map/pallas_call | solution.py:310
  110.3 7.9 %collective-permute-done.32.refs_2_ = bf16[128,1280]{1,0:T(8,128)(2,1)S(1)} collective-permute-done((bf16[128,1280]{1,0:T(8,128)(2,1)S(1)}, bf16[128,1280]{1,0:T(8,128)(2,1)S(1)}, u32[]{:S(2)}, u32[]{:S(2)}) %collective-permute-start.32) | collective-permute-done | bytes 327712 | tf_op jit(solution)/shard_map/ppermute | solution.py:41
  118.4 1.9 %collective-permute-start.33 = (bf16[128,1280]{1,0:T(8,128)(2,1)S(1)}, bf16[128,1280]{1,0:T(8,128)(2,1)S(1)}, u32[]{:S(2)}, u32[]{:S(2)}) collective-permute-start(bf16[128,1280]{1,0:T(8,128)(2,1)S(1)} %get-tuple-element.52), channel_id=1, source_target_pairs={{0,32},{32,0},{1,33},{33,1},{2,34},{34,2},{3,35},{35,3},{4,36},{36... | collective-permute-start | bytes 983048 | tf_op jit(solution)/shard_map/ppermute | solution.py:45
  120.4 1.2 collective-permute-done.24.refs_2_
  121.6 0.3 shard_map.67
  121.9 1.9 %collective-permute-start.26 = (bf16[64,1280]{1,0:T(8,128)(2,1)S(1)}, bf16[64,1280]{1,0:T(8,128)(2,1)S(1)}, u32[]{:S(2)}, u32[]{:S(2)}) collective-permute-start(bf16[64,1280]{1,0:T(8,128)(2,1)S(1)} %get-tuple-element.41), channel_id=1, source_target_pairs={{0,2},{1,3},{2,0},{3,1},{4,6},{5,7},{6,4},{7,5},{8,10},{9,11},{10,... | collective-permute-start | bytes 491528 | tf_op jit(solution)/shard_map/ppermute | solution.py:32
  123.8 0.3 collective-permute-start.27
  124.1 1.2 collective-permute-start.28
  125.4 3.9 %collective-permute-start.34 = (bf16[64,1280]{1,0:T(8,128)(2,1)S(1)}, bf16[64,1280]{1,0:T(8,128)(2,1)S(1)}, u32[]{:S(2)}, u32[]{:S(2)}) collective-permute-start(bf16[64,1280]{1,0:T(8,128)(2,1)S(1)} %get-tuple-element.54), channel_id=1, source_target_pairs={{0,16},{64,80},{128,144},{192,208},{16,0},{80,64},{144,128},{208,1... | collective-permute-start | bytes 491528 | tf_op jit(solution)/shard_map/ppermute | solution.py:41
  129.3 1.2 collective-permute-start.19
  130.6 2.7 %collective-permute-done.19 = f32[8,128]{1,0:T(8,128)S(1)} collective-permute-done((f32[8,128]{1,0:T(8,128)S(1)}, f32[8,128]{1,0:T(8,128)S(1)}, u32[]{:S(2)}, u32[]{:S(2)}) %collective-permute-start.19) | collective-permute-done | bytes 4128 | tf_op jit(solution)/shard_map/ppermute | solution.py:58
  133.3 2.8 %collective-permute-start.20 = (f32[8,128]{1,0:T(8,128)S(1)}, f32[8,128]{1,0:T(8,128)S(1)}, u32[]{:S(2)}, u32[]{:S(2)}) collective-permute-start(f32[8,128]{1,0:T(8,128)S(1)} %add.74), channel_id=1, source_target_pairs={{32,36},{33,37},{34,38},{35,39},{36,32},{37,33},{38,34},{39,35},{4... | collective-permute-start | bytes 12296 | tf_op jit(solution)/shard_map/ppermute | solution.py:58
  136.1 1.5 %collective-permute-done.20 = f32[8,128]{1,0:T(8,128)S(1)} collective-permute-done((f32[8,128]{1,0:T(8,128)S(1)}, f32[8,128]{1,0:T(8,128)S(1)}, u32[]{:S(2)}, u32[]{:S(2)}) %collective-permute-start.20) | collective-permute-done | bytes 4128 | tf_op jit(solution)/shard_map/ppermute | solution.py:58
  137.6 6.4 %collective-permute-start.21 = (f32[8,128]{1,0:T(8,128)S(1)}, f32[8,128]{1,0:T(8,128)S(1)}, u32[]{:S(2)}, u32[]{:S(2)}) collective-permute-start(f32[8,128]{1,0:T(8,128)S(1)} %add.75.a), channel_id=1, source_target_pairs={{0,32},{32,0},{1,33},{33,1},{2,34},{34,2},{3,35},{35,3},{4,36},{36... | collective-permute-start | bytes 12296 | tf_op jit(solution)/shard_map/ppermute | solution.py:45
  144.0 0.8 collective-permute-done.21.b
  144.8 0.5 shard_map.63
  145.3 0.8 shard_map.68
  146.1 0.7 shard_map.72
  (50 shorter events, 1.3 us)
Async XLA Ops:
  0.6 13.2 %collective-permute-start.3 = (bf16[64,1280]{1,0:T(8,128)(2,1)}, bf16[64,1280]{1,0:T(8,128)(2,1)S(1)}, u32[]{:S(2)}, u32[]{:S(2)}) collective-permute-start(bf16[64,1280]{1,0:T(8,128)(2,1)} %refs_0_.2), channel_id=1, source_target_pairs={{0,16},{64,80},{128,144},{192,208},{16,0},{80,64},{144,128},{208,1... | collective-permute-start | bytes 491528 | tf_op jit(solution)/shard_map/ppermute | solution.py:41
  13.8 0.9 copy-start
  14.9 10.2 %collective-permute-start.4 = (bf16[128,1280]{1,0:T(8,128)(2,1)S(1)}, bf16[128,1280]{1,0:T(8,128)(2,1)S(1)}, u32[]{:S(2)}, u32[]{:S(2)}) collective-permute-start(bf16[128,1280]{1,0:T(8,128)(2,1)S(1)} %shard_map.58.refs_4_), channel_id=1, source_target_pairs={{0,32},{32,0},{1,33},{33,1},{2,34},{34,2},{3,35},{35,3},{4,36},{36... | collective-permute-start | bytes 983048 | tf_op jit(solution)/shard_map/ppermute | solution.py:45
  16.3 6.2 %collective-permute-start.1 = (bf16[64,1280]{1,0:T(8,128)(2,1)}, bf16[64,1280]{1,0:T(8,128)(2,1)S(1)}, u32[]{:S(2)}, u32[]{:S(2)}) collective-permute-start(bf16[64,1280]{1,0:T(8,128)(2,1)} %refs_0_.3), channel_id=1, source_target_pairs={{0,2},{1,3},{2,0},{3,1},{4,6},{5,7},{6,4},{7,5},{8,10},{9,11},{10,... | collective-permute-start | bytes 491528 | tf_op jit(solution)/shard_map/ppermute | solution.py:32
  19.2 5.9 %collective-permute-start = (bf16[64,1280]{1,0:T(8,128)(2,1)}, bf16[64,1280]{1,0:T(8,128)(2,1)S(1)}, u32[]{:S(2)}, u32[]{:S(2)}) collective-permute-start(bf16[64,1280]{1,0:T(8,128)(2,1)} %refs_0_.3), channel_id=1, source_target_pairs={{0,1},{1,2},{2,3},{3,0},{4,5},{5,6},{6,7},{7,4},{8,9},{9,10},{10,1... | collective-permute-start | bytes 491528 | tf_op jit(solution)/shard_map/ppermute | solution.py:32
  19.6 5.5 %collective-permute-start.2 = (bf16[64,1280]{1,0:T(8,128)(2,1)}, bf16[64,1280]{1,0:T(8,128)(2,1)S(1)}, u32[]{:S(2)}, u32[]{:S(2)}) collective-permute-start(bf16[64,1280]{1,0:T(8,128)(2,1)} %refs_0_.3), channel_id=1, source_target_pairs={{0,3},{1,0},{2,1},{3,2},{4,7},{5,4},{6,5},{7,6},{8,11},{9,8},{10,9... | collective-permute-start | bytes 491528 | tf_op jit(solution)/shard_map/ppermute | solution.py:32
  25.1 0.9 copy-start.1
  26.3 12.1 %collective-permute-start.8 = (bf16[256,1280]{1,0:T(8,128)(2,1)S(1)}, bf16[256,1280]{1,0:T(8,128)(2,1)S(1)}, u32[]{:S(2)}, u32[]{:S(2)}) collective-permute-start(bf16[256,1280]{1,0:T(8,128)(2,1)S(1)} %get-tuple-element.30.refs_4_.refs_0_), channel_id=1, source_target_pairs={{0,208},{64,0},{128,64},{192,128},{16,192},{80,16},{144,80},{208,1... | collective-permute-start | bytes 1966088 | tf_op jit(solution)/shard_map/ppermute | solution.py:41
  26.4 15.3 %collective-permute-start.10 = (bf16[128,1280]{1,0:T(8,128)(2,1)S(1)}, bf16[128,1280]{1,0:T(8,128)(2,1)}, u32[]{:S(2)}, u32[]{:S(2)}) collective-permute-start(bf16[128,1280]{1,0:T(8,128)(2,1)S(1)} %shard_map.58.refs_4_), channel_id=1, source_target_pairs={{0,144},{64,208},{128,0},{192,64},{16,128},{80,192},{144,16},{208,... | collective-permute-start | bytes 983048 | tf_op jit(solution)/shard_map/ppermute | solution.py:41
  31.2 19.2 %collective-permute-start.7 = (bf16[256,1280]{1,0:T(8,128)(2,1)S(1)}, bf16[256,1280]{1,0:T(8,128)(2,1)S(1)}, u32[]{:S(2)}, u32[]{:S(2)}) collective-permute-start(bf16[256,1280]{1,0:T(8,128)(2,1)S(1)} %get-tuple-element.29.refs_0_), channel_id=1, source_target_pairs={{0,12},{1,13},{2,14},{3,15},{4,0},{5,1},{6,2},{7,3},{8,4},{9,5},{1... | collective-permute-start | bytes 1966088 | tf_op jit(solution)/shard_map/ppermute | solution.py:32
  33.7 16.7 %collective-permute-start.6 = (bf16[256,1280]{1,0:T(8,128)(2,1)S(1)}, bf16[256,1280]{1,0:T(8,128)(2,1)S(1)}, u32[]{:S(2)}, u32[]{:S(2)}) collective-permute-start(bf16[256,1280]{1,0:T(8,128)(2,1)S(1)} %get-tuple-element.29.refs_0_), channel_id=1, source_target_pairs={{0,8},{1,9},{2,10},{3,11},{4,12},{5,13},{6,14},{7,15},{8,0},{9,1},... | collective-permute-start | bytes 1966088 | tf_op jit(solution)/shard_map/ppermute | solution.py:32
  33.9 18.1 %collective-permute-start.5 = (bf16[256,1280]{1,0:T(8,128)(2,1)S(1)}, bf16[256,1280]{1,0:T(8,128)(2,1)}, u32[]{:S(2)}, u32[]{:S(2)}) collective-permute-start(bf16[256,1280]{1,0:T(8,128)(2,1)S(1)} %get-tuple-element.29.refs_0_), channel_id=1, source_target_pairs={{0,4},{1,5},{2,6},{3,7},{4,8},{5,9},{6,10},{7,11},{8,12},{9,13},{1... | collective-permute-start | bytes 1966088 | tf_op jit(solution)/shard_map/ppermute | solution.py:32
  38.4 13.6 %collective-permute-start.9 = (bf16[256,1280]{1,0:T(8,128)(2,1)S(1)}, bf16[256,1280]{1,0:T(8,128)(2,1)}, u32[]{:S(2)}, u32[]{:S(2)}) collective-permute-start(bf16[256,1280]{1,0:T(8,128)(2,1)S(1)} %collective-permute-done.8.refs_5_.refs_1_), channel_id=1, source_target_pairs={{0,32},{32,0},{1,33},{33,1},{2,34},{34,2},{3,35},{35,3},{4,36},{36... | collective-permute-start | bytes 1966088 | tf_op jit(solution)/shard_map/ppermute | solution.py:45
  41.7 6.7 %collective-permute-start.11 = (bf16[128,1280]{1,0:T(8,128)(2,1)}, bf16[128,1280]{1,0:T(8,128)(2,1)}, u32[]{:S(2)}, u32[]{:S(2)}) collective-permute-start(bf16[128,1280]{1,0:T(8,128)(2,1)} %collective-permute-done.10.refs_0_), channel_id=1, source_target_pairs={{0,32},{32,0},{1,33},{33,1},{2,34},{34,2},{3,35},{35,3},{4,36},{36... | collective-permute-start | bytes 983048 | tf_op jit(solution)/shard_map/ppermute | solution.py:45
  57.6 3.1 %collective-permute-start.12 = (f32[24,128]{1,0:T(8,128)S(1)}, f32[24,128]{1,0:T(8,128)S(1)}, u32[]{:S(2)}, u32[]{:S(2)}) collective-permute-start(f32[24,128]{1,0:T(8,128)S(1)} %pad_maximum_fusion.4), channel_id=1, source_target_pairs={{0,32},{32,0},{1,33},{33,1},{2,34},{34,2},{3,35},{35,3},{4,36},{36... | collective-permute-start | bytes 36872 | tf_op jit(solution)/shard_map/ppermute | solution.py:45
  60.8 6.6 %collective-permute-start.13 = (f32[40,128]{1,0:T(8,128)S(1)}, f32[40,128]{1,0:T(8,128)S(1)}, u32[]{:S(2)}, u32[]{:S(2)}) collective-permute-start(f32[40,128]{1,0:T(8,128)S(1)} %pad_maximum_fusion), channel_id=1, source_target_pairs={{0,2},{1,3},{2,0},{3,1},{4,6},{5,7},{6,4},{7,5},{8,10},{9,11},{10,... | collective-permute-start | bytes 61448 | tf_op jit(solution)/shard_map/ppermute | solution.py:58
  67.5 3.6 %collective-permute-start.14 = (f32[40,128]{1,0:T(8,128)S(1)}, f32[40,128]{1,0:T(8,128)S(1)}, u32[]{:S(2)}, u32[]{:S(2)}) collective-permute-start(f32[40,128]{1,0:T(8,128)S(1)} %pad_maximum_fusion.1), channel_id=1, source_target_pairs={{0,1},{1,0},{2,3},{3,2},{4,5},{5,4},{6,7},{7,6},{8,9},{9,8},{10,11... | collective-permute-start | bytes 61448 | tf_op jit(solution)/shard_map/ppermute | solution.py:58
  71.2 2.7 %collective-permute-start.15 = (f32[40,128]{1,0:T(8,128)S(1)}, f32[40,128]{1,0:T(8,128)S(1)}, u32[]{:S(2)}, u32[]{:S(2)}) collective-permute-start(f32[40,128]{1,0:T(8,128)S(1)} %pad_maximum_fusion.2), channel_id=1, source_target_pairs={{0,8},{1,9},{2,10},{3,11},{4,12},{5,13},{6,14},{7,15},{8,0},{9,1},... | collective-permute-start | bytes 61448 | tf_op jit(solution)/shard_map/ppermute | solution.py:58
  73.9 0.7 collective-permute-start.16
  74.7 7.9 %collective-permute-start.22 = (f32[16,128]{1,0:T(8,128)S(1)}, f32[16,128]{1,0:T(8,128)S(1)}, u32[]{:S(2)}, u32[]{:S(2)}) collective-permute-start(f32[16,128]{1,0:T(8,128)S(1)} %slice_select_fusion), channel_id=1, source_target_pairs={{0,32},{32,0},{1,33},{33,1},{2,34},{34,2},{3,35},{35,3},{4,36},{36... | collective-permute-start | bytes 24584 | tf_op jit(solution)/shard_map/ppermute | solution.py:45
  89.0 8.1 %collective-permute-start.29 = (bf16[256,1280]{1,0:T(8,128)(2,1)S(1)}, bf16[256,1280]{1,0:T(8,128)(2,1)S(1)}, u32[]{:S(2)}, u32[]{:S(2)}) collective-permute-start(bf16[256,1280]{1,0:T(8,128)(2,1)S(1)} %get-tuple-element.46), channel_id=1, source_target_pairs={{0,32},{32,0},{1,33},{33,1},{2,34},{34,2},{3,35},{35,3},{4,36},{36... | collective-permute-start | bytes 1966088 | tf_op jit(solution)/shard_map/ppermute | solution.py:45
  89.4 7.7 %collective-permute-start.30 = (bf16[128,1280]{1,0:T(8,128)(2,1)S(1)}, bf16[128,1280]{1,0:T(8,128)(2,1)S(1)}, u32[]{:S(2)}, u32[]{:S(2)}) collective-permute-start(bf16[128,1280]{1,0:T(8,128)(2,1)S(1)} %get-tuple-element.48), channel_id=1, source_target_pairs={{0,32},{32,0},{1,33},{33,1},{2,34},{34,2},{3,35},{35,3},{4,36},{36... | collective-permute-start | bytes 983048 | tf_op jit(solution)/shard_map/ppermute | solution.py:45
  90.3 4.0 %collective-permute-start.17 = (f32[8,128]{1,0:T(8,128)S(1)}, f32[8,128]{1,0:T(8,128)S(1)}, u32[]{:S(2)}, u32[]{:S(2)}) collective-permute-start(f32[8,128]{1,0:T(8,128)S(1)} %shard_map.62), channel_id=1, source_target_pairs={{0,16},{1,17},{2,18},{3,19},{4,20},{5,21},{6,22},{7,23},{8,24},{9,... | collective-permute-start | bytes 12296 | tf_op jit(solution)/shard_map/ppermute | solution.py:58
  94.3 2.8 %collective-permute-start.18 = (f32[8,128]{1,0:T(8,128)S(1)}, f32[8,128]{1,0:T(8,128)S(1)}, u32[]{:S(2)}, u32[]{:S(2)}) collective-permute-start(f32[8,128]{1,0:T(8,128)S(1)} %add.72.after), channel_id=1, source_target_pairs={{0,128},{1,129},{2,130},{3,131},{4,132},{5,133},{6,134},{7,135},{8... | collective-permute-start | bytes 12296 | tf_op jit(solution)/shard_map/ppermute | solution.py:58
  97.3 20.9 %collective-permute-start.31 = (bf16[256,1280]{1,0:T(8,128)(2,1)S(1)}, bf16[256,1280]{1,0:T(8,128)(2,1)S(1)}, u32[]{:S(2)}, u32[]{:S(2)}) collective-permute-start(bf16[256,1280]{1,0:T(8,128)(2,1)S(1)} %get-tuple-element.49), channel_id=1, source_target_pairs={{0,64},{64,128},{128,192},{192,16},{16,80},{80,144},{144,208},{208... | collective-permute-start | bytes 1966088 | tf_op jit(solution)/shard_map/ppermute | solution.py:41
  102.7 17.7 %collective-permute-start.23 = (bf16[256,1280]{1,0:T(8,128)(2,1)S(1)}, bf16[256,1280]{1,0:T(8,128)(2,1)S(1)}, u32[]{:S(2)}, u32[]{:S(2)}) collective-permute-start(bf16[256,1280]{1,0:T(8,128)(2,1)S(1)} %get-tuple-element.37), channel_id=1, source_target_pairs={{0,8},{1,9},{2,10},{3,11},{4,12},{5,13},{6,14},{7,15},{8,0},{9,1},... | collective-permute-start | bytes 1966088 | tf_op jit(solution)/shard_map/ppermute | solution.py:32
  105.4 16.2 %collective-permute-start.24 = (bf16[256,1280]{1,0:T(8,128)(2,1)S(1)}, bf16[256,1280]{1,0:T(8,128)(2,1)S(1)}, u32[]{:S(2)}, u32[]{:S(2)}) collective-permute-start(bf16[256,1280]{1,0:T(8,128)(2,1)S(1)} %get-tuple-element.38), channel_id=1, source_target_pairs={{0,12},{1,13},{2,14},{3,15},{4,0},{5,1},{6,2},{7,3},{8,4},{9,5},{1... | collective-permute-start | bytes 1966088 | tf_op jit(solution)/shard_map/ppermute | solution.py:32
  105.8 15.8 %collective-permute-start.25 = (bf16[256,1280]{1,0:T(8,128)(2,1)S(1)}, bf16[256,1280]{1,0:T(8,128)(2,1)S(1)}, u32[]{:S(2)}, u32[]{:S(2)}) collective-permute-start(bf16[256,1280]{1,0:T(8,128)(2,1)S(1)} %get-tuple-element.39), channel_id=1, source_target_pairs={{0,4},{1,5},{2,6},{3,7},{4,8},{5,9},{6,10},{7,11},{8,12},{9,13},{1... | collective-permute-start | bytes 1966088 | tf_op jit(solution)/shard_map/ppermute | solution.py:32
  106.9 11.3 %collective-permute-start.32 = (bf16[128,1280]{1,0:T(8,128)(2,1)S(1)}, bf16[128,1280]{1,0:T(8,128)(2,1)S(1)}, u32[]{:S(2)}, u32[]{:S(2)}) collective-permute-start(bf16[128,1280]{1,0:T(8,128)(2,1)S(1)} %get-tuple-element.50), channel_id=1, source_target_pairs={{0,128},{64,192},{128,16},{192,80},{16,144},{80,208},{144,0},{208,... | collective-permute-start | bytes 983048 | tf_op jit(solution)/shard_map/ppermute | solution.py:41
  118.4 6.9 %collective-permute-start.33 = (bf16[128,1280]{1,0:T(8,128)(2,1)S(1)}, bf16[128,1280]{1,0:T(8,128)(2,1)S(1)}, u32[]{:S(2)}, u32[]{:S(2)}) collective-permute-start(bf16[128,1280]{1,0:T(8,128)(2,1)S(1)} %get-tuple-element.52), channel_id=1, source_target_pairs={{0,32},{32,0},{1,33},{33,1},{2,34},{34,2},{3,35},{35,3},{4,36},{36... | collective-permute-start | bytes 983048 | tf_op jit(solution)/shard_map/ppermute | solution.py:45
  121.9 23.4 %collective-permute-start.26 = (bf16[64,1280]{1,0:T(8,128)(2,1)S(1)}, bf16[64,1280]{1,0:T(8,128)(2,1)S(1)}, u32[]{:S(2)}, u32[]{:S(2)}) collective-permute-start(bf16[64,1280]{1,0:T(8,128)(2,1)S(1)} %get-tuple-element.41), channel_id=1, source_target_pairs={{0,2},{1,3},{2,0},{3,1},{4,6},{5,7},{6,4},{7,5},{8,10},{9,11},{10,... | collective-permute-start | bytes 491528 | tf_op jit(solution)/shard_map/ppermute | solution.py:32
  123.8 21.5 %collective-permute-start.27 = (bf16[64,1280]{1,0:T(8,128)(2,1)S(1)}, bf16[64,1280]{1,0:T(8,128)(2,1)S(1)}, u32[]{:S(2)}, u32[]{:S(2)}) collective-permute-start(bf16[64,1280]{1,0:T(8,128)(2,1)S(1)} %get-tuple-element.42), channel_id=1, source_target_pairs={{0,3},{1,0},{2,1},{3,2},{4,7},{5,4},{6,5},{7,6},{8,11},{9,8},{10,9... | collective-permute-start | bytes 491528 | tf_op jit(solution)/shard_map/ppermute | solution.py:32
  124.1 21.2 %collective-permute-start.28 = (bf16[64,1280]{1,0:T(8,128)(2,1)S(1)}, bf16[64,1280]{1,0:T(8,128)(2,1)S(1)}, u32[]{:S(2)}, u32[]{:S(2)}) collective-permute-start(bf16[64,1280]{1,0:T(8,128)(2,1)S(1)} %get-tuple-element.43), channel_id=1, source_target_pairs={{0,1},{1,2},{2,3},{3,0},{4,5},{5,6},{6,7},{7,4},{8,9},{9,10},{10,1... | collective-permute-start | bytes 491528 | tf_op jit(solution)/shard_map/ppermute | solution.py:32
  125.4 20.7 %collective-permute-start.34 = (bf16[64,1280]{1,0:T(8,128)(2,1)S(1)}, bf16[64,1280]{1,0:T(8,128)(2,1)S(1)}, u32[]{:S(2)}, u32[]{:S(2)}) collective-permute-start(bf16[64,1280]{1,0:T(8,128)(2,1)S(1)} %get-tuple-element.54), channel_id=1, source_target_pairs={{0,16},{64,80},{128,144},{192,208},{16,0},{80,64},{144,128},{208,1... | collective-permute-start | bytes 491528 | tf_op jit(solution)/shard_map/ppermute | solution.py:41
  129.3 4.0 %collective-permute-start.19 = (f32[8,128]{1,0:T(8,128)S(1)}, f32[8,128]{1,0:T(8,128)S(1)}, u32[]{:S(2)}, u32[]{:S(2)}) collective-permute-start(f32[8,128]{1,0:T(8,128)S(1)} %add.73.refs_4_), channel_id=1, source_target_pairs={{0,64},{1,65},{2,66},{3,67},{4,68},{5,69},{6,70},{7,71},{8,72},{9,... | collective-permute-start | bytes 12296 | tf_op jit(solution)/shard_map/ppermute | solution.py:58
  133.3 4.3 %collective-permute-start.20 = (f32[8,128]{1,0:T(8,128)S(1)}, f32[8,128]{1,0:T(8,128)S(1)}, u32[]{:S(2)}, u32[]{:S(2)}) collective-permute-start(f32[8,128]{1,0:T(8,128)S(1)} %add.74), channel_id=1, source_target_pairs={{32,36},{33,37},{34,38},{35,39},{36,32},{37,33},{38,34},{39,35},{4... | collective-permute-start | bytes 12296 | tf_op jit(solution)/shard_map/ppermute | solution.py:58
  137.6 7.2 %collective-permute-start.21 = (f32[8,128]{1,0:T(8,128)S(1)}, f32[8,128]{1,0:T(8,128)S(1)}, u32[]{:S(2)}, u32[]{:S(2)}) collective-permute-start(f32[8,128]{1,0:T(8,128)S(1)} %add.75.a), channel_id=1, source_target_pairs={{0,32},{32,0},{1,33},{33,1},{2,34},{34,2},{3,35},{35,3},{4,36},{36... | collective-permute-start | bytes 12296 | tf_op jit(solution)/shard_map/ppermute | solution.py:45

commit v4 on v3

--- a/solution.py
+++ b/solution.py
@@ -13,7 +13,7 @@
 BF16, F32 = jnp.bfloat16, jnp.float32
 VMEM = pl.BlockSpec(memory_space=pltpu.VMEM)
 SMEM = pl.BlockSpec(memory_space=pltpu.SMEM)
-ANY = pl.BlockSpec(memory_space=pl.ANY)
+HBM = pl.BlockSpec(memory_space=pltpu.HBM)
 PARAMS = pltpu.CompilerParams(vmem_limit_bytes=12 * 1024 * 1024)
 
 
@@ -45,26 +45,26 @@
     return lax.ppermute(v, "core", [(0, 1), (1, 0)])
 
 
-def split_move(v, to_0, to_1):
-    pairs = []
-    for c, to in ((0, to_0), (1, to_1)):
-        if to is None:
-            continue
-        for z in range(NZ):
-            for y in range(NY):
-                for x in range(NX):
-                    ty, tx, tz = to(y, x, z)
-                    pairs.append((device(c, y, x, z), device(c, ty % NY, tx % NX, tz % NZ)))
-    return lax.ppermute(v, AXES, pairs)
-
-
 def device(c, y, x, z):
     return ((((z % 4) * 2 + c) * 2 + z // 4) * NY + y) * NX + x
 
 
-def lse2(a, b):
-    top = jnp.maximum(a, b)
-    return top + jnp.log(jnp.exp(a - top) + jnp.exp(b - top))
+def groups(plane_core):
+    out = []
+    for c in range(2):
+        if c == plane_core:
+            out += [[device(c, y, x, z) for y in range(NY) for x in range(NX)] for z in range(NZ)]
+        else:
+            out += [
+                [device(c, y + d, x, z) for z in range(NZ) for d in (0, 2)]
+                for y in range(2)
+                for x in range(NX)
+            ]
+    return out
+
+
+def exchange(v, plane_core):
+    return lax.all_to_all(v, AXES, 0, 0, axis_index_groups=groups(plane_core))
 
 
 def row_place(where, a, b):
@@ -76,9 +76,10 @@
 
 def col_place(where, j, i):
     zl, c, zh, y, x = where
-    core = c if (i < 2) == (j != 2) else 1 - c
+    core = c if (i % 2 == 0) == (j < 2) else 1 - c
     sign = 1 - 2 * c
-    off = sign * ((0, 1, -1, 2 if i < 2 else -2)[j]) + 4 * (i % 2)
+    off = ((0, 0, 1, 1), (2, 2, 3, 3), (-2, -2, -3, -3), (-1, -1, 4, 4))[j][i]
+    off = 4 if off == 4 else sign * off
     z = (zh * 4 + zl + off) & 7
     return z * 2 + core, ((z >> 2) * 16 + y * 4 + x) * 8 + (z & 3) * 2 + core
 
@@ -98,42 +99,41 @@
     return out
 
 
-def pack_body(counts, *refs):
-    n = sum(counts)
+def pack_body(plan, n, *refs):
     outs, sem = refs[n:-1], refs[-1]
-    at = 0
     local_copy = None
-    for count, out in zip(counts, outs):
+    for parts, out in zip(plan, outs):
         row = 0
-        for r in refs[at : at + count]:
-            rows = out.at[row : row + r.shape[0], :]
-            if at == 0 and row == 0:
-                local_copy = pltpu.make_async_copy(r, rows, sem)
+        for i, skip, rows in parts:
+            into = out.at[row : row + rows, :]
+            if i == 0:
+                local_copy = pltpu.make_async_copy(refs[i], into, sem)
                 local_copy.start()
             else:
-                rows[...] = r[...]
-            row += r.shape[0]
-        at += count
+                into[...] = refs[i][skip : skip + rows, :]
+            row += rows
     local_copy.wait()
 
 
-def pack(*groups):
-    parts = [p for g in groups for p in g]
-    shapes = [jax.ShapeDtypeStruct((sum(p.shape[0] for p in g), EMBED), BF16) for g in groups]
-    return pl.pallas_call(
-        lambda *refs: pack_body([len(g) for g in groups], *refs),
+def pack(arrays, *plan):
+    shapes = [jax.ShapeDtypeStruct((sum(p[2] for p in parts), EMBED), BF16) for parts in plan]
+    return pl.pallas_call(
+        lambda *refs: pack_body(plan, len(arrays), *refs),
         out_shape=tuple(shapes),
-        in_specs=[ANY] + [VMEM] * (len(parts) - 1),
-        out_specs=(VMEM,) * len(groups),
+        in_specs=[HBM] + [VMEM] * (len(arrays) - 1),
+        out_specs=(VMEM,) * len(plan),
         scratch_shapes=[pltpu.SemaphoreType.DMA],
         compiler_params=PARAMS,
-    )(*parts)
+    )(*arrays)
 
 
 def logits_body(place, scale, *refs):
-    images, texts = refs[:4], refs[4:8]
-    logits, row_out, col_out, match_out = refs[8:12]
-    row_wide = refs[12]
+    images = refs[:4]
+    texts = (*refs[4:7], refs[14])
+    logits, row_out, col_out, message, match_out, text_3 = refs[9:15]
+    row_wide = refs[15]
+    text_3[: 3 * ROWS, :] = refs[7][...]
+    text_3[3 * ROWS :, :] = refs[8][...]
     where = [place[i] for i in range(5)]
     multiplier = scale[0]
     for a in range(4):
@@ -171,9 +171,9 @@
                     matched += jnp.sum(hit.reshape(step // 8, 8, 128), axis=0)
                 part = top + jnp.log(jnp.sum(total, axis=1, keepdims=True))
                 row_wide[at : at + step, :] = jnp.broadcast_to(part, (step, 128))
-    match_out[...] = jnp.broadcast_to(jnp.sum(matched, keepdims=True), (8, 128))
-    col_out[...] = jnp.zeros((16, 128), F32)
-    row_out[...] = jnp.zeros((16, 128), F32)
+    matched = jnp.broadcast_to(jnp.sum(matched, keepdims=True), (8, 128))
+    match_out[...] = matched
+    message[16:24, :] = matched
     for t in range(8):
         top = jnp.max(col_top[t], axis=0, keepdims=True)
 
@@ -189,6 +189,7 @@
         line = jnp.transpose(row_wide[t * 128 : (t + 1) * 128, :])[0:1]
         row_out[pl.ds(row_place(where, j, i)[0], 1), :] = line
         row_out[pl.ds(row_place(where, j, i + 1)[0], 1), :] = pltpu.roll(line, 64, 1)
+    message[:16, :] = jnp.where(where[1] == 0, col_out[...], row_out[...])
 
 
 def logits_call(place, scale, images, texts):
@@ -198,20 +199,103 @@
             jax.ShapeDtypeStruct((BLOCK, BLOCK), F32),
             jax.ShapeDtypeStruct((16, 128), F32),
             jax.ShapeDtypeStruct((16, 128), F32),
+            jax.ShapeDtypeStruct((24, 128), F32),
+            jax.ShapeDtypeStruct((8, 128), F32),
+            PART,
+        ),
+        in_specs=[SMEM, SMEM] + [VMEM] * 9,
+        out_specs=(VMEM,) * 6,
+        scratch_shapes=[pltpu.VMEM((BLOCK, 128), F32)],
+        compiler_params=PARAMS,
+    )(place, scale, *images, *texts)
+
+
+def spread_body(place, row, col, matched, got, out):
+    first = place[1] == 0
+    mine, other = row[...], got[:16, :]
+    top = jnp.maximum(col[...], other)
+    both = top + jnp.log(jnp.exp(col[...] - top) + jnp.exp(other - top))
+    hits = matched[...] + got[16:24, :]
+    for i in range(16):
+        out[i, :16, :] = jnp.where(first, mine, both)
+        out[i, 16:32, :] = jnp.where(first, other, both)
+        out[i, 32:40, :] = hits
+
+
+def spread_call(place, *parts):
+    return pl.pallas_call(
+        spread_body,
+        out_shape=jax.ShapeDtypeStruct((16, 40, 128), F32),
+        in_specs=[SMEM] + [VMEM] * 4,
+        out_specs=VMEM,
+        compiler_params=PARAMS,
+    )(place, *parts)
+
+
+def in_ring(place, i, plane_core):
+    return jnp.logical_or(place[1] == plane_core, (place[3] >> 1) == i % 2)
+
+
+def join_body(place, got, mine, message, share):
+    first = place[1] == 0
+    parts = [jnp.where(in_ring(place, i, 0), got[i, :32, :], -jnp.inf) for i in range(16)]
+    top = parts[0]
+    for p in parts[1:]:
+        top = jnp.maximum(top, p)
+    total = jnp.exp(parts[0] - top)
+    for p in parts[1:]:
+        total += jnp.exp(p - top)
+    state = top + jnp.log(total)
+    hits = got[0, 32:40, :]
+    for i in range(1, 16):
+        hits += got[i, 32:40, :]
+    mine[...] = state[:16]
+    message[...] = jnp.where(first, state[16:], state[:16])
+    real = lax.broadcasted_iota(jnp.int32, (16, 128), 1) < ROWS
+    both = jnp.where(real, state[:16] + jnp.where(first, state[16:], 0.0), 0.0)
+    share[...] = jnp.sum(both, keepdims=True) - jnp.where(first, 2.0 * hits, 0.0)
+
+
+def join_call(place, got):
+    return pl.pallas_call(
+        join_body,
+        out_shape=(
+            jax.ShapeDtypeStruct((16, 128), F32),
+            jax.ShapeDtypeStruct((16, 128), F32),
             jax.ShapeDtypeStruct((8, 128), F32),
         ),
-        in_specs=[SMEM, SMEM] + [VMEM] * 8,
-        out_specs=(VMEM,) * 4,
-        scratch_shapes=[pltpu.VMEM((BLOCK, 128), F32)],
-        compiler_params=PARAMS,
-    )(place, scale, *images, *texts)
-
-
-def weights_body(place, scale, logits, row_lse, col_lse, *refs):
+        in_specs=[SMEM, VMEM],
+        out_specs=(VMEM,) * 3,
+        compiler_params=PARAMS,
+    )(place, got)
+
+
+def loss_body(place, got, out):
+    total = None
+    for i in range(16):
+        v = jnp.where(in_ring(place, i, 1), got[i], 0.0)
+        total = v if total is None else total + v
+    out[...] = total
+
+
+def loss_call(place, got):
+    return pl.pallas_call(
+        loss_body,
+        out_shape=jax.ShapeDtypeStruct((8, 128), F32),
+        in_specs=[SMEM, VMEM],
+        out_specs=VMEM,
+        compiler_params=PARAMS,
+    )(place, got)
+
+
+def weights_body(place, scale, logits, mine, other, *refs):
     images = refs[:4]
     weights = refs[4]
     outs = refs[5:9]
-    row_wide = refs[9]
+    row_wide, row_lse, col_lse = refs[9:12]
+    first = place[1] == 0
+    row_lse[...] = jnp.where(first, mine[...], other[...])
+    col_lse[...] = jnp.where(first, other[...], mine[...])
     where = [place[i] for i in range(5)]
     multiplier = scale[0]
     lane = lax.broadcasted_iota(jnp.int32, (1, 128), 1)
@@ -236,7 +320,7 @@
                 both = 0.5 * jnp.exp(tile - wide) + 0.5 * jnp.exp(tile - col_line[t])
                 both = both - jnp.where(ids[b] == cols[t][0:1], 1.0, 0.0)
                 weights[at : at + ROWS, t * 128 : (t + 1) * 128] = both.astype(BF16)
-    text_terms(multiplier, weights, images, ((2, 0, outs[0]), (3, 128, outs[1]), (3, 0, outs[2]), (1, 0, outs[3])))
+    text_terms(multiplier, weights, images, ((2, 0, outs[0]), (3, 0, outs[1]), (1, 0, outs[2]), (3, 3 * ROWS, outs[3])))
 
 
 def text_terms(multiplier, weights, images, outs):
@@ -272,48 +356,57 @@
 PART = jax.ShapeDtypeStruct((CHUNK, EMBED), BF16)
 
 
-HALF = jax.ShapeDtypeStruct((CHUNK // 2, EMBED), BF16)
-
-
-def weights_call(place, scale, logits, row_lse, col_lse, images):
+def weights_call(place, scale, logits, mine, other, images):
     return pl.pallas_call(
         weights_body,
-        out_shape=(jax.ShapeDtypeStruct((BLOCK, BLOCK), BF16), PART, HALF, HALF, PART),
+        out_shape=(
+            jax.ShapeDtypeStruct((BLOCK, BLOCK), BF16),
+            PART,
+            jax.ShapeDtypeStruct((3 * ROWS, EMBED), BF16),
+            PART,
+            jax.ShapeDtypeStruct((ROWS, EMBED), BF16),
+        ),
         in_specs=[SMEM, SMEM] + [VMEM] * 7,
         out_specs=(VMEM,) * 5,
-        scratch_shapes=[pltpu.VMEM((BLOCK, 128), F32)],
-        compiler_params=PARAMS,
-    )(place, scale, logits, row_lse, col_lse, *images)
-
-
-def image_body(scale, after, weights, *refs):
+        scratch_shapes=[
+            pltpu.VMEM((BLOCK, 128), F32),
+            pltpu.VMEM((16, 128), F32),
+            pltpu.VMEM((16, 128), F32),
+        ],
+        compiler_params=PARAMS,
+    )(place, scale, logits, mine, other, *images)
+
+
+def image_body(scale, weights, *refs):
     image_terms(scale[0], weights, refs[:4], dict(zip((2, 1, 3), refs[4:])))
 
 
-def image_call(scale, after, weights, texts):
+def image_call(scale, weights, texts):
     return pl.pallas_call(
         image_body,
         out_shape=(PART,) * 3,
-        in_specs=[SMEM] + [VMEM] * 6,
+        in_specs=[SMEM] + [VMEM] * 5,
         out_specs=(VMEM,) * 3,
         compiler_params=PARAMS,
-    )(scale, after, weights, *texts)
-
-
-def rest_body(scale, weights, *refs):
+    )(scale, weights, *texts)
+
+
+def rest_body(scale, share, weights, *refs):
     images, texts, outs = refs[:4], refs[4:8], refs[8:]
     text_terms(scale[0], weights, images, ((0, 0, outs[0]),))
     image_terms(scale[0], weights, texts, {0: outs[1]})
-
-
-def rest_call(scale, weights, images, texts):
+    for i in range(16):
+        outs[2][i] = share[...]
+
+
+def rest_call(scale, share, weights, images, texts):
     return pl.pallas_call(
         rest_body,
-        out_shape=(PART,) * 2,
-        in_specs=[SMEM] + [VMEM] * 9,
-        out_specs=(VMEM,) * 2,
-        compiler_params=PARAMS,
-    )(scale, weights, *images, *texts)
+        out_shape=(PART, PART, jax.ShapeDtypeStruct((16, 8, 128), F32)),
+        in_specs=[SMEM] + [VMEM] * 10,
+        out_specs=(VMEM,) * 3,
+        compiler_params=PARAMS,
+    )(scale, share, weights, *images, *texts)
 
 
 def sums_body(n, plan, *refs):
@@ -337,26 +430,6 @@
     return out if len(plan) > 1 else out[0]
 
 
-def share_body(place, state, out):
-    real = lax.broadcasted_iota(jnp.int32, (16, 128), 1) < ROWS
-    both = jnp.where(real, state[:16, :], 0.0)
-    more = jnp.where(real, state[16:32, :], 0.0)
-    first = place[1] == 0
-    both = both + jnp.where(first, more, 0.0)
-    total = jnp.sum(both, keepdims=True) - jnp.where(first, 2.0, 0.0) * state[32:33, 0:1]
-    out[...] = jnp.broadcast_to(total, (8, 128))
-
-
-def share_call(place, state):
-    return pl.pallas_call(
-        share_body,
-        out_shape=jax.ShapeDtypeStruct((8, 128), F32),
-        in_specs=[SMEM, VMEM],
-        out_specs=VMEM,
-        compiler_params=PARAMS,
-    )(place, state)
-
-
 def mean_body(a, b, out):
     out[...] = (a[0:1, 0:1] + b[0:1, 0:1]) * (1.0 / (2.0 * ROWS * 256))
 
@@ -374,60 +447,53 @@
 def local(image_emb, text_emb, logit_scale):
     place = jnp.stack([lax.axis_index(n) for n in AXES]).astype(jnp.int32)
 
-    far = z_shift(text_emb, 4)
+    (chip,) = pack([text_emb, core_swap(text_emb)], ((0, 0, 64), (1, 0, 64)))
+    next_1, next_4 = z_shift(chip, -1), z_shift(text_emb, 4)
     near = [plane_shift(image_emb, k, True) for k in (1, 2, 3)]
-    (pair,) = pack([text_emb, far])
-    own, text_0 = pack([image_emb] + near, [pair, core_swap(pair)])
-    text_1 = z_shift(text_0, -1)
-    text_3 = z_shift(pair, -2)
+    own, text_0, side = pack(
+        [image_emb] + near + [chip, next_1, next_4],
+        ((0, 0, 64), (1, 0, 64), (2, 0, 64), (3, 0, 64)),
+        ((4, 0, 128), (5, 0, 128)),
+        ((5, 0, 128), (6, 0, 64)),
+    )
+    text_1, text_3 = z_shift(text_0, -2), core_swap(side)
     images = [own] + [plane_shift(own, k, False) for k in (1, 2, 3)]
-    (text_3,) = pack([text_3, core_swap(text_3)])
-    texts = [text_0, text_1, core_swap(text_1), text_3]
-
-    logits, row_part, col_part, matched = logits_call(place, logit_scale, images, texts)
-
-    first = place[1] == 0
-    got = core_swap(jnp.concatenate([jnp.where(first, col_part, row_part), matched]))
-    rows_first = jnp.concatenate([row_part, got[:16]])
-    cols_first = jnp.concatenate([lse2(col_part, got[:16])] * 2)
-    state = jnp.concatenate([jnp.where(first, rows_first, cols_first), matched + got[16:]])
-    for to_0, to_1 in (
-        (lambda y, x, z: (y, x ^ 2, z), lambda y, x, z: (y, x, z ^ 4)),
-        (lambda y, x, z: (y, x ^ 1, z), lambda y, x, z: (y, x, z ^ 2)),
-        (lambda y, x, z: (y ^ 2, x, z), lambda y, x, z: (y, x, z ^ 1)),
-        (lambda y, x, z: (y ^ 1, x, z), None),
-    ):
-        other = split_move(state, to_0, to_1)
-        joined = jnp.concatenate([lse2(state[:32], other[:32]), state[32:] + other[32:]])
-        state = joined if to_1 is not None else jnp.where(first, joined, state)
-    got = core_swap(jnp.where(first, state[16:32], state[:16]))
-    row_lse = jnp.where(first, state[:16], got)
-    col_lse = jnp.where(first, got, state[:16])
-
-    s = share_call(place, state)
-    s_1 = s + split_move(s, lambda y, x, z: (y, x, z ^ 4), lambda y, x, z: (y, x ^ 2, z))
-    s_2 = s_1 + split_move(s_1, lambda y, x, z: (y, x, z ^ 2), lambda y, x, z: (y, x ^ 1, z))
-    s = s_2 + split_move(s_2, lambda y, x, z: (y, x, z ^ 1), lambda y, x, z: (y ^ 2, x, z))
-    s = s + split_move(s, None, lambda y, x, z: (y ^ 1, x, z))
+    texts = [text_0, text_1, core_swap(text_1)]
+
+    logits, row_part, col_part, message, matched, text_3 = logits_call(
+        place, logit_scale, images, texts + [text_3, next_4]
+    )
+    texts.append(text_3)
+
+    spread = spread_call(place, row_part, col_part, matched, core_swap(message))
+    mine, message, share = join_call(place, exchange(spread, 0))
+    weights, text_2, text_3, text_1, far = weights_call(
+        place, logit_scale, logits, mine, core_swap(message), images
+    )
+
+    other_1, other_3 = core_swap(text_2), core_swap(text_3)
+    pairs, far = sums(
+        [text_1, other_1, far, other_3], (256, ((0, 0), (1, 0))), (64, ((2, 0), (3, 128)))
+    )
+    pairs = z_shift(pairs, 2)
+    image_parts = image_call(logit_scale, weights, texts)
+    back = [plane_shift(v, -k, False) for v, k in zip(image_parts, (2, 1, 3))]
+    text_0, image_0, shares = rest_call(logit_scale, share, weights, images, texts)
+
+    s = loss_call(place, exchange(shares, 1))
     mean_loss = mean_call(s, core_swap(s)).reshape(1)
 
-    weights, text_2, text_3b, text_3a, text_1 = weights_call(
-        place, logit_scale, logits, row_lse, col_lse, images
+    next_1, mine, *pieces = sums(
+        [text_0, other_3, pairs, image_0] + back + [s],
+        (128, ((0, 128), (1, 0), (2, 128))),
+        (128, ((0, 0), (2, 0))),
+        *[(64, [(i, 64 * k) for i in range(3, 7)]) for k in range(4)],
     )
-    near, far = core_swap(text_2), core_swap(text_3b)
-    image_parts = image_call(logit_scale, s_1, weights, texts)
-    near, far = sums([text_1, near, text_3a, far, s_2], (256, ((0, 0), (1, 0))), (128, ((2, 0), (3, 0))))
-    near, far = z_shift(near, 1), z_shift(far, 2)
-    back = [plane_shift(v, -k, False) for v, k in zip(image_parts, (2, 1, 3))]
-    text_0, image_0 = rest_call(logit_scale, weights, images, texts)
-    mine, other = sums(
-        [text_0, near, far], (128, ((0, 0), (1, 0), (2, 0))), (128, ((0, 128), (1, 128)))
-    )
-    mine, far = sums([mine, core_swap(other)], (64, ((0, 0), (1, 0))), (64, ((0, 64), (1, 64))))
-    pieces = sums([image_0] + back, *[(64, [(i, 64 * k) for i in range(4)]) for k in range(4)])
+    next_1, next_4 = z_shift(next_1, 1), z_shift(far, 4)
     shards = [pieces[0]] + [plane_shift(pieces[k], -k, True) for k in (2, 1, 3)]
+    mine, other = sums([mine, next_1], (64, ((0, 0), (1, 0))), (64, ((0, 64), (1, 64))))
     image_grad = sums(shards, (64, [(i, 0) for i in range(4)]))
-    text_grad = sums([mine, z_shift(far, 4)], (64, ((0, 0), (1, 0))))
+    text_grad = sums([mine, core_swap(other), next_4], (64, ((0, 0), (1, 0), (2, 0))))
     return mean_loss, image_grad, text_grad
 
 

time: 147 us -> 135 us (0.918)
  the two profiles are of different devices: /device:TPU:65 before, /device:TPU:8 now
where the time goes in v4:
time: 135 us
  starting transfers between devices  39.2 us (29%)
  blocking collectives  34.5 us (26%)
  waiting for transfers between devices  34.1 us (25%)
  Pallas kernels  24 us (18%)
  local copies, waits for them, and re-layouts  1.91 us (1%)
  between operations  1.45 us (1%)
    all_to_all x2, blocking collectives, exchange(): return lax.all_to_all(v, AXES, 0, 0, axis_index_groups=groups(plane_core))  34.5 us
    ppermute x6, waiting for transfers between devices, z_shift(): return lax.ppermute(v, ('zl', 'core', 'zh'), pairs)  21.8 us
    ppermute x12, starting transfers between devices, plane_shift(): return lax.ppermute(v, ('core', 'zh', 'y', 'x'), pairs)  19.8 us
    ppermute x6, starting transfers between devices, z_shift(): return lax.ppermute(v, ('zl', 'core', 'zh'), pairs)  13.2 us
    pallas_call x1, Pallas kernels, weights_call(): pl.pallas_call(weights_body, out_shape=(jax.ShapeDtypeStruct((BLOCK, BLOC...  7.46 us
    ppermute x12, waiting for transfers between devices, plane_shift(): return lax.ppermute(v, ('core', 'zh', 'y', 'x'), pairs)  7.17 us
    ppermute x9, starting transfers between devices, core_swap(): return lax.ppermute(v, 'core', [(0, 1), (1, 0)])  6.27 us
    pallas_call x1, Pallas kernels, logits_call(): pl.pallas_call(logits_body, out_shape=(jax.ShapeDtypeStruct((BLOCK, BLOCK...  5.55 us
  transfers between devices with their start and end apart: 27, of which 10 were waited for; matrix products, arithmetic and copies ran while one was open for 0% of the time, Pallas kernels for 5%

profile of v4, /device:TPU:8, one launch (start us, length us, event | category | flops | bytes accessed | tf_op | source)
XLA Modules:
  0.0 135.1 jit_solution(18385946343303929782)
XLA Ops:
  0.6 0.1 collective-permute-start.3
  0.7 1.6 %collective-permute-done.3.refs_1_ = bf16[64,1280]{1,0:T(8,128)(2,1)S(1)} collective-permute-done((bf16[64,1280]{1,0:T(8,128)(2,1)}, bf16[64,1280]{1,0:T(8,128)(2,1)S(1)}, u32[]{:S(2)}, u32[]{:S(2)}) %collective-permute-start.3) | collective-permute-done | bytes 163872 | tf_op jit(solution)/shard_map/ppermute | solution.py:45
  2.3 0.9 copy-done
  3.2 0.2 shard_map.58.refs_4_
  3.4 5.9 %collective-permute-start.4 = (bf16[128,1280]{1,0:T(8,128)(2,1)S(1)}, bf16[128,1280]{1,0:T(8,128)(2,1)S(1)}, u32[]{:S(2)}, u32[]{:S(2)}) collective-permute-start(bf16[128,1280]{1,0:T(8,128)(2,1)S(1)} %shard_map.58.refs_4_), channel_id=1, source_target_pairs={{0,208},{64,0},{128,64},{192,128},{16,192},{80,16},{144,80},{208,1... | collective-permute-start | bytes 983048 | tf_op jit(solution)/shard_map/ppermute | solution.py:41
  9.4 1.4 %collective-permute-start.5 = (bf16[64,1280]{1,0:T(8,128)(2,1)S(1)}, bf16[64,1280]{1,0:T(8,128)(2,1)S(1)}, u32[]{:S(2)}, u32[]{:S(2)}) collective-permute-start(bf16[64,1280]{1,0:T(8,128)(2,1)S(1)} %copy-done), channel_id=1, source_target_pairs={{0,16},{64,80},{128,144},{192,208},{16,0},{80,64},{144,128},{208,1... | collective-permute-start | bytes 491528 | tf_op jit(solution)/shard_map/ppermute | solution.py:41
  10.8 3.0 %collective-permute-start.1 = (bf16[64,1280]{1,0:T(8,128)(2,1)}, bf16[64,1280]{1,0:T(8,128)(2,1)S(1)}, u32[]{:S(2)}, u32[]{:S(2)}) collective-permute-start(bf16[64,1280]{1,0:T(8,128)(2,1)} %refs_0_.3), channel_id=1, source_target_pairs={{0,2},{1,3},{2,0},{3,1},{4,6},{5,7},{6,4},{7,5},{8,10},{9,11},{10,... | collective-permute-start | bytes 491528 | tf_op jit(solution)/shard_map/ppermute | solution.py:32
  13.8 0.6 collective-permute-start
  14.4 2.6 %collective-permute-start.2 = (bf16[64,1280]{1,0:T(8,128)(2,1)}, bf16[64,1280]{1,0:T(8,128)(2,1)S(1)}, u32[]{:S(2)}, u32[]{:S(2)}) collective-permute-start(bf16[64,1280]{1,0:T(8,128)(2,1)} %refs_0_.3), channel_id=1, source_target_pairs={{0,3},{1,0},{2,1},{3,2},{4,7},{5,4},{6,5},{7,6},{8,11},{9,8},{10,9... | collective-permute-start | bytes 491528 | tf_op jit(solution)/shard_map/ppermute | solution.py:32
  17.1 4.8 %collective-permute-done.5.refs_6_.refs_8_ = bf16[64,1280]{1,0:T(8,128)(2,1)S(1)} collective-permute-done((bf16[64,1280]{1,0:T(8,128)(2,1)S(1)}, bf16[64,1280]{1,0:T(8,128)(2,1)S(1)}, u32[]{:S(2)}, u32[]{:S(2)}) %collective-permute-start.5) | collective-permute-done | bytes 163872 | tf_op jit(solution)/shard_map/ppermute | solution.py:41
  21.9 0.0 collective-permute-done.refs_1_
  21.9 0.0 collective-permute-done.2.refs_3_
  21.9 0.0 collective-permute-done.4.refs_5_
  21.9 0.9 copy-done.1
  22.8 1.1 shard_map.59
  23.9 2.5 %collective-permute-start.9 = (bf16[256,1280]{1,0:T(8,128)(2,1)S(1)}, bf16[256,1280]{1,0:T(8,128)(2,1)S(1)}, u32[]{:S(2)}, u32[]{:S(2)}) collective-permute-start(bf16[256,1280]{1,0:T(8,128)(2,1)S(1)} %get-tuple-element.37.refs_4_.refs_0_), channel_id=1, source_target_pairs={{0,144},{64,208},{128,0},{192,64},{16,128},{80,192},{144,16},{208,... | collective-permute-start | bytes 1966088 | tf_op jit(solution)/shard_map/ppermute | solution.py:41
  26.5 0.4 collective-permute-start.8
  26.9 2.6 %collective-permute-start.7 = (bf16[256,1280]{1,0:T(8,128)(2,1)S(1)}, bf16[256,1280]{1,0:T(8,128)(2,1)}, u32[]{:S(2)}, u32[]{:S(2)}) collective-permute-start(bf16[256,1280]{1,0:T(8,128)(2,1)S(1)} %get-tuple-element.36.refs_0_), channel_id=1, source_target_pairs={{0,8},{1,9},{2,10},{3,11},{4,12},{5,13},{6,14},{7,15},{8,0},{9,1},... | collective-permute-start | bytes 1966088 | tf_op jit(solution)/shard_map/ppermute | solution.py:32
  29.5 1.9 %collective-permute-start.6 = (bf16[256,1280]{1,0:T(8,128)(2,1)S(1)}, bf16[256,1280]{1,0:T(8,128)(2,1)}, u32[]{:S(2)}, u32[]{:S(2)}) collective-permute-start(bf16[256,1280]{1,0:T(8,128)(2,1)S(1)} %get-tuple-element.36.refs_0_), channel_id=1, source_target_pairs={{0,4},{1,5},{2,6},{3,7},{4,8},{5,9},{6,10},{7,11},{8,12},{9,13},{1... | collective-permute-start | bytes 1966088 | tf_op jit(solution)/shard_map/ppermute | solution.py:32
  31.4 7.7 %collective-permute-done.9.refs_5_.refs_1_ = bf16[256,1280]{1,0:T(8,128)(2,1)S(1)} collective-permute-done((bf16[256,1280]{1,0:T(8,128)(2,1)S(1)}, bf16[256,1280]{1,0:T(8,128)(2,1)S(1)}, u32[]{:S(2)}, u32[]{:S(2)}) %collective-permute-start.9) | collective-permute-done | bytes 655392 | tf_op jit(solution)/shard_map/ppermute | solution.py:41
  39.1 1.7 %collective-permute-start.10 = (bf16[256,1280]{1,0:T(8,128)(2,1)S(1)}, bf16[256,1280]{1,0:T(8,128)(2,1)S(1)}, u32[]{:S(2)}, u32[]{:S(2)}) collective-permute-start(bf16[256,1280]{1,0:T(8,128)(2,1)S(1)} %collective-permute-done.9.refs_5_.refs_1_), channel_id=1, source_target_pairs={{0,32},{32,0},{1,33},{33,1},{2,34},{34,2},{3,35},{35,3},{4,36},{36... | collective-permute-start | bytes 1966088 | tf_op jit(solution)/shard_map/ppermute | solution.py:45
  40.8 0.0 collective-permute-start.11
  41.5 0.1 stack.23.place
  41.6 1.9 %collective-permute-done.11.refs_7_ = bf16[192,1280]{1,0:T(8,128)(2,1)} collective-permute-done((bf16[192,1280]{1,0:T(8,128)(2,1)}, bf16[192,1280]{1,0:T(8,128)(2,1)}, u32[]{:S(2)}, u32[]{:S(2)}) %collective-permute-start.11) | collective-permute-done | bytes 491552 | tf_op jit(solution)/shard_map/ppermute | solution.py:45
  43.5 1.7 %collective-permute-done.7.refs_2_ = bf16[256,1280]{1,0:T(8,128)(2,1)} collective-permute-done((bf16[256,1280]{1,0:T(8,128)(2,1)S(1)}, bf16[256,1280]{1,0:T(8,128)(2,1)}, u32[]{:S(2)}, u32[]{:S(2)}) %collective-permute-start.7) | collective-permute-done | bytes 655392 | tf_op jit(solution)/shard_map/ppermute | solution.py:32
  45.2 1.1 collective-permute-done.6.refs_1_
  46.3 5.6 %shard_map.60 = (f32[1024,1024]{1,0:T(8,128)S(1)}, f32[16,128]{1,0:T(8,128)S(1)}, f32[16,128]{1,0:T(8,128)S(1)}, f32[24,128]{1,0:T(8,128)S(1)}, f32[8,128]{1,0:T(8,128)S(1)}, /*index=5*/bf16[256,1280]{1,0:T(8,128)(2,1)S(1)}) custom-call(s32[5]{0:T(128)S(1)} %stack.23.place, f32[1]{0:T(128)S(6)} %copy.6.scale, ...), custom_call_target="tpu_custom_call" | custom-call | tf_op jit(solution)/shard_map/pallas_call | solution.py:196
  51.8 0.6 collective-permute-start.12
  52.5 0.8 collective-permute-done.12.got
  53.3 0.6 shard_map.61
  53.9 14.3 %all_to_all.10.got = f32[16,40,128]{2,1,0:T(8,128)S(1)} all-to-all(f32[16,40,128]{2,1,0:T(8,128)S(1)} %shard_map.61), channel_id=1, replica_groups={{0,1,2,3,4,5,6,7,8,9,10,11,12,13,14,15},{64,65,66,67,68,69,70,71,72,73,..., dimensions={0} | all-to-all | bytes 655360 | tf_op jit(solution)/shard_map/all_to_all | solution.py:67
  68.2 0.7 shard_map.62
  68.9 3.1 %collective-permute-start.13 = (f32[16,128]{1,0:T(8,128)S(1)}, f32[16,128]{1,0:T(8,128)S(1)}, u32[]{:S(2)}, u32[]{:S(2)}) collective-permute-start(f32[16,128]{1,0:T(8,128)S(1)} %get-tuple-element.46), channel_id=1, source_target_pairs={{0,32},{32,0},{1,33},{33,1},{2,34},{34,2},{3,35},{35,3},{4,36},{36... | collective-permute-start | bytes 24584 | tf_op jit(solution)/shard_map/ppermute | solution.py:45
  72.1 0.8 collective-permute-done.13.other
  72.9 7.5 %shard_map.63 = (bf16[1024,1024]{1,0:T(8,128)(2,1)S(1)}, bf16[256,1280]{1,0:T(8,128)(2,1)S(1)}, bf16[192,1280]{1,0:T(8,128)(2,1)S(1)}, bf16[256,1280]{1,0:T(8,128)(2,1)S(1)}, bf16[64,1280]{1,0:T(8,128)(2,1)S(1)}) custom-call(s32[5]{0:T(128)S(1)} %stack.23.place, f32[1]{0:T(128)S(6)} %copy.6.scale, f32[1024,1024]{1,0:T(8,128)S(1)} %get-tuple-element.44.logits, ...), custom_call_target="tpu_custom_call" | custom-call | tf_op jit(solution)/shard_map/pallas_call | solution.py:360
  80.4 0.4 collective-permute-start.16
  80.8 0.2 collective-permute-start.15
  81.0 2.2 %shard_map.68 = (bf16[256,1280]{1,0:T(8,128)(2,1)S(1)}, bf16[256,1280]{1,0:T(8,128)(2,1)S(1)}, bf16[256,1280]{1,0:T(8,128)(2,1)S(1)}) custom-call(f32[1]{0:T(128)S(6)} %copy.6.scale, bf16[1024,1024]{1,0:T(8,128)(2,1)S(1)} %get-tuple-element.47.weights, bf16[256,1280]{1,0:T(8,128)(2,1)S(1)} %get-tuple-element.37.refs_4_.refs_0_, ...), custom_call_target="tpu_custom_call" | custom-call | tf_op jit(solution)/shard_map/pallas_call | solution.py:385
  83.2 0.6 collective-permute-start.18
  83.8 1.3 collective-permute-start.19
  85.1 1.0 collective-permute-start.20
  86.1 0.0 collective-permute-done.15.refs_3_.refs_1_
  86.1 0.0 collective-permute-done.16.refs_1_
  86.1 0.2 shard_map.67
  86.3 1.3 collective-permute-start.17
  87.6 2.9 %shard_map.64 = (bf16[256,1280]{1,0:T(8,128)(2,1)S(1)}, bf16[256,1280]{1,0:T(8,128)(2,1)S(1)}, f32[16,8,128]{2,1,0:T(8,128)S(1)}) custom-call(f32[1]{0:T(128)S(6)} %copy.6.scale, f32[8,128]{1,0:T(8,128)S(1)} %get-tuple-element.43.share, bf16[1024,1024]{1,0:T(8,128)(2,1)S(1)} %get-tuple-element.47.weights, bf16[256,1280]{1,0:T(8,128)(2,1)S(1)} %get-tuple-element.36.refs_0_, ...), custom_call_target="tpu_custom_call" | custom-call | tf_op jit(solution)/shard_map/pallas_call | solution.py:403
  90.4 20.2 %all_to_all.11.got = f32[16,8,128]{2,1,0:T(8,128)S(1)} all-to-all(f32[16,8,128]{2,1,0:T(8,128)S(1)} %get-tuple-element.49), channel_id=1, replica_groups={{0,8,64,72,128,136,192,200,16,24,80,88,144,152,208,216},{1,9,65,73,129,..., dimensions={0} | all-to-all | bytes 131072 | tf_op jit(solution)/shard_map/all_to_all | solution.py:67
  110.6 0.6 shard_map.65.a.refs_7_
  111.2 0.0 collective-permute-done.18.refs_4_
  111.2 0.0 collective-permute-done.17.refs_2_
  111.2 0.5 shard_map.69
  111.7 0.3 collective-permute-start.24
  112.0 0.0 collective-permute-start.14
  112.0 1.7 %collective-permute-start.26 = (bf16[64,1280]{1,0:T(8,128)(2,1)S(1)}, bf16[64,1280]{1,0:T(8,128)(2,1)S(1)}, u32[]{:S(2)}, u32[]{:S(2)}) collective-permute-start(bf16[64,1280]{1,0:T(8,128)(2,1)S(1)} %get-tuple-element.68), channel_id=1, source_target_pairs={{0,16},{64,80},{128,144},{192,208},{16,0},{80,64},{144,128},{208,1... | collective-permute-start | bytes 491528 | tf_op jit(solution)/shard_map/ppermute | solution.py:41
  113.7 3.0 %collective-permute-start.21 = (bf16[64,1280]{1,0:T(8,128)(2,1)S(1)}, bf16[64,1280]{1,0:T(8,128)(2,1)S(1)}, u32[]{:S(2)}, u32[]{:S(2)}) collective-permute-start(bf16[64,1280]{1,0:T(8,128)(2,1)S(1)} %get-tuple-element.61), channel_id=1, source_target_pairs={{0,2},{1,3},{2,0},{3,1},{4,6},{5,7},{6,4},{7,5},{8,10},{9,11},{10,... | collective-permute-start | bytes 491528 | tf_op jit(solution)/shard_map/ppermute | solution.py:32
  116.7 1.1 collective-permute-start.22
  117.9 9.2 %collective-permute-done.24.refs_1_ = bf16[128,1280]{1,0:T(8,128)(2,1)S(1)} collective-permute-done((bf16[128,1280]{1,0:T(8,128)(2,1)S(1)}, bf16[128,1280]{1,0:T(8,128)(2,1)S(1)}, u32[]{:S(2)}, u32[]{:S(2)}) %collective-permute-start.24) | collective-permute-done | bytes 327712 | tf_op jit(solution)/shard_map/ppermute | solution.py:41
  127.1 1.5 %collective-permute-start.23 = (bf16[64,1280]{1,0:T(8,128)(2,1)S(1)}, bf16[64,1280]{1,0:T(8,128)(2,1)S(1)}, u32[]{:S(2)}, u32[]{:S(2)}) collective-permute-start(bf16[64,1280]{1,0:T(8,128)(2,1)S(1)} %get-tuple-element.63), channel_id=1, source_target_pairs={{0,1},{1,2},{2,3},{3,0},{4,5},{5,6},{6,7},{7,4},{8,9},{9,10},{10,1... | collective-permute-start | bytes 491528 | tf_op jit(solution)/shard_map/ppermute | solution.py:32
  128.6 0.1 shard_map.71
  128.7 0.1 collective-permute-start.25
  128.8 0.5 shard_map.66
  129.3 4.3 %collective-permute-done.23.refs_3_ = bf16[64,1280]{1,0:T(8,128)(2,1)S(1)} collective-permute-done((bf16[64,1280]{1,0:T(8,128)(2,1)S(1)}, bf16[64,1280]{1,0:T(8,128)(2,1)S(1)}, u32[]{:S(2)}, u32[]{:S(2)}) %collective-permute-start.23) | collective-permute-done | bytes 163872 | tf_op jit(solution)/shard_map/ppermute | solution.py:32
  133.7 0.7 shard_map.70
  134.4 0.7 shard_map.72
  (12 shorter events, 0.0 us)
Async XLA Ops:
  0.6 1.7 %collective-permute-start.3 = (bf16[64,1280]{1,0:T(8,128)(2,1)}, bf16[64,1280]{1,0:T(8,128)(2,1)S(1)}, u32[]{:S(2)}, u32[]{:S(2)}) collective-permute-start(bf16[64,1280]{1,0:T(8,128)(2,1)} %refs_0_.2), channel_id=1, source_target_pairs={{0,32},{32,0},{1,33},{33,1},{2,34},{34,2},{3,35},{35,3},{4,36},{36... | collective-permute-start | bytes 491528 | tf_op jit(solution)/shard_map/ppermute | solution.py:45
  2.3 0.9 copy-start
  3.4 18.5 %collective-permute-start.4 = (bf16[128,1280]{1,0:T(8,128)(2,1)S(1)}, bf16[128,1280]{1,0:T(8,128)(2,1)S(1)}, u32[]{:S(2)}, u32[]{:S(2)}) collective-permute-start(bf16[128,1280]{1,0:T(8,128)(2,1)S(1)} %shard_map.58.refs_4_), channel_id=1, source_target_pairs={{0,208},{64,0},{128,64},{192,128},{16,192},{80,16},{144,80},{208,1... | collective-permute-start | bytes 983048 | tf_op jit(solution)/shard_map/ppermute | solution.py:41
  9.4 12.5 %collective-permute-start.5 = (bf16[64,1280]{1,0:T(8,128)(2,1)S(1)}, bf16[64,1280]{1,0:T(8,128)(2,1)S(1)}, u32[]{:S(2)}, u32[]{:S(2)}) collective-permute-start(bf16[64,1280]{1,0:T(8,128)(2,1)S(1)} %copy-done), channel_id=1, source_target_pairs={{0,16},{64,80},{128,144},{192,208},{16,0},{80,64},{144,128},{208,1... | collective-permute-start | bytes 491528 | tf_op jit(solution)/shard_map/ppermute | solution.py:41
  10.8 11.1 %collective-permute-start.1 = (bf16[64,1280]{1,0:T(8,128)(2,1)}, bf16[64,1280]{1,0:T(8,128)(2,1)S(1)}, u32[]{:S(2)}, u32[]{:S(2)}) collective-permute-start(bf16[64,1280]{1,0:T(8,128)(2,1)} %refs_0_.3), channel_id=1, source_target_pairs={{0,2},{1,3},{2,0},{3,1},{4,6},{5,7},{6,4},{7,5},{8,10},{9,11},{10,... | collective-permute-start | bytes 491528 | tf_op jit(solution)/shard_map/ppermute | solution.py:32
  13.8 8.0 %collective-permute-start = (bf16[64,1280]{1,0:T(8,128)(2,1)}, bf16[64,1280]{1,0:T(8,128)(2,1)S(1)}, u32[]{:S(2)}, u32[]{:S(2)}) collective-permute-start(bf16[64,1280]{1,0:T(8,128)(2,1)} %refs_0_.3), channel_id=1, source_target_pairs={{0,1},{1,2},{2,3},{3,0},{4,5},{5,6},{6,7},{7,4},{8,9},{9,10},{10,1... | collective-permute-start | bytes 491528 | tf_op jit(solution)/shard_map/ppermute | solution.py:32
  14.4 7.5 %collective-permute-start.2 = (bf16[64,1280]{1,0:T(8,128)(2,1)}, bf16[64,1280]{1,0:T(8,128)(2,1)S(1)}, u32[]{:S(2)}, u32[]{:S(2)}) collective-permute-start(bf16[64,1280]{1,0:T(8,128)(2,1)} %refs_0_.3), channel_id=1, source_target_pairs={{0,3},{1,0},{2,1},{3,2},{4,7},{5,4},{6,5},{7,6},{8,11},{9,8},{10,9... | collective-permute-start | bytes 491528 | tf_op jit(solution)/shard_map/ppermute | solution.py:32
  21.9 0.9 copy-start.1
  23.9 15.2 %collective-permute-start.9 = (bf16[256,1280]{1,0:T(8,128)(2,1)S(1)}, bf16[256,1280]{1,0:T(8,128)(2,1)S(1)}, u32[]{:S(2)}, u32[]{:S(2)}) collective-permute-start(bf16[256,1280]{1,0:T(8,128)(2,1)S(1)} %get-tuple-element.37.refs_4_.refs_0_), channel_id=1, source_target_pairs={{0,144},{64,208},{128,0},{192,64},{16,128},{80,192},{144,16},{208,... | collective-permute-start | bytes 1966088 | tf_op jit(solution)/shard_map/ppermute | solution.py:41
  26.5 17.0 %collective-permute-start.8 = (bf16[256,1280]{1,0:T(8,128)(2,1)S(1)}, bf16[256,1280]{1,0:T(8,128)(2,1)S(1)}, u32[]{:S(2)}, u32[]{:S(2)}) collective-permute-start(bf16[256,1280]{1,0:T(8,128)(2,1)S(1)} %get-tuple-element.36.refs_0_), channel_id=1, source_target_pairs={{0,12},{1,13},{2,14},{3,15},{4,0},{5,1},{6,2},{7,3},{8,4},{9,5},{1... | collective-permute-start | bytes 1966088 | tf_op jit(solution)/shard_map/ppermute | solution.py:32
  26.9 18.3 %collective-permute-start.7 = (bf16[256,1280]{1,0:T(8,128)(2,1)S(1)}, bf16[256,1280]{1,0:T(8,128)(2,1)}, u32[]{:S(2)}, u32[]{:S(2)}) collective-permute-start(bf16[256,1280]{1,0:T(8,128)(2,1)S(1)} %get-tuple-element.36.refs_0_), channel_id=1, source_target_pairs={{0,8},{1,9},{2,10},{3,11},{4,12},{5,13},{6,14},{7,15},{8,0},{9,1},... | collective-permute-start | bytes 1966088 | tf_op jit(solution)/shard_map/ppermute | solution.py:32
  29.5 16.8 %collective-permute-start.6 = (bf16[256,1280]{1,0:T(8,128)(2,1)S(1)}, bf16[256,1280]{1,0:T(8,128)(2,1)}, u32[]{:S(2)}, u32[]{:S(2)}) collective-permute-start(bf16[256,1280]{1,0:T(8,128)(2,1)S(1)} %get-tuple-element.36.refs_0_), channel_id=1, source_target_pairs={{0,4},{1,5},{2,6},{3,7},{4,8},{5,9},{6,10},{7,11},{8,12},{9,13},{1... | collective-permute-start | bytes 1966088 | tf_op jit(solution)/shard_map/ppermute | solution.py:32
  39.1 7.2 %collective-permute-start.10 = (bf16[256,1280]{1,0:T(8,128)(2,1)S(1)}, bf16[256,1280]{1,0:T(8,128)(2,1)S(1)}, u32[]{:S(2)}, u32[]{:S(2)}) collective-permute-start(bf16[256,1280]{1,0:T(8,128)(2,1)S(1)} %collective-permute-done.9.refs_5_.refs_1_), channel_id=1, source_target_pairs={{0,32},{32,0},{1,33},{33,1},{2,34},{34,2},{3,35},{35,3},{4,36},{36... | collective-permute-start | bytes 1966088 | tf_op jit(solution)/shard_map/ppermute | solution.py:45
  40.8 2.6 %collective-permute-start.11 = (bf16[192,1280]{1,0:T(8,128)(2,1)}, bf16[192,1280]{1,0:T(8,128)(2,1)}, u32[]{:S(2)}, u32[]{:S(2)}) collective-permute-start(bf16[192,1280]{1,0:T(8,128)(2,1)} %get-tuple-element.38), channel_id=1, source_target_pairs={{0,32},{32,0},{1,33},{33,1},{2,34},{34,2},{3,35},{35,3},{4,36},{36... | collective-permute-start | bytes 1474568 | tf_op jit(solution)/shard_map/ppermute | solution.py:45
  51.8 1.5 %collective-permute-start.12 = (f32[24,128]{1,0:T(8,128)S(1)}, f32[24,128]{1,0:T(8,128)S(1)}, u32[]{:S(2)}, u32[]{:S(2)}) collective-permute-start(f32[24,128]{1,0:T(8,128)S(1)} %get-tuple-element.42), channel_id=1, source_target_pairs={{0,32},{32,0},{1,33},{33,1},{2,34},{34,2},{3,35},{35,3},{4,36},{36... | collective-permute-start | bytes 36872 | tf_op jit(solution)/shard_map/ppermute | solution.py:45
  68.9 4.0 %collective-permute-start.13 = (f32[16,128]{1,0:T(8,128)S(1)}, f32[16,128]{1,0:T(8,128)S(1)}, u32[]{:S(2)}, u32[]{:S(2)}) collective-permute-start(f32[16,128]{1,0:T(8,128)S(1)} %get-tuple-element.46), channel_id=1, source_target_pairs={{0,32},{32,0},{1,33},{33,1},{2,34},{34,2},{3,35},{35,3},{4,36},{36... | collective-permute-start | bytes 24584 | tf_op jit(solution)/shard_map/ppermute | solution.py:45
  80.4 5.7 %collective-permute-start.16 = (bf16[256,1280]{1,0:T(8,128)(2,1)S(1)}, bf16[256,1280]{1,0:T(8,128)(2,1)S(1)}, u32[]{:S(2)}, u32[]{:S(2)}) collective-permute-start(bf16[256,1280]{1,0:T(8,128)(2,1)S(1)} %get-tuple-element.53), channel_id=1, source_target_pairs={{0,32},{32,0},{1,33},{33,1},{2,34},{34,2},{3,35},{35,3},{4,36},{36... | collective-permute-start | bytes 1966088 | tf_op jit(solution)/shard_map/ppermute | solution.py:45
  80.8 5.3 %collective-permute-start.15 = (bf16[192,1280]{1,0:T(8,128)(2,1)S(1)}, bf16[192,1280]{1,0:T(8,128)(2,1)S(1)}, u32[]{:S(2)}, u32[]{:S(2)}) collective-permute-start(bf16[192,1280]{1,0:T(8,128)(2,1)S(1)} %get-tuple-element.51), channel_id=1, source_target_pairs={{0,32},{32,0},{1,33},{33,1},{2,34},{34,2},{3,35},{35,3},{4,36},{36... | collective-permute-start | bytes 1474568 | tf_op jit(solution)/shard_map/ppermute | solution.py:45
  83.2 28.0 %collective-permute-start.18 = (bf16[256,1280]{1,0:T(8,128)(2,1)S(1)}, bf16[256,1280]{1,0:T(8,128)(2,1)S(1)}, u32[]{:S(2)}, u32[]{:S(2)}) collective-permute-start(bf16[256,1280]{1,0:T(8,128)(2,1)S(1)} %get-tuple-element.57), channel_id=1, source_target_pairs={{0,8},{1,9},{2,10},{3,11},{4,12},{5,13},{6,14},{7,15},{8,0},{9,1},... | collective-permute-start | bytes 1966088 | tf_op jit(solution)/shard_map/ppermute | solution.py:32
  83.8 27.4 %collective-permute-start.19 = (bf16[256,1280]{1,0:T(8,128)(2,1)S(1)}, bf16[256,1280]{1,0:T(8,128)(2,1)S(1)}, u32[]{:S(2)}, u32[]{:S(2)}) collective-permute-start(bf16[256,1280]{1,0:T(8,128)(2,1)S(1)} %get-tuple-element.58), channel_id=1, source_target_pairs={{0,12},{1,13},{2,14},{3,15},{4,0},{5,1},{6,2},{7,3},{8,4},{9,5},{1... | collective-permute-start | bytes 1966088 | tf_op jit(solution)/shard_map/ppermute | solution.py:32
  85.1 26.1 %collective-permute-start.20 = (bf16[256,1280]{1,0:T(8,128)(2,1)S(1)}, bf16[256,1280]{1,0:T(8,128)(2,1)S(1)}, u32[]{:S(2)}, u32[]{:S(2)}) collective-permute-start(bf16[256,1280]{1,0:T(8,128)(2,1)S(1)} %get-tuple-element.59), channel_id=1, source_target_pairs={{0,4},{1,5},{2,6},{3,7},{4,8},{5,9},{6,10},{7,11},{8,12},{9,13},{1... | collective-permute-start | bytes 1966088 | tf_op jit(solution)/shard_map/ppermute | solution.py:32
  86.3 24.9 %collective-permute-start.17 = (bf16[256,1280]{1,0:T(8,128)(2,1)S(1)}, bf16[256,1280]{1,0:T(8,128)(2,1)S(1)}, u32[]{:S(2)}, u32[]{:S(2)}) collective-permute-start(bf16[256,1280]{1,0:T(8,128)(2,1)S(1)} %get-tuple-element.55), channel_id=1, source_target_pairs={{0,128},{64,192},{128,16},{192,80},{16,144},{80,208},{144,0},{208,... | collective-permute-start | bytes 1966088 | tf_op jit(solution)/shard_map/ppermute | solution.py:41
  111.7 15.4 %collective-permute-start.24 = (bf16[128,1280]{1,0:T(8,128)(2,1)S(1)}, bf16[128,1280]{1,0:T(8,128)(2,1)S(1)}, u32[]{:S(2)}, u32[]{:S(2)}) collective-permute-start(bf16[128,1280]{1,0:T(8,128)(2,1)S(1)} %get-tuple-element.65), channel_id=1, source_target_pairs={{0,64},{64,128},{128,192},{192,16},{16,80},{80,144},{144,208},{208... | collective-permute-start | bytes 983048 | tf_op jit(solution)/shard_map/ppermute | solution.py:41
  112.0 16.7 %collective-permute-start.14 = (f32[8,128]{1,0:T(8,128)S(1)}, f32[8,128]{1,0:T(8,128)S(1)}, u32[]{:S(2)}, u32[]{:S(2)}) collective-permute-start(f32[8,128]{1,0:T(8,128)S(1)} %shard_map.65.a.refs_7_), channel_id=1, source_target_pairs={{0,32},{32,0},{1,33},{33,1},{2,34},{34,2},{3,35},{35,3},{4,36},{36... | collective-permute-start | bytes 12296 | tf_op jit(solution)/shard_map/ppermute | solution.py:45
  112.0 22.4 %collective-permute-start.26 = (bf16[64,1280]{1,0:T(8,128)(2,1)S(1)}, bf16[64,1280]{1,0:T(8,128)(2,1)S(1)}, u32[]{:S(2)}, u32[]{:S(2)}) collective-permute-start(bf16[64,1280]{1,0:T(8,128)(2,1)S(1)} %get-tuple-element.68), channel_id=1, source_target_pairs={{0,16},{64,80},{128,144},{192,208},{16,0},{80,64},{144,128},{208,1... | collective-permute-start | bytes 491528 | tf_op jit(solution)/shard_map/ppermute | solution.py:41
  113.7 15.6 %collective-permute-start.21 = (bf16[64,1280]{1,0:T(8,128)(2,1)S(1)}, bf16[64,1280]{1,0:T(8,128)(2,1)S(1)}, u32[]{:S(2)}, u32[]{:S(2)}) collective-permute-start(bf16[64,1280]{1,0:T(8,128)(2,1)S(1)} %get-tuple-element.61), channel_id=1, source_target_pairs={{0,2},{1,3},{2,0},{3,1},{4,6},{5,7},{6,4},{7,5},{8,10},{9,11},{10,... | collective-permute-start | bytes 491528 | tf_op jit(solution)/shard_map/ppermute | solution.py:32
  116.7 12.6 %collective-permute-start.22 = (bf16[64,1280]{1,0:T(8,128)(2,1)S(1)}, bf16[64,1280]{1,0:T(8,128)(2,1)S(1)}, u32[]{:S(2)}, u32[]{:S(2)}) collective-permute-start(bf16[64,1280]{1,0:T(8,128)(2,1)S(1)} %get-tuple-element.62), channel_id=1, source_target_pairs={{0,3},{1,0},{2,1},{3,2},{4,7},{5,4},{6,5},{7,6},{8,11},{9,8},{10,9... | collective-permute-start | bytes 491528 | tf_op jit(solution)/shard_map/ppermute | solution.py:32
  127.1 6.5 %collective-permute-start.23 = (bf16[64,1280]{1,0:T(8,128)(2,1)S(1)}, bf16[64,1280]{1,0:T(8,128)(2,1)S(1)}, u32[]{:S(2)}, u32[]{:S(2)}) collective-permute-start(bf16[64,1280]{1,0:T(8,128)(2,1)S(1)} %get-tuple-element.63), channel_id=1, source_target_pairs={{0,1},{1,2},{2,3},{3,0},{4,5},{5,6},{6,7},{7,4},{8,9},{9,10},{10,1... | collective-permute-start | bytes 491528 | tf_op jit(solution)/shard_map/ppermute | solution.py:32
  128.7 5.7 %collective-permute-start.25 = (bf16[64,1280]{1,0:T(8,128)(2,1)S(1)}, bf16[64,1280]{1,0:T(8,128)(2,1)S(1)}, u32[]{:S(2)}, u32[]{:S(2)}) collective-permute-start(bf16[64,1280]{1,0:T(8,128)(2,1)S(1)} %get-tuple-element.67), channel_id=1, source_target_pairs={{0,32},{32,0},{1,33},{33,1},{2,34},{34,2},{3,35},{35,3},{4,36},{36... | collective-permute-start | bytes 491528 | tf_op jit(solution)/shard_map/ppermute | solution.py:45

commit v5 on v4

--- a/solution.py
+++ b/solution.py
@@ -1,3 +1,5 @@
+import math
+
 import jax
 import jax.numpy as jnp
 from jax import lax
@@ -11,9 +13,9 @@
 CHUNK = 4 * ROWS
 BLOCK = 16 * ROWS
 BF16, F32 = jnp.bfloat16, jnp.float32
+LOG2E, LN2 = math.log2(math.e), math.log(2.0)
 VMEM = pl.BlockSpec(memory_space=pltpu.VMEM)
 SMEM = pl.BlockSpec(memory_space=pltpu.SMEM)
-HBM = pl.BlockSpec(memory_space=pltpu.HBM)
 PARAMS = pltpu.CompilerParams(vmem_limit_bytes=12 * 1024 * 1024)
 
 
@@ -49,22 +51,21 @@
     return ((((z % 4) * 2 + c) * 2 + z // 4) * NY + y) * NX + x
 
 
-def groups(plane_core):
-    out = []
-    for c in range(2):
-        if c == plane_core:
-            out += [[device(c, y, x, z) for y in range(NY) for x in range(NX)] for z in range(NZ)]
-        else:
-            out += [
-                [device(c, y + d, x, z) for z in range(NZ) for d in (0, 2)]
-                for y in range(2)
-                for x in range(NX)
-            ]
-    return out
-
-
-def exchange(v, plane_core):
-    return lax.all_to_all(v, AXES, 0, 0, axis_index_groups=groups(plane_core))
+def plane_or_ring():
+    out = [[device(0, y, x, z) for y in range(NY) for x in range(NX)] for z in range(NZ)]
+    return out + [
+        [device(1, y + d, x, z) for z in range(NZ) for d in (0, 2)] for y in range(2) for x in range(NX)
+    ]
+
+
+def slanted():
+    return [
+        [device(c, p // 4, p % 4, (g + p // 2) % NZ) for p in range(16)] for c in range(2) for g in range(NZ)
+    ]
+
+
+def exchange(v, groups):
+    return lax.all_to_all(v, AXES, 0, 0, axis_index_groups=groups)
 
 
 def row_place(where, a, b):
@@ -100,42 +101,34 @@
 
 
 def pack_body(plan, n, *refs):
-    outs, sem = refs[n:-1], refs[-1]
-    local_copy = None
-    for parts, out in zip(plan, outs):
+    for parts, out in zip(plan, refs[n:]):
         row = 0
-        for i, skip, rows in parts:
-            into = out.at[row : row + rows, :]
-            if i == 0:
-                local_copy = pltpu.make_async_copy(refs[i], into, sem)
-                local_copy.start()
-            else:
-                into[...] = refs[i][skip : skip + rows, :]
+        for i, rows in parts:
+            out[row : row + rows, :] = refs[i][...]
             row += rows
-    local_copy.wait()
 
 
 def pack(arrays, *plan):
-    shapes = [jax.ShapeDtypeStruct((sum(p[2] for p in parts), EMBED), BF16) for parts in plan]
+    shapes = [jax.ShapeDtypeStruct((sum(p[1] for p in parts), EMBED), BF16) for parts in plan]
     return pl.pallas_call(
         lambda *refs: pack_body(plan, len(arrays), *refs),
         out_shape=tuple(shapes),
-        in_specs=[HBM] + [VMEM] * (len(arrays) - 1),
+        in_specs=[VMEM] * len(arrays),
         out_specs=(VMEM,) * len(plan),
-        scratch_shapes=[pltpu.SemaphoreType.DMA],
         compiler_params=PARAMS,
     )(*arrays)
 
 
 def logits_body(place, scale, *refs):
     images = refs[:4]
-    texts = (*refs[4:7], refs[14])
-    logits, row_out, col_out, message, match_out, text_3 = refs[9:15]
-    row_wide = refs[15]
-    text_3[: 3 * ROWS, :] = refs[7][...]
-    text_3[3 * ROWS :, :] = refs[8][...]
+    texts = (*refs[4:7], refs[15])
+    logits, row_out, col_out, message, match_out, text_3 = refs[10:16]
+    row_wide = refs[16]
+    text_3[: 2 * ROWS, :] = refs[7][...]
+    text_3[2 * ROWS : 3 * ROWS, :] = refs[8][...]
+    text_3[3 * ROWS :, :] = refs[9][...]
     where = [place[i] for i in range(5)]
-    multiplier = scale[0]
+    multiplier = scale[0] * LOG2E
     for a in range(4):
         for j in range(4):
             logits[a * CHUNK : (a + 1) * CHUNK, j * CHUNK : (j + 1) * CHUNK] = (
@@ -164,12 +157,12 @@
                 mine = ids[b][half * step : (half + 1) * step]
                 total = jnp.zeros((step, 128), F32)
                 for t in range(8):
-                    total += jnp.exp(tiles[t] - top)
+                    total += jnp.exp2(tiles[t] - top)
                     folded = tiles[t].reshape(step // 8, 8, 128)
                     col_top[t] = jnp.maximum(col_top[t], jnp.max(folded, axis=0))
                     hit = jnp.where(mine == cols[t][0:1], tiles[t], 0.0)
                     matched += jnp.sum(hit.reshape(step // 8, 8, 128), axis=0)
-                part = top + jnp.log(jnp.sum(total, axis=1, keepdims=True))
+                part = top + LOG2E * jnp.log(jnp.sum(total, axis=1, keepdims=True))
                 row_wide[at : at + step, :] = jnp.broadcast_to(part, (step, 128))
     matched = jnp.broadcast_to(jnp.sum(matched, keepdims=True), (8, 128))
     match_out[...] = matched
@@ -179,10 +172,10 @@
 
         def cols_pass(i, total, t=t, top=top):
             tile = logits[pl.ds(pl.multiple_of(i * 128, 128), 128), t * 128 : (t + 1) * 128]
-            return total + jnp.sum(jnp.exp(tile - top).reshape(16, 8, 128), axis=0)
+            return total + jnp.sum(jnp.exp2(tile - top).reshape(16, 8, 128), axis=0)
 
         total = lax.fori_loop(0, 8, cols_pass, jnp.zeros((8, 128), F32), unroll=True)
-        part = top + jnp.log(jnp.sum(total, axis=0, keepdims=True))
+        part = top + LOG2E * jnp.log(jnp.sum(total, axis=0, keepdims=True))
         j, i = t // 2, (t % 2) * 2
         col_out[pl.ds(col_place(where, j, i)[0], 1), :] = part
         col_out[pl.ds(col_place(where, j, i + 1)[0], 1), :] = pltpu.roll(part, 64, 1)
@@ -203,7 +196,7 @@
             jax.ShapeDtypeStruct((8, 128), F32),
             PART,
         ),
-        in_specs=[SMEM, SMEM] + [VMEM] * 9,
+        in_specs=[SMEM, SMEM] + [VMEM] * 10,
         out_specs=(VMEM,) * 6,
         scratch_shapes=[pltpu.VMEM((BLOCK, 128), F32)],
         compiler_params=PARAMS,
@@ -214,7 +207,7 @@
     first = place[1] == 0
     mine, other = row[...], got[:16, :]
     top = jnp.maximum(col[...], other)
-    both = top + jnp.log(jnp.exp(col[...] - top) + jnp.exp(other - top))
+    both = top + LOG2E * jnp.log(jnp.exp2(col[...] - top) + jnp.exp2(other - top))
     hits = matched[...] + got[16:24, :]
     for i in range(16):
         out[i, :16, :] = jnp.where(first, mine, both)
@@ -232,56 +225,53 @@
     )(place, *parts)
 
 
-def in_ring(place, i, plane_core):
-    return jnp.logical_or(place[1] == plane_core, (place[3] >> 1) == i % 2)
-
-
-def join_body(place, got, mine, message, share):
+def join_body(place, got, mine, message):
     first = place[1] == 0
-    parts = [jnp.where(in_ring(place, i, 0), got[i, :32, :], -jnp.inf) for i in range(16)]
+    counts = [jnp.logical_or(first, (place[3] >> 1) == i % 2) for i in range(16)]
+    parts = [jnp.where(counts[i], got[i, :32, :], -jnp.inf) for i in range(16)]
     top = parts[0]
     for p in parts[1:]:
         top = jnp.maximum(top, p)
-    total = jnp.exp(parts[0] - top)
+    total = jnp.exp2(parts[0] - top)
     for p in parts[1:]:
-        total += jnp.exp(p - top)
-    state = top + jnp.log(total)
+        total += jnp.exp2(p - top)
+    state = top + LOG2E * jnp.log(total)
     hits = got[0, 32:40, :]
     for i in range(1, 16):
         hits += got[i, 32:40, :]
-    mine[...] = state[:16]
-    message[...] = jnp.where(first, state[16:], state[:16])
     real = lax.broadcasted_iota(jnp.int32, (16, 128), 1) < ROWS
     both = jnp.where(real, state[:16] + jnp.where(first, state[16:], 0.0), 0.0)
-    share[...] = jnp.sum(both, keepdims=True) - jnp.where(first, 2.0 * hits, 0.0)
+    share = jnp.sum(both, keepdims=True) - jnp.where(first, 2.0 * hits, 0.0)
+    mine[:16, :] = state[:16]
+    mine[16:24, :] = share
+    message[:16, :] = jnp.where(first, state[16:], state[:16])
+    message[16:24, :] = share
 
 
 def join_call(place, got):
     return pl.pallas_call(
         join_body,
-        out_shape=(
-            jax.ShapeDtypeStruct((16, 128), F32),
-            jax.ShapeDtypeStruct((16, 128), F32),
-            jax.ShapeDtypeStruct((8, 128), F32),
-        ),
+        out_shape=(jax.ShapeDtypeStruct((24, 128), F32),) * 2,
         in_specs=[SMEM, VMEM],
-        out_specs=(VMEM,) * 3,
+        out_specs=(VMEM,) * 2,
         compiler_params=PARAMS,
     )(place, got)
 
 
 def loss_body(place, got, out):
-    total = None
-    for i in range(16):
-        v = jnp.where(in_ring(place, i, 1), got[i], 0.0)
-        total = v if total is None else total + v
-    out[...] = total
+    group = place[2] * 4 + place[0] - ((place[3] * 4 + place[4]) >> 1)
+    total = got[0, 4:5, 0:1]
+    for p in range(1, 16):
+        total = total + got[p, 4:5, 0:1]
+    for z in range(NZ):
+        total = total + got[2 * ((z - group) & 7), 0:1, 0:1]
+    out[...] = total * (LN2 / (2.0 * ROWS * 256))
 
 
 def loss_call(place, got):
     return pl.pallas_call(
         loss_body,
-        out_shape=jax.ShapeDtypeStruct((8, 128), F32),
+        out_shape=jax.ShapeDtypeStruct((1, 1), F32),
         in_specs=[SMEM, VMEM],
         out_specs=VMEM,
         compiler_params=PARAMS,
@@ -294,8 +284,8 @@
     outs = refs[5:9]
     row_wide, row_lse, col_lse = refs[9:12]
     first = place[1] == 0
-    row_lse[...] = jnp.where(first, mine[...], other[...])
-    col_lse[...] = jnp.where(first, other[...], mine[...])
+    row_lse[...] = jnp.where(first, mine[:16, :], other[:16, :]) + 1.0
+    col_lse[...] = jnp.where(first, other[:16, :], mine[:16, :]) + 1.0
     where = [place[i] for i in range(5)]
     multiplier = scale[0]
     lane = lax.broadcasted_iota(jnp.int32, (1, 128), 1)
@@ -317,7 +307,7 @@
             wide = row_wide[at : at + ROWS, :]
             for t in range(8):
                 tile = logits[at : at + ROWS, t * 128 : (t + 1) * 128]
-                both = 0.5 * jnp.exp(tile - wide) + 0.5 * jnp.exp(tile - col_line[t])
+                both = jnp.exp2(tile - wide) + jnp.exp2(tile - col_line[t])
                 both = both - jnp.where(ids[b] == cols[t][0:1], 1.0, 0.0)
                 weights[at : at + ROWS, t * 128 : (t + 1) * 128] = both.astype(BF16)
     text_terms(multiplier, weights, images, ((2, 0, outs[0]), (3, 0, outs[1]), (1, 0, outs[2]), (3, 3 * ROWS, outs[3])))
@@ -391,22 +381,25 @@
     )(scale, weights, *texts)
 
 
-def rest_body(scale, share, weights, *refs):
+def rest_body(place, scale, mine, other, weights, *refs):
     images, texts, outs = refs[:4], refs[4:8], refs[8:]
     text_terms(scale[0], weights, images, ((0, 0, outs[0]),))
     image_terms(scale[0], weights, texts, {0: outs[1]})
+    core_0 = jnp.where(place[1] == 0, mine[16:24, :], other[16:24, :])
+    core_1 = jnp.where(place[1] == 0, other[16:24, :], mine[16:24, :])
+    both = jnp.where(lax.broadcasted_iota(jnp.int32, (8, 128), 0) < 4, core_0, core_1)
     for i in range(16):
-        outs[2][i] = share[...]
-
-
-def rest_call(scale, share, weights, images, texts):
+        outs[2][i] = both
+
+
+def rest_call(place, scale, mine, other, weights, images, texts):
     return pl.pallas_call(
         rest_body,
         out_shape=(PART, PART, jax.ShapeDtypeStruct((16, 8, 128), F32)),
-        in_specs=[SMEM] + [VMEM] * 10,
+        in_specs=[SMEM, SMEM] + [VMEM] * 11,
         out_specs=(VMEM,) * 3,
         compiler_params=PARAMS,
-    )(scale, share, weights, *images, *texts)
+    )(place, scale, mine, other, weights, *images, *texts)
 
 
 def sums_body(n, plan, *refs):
@@ -430,71 +423,54 @@
     return out if len(plan) > 1 else out[0]
 
 
-def mean_body(a, b, out):
-    out[...] = (a[0:1, 0:1] + b[0:1, 0:1]) * (1.0 / (2.0 * ROWS * 256))
-
-
-def mean_call(a, b):
-    return pl.pallas_call(
-        mean_body,
-        out_shape=jax.ShapeDtypeStruct((1, 1), F32),
-        in_specs=[VMEM] * 2,
-        out_specs=VMEM,
-        compiler_params=PARAMS,
-    )(a, b)
-
-
 def local(image_emb, text_emb, logit_scale):
     place = jnp.stack([lax.axis_index(n) for n in AXES]).astype(jnp.int32)
 
-    (chip,) = pack([text_emb, core_swap(text_emb)], ((0, 0, 64), (1, 0, 64)))
+    chip, image = pack([text_emb, core_swap(text_emb), image_emb], ((0, 64), (1, 64)), ((2, 64),))
     next_1, next_4 = z_shift(chip, -1), z_shift(text_emb, 4)
-    near = [plane_shift(image_emb, k, True) for k in (1, 2, 3)]
-    own, text_0, side = pack(
-        [image_emb] + near + [chip, next_1, next_4],
-        ((0, 0, 64), (1, 0, 64), (2, 0, 64), (3, 0, 64)),
-        ((4, 0, 128), (5, 0, 128)),
-        ((5, 0, 128), (6, 0, 64)),
+    near = [plane_shift(image, k, True) for k in (1, 2, 3)]
+    own, text_0, next_4 = pack(
+        [image] + near + [chip, next_1, next_4],
+        ((0, 64), (1, 64), (2, 64), (3, 64)),
+        ((4, 128), (5, 128)),
+        ((6, 64),),
     )
-    text_1, text_3 = z_shift(text_0, -2), core_swap(side)
+    text_1 = z_shift(text_0, -2)
     images = [own] + [plane_shift(own, k, False) for k in (1, 2, 3)]
     texts = [text_0, text_1, core_swap(text_1)]
 
     logits, row_part, col_part, message, matched, text_3 = logits_call(
-        place, logit_scale, images, texts + [text_3, next_4]
+        place, logit_scale, images, texts + [core_swap(next_1), core_swap(next_4), next_4]
     )
     texts.append(text_3)
 
     spread = spread_call(place, row_part, col_part, matched, core_swap(message))
-    mine, message, share = join_call(place, exchange(spread, 0))
-    weights, text_2, text_3, text_1, far = weights_call(
-        place, logit_scale, logits, mine, core_swap(message), images
-    )
+    mine, message = join_call(place, exchange(spread, plane_or_ring()))
+    other = core_swap(message)
+    weights, text_2, text_3, text_1, far = weights_call(place, logit_scale, logits, mine, other, images)
 
     other_1, other_3 = core_swap(text_2), core_swap(text_3)
     pairs, far = sums(
         [text_1, other_1, far, other_3], (256, ((0, 0), (1, 0))), (64, ((2, 0), (3, 128)))
     )
-    pairs = z_shift(pairs, 2)
+    pairs, next_4 = z_shift(pairs, 2), z_shift(far, 4)
     image_parts = image_call(logit_scale, weights, texts)
     back = [plane_shift(v, -k, False) for v, k in zip(image_parts, (2, 1, 3))]
-    text_0, image_0, shares = rest_call(logit_scale, share, weights, images, texts)
-
-    s = loss_call(place, exchange(shares, 1))
-    mean_loss = mean_call(s, core_swap(s)).reshape(1)
+    text_0, image_0, shares = rest_call(place, logit_scale, mine, other, weights, images, texts)
+    mean_loss = loss_call(place, exchange(shares, slanted()))
 
     next_1, mine, *pieces = sums(
-        [text_0, other_3, pairs, image_0] + back + [s],
+        [text_0, other_3, pairs, image_0] + back + [next_4, mean_loss],
         (128, ((0, 128), (1, 0), (2, 128))),
         (128, ((0, 0), (2, 0))),
         *[(64, [(i, 64 * k) for i in range(3, 7)]) for k in range(4)],
     )
-    next_1, next_4 = z_shift(next_1, 1), z_shift(far, 4)
+    next_1 = z_shift(next_1, 1)
     shards = [pieces[0]] + [plane_shift(pieces[k], -k, True) for k in (2, 1, 3)]
     mine, other = sums([mine, next_1], (64, ((0, 0), (1, 0))), (64, ((0, 64), (1, 64))))
     image_grad = sums(shards, (64, [(i, 0) for i in range(4)]))
     text_grad = sums([mine, core_swap(other), next_4], (64, ((0, 0), (1, 0), (2, 0))))
-    return mean_loss, image_grad, text_grad
+    return mean_loss.reshape(1), image_grad, text_grad
 
 
 def solution(mesh):

time: 135 us -> 137 us (1.015)
  the two profiles are of different devices: /device:TPU:8 before, /device:TPU:32 now
where the time goes in v5:
time: 137 us; the launch traced here: 136 us
  blocking collectives  39.2 us (29%)
  starting transfers between devices  36 us (26%)
  waiting for transfers between devices  31.6 us (23%)
  Pallas kernels  24.6 us (18%)
  local copies, waits for them, and re-layouts  3.5 us (3%)
  between operations  1.43 us (1%)
    all_to_all x2, blocking collectives, exchange(): return lax.all_to_all(v, AXES, 0, 0, axis_index_groups=groups)  39.2 us
    ppermute x6, waiting for transfers between devices, z_shift(): return lax.ppermute(v, ('zl', 'core', 'zh'), pairs)  19 us
    ppermute x12, starting transfers between devices, plane_shift(): return lax.ppermute(v, ('core', 'zh', 'y', 'x'), pairs)  16.8 us
    ppermute x6, starting transfers between devices, z_shift(): return lax.ppermute(v, ('zl', 'core', 'zh'), pairs)  14.7 us
    pallas_call x1, Pallas kernels, weights_call(): pl.pallas_call(weights_body, out_shape=(jax.ShapeDtypeStruct((BLOCK, BLOC...  7.31 us
    ppermute x9, waiting for transfers between devices, core_swap(): return lax.ppermute(v, 'core', [(0, 1), (1, 0)])  6.52 us
    ppermute x12, waiting for transfers between devices, plane_shift(): return lax.ppermute(v, ('core', 'zh', 'y', 'x'), pairs)  6.16 us
    pallas_call x1, Pallas kernels, logits_call(): pl.pallas_call(logits_body, out_shape=(jax.ShapeDtypeStruct((BLOCK, BLOCK...  5.68 us
  transfers between devices with their start and end apart: 27, of which 12 were waited for; matrix products, arithmetic and copies ran while one was open for 0% of the time, Pallas kernels for 5%

profile of v5, /device:TPU:32, one launch (start us, length us, event | category | flops | bytes accessed | tf_op | source)
XLA Modules:
  0.0 136.3 jit_solution(16650121003671109727)
XLA Ops:
  0.6 0.1 collective-permute-start
  0.7 1.6 %collective-permute-done.refs_1_ = bf16[64,1280]{1,0:T(8,128)(2,1)S(1)} collective-permute-done((bf16[64,1280]{1,0:T(8,128)(2,1)}, bf16[64,1280]{1,0:T(8,128)(2,1)S(1)}, u32[]{:S(2)}, u32[]{:S(2)}) %collective-permute-start) | collective-permute-done | bytes 163872 | tf_op jit(solution)/shard_map/ppermute | solution.py:47
  2.3 0.9 copy-done.2
  3.2 0.9 copy-done.3
  4.2 1.9 %collective-permute-start.4 = (bf16[128,1280]{1,0:T(8,128)(2,1)S(1)}, bf16[128,1280]{1,0:T(8,128)(2,1)}, u32[]{:S(2)}, u32[]{:S(2)}) collective-permute-start(bf16[128,1280]{1,0:T(8,128)(2,1)S(1)} %get-tuple-element.38.refs_4_), channel_id=1, source_target_pairs={{0,208},{64,0},{128,64},{192,128},{16,192},{80,16},{144,80},{208,1... | collective-permute-start | bytes 983048 | tf_op jit(solution)/shard_map/ppermute | solution.py:43
  6.1 5.5 %collective-permute-start.5 = (bf16[64,1280]{1,0:T(8,128)(2,1)S(1)}, bf16[64,1280]{1,0:T(8,128)(2,1)S(1)}, u32[]{:S(2)}, u32[]{:S(2)}) collective-permute-start(bf16[64,1280]{1,0:T(8,128)(2,1)S(1)} %copy-done.3), channel_id=1, source_target_pairs={{0,16},{64,80},{128,144},{192,208},{16,0},{80,64},{144,128},{208,1... | collective-permute-start | bytes 491528 | tf_op jit(solution)/shard_map/ppermute | solution.py:43
  11.6 2.8 %collective-permute-start.3 = (bf16[64,1280]{1,0:T(8,128)(2,1)S(1)}, bf16[64,1280]{1,0:T(8,128)(2,1)S(1)}, u32[]{:S(2)}, u32[]{:S(2)}) collective-permute-start(bf16[64,1280]{1,0:T(8,128)(2,1)S(1)} %get-tuple-element.37.refs_0_), channel_id=1, source_target_pairs={{0,3},{1,0},{2,1},{3,2},{4,7},{5,4},{6,5},{7,6},{8,11},{9,8},{10,9... | collective-permute-start | bytes 491528 | tf_op jit(solution)/shard_map/ppermute | solution.py:34
  14.3 0.8 collective-permute-start.2
  15.1 0.9 collective-permute-start.1
  16.0 7.1 %collective-permute-done.5.refs_6_ = bf16[64,1280]{1,0:T(8,128)(2,1)S(1)} collective-permute-done((bf16[64,1280]{1,0:T(8,128)(2,1)S(1)}, bf16[64,1280]{1,0:T(8,128)(2,1)S(1)}, u32[]{:S(2)}, u32[]{:S(2)}) %collective-permute-start.5) | collective-permute-done | bytes 163872 | tf_op jit(solution)/shard_map/ppermute | solution.py:43
  23.1 0.0 collective-permute-done.3.refs_3_
  23.1 0.0 collective-permute-done.2.refs_2_
  23.1 0.0 collective-permute-done.1.refs_1_
  23.1 0.0 collective-permute-done.4.refs_5_
  23.1 1.1 shard_map.59
  24.2 2.0 %collective-permute-start.9 = (bf16[256,1280]{1,0:T(8,128)(2,1)S(1)}, bf16[256,1280]{1,0:T(8,128)(2,1)S(1)}, u32[]{:S(2)}, u32[]{:S(2)}) collective-permute-start(bf16[256,1280]{1,0:T(8,128)(2,1)S(1)} %get-tuple-element.40.refs_4_.refs_0_), channel_id=1, source_target_pairs={{0,144},{64,208},{128,0},{192,64},{16,128},{80,192},{144,16},{208,... | collective-permute-start | bytes 1966088 | tf_op jit(solution)/shard_map/ppermute | solution.py:43
  26.2 3.0 %collective-permute-start.8 = (bf16[256,1280]{1,0:T(8,128)(2,1)S(1)}, bf16[256,1280]{1,0:T(8,128)(2,1)S(1)}, u32[]{:S(2)}, u32[]{:S(2)}) collective-permute-start(bf16[256,1280]{1,0:T(8,128)(2,1)S(1)} %get-tuple-element.39.refs_0_), channel_id=1, source_target_pairs={{0,12},{1,13},{2,14},{3,15},{4,0},{5,1},{6,2},{7,3},{8,4},{9,5},{1... | collective-permute-start | bytes 1966088 | tf_op jit(solution)/shard_map/ppermute | solution.py:34
  29.2 0.6 collective-permute-start.7
  29.9 1.0 collective-permute-start.6
  30.8 10.8 %collective-permute-done.9.refs_5_.refs_1_ = bf16[256,1280]{1,0:T(8,128)(2,1)S(1)} collective-permute-done((bf16[256,1280]{1,0:T(8,128)(2,1)S(1)}, bf16[256,1280]{1,0:T(8,128)(2,1)S(1)}, u32[]{:S(2)}, u32[]{:S(2)}) %collective-permute-start.9) | collective-permute-done | bytes 655392 | tf_op jit(solution)/shard_map/ppermute | solution.py:43
  41.7 0.0 collective-permute-start.10
  41.7 0.5 collective-permute-start.12
  42.2 1.8 %collective-permute-done.12.refs_8_ = bf16[64,1280]{1,0:T(8,128)(2,1)S(1)} collective-permute-done((bf16[64,1280]{1,0:T(8,128)(2,1)S(1)}, bf16[64,1280]{1,0:T(8,128)(2,1)S(1)}, u32[]{:S(2)}, u32[]{:S(2)}) %collective-permute-start.12) | collective-permute-done | bytes 163872 | tf_op jit(solution)/shard_map/ppermute | solution.py:47
  44.0 0.7 copy-done
  44.7 0.1 collective-permute-start.11
  45.5 0.1 stack.23.place
  45.5 1.1 collective-permute-done.11.refs_7_
  46.6 1.8 %collective-permute-done.6.refs_1_ = bf16[256,1280]{1,0:T(8,128)(2,1)} collective-permute-done((bf16[256,1280]{1,0:T(8,128)(2,1)S(1)}, bf16[256,1280]{1,0:T(8,128)(2,1)}, u32[]{:S(2)}, u32[]{:S(2)}) %collective-permute-start.6) | collective-permute-done | bytes 655392 | tf_op jit(solution)/shard_map/ppermute | solution.py:34
  48.5 0.0 collective-permute-done.10.refs_6_.refs_2_
  48.5 0.9 copy-done.1
  49.4 5.7 %shard_map.60 = (f32[1024,1024]{1,0:T(8,128)S(1)}, f32[16,128]{1,0:T(8,128)S(1)}, f32[16,128]{1,0:T(8,128)S(1)}, f32[24,128]{1,0:T(8,128)S(1)}, f32[8,128]{1,0:T(8,128)S(1)}, /*index=5*/bf16[256,1280]{1,0:T(8,128)(2,1)S(1)}) custom-call(s32[5]{0:T(128)S(1)} %stack.23.place, f32[1]{0:T(128)S(6)} %copy.6.scale, ...), custom_call_target="tpu_custom_call" | custom-call | tf_op jit(solution)/shard_map/pallas_call | solution.py:189
  55.1 0.1 collective-permute-start.13
  55.2 1.2 collective-permute-done.13.got
  56.3 0.6 shard_map.61
  56.9 14.5 %all_to_all.10.got = f32[16,40,128]{2,1,0:T(8,128)S(1)} all-to-all(f32[16,40,128]{2,1,0:T(8,128)S(1)} %shard_map.61), channel_id=1, replica_groups={{0,1,2,3,4,5,6,7,8,9,10,11,12,13,14,15},{64,65,66,67,68,69,70,71,72,73,..., dimensions={0} | all-to-all | bytes 655360 | tf_op jit(solution)/shard_map/all_to_all | solution.py:68
  71.4 0.7 shard_map.62
  72.1 2.8 %collective-permute-start.14 = (f32[24,128]{1,0:T(8,128)S(1)}, f32[24,128]{1,0:T(8,128)S(1)}, u32[]{:S(2)}, u32[]{:S(2)}) collective-permute-start(f32[24,128]{1,0:T(8,128)S(1)} %get-tuple-element.47), channel_id=1, source_target_pairs={{0,32},{32,0},{1,33},{33,1},{2,34},{34,2},{3,35},{35,3},{4,36},{36... | collective-permute-start | bytes 36872 | tf_op jit(solution)/shard_map/ppermute | solution.py:47
  75.0 0.8 collective-permute-done.14.other
  75.8 7.3 %shard_map.63 = (bf16[1024,1024]{1,0:T(8,128)(2,1)S(1)}, bf16[256,1280]{1,0:T(8,128)(2,1)S(1)}, bf16[192,1280]{1,0:T(8,128)(2,1)S(1)}, bf16[256,1280]{1,0:T(8,128)(2,1)S(1)}, bf16[64,1280]{1,0:T(8,128)(2,1)S(1)}) custom-call(s32[5]{0:T(128)S(1)} %stack.23.place, f32[1]{0:T(128)S(6)} %copy.6.scale, f32[1024,1024]{1,0:T(8,128)S(1)} %get-tuple-element.48.logits, ...), custom_call_target="tpu_custom_call" | custom-call | tf_op jit(solution)/shard_map/pallas_call | solution.py:350
  83.1 0.4 collective-permute-start.16
  83.6 0.3 collective-permute-start.15
  83.9 2.3 %shard_map.67 = (bf16[256,1280]{1,0:T(8,128)(2,1)S(1)}, bf16[256,1280]{1,0:T(8,128)(2,1)S(1)}, bf16[256,1280]{1,0:T(8,128)(2,1)S(1)}) custom-call(f32[1]{0:T(128)S(6)} %copy.6.scale, bf16[1024,1024]{1,0:T(8,128)(2,1)S(1)} %get-tuple-element.49.weights, bf16[256,1280]{1,0:T(8,128)(2,1)S(1)} %get-tuple-element.40.refs_4_.refs_0_, ...), custom_call_target="tpu_custom_call" | custom-call | tf_op jit(solution)/shard_map/pallas_call | solution.py:375
  86.2 0.4 collective-permute-start.18
  86.6 3.0 %collective-permute-start.19 = (bf16[256,1280]{1,0:T(8,128)(2,1)S(1)}, bf16[256,1280]{1,0:T(8,128)(2,1)S(1)}, u32[]{:S(2)}, u32[]{:S(2)}) collective-permute-start(bf16[256,1280]{1,0:T(8,128)(2,1)S(1)} %get-tuple-element.60), channel_id=1, source_target_pairs={{0,12},{1,13},{2,14},{3,15},{4,0},{5,1},{6,2},{7,3},{8,4},{9,5},{1... | collective-permute-start | bytes 1966088 | tf_op jit(solution)/shard_map/ppermute | solution.py:34
  89.6 0.0 collective-permute-start.20
  89.6 0.2 shard_map.66
  89.8 1.3 collective-permute-start.17
  91.1 2.2 %collective-permute-start.21 = (bf16[64,1280]{1,0:T(8,128)(2,1)S(1)}, bf16[64,1280]{1,0:T(8,128)(2,1)S(1)}, u32[]{:S(2)}, u32[]{:S(2)}) collective-permute-start(bf16[64,1280]{1,0:T(8,128)(2,1)S(1)} %get-tuple-element.62), channel_id=1, source_target_pairs={{0,16},{64,80},{128,144},{192,208},{16,0},{80,64},{144,128},{208,1... | collective-permute-start | bytes 491528 | tf_op jit(solution)/shard_map/ppermute | solution.py:43
  93.3 2.9 %shard_map.64 = (bf16[256,1280]{1,0:T(8,128)(2,1)S(1)}, bf16[256,1280]{1,0:T(8,128)(2,1)S(1)}, f32[16,8,128]{2,1,0:T(8,128)S(1)}) custom-call(s32[5]{0:T(128)S(1)} %stack.23.place, f32[1]{0:T(128)S(6)} %copy.6.scale, f32[24,128]{1,0:T(8,128)S(1)} %get-tuple-element.46.mine, f32[24,128]{1,0:T(8,128)S(1)} %collective-permute-done.14.other, ...), custom_call_target="tpu_custom_call" | custom-call | tf_op jit(solution)/shard_map/pallas_call | solution.py:396
  96.2 24.7 %all_to_all.11.got = f32[16,8,128]{2,1,0:T(8,128)S(1)} all-to-all(f32[16,8,128]{2,1,0:T(8,128)S(1)} %get-tuple-element.51), channel_id=1, replica_groups={{0,1,66,67,132,133,198,199,24,25,90,91,156,157,222,223},{64,65,130,131,..., dimensions={0} | all-to-all | bytes 131072 | tf_op jit(solution)/shard_map/all_to_all | solution.py:68
  120.9 1.1 shard_map.65.refs_8_
  122.0 1.2 shard_map.68
  123.2 1.8 %collective-permute-start.25 = (bf16[128,1280]{1,0:T(8,128)(2,1)S(1)}, bf16[128,1280]{1,0:T(8,128)(2,1)S(1)}, u32[]{:S(2)}, u32[]{:S(2)}) collective-permute-start(bf16[128,1280]{1,0:T(8,128)(2,1)S(1)} %get-tuple-element.68), channel_id=1, source_target_pairs={{0,64},{64,128},{128,192},{192,16},{16,80},{80,144},{144,208},{208... | collective-permute-start | bytes 983048 | tf_op jit(solution)/shard_map/ppermute | solution.py:43
  125.0 2.2 %collective-permute-start.22 = (bf16[64,1280]{1,0:T(8,128)(2,1)S(1)}, bf16[64,1280]{1,0:T(8,128)(2,1)S(1)}, u32[]{:S(2)}, u32[]{:S(2)}) collective-permute-start(bf16[64,1280]{1,0:T(8,128)(2,1)S(1)} %get-tuple-element.64), channel_id=1, source_target_pairs={{0,2},{1,3},{2,0},{3,1},{4,6},{5,7},{6,4},{7,5},{8,10},{9,11},{10,... | collective-permute-start | bytes 491528 | tf_op jit(solution)/shard_map/ppermute | solution.py:34
  127.3 1.1 collective-permute-start.23
  128.3 1.0 collective-permute-start.24
  129.3 1.1 collective-permute-done.25.refs_1_
  130.3 0.1 shard_map.70
  130.4 0.1 collective-permute-start.26
  130.5 1.3 collective-permute-done.22.refs_1_
  131.8 1.2 collective-permute-done.23.refs_2_
  133.0 1.8 %collective-permute-done.24.refs_3_ = bf16[64,1280]{1,0:T(8,128)(2,1)S(1)} collective-permute-done((bf16[64,1280]{1,0:T(8,128)(2,1)S(1)}, bf16[64,1280]{1,0:T(8,128)(2,1)S(1)}, u32[]{:S(2)}, u32[]{:S(2)}) %collective-permute-start.24) | collective-permute-done | bytes 163872 | tf_op jit(solution)/shard_map/ppermute | solution.py:34
  134.9 0.7 shard_map.69
  135.6 0.7 shard_map.71
  (15 shorter events, 0.1 us)
Async XLA Ops:
  0.6 1.7 %collective-permute-start = (bf16[64,1280]{1,0:T(8,128)(2,1)}, bf16[64,1280]{1,0:T(8,128)(2,1)S(1)}, u32[]{:S(2)}, u32[]{:S(2)}) collective-permute-start(bf16[64,1280]{1,0:T(8,128)(2,1)} %refs_0_.1), channel_id=1, source_target_pairs={{0,32},{32,0},{1,33},{33,1},{2,34},{34,2},{3,35},{35,3},{4,36},{36... | collective-permute-start | bytes 491528 | tf_op jit(solution)/shard_map/ppermute | solution.py:47
  2.3 0.9 copy-start.2
  3.2 0.9 copy-start.3
  4.2 18.9 %collective-permute-start.4 = (bf16[128,1280]{1,0:T(8,128)(2,1)S(1)}, bf16[128,1280]{1,0:T(8,128)(2,1)}, u32[]{:S(2)}, u32[]{:S(2)}) collective-permute-start(bf16[128,1280]{1,0:T(8,128)(2,1)S(1)} %get-tuple-element.38.refs_4_), channel_id=1, source_target_pairs={{0,208},{64,0},{128,64},{192,128},{16,192},{80,16},{144,80},{208,1... | collective-permute-start | bytes 983048 | tf_op jit(solution)/shard_map/ppermute | solution.py:43
  6.1 17.0 %collective-permute-start.5 = (bf16[64,1280]{1,0:T(8,128)(2,1)S(1)}, bf16[64,1280]{1,0:T(8,128)(2,1)S(1)}, u32[]{:S(2)}, u32[]{:S(2)}) collective-permute-start(bf16[64,1280]{1,0:T(8,128)(2,1)S(1)} %copy-done.3), channel_id=1, source_target_pairs={{0,16},{64,80},{128,144},{192,208},{16,0},{80,64},{144,128},{208,1... | collective-permute-start | bytes 491528 | tf_op jit(solution)/shard_map/ppermute | solution.py:43
  11.6 11.5 %collective-permute-start.3 = (bf16[64,1280]{1,0:T(8,128)(2,1)S(1)}, bf16[64,1280]{1,0:T(8,128)(2,1)S(1)}, u32[]{:S(2)}, u32[]{:S(2)}) collective-permute-start(bf16[64,1280]{1,0:T(8,128)(2,1)S(1)} %get-tuple-element.37.refs_0_), channel_id=1, source_target_pairs={{0,3},{1,0},{2,1},{3,2},{4,7},{5,4},{6,5},{7,6},{8,11},{9,8},{10,9... | collective-permute-start | bytes 491528 | tf_op jit(solution)/shard_map/ppermute | solution.py:34
  14.3 8.8 %collective-permute-start.2 = (bf16[64,1280]{1,0:T(8,128)(2,1)S(1)}, bf16[64,1280]{1,0:T(8,128)(2,1)S(1)}, u32[]{:S(2)}, u32[]{:S(2)}) collective-permute-start(bf16[64,1280]{1,0:T(8,128)(2,1)S(1)} %get-tuple-element.37.refs_0_), channel_id=1, source_target_pairs={{0,2},{1,3},{2,0},{3,1},{4,6},{5,7},{6,4},{7,5},{8,10},{9,11},{10,... | collective-permute-start | bytes 491528 | tf_op jit(solution)/shard_map/ppermute | solution.py:34
  15.1 8.0 %collective-permute-start.1 = (bf16[64,1280]{1,0:T(8,128)(2,1)S(1)}, bf16[64,1280]{1,0:T(8,128)(2,1)S(1)}, u32[]{:S(2)}, u32[]{:S(2)}) collective-permute-start(bf16[64,1280]{1,0:T(8,128)(2,1)S(1)} %get-tuple-element.37.refs_0_), channel_id=1, source_target_pairs={{0,1},{1,2},{2,3},{3,0},{4,5},{5,6},{6,7},{7,4},{8,9},{9,10},{10,1... | collective-permute-start | bytes 491528 | tf_op jit(solution)/shard_map/ppermute | solution.py:34
  24.2 17.5 %collective-permute-start.9 = (bf16[256,1280]{1,0:T(8,128)(2,1)S(1)}, bf16[256,1280]{1,0:T(8,128)(2,1)S(1)}, u32[]{:S(2)}, u32[]{:S(2)}) collective-permute-start(bf16[256,1280]{1,0:T(8,128)(2,1)S(1)} %get-tuple-element.40.refs_4_.refs_0_), channel_id=1, source_target_pairs={{0,144},{64,208},{128,0},{192,64},{16,128},{80,192},{144,16},{208,... | collective-permute-start | bytes 1966088 | tf_op jit(solution)/shard_map/ppermute | solution.py:43
  26.2 20.4 %collective-permute-start.8 = (bf16[256,1280]{1,0:T(8,128)(2,1)S(1)}, bf16[256,1280]{1,0:T(8,128)(2,1)S(1)}, u32[]{:S(2)}, u32[]{:S(2)}) collective-permute-start(bf16[256,1280]{1,0:T(8,128)(2,1)S(1)} %get-tuple-element.39.refs_0_), channel_id=1, source_target_pairs={{0,12},{1,13},{2,14},{3,15},{4,0},{5,1},{6,2},{7,3},{8,4},{9,5},{1... | collective-permute-start | bytes 1966088 | tf_op jit(solution)/shard_map/ppermute | solution.py:34
  29.2 17.4 %collective-permute-start.7 = (bf16[256,1280]{1,0:T(8,128)(2,1)S(1)}, bf16[256,1280]{1,0:T(8,128)(2,1)}, u32[]{:S(2)}, u32[]{:S(2)}) collective-permute-start(bf16[256,1280]{1,0:T(8,128)(2,1)S(1)} %get-tuple-element.39.refs_0_), channel_id=1, source_target_pairs={{0,8},{1,9},{2,10},{3,11},{4,12},{5,13},{6,14},{7,15},{8,0},{9,1},... | collective-permute-start | bytes 1966088 | tf_op jit(solution)/shard_map/ppermute | solution.py:34
  29.9 18.6 %collective-permute-start.6 = (bf16[256,1280]{1,0:T(8,128)(2,1)S(1)}, bf16[256,1280]{1,0:T(8,128)(2,1)}, u32[]{:S(2)}, u32[]{:S(2)}) collective-permute-start(bf16[256,1280]{1,0:T(8,128)(2,1)S(1)} %get-tuple-element.39.refs_0_), channel_id=1, source_target_pairs={{0,4},{1,5},{2,6},{3,7},{4,8},{5,9},{6,10},{7,11},{8,12},{9,13},{1... | collective-permute-start | bytes 1966088 | tf_op jit(solution)/shard_map/ppermute | solution.py:34
  41.7 6.8 %collective-permute-start.10 = (bf16[256,1280]{1,0:T(8,128)(2,1)S(1)}, bf16[256,1280]{1,0:T(8,128)(2,1)S(1)}, u32[]{:S(2)}, u32[]{:S(2)}) collective-permute-start(bf16[256,1280]{1,0:T(8,128)(2,1)S(1)} %collective-permute-done.9.refs_5_.refs_1_), channel_id=1, source_target_pairs={{0,32},{32,0},{1,33},{33,1},{2,34},{34,2},{3,35},{35,3},{4,36},{36... | collective-permute-start | bytes 1966088 | tf_op jit(solution)/shard_map/ppermute | solution.py:47
  41.7 2.3 %collective-permute-start.12 = (bf16[64,1280]{1,0:T(8,128)(2,1)S(1)}, bf16[64,1280]{1,0:T(8,128)(2,1)S(1)}, u32[]{:S(2)}, u32[]{:S(2)}) collective-permute-start(bf16[64,1280]{1,0:T(8,128)(2,1)S(1)} %get-tuple-element.41.refs_9_), channel_id=1, source_target_pairs={{0,32},{32,0},{1,33},{33,1},{2,34},{34,2},{3,35},{35,3},{4,36},{36... | collective-permute-start | bytes 491528 | tf_op jit(solution)/shard_map/ppermute | solution.py:47
  44.0 0.7 copy-start
  44.7 2.0 %collective-permute-start.11 = (bf16[128,1280]{1,0:T(8,128)(2,1)}, bf16[128,1280]{1,0:T(8,128)(2,1)}, u32[]{:S(2)}, u32[]{:S(2)}) collective-permute-start(bf16[128,1280]{1,0:T(8,128)(2,1)} %collective-permute-done.4.refs_5_), channel_id=1, source_target_pairs={{0,32},{32,0},{1,33},{33,1},{2,34},{34,2},{3,35},{35,3},{4,36},{36... | collective-permute-start | bytes 983048 | tf_op jit(solution)/shard_map/ppermute | solution.py:47
  48.5 0.9 copy-start.1
  55.1 1.3 collective-permute-start.13
  72.1 3.7 %collective-permute-start.14 = (f32[24,128]{1,0:T(8,128)S(1)}, f32[24,128]{1,0:T(8,128)S(1)}, u32[]{:S(2)}, u32[]{:S(2)}) collective-permute-start(f32[24,128]{1,0:T(8,128)S(1)} %get-tuple-element.47), channel_id=1, source_target_pairs={{0,32},{32,0},{1,33},{33,1},{2,34},{34,2},{3,35},{35,3},{4,36},{36... | collective-permute-start | bytes 36872 | tf_op jit(solution)/shard_map/ppermute | solution.py:47
  83.1 6.5 %collective-permute-start.16 = (bf16[256,1280]{1,0:T(8,128)(2,1)S(1)}, bf16[256,1280]{1,0:T(8,128)(2,1)S(1)}, u32[]{:S(2)}, u32[]{:S(2)}) collective-permute-start(bf16[256,1280]{1,0:T(8,128)(2,1)S(1)} %get-tuple-element.55), channel_id=1, source_target_pairs={{0,32},{32,0},{1,33},{33,1},{2,34},{34,2},{3,35},{35,3},{4,36},{36... | collective-permute-start | bytes 1966088 | tf_op jit(solution)/shard_map/ppermute | solution.py:47
  83.6 6.1 %collective-permute-start.15 = (bf16[192,1280]{1,0:T(8,128)(2,1)S(1)}, bf16[192,1280]{1,0:T(8,128)(2,1)S(1)}, u32[]{:S(2)}, u32[]{:S(2)}) collective-permute-start(bf16[192,1280]{1,0:T(8,128)(2,1)S(1)} %get-tuple-element.53), channel_id=1, source_target_pairs={{0,32},{32,0},{1,33},{33,1},{2,34},{34,2},{3,35},{35,3},{4,36},{36... | collective-permute-start | bytes 1474568 | tf_op jit(solution)/shard_map/ppermute | solution.py:47
  86.2 35.8 %collective-permute-start.18 = (bf16[256,1280]{1,0:T(8,128)(2,1)S(1)}, bf16[256,1280]{1,0:T(8,128)(2,1)S(1)}, u32[]{:S(2)}, u32[]{:S(2)}) collective-permute-start(bf16[256,1280]{1,0:T(8,128)(2,1)S(1)} %get-tuple-element.59), channel_id=1, source_target_pairs={{0,8},{1,9},{2,10},{3,11},{4,12},{5,13},{6,14},{7,15},{8,0},{9,1},... | collective-permute-start | bytes 1966088 | tf_op jit(solution)/shard_map/ppermute | solution.py:34
  86.6 35.4 %collective-permute-start.19 = (bf16[256,1280]{1,0:T(8,128)(2,1)S(1)}, bf16[256,1280]{1,0:T(8,128)(2,1)S(1)}, u32[]{:S(2)}, u32[]{:S(2)}) collective-permute-start(bf16[256,1280]{1,0:T(8,128)(2,1)S(1)} %get-tuple-element.60), channel_id=1, source_target_pairs={{0,12},{1,13},{2,14},{3,15},{4,0},{5,1},{6,2},{7,3},{8,4},{9,5},{1... | collective-permute-start | bytes 1966088 | tf_op jit(solution)/shard_map/ppermute | solution.py:34
  89.6 32.4 %collective-permute-start.20 = (bf16[256,1280]{1,0:T(8,128)(2,1)S(1)}, bf16[256,1280]{1,0:T(8,128)(2,1)S(1)}, u32[]{:S(2)}, u32[]{:S(2)}) collective-permute-start(bf16[256,1280]{1,0:T(8,128)(2,1)S(1)} %get-tuple-element.61), channel_id=1, source_target_pairs={{0,4},{1,5},{2,6},{3,7},{4,8},{5,9},{6,10},{7,11},{8,12},{9,13},{1... | collective-permute-start | bytes 1966088 | tf_op jit(solution)/shard_map/ppermute | solution.py:34
  89.8 32.2 %collective-permute-start.17 = (bf16[256,1280]{1,0:T(8,128)(2,1)S(1)}, bf16[256,1280]{1,0:T(8,128)(2,1)S(1)}, u32[]{:S(2)}, u32[]{:S(2)}) collective-permute-start(bf16[256,1280]{1,0:T(8,128)(2,1)S(1)} %get-tuple-element.57), channel_id=1, source_target_pairs={{0,128},{64,192},{128,16},{192,80},{16,144},{80,208},{144,0},{208,... | collective-permute-start | bytes 1966088 | tf_op jit(solution)/shard_map/ppermute | solution.py:43
  91.1 30.9 %collective-permute-start.21 = (bf16[64,1280]{1,0:T(8,128)(2,1)S(1)}, bf16[64,1280]{1,0:T(8,128)(2,1)S(1)}, u32[]{:S(2)}, u32[]{:S(2)}) collective-permute-start(bf16[64,1280]{1,0:T(8,128)(2,1)S(1)} %get-tuple-element.62), channel_id=1, source_target_pairs={{0,16},{64,80},{128,144},{192,208},{16,0},{80,64},{144,128},{208,1... | collective-permute-start | bytes 491528 | tf_op jit(solution)/shard_map/ppermute | solution.py:43
  123.2 7.2 %collective-permute-start.25 = (bf16[128,1280]{1,0:T(8,128)(2,1)S(1)}, bf16[128,1280]{1,0:T(8,128)(2,1)S(1)}, u32[]{:S(2)}, u32[]{:S(2)}) collective-permute-start(bf16[128,1280]{1,0:T(8,128)(2,1)S(1)} %get-tuple-element.68), channel_id=1, source_target_pairs={{0,64},{64,128},{128,192},{192,16},{16,80},{80,144},{144,208},{208... | collective-permute-start | bytes 983048 | tf_op jit(solution)/shard_map/ppermute | solution.py:43
  125.0 6.8 %collective-permute-start.22 = (bf16[64,1280]{1,0:T(8,128)(2,1)S(1)}, bf16[64,1280]{1,0:T(8,128)(2,1)S(1)}, u32[]{:S(2)}, u32[]{:S(2)}) collective-permute-start(bf16[64,1280]{1,0:T(8,128)(2,1)S(1)} %get-tuple-element.64), channel_id=1, source_target_pairs={{0,2},{1,3},{2,0},{3,1},{4,6},{5,7},{6,4},{7,5},{8,10},{9,11},{10,... | collective-permute-start | bytes 491528 | tf_op jit(solution)/shard_map/ppermute | solution.py:34
  127.3 5.8 %collective-permute-start.23 = (bf16[64,1280]{1,0:T(8,128)(2,1)S(1)}, bf16[64,1280]{1,0:T(8,128)(2,1)S(1)}, u32[]{:S(2)}, u32[]{:S(2)}) collective-permute-start(bf16[64,1280]{1,0:T(8,128)(2,1)S(1)} %get-tuple-element.65), channel_id=1, source_target_pairs={{0,3},{1,0},{2,1},{3,2},{4,7},{5,4},{6,5},{7,6},{8,11},{9,8},{10,9... | collective-permute-start | bytes 491528 | tf_op jit(solution)/shard_map/ppermute | solution.py:34
  128.3 6.5 %collective-permute-start.24 = (bf16[64,1280]{1,0:T(8,128)(2,1)S(1)}, bf16[64,1280]{1,0:T(8,128)(2,1)S(1)}, u32[]{:S(2)}, u32[]{:S(2)}) collective-permute-start(bf16[64,1280]{1,0:T(8,128)(2,1)S(1)} %get-tuple-element.66), channel_id=1, source_target_pairs={{0,1},{1,2},{2,3},{3,0},{4,5},{5,6},{6,7},{7,4},{8,9},{9,10},{10,1... | collective-permute-start | bytes 491528 | tf_op jit(solution)/shard_map/ppermute | solution.py:34
  130.4 5.2 %collective-permute-start.26 = (bf16[64,1280]{1,0:T(8,128)(2,1)S(1)}, bf16[64,1280]{1,0:T(8,128)(2,1)S(1)}, u32[]{:S(2)}, u32[]{:S(2)}) collective-permute-start(bf16[64,1280]{1,0:T(8,128)(2,1)S(1)} %get-tuple-element.70), channel_id=1, source_target_pairs={{0,32},{32,0},{1,33},{33,1},{2,34},{34,2},{3,35},{35,3},{4,36},{36... | collective-permute-start | bytes 491528 | tf_op jit(solution)/shard_map/ppermute | solution.py:47

commit v6 on v5

--- a/solution.py
+++ b/solution.py
@@ -11,6 +11,7 @@
 NX, NY, NZ = 4, 4, 8
 ROWS, EMBED = 64, 1280
 CHUNK = 4 * ROWS
+TAIL, DIGITS = 16, 13
 BLOCK = 16 * ROWS
 BF16, F32 = jnp.bfloat16, jnp.float32
 LOG2E, LN2 = math.log2(math.e), math.log(2.0)
@@ -58,12 +59,6 @@
     ]
 
 
-def slanted():
-    return [
-        [device(c, p // 4, p % 4, (g + p // 2) % NZ) for p in range(16)] for c in range(2) for g in range(NZ)
-    ]
-
-
 def exchange(v, groups):
     return lax.all_to_all(v, AXES, 0, 0, axis_index_groups=groups)
 
@@ -119,37 +114,78 @@
     )(*arrays)
 
 
-def logits_body(place, scale, *refs):
-    images = refs[:4]
-    texts = (*refs[4:7], refs[15])
-    logits, row_out, col_out, message, match_out, text_3 = refs[10:16]
-    row_wide = refs[16]
-    text_3[: 2 * ROWS, :] = refs[7][...]
-    text_3[2 * ROWS : 3 * ROWS, :] = refs[8][...]
-    text_3[3 * ROWS :, :] = refs[9][...]
-    where = [place[i] for i in range(5)]
-    multiplier = scale[0] * LOG2E
+def block_logits(multiplier, images, texts, logits):
     for a in range(4):
-        for j in range(4):
+        for j, text in enumerate(texts):
             logits[a * CHUNK : (a + 1) * CHUNK, j * CHUNK : (j + 1) * CHUNK] = (
                 multiplier
                 * lax.dot_general(
-                    images[a][...],
-                    texts[j][...],
-                    (((1,), (1,)), ((), ())),
-                    preferred_element_type=F32,
+                    images[a][...], text[...], (((1,), (1,)), ((), ())), preferred_element_type=F32
                 )
             )
+
+
+def fold(v):
+    return v.reshape(v.shape[0] // 8, 8, 128)
+
+
+def column_part(logits, t, top):
+    top = jnp.max(top, axis=0, keepdims=True)
+
+    def step(i, total):
+        tile = logits[pl.ds(pl.multiple_of(i * 128, 128), 128), t * 128 : (t + 1) * 128]
+        return total + jnp.sum(fold(jnp.exp2(tile - top)), axis=0)
+
+    total = lax.fori_loop(0, 8, step, jnp.zeros((8, 128), F32), unroll=True)
+    return top + LOG2E * jnp.log(jnp.sum(total, axis=0, keepdims=True))
+
+
+def first_body(scale, *refs):
+    images, texts = refs[:4], refs[4:6]
+    logits, col_out = refs[6:]
+    block_logits(scale[0] * LOG2E, images, texts, logits)
+    for t in range(4):
+        top = jnp.max(fold(logits[:128, t * 128 : (t + 1) * 128]), axis=0)
+        for i in range(1, 8):
+            tile = logits[i * 128 : (i + 1) * 128, t * 128 : (t + 1) * 128]
+            top = jnp.maximum(top, jnp.max(fold(tile), axis=0))
+        col_out[t : t + 1, :] = column_part(logits, t, top)
+
+
+def first_call(scale, images, texts):
+    return pl.pallas_call(
+        first_body,
+        out_shape=(
+            jax.ShapeDtypeStruct((BLOCK, BLOCK // 2), F32),
+            jax.ShapeDtypeStruct((8, 128), F32),
+        ),
+        in_specs=[SMEM] + [VMEM] * 6,
+        out_specs=(VMEM,) * 2,
+        compiler_params=PARAMS,
+    )(scale, *images, *texts)
+
+
+def second_body(place, scale, logits_0, col_parts, *refs):
+    images = refs[:4]
+    logits_1, row_out, col_out, message, match_out, text_3 = refs[7:13]
+    row_wide = refs[13]
+    text_3[: 3 * ROWS, :] = refs[5][...]
+    text_3[3 * ROWS :, :] = refs[6][...]
+    where = [place[i] for i in range(5)]
+    block_logits(scale[0] * LOG2E, images, (refs[4], text_3), logits_1)
+    halves = (logits_0, logits_1)
     cols = col_ids(where)
     step = 32
     matched = jnp.zeros((8, 128), F32)
-    col_top = [jnp.full((8, 128), -jnp.inf, F32) for _ in range(8)]
+    col_top = [jnp.full((8, 128), -jnp.inf, F32) for _ in range(4)]
     for a in range(4):
         ids = row_ids(where, a)
         for b in range(4):
             for half in range(ROWS // step):
                 at = a * CHUNK + b * ROWS + half * step
-                tiles = [logits[at : at + step, t * 128 : (t + 1) * 128] for t in range(8)]
+                tiles = [
+                    halves[t // 4][at : at + step, (t % 4) * 128 : (t % 4 + 1) * 128] for t in range(8)
+                ]
                 top = tiles[0]
                 for t in range(1, 8):
                     top = jnp.maximum(top, tiles[t])
@@ -158,24 +194,17 @@
                 total = jnp.zeros((step, 128), F32)
                 for t in range(8):
                     total += jnp.exp2(tiles[t] - top)
-                    folded = tiles[t].reshape(step // 8, 8, 128)
-                    col_top[t] = jnp.maximum(col_top[t], jnp.max(folded, axis=0))
+                    if t > 3:
+                        col_top[t - 4] = jnp.maximum(col_top[t - 4], jnp.max(fold(tiles[t]), axis=0))
                     hit = jnp.where(mine == cols[t][0:1], tiles[t], 0.0)
-                    matched += jnp.sum(hit.reshape(step // 8, 8, 128), axis=0)
+                    matched += jnp.sum(fold(hit), axis=0)
                 part = top + LOG2E * jnp.log(jnp.sum(total, axis=1, keepdims=True))
                 row_wide[at : at + step, :] = jnp.broadcast_to(part, (step, 128))
     matched = jnp.broadcast_to(jnp.sum(matched, keepdims=True), (8, 128))
     match_out[...] = matched
     message[16:24, :] = matched
     for t in range(8):
-        top = jnp.max(col_top[t], axis=0, keepdims=True)
-
-        def cols_pass(i, total, t=t, top=top):
-            tile = logits[pl.ds(pl.multiple_of(i * 128, 128), 128), t * 128 : (t + 1) * 128]
-            return total + jnp.sum(jnp.exp2(tile - top).reshape(16, 8, 128), axis=0)
-
-        total = lax.fori_loop(0, 8, cols_pass, jnp.zeros((8, 128), F32), unroll=True)
-        part = top + LOG2E * jnp.log(jnp.sum(total, axis=0, keepdims=True))
+        part = col_parts[t : t + 1, :] if t < 4 else column_part(logits_1, t - 4, col_top[t - 4])
         j, i = t // 2, (t % 2) * 2
         col_out[pl.ds(col_place(where, j, i)[0], 1), :] = part
         col_out[pl.ds(col_place(where, j, i + 1)[0], 1), :] = pltpu.roll(part, 64, 1)
@@ -185,22 +214,22 @@
     message[:16, :] = jnp.where(where[1] == 0, col_out[...], row_out[...])
 
 
-def logits_call(place, scale, images, texts):
-    return pl.pallas_call(
-        logits_body,
+def second_call(place, scale, logits_0, col_parts, images, texts):
+    return pl.pallas_call(
+        second_body,
         out_shape=(
-            jax.ShapeDtypeStruct((BLOCK, BLOCK), F32),
+            jax.ShapeDtypeStruct((BLOCK, BLOCK // 2), F32),
             jax.ShapeDtypeStruct((16, 128), F32),
             jax.ShapeDtypeStruct((16, 128), F32),
             jax.ShapeDtypeStruct((24, 128), F32),
             jax.ShapeDtypeStruct((8, 128), F32),
             PART,
         ),
-        in_specs=[SMEM, SMEM] + [VMEM] * 10,
+        in_specs=[SMEM, SMEM] + [VMEM] * 9,
         out_specs=(VMEM,) * 6,
         scratch_shapes=[pltpu.VMEM((BLOCK, 128), F32)],
         compiler_params=PARAMS,
-    )(place, scale, *images, *texts)
+    )(place, scale, logits_0, col_parts, *images, *texts)
 
 
 def spread_body(place, row, col, matched, got, out):
@@ -258,32 +287,36 @@
     )(place, got)
 
 
-def loss_body(place, got, out):
-    group = place[2] * 4 + place[0] - ((place[3] * 4 + place[4]) >> 1)
-    total = got[0, 4:5, 0:1]
-    for p in range(1, 16):
-        total = total + got[p, 4:5, 0:1]
-    for z in range(NZ):
-        total = total + got[2 * ((z - group) & 7), 0:1, 0:1]
-    out[...] = total * (LN2 / (2.0 * ROWS * 256))
-
-
-def loss_call(place, got):
-    return pl.pallas_call(
-        loss_body,
-        out_shape=jax.ShapeDtypeStruct((1, 1), F32),
-        in_specs=[SMEM, VMEM],
-        out_specs=VMEM,
-        compiler_params=PARAMS,
-    )(place, got)
-
-
-def weights_body(place, scale, logits, mine, other, *refs):
+def digits_of(v):
+    place = lax.broadcasted_iota(jnp.int32, (16, 128), 0)
+    out = jnp.zeros((16, 128), F32)
+    for i in range(DIGITS):
+        unit = 16.0 ** (7 - i)
+        d = jnp.floor(v * (1.0 / unit) + 0.5)
+        v = v - d * unit
+        out = jnp.where(place == i, d, out)
+    return out
+
+
+def value_of(digits):
+    place = lax.broadcasted_iota(jnp.int32, (16, 128), 0)
+    units = jnp.zeros((16, 128), F32)
+    for i in range(DIGITS):
+        units = jnp.where(place == i, 16.0 ** (7 - i), units)
+    return jnp.sum(digits * units, axis=0, keepdims=True)
+
+
+def weights_body(place, scale, logits_0, logits_1, mine, other, *refs):
     images = refs[:4]
     weights = refs[4]
-    outs = refs[5:9]
-    row_wide, row_lse, col_lse = refs[9:12]
+    outs = refs[5:8]
+    row_wide, row_lse, col_lse = refs[8:11]
     first = place[1] == 0
+    shares = jnp.where(first, mine[16:17, :], other[16:17, :]), jnp.where(first, other[16:17, :], mine[16:17, :])
+    for i, share in enumerate(shares):
+        tail = digits_of(share).astype(BF16)
+        for e in range(EMBED // 128):
+            outs[2][i * TAIL : (i + 1) * TAIL, e * 128 : (e + 1) * 128] = tail
     row_lse[...] = jnp.where(first, mine[:16, :], other[:16, :]) + 1.0
     col_lse[...] = jnp.where(first, other[:16, :], mine[:16, :]) + 1.0
     where = [place[i] for i in range(5)]
@@ -306,11 +339,11 @@
             at = a * CHUNK + b * ROWS
             wide = row_wide[at : at + ROWS, :]
             for t in range(8):
-                tile = logits[at : at + ROWS, t * 128 : (t + 1) * 128]
+                tile = (logits_0, logits_1)[t // 4][at : at + ROWS, (t % 4) * 128 : (t % 4 + 1) * 128]
                 both = jnp.exp2(tile - wide) + jnp.exp2(tile - col_line[t])
                 both = both - jnp.where(ids[b] == cols[t][0:1], 1.0, 0.0)
                 weights[at : at + ROWS, t * 128 : (t + 1) * 128] = both.astype(BF16)
-    text_terms(multiplier, weights, images, ((2, 0, outs[0]), (3, 0, outs[1]), (1, 0, outs[2]), (3, 3 * ROWS, outs[3])))
+    text_terms(multiplier, weights, images, ((2, 0, outs[0]), (3, 0, outs[1])))
 
 
 def text_terms(multiplier, weights, images, outs):
@@ -340,7 +373,7 @@
                     preferred_element_type=F32,
                 )
                 acc = term if acc is None else acc + term
-            out[:, e * 256 : (e + 1) * 256] = (multiplier * acc).astype(BF16)
+            out[:CHUNK, e * 256 : (e + 1) * 256] = (multiplier * acc).astype(BF16)
 
 
 PART = jax.ShapeDtypeStruct((CHUNK, EMBED), BF16)
@@ -353,74 +386,113 @@
             jax.ShapeDtypeStruct((BLOCK, BLOCK), BF16),
             PART,
             jax.ShapeDtypeStruct((3 * ROWS, EMBED), BF16),
-            PART,
-            jax.ShapeDtypeStruct((ROWS, EMBED), BF16),
+            jax.ShapeDtypeStruct((2 * TAIL, EMBED), BF16),
         ),
-        in_specs=[SMEM, SMEM] + [VMEM] * 7,
-        out_specs=(VMEM,) * 5,
+        in_specs=[SMEM, SMEM] + [VMEM] * 8,
+        out_specs=(VMEM,) * 4,
         scratch_shapes=[
             pltpu.VMEM((BLOCK, 128), F32),
             pltpu.VMEM((16, 128), F32),
             pltpu.VMEM((16, 128), F32),
         ],
         compiler_params=PARAMS,
-    )(place, scale, logits, mine, other, *images)
-
-
-def image_body(scale, weights, *refs):
+    )(place, scale, *logits, mine, other, *images)
+
+
+def text_body(scale, weights, *refs):
+    text_terms(scale[0], weights, refs[:4], ((1, 0, refs[4]), (3, 3 * ROWS, refs[5])))
+
+
+def text_call(scale, weights, images):
+    return pl.pallas_call(
+        text_body,
+        out_shape=(PART, jax.ShapeDtypeStruct((ROWS, EMBED), BF16)),
+        in_specs=[SMEM] + [VMEM] * 5,
+        out_specs=(VMEM,) * 2,
+        compiler_params=PARAMS,
+    )(scale, weights, *images)
+
+
+def image_body(scale, after, digits, weights, *refs):
     image_terms(scale[0], weights, refs[:4], dict(zip((2, 1, 3), refs[4:])))
-
-
-def image_call(scale, weights, texts):
+    for out in refs[4:]:
+        out[CHUNK:, :] = digits[TAIL:, :]
+
+
+def image_call(scale, after, digits, weights, texts):
     return pl.pallas_call(
         image_body,
-        out_shape=(PART,) * 3,
-        in_specs=[SMEM] + [VMEM] * 5,
+        out_shape=(jax.ShapeDtypeStruct((CHUNK + TAIL, EMBED), BF16),) * 3,
+        in_specs=[SMEM] + [VMEM] * 7,
         out_specs=(VMEM,) * 3,
         compiler_params=PARAMS,
-    )(scale, weights, *texts)
-
-
-def rest_body(place, scale, mine, other, weights, *refs):
+    )(scale, after, digits, weights, *texts)
+
+
+def rest_body(scale, weights, *refs):
     images, texts, outs = refs[:4], refs[4:8], refs[8:]
     text_terms(scale[0], weights, images, ((0, 0, outs[0]),))
     image_terms(scale[0], weights, texts, {0: outs[1]})
-    core_0 = jnp.where(place[1] == 0, mine[16:24, :], other[16:24, :])
-    core_1 = jnp.where(place[1] == 0, other[16:24, :], mine[16:24, :])
-    both = jnp.where(lax.broadcasted_iota(jnp.int32, (8, 128), 0) < 4, core_0, core_1)
-    for i in range(16):
-        outs[2][i] = both
-
-
-def rest_call(place, scale, mine, other, weights, images, texts):
+
+
+def rest_call(scale, weights, images, texts):
     return pl.pallas_call(
         rest_body,
-        out_shape=(PART, PART, jax.ShapeDtypeStruct((16, 8, 128), F32)),
-        in_specs=[SMEM, SMEM] + [VMEM] * 11,
-        out_specs=(VMEM,) * 3,
-        compiler_params=PARAMS,
-    )(place, scale, mine, other, weights, *images, *texts)
+        out_shape=(PART, PART),
+        in_specs=[SMEM] + [VMEM] * 9,
+        out_specs=(VMEM,) * 2,
+        compiler_params=PARAMS,
+    )(scale, weights, *images, *texts)
+
+
+def add_rows(refs, rows, terms, out, to):
+    for at in range(0, rows, 16):
+        total = None
+        for i, skip in terms:
+            v = refs[i][skip + at : skip + at + 16, :].astype(F32)
+            total = v if total is None else total + v
+        out[to + at : to + at + 16, :] = total.astype(out.dtype)
 
 
 def sums_body(n, plan, *refs):
-    for (rows, terms), out in zip(plan, refs[n:]):
-        for at in range(0, rows, 16):
-            total = None
-            for i, skip in terms:
-                v = refs[i][skip + at : skip + at + 16, :].astype(F32)
-                total = v if total is None else total + v
-            out[at : at + 16, :] = total.astype(out.dtype)
+    for parts, out in zip(plan, refs[n:]):
+        to = 0
+        for rows, terms in parts:
+            add_rows(refs, rows, terms, out, to)
+            to += rows
 
 
 def sums(arrays, *plan):
-    out = pl.pallas_call(
+    return pl.pallas_call(
         lambda *refs: sums_body(len(arrays), plan, *refs),
-        out_shape=tuple(jax.ShapeDtypeStruct((rows, EMBED), BF16) for rows, _ in plan),
+        out_shape=tuple(
+            jax.ShapeDtypeStruct((sum(rows for rows, _ in parts), EMBED), BF16) for parts in plan
+        ),
         in_specs=[VMEM] * len(arrays),
         out_specs=(VMEM,) * len(plan),
         compiler_params=PARAMS,
     )(*arrays)
-    return out if len(plan) > 1 else out[0]
+
+
+def last_body(*refs):
+    digits, image_out, text_out, loss_out = refs[7:]
+    add_rows(refs, ROWS, [(i, 0) for i in range(4)], image_out, 0)
+    add_rows(refs, ROWS, [(i, 0) for i in range(4, 7)], text_out, 0)
+    total = -digits[:TAIL, :128].astype(F32)
+    for r in refs[:7]:
+        total += r[ROWS:, :128].astype(F32)
+    loss_out[...] = value_of(total)[:, 0:1] * (LN2 / (2.0 * ROWS * 256))
+
+
+def last_call(shards, texts, digits):
+    grad = jax.ShapeDtypeStruct((ROWS, EMBED), BF16)
+    return pl.pallas_call(
+        last_body,
+        out_shape=(grad, grad, jax.ShapeDtypeStruct((1, 1), F32)),
+        in_specs=[VMEM] * 8,
+        out_specs=(VMEM,) * 3,
+        compiler_params=PARAMS,
+    )(*shards, *texts, digits)
 
 
 def local(image_emb, text_emb, logit_scale):
@@ -429,47 +501,57 @@
     chip, image = pack([text_emb, core_swap(text_emb), image_emb], ((0, 64), (1, 64)), ((2, 64),))
     next_1, next_4 = z_shift(chip, -1), z_shift(text_emb, 4)
     near = [plane_shift(image, k, True) for k in (1, 2, 3)]
-    own, text_0, next_4 = pack(
+    own, text_0, side = pack(
         [image] + near + [chip, next_1, next_4],
         ((0, 64), (1, 64), (2, 64), (3, 64)),
         ((4, 128), (5, 128)),
-        ((6, 64),),
+        ((5, 128), (6, 64)),
     )
     text_1 = z_shift(text_0, -2)
     images = [own] + [plane_shift(own, k, False) for k in (1, 2, 3)]
-    texts = [text_0, text_1, core_swap(text_1)]
-
-    logits, row_part, col_part, message, matched, text_3 = logits_call(
-        place, logit_scale, images, texts + [core_swap(next_1), core_swap(next_4), next_4]
-    )
-    texts.append(text_3)
+    text_2 = core_swap(text_1)
+    logits_0, col_parts = first_call(logit_scale, images, [text_0, text_1])
+    logits_1, row_part, col_part, message, matched, text_3 = second_call(
+        place, logit_scale, logits_0, col_parts, images, [text_2, core_swap(side), next_4]
+    )
+    texts = [text_0, text_1, text_2, text_3]
 
     spread = spread_call(place, row_part, col_part, matched, core_swap(message))
     mine, message = join_call(place, exchange(spread, plane_or_ring()))
-    other = core_swap(message)
-    weights, text_2, text_3, text_1, far = weights_call(place, logit_scale, logits, mine, other, images)
+    weights, text_2, text_3, digits = weights_call(
+        place, logit_scale, (logits_0, logits_1), mine, core_swap(message), images
+    )
 
     other_1, other_3 = core_swap(text_2), core_swap(text_3)
+    text_1, far = text_call(logit_scale, weights, images)
+    rows_tail = (TAIL, ((4, 0),))
     pairs, far = sums(
-        [text_1, other_1, far, other_3], (256, ((0, 0), (1, 0))), (64, ((2, 0), (3, 128)))
-    )
+        [text_1, other_1, far, other_3, digits],
+        ((256, ((0, 0), (1, 0))), rows_tail),
+        ((64, ((2, 0), (3, 128))), rows_tail),
+    )
+    image_parts = image_call(logit_scale, pairs, digits, weights, texts)
     pairs, next_4 = z_shift(pairs, 2), z_shift(far, 4)
-    image_parts = image_call(logit_scale, weights, texts)
     back = [plane_shift(v, -k, False) for v, k in zip(image_parts, (2, 1, 3))]
-    text_0, image_0, shares = rest_call(place, logit_scale, mine, other, weights, images, texts)
-    mean_loss = loss_call(place, exchange(shares, slanted()))
-
+    text_0, image_0 = rest_call(logit_scale, weights, images, texts)
+
+    rows_tail = (TAIL, ((2, 256), (7, 0)))
+    cols_tail = (TAIL, ((4, 256), (5, 256), (6, 256), (7, 16)))
     next_1, mine, *pieces = sums(
-        [text_0, other_3, pairs, image_0] + back + [next_4, mean_loss],
-        (128, ((0, 128), (1, 0), (2, 128))),
-        (128, ((0, 0), (2, 0))),
-        *[(64, [(i, 64 * k) for i in range(3, 7)]) for k in range(4)],
+        [text_0, other_3, pairs, image_0] + back + [digits, next_4],
+        ((128, ((0, 128), (1, 0), (2, 128))), rows_tail),
+        ((128, ((0, 0), (2, 0))), rows_tail),
+        *[((64, [(i, 64 * k) for i in range(3, 7)]), cols_tail) for k in range(4)],
     )
     next_1 = z_shift(next_1, 1)
     shards = [pieces[0]] + [plane_shift(pieces[k], -k, True) for k in (2, 1, 3)]
-    mine, other = sums([mine, next_1], (64, ((0, 0), (1, 0))), (64, ((0, 64), (1, 64))))
-    image_grad = sums(shards, (64, [(i, 0) for i in range(4)]))
-    text_grad = sums([mine, core_swap(other), next_4], (64, ((0, 0), (1, 0), (2, 0))))
+    rows_tail = (TAIL, ((0, 128), (1, 128)))
+    mine, other = sums(
+        [mine, next_1],
+        ((64, ((0, 0), (1, 0))), rows_tail),
+        ((64, ((0, 64), (1, 64))), rows_tail),
+    )
+    image_grad, text_grad, mean_loss = last_call(shards, [mine, core_swap(other), next_4], digits)
     return mean_loss.reshape(1), image_grad, text_grad
 
 

time: 137 us -> 131 us (0.956)
  blocking collectives: 39.2 us -> 13.3 us
  waiting for transfers between devices: 31.6 us -> 55.9 us
  starting transfers between devices: 36 us -> 34.1 us
  local copies, waits for them, and re-layouts: 3.5 us -> 1.92 us
    all_to_all x2 -> x1, blocking collectives: 39.2 us -> 13.3 us  [exchange(): return lax.all_to_all(v, AXES, 0, 0, axis_index_groups=groups)]
    ppermute x6, waiting for transfers between devices: 19 us -> 42.7 us  [z_shift(): return lax.ppermute(v, ('zl', 'core', 'zh'), pairs)]
    pallas_call x4 -> x6, Pallas kernels: 12 us -> 16.9 us  [the longest x1 3.93 us: second_call(): pl.pallas_call(second_body, out_shape=(jax.ShapeDtypeStruct((BLOCK, BLOCK...]
    pallas_call x1, Pallas kernels: 7.31 us -> 3.77 us  [weights_call(): pl.pallas_call(weights_body, out_shape=(jax.ShapeDtypeStruct((BLOCK, BLOC...]
    ppermute x12, waiting for transfers between devices: 6.16 us -> 9.62 us  [plane_shift(): return lax.ppermute(v, ('core', 'zh', 'y', 'x'), pairs)]
    ppermute x9 -> x8, waiting for transfers between devices: 6.52 us -> 3.6 us  [core_swap(): return lax.ppermute(v, 'core', [(0, 1), (1, 0)])]
    pallas_call x5 -> x3, Pallas kernels: 2.91 us -> 0.88 us  [sums(): pl.pallas_call(lambda *refs: sums_body(len(arrays), plan, *refs), out_sha...]
    unnamed x8 -> x4, local copies, waits for them, and re-layouts: 3.41 us -> 1.83 us
  transfers between devices with their start and end apart: 27 -> 26, of which waited for: 12 -> 14; matrix products, arithmetic and copies ran while one was open for 0% -> 0% of each run, Pallas kernels for 5% -> 7%
where the time goes in v6:
time: 131 us; the launch traced here: 130 us
  waiting for transfers between devices  55.9 us (43%)
  starting transfers between devices  34.1 us (26%)
  Pallas kernels  23.8 us (18%)
  blocking collectives  13.3 us (10%)
  local copies, waits for them, and re-layouts  1.92 us (1%)
  between operations  1.44 us (1%)
    ppermute x6, waiting for transfers between devices, z_shift(): return lax.ppermute(v, ('zl', 'core', 'zh'), pairs)  42.7 us
    ppermute x12, starting transfers between devices, plane_shift(): return lax.ppermute(v, ('core', 'zh', 'y', 'x'), pairs)  16.4 us
    ppermute x6, starting transfers between devices, z_shift(): return lax.ppermute(v, ('zl', 'core', 'zh'), pairs)  14.1 us
    all_to_all x1, blocking collectives, exchange(): return lax.all_to_all(v, AXES, 0, 0, axis_index_groups=groups)  13.3 us
    ppermute x12, waiting for transfers between devices, plane_shift(): return lax.ppermute(v, ('core', 'zh', 'y', 'x'), pairs)  9.62 us
    pallas_call x1, Pallas kernels, second_call(): pl.pallas_call(second_body, out_shape=(jax.ShapeDtypeStruct((BLOCK, BLOCK...  3.93 us
    pallas_call x1, Pallas kernels, weights_call(): pl.pallas_call(weights_body, out_shape=(jax.ShapeDtypeStruct((BLOCK, BLOC...  3.77 us
    ppermute x8, starting transfers between devices, core_swap(): return lax.ppermute(v, 'core', [(0, 1), (1, 0)])  3.66 us
  transfers between devices with their start and end apart: 26, of which 14 were waited for; matrix products, arithmetic and copies ran while one was open for 0% of the time, Pallas kernels for 7%

profile of v6, /device:TPU:32, one launch (start us, length us, event | category | flops | bytes accessed | tf_op | source)
XLA Modules:
  0.0 130.5 jit_solution(5767497172962077244)
XLA Ops:
  0.6 0.1 collective-permute-start
  0.7 1.6 %collective-permute-done.refs_1_ = bf16[64,1280]{1,0:T(8,128)(2,1)S(1)} collective-permute-done((bf16[64,1280]{1,0:T(8,128)(2,1)}, bf16[64,1280]{1,0:T(8,128)(2,1)S(1)}, u32[]{:S(2)}, u32[]{:S(2)}) %collective-permute-start) | collective-permute-done | bytes 163872 | tf_op jit(solution)/shard_map/ppermute | solution.py:48
  2.3 0.9 copy-done
  3.2 0.9 copy-done.1
  4.2 1.9 %collective-permute-start.4 = (bf16[128,1280]{1,0:T(8,128)(2,1)S(1)}, bf16[128,1280]{1,0:T(8,128)(2,1)S(1)}, u32[]{:S(2)}, u32[]{:S(2)}) collective-permute-start(bf16[128,1280]{1,0:T(8,128)(2,1)S(1)} %get-tuple-element.43.refs_4_), channel_id=1, source_target_pairs={{0,208},{64,0},{128,64},{192,128},{16,192},{80,16},{144,80},{208,1... | collective-permute-start | bytes 983048 | tf_op jit(solution)/shard_map/ppermute | solution.py:44
  6.1 5.5 %collective-permute-start.5 = (bf16[64,1280]{1,0:T(8,128)(2,1)S(1)}, bf16[64,1280]{1,0:T(8,128)(2,1)S(1)}, u32[]{:S(2)}, u32[]{:S(2)}) collective-permute-start(bf16[64,1280]{1,0:T(8,128)(2,1)S(1)} %copy-done.1), channel_id=1, source_target_pairs={{0,16},{64,80},{128,144},{192,208},{16,0},{80,64},{144,128},{208,1... | collective-permute-start | bytes 491528 | tf_op jit(solution)/shard_map/ppermute | solution.py:44
  11.6 2.8 %collective-permute-start.3 = (bf16[64,1280]{1,0:T(8,128)(2,1)S(1)}, bf16[64,1280]{1,0:T(8,128)(2,1)S(1)}, u32[]{:S(2)}, u32[]{:S(2)}) collective-permute-start(bf16[64,1280]{1,0:T(8,128)(2,1)S(1)} %get-tuple-element.42.refs_0_), channel_id=1, source_target_pairs={{0,3},{1,0},{2,1},{3,2},{4,7},{5,4},{6,5},{7,6},{8,11},{9,8},{10,9... | collective-permute-start | bytes 491528 | tf_op jit(solution)/shard_map/ppermute | solution.py:35
  14.3 0.8 collective-permute-start.2
  15.1 0.9 collective-permute-start.1
  16.0 7.1 %collective-permute-done.5.refs_6_ = bf16[64,1280]{1,0:T(8,128)(2,1)S(1)} collective-permute-done((bf16[64,1280]{1,0:T(8,128)(2,1)S(1)}, bf16[64,1280]{1,0:T(8,128)(2,1)S(1)}, u32[]{:S(2)}, u32[]{:S(2)}) %collective-permute-start.5) | collective-permute-done | bytes 163872 | tf_op jit(solution)/shard_map/ppermute | solution.py:44
  23.1 0.0 collective-permute-done.3.refs_3_
  23.1 0.0 collective-permute-done.2.refs_2_
  23.1 0.9 shard_map.59
  24.0 1.9 %collective-permute-start.9 = (bf16[256,1280]{1,0:T(8,128)(2,1)S(1)}, bf16[256,1280]{1,0:T(8,128)(2,1)}, u32[]{:S(2)}, u32[]{:S(2)}) collective-permute-start(bf16[256,1280]{1,0:T(8,128)(2,1)S(1)} %get-tuple-element.45.refs_4_.refs_0_), channel_id=1, source_target_pairs={{0,144},{64,208},{128,0},{192,64},{16,128},{80,192},{144,16},{208,... | collective-permute-start | bytes 1966088 | tf_op jit(solution)/shard_map/ppermute | solution.py:44
  25.9 3.0 %collective-permute-start.8 = (bf16[256,1280]{1,0:T(8,128)(2,1)S(1)}, bf16[256,1280]{1,0:T(8,128)(2,1)S(1)}, u32[]{:S(2)}, u32[]{:S(2)}) collective-permute-start(bf16[256,1280]{1,0:T(8,128)(2,1)S(1)} %get-tuple-element.44.refs_0_), channel_id=1, source_target_pairs={{0,12},{1,13},{2,14},{3,15},{4,0},{5,1},{6,2},{7,3},{8,4},{9,5},{1... | collective-permute-start | bytes 1966088 | tf_op jit(solution)/shard_map/ppermute | solution.py:35
  28.9 0.6 collective-permute-start.7
  29.5 1.0 collective-permute-start.6
  30.5 11.0 %collective-permute-done.9.refs_5_.refs_1_ = bf16[256,1280]{1,0:T(8,128)(2,1)} collective-permute-done((bf16[256,1280]{1,0:T(8,128)(2,1)S(1)}, bf16[256,1280]{1,0:T(8,128)(2,1)}, u32[]{:S(2)}, u32[]{:S(2)}) %collective-permute-start.9) | collective-permute-done | bytes 655392 | tf_op jit(solution)/shard_map/ppermute | solution.py:44
  41.5 0.0 collective-permute-start.10
  41.5 0.5 collective-permute-start.11
  42.7 0.1 stack.23.place
  42.8 1.2 collective-permute-done.8.refs_3_
  44.0 0.0 collective-permute-done.7.refs_2_
  44.0 4.0 %collective-permute-done.6.refs_1_ = bf16[256,1280]{1,0:T(8,128)(2,1)S(1)} collective-permute-done((bf16[256,1280]{1,0:T(8,128)(2,1)S(1)}, bf16[256,1280]{1,0:T(8,128)(2,1)S(1)}, u32[]{:S(2)}, u32[]{:S(2)}) %collective-permute-start.6) | collective-permute-done | bytes 655392 | tf_op jit(solution)/shard_map/ppermute | solution.py:35
  48.0 2.9 %shard_map.60 = (f32[1024,512]{1,0:T(8,128)S(1)}, f32[8,128]{1,0:T(8,128)S(1)}) custom-call(f32[1]{0:T(128)S(6)} %copy.6.scale, bf16[256,1280]{1,0:T(8,128)(2,1)S(1)} %get-tuple-element.44.refs_0_, bf16[256,1280]{1,0:T(8,128)(2,1)S(1)} %collective-permute-done.6.refs_1_, bf16[256,1280]{1,0:T(8,128)(2,1)S(1)} %collective-permute-done.7.refs_2_, ...), custom_call_target="tpu_custom_call" | custom-call | tf_op jit(solution)/shard_map/pallas_call | solution.py:156
  51.0 0.0 collective-permute-done.11.refs_5_
  51.0 0.0 collective-permute-done.10.refs_4_.refs_6_.refs_2_
  51.0 3.9 %shard_map.61 = (f32[1024,512]{1,0:T(8,128)S(1)}, f32[16,128]{1,0:T(8,128)S(1)}, f32[16,128]{1,0:T(8,128)S(1)}, f32[24,128]{1,0:T(8,128)S(1)}, f32[8,128]{1,0:T(8,128)S(1)}, /*index=5*/bf16[256,1280]{1,0:T(8,128)(2,1)S(1)}) custom-call(s32[5]{0:T(128)S(1)} %stack.23.place, f32[1]{0:T(128)S(6)} %copy.6.scale, f32[1024,512]{1,0:T(8,128)S(1)} %get-tuple-element.46.logits_0, ...), custom_call_target="tpu_custom_call" | custom-call | tf_op jit(solution)/shard_map/pallas_call | solution.py:218
  54.9 0.3 collective-permute-start.12
  55.2 1.2 collective-permute-done.12.got
  56.4 0.6 shard_map.62
  56.9 13.3 %all_to_all.5.got = f32[16,40,128]{2,1,0:T(8,128)S(1)} all-to-all(f32[16,40,128]{2,1,0:T(8,128)S(1)} %shard_map.62), channel_id=1, replica_groups={{0,1,2,3,4,5,6,7,8,9,10,11,12,13,14,15},{64,65,66,67,68,69,70,71,72,73,..., dimensions={0} | all-to-all | bytes 655360 | tf_op jit(solution)/shard_map/all_to_all | solution.py:63
  70.3 0.7 shard_map.63
  71.0 2.1 %collective-permute-start.13 = (f32[24,128]{1,0:T(8,128)S(1)}, f32[24,128]{1,0:T(8,128)S(1)}, u32[]{:S(2)}, u32[]{:S(2)}) collective-permute-start(f32[24,128]{1,0:T(8,128)S(1)} %get-tuple-element.55), channel_id=1, source_target_pairs={{0,32},{32,0},{1,33},{33,1},{2,34},{34,2},{3,35},{35,3},{4,36},{36... | collective-permute-start | bytes 36872 | tf_op jit(solution)/shard_map/ppermute | solution.py:48
  73.1 0.8 collective-permute-done.13.other
  73.9 3.8 %shard_map.64 = (bf16[1024,1024]{1,0:T(8,128)(2,1)S(1)}, bf16[256,1280]{1,0:T(8,128)(2,1)S(1)}, bf16[192,1280]{1,0:T(8,128)(2,1)S(1)}, bf16[32,1280]{1,0:T(8,128)(2,1)S(1)}) custom-call(s32[5]{0:T(128)S(1)} %stack.23.place, f32[1]{0:T(128)S(6)} %copy.6.scale, f32[1024,512]{1,0:T(8,128)S(1)} %get-tuple-element.46.logits_0, ...), custom_call_target="tpu_custom_call" | custom-call | tf_op jit(solution)/shard_map/pallas_call | solution.py:383
  77.7 0.4 collective-permute-start.15
  78.1 0.2 collective-permute-start.14
  78.3 2.7 %shard_map.66 = (bf16[256,1280]{1,0:T(8,128)(2,1)S(1)}, bf16[64,1280]{1,0:T(8,128)(2,1)S(1)}) custom-call(f32[1]{0:T(128)S(6)} %copy.6.scale, bf16[1024,1024]{1,0:T(8,128)(2,1)S(1)} %get-tuple-element.56.weights, bf16[256,1280]{1,0:T(8,128)(2,1)S(1)} %get-tuple-element.44.refs_0_, bf16[256,1280]{1,0:T(8,128)(2,1)S(1)} %collective-permute-done.6.refs_1_, ...), custom_call_target="tpu_custom_call" | custom-call | tf_op jit(solution)/shard_map/pallas_call | solution.py:407
  81.0 0.0 collective-permute-done.14.refs_3_.refs_1_
  81.0 0.2 shard_map.67
  81.2 3.6 %shard_map.68 = (bf16[272,1280]{1,0:T(8,128)(2,1)S(1)}, bf16[272,1280]{1,0:T(8,128)(2,1)S(1)}, bf16[272,1280]{1,0:T(8,128)(2,1)S(1)}) custom-call(f32[1]{0:T(128)S(6)} %copy.6.scale, bf16[272,1280]{1,0:T(8,128)(2,1)S(1)} %get-tuple-element.64.after, bf16[32,1280]{1,0:T(8,128)(2,1)S(1)} %get-tuple-element.63.refs_4_.digits.refs_7_, ...), custom_call_target="tpu_custom_call" | custom-call | tf_op jit(solution)/shard_map/pallas_call | solution.py:423
  84.8 0.4 collective-permute-start.17
  85.3 3.2 %collective-permute-start.18 = (bf16[272,1280]{1,0:T(8,128)(2,1)S(1)}, bf16[272,1280]{1,0:T(8,128)(2,1)S(1)}, u32[]{:S(2)}, u32[]{:S(2)}) collective-permute-start(bf16[272,1280]{1,0:T(8,128)(2,1)S(1)} %get-tuple-element.67), channel_id=1, source_target_pairs={{0,12},{1,13},{2,14},{3,15},{4,0},{5,1},{6,2},{7,3},{8,4},{9,5},{1... | collective-permute-start | bytes 2088968 | tf_op jit(solution)/shard_map/ppermute | solution.py:35
  88.4 1.2 collective-permute-start.16
  89.7 2.2 %collective-permute-start.20 = (bf16[80,1280]{1,0:T(8,128)(2,1)S(1)}, bf16[80,1280]{1,0:T(8,128)(2,1)S(1)}, u32[]{:S(2)}, u32[]{:S(2)}) collective-permute-start(bf16[80,1280]{1,0:T(8,128)(2,1)S(1)} %get-tuple-element.69), channel_id=1, source_target_pairs={{0,16},{64,80},{128,144},{192,208},{16,0},{80,64},{144,128},{208,1... | collective-permute-start | bytes 614408 | tf_op jit(solution)/shard_map/ppermute | solution.py:44
  91.8 2.9 %shard_map.65 = (bf16[256,1280]{1,0:T(8,128)(2,1)S(1)}, bf16[256,1280]{1,0:T(8,128)(2,1)S(1)}) custom-call(f32[1]{0:T(128)S(6)} %copy.6.scale, bf16[1024,1024]{1,0:T(8,128)(2,1)S(1)} %get-tuple-element.56.weights, bf16[256,1280]{1,0:T(8,128)(2,1)S(1)} %get-tuple-element.44.refs_0_, bf16[256,1280]{1,0:T(8,128)(2,1)S(1)} %collective-permute-done.6.refs_1_, ...), custom_call_target="tpu_custom_call" | custom-call | tf_op jit(solution)/shard_map/pallas_call | solution.py:439
  94.8 9.2 %collective-permute-done.20.refs_8_.refs_6_ = bf16[80,1280]{1,0:T(8,128)(2,1)S(1)} collective-permute-done((bf16[80,1280]{1,0:T(8,128)(2,1)S(1)}, bf16[80,1280]{1,0:T(8,128)(2,1)S(1)}, u32[]{:S(2)}, u32[]{:S(2)}) %collective-permute-start.20) | collective-permute-done | bytes 204832 | tf_op jit(solution)/shard_map/ppermute | solution.py:44
  104.0 0.0 collective-permute-done.17.refs_4_
  104.0 0.0 collective-permute-done.18.refs_5_
  104.0 0.9 collective-permute-done.19.refs_6_
  104.9 12.9 %collective-permute-done.16.refs_2_ = bf16[272,1280]{1,0:T(8,128)(2,1)S(1)} collective-permute-done((bf16[272,1280]{1,0:T(8,128)(2,1)S(1)}, bf16[272,1280]{1,0:T(8,128)(2,1)S(1)}, u32[]{:S(2)}, u32[]{:S(2)}) %collective-permute-start.16) | collective-permute-done | bytes 696352 | tf_op jit(solution)/shard_map/ppermute | solution.py:44
  117.8 0.6 shard_map.69
  118.4 1.4 %collective-permute-start.24 = (bf16[144,1280]{1,0:T(8,128)(2,1)S(1)}, bf16[144,1280]{1,0:T(8,128)(2,1)S(1)}, u32[]{:S(2)}, u32[]{:S(2)}) collective-permute-start(bf16[144,1280]{1,0:T(8,128)(2,1)S(1)} %get-tuple-element.75), channel_id=1, source_target_pairs={{0,64},{64,128},{128,192},{192,16},{16,80},{80,144},{144,208},{208... | collective-permute-start | bytes 1105928 | tf_op jit(solution)/shard_map/ppermute | solution.py:44
  119.9 1.7 %collective-permute-start.21 = (bf16[80,1280]{1,0:T(8,128)(2,1)S(1)}, bf16[80,1280]{1,0:T(8,128)(2,1)S(1)}, u32[]{:S(2)}, u32[]{:S(2)}) collective-permute-start(bf16[80,1280]{1,0:T(8,128)(2,1)S(1)} %get-tuple-element.71), channel_id=1, source_target_pairs={{0,2},{1,3},{2,0},{3,1},{4,6},{5,7},{6,4},{7,5},{8,10},{9,11},{10,... | collective-permute-start | bytes 614408 | tf_op jit(solution)/shard_map/ppermute | solution.py:35
  121.5 1.1 collective-permute-start.22
  122.7 0.9 collective-permute-start.23
  123.6 2.5 %collective-permute-done.24.refs_1_ = bf16[144,1280]{1,0:T(8,128)(2,1)S(1)} collective-permute-done((bf16[144,1280]{1,0:T(8,128)(2,1)S(1)}, bf16[144,1280]{1,0:T(8,128)(2,1)S(1)}, u32[]{:S(2)}, u32[]{:S(2)}) %collective-permute-start.24) | collective-permute-done | bytes 368672 | tf_op jit(solution)/shard_map/ppermute | solution.py:44
  126.0 0.1 shard_map.70
  126.1 0.1 collective-permute-start.25
  126.2 0.9 collective-permute-done.21.refs_1_
  127.1 0.9 collective-permute-done.22.refs_2_
  128.1 1.6 %collective-permute-done.23.refs_3_ = bf16[80,1280]{1,0:T(8,128)(2,1)S(1)} collective-permute-done((bf16[80,1280]{1,0:T(8,128)(2,1)S(1)}, bf16[80,1280]{1,0:T(8,128)(2,1)S(1)}, u32[]{:S(2)}, u32[]{:S(2)}) %collective-permute-start.23) | collective-permute-done | bytes 204832 | tf_op jit(solution)/shard_map/ppermute | solution.py:35
  129.6 0.8 shard_map.71
  (8 shorter events, 0.0 us)
Async XLA Ops:
  0.6 1.7 %collective-permute-start = (bf16[64,1280]{1,0:T(8,128)(2,1)}, bf16[64,1280]{1,0:T(8,128)(2,1)S(1)}, u32[]{:S(2)}, u32[]{:S(2)}) collective-permute-start(bf16[64,1280]{1,0:T(8,128)(2,1)} %refs_0_.1), channel_id=1, source_target_pairs={{0,32},{32,0},{1,33},{33,1},{2,34},{34,2},{3,35},{35,3},{4,36},{36... | collective-permute-start | bytes 491528 | tf_op jit(solution)/shard_map/ppermute | solution.py:48
  2.3 0.9 copy-start
  3.2 0.9 copy-start.1
  4.2 18.9 %collective-permute-start.4 = (bf16[128,1280]{1,0:T(8,128)(2,1)S(1)}, bf16[128,1280]{1,0:T(8,128)(2,1)S(1)}, u32[]{:S(2)}, u32[]{:S(2)}) collective-permute-start(bf16[128,1280]{1,0:T(8,128)(2,1)S(1)} %get-tuple-element.43.refs_4_), channel_id=1, source_target_pairs={{0,208},{64,0},{128,64},{192,128},{16,192},{80,16},{144,80},{208,1... | collective-permute-start | bytes 983048 | tf_op jit(solution)/shard_map/ppermute | solution.py:44
  6.1 17.0 %collective-permute-start.5 = (bf16[64,1280]{1,0:T(8,128)(2,1)S(1)}, bf16[64,1280]{1,0:T(8,128)(2,1)S(1)}, u32[]{:S(2)}, u32[]{:S(2)}) collective-permute-start(bf16[64,1280]{1,0:T(8,128)(2,1)S(1)} %copy-done.1), channel_id=1, source_target_pairs={{0,16},{64,80},{128,144},{192,208},{16,0},{80,64},{144,128},{208,1... | collective-permute-start | bytes 491528 | tf_op jit(solution)/shard_map/ppermute | solution.py:44
  11.6 11.5 %collective-permute-start.3 = (bf16[64,1280]{1,0:T(8,128)(2,1)S(1)}, bf16[64,1280]{1,0:T(8,128)(2,1)S(1)}, u32[]{:S(2)}, u32[]{:S(2)}) collective-permute-start(bf16[64,1280]{1,0:T(8,128)(2,1)S(1)} %get-tuple-element.42.refs_0_), channel_id=1, source_target_pairs={{0,3},{1,0},{2,1},{3,2},{4,7},{5,4},{6,5},{7,6},{8,11},{9,8},{10,9... | collective-permute-start | bytes 491528 | tf_op jit(solution)/shard_map/ppermute | solution.py:35
  14.3 8.8 %collective-permute-start.2 = (bf16[64,1280]{1,0:T(8,128)(2,1)S(1)}, bf16[64,1280]{1,0:T(8,128)(2,1)S(1)}, u32[]{:S(2)}, u32[]{:S(2)}) collective-permute-start(bf16[64,1280]{1,0:T(8,128)(2,1)S(1)} %get-tuple-element.42.refs_0_), channel_id=1, source_target_pairs={{0,2},{1,3},{2,0},{3,1},{4,6},{5,7},{6,4},{7,5},{8,10},{9,11},{10,... | collective-permute-start | bytes 491528 | tf_op jit(solution)/shard_map/ppermute | solution.py:35
  15.1 8.0 %collective-permute-start.1 = (bf16[64,1280]{1,0:T(8,128)(2,1)S(1)}, bf16[64,1280]{1,0:T(8,128)(2,1)S(1)}, u32[]{:S(2)}, u32[]{:S(2)}) collective-permute-start(bf16[64,1280]{1,0:T(8,128)(2,1)S(1)} %get-tuple-element.42.refs_0_), channel_id=1, source_target_pairs={{0,1},{1,2},{2,3},{3,0},{4,5},{5,6},{6,7},{7,4},{8,9},{9,10},{10,1... | collective-permute-start | bytes 491528 | tf_op jit(solution)/shard_map/ppermute | solution.py:35
  24.0 17.5 %collective-permute-start.9 = (bf16[256,1280]{1,0:T(8,128)(2,1)S(1)}, bf16[256,1280]{1,0:T(8,128)(2,1)}, u32[]{:S(2)}, u32[]{:S(2)}) collective-permute-start(bf16[256,1280]{1,0:T(8,128)(2,1)S(1)} %get-tuple-element.45.refs_4_.refs_0_), channel_id=1, source_target_pairs={{0,144},{64,208},{128,0},{192,64},{16,128},{80,192},{144,16},{208,... | collective-permute-start | bytes 1966088 | tf_op jit(solution)/shard_map/ppermute | solution.py:44
  25.9 18.1 %collective-permute-start.8 = (bf16[256,1280]{1,0:T(8,128)(2,1)S(1)}, bf16[256,1280]{1,0:T(8,128)(2,1)S(1)}, u32[]{:S(2)}, u32[]{:S(2)}) collective-permute-start(bf16[256,1280]{1,0:T(8,128)(2,1)S(1)} %get-tuple-element.44.refs_0_), channel_id=1, source_target_pairs={{0,12},{1,13},{2,14},{3,15},{4,0},{5,1},{6,2},{7,3},{8,4},{9,5},{1... | collective-permute-start | bytes 1966088 | tf_op jit(solution)/shard_map/ppermute | solution.py:35
  28.9 15.1 %collective-permute-start.7 = (bf16[256,1280]{1,0:T(8,128)(2,1)S(1)}, bf16[256,1280]{1,0:T(8,128)(2,1)S(1)}, u32[]{:S(2)}, u32[]{:S(2)}) collective-permute-start(bf16[256,1280]{1,0:T(8,128)(2,1)S(1)} %get-tuple-element.44.refs_0_), channel_id=1, source_target_pairs={{0,8},{1,9},{2,10},{3,11},{4,12},{5,13},{6,14},{7,15},{8,0},{9,1},... | collective-permute-start | bytes 1966088 | tf_op jit(solution)/shard_map/ppermute | solution.py:35
  29.5 18.5 %collective-permute-start.6 = (bf16[256,1280]{1,0:T(8,128)(2,1)S(1)}, bf16[256,1280]{1,0:T(8,128)(2,1)S(1)}, u32[]{:S(2)}, u32[]{:S(2)}) collective-permute-start(bf16[256,1280]{1,0:T(8,128)(2,1)S(1)} %get-tuple-element.44.refs_0_), channel_id=1, source_target_pairs={{0,4},{1,5},{2,6},{3,7},{4,8},{5,9},{6,10},{7,11},{8,12},{9,13},{1... | collective-permute-start | bytes 1966088 | tf_op jit(solution)/shard_map/ppermute | solution.py:35
  41.5 9.4 %collective-permute-start.10 = (bf16[256,1280]{1,0:T(8,128)(2,1)}, bf16[256,1280]{1,0:T(8,128)(2,1)}, u32[]{:S(2)}, u32[]{:S(2)}) collective-permute-start(bf16[256,1280]{1,0:T(8,128)(2,1)} %collective-permute-done.9.refs_5_.refs_1_), channel_id=1, source_target_pairs={{0,32},{32,0},{1,33},{33,1},{2,34},{34,2},{3,35},{35,3},{4,36},{36... | collective-permute-start | bytes 1966088 | tf_op jit(solution)/shard_map/ppermute | solution.py:48
  41.5 9.4 %collective-permute-start.11 = (bf16[192,1280]{1,0:T(8,128)(2,1)}, bf16[192,1280]{1,0:T(8,128)(2,1)}, u32[]{:S(2)}, u32[]{:S(2)}) collective-permute-start(bf16[192,1280]{1,0:T(8,128)(2,1)} %get-tuple-element.48), channel_id=1, source_target_pairs={{0,32},{32,0},{1,33},{33,1},{2,34},{34,2},{3,35},{35,3},{4,36},{36... | collective-permute-start | bytes 1474568 | tf_op jit(solution)/shard_map/ppermute | solution.py:48
  54.9 1.4 %collective-permute-start.12 = (f32[24,128]{1,0:T(8,128)S(1)}, f32[24,128]{1,0:T(8,128)S(1)}, u32[]{:S(2)}, u32[]{:S(2)}) collective-permute-start(f32[24,128]{1,0:T(8,128)S(1)} %get-tuple-element.53), channel_id=1, source_target_pairs={{0,32},{32,0},{1,33},{33,1},{2,34},{34,2},{3,35},{35,3},{4,36},{36... | collective-permute-start | bytes 36872 | tf_op jit(solution)/shard_map/ppermute | solution.py:48
  71.0 2.9 %collective-permute-start.13 = (f32[24,128]{1,0:T(8,128)S(1)}, f32[24,128]{1,0:T(8,128)S(1)}, u32[]{:S(2)}, u32[]{:S(2)}) collective-permute-start(f32[24,128]{1,0:T(8,128)S(1)} %get-tuple-element.55), channel_id=1, source_target_pairs={{0,32},{32,0},{1,33},{33,1},{2,34},{34,2},{3,35},{35,3},{4,36},{36... | collective-permute-start | bytes 36872 | tf_op jit(solution)/shard_map/ppermute | solution.py:48
  77.7 3.3 %collective-permute-start.15 = (bf16[256,1280]{1,0:T(8,128)(2,1)S(1)}, bf16[256,1280]{1,0:T(8,128)(2,1)S(1)}, u32[]{:S(2)}, u32[]{:S(2)}) collective-permute-start(bf16[256,1280]{1,0:T(8,128)(2,1)S(1)} %get-tuple-element.61), channel_id=1, source_target_pairs={{0,32},{32,0},{1,33},{33,1},{2,34},{34,2},{3,35},{35,3},{4,36},{36... | collective-permute-start | bytes 1966088 | tf_op jit(solution)/shard_map/ppermute | solution.py:48
  78.1 2.9 %collective-permute-start.14 = (bf16[192,1280]{1,0:T(8,128)(2,1)S(1)}, bf16[192,1280]{1,0:T(8,128)(2,1)S(1)}, u32[]{:S(2)}, u32[]{:S(2)}) collective-permute-start(bf16[192,1280]{1,0:T(8,128)(2,1)S(1)} %get-tuple-element.59), channel_id=1, source_target_pairs={{0,32},{32,0},{1,33},{33,1},{2,34},{34,2},{3,35},{35,3},{4,36},{36... | collective-permute-start | bytes 1474568 | tf_op jit(solution)/shard_map/ppermute | solution.py:48
  84.8 19.1 %collective-permute-start.17 = (bf16[272,1280]{1,0:T(8,128)(2,1)S(1)}, bf16[272,1280]{1,0:T(8,128)(2,1)S(1)}, u32[]{:S(2)}, u32[]{:S(2)}) collective-permute-start(bf16[272,1280]{1,0:T(8,128)(2,1)S(1)} %get-tuple-element.66), channel_id=1, source_target_pairs={{0,8},{1,9},{2,10},{3,11},{4,12},{5,13},{6,14},{7,15},{8,0},{9,1},... | collective-permute-start | bytes 2088968 | tf_op jit(solution)/shard_map/ppermute | solution.py:35
  85.3 18.7 %collective-permute-start.18 = (bf16[272,1280]{1,0:T(8,128)(2,1)S(1)}, bf16[272,1280]{1,0:T(8,128)(2,1)S(1)}, u32[]{:S(2)}, u32[]{:S(2)}) collective-permute-start(bf16[272,1280]{1,0:T(8,128)(2,1)S(1)} %get-tuple-element.67), channel_id=1, source_target_pairs={{0,12},{1,13},{2,14},{3,15},{4,0},{5,1},{6,2},{7,3},{8,4},{9,5},{1... | collective-permute-start | bytes 2088968 | tf_op jit(solution)/shard_map/ppermute | solution.py:35
  88.4 16.5 %collective-permute-start.19 = (bf16[272,1280]{1,0:T(8,128)(2,1)S(1)}, bf16[272,1280]{1,0:T(8,128)(2,1)S(1)}, u32[]{:S(2)}, u32[]{:S(2)}) collective-permute-start(bf16[272,1280]{1,0:T(8,128)(2,1)S(1)} %get-tuple-element.68), channel_id=1, source_target_pairs={{0,4},{1,5},{2,6},{3,7},{4,8},{5,9},{6,10},{7,11},{8,12},{9,13},{1... | collective-permute-start | bytes 2088968 | tf_op jit(solution)/shard_map/ppermute | solution.py:35
  88.4 29.4 %collective-permute-start.16 = (bf16[272,1280]{1,0:T(8,128)(2,1)S(1)}, bf16[272,1280]{1,0:T(8,128)(2,1)S(1)}, u32[]{:S(2)}, u32[]{:S(2)}) collective-permute-start(bf16[272,1280]{1,0:T(8,128)(2,1)S(1)} %get-tuple-element.64.after), channel_id=1, source_target_pairs={{0,128},{64,192},{128,16},{192,80},{16,144},{80,208},{144,0},{208,... | collective-permute-start | bytes 2088968 | tf_op jit(solution)/shard_map/ppermute | solution.py:44
  89.7 14.3 %collective-permute-start.20 = (bf16[80,1280]{1,0:T(8,128)(2,1)S(1)}, bf16[80,1280]{1,0:T(8,128)(2,1)S(1)}, u32[]{:S(2)}, u32[]{:S(2)}) collective-permute-start(bf16[80,1280]{1,0:T(8,128)(2,1)S(1)} %get-tuple-element.69), channel_id=1, source_target_pairs={{0,16},{64,80},{128,144},{192,208},{16,0},{80,64},{144,128},{208,1... | collective-permute-start | bytes 614408 | tf_op jit(solution)/shard_map/ppermute | solution.py:44
  118.4 7.6 %collective-permute-start.24 = (bf16[144,1280]{1,0:T(8,128)(2,1)S(1)}, bf16[144,1280]{1,0:T(8,128)(2,1)S(1)}, u32[]{:S(2)}, u32[]{:S(2)}) collective-permute-start(bf16[144,1280]{1,0:T(8,128)(2,1)S(1)} %get-tuple-element.75), channel_id=1, source_target_pairs={{0,64},{64,128},{128,192},{192,16},{16,80},{80,144},{144,208},{208... | collective-permute-start | bytes 1105928 | tf_op jit(solution)/shard_map/ppermute | solution.py:44
  119.9 7.3 %collective-permute-start.21 = (bf16[80,1280]{1,0:T(8,128)(2,1)S(1)}, bf16[80,1280]{1,0:T(8,128)(2,1)S(1)}, u32[]{:S(2)}, u32[]{:S(2)}) collective-permute-start(bf16[80,1280]{1,0:T(8,128)(2,1)S(1)} %get-tuple-element.71), channel_id=1, source_target_pairs={{0,2},{1,3},{2,0},{3,1},{4,6},{5,7},{6,4},{7,5},{8,10},{9,11},{10,... | collective-permute-start | bytes 614408 | tf_op jit(solution)/shard_map/ppermute | solution.py:35
  121.5 6.5 %collective-permute-start.22 = (bf16[80,1280]{1,0:T(8,128)(2,1)S(1)}, bf16[80,1280]{1,0:T(8,128)(2,1)S(1)}, u32[]{:S(2)}, u32[]{:S(2)}) collective-permute-start(bf16[80,1280]{1,0:T(8,128)(2,1)S(1)} %get-tuple-element.72), channel_id=1, source_target_pairs={{0,3},{1,0},{2,1},{3,2},{4,7},{5,4},{6,5},{7,6},{8,11},{9,8},{10,9... | collective-permute-start | bytes 614408 | tf_op jit(solution)/shard_map/ppermute | solution.py:35
  122.7 7.0 %collective-permute-start.23 = (bf16[80,1280]{1,0:T(8,128)(2,1)S(1)}, bf16[80,1280]{1,0:T(8,128)(2,1)S(1)}, u32[]{:S(2)}, u32[]{:S(2)}) collective-permute-start(bf16[80,1280]{1,0:T(8,128)(2,1)S(1)} %get-tuple-element.73), channel_id=1, source_target_pairs={{0,1},{1,2},{2,3},{3,0},{4,5},{5,6},{6,7},{7,4},{8,9},{9,10},{10,1... | collective-permute-start | bytes 614408 | tf_op jit(solution)/shard_map/ppermute | solution.py:35
  126.1 3.5 %collective-permute-start.25 = (bf16[80,1280]{1,0:T(8,128)(2,1)S(1)}, bf16[80,1280]{1,0:T(8,128)(2,1)S(1)}, u32[]{:S(2)}, u32[]{:S(2)}) collective-permute-start(bf16[80,1280]{1,0:T(8,128)(2,1)S(1)} %get-tuple-element.77), channel_id=1, source_target_pairs={{0,32},{32,0},{1,33},{33,1},{2,34},{34,2},{3,35},{35,3},{4,36},{36... | collective-permute-start | bytes 614408 | tf_op jit(solution)/shard_map/ppermute | solution.py:48

commit v7 on v6

--- a/solution.py
+++ b/solution.py
@@ -95,6 +95,10 @@
     return out
 
 
+PART = jax.ShapeDtypeStruct((CHUNK, EMBED), BF16)
+ALL = jax.ShapeDtypeStruct((BLOCK, EMBED), BF16)
+
+
 def pack_body(plan, n, *refs):
     for parts, out in zip(plan, refs[n:]):
         row = 0
@@ -114,17 +118,6 @@
     )(*arrays)
 
 
-def block_logits(multiplier, images, texts, logits):
-    for a in range(4):
-        for j, text in enumerate(texts):
-            logits[a * CHUNK : (a + 1) * CHUNK, j * CHUNK : (j + 1) * CHUNK] = (
-                multiplier
-                * lax.dot_general(
-                    images[a][...], text[...], (((1,), (1,)), ((), ())), preferred_element_type=F32
-                )
-            )
-
-
 def fold(v):
     return v.reshape(v.shape[0] // 8, 8, 128)
 
@@ -140,52 +133,41 @@
     return top + LOG2E * jnp.log(jnp.sum(total, axis=0, keepdims=True))
 
 
-def first_body(scale, *refs):
-    images, texts = refs[:4], refs[4:6]
-    logits, col_out = refs[6:]
-    block_logits(scale[0] * LOG2E, images, texts, logits)
-    for t in range(4):
-        top = jnp.max(fold(logits[:128, t * 128 : (t + 1) * 128]), axis=0)
-        for i in range(1, 8):
-            tile = logits[i * 128 : (i + 1) * 128, t * 128 : (t + 1) * 128]
-            top = jnp.maximum(top, jnp.max(fold(tile), axis=0))
-        col_out[t : t + 1, :] = column_part(logits, t, top)
-
-
-def first_call(scale, images, texts):
-    return pl.pallas_call(
-        first_body,
-        out_shape=(
-            jax.ShapeDtypeStruct((BLOCK, BLOCK // 2), F32),
-            jax.ShapeDtypeStruct((8, 128), F32),
-        ),
-        in_specs=[SMEM] + [VMEM] * 6,
-        out_specs=(VMEM,) * 2,
-        compiler_params=PARAMS,
-    )(scale, *images, *texts)
-
-
-def second_body(place, scale, logits_0, col_parts, *refs):
-    images = refs[:4]
-    logits_1, row_out, col_out, message, match_out, text_3 = refs[7:13]
-    row_wide = refs[13]
-    text_3[: 3 * ROWS, :] = refs[5][...]
-    text_3[3 * ROWS :, :] = refs[6][...]
+def logits_body(place, scale, *refs):
+    images, texts = refs[:4], refs[4:7]
+    logits, row_out, col_out, message, match_out, all_images, all_texts = refs[9:16]
+    row_wide, sems = refs[16:]
+    copies = []
+    for i, (out, at) in enumerate(
+        [(all_texts, 3 * CHUNK), (all_texts, BLOCK - ROWS)]
+        + [(all_images, a * CHUNK) for a in range(4)]
+        + [(all_texts, j * CHUNK) for j in range(3)]
+    ):
+        source = (refs[7], refs[8], *images, *texts)[i]
+        into = out.at[at : at + source.shape[0], :]
+        copies.append(pltpu.make_async_copy(source, into, sems.at[i]))
+        copies[-1].start()
     where = [place[i] for i in range(5)]
-    block_logits(scale[0] * LOG2E, images, (refs[4], text_3), logits_1)
-    halves = (logits_0, logits_1)
+    multiplier = scale[0] * LOG2E
+    for j in range(4):
+        if j == 3:
+            copies[0].wait()
+            copies[1].wait()
+        for a in range(4):
+            text = texts[j][...] if j < 3 else all_texts[3 * CHUNK :, :]
+            logits[a * CHUNK : (a + 1) * CHUNK, j * CHUNK : (j + 1) * CHUNK] = multiplier * lax.dot_general(
+                images[a][...], text, (((1,), (1,)), ((), ())), preferred_element_type=F32
+            )
     cols = col_ids(where)
     step = 32
     matched = jnp.zeros((8, 128), F32)
-    col_top = [jnp.full((8, 128), -jnp.inf, F32) for _ in range(4)]
+    col_top = [jnp.full((8, 128), -jnp.inf, F32) for _ in range(8)]
     for a in range(4):
         ids = row_ids(where, a)
         for b in range(4):
             for half in range(ROWS // step):
                 at = a * CHUNK + b * ROWS + half * step
-                tiles = [
-                    halves[t // 4][at : at + step, (t % 4) * 128 : (t % 4 + 1) * 128] for t in range(8)
-                ]
+                tiles = [logits[at : at + step, t * 128 : (t + 1) * 128] for t in range(8)]
                 top = tiles[0]
                 for t in range(1, 8):
                     top = jnp.maximum(top, tiles[t])
@@ -194,8 +176,7 @@
                 total = jnp.zeros((step, 128), F32)
                 for t in range(8):
                     total += jnp.exp2(tiles[t] - top)
-                    if t > 3:
-                        col_top[t - 4] = jnp.maximum(col_top[t - 4], jnp.max(fold(tiles[t]), axis=0))
+                    col_top[t] = jnp.maximum(col_top[t], jnp.max(fold(tiles[t]), axis=0))
                     hit = jnp.where(mine == cols[t][0:1], tiles[t], 0.0)
                     matched += jnp.sum(fold(hit), axis=0)
                 part = top + LOG2E * jnp.log(jnp.sum(total, axis=1, keepdims=True))
@@ -204,7 +185,7 @@
     match_out[...] = matched
     message[16:24, :] = matched
     for t in range(8):
-        part = col_parts[t : t + 1, :] if t < 4 else column_part(logits_1, t - 4, col_top[t - 4])
+        part = column_part(logits, t, col_top[t])
         j, i = t // 2, (t % 2) * 2
         col_out[pl.ds(col_place(where, j, i)[0], 1), :] = part
         col_out[pl.ds(col_place(where, j, i + 1)[0], 1), :] = pltpu.roll(part, 64, 1)
@@ -212,24 +193,27 @@
         row_out[pl.ds(row_place(where, j, i)[0], 1), :] = line
         row_out[pl.ds(row_place(where, j, i + 1)[0], 1), :] = pltpu.roll(line, 64, 1)
     message[:16, :] = jnp.where(where[1] == 0, col_out[...], row_out[...])
-
-
-def second_call(place, scale, logits_0, col_parts, images, texts):
-    return pl.pallas_call(
-        second_body,
+    for copy in copies[2:]:
+        copy.wait()
+
+
+def logits_call(place, scale, images, texts):
+    return pl.pallas_call(
+        logits_body,
         out_shape=(
-            jax.ShapeDtypeStruct((BLOCK, BLOCK // 2), F32),
+            jax.ShapeDtypeStruct((BLOCK, BLOCK), F32),
             jax.ShapeDtypeStruct((16, 128), F32),
             jax.ShapeDtypeStruct((16, 128), F32),
             jax.ShapeDtypeStruct((24, 128), F32),
             jax.ShapeDtypeStruct((8, 128), F32),
-            PART,
+            ALL,
+            ALL,
         ),
         in_specs=[SMEM, SMEM] + [VMEM] * 9,
-        out_specs=(VMEM,) * 6,
-        scratch_shapes=[pltpu.VMEM((BLOCK, 128), F32)],
-        compiler_params=PARAMS,
-    )(place, scale, logits_0, col_parts, *images, *texts)
+        out_specs=(VMEM,) * 7,
+        scratch_shapes=[pltpu.VMEM((BLOCK, 128), F32), pltpu.SemaphoreType.DMA((9,))],
+        compiler_params=PARAMS,
+    )(place, scale, *images, *texts)
 
 
 def spread_body(place, row, col, matched, got, out):
@@ -306,11 +290,9 @@
     return jnp.sum(digits * units, axis=0, keepdims=True)
 
 
-def weights_body(place, scale, logits_0, logits_1, mine, other, *refs):
-    images = refs[:4]
-    weights = refs[4]
-    outs = refs[5:8]
-    row_wide, row_lse, col_lse = refs[8:11]
+def weights_body(place, scale, logits, mine, other, images, *refs):
+    weights, outs = refs[0], refs[1:4]
+    row_wide, row_lse, col_lse = refs[4:]
     first = place[1] == 0
     shares = jnp.where(first, mine[16:17, :], other[16:17, :]), jnp.where(first, other[16:17, :], mine[16:17, :])
     for i, share in enumerate(shares):
@@ -339,44 +321,34 @@
             at = a * CHUNK + b * ROWS
             wide = row_wide[at : at + ROWS, :]
             for t in range(8):
-                tile = (logits_0, logits_1)[t // 4][at : at + ROWS, (t % 4) * 128 : (t % 4 + 1) * 128]
+                tile = logits[at : at + ROWS, t * 128 : (t + 1) * 128]
                 both = jnp.exp2(tile - wide) + jnp.exp2(tile - col_line[t])
                 both = both - jnp.where(ids[b] == cols[t][0:1], 1.0, 0.0)
                 weights[at : at + ROWS, t * 128 : (t + 1) * 128] = both.astype(BF16)
-    text_terms(multiplier, weights, images, ((2, 0, outs[0]), (3, 0, outs[1])))
+    text_terms(multiplier, weights, images, ((2 * CHUNK, outs[0]), (3 * CHUNK, outs[1])))
 
 
 def text_terms(multiplier, weights, images, outs):
-    for j, skip, out in outs:
-        at = j * CHUNK + skip
+    for skip, out in outs:
         for e in range(5):
-            acc = None
-            for a in range(4):
-                term = lax.dot_general(
-                    weights[a * CHUNK : (a + 1) * CHUNK, at : at + out.shape[0]],
-                    images[a][:, e * 256 : (e + 1) * 256],
-                    (((0,), (0,)), ((), ())),
-                    preferred_element_type=F32,
-                )
-                acc = term if acc is None else acc + term
-            out[:, e * 256 : (e + 1) * 256] = (multiplier * acc).astype(BF16)
+            term = lax.dot_general(
+                weights[:, skip : skip + out.shape[0]],
+                images[:, e * 256 : (e + 1) * 256],
+                (((0,), (0,)), ((), ())),
+                preferred_element_type=F32,
+            )
+            out[:, e * 256 : (e + 1) * 256] = (multiplier * term).astype(BF16)
 
 
 def image_terms(multiplier, weights, texts, outs):
     for a, out in outs.items():
         for e in range(5):
-            acc = None
-            for j in range(4):
-                term = jnp.dot(
-                    weights[a * CHUNK : (a + 1) * CHUNK, j * CHUNK : (j + 1) * CHUNK],
-                    texts[j][:, e * 256 : (e + 1) * 256],
-                    preferred_element_type=F32,
-                )
-                acc = term if acc is None else acc + term
-            out[:CHUNK, e * 256 : (e + 1) * 256] = (multiplier * acc).astype(BF16)
-
-
-PART = jax.ShapeDtypeStruct((CHUNK, EMBED), BF16)
+            term = jnp.dot(
+                weights[a * CHUNK : (a + 1) * CHUNK, :],
+                texts[:, e * 256 : (e + 1) * 256],
+                preferred_element_type=F32,
+            )
+            out[:CHUNK, e * 256 : (e + 1) * 256] = (multiplier * term).astype(BF16)
 
 
 def weights_call(place, scale, logits, mine, other, images):
@@ -388,7 +360,7 @@
             jax.ShapeDtypeStruct((3 * ROWS, EMBED), BF16),
             jax.ShapeDtypeStruct((2 * TAIL, EMBED), BF16),
         ),
-        in_specs=[SMEM, SMEM] + [VMEM] * 8,
+        in_specs=[SMEM, SMEM] + [VMEM] * 4,
         out_specs=(VMEM,) * 4,
         scratch_shapes=[
             pltpu.VMEM((BLOCK, 128), F32),
@@ -396,26 +368,26 @@
             pltpu.VMEM((16, 128), F32),
         ],
         compiler_params=PARAMS,
-    )(place, scale, *logits, mine, other, *images)
-
-
-def text_body(scale, weights, *refs):
-    text_terms(scale[0], weights, refs[:4], ((1, 0, refs[4]), (3, 3 * ROWS, refs[5])))
+    )(place, scale, logits, mine, other, images)
+
+
+def text_body(scale, weights, images, near, far):
+    text_terms(scale[0], weights, images, ((CHUNK, near), (BLOCK - ROWS, far)))
 
 
 def text_call(scale, weights, images):
     return pl.pallas_call(
         text_body,
         out_shape=(PART, jax.ShapeDtypeStruct((ROWS, EMBED), BF16)),
-        in_specs=[SMEM] + [VMEM] * 5,
+        in_specs=[SMEM] + [VMEM] * 2,
         out_specs=(VMEM,) * 2,
         compiler_params=PARAMS,
-    )(scale, weights, *images)
-
-
-def image_body(scale, after, digits, weights, *refs):
-    image_terms(scale[0], weights, refs[:4], dict(zip((2, 1, 3), refs[4:])))
-    for out in refs[4:]:
+    )(scale, weights, images)
+
+
+def image_body(scale, after, digits, weights, texts, *outs):
+    image_terms(scale[0], weights, texts, dict(zip((2, 1, 3), outs)))
+    for out in outs:
         out[CHUNK:, :] = digits[TAIL:, :]
 
 
@@ -423,26 +395,25 @@
     return pl.pallas_call(
         image_body,
         out_shape=(jax.ShapeDtypeStruct((CHUNK + TAIL, EMBED), BF16),) * 3,
-        in_specs=[SMEM] + [VMEM] * 7,
+        in_specs=[SMEM] + [VMEM] * 4,
         out_specs=(VMEM,) * 3,
         compiler_params=PARAMS,
-    )(scale, after, digits, weights, *texts)
-
-
-def rest_body(scale, weights, *refs):
-    images, texts, outs = refs[:4], refs[4:8], refs[8:]
-    text_terms(scale[0], weights, images, ((0, 0, outs[0]),))
-    image_terms(scale[0], weights, texts, {0: outs[1]})
+    )(scale, after, digits, weights, texts)
+
+
+def rest_body(scale, weights, images, texts, text_out, image_out):
+    text_terms(scale[0], weights, images, ((0, text_out),))
+    image_terms(scale[0], weights, texts, {0: image_out})
 
 
 def rest_call(scale, weights, images, texts):
     return pl.pallas_call(
         rest_body,
         out_shape=(PART, PART),
-        in_specs=[SMEM] + [VMEM] * 9,
+        in_specs=[SMEM] + [VMEM] * 3,
         out_specs=(VMEM,) * 2,
         compiler_params=PARAMS,
-    )(scale, weights, *images, *texts)
+    )(scale, weights, images, texts)
 
 
 def add_rows(refs, rows, terms, out, to):
@@ -475,12 +446,12 @@
 
 
 def last_body(*refs):
-    digits, image_out, text_out, loss_out = refs[7:]
+    digits, image_out, text_out, loss_out = refs[6:]
     add_rows(refs, ROWS, [(i, 0) for i in range(4)], image_out, 0)
-    add_rows(refs, ROWS, [(i, 0) for i in range(4, 7)], text_out, 0)
+    add_rows(refs, ROWS, [(4, 0), (5, 0)], text_out, 0)
     total = -digits[:TAIL, :128].astype(F32)
-    for r in refs[:7]:
-        total += r[ROWS:, :128].astype(F32)
+    for r in refs[:6]:
+        total += r[ROWS : ROWS + TAIL, :128].astype(F32)
     loss_out[...] = value_of(total)[:, 0:1] * (LN2 / (2.0 * ROWS * 256))
 
 
@@ -489,7 +460,7 @@
     return pl.pallas_call(
         last_body,
         out_shape=(grad, grad, jax.ShapeDtypeStruct((1, 1), F32)),
-        in_specs=[VMEM] * 8,
+        in_specs=[VMEM] * 7,
         out_specs=(VMEM,) * 3,
         compiler_params=PARAMS,
     )(*shards, *texts, digits)
@@ -508,18 +479,15 @@
         ((5, 128), (6, 64)),
     )
     text_1 = z_shift(text_0, -2)
-    images = [own] + [plane_shift(own, k, False) for k in (1, 2, 3)]
-    text_2 = core_swap(text_1)
-    logits_0, col_parts = first_call(logit_scale, images, [text_0, text_1])
-    logits_1, row_part, col_part, message, matched, text_3 = second_call(
-        place, logit_scale, logits_0, col_parts, images, [text_2, core_swap(side), next_4]
-    )
-    texts = [text_0, text_1, text_2, text_3]
+    near = [own] + [plane_shift(own, k, False) for k in (1, 2, 3)]
+    logits, row_part, col_part, message, matched, images, texts = logits_call(
+        place, logit_scale, near, [text_0, text_1, core_swap(text_1), core_swap(side), next_4]
+    )
 
     spread = spread_call(place, row_part, col_part, matched, core_swap(message))
     mine, message = join_call(place, exchange(spread, plane_or_ring()))
     weights, text_2, text_3, digits = weights_call(
-        place, logit_scale, (logits_0, logits_1), mine, core_swap(message), images
+        place, logit_scale, logits, mine, core_swap(message), images
     )
 
     other_1, other_3 = core_swap(text_2), core_swap(text_3)
@@ -535,23 +503,30 @@
     back = [plane_shift(v, -k, False) for v, k in zip(image_parts, (2, 1, 3))]
     text_0, image_0 = rest_call(logit_scale, weights, images, texts)
 
-    rows_tail = (TAIL, ((2, 256), (7, 0)))
-    cols_tail = (TAIL, ((4, 256), (5, 256), (6, 256), (7, 16)))
-    next_1, mine, *pieces = sums(
-        [text_0, other_3, pairs, image_0] + back + [digits, next_4],
-        ((128, ((0, 128), (1, 0), (2, 128))), rows_tail),
-        ((128, ((0, 0), (2, 0))), rows_tail),
-        *[((64, [(i, 64 * k) for i in range(3, 7)]), cols_tail) for k in range(4)],
+    next_1, mine = sums(
+        [text_0, other_3, pairs, next_4, digits],
+        ((128, ((0, 128), (1, 0), (2, 128))), (TAIL, ((2, 256), (4, 0)))),
+        (
+            (64, ((0, 0), (2, 0), (3, 0))),
+            (64, ((0, 64), (2, 64))),
+            (TAIL, ((2, 256), (3, 64), (4, 0))),
+            (TAIL, ((2, 256), (4, 0))),
+        ),
     )
     next_1 = z_shift(next_1, 1)
-    shards = [pieces[0]] + [plane_shift(pieces[k], -k, True) for k in (2, 1, 3)]
-    rows_tail = (TAIL, ((0, 128), (1, 128)))
     mine, other = sums(
         [mine, next_1],
-        ((64, ((0, 0), (1, 0))), rows_tail),
-        ((64, ((0, 64), (1, 64))), rows_tail),
-    )
-    image_grad, text_grad, mean_loss = last_call(shards, [mine, core_swap(other), next_4], digits)
+        ((64, ((0, 0), (1, 0))), (TAIL, ((0, 128), (1, 128)))),
+        ((64, ((0, 64), (1, 64))), (TAIL, ((0, 144), (1, 128)))),
+    )
+
+    cols_tail = (TAIL, ((1, 256), (2, 256), (3, 256), (4, 16)))
+    pieces = sums(
+        [image_0] + back + [digits],
+        *[((64, [(i, 64 * k) for i in range(4)]), cols_tail) for k in range(4)],
+    )
+    shards = [pieces[0]] + [plane_shift(pieces[k], -k, True) for k in (2, 1, 3)]
+    image_grad, text_grad, mean_loss = last_call(shards, [mine, core_swap(other)], digits)
     return mean_loss.reshape(1), image_grad, text_grad
 
 

time: 131 us -> 125 us (0.954)
  waiting for transfers between devices: 55.9 us -> 52 us
  Pallas kernels: 23.8 us -> 21.6 us
    ppermute x6, waiting for transfers between devices: 42.7 us -> 38 us  [z_shift(): return lax.ppermute(v, ('zl', 'core', 'zh'), pairs)]
    ppermute x8, waiting for transfers between devices: 3.6 us -> 5.69 us  [core_swap(): return lax.ppermute(v, 'core', [(0, 1), (1, 0)])]
    pallas_call x2 -> x1, Pallas kernels: 6.87 us -> 8.36 us  [logits_call(): pl.pallas_call(logits_body, out_shape=(jax.ShapeDtypeStruct((BLOCK, BLOCK...]
    pallas_call x1, Pallas kernels: 3.62 us -> 2.2 us  [image_call(): pl.pallas_call(image_body, out_shape=(jax.ShapeDtypeStruct((CHUNK + TAIL,...]
    pallas_call x1, Pallas kernels: 2.92 us -> 1.57 us  [rest_call(): pl.pallas_call(rest_body, out_shape=(PART, PART), in_specs=[SMEM] + [VMEM...]
    ppermute x12, waiting for transfers between devices: 9.62 us -> 8.29 us  [plane_shift(): return lax.ppermute(v, ('core', 'zh', 'y', 'x'), pairs)]
  transfers between devices with their start and end apart: 26 -> 26, of which waited for: 14 -> 14; matrix products, arithmetic and copies ran while one was open for 0% -> 0% of each run, Pallas kernels for 7% -> 5%
where the time goes in v7:
time: 125 us
  waiting for transfers between devices  52 us (42%)
  starting transfers between devices  34.9 us (28%)
  Pallas kernels  21.6 us (17%)
  blocking collectives  13.3 us (11%)
  local copies, waits for them, and re-layouts  1.92 us (2%)
  between operations  1.41 us (1%)
    ppermute x6, waiting for transfers between devices, z_shift(): return lax.ppermute(v, ('zl', 'core', 'zh'), pairs)  38 us
    ppermute x12, starting transfers between devices, plane_shift(): return lax.ppermute(v, ('core', 'zh', 'y', 'x'), pairs)  17 us
    ppermute x6, starting transfers between devices, z_shift(): return lax.ppermute(v, ('zl', 'core', 'zh'), pairs)  14.3 us
    all_to_all x1, blocking collectives, exchange(): return lax.all_to_all(v, AXES, 0, 0, axis_index_groups=groups)  13.3 us
    pallas_call x1, Pallas kernels, logits_call(): pl.pallas_call(logits_body, out_shape=(jax.ShapeDtypeStruct((BLOCK, BLOCK...  8.36 us
    ppermute x12, waiting for transfers between devices, plane_shift(): return lax.ppermute(v, ('core', 'zh', 'y', 'x'), pairs)  8.29 us
    ppermute x8, waiting for transfers between devices, core_swap(): return lax.ppermute(v, 'core', [(0, 1), (1, 0)])  5.69 us
    pallas_call x1, Pallas kernels, weights_call(): pl.pallas_call(weights_body, out_shape=(jax.ShapeDtypeStruct((BLOCK, BLOC...  3.58 us
  transfers between devices with their start and end apart: 26, of which 14 were waited for; matrix products, arithmetic and copies ran while one was open for 0% of the time, Pallas kernels for 5%

profile of v7, /device:TPU:32, one launch (start us, length us, event | category | flops | bytes accessed | tf_op | source)
XLA Modules:
  0.0 125.1 jit_solution(16921169383312613368)
XLA Ops:
  0.6 0.1 collective-permute-start
  0.7 1.6 %collective-permute-done.refs_1_ = bf16[64,1280]{1,0:T(8,128)(2,1)S(1)} collective-permute-done((bf16[64,1280]{1,0:T(8,128)(2,1)}, bf16[64,1280]{1,0:T(8,128)(2,1)S(1)}, u32[]{:S(2)}, u32[]{:S(2)}) %collective-permute-start) | collective-permute-done | bytes 163872 | tf_op jit(solution)/shard_map/ppermute | solution.py:48
  2.3 0.9 copy-done
  3.2 0.9 copy-done.1
  4.2 1.9 %collective-permute-start.4 = (bf16[128,1280]{1,0:T(8,128)(2,1)S(1)}, bf16[128,1280]{1,0:T(8,128)(2,1)S(1)}, u32[]{:S(2)}, u32[]{:S(2)}) collective-permute-start(bf16[128,1280]{1,0:T(8,128)(2,1)S(1)} %get-tuple-element.42.refs_4_), channel_id=1, source_target_pairs={{0,208},{64,0},{128,64},{192,128},{16,192},{80,16},{144,80},{208,1... | collective-permute-start | bytes 983048 | tf_op jit(solution)/shard_map/ppermute | solution.py:44
  6.1 5.5 %collective-permute-start.5 = (bf16[64,1280]{1,0:T(8,128)(2,1)S(1)}, bf16[64,1280]{1,0:T(8,128)(2,1)S(1)}, u32[]{:S(2)}, u32[]{:S(2)}) collective-permute-start(bf16[64,1280]{1,0:T(8,128)(2,1)S(1)} %copy-done.1), channel_id=1, source_target_pairs={{0,16},{64,80},{128,144},{192,208},{16,0},{80,64},{144,128},{208,1... | collective-permute-start | bytes 491528 | tf_op jit(solution)/shard_map/ppermute | solution.py:44
  11.6 2.8 %collective-permute-start.3 = (bf16[64,1280]{1,0:T(8,128)(2,1)S(1)}, bf16[64,1280]{1,0:T(8,128)(2,1)S(1)}, u32[]{:S(2)}, u32[]{:S(2)}) collective-permute-start(bf16[64,1280]{1,0:T(8,128)(2,1)S(1)} %get-tuple-element.41.refs_0_), channel_id=1, source_target_pairs={{0,3},{1,0},{2,1},{3,2},{4,7},{5,4},{6,5},{7,6},{8,11},{9,8},{10,9... | collective-permute-start | bytes 491528 | tf_op jit(solution)/shard_map/ppermute | solution.py:35
  14.3 0.8 collective-permute-start.2
  15.1 0.9 collective-permute-start.1
  16.0 7.1 %collective-permute-done.5.refs_6_.refs_8_ = bf16[64,1280]{1,0:T(8,128)(2,1)S(1)} collective-permute-done((bf16[64,1280]{1,0:T(8,128)(2,1)S(1)}, bf16[64,1280]{1,0:T(8,128)(2,1)S(1)}, u32[]{:S(2)}, u32[]{:S(2)}) %collective-permute-start.5) | collective-permute-done | bytes 163872 | tf_op jit(solution)/shard_map/ppermute | solution.py:44
  23.1 0.0 collective-permute-done.3.refs_3_
  23.1 0.0 collective-permute-done.2.refs_2_
  23.1 0.9 shard_map.59
  24.0 1.9 %collective-permute-start.9 = (bf16[256,1280]{1,0:T(8,128)(2,1)S(1)}, bf16[256,1280]{1,0:T(8,128)(2,1)S(1)}, u32[]{:S(2)}, u32[]{:S(2)}) collective-permute-start(bf16[256,1280]{1,0:T(8,128)(2,1)S(1)} %get-tuple-element.44.refs_4_), channel_id=1, source_target_pairs={{0,144},{64,208},{128,0},{192,64},{16,128},{80,192},{144,16},{208,... | collective-permute-start | bytes 1966088 | tf_op jit(solution)/shard_map/ppermute | solution.py:44
  25.9 3.0 %collective-permute-start.8 = (bf16[256,1280]{1,0:T(8,128)(2,1)S(1)}, bf16[256,1280]{1,0:T(8,128)(2,1)S(1)}, u32[]{:S(2)}, u32[]{:S(2)}) collective-permute-start(bf16[256,1280]{1,0:T(8,128)(2,1)S(1)} %get-tuple-element.43.refs_0_), channel_id=1, source_target_pairs={{0,12},{1,13},{2,14},{3,15},{4,0},{5,1},{6,2},{7,3},{8,4},{9,5},{1... | collective-permute-start | bytes 1966088 | tf_op jit(solution)/shard_map/ppermute | solution.py:35
  28.9 0.6 collective-permute-start.7
  29.5 1.0 collective-permute-start.6
  30.5 10.9 %collective-permute-done.9.refs_5_ = bf16[256,1280]{1,0:T(8,128)(2,1)S(1)} collective-permute-done((bf16[256,1280]{1,0:T(8,128)(2,1)S(1)}, bf16[256,1280]{1,0:T(8,128)(2,1)S(1)}, u32[]{:S(2)}, u32[]{:S(2)}) %collective-permute-start.9) | collective-permute-done | bytes 655392 | tf_op jit(solution)/shard_map/ppermute | solution.py:44
  41.4 0.5 collective-permute-start.11
  42.6 0.1 stack.23.place
  42.7 1.7 %collective-permute-done.11.refs_7_ = bf16[192,1280]{1,0:T(8,128)(2,1)} collective-permute-done((bf16[192,1280]{1,0:T(8,128)(2,1)}, bf16[192,1280]{1,0:T(8,128)(2,1)}, u32[]{:S(2)}, u32[]{:S(2)}) %collective-permute-start.11) | collective-permute-done | bytes 491552 | tf_op jit(solution)/shard_map/ppermute | solution.py:48
  44.4 0.0 collective-permute-done.8.refs_3_
  44.4 0.0 collective-permute-done.7.refs_2_
  44.4 3.7 %collective-permute-done.6.refs_1_ = bf16[256,1280]{1,0:T(8,128)(2,1)} collective-permute-done((bf16[256,1280]{1,0:T(8,128)(2,1)S(1)}, bf16[256,1280]{1,0:T(8,128)(2,1)}, u32[]{:S(2)}, u32[]{:S(2)}) %collective-permute-start.6) | collective-permute-done | bytes 655392 | tf_op jit(solution)/shard_map/ppermute | solution.py:35
  48.1 8.4 %shard_map.60 = (f32[1024,1024]{1,0:T(8,128)S(1)}, f32[16,128]{1,0:T(8,128)S(1)}, f32[16,128]{1,0:T(8,128)S(1)}, f32[24,128]{1,0:T(8,128)S(1)}, f32[8,128]{1,0:T...) custom-call(s32[5]{0:T(128)S(1)} %stack.23.place, f32[1]{0:T(128)S(6)} %copy.6.scale, ...), custom_call_target="tpu_custom_call" | custom-call | tf_op jit(solution)/shard_map/pallas_call | solution.py:201
  56.5 0.1 collective-permute-start.12
  56.6 1.2 collective-permute-done.12.got
  57.8 0.6 shard_map.61
  58.3 13.3 %all_to_all.5.got = f32[16,40,128]{2,1,0:T(8,128)S(1)} all-to-all(f32[16,40,128]{2,1,0:T(8,128)S(1)} %shard_map.61), channel_id=1, replica_groups={{0,1,2,3,4,5,6,7,8,9,10,11,12,13,14,15},{64,65,66,67,68,69,70,71,72,73,..., dimensions={0} | all-to-all | bytes 655360 | tf_op jit(solution)/shard_map/all_to_all | solution.py:63
  71.7 0.7 shard_map.62
  72.4 2.1 %collective-permute-start.13 = (f32[24,128]{1,0:T(8,128)S(1)}, f32[24,128]{1,0:T(8,128)S(1)}, u32[]{:S(2)}, u32[]{:S(2)}) collective-permute-start(f32[24,128]{1,0:T(8,128)S(1)} %get-tuple-element.52), channel_id=1, source_target_pairs={{0,32},{32,0},{1,33},{33,1},{2,34},{34,2},{3,35},{35,3},{4,36},{36... | collective-permute-start | bytes 36872 | tf_op jit(solution)/shard_map/ppermute | solution.py:48
  74.6 0.8 collective-permute-done.13.other
  75.4 3.6 %shard_map.63 = (bf16[1024,1024]{1,0:T(8,128)(2,1)S(1)}, bf16[256,1280]{1,0:T(8,128)(2,1)S(1)}, bf16[192,1280]{1,0:T(8,128)(2,1)S(1)}, bf16[32,1280]{1,0:T(8,128)(2,1)S(1)}) custom-call(s32[5]{0:T(128)S(1)} %stack.23.place, f32[1]{0:T(128)S(6)} %copy.6.scale, f32[1024,1024]{1,0:T(8,128)S(1)} %get-tuple-element.46.logits, ...), custom_call_target="tpu_custom_call" | custom-call | tf_op jit(solution)/shard_map/pallas_call | solution.py:355
  79.0 0.4 collective-permute-start.14
  79.4 0.2 collective-permute-start.15
  79.6 1.9 %shard_map.65 = (bf16[256,1280]{1,0:T(8,128)(2,1)S(1)}, bf16[64,1280]{1,0:T(8,128)(2,1)S(1)}) custom-call(f32[1]{0:T(128)S(6)} %copy.6.scale, bf16[1024,1024]{1,0:T(8,128)(2,1)S(1)} %get-tuple-element.54.weights, bf16[1024,1280]{1,0:T(8,128)(2,1)S(1)} %get-tuple-element.53.images), custom_call_target="tpu_custom_call" | custom-call | tf_op jit(solution)/shard_map/pallas_call | solution.py:379
  81.5 0.4 collective-permute-done.15.refs_3_.refs_1_
  81.9 0.0 collective-permute-done.14.refs_1_
  81.9 0.2 shard_map.66
  82.1 1.5 %collective-permute-start.22 = (bf16[272,1280]{1,0:T(8,128)(2,1)S(1)}, bf16[272,1280]{1,0:T(8,128)(2,1)S(1)}, u32[]{:S(2)}, u32[]{:S(2)}) collective-permute-start(bf16[272,1280]{1,0:T(8,128)(2,1)S(1)} %get-tuple-element.62.after), channel_id=1, source_target_pairs={{0,128},{64,192},{128,16},{192,80},{16,144},{80,208},{144,0},{208,... | collective-permute-start | bytes 2088968 | tf_op jit(solution)/shard_map/ppermute | solution.py:44
  83.6 2.2 %shard_map.67 = (bf16[272,1280]{1,0:T(8,128)(2,1)S(1)}, bf16[272,1280]{1,0:T(8,128)(2,1)S(1)}, bf16[272,1280]{1,0:T(8,128)(2,1)S(1)}) custom-call(f32[1]{0:T(128)S(6)} %copy.6.scale, bf16[272,1280]{1,0:T(8,128)(2,1)S(1)} %get-tuple-element.62.after, bf16[32,1280]{1,0:T(8,128)(2,1)S(1)} %get-tuple-element.61.refs_4_.digits.refs_6_, ...), custom_call_target="tpu_custom_call" | custom-call | tf_op jit(solution)/shard_map/pallas_call | solution.py:395
  85.8 0.7 collective-permute-start.16
  86.4 2.9 %collective-permute-start.17 = (bf16[272,1280]{1,0:T(8,128)(2,1)S(1)}, bf16[272,1280]{1,0:T(8,128)(2,1)S(1)}, u32[]{:S(2)}, u32[]{:S(2)}) collective-permute-start(bf16[272,1280]{1,0:T(8,128)(2,1)S(1)} %get-tuple-element.64), channel_id=1, source_target_pairs={{0,12},{1,13},{2,14},{3,15},{4,0},{5,1},{6,2},{7,3},{8,4},{9,5},{1... | collective-permute-start | bytes 2088968 | tf_op jit(solution)/shard_map/ppermute | solution.py:35
  89.3 0.0 collective-permute-start.18
  89.3 2.2 %collective-permute-start.23 = (bf16[80,1280]{1,0:T(8,128)(2,1)S(1)}, bf16[80,1280]{1,0:T(8,128)(2,1)S(1)}, u32[]{:S(2)}, u32[]{:S(2)}) collective-permute-start(bf16[80,1280]{1,0:T(8,128)(2,1)S(1)} %get-tuple-element.71), channel_id=1, source_target_pairs={{0,16},{64,80},{128,144},{192,208},{16,0},{80,64},{144,128},{208,1... | collective-permute-start | bytes 614408 | tf_op jit(solution)/shard_map/ppermute | solution.py:44
  91.5 1.6 %shard_map.64 = (bf16[256,1280]{1,0:T(8,128)(2,1)S(1)}, bf16[256,1280]{1,0:T(8,128)(2,1)S(1)}) custom-call(f32[1]{0:T(128)S(6)} %copy.6.scale, bf16[1024,1024]{1,0:T(8,128)(2,1)S(1)} %get-tuple-element.54.weights, bf16[1024,1280]{1,0:T(8,128)(2,1)S(1)} %get-tuple-element.53.images, bf16[1024,1280]{1,0:T(8,128)(2,1)S(1)} %get-tuple-element.55.texts), custom_call_target="tpu_custom_call" | custom-call | tf_op jit(solution)/shard_map/pallas_call | solution.py:410
  93.1 17.6 %collective-permute-done.23.refs_3_ = bf16[80,1280]{1,0:T(8,128)(2,1)S(1)} collective-permute-done((bf16[80,1280]{1,0:T(8,128)(2,1)S(1)}, bf16[80,1280]{1,0:T(8,128)(2,1)S(1)}, u32[]{:S(2)}, u32[]{:S(2)}) %collective-permute-start.23) | collective-permute-done | bytes 204832 | tf_op jit(solution)/shard_map/ppermute | solution.py:44
  110.7 1.0 collective-permute-done.22.refs_2_
  111.7 0.2 shard_map.69
  112.0 1.4 %collective-permute-start.24 = (bf16[144,1280]{1,0:T(8,128)(2,1)S(1)}, bf16[144,1280]{1,0:T(8,128)(2,1)S(1)}, u32[]{:S(2)}, u32[]{:S(2)}) collective-permute-start(bf16[144,1280]{1,0:T(8,128)(2,1)S(1)} %get-tuple-element.73), channel_id=1, source_target_pairs={{0,64},{64,128},{128,192},{192,16},{16,80},{80,144},{144,208},{208... | collective-permute-start | bytes 1105928 | tf_op jit(solution)/shard_map/ppermute | solution.py:44
  113.4 0.0 collective-permute-done.16.refs_1_
  113.4 0.0 collective-permute-done.17.refs_2_
  113.4 0.0 collective-permute-done.18.refs_3_
  113.4 0.4 shard_map.68
  113.8 2.4 %collective-permute-start.19 = (bf16[80,1280]{1,0:T(8,128)(2,1)S(1)}, bf16[80,1280]{1,0:T(8,128)(2,1)S(1)}, u32[]{:S(2)}, u32[]{:S(2)}) collective-permute-start(bf16[80,1280]{1,0:T(8,128)(2,1)S(1)} %get-tuple-element.67), channel_id=1, source_target_pairs={{0,2},{1,3},{2,0},{3,1},{4,6},{5,7},{6,4},{7,5},{8,10},{9,11},{10,... | collective-permute-start | bytes 614408 | tf_op jit(solution)/shard_map/ppermute | solution.py:35
  116.2 1.1 collective-permute-start.20
  117.3 0.9 collective-permute-start.21
  118.2 1.3 %collective-permute-done.24.refs_1_ = bf16[144,1280]{1,0:T(8,128)(2,1)S(1)} collective-permute-done((bf16[144,1280]{1,0:T(8,128)(2,1)S(1)}, bf16[144,1280]{1,0:T(8,128)(2,1)S(1)}, u32[]{:S(2)}, u32[]{:S(2)}) %collective-permute-start.24) | collective-permute-done | bytes 368672 | tf_op jit(solution)/shard_map/ppermute | solution.py:44
  119.6 0.1 shard_map.70
  119.7 0.1 collective-permute-start.25
  119.8 1.4 %collective-permute-done.19.refs_1_ = bf16[80,1280]{1,0:T(8,128)(2,1)S(1)} collective-permute-done((bf16[80,1280]{1,0:T(8,128)(2,1)S(1)}, bf16[80,1280]{1,0:T(8,128)(2,1)S(1)}, u32[]{:S(2)}, u32[]{:S(2)}) %collective-permute-start.19) | collective-permute-done | bytes 204832 | tf_op jit(solution)/shard_map/ppermute | solution.py:35
  121.1 1.6 %collective-permute-done.20.refs_2_ = bf16[80,1280]{1,0:T(8,128)(2,1)S(1)} collective-permute-done((bf16[80,1280]{1,0:T(8,128)(2,1)S(1)}, bf16[80,1280]{1,0:T(8,128)(2,1)S(1)}, u32[]{:S(2)}, u32[]{:S(2)}) %collective-permute-start.20) | collective-permute-done | bytes 204832 | tf_op jit(solution)/shard_map/ppermute | solution.py:35
  122.7 1.6 %collective-permute-done.21.refs_3_ = bf16[80,1280]{1,0:T(8,128)(2,1)S(1)} collective-permute-done((bf16[80,1280]{1,0:T(8,128)(2,1)S(1)}, bf16[80,1280]{1,0:T(8,128)(2,1)S(1)}, u32[]{:S(2)}, u32[]{:S(2)}) %collective-permute-start.21) | collective-permute-done | bytes 204832 | tf_op jit(solution)/shard_map/ppermute | solution.py:35
  124.3 0.8 shard_map.71
  (8 shorter events, 0.0 us)
Async XLA Ops:
  0.6 1.7 %collective-permute-start = (bf16[64,1280]{1,0:T(8,128)(2,1)}, bf16[64,1280]{1,0:T(8,128)(2,1)S(1)}, u32[]{:S(2)}, u32[]{:S(2)}) collective-permute-start(bf16[64,1280]{1,0:T(8,128)(2,1)} %refs_0_.1), channel_id=1, source_target_pairs={{0,32},{32,0},{1,33},{33,1},{2,34},{34,2},{3,35},{35,3},{4,36},{36... | collective-permute-start | bytes 491528 | tf_op jit(solution)/shard_map/ppermute | solution.py:48
  2.3 0.9 copy-start
  3.2 0.9 copy-start.1
  4.2 18.9 %collective-permute-start.4 = (bf16[128,1280]{1,0:T(8,128)(2,1)S(1)}, bf16[128,1280]{1,0:T(8,128)(2,1)S(1)}, u32[]{:S(2)}, u32[]{:S(2)}) collective-permute-start(bf16[128,1280]{1,0:T(8,128)(2,1)S(1)} %get-tuple-element.42.refs_4_), channel_id=1, source_target_pairs={{0,208},{64,0},{128,64},{192,128},{16,192},{80,16},{144,80},{208,1... | collective-permute-start | bytes 983048 | tf_op jit(solution)/shard_map/ppermute | solution.py:44
  6.1 17.0 %collective-permute-start.5 = (bf16[64,1280]{1,0:T(8,128)(2,1)S(1)}, bf16[64,1280]{1,0:T(8,128)(2,1)S(1)}, u32[]{:S(2)}, u32[]{:S(2)}) collective-permute-start(bf16[64,1280]{1,0:T(8,128)(2,1)S(1)} %copy-done.1), channel_id=1, source_target_pairs={{0,16},{64,80},{128,144},{192,208},{16,0},{80,64},{144,128},{208,1... | collective-permute-start | bytes 491528 | tf_op jit(solution)/shard_map/ppermute | solution.py:44
  11.6 11.5 %collective-permute-start.3 = (bf16[64,1280]{1,0:T(8,128)(2,1)S(1)}, bf16[64,1280]{1,0:T(8,128)(2,1)S(1)}, u32[]{:S(2)}, u32[]{:S(2)}) collective-permute-start(bf16[64,1280]{1,0:T(8,128)(2,1)S(1)} %get-tuple-element.41.refs_0_), channel_id=1, source_target_pairs={{0,3},{1,0},{2,1},{3,2},{4,7},{5,4},{6,5},{7,6},{8,11},{9,8},{10,9... | collective-permute-start | bytes 491528 | tf_op jit(solution)/shard_map/ppermute | solution.py:35
  14.3 8.8 %collective-permute-start.2 = (bf16[64,1280]{1,0:T(8,128)(2,1)S(1)}, bf16[64,1280]{1,0:T(8,128)(2,1)S(1)}, u32[]{:S(2)}, u32[]{:S(2)}) collective-permute-start(bf16[64,1280]{1,0:T(8,128)(2,1)S(1)} %get-tuple-element.41.refs_0_), channel_id=1, source_target_pairs={{0,2},{1,3},{2,0},{3,1},{4,6},{5,7},{6,4},{7,5},{8,10},{9,11},{10,... | collective-permute-start | bytes 491528 | tf_op jit(solution)/shard_map/ppermute | solution.py:35
  15.1 8.0 %collective-permute-start.1 = (bf16[64,1280]{1,0:T(8,128)(2,1)S(1)}, bf16[64,1280]{1,0:T(8,128)(2,1)S(1)}, u32[]{:S(2)}, u32[]{:S(2)}) collective-permute-start(bf16[64,1280]{1,0:T(8,128)(2,1)S(1)} %get-tuple-element.41.refs_0_), channel_id=1, source_target_pairs={{0,1},{1,2},{2,3},{3,0},{4,5},{5,6},{6,7},{7,4},{8,9},{9,10},{10,1... | collective-permute-start | bytes 491528 | tf_op jit(solution)/shard_map/ppermute | solution.py:35
  24.0 17.4 %collective-permute-start.9 = (bf16[256,1280]{1,0:T(8,128)(2,1)S(1)}, bf16[256,1280]{1,0:T(8,128)(2,1)S(1)}, u32[]{:S(2)}, u32[]{:S(2)}) collective-permute-start(bf16[256,1280]{1,0:T(8,128)(2,1)S(1)} %get-tuple-element.44.refs_4_), channel_id=1, source_target_pairs={{0,144},{64,208},{128,0},{192,64},{16,128},{80,192},{144,16},{208,... | collective-permute-start | bytes 1966088 | tf_op jit(solution)/shard_map/ppermute | solution.py:44
  25.9 18.5 %collective-permute-start.8 = (bf16[256,1280]{1,0:T(8,128)(2,1)S(1)}, bf16[256,1280]{1,0:T(8,128)(2,1)S(1)}, u32[]{:S(2)}, u32[]{:S(2)}) collective-permute-start(bf16[256,1280]{1,0:T(8,128)(2,1)S(1)} %get-tuple-element.43.refs_0_), channel_id=1, source_target_pairs={{0,12},{1,13},{2,14},{3,15},{4,0},{5,1},{6,2},{7,3},{8,4},{9,5},{1... | collective-permute-start | bytes 1966088 | tf_op jit(solution)/shard_map/ppermute | solution.py:35
  28.9 15.5 %collective-permute-start.7 = (bf16[256,1280]{1,0:T(8,128)(2,1)S(1)}, bf16[256,1280]{1,0:T(8,128)(2,1)S(1)}, u32[]{:S(2)}, u32[]{:S(2)}) collective-permute-start(bf16[256,1280]{1,0:T(8,128)(2,1)S(1)} %get-tuple-element.43.refs_0_), channel_id=1, source_target_pairs={{0,8},{1,9},{2,10},{3,11},{4,12},{5,13},{6,14},{7,15},{8,0},{9,1},... | collective-permute-start | bytes 1966088 | tf_op jit(solution)/shard_map/ppermute | solution.py:35
  29.5 18.6 %collective-permute-start.6 = (bf16[256,1280]{1,0:T(8,128)(2,1)S(1)}, bf16[256,1280]{1,0:T(8,128)(2,1)}, u32[]{:S(2)}, u32[]{:S(2)}) collective-permute-start(bf16[256,1280]{1,0:T(8,128)(2,1)S(1)} %get-tuple-element.43.refs_0_), channel_id=1, source_target_pairs={{0,4},{1,5},{2,6},{3,7},{4,8},{5,9},{6,10},{7,11},{8,12},{9,13},{1... | collective-permute-start | bytes 1966088 | tf_op jit(solution)/shard_map/ppermute | solution.py:35
  41.4 6.7 %collective-permute-start.10 = (bf16[256,1280]{1,0:T(8,128)(2,1)S(1)}, bf16[256,1280]{1,0:T(8,128)(2,1)}, u32[]{:S(2)}, u32[]{:S(2)}) collective-permute-start(bf16[256,1280]{1,0:T(8,128)(2,1)S(1)} %collective-permute-done.9.refs_5_), channel_id=1, source_target_pairs={{0,32},{32,0},{1,33},{33,1},{2,34},{34,2},{3,35},{35,3},{4,36},{36... | collective-permute-start | bytes 1966088 | tf_op jit(solution)/shard_map/ppermute | solution.py:48
  41.4 2.9 %collective-permute-start.11 = (bf16[192,1280]{1,0:T(8,128)(2,1)}, bf16[192,1280]{1,0:T(8,128)(2,1)}, u32[]{:S(2)}, u32[]{:S(2)}) collective-permute-start(bf16[192,1280]{1,0:T(8,128)(2,1)} %get-tuple-element.45), channel_id=1, source_target_pairs={{0,32},{32,0},{1,33},{33,1},{2,34},{34,2},{3,35},{35,3},{4,36},{36... | collective-permute-start | bytes 1474568 | tf_op jit(solution)/shard_map/ppermute | solution.py:48
  56.5 1.3 %collective-permute-start.12 = (f32[24,128]{1,0:T(8,128)S(1)}, f32[24,128]{1,0:T(8,128)S(1)}, u32[]{:S(2)}, u32[]{:S(2)}) collective-permute-start(f32[24,128]{1,0:T(8,128)S(1)} %get-tuple-element.50), channel_id=1, source_target_pairs={{0,32},{32,0},{1,33},{33,1},{2,34},{34,2},{3,35},{35,3},{4,36},{36... | collective-permute-start | bytes 36872 | tf_op jit(solution)/shard_map/ppermute | solution.py:48
  72.4 3.0 %collective-permute-start.13 = (f32[24,128]{1,0:T(8,128)S(1)}, f32[24,128]{1,0:T(8,128)S(1)}, u32[]{:S(2)}, u32[]{:S(2)}) collective-permute-start(f32[24,128]{1,0:T(8,128)S(1)} %get-tuple-element.52), channel_id=1, source_target_pairs={{0,32},{32,0},{1,33},{33,1},{2,34},{34,2},{3,35},{35,3},{4,36},{36... | collective-permute-start | bytes 36872 | tf_op jit(solution)/shard_map/ppermute | solution.py:48
  79.0 2.9 %collective-permute-start.14 = (bf16[256,1280]{1,0:T(8,128)(2,1)S(1)}, bf16[256,1280]{1,0:T(8,128)(2,1)S(1)}, u32[]{:S(2)}, u32[]{:S(2)}) collective-permute-start(bf16[256,1280]{1,0:T(8,128)(2,1)S(1)} %get-tuple-element.58), channel_id=1, source_target_pairs={{0,32},{32,0},{1,33},{33,1},{2,34},{34,2},{3,35},{35,3},{4,36},{36... | collective-permute-start | bytes 1966088 | tf_op jit(solution)/shard_map/ppermute | solution.py:48
  79.4 2.5 %collective-permute-start.15 = (bf16[192,1280]{1,0:T(8,128)(2,1)S(1)}, bf16[192,1280]{1,0:T(8,128)(2,1)S(1)}, u32[]{:S(2)}, u32[]{:S(2)}) collective-permute-start(bf16[192,1280]{1,0:T(8,128)(2,1)S(1)} %get-tuple-element.60), channel_id=1, source_target_pairs={{0,32},{32,0},{1,33},{33,1},{2,34},{34,2},{3,35},{35,3},{4,36},{36... | collective-permute-start | bytes 1474568 | tf_op jit(solution)/shard_map/ppermute | solution.py:48
  82.1 29.7 %collective-permute-start.22 = (bf16[272,1280]{1,0:T(8,128)(2,1)S(1)}, bf16[272,1280]{1,0:T(8,128)(2,1)S(1)}, u32[]{:S(2)}, u32[]{:S(2)}) collective-permute-start(bf16[272,1280]{1,0:T(8,128)(2,1)S(1)} %get-tuple-element.62.after), channel_id=1, source_target_pairs={{0,128},{64,192},{128,16},{192,80},{16,144},{80,208},{144,0},{208,... | collective-permute-start | bytes 2088968 | tf_op jit(solution)/shard_map/ppermute | solution.py:44
  85.8 27.6 %collective-permute-start.16 = (bf16[272,1280]{1,0:T(8,128)(2,1)S(1)}, bf16[272,1280]{1,0:T(8,128)(2,1)S(1)}, u32[]{:S(2)}, u32[]{:S(2)}) collective-permute-start(bf16[272,1280]{1,0:T(8,128)(2,1)S(1)} %get-tuple-element.63), channel_id=1, source_target_pairs={{0,8},{1,9},{2,10},{3,11},{4,12},{5,13},{6,14},{7,15},{8,0},{9,1},... | collective-permute-start | bytes 2088968 | tf_op jit(solution)/shard_map/ppermute | solution.py:35
  86.4 26.9 %collective-permute-start.17 = (bf16[272,1280]{1,0:T(8,128)(2,1)S(1)}, bf16[272,1280]{1,0:T(8,128)(2,1)S(1)}, u32[]{:S(2)}, u32[]{:S(2)}) collective-permute-start(bf16[272,1280]{1,0:T(8,128)(2,1)S(1)} %get-tuple-element.64), channel_id=1, source_target_pairs={{0,12},{1,13},{2,14},{3,15},{4,0},{5,1},{6,2},{7,3},{8,4},{9,5},{1... | collective-permute-start | bytes 2088968 | tf_op jit(solution)/shard_map/ppermute | solution.py:35
  89.3 24.0 %collective-permute-start.18 = (bf16[272,1280]{1,0:T(8,128)(2,1)S(1)}, bf16[272,1280]{1,0:T(8,128)(2,1)S(1)}, u32[]{:S(2)}, u32[]{:S(2)}) collective-permute-start(bf16[272,1280]{1,0:T(8,128)(2,1)S(1)} %get-tuple-element.65), channel_id=1, source_target_pairs={{0,4},{1,5},{2,6},{3,7},{4,8},{5,9},{6,10},{7,11},{8,12},{9,13},{1... | collective-permute-start | bytes 2088968 | tf_op jit(solution)/shard_map/ppermute | solution.py:35
  89.3 21.4 %collective-permute-start.23 = (bf16[80,1280]{1,0:T(8,128)(2,1)S(1)}, bf16[80,1280]{1,0:T(8,128)(2,1)S(1)}, u32[]{:S(2)}, u32[]{:S(2)}) collective-permute-start(bf16[80,1280]{1,0:T(8,128)(2,1)S(1)} %get-tuple-element.71), channel_id=1, source_target_pairs={{0,16},{64,80},{128,144},{192,208},{16,0},{80,64},{144,128},{208,1... | collective-permute-start | bytes 614408 | tf_op jit(solution)/shard_map/ppermute | solution.py:44
  112.0 7.6 %collective-permute-start.24 = (bf16[144,1280]{1,0:T(8,128)(2,1)S(1)}, bf16[144,1280]{1,0:T(8,128)(2,1)S(1)}, u32[]{:S(2)}, u32[]{:S(2)}) collective-permute-start(bf16[144,1280]{1,0:T(8,128)(2,1)S(1)} %get-tuple-element.73), channel_id=1, source_target_pairs={{0,64},{64,128},{128,192},{192,16},{16,80},{80,144},{144,208},{208... | collective-permute-start | bytes 1105928 | tf_op jit(solution)/shard_map/ppermute | solution.py:44
  113.8 7.3 %collective-permute-start.19 = (bf16[80,1280]{1,0:T(8,128)(2,1)S(1)}, bf16[80,1280]{1,0:T(8,128)(2,1)S(1)}, u32[]{:S(2)}, u32[]{:S(2)}) collective-permute-start(bf16[80,1280]{1,0:T(8,128)(2,1)S(1)} %get-tuple-element.67), channel_id=1, source_target_pairs={{0,2},{1,3},{2,0},{3,1},{4,6},{5,7},{6,4},{7,5},{8,10},{9,11},{10,... | collective-permute-start | bytes 614408 | tf_op jit(solution)/shard_map/ppermute | solution.py:35
  116.2 6.5 %collective-permute-start.20 = (bf16[80,1280]{1,0:T(8,128)(2,1)S(1)}, bf16[80,1280]{1,0:T(8,128)(2,1)S(1)}, u32[]{:S(2)}, u32[]{:S(2)}) collective-permute-start(bf16[80,1280]{1,0:T(8,128)(2,1)S(1)} %get-tuple-element.68), channel_id=1, source_target_pairs={{0,3},{1,0},{2,1},{3,2},{4,7},{5,4},{6,5},{7,6},{8,11},{9,8},{10,9... | collective-permute-start | bytes 614408 | tf_op jit(solution)/shard_map/ppermute | solution.py:35
  117.3 7.0 %collective-permute-start.21 = (bf16[80,1280]{1,0:T(8,128)(2,1)S(1)}, bf16[80,1280]{1,0:T(8,128)(2,1)S(1)}, u32[]{:S(2)}, u32[]{:S(2)}) collective-permute-start(bf16[80,1280]{1,0:T(8,128)(2,1)S(1)} %get-tuple-element.69), channel_id=1, source_target_pairs={{0,1},{1,2},{2,3},{3,0},{4,5},{5,6},{6,7},{7,4},{8,9},{9,10},{10,1... | collective-permute-start | bytes 614408 | tf_op jit(solution)/shard_map/ppermute | solution.py:35
  119.7 4.6 %collective-permute-start.25 = (bf16[80,1280]{1,0:T(8,128)(2,1)S(1)}, bf16[80,1280]{1,0:T(8,128)(2,1)S(1)}, u32[]{:S(2)}, u32[]{:S(2)}) collective-permute-start(bf16[80,1280]{1,0:T(8,128)(2,1)S(1)} %get-tuple-element.75), channel_id=1, source_target_pairs={{0,32},{32,0},{1,33},{33,1},{2,34},{34,2},{3,35},{35,3},{4,36},{36... | collective-permute-start | bytes 614408 | tf_op jit(solution)/shard_map/ppermute | solution.py:48

commit v8 on v7

--- a/solution.py
+++ b/solution.py
@@ -136,23 +136,15 @@
 def logits_body(place, scale, *refs):
     images, texts = refs[:4], refs[4:7]
     logits, row_out, col_out, message, match_out, all_images, all_texts = refs[9:16]
-    row_wide, sems = refs[16:]
-    copies = []
-    for i, (out, at) in enumerate(
-        [(all_texts, 3 * CHUNK), (all_texts, BLOCK - ROWS)]
-        + [(all_images, a * CHUNK) for a in range(4)]
-        + [(all_texts, j * CHUNK) for j in range(3)]
-    ):
-        source = (refs[7], refs[8], *images, *texts)[i]
-        into = out.at[at : at + source.shape[0], :]
-        copies.append(pltpu.make_async_copy(source, into, sems.at[i]))
-        copies[-1].start()
+    row_wide = refs[16]
+    all_texts[3 * CHUNK : BLOCK - ROWS, :] = refs[7][...]
+    all_texts[BLOCK - ROWS :, :] = refs[8][...]
     where = [place[i] for i in range(5)]
     multiplier = scale[0] * LOG2E
     for j in range(4):
-        if j == 3:
-            copies[0].wait()
-            copies[1].wait()
+        if j < 3:
+            all_texts[j * CHUNK : (j + 1) * CHUNK, :] = texts[j][...]
+        all_images[j * CHUNK : (j + 1) * CHUNK, :] = images[j][...]
         for a in range(4):
             text = texts[j][...] if j < 3 else all_texts[3 * CHUNK :, :]
             logits[a * CHUNK : (a + 1) * CHUNK, j * CHUNK : (j + 1) * CHUNK] = multiplier * lax.dot_general(
@@ -193,8 +185,6 @@
         row_out[pl.ds(row_place(where, j, i)[0], 1), :] = line
         row_out[pl.ds(row_place(where, j, i + 1)[0], 1), :] = pltpu.roll(line, 64, 1)
     message[:16, :] = jnp.where(where[1] == 0, col_out[...], row_out[...])
-    for copy in copies[2:]:
-        copy.wait()
 
 
 def logits_call(place, scale, images, texts):
@@ -211,9 +201,18 @@
         ),
         in_specs=[SMEM, SMEM] + [VMEM] * 9,
         out_specs=(VMEM,) * 7,
-        scratch_shapes=[pltpu.VMEM((BLOCK, 128), F32), pltpu.SemaphoreType.DMA((9,))],
+        scratch_shapes=[pltpu.VMEM((BLOCK, 128), F32)],
         compiler_params=PARAMS,
     )(place, scale, *images, *texts)
+
+
+def pair_up(rows):
+    low = lax.broadcasted_iota(jnp.int32, (1, 128), 1) < ROWS
+    pairs = [
+        jnp.where(low, rows[i : i + 1], pltpu.roll(rows[i + 1 : i + 2], 64, 1))
+        for i in range(0, rows.shape[0], 2)
+    ]
+    return jnp.concatenate(pairs)
 
 
 def spread_body(place, row, col, matched, got, out):
@@ -221,17 +220,19 @@
     mine, other = row[...], got[:16, :]
     top = jnp.maximum(col[...], other)
     both = top + LOG2E * jnp.log(jnp.exp2(col[...] - top) + jnp.exp2(other - top))
+    low = pair_up(jnp.where(first, mine, both))
+    high = pair_up(other)
     hits = matched[...] + got[16:24, :]
     for i in range(16):
-        out[i, :16, :] = jnp.where(first, mine, both)
-        out[i, 16:32, :] = jnp.where(first, other, both)
-        out[i, 32:40, :] = hits
+        out[i, :8, :] = low
+        out[i, 8:16, :] = high
+        out[i, 16:24, :] = hits
 
 
 def spread_call(place, *parts):
     return pl.pallas_call(
         spread_body,
-        out_shape=jax.ShapeDtypeStruct((16, 40, 128), F32),
+        out_shape=jax.ShapeDtypeStruct((16, 24, 128), F32),
         in_specs=[SMEM] + [VMEM] * 4,
         out_specs=VMEM,
         compiler_params=PARAMS,
@@ -241,7 +242,7 @@
 def join_body(place, got, mine, message):
     first = place[1] == 0
     counts = [jnp.logical_or(first, (place[3] >> 1) == i % 2) for i in range(16)]
-    parts = [jnp.where(counts[i], got[i, :32, :], -jnp.inf) for i in range(16)]
+    parts = [jnp.where(counts[i], got[i, :16, :], -jnp.inf) for i in range(16)]
     top = parts[0]
     for p in parts[1:]:
         top = jnp.maximum(top, p)
@@ -249,16 +250,17 @@
     for p in parts[1:]:
         total += jnp.exp2(p - top)
     state = top + LOG2E * jnp.log(total)
-    hits = got[0, 32:40, :]
+    low, high = state[:8], state[8:]
+    hits = got[0, 16:24, :]
     for i in range(1, 16):
-        hits += got[i, 32:40, :]
-    real = lax.broadcasted_iota(jnp.int32, (16, 128), 1) < ROWS
-    both = jnp.where(real, state[:16] + jnp.where(first, state[16:], 0.0), 0.0)
+        hits += got[i, 16:24, :]
+    both = low + jnp.where(first, high, 0.0)
     share = jnp.sum(both, keepdims=True) - jnp.where(first, 2.0 * hits, 0.0)
-    mine[:16, :] = state[:16]
-    mine[16:24, :] = share
-    message[:16, :] = jnp.where(first, state[16:], state[:16])
-    message[16:24, :] = share
+    for out, pairs in ((mine, low), (message, jnp.where(first, high, low))):
+        for i in range(8):
+            out[2 * i : 2 * i + 1, :] = pairs[i : i + 1]
+            out[2 * i + 1 : 2 * i + 2, :] = pltpu.roll(pairs[i : i + 1], 64, 1)
+        out[16:24, :] = share
 
 
 def join_call(place, got):
@@ -446,11 +448,11 @@
 
 
 def last_body(*refs):
-    digits, image_out, text_out, loss_out = refs[6:]
+    digits, image_out, text_out, loss_out = refs[7:]
     add_rows(refs, ROWS, [(i, 0) for i in range(4)], image_out, 0)
-    add_rows(refs, ROWS, [(4, 0), (5, 0)], text_out, 0)
+    add_rows(refs, ROWS, [(4, 0), (5, 0), (6, 0)], text_out, 0)
     total = -digits[:TAIL, :128].astype(F32)
-    for r in refs[:6]:
+    for r in refs[:7]:
         total += r[ROWS : ROWS + TAIL, :128].astype(F32)
     loss_out[...] = value_of(total)[:, 0:1] * (LN2 / (2.0 * ROWS * 256))
 
@@ -460,7 +462,7 @@
     return pl.pallas_call(
         last_body,
         out_shape=(grad, grad, jax.ShapeDtypeStruct((1, 1), F32)),
-        in_specs=[VMEM] * 7,
+        in_specs=[VMEM] * 8,
         out_specs=(VMEM,) * 3,
         compiler_params=PARAMS,
     )(*shards, *texts, digits)
@@ -492,32 +494,28 @@
 
     other_1, other_3 = core_swap(text_2), core_swap(text_3)
     text_1, far = text_call(logit_scale, weights, images)
-    rows_tail = (TAIL, ((4, 0),))
-    pairs, far = sums(
+    pairs = sums(
         [text_1, other_1, far, other_3, digits],
-        ((256, ((0, 0), (1, 0))), rows_tail),
-        ((64, ((2, 0), (3, 128))), rows_tail),
-    )
+        ((256, ((0, 0), (1, 0))), (64, ((2, 0), (3, 128))), (TAIL, ((4, 0),))),
+    )[0]
     image_parts = image_call(logit_scale, pairs, digits, weights, texts)
-    pairs, next_4 = z_shift(pairs, 2), z_shift(far, 4)
+    pairs = z_shift(pairs, 2)
     back = [plane_shift(v, -k, False) for v, k in zip(image_parts, (2, 1, 3))]
     text_0, image_0 = rest_call(logit_scale, weights, images, texts)
 
-    next_1, mine = sums(
-        [text_0, other_3, pairs, next_4, digits],
-        ((128, ((0, 128), (1, 0), (2, 128))), (TAIL, ((2, 256), (4, 0)))),
-        (
-            (64, ((0, 0), (2, 0), (3, 0))),
-            (64, ((0, 64), (2, 64))),
-            (TAIL, ((2, 256), (3, 64), (4, 0))),
-            (TAIL, ((2, 256), (4, 0))),
-        ),
-    )
-    next_1 = z_shift(next_1, 1)
+    rows_tail = (TAIL, ((2, 320), (3, 0)))
+    next_1, mine, next_4 = sums(
+        [text_0, other_3, pairs, digits],
+        ((128, ((0, 128), (1, 0), (2, 128))), rows_tail),
+        ((128, ((0, 0), (2, 0))), rows_tail),
+        ((80, ((2, 256),)),),
+    )
+    next_1, next_4 = z_shift(next_1, 1), z_shift(next_4, 2)
+    rows_tail = (TAIL, ((0, 128), (1, 128)))
     mine, other = sums(
         [mine, next_1],
-        ((64, ((0, 0), (1, 0))), (TAIL, ((0, 128), (1, 128)))),
-        ((64, ((0, 64), (1, 64))), (TAIL, ((0, 144), (1, 128)))),
+        ((64, ((0, 0), (1, 0))), rows_tail),
+        ((64, ((0, 64), (1, 64))), rows_tail),
     )
 
     cols_tail = (TAIL, ((1, 256), (2, 256), (3, 256), (4, 16)))
@@ -526,7 +524,7 @@
         *[((64, [(i, 64 * k) for i in range(4)]), cols_tail) for k in range(4)],
     )
     shards = [pieces[0]] + [plane_shift(pieces[k], -k, True) for k in (2, 1, 3)]
-    image_grad, text_grad, mean_loss = last_call(shards, [mine, core_swap(other)], digits)
+    image_grad, text_grad, mean_loss = last_call(shards, [mine, core_swap(other), next_4], digits)
     return mean_loss.reshape(1), image_grad, text_grad
 
 

time: 125 us -> 119 us (0.952); the launches traced: 125 us -> 117 us
  starting transfers between devices: 34.9 us -> 31.3 us
  Pallas kernels: 21.6 us -> 19.1 us
  waiting for transfers between devices: 52 us -> 50.7 us
    ppermute x6, starting transfers between devices: 14.3 us -> 11.1 us  [z_shift(): return lax.ppermute(v, ('zl', 'core', 'zh'), pairs)]
    pallas_call x1, Pallas kernels: 8.36 us -> 5.8 us  [logits_call(): pl.pallas_call(logits_body, out_shape=(jax.ShapeDtypeStruct((BLOCK, BLOCK...]
    ppermute x12, waiting for transfers between devices: 8.29 us -> 7.03 us  [plane_shift(): return lax.ppermute(v, ('core', 'zh', 'y', 'x'), pairs)]
where the time goes in v8:
time: 119 us; the launch traced here: 117 us
  waiting for transfers between devices  50.7 us (43%)
  starting transfers between devices  31.3 us (26%)
  Pallas kernels  19.1 us (16%)
  blocking collectives  12.7 us (11%)
  local copies, waits for them, and re-layouts  1.92 us (2%)
  between operations  1.43 us (1%)
    ppermute x6, waiting for transfers between devices, z_shift(): return lax.ppermute(v, ('zl', 'core', 'zh'), pairs)  38 us
    ppermute x12, starting transfers between devices, plane_shift(): return lax.ppermute(v, ('core', 'zh', 'y', 'x'), pairs)  17.1 us
    all_to_all x1, blocking collectives, exchange(): return lax.all_to_all(v, AXES, 0, 0, axis_index_groups=groups)  12.7 us
    ppermute x6, starting transfers between devices, z_shift(): return lax.ppermute(v, ('zl', 'core', 'zh'), pairs)  11.1 us
    ppermute x12, waiting for transfers between devices, plane_shift(): return lax.ppermute(v, ('core', 'zh', 'y', 'x'), pairs)  7.03 us
    pallas_call x1, Pallas kernels, logits_call(): pl.pallas_call(logits_body, out_shape=(jax.ShapeDtypeStruct((BLOCK, BLOCK...  5.8 us
    ppermute x8, waiting for transfers between devices, core_swap(): return lax.ppermute(v, 'core', [(0, 1), (1, 0)])  5.68 us
    pallas_call x1, Pallas kernels, weights_call(): pl.pallas_call(weights_body, out_shape=(jax.ShapeDtypeStruct((BLOCK, BLOC...  3.58 us
  transfers between devices with their start and end apart: 26, of which 14 were waited for; matrix products, arithmetic and copies ran while one was open for 0% of the time, Pallas kernels for 5%

profile of v8, /device:TPU:32, one launch (start us, length us, event | category | flops | bytes accessed | tf_op | source)
XLA Modules:
  0.0 117.1 jit_solution(4621848557194382166)
XLA Ops:
  0.6 0.1 collective-permute-start
  0.7 1.6 %collective-permute-done.refs_1_ = bf16[64,1280]{1,0:T(8,128)(2,1)S(1)} collective-permute-done((bf16[64,1280]{1,0:T(8,128)(2,1)}, bf16[64,1280]{1,0:T(8,128)(2,1)S(1)}, u32[]{:S(2)}, u32[]{:S(2)}) %collective-permute-start) | collective-permute-done | bytes 163872 | tf_op jit(solution)/shard_map/ppermute | solution.py:48
  2.3 0.9 copy-done
  3.2 0.9 copy-done.1
  4.2 1.9 %collective-permute-start.4 = (bf16[128,1280]{1,0:T(8,128)(2,1)S(1)}, bf16[128,1280]{1,0:T(8,128)(2,1)S(1)}, u32[]{:S(2)}, u32[]{:S(2)}) collective-permute-start(bf16[128,1280]{1,0:T(8,128)(2,1)S(1)} %get-tuple-element.41.refs_4_), channel_id=1, source_target_pairs={{0,208},{64,0},{128,64},{192,128},{16,192},{80,16},{144,80},{208,1... | collective-permute-start | bytes 983048 | tf_op jit(solution)/shard_map/ppermute | solution.py:44
  6.1 5.5 %collective-permute-start.5 = (bf16[64,1280]{1,0:T(8,128)(2,1)S(1)}, bf16[64,1280]{1,0:T(8,128)(2,1)S(1)}, u32[]{:S(2)}, u32[]{:S(2)}) collective-permute-start(bf16[64,1280]{1,0:T(8,128)(2,1)S(1)} %copy-done.1), channel_id=1, source_target_pairs={{0,16},{64,80},{128,144},{192,208},{16,0},{80,64},{144,128},{208,1... | collective-permute-start | bytes 491528 | tf_op jit(solution)/shard_map/ppermute | solution.py:44
  11.6 2.8 %collective-permute-start.3 = (bf16[64,1280]{1,0:T(8,128)(2,1)S(1)}, bf16[64,1280]{1,0:T(8,128)(2,1)S(1)}, u32[]{:S(2)}, u32[]{:S(2)}) collective-permute-start(bf16[64,1280]{1,0:T(8,128)(2,1)S(1)} %get-tuple-element.40.refs_0_), channel_id=1, source_target_pairs={{0,3},{1,0},{2,1},{3,2},{4,7},{5,4},{6,5},{7,6},{8,11},{9,8},{10,9... | collective-permute-start | bytes 491528 | tf_op jit(solution)/shard_map/ppermute | solution.py:35
  14.3 0.8 collective-permute-start.2
  15.1 0.9 collective-permute-start.1
  16.0 7.1 %collective-permute-done.5.refs_6_.refs_8_ = bf16[64,1280]{1,0:T(8,128)(2,1)S(1)} collective-permute-done((bf16[64,1280]{1,0:T(8,128)(2,1)S(1)}, bf16[64,1280]{1,0:T(8,128)(2,1)S(1)}, u32[]{:S(2)}, u32[]{:S(2)}) %collective-permute-start.5) | collective-permute-done | bytes 163872 | tf_op jit(solution)/shard_map/ppermute | solution.py:44
  23.1 0.0 collective-permute-done.1.refs_1_
  23.1 0.0 collective-permute-done.4.refs_5_
  23.1 0.9 shard_map.59
  24.0 1.9 %collective-permute-start.9 = (bf16[256,1280]{1,0:T(8,128)(2,1)S(1)}, bf16[256,1280]{1,0:T(8,128)(2,1)S(1)}, u32[]{:S(2)}, u32[]{:S(2)}) collective-permute-start(bf16[256,1280]{1,0:T(8,128)(2,1)S(1)} %get-tuple-element.43.refs_4_), channel_id=1, source_target_pairs={{0,144},{64,208},{128,0},{192,64},{16,128},{80,192},{144,16},{208,... | collective-permute-start | bytes 1966088 | tf_op jit(solution)/shard_map/ppermute | solution.py:44
  25.9 3.0 %collective-permute-start.8 = (bf16[256,1280]{1,0:T(8,128)(2,1)S(1)}, bf16[256,1280]{1,0:T(8,128)(2,1)S(1)}, u32[]{:S(2)}, u32[]{:S(2)}) collective-permute-start(bf16[256,1280]{1,0:T(8,128)(2,1)S(1)} %get-tuple-element.42.refs_0_), channel_id=1, source_target_pairs={{0,12},{1,13},{2,14},{3,15},{4,0},{5,1},{6,2},{7,3},{8,4},{9,5},{1... | collective-permute-start | bytes 1966088 | tf_op jit(solution)/shard_map/ppermute | solution.py:35
  28.9 0.6 collective-permute-start.7
  29.5 1.0 collective-permute-start.6
  30.5 10.9 %collective-permute-done.9.refs_5_ = bf16[256,1280]{1,0:T(8,128)(2,1)S(1)} collective-permute-done((bf16[256,1280]{1,0:T(8,128)(2,1)S(1)}, bf16[256,1280]{1,0:T(8,128)(2,1)S(1)}, u32[]{:S(2)}, u32[]{:S(2)}) %collective-permute-start.9) | collective-permute-done | bytes 655392 | tf_op jit(solution)/shard_map/ppermute | solution.py:44
  41.4 0.0 collective-permute-start.10
  41.4 0.5 collective-permute-start.11
  42.6 0.1 stack.23.place
  42.7 1.7 %collective-permute-done.11.refs_7_ = bf16[192,1280]{1,0:T(8,128)(2,1)} collective-permute-done((bf16[192,1280]{1,0:T(8,128)(2,1)}, bf16[192,1280]{1,0:T(8,128)(2,1)}, u32[]{:S(2)}, u32[]{:S(2)}) %collective-permute-start.11) | collective-permute-done | bytes 491552 | tf_op jit(solution)/shard_map/ppermute | solution.py:48
  44.4 0.0 collective-permute-done.8.refs_3_
  44.4 0.0 collective-permute-done.7.refs_2_
  44.4 3.7 %collective-permute-done.6.refs_1_ = bf16[256,1280]{1,0:T(8,128)(2,1)} collective-permute-done((bf16[256,1280]{1,0:T(8,128)(2,1)S(1)}, bf16[256,1280]{1,0:T(8,128)(2,1)}, u32[]{:S(2)}, u32[]{:S(2)}) %collective-permute-start.6) | collective-permute-done | bytes 655392 | tf_op jit(solution)/shard_map/ppermute | solution.py:35
  48.1 0.0 collective-permute-done.10.refs_6_
  48.1 5.8 %shard_map.60 = (f32[1024,1024]{1,0:T(8,128)S(1)}, f32[16,128]{1,0:T(8,128)S(1)}, f32[16,128]{1,0:T(8,128)S(1)}, f32[24,128]{1,0:T(8,128)S(1)}, f32[8,128]{1,0:T...) custom-call(s32[5]{0:T(128)S(1)} %stack.23.place, f32[1]{0:T(128)S(6)} %copy.6.scale, ...), custom_call_target="tpu_custom_call" | custom-call | tf_op jit(solution)/shard_map/pallas_call | solution.py:191
  53.9 0.3 collective-permute-start.12
  54.2 1.2 collective-permute-done.12.got
  55.4 0.6 shard_map.61
  56.0 12.7 %all_to_all.5.got = f32[16,24,128]{2,1,0:T(8,128)S(1)} all-to-all(f32[16,24,128]{2,1,0:T(8,128)S(1)} %shard_map.61), channel_id=1, replica_groups={{0,1,2,3,4,5,6,7,8,9,10,11,12,13,14,15},{64,65,66,67,68,69,70,71,72,73,..., dimensions={0} | all-to-all | bytes 393216 | tf_op jit(solution)/shard_map/all_to_all | solution.py:63
  68.8 0.7 shard_map.62
  69.5 1.6 %collective-permute-start.13 = (f32[24,128]{1,0:T(8,128)S(1)}, f32[24,128]{1,0:T(8,128)S(1)}, u32[]{:S(2)}, u32[]{:S(2)}) collective-permute-start(f32[24,128]{1,0:T(8,128)S(1)} %get-tuple-element.51), channel_id=1, source_target_pairs={{0,32},{32,0},{1,33},{33,1},{2,34},{34,2},{3,35},{35,3},{4,36},{36... | collective-permute-start | bytes 36872 | tf_op jit(solution)/shard_map/ppermute | solution.py:48
  71.1 0.8 collective-permute-done.13.other
  71.9 3.6 %shard_map.63 = (bf16[1024,1024]{1,0:T(8,128)(2,1)S(1)}, bf16[256,1280]{1,0:T(8,128)(2,1)S(1)}, bf16[192,1280]{1,0:T(8,128)(2,1)S(1)}, bf16[32,1280]{1,0:T(8,128)(2,1)S(1)}) custom-call(s32[5]{0:T(128)S(1)} %stack.23.place, f32[1]{0:T(128)S(6)} %copy.6.scale, f32[1024,1024]{1,0:T(8,128)S(1)} %get-tuple-element.45.logits, ...), custom_call_target="tpu_custom_call" | custom-call | tf_op jit(solution)/shard_map/pallas_call | solution.py:357
  75.5 0.4 collective-permute-start.14
  75.9 0.2 collective-permute-start.15
  76.1 1.9 %shard_map.65 = (bf16[256,1280]{1,0:T(8,128)(2,1)S(1)}, bf16[64,1280]{1,0:T(8,128)(2,1)S(1)}) custom-call(f32[1]{0:T(128)S(6)} %copy.6.scale, bf16[1024,1024]{1,0:T(8,128)(2,1)S(1)} %get-tuple-element.53.weights, bf16[1024,1280]{1,0:T(8,128)(2,1)S(1)} %get-tuple-element.52.images), custom_call_target="tpu_custom_call" | custom-call | tf_op jit(solution)/shard_map/pallas_call | solution.py:381
  78.0 0.4 collective-permute-done.15.refs_3_.refs_1_
  78.4 0.0 collective-permute-done.14.refs_1_
  78.4 0.2 shard_map.66.after
  78.6 1.1 collective-permute-start.22
  79.6 2.2 %shard_map.67 = (bf16[272,1280]{1,0:T(8,128)(2,1)S(1)}, bf16[272,1280]{1,0:T(8,128)(2,1)S(1)}, bf16[272,1280]{1,0:T(8,128)(2,1)S(1)}) custom-call(f32[1]{0:T(128)S(6)} %copy.6.scale, bf16[336,1280]{1,0:T(8,128)(2,1)S(1)} %shard_map.66.after, bf16[32,1280]{1,0:T(8,128)(2,1)S(1)} %get-tuple-element.60.refs_4_.digits.refs_3_.refs_7_, ...), custom_call_target="tpu_custom_call" | custom-call | tf_op jit(solution)/shard_map/pallas_call | solution.py:397
  81.8 0.6 collective-permute-start.16
  82.5 2.9 %collective-permute-start.17 = (bf16[272,1280]{1,0:T(8,128)(2,1)S(1)}, bf16[272,1280]{1,0:T(8,128)(2,1)S(1)}, u32[]{:S(2)}, u32[]{:S(2)}) collective-permute-start(bf16[272,1280]{1,0:T(8,128)(2,1)S(1)} %get-tuple-element.62), channel_id=1, source_target_pairs={{0,12},{1,13},{2,14},{3,15},{4,0},{5,1},{6,2},{7,3},{8,4},{9,5},{1... | collective-permute-start | bytes 2088968 | tf_op jit(solution)/shard_map/ppermute | solution.py:35
  85.4 0.0 collective-permute-start.18
  85.4 1.6 %shard_map.64 = (bf16[256,1280]{1,0:T(8,128)(2,1)S(1)}, bf16[256,1280]{1,0:T(8,128)(2,1)S(1)}) custom-call(f32[1]{0:T(128)S(6)} %copy.6.scale, bf16[1024,1024]{1,0:T(8,128)(2,1)S(1)} %get-tuple-element.53.weights, bf16[1024,1280]{1,0:T(8,128)(2,1)S(1)} %get-tuple-element.52.images, bf16[1024,1280]{1,0:T(8,128)(2,1)S(1)} %get-tuple-element.54.texts), custom_call_target="tpu_custom_call" | custom-call | tf_op jit(solution)/shard_map/pallas_call | solution.py:412
  87.0 15.1 %collective-permute-done.22.refs_2_ = bf16[336,1280]{1,0:T(8,128)(2,1)S(1)} collective-permute-done((bf16[336,1280]{1,0:T(8,128)(2,1)S(1)}, bf16[336,1280]{1,0:T(8,128)(2,1)S(1)}, u32[]{:S(2)}, u32[]{:S(2)}) %collective-permute-start.22) | collective-permute-done | bytes 860192 | tf_op jit(solution)/shard_map/ppermute | solution.py:44
  102.0 0.2 shard_map.69
  102.2 0.1 collective-permute-start.23
  102.3 0.0 collective-permute-done.16.refs_1_
  102.4 0.4 shard_map.68
  102.8 2.4 %collective-permute-start.19 = (bf16[80,1280]{1,0:T(8,128)(2,1)S(1)}, bf16[80,1280]{1,0:T(8,128)(2,1)S(1)}, u32[]{:S(2)}, u32[]{:S(2)}) collective-permute-start(bf16[80,1280]{1,0:T(8,128)(2,1)S(1)} %get-tuple-element.65), channel_id=1, source_target_pairs={{0,2},{1,3},{2,0},{3,1},{4,6},{5,7},{6,4},{7,5},{8,10},{9,11},{10,... | collective-permute-start | bytes 614408 | tf_op jit(solution)/shard_map/ppermute | solution.py:35
  105.2 1.1 collective-permute-start.20
  106.3 0.9 collective-permute-start.21
  107.2 0.7 collective-permute-start.25
  107.9 1.9 %collective-permute-done.23.refs_1_ = bf16[144,1280]{1,0:T(8,128)(2,1)S(1)} collective-permute-done((bf16[144,1280]{1,0:T(8,128)(2,1)S(1)}, bf16[144,1280]{1,0:T(8,128)(2,1)S(1)}, u32[]{:S(2)}, u32[]{:S(2)}) %collective-permute-start.23) | collective-permute-done | bytes 368672 | tf_op jit(solution)/shard_map/ppermute | solution.py:44
  109.8 0.1 shard_map.70
  109.9 0.1 collective-permute-start.24
  110.0 0.1 collective-permute-done.19.refs_1_
  110.1 1.6 %collective-permute-done.20.refs_2_ = bf16[80,1280]{1,0:T(8,128)(2,1)S(1)} collective-permute-done((bf16[80,1280]{1,0:T(8,128)(2,1)S(1)}, bf16[80,1280]{1,0:T(8,128)(2,1)S(1)}, u32[]{:S(2)}, u32[]{:S(2)}) %collective-permute-start.20) | collective-permute-done | bytes 204832 | tf_op jit(solution)/shard_map/ppermute | solution.py:35
  111.7 1.6 %collective-permute-done.21.refs_3_ = bf16[80,1280]{1,0:T(8,128)(2,1)S(1)} collective-permute-done((bf16[80,1280]{1,0:T(8,128)(2,1)S(1)}, bf16[80,1280]{1,0:T(8,128)(2,1)S(1)}, u32[]{:S(2)}, u32[]{:S(2)}) %collective-permute-start.21) | collective-permute-done | bytes 204832 | tf_op jit(solution)/shard_map/ppermute | solution.py:35
  113.3 3.0 %collective-permute-done.25.refs_6_ = bf16[80,1280]{1,0:T(8,128)(2,1)S(1)} collective-permute-done((bf16[80,1280]{1,0:T(8,128)(2,1)S(1)}, bf16[80,1280]{1,0:T(8,128)(2,1)S(1)}, u32[]{:S(2)}, u32[]{:S(2)}) %collective-permute-start.25) | collective-permute-done | bytes 204832 | tf_op jit(solution)/shard_map/ppermute | solution.py:44
  116.3 0.8 shard_map.71
  (8 shorter events, 0.0 us)
Async XLA Ops:
  0.6 1.7 %collective-permute-start = (bf16[64,1280]{1,0:T(8,128)(2,1)}, bf16[64,1280]{1,0:T(8,128)(2,1)S(1)}, u32[]{:S(2)}, u32[]{:S(2)}) collective-permute-start(bf16[64,1280]{1,0:T(8,128)(2,1)} %refs_0_.1), channel_id=1, source_target_pairs={{0,32},{32,0},{1,33},{33,1},{2,34},{34,2},{3,35},{35,3},{4,36},{36... | collective-permute-start | bytes 491528 | tf_op jit(solution)/shard_map/ppermute | solution.py:48
  2.3 0.9 copy-start
  3.2 0.9 copy-start.1
  4.2 18.9 %collective-permute-start.4 = (bf16[128,1280]{1,0:T(8,128)(2,1)S(1)}, bf16[128,1280]{1,0:T(8,128)(2,1)S(1)}, u32[]{:S(2)}, u32[]{:S(2)}) collective-permute-start(bf16[128,1280]{1,0:T(8,128)(2,1)S(1)} %get-tuple-element.41.refs_4_), channel_id=1, source_target_pairs={{0,208},{64,0},{128,64},{192,128},{16,192},{80,16},{144,80},{208,1... | collective-permute-start | bytes 983048 | tf_op jit(solution)/shard_map/ppermute | solution.py:44
  6.1 17.0 %collective-permute-start.5 = (bf16[64,1280]{1,0:T(8,128)(2,1)S(1)}, bf16[64,1280]{1,0:T(8,128)(2,1)S(1)}, u32[]{:S(2)}, u32[]{:S(2)}) collective-permute-start(bf16[64,1280]{1,0:T(8,128)(2,1)S(1)} %copy-done.1), channel_id=1, source_target_pairs={{0,16},{64,80},{128,144},{192,208},{16,0},{80,64},{144,128},{208,1... | collective-permute-start | bytes 491528 | tf_op jit(solution)/shard_map/ppermute | solution.py:44
  11.6 11.5 %collective-permute-start.3 = (bf16[64,1280]{1,0:T(8,128)(2,1)S(1)}, bf16[64,1280]{1,0:T(8,128)(2,1)S(1)}, u32[]{:S(2)}, u32[]{:S(2)}) collective-permute-start(bf16[64,1280]{1,0:T(8,128)(2,1)S(1)} %get-tuple-element.40.refs_0_), channel_id=1, source_target_pairs={{0,3},{1,0},{2,1},{3,2},{4,7},{5,4},{6,5},{7,6},{8,11},{9,8},{10,9... | collective-permute-start | bytes 491528 | tf_op jit(solution)/shard_map/ppermute | solution.py:35
  14.3 8.8 %collective-permute-start.2 = (bf16[64,1280]{1,0:T(8,128)(2,1)S(1)}, bf16[64,1280]{1,0:T(8,128)(2,1)S(1)}, u32[]{:S(2)}, u32[]{:S(2)}) collective-permute-start(bf16[64,1280]{1,0:T(8,128)(2,1)S(1)} %get-tuple-element.40.refs_0_), channel_id=1, source_target_pairs={{0,2},{1,3},{2,0},{3,1},{4,6},{5,7},{6,4},{7,5},{8,10},{9,11},{10,... | collective-permute-start | bytes 491528 | tf_op jit(solution)/shard_map/ppermute | solution.py:35
  15.1 8.0 %collective-permute-start.1 = (bf16[64,1280]{1,0:T(8,128)(2,1)S(1)}, bf16[64,1280]{1,0:T(8,128)(2,1)S(1)}, u32[]{:S(2)}, u32[]{:S(2)}) collective-permute-start(bf16[64,1280]{1,0:T(8,128)(2,1)S(1)} %get-tuple-element.40.refs_0_), channel_id=1, source_target_pairs={{0,1},{1,2},{2,3},{3,0},{4,5},{5,6},{6,7},{7,4},{8,9},{9,10},{10,1... | collective-permute-start | bytes 491528 | tf_op jit(solution)/shard_map/ppermute | solution.py:35
  24.0 17.4 %collective-permute-start.9 = (bf16[256,1280]{1,0:T(8,128)(2,1)S(1)}, bf16[256,1280]{1,0:T(8,128)(2,1)S(1)}, u32[]{:S(2)}, u32[]{:S(2)}) collective-permute-start(bf16[256,1280]{1,0:T(8,128)(2,1)S(1)} %get-tuple-element.43.refs_4_), channel_id=1, source_target_pairs={{0,144},{64,208},{128,0},{192,64},{16,128},{80,192},{144,16},{208,... | collective-permute-start | bytes 1966088 | tf_op jit(solution)/shard_map/ppermute | solution.py:44
  25.9 18.5 %collective-permute-start.8 = (bf16[256,1280]{1,0:T(8,128)(2,1)S(1)}, bf16[256,1280]{1,0:T(8,128)(2,1)S(1)}, u32[]{:S(2)}, u32[]{:S(2)}) collective-permute-start(bf16[256,1280]{1,0:T(8,128)(2,1)S(1)} %get-tuple-element.42.refs_0_), channel_id=1, source_target_pairs={{0,12},{1,13},{2,14},{3,15},{4,0},{5,1},{6,2},{7,3},{8,4},{9,5},{1... | collective-permute-start | bytes 1966088 | tf_op jit(solution)/shard_map/ppermute | solution.py:35
  28.9 15.5 %collective-permute-start.7 = (bf16[256,1280]{1,0:T(8,128)(2,1)S(1)}, bf16[256,1280]{1,0:T(8,128)(2,1)S(1)}, u32[]{:S(2)}, u32[]{:S(2)}) collective-permute-start(bf16[256,1280]{1,0:T(8,128)(2,1)S(1)} %get-tuple-element.42.refs_0_), channel_id=1, source_target_pairs={{0,8},{1,9},{2,10},{3,11},{4,12},{5,13},{6,14},{7,15},{8,0},{9,1},... | collective-permute-start | bytes 1966088 | tf_op jit(solution)/shard_map/ppermute | solution.py:35
  29.5 18.6 %collective-permute-start.6 = (bf16[256,1280]{1,0:T(8,128)(2,1)S(1)}, bf16[256,1280]{1,0:T(8,128)(2,1)}, u32[]{:S(2)}, u32[]{:S(2)}) collective-permute-start(bf16[256,1280]{1,0:T(8,128)(2,1)S(1)} %get-tuple-element.42.refs_0_), channel_id=1, source_target_pairs={{0,4},{1,5},{2,6},{3,7},{4,8},{5,9},{6,10},{7,11},{8,12},{9,13},{1... | collective-permute-start | bytes 1966088 | tf_op jit(solution)/shard_map/ppermute | solution.py:35
  41.4 6.7 %collective-permute-start.10 = (bf16[256,1280]{1,0:T(8,128)(2,1)S(1)}, bf16[256,1280]{1,0:T(8,128)(2,1)}, u32[]{:S(2)}, u32[]{:S(2)}) collective-permute-start(bf16[256,1280]{1,0:T(8,128)(2,1)S(1)} %collective-permute-done.9.refs_5_), channel_id=1, source_target_pairs={{0,32},{32,0},{1,33},{33,1},{2,34},{34,2},{3,35},{35,3},{4,36},{36... | collective-permute-start | bytes 1966088 | tf_op jit(solution)/shard_map/ppermute | solution.py:48
  41.4 2.9 %collective-permute-start.11 = (bf16[192,1280]{1,0:T(8,128)(2,1)}, bf16[192,1280]{1,0:T(8,128)(2,1)}, u32[]{:S(2)}, u32[]{:S(2)}) collective-permute-start(bf16[192,1280]{1,0:T(8,128)(2,1)} %get-tuple-element.44), channel_id=1, source_target_pairs={{0,32},{32,0},{1,33},{33,1},{2,34},{34,2},{3,35},{35,3},{4,36},{36... | collective-permute-start | bytes 1474568 | tf_op jit(solution)/shard_map/ppermute | solution.py:48
  53.9 1.4 %collective-permute-start.12 = (f32[24,128]{1,0:T(8,128)S(1)}, f32[24,128]{1,0:T(8,128)S(1)}, u32[]{:S(2)}, u32[]{:S(2)}) collective-permute-start(f32[24,128]{1,0:T(8,128)S(1)} %get-tuple-element.49), channel_id=1, source_target_pairs={{0,32},{32,0},{1,33},{33,1},{2,34},{34,2},{3,35},{35,3},{4,36},{36... | collective-permute-start | bytes 36872 | tf_op jit(solution)/shard_map/ppermute | solution.py:48
  69.5 2.4 %collective-permute-start.13 = (f32[24,128]{1,0:T(8,128)S(1)}, f32[24,128]{1,0:T(8,128)S(1)}, u32[]{:S(2)}, u32[]{:S(2)}) collective-permute-start(f32[24,128]{1,0:T(8,128)S(1)} %get-tuple-element.51), channel_id=1, source_target_pairs={{0,32},{32,0},{1,33},{33,1},{2,34},{34,2},{3,35},{35,3},{4,36},{36... | collective-permute-start | bytes 36872 | tf_op jit(solution)/shard_map/ppermute | solution.py:48
  75.5 2.9 %collective-permute-start.14 = (bf16[256,1280]{1,0:T(8,128)(2,1)S(1)}, bf16[256,1280]{1,0:T(8,128)(2,1)S(1)}, u32[]{:S(2)}, u32[]{:S(2)}) collective-permute-start(bf16[256,1280]{1,0:T(8,128)(2,1)S(1)} %get-tuple-element.57), channel_id=1, source_target_pairs={{0,32},{32,0},{1,33},{33,1},{2,34},{34,2},{3,35},{35,3},{4,36},{36... | collective-permute-start | bytes 1966088 | tf_op jit(solution)/shard_map/ppermute | solution.py:48
  75.9 2.5 %collective-permute-start.15 = (bf16[192,1280]{1,0:T(8,128)(2,1)S(1)}, bf16[192,1280]{1,0:T(8,128)(2,1)S(1)}, u32[]{:S(2)}, u32[]{:S(2)}) collective-permute-start(bf16[192,1280]{1,0:T(8,128)(2,1)S(1)} %get-tuple-element.59), channel_id=1, source_target_pairs={{0,32},{32,0},{1,33},{33,1},{2,34},{34,2},{3,35},{35,3},{4,36},{36... | collective-permute-start | bytes 1474568 | tf_op jit(solution)/shard_map/ppermute | solution.py:48
  78.6 23.5 %collective-permute-start.22 = (bf16[336,1280]{1,0:T(8,128)(2,1)S(1)}, bf16[336,1280]{1,0:T(8,128)(2,1)S(1)}, u32[]{:S(2)}, u32[]{:S(2)}) collective-permute-start(bf16[336,1280]{1,0:T(8,128)(2,1)S(1)} %shard_map.66.after), channel_id=1, source_target_pairs={{0,128},{64,192},{128,16},{192,80},{16,144},{80,208},{144,0},{208,... | collective-permute-start | bytes 2580488 | tf_op jit(solution)/shard_map/ppermute | solution.py:44
  81.8 20.5 %collective-permute-start.16 = (bf16[272,1280]{1,0:T(8,128)(2,1)S(1)}, bf16[272,1280]{1,0:T(8,128)(2,1)S(1)}, u32[]{:S(2)}, u32[]{:S(2)}) collective-permute-start(bf16[272,1280]{1,0:T(8,128)(2,1)S(1)} %get-tuple-element.61), channel_id=1, source_target_pairs={{0,8},{1,9},{2,10},{3,11},{4,12},{5,13},{6,14},{7,15},{8,0},{9,1},... | collective-permute-start | bytes 2088968 | tf_op jit(solution)/shard_map/ppermute | solution.py:35
  82.5 19.9 %collective-permute-start.17 = (bf16[272,1280]{1,0:T(8,128)(2,1)S(1)}, bf16[272,1280]{1,0:T(8,128)(2,1)S(1)}, u32[]{:S(2)}, u32[]{:S(2)}) collective-permute-start(bf16[272,1280]{1,0:T(8,128)(2,1)S(1)} %get-tuple-element.62), channel_id=1, source_target_pairs={{0,12},{1,13},{2,14},{3,15},{4,0},{5,1},{6,2},{7,3},{8,4},{9,5},{1... | collective-permute-start | bytes 2088968 | tf_op jit(solution)/shard_map/ppermute | solution.py:35
  85.4 17.0 %collective-permute-start.18 = (bf16[272,1280]{1,0:T(8,128)(2,1)S(1)}, bf16[272,1280]{1,0:T(8,128)(2,1)S(1)}, u32[]{:S(2)}, u32[]{:S(2)}) collective-permute-start(bf16[272,1280]{1,0:T(8,128)(2,1)S(1)} %get-tuple-element.63), channel_id=1, source_target_pairs={{0,4},{1,5},{2,6},{3,7},{4,8},{5,9},{6,10},{7,11},{8,12},{9,13},{1... | collective-permute-start | bytes 2088968 | tf_op jit(solution)/shard_map/ppermute | solution.py:35
  102.2 7.6 %collective-permute-start.23 = (bf16[144,1280]{1,0:T(8,128)(2,1)S(1)}, bf16[144,1280]{1,0:T(8,128)(2,1)S(1)}, u32[]{:S(2)}, u32[]{:S(2)}) collective-permute-start(bf16[144,1280]{1,0:T(8,128)(2,1)S(1)} %get-tuple-element.70), channel_id=1, source_target_pairs={{0,64},{64,128},{128,192},{192,16},{16,80},{80,144},{144,208},{208... | collective-permute-start | bytes 1105928 | tf_op jit(solution)/shard_map/ppermute | solution.py:44
  102.8 7.3 %collective-permute-start.19 = (bf16[80,1280]{1,0:T(8,128)(2,1)S(1)}, bf16[80,1280]{1,0:T(8,128)(2,1)S(1)}, u32[]{:S(2)}, u32[]{:S(2)}) collective-permute-start(bf16[80,1280]{1,0:T(8,128)(2,1)S(1)} %get-tuple-element.65), channel_id=1, source_target_pairs={{0,2},{1,3},{2,0},{3,1},{4,6},{5,7},{6,4},{7,5},{8,10},{9,11},{10,... | collective-permute-start | bytes 614408 | tf_op jit(solution)/shard_map/ppermute | solution.py:35
  105.2 6.5 %collective-permute-start.20 = (bf16[80,1280]{1,0:T(8,128)(2,1)S(1)}, bf16[80,1280]{1,0:T(8,128)(2,1)S(1)}, u32[]{:S(2)}, u32[]{:S(2)}) collective-permute-start(bf16[80,1280]{1,0:T(8,128)(2,1)S(1)} %get-tuple-element.66), channel_id=1, source_target_pairs={{0,3},{1,0},{2,1},{3,2},{4,7},{5,4},{6,5},{7,6},{8,11},{9,8},{10,9... | collective-permute-start | bytes 614408 | tf_op jit(solution)/shard_map/ppermute | solution.py:35
  106.3 7.0 %collective-permute-start.21 = (bf16[80,1280]{1,0:T(8,128)(2,1)S(1)}, bf16[80,1280]{1,0:T(8,128)(2,1)S(1)}, u32[]{:S(2)}, u32[]{:S(2)}) collective-permute-start(bf16[80,1280]{1,0:T(8,128)(2,1)S(1)} %get-tuple-element.67), channel_id=1, source_target_pairs={{0,1},{1,2},{2,3},{3,0},{4,5},{5,6},{6,7},{7,4},{8,9},{9,10},{10,1... | collective-permute-start | bytes 614408 | tf_op jit(solution)/shard_map/ppermute | solution.py:35
  107.2 9.1 %collective-permute-start.25 = (bf16[80,1280]{1,0:T(8,128)(2,1)S(1)}, bf16[80,1280]{1,0:T(8,128)(2,1)S(1)}, u32[]{:S(2)}, u32[]{:S(2)}) collective-permute-start(bf16[80,1280]{1,0:T(8,128)(2,1)S(1)} %get-tuple-element.73), channel_id=1, source_target_pairs={{0,128},{64,192},{128,16},{192,80},{16,144},{80,208},{144,0},{208,... | collective-permute-start | bytes 614408 | tf_op jit(solution)/shard_map/ppermute | solution.py:44
  109.9 6.4 %collective-permute-start.24 = (bf16[80,1280]{1,0:T(8,128)(2,1)S(1)}, bf16[80,1280]{1,0:T(8,128)(2,1)S(1)}, u32[]{:S(2)}, u32[]{:S(2)}) collective-permute-start(bf16[80,1280]{1,0:T(8,128)(2,1)S(1)} %get-tuple-element.72), channel_id=1, source_target_pairs={{0,32},{32,0},{1,33},{33,1},{2,34},{34,2},{3,35},{35,3},{4,36},{36... | collective-permute-start | bytes 614408 | tf_op jit(solution)/shard_map/ppermute | solution.py:48

commit v9 on v8

--- a/solution.py
+++ b/solution.py
@@ -95,6 +95,7 @@
     return out
 
 
+PLANE_ORDER = (0, 1, 3, 2)
 PART = jax.ShapeDtypeStruct((CHUNK, EMBED), BF16)
 ALL = jax.ShapeDtypeStruct((BLOCK, EMBED), BF16)
 
@@ -134,7 +135,7 @@
 
 
 def logits_body(place, scale, *refs):
-    images, texts = refs[:4], refs[4:7]
+    images, texts = [refs[i] for i in PLANE_ORDER], refs[4:7]
     logits, row_out, col_out, message, match_out, all_images, all_texts = refs[9:16]
     row_wide = refs[16]
     all_texts[3 * CHUNK : BLOCK - ROWS, :] = refs[7][...]
@@ -448,11 +449,11 @@
 
 
 def last_body(*refs):
-    digits, image_out, text_out, loss_out = refs[7:]
+    digits, image_out, text_out, loss_out = refs[6:]
     add_rows(refs, ROWS, [(i, 0) for i in range(4)], image_out, 0)
-    add_rows(refs, ROWS, [(4, 0), (5, 0), (6, 0)], text_out, 0)
+    add_rows(refs, ROWS, [(4, 0), (5, 0)], text_out, 0)
     total = -digits[:TAIL, :128].astype(F32)
-    for r in refs[:7]:
+    for r in refs[:6]:
         total += r[ROWS : ROWS + TAIL, :128].astype(F32)
     loss_out[...] = value_of(total)[:, 0:1] * (LN2 / (2.0 * ROWS * 256))
 
@@ -462,7 +463,7 @@
     return pl.pallas_call(
         last_body,
         out_shape=(grad, grad, jax.ShapeDtypeStruct((1, 1), F32)),
-        in_specs=[VMEM] * 8,
+        in_specs=[VMEM] * 7,
         out_specs=(VMEM,) * 3,
         compiler_params=PARAMS,
     )(*shards, *texts, digits)
@@ -481,7 +482,7 @@
         ((5, 128), (6, 64)),
     )
     text_1 = z_shift(text_0, -2)
-    near = [own] + [plane_shift(own, k, False) for k in (1, 2, 3)]
+    near = [own] + [plane_shift(own, k, False) for k in PLANE_ORDER[1:]]
     logits, row_part, col_part, message, matched, images, texts = logits_call(
         place, logit_scale, near, [text_0, text_1, core_swap(text_1), core_swap(side), next_4]
     )
@@ -511,11 +512,9 @@
         ((80, ((2, 256),)),),
     )
     next_1, next_4 = z_shift(next_1, 1), z_shift(next_4, 2)
-    rows_tail = (TAIL, ((0, 128), (1, 128)))
-    mine, other = sums(
-        [mine, next_1],
-        ((64, ((0, 0), (1, 0))), rows_tail),
-        ((64, ((0, 64), (1, 64))), rows_tail),
+    (other,) = sums([mine, next_1], ((64, ((0, 64), (1, 64))), (TAIL, ((0, 128), (1, 128)))))
+    (mine,) = sums(
+        [mine, next_1, next_4], ((64, ((0, 0), (1, 0), (2, 0))), (TAIL, ((0, 128), (1, 128), (2, 64))))
     )
 
     cols_tail = (TAIL, ((1, 256), (2, 256), (3, 256), (4, 16)))
@@ -524,7 +523,7 @@
         *[((64, [(i, 64 * k) for i in range(4)]), cols_tail) for k in range(4)],
     )
     shards = [pieces[0]] + [plane_shift(pieces[k], -k, True) for k in (2, 1, 3)]
-    image_grad, text_grad, mean_loss = last_call(shards, [mine, core_swap(other), next_4], digits)
+    image_grad, text_grad, mean_loss = last_call(shards, [mine, core_swap(other)], digits)
     return mean_loss.reshape(1), image_grad, text_grad
 
 

time: 119 us -> 118 us (level)
  waiting for transfers between devices: 50.7 us -> 46.6 us
  blocking collectives: 12.7 us -> 14.9 us
    ppermute x12, waiting for transfers between devices: 7.03 us -> 1.03 us  [plane_shift(): return lax.ppermute(v, ('core', 'zh', 'y', 'x'), pairs)]
    all_to_all x1, blocking collectives: 12.7 us -> 14.9 us  [exchange(): return lax.all_to_all(v, AXES, 0, 0, axis_index_groups=groups)]
    ppermute x6, waiting for transfers between devices: 38 us -> 39.9 us  [z_shift(): return lax.ppermute(v, ('zl', 'core', 'zh'), pairs)]
  transfers between devices with their start and end apart: 26 -> 26, of which waited for: 14 -> 11; matrix products, arithmetic and copies ran while one was open for 0% -> 0% of each run, Pallas kernels for 5% -> 6%
where the time goes in v9:
time: 118 us; the launch traced here: 116 us
  waiting for transfers between devices  46.6 us (39%)
  starting transfers between devices  32.3 us (27%)
  Pallas kernels  19.1 us (16%)
  blocking collectives  14.9 us (13%)
  local copies, waits for them, and re-layouts  1.92 us (2%)
  between operations  1.47 us (1%)
    ppermute x6, waiting for transfers between devices, z_shift(): return lax.ppermute(v, ('zl', 'core', 'zh'), pairs)  39.9 us
    ppermute x12, starting transfers between devices, plane_shift(): return lax.ppermute(v, ('core', 'zh', 'y', 'x'), pairs)  17.5 us
    all_to_all x1, blocking collectives, exchange(): return lax.all_to_all(v, AXES, 0, 0, axis_index_groups=groups)  14.9 us
    ppermute x6, starting transfers between devices, z_shift(): return lax.ppermute(v, ('zl', 'core', 'zh'), pairs)  11.1 us
    pallas_call x1, Pallas kernels, logits_call(): pl.pallas_call(logits_body, out_shape=(jax.ShapeDtypeStruct((BLOCK, BLOCK...  5.81 us
    ppermute x8, waiting for transfers between devices, core_swap(): return lax.ppermute(v, 'core', [(0, 1), (1, 0)])  5.68 us
    ppermute x8, starting transfers between devices, core_swap(): return lax.ppermute(v, 'core', [(0, 1), (1, 0)])  3.7 us
    pallas_call x1, Pallas kernels, weights_call(): pl.pallas_call(weights_body, out_shape=(jax.ShapeDtypeStruct((BLOCK, BLOC...  3.58 us
  transfers between devices with their start and end apart: 26, of which 11 were waited for; matrix products, arithmetic and copies ran while one was open for 0% of the time, Pallas kernels for 6%

profile of v9, /device:TPU:32, one launch (start us, length us, event | category | flops | bytes accessed | tf_op | source)
XLA Modules:
  0.0 116.3 jit_solution(2228097524557017321)
XLA Ops:
  0.6 0.1 collective-permute-start
  0.7 1.6 %collective-permute-done.refs_1_ = bf16[64,1280]{1,0:T(8,128)(2,1)S(1)} collective-permute-done((bf16[64,1280]{1,0:T(8,128)(2,1)}, bf16[64,1280]{1,0:T(8,128)(2,1)S(1)}, u32[]{:S(2)}, u32[]{:S(2)}) %collective-permute-start) | collective-permute-done | bytes 163872 | tf_op jit(solution)/shard_map/ppermute | solution.py:48
  2.3 0.9 copy-done
  3.2 0.9 copy-done.1
  4.2 1.9 %collective-permute-start.4 = (bf16[128,1280]{1,0:T(8,128)(2,1)S(1)}, bf16[128,1280]{1,0:T(8,128)(2,1)S(1)}, u32[]{:S(2)}, u32[]{:S(2)}) collective-permute-start(bf16[128,1280]{1,0:T(8,128)(2,1)S(1)} %get-tuple-element.39.refs_4_), channel_id=1, source_target_pairs={{0,208},{64,0},{128,64},{192,128},{16,192},{80,16},{144,80},{208,1... | collective-permute-start | bytes 983048 | tf_op jit(solution)/shard_map/ppermute | solution.py:44
  6.1 5.5 %collective-permute-start.5 = (bf16[64,1280]{1,0:T(8,128)(2,1)S(1)}, bf16[64,1280]{1,0:T(8,128)(2,1)S(1)}, u32[]{:S(2)}, u32[]{:S(2)}) collective-permute-start(bf16[64,1280]{1,0:T(8,128)(2,1)S(1)} %copy-done.1), channel_id=1, source_target_pairs={{0,16},{64,80},{128,144},{192,208},{16,0},{80,64},{144,128},{208,1... | collective-permute-start | bytes 491528 | tf_op jit(solution)/shard_map/ppermute | solution.py:44
  11.6 2.8 %collective-permute-start.3 = (bf16[64,1280]{1,0:T(8,128)(2,1)S(1)}, bf16[64,1280]{1,0:T(8,128)(2,1)S(1)}, u32[]{:S(2)}, u32[]{:S(2)}) collective-permute-start(bf16[64,1280]{1,0:T(8,128)(2,1)S(1)} %get-tuple-element.38.refs_0_), channel_id=1, source_target_pairs={{0,3},{1,0},{2,1},{3,2},{4,7},{5,4},{6,5},{7,6},{8,11},{9,8},{10,9... | collective-permute-start | bytes 491528 | tf_op jit(solution)/shard_map/ppermute | solution.py:35
  14.3 0.8 collective-permute-start.2
  15.1 0.9 collective-permute-start.1
  16.0 7.1 %collective-permute-done.5.refs_6_.refs_8_ = bf16[64,1280]{1,0:T(8,128)(2,1)S(1)} collective-permute-done((bf16[64,1280]{1,0:T(8,128)(2,1)S(1)}, bf16[64,1280]{1,0:T(8,128)(2,1)S(1)}, u32[]{:S(2)}, u32[]{:S(2)}) %collective-permute-start.5) | collective-permute-done | bytes 163872 | tf_op jit(solution)/shard_map/ppermute | solution.py:44
  23.1 0.0 collective-permute-done.3.refs_3_
  23.1 0.0 collective-permute-done.2.refs_2_
  23.1 0.0 collective-permute-done.1.refs_1_
  23.1 0.0 collective-permute-done.4.refs_5_
  23.1 0.9 shard_map.59
  24.0 1.9 %collective-permute-start.9 = (bf16[256,1280]{1,0:T(8,128)(2,1)S(1)}, bf16[256,1280]{1,0:T(8,128)(2,1)S(1)}, u32[]{:S(2)}, u32[]{:S(2)}) collective-permute-start(bf16[256,1280]{1,0:T(8,128)(2,1)S(1)} %get-tuple-element.41.refs_4_), channel_id=1, source_target_pairs={{0,144},{64,208},{128,0},{192,64},{16,128},{80,192},{144,16},{208,... | collective-permute-start | bytes 1966088 | tf_op jit(solution)/shard_map/ppermute | solution.py:44
  25.9 3.2 %collective-permute-start.8 = (bf16[256,1280]{1,0:T(8,128)(2,1)S(1)}, bf16[256,1280]{1,0:T(8,128)(2,1)S(1)}, u32[]{:S(2)}, u32[]{:S(2)}) collective-permute-start(bf16[256,1280]{1,0:T(8,128)(2,1)S(1)} %get-tuple-element.40.refs_0_), channel_id=1, source_target_pairs={{0,8},{1,9},{2,10},{3,11},{4,12},{5,13},{6,14},{7,15},{8,0},{9,1},... | collective-permute-start | bytes 1966088 | tf_op jit(solution)/shard_map/ppermute | solution.py:35
  29.1 1.1 collective-permute-start.7
  30.2 1.0 collective-permute-start.6
  31.1 10.3 %collective-permute-done.9.refs_5_ = bf16[256,1280]{1,0:T(8,128)(2,1)S(1)} collective-permute-done((bf16[256,1280]{1,0:T(8,128)(2,1)S(1)}, bf16[256,1280]{1,0:T(8,128)(2,1)S(1)}, u32[]{:S(2)}, u32[]{:S(2)}) %collective-permute-start.9) | collective-permute-done | bytes 655392 | tf_op jit(solution)/shard_map/ppermute | solution.py:44
  41.5 0.0 collective-permute-start.10
  41.5 0.5 collective-permute-start.11
  42.6 0.1 stack.23.place
  42.7 1.7 %collective-permute-done.11.refs_7_ = bf16[192,1280]{1,0:T(8,128)(2,1)} collective-permute-done((bf16[192,1280]{1,0:T(8,128)(2,1)}, bf16[192,1280]{1,0:T(8,128)(2,1)}, u32[]{:S(2)}, u32[]{:S(2)}) %collective-permute-start.11) | collective-permute-done | bytes 491552 | tf_op jit(solution)/shard_map/ppermute | solution.py:48
  44.4 1.0 collective-permute-done.7.refs_2_
  45.4 0.0 collective-permute-done.6.refs_1_
  45.4 0.0 collective-permute-done.10.refs_6_
  45.4 5.8 %shard_map.60 = (f32[1024,1024]{1,0:T(8,128)S(1)}, f32[16,128]{1,0:T(8,128)S(1)}, f32[16,128]{1,0:T(8,128)S(1)}, f32[24,128]{1,0:T(8,128)S(1)}, f32[8,128]{1,0:T...) custom-call(s32[5]{0:T(128)S(1)} %stack.23.place, f32[1]{0:T(128)S(6)} %copy.6.scale, ...), custom_call_target="tpu_custom_call" | custom-call | tf_op jit(solution)/shard_map/pallas_call | solution.py:192
  51.2 0.3 collective-permute-start.12
  51.5 1.2 %collective-permute-done.12.got = f32[24,128]{1,0:T(8,128)S(1)} collective-permute-done((f32[24,128]{1,0:T(8,128)S(1)}, f32[24,128]{1,0:T(8,128)S(1)}, u32[]{:S(2)}, u32[]{:S(2)}) %collective-permute-start.12) | collective-permute-done | bytes 12320 | tf_op jit(solution)/shard_map/ppermute | solution.py:48
  52.7 0.6 shard_map.61
  53.3 14.9 %all_to_all.5.got = f32[16,24,128]{2,1,0:T(8,128)S(1)} all-to-all(f32[16,24,128]{2,1,0:T(8,128)S(1)} %shard_map.61), channel_id=1, replica_groups={{0,1,2,3,4,5,6,7,8,9,10,11,12,13,14,15},{64,65,66,67,68,69,70,71,72,73,..., dimensions={0} | all-to-all | bytes 393216 | tf_op jit(solution)/shard_map/all_to_all | solution.py:63
  68.2 0.7 shard_map.62
  68.9 2.1 %collective-permute-start.13 = (f32[24,128]{1,0:T(8,128)S(1)}, f32[24,128]{1,0:T(8,128)S(1)}, u32[]{:S(2)}, u32[]{:S(2)}) collective-permute-start(f32[24,128]{1,0:T(8,128)S(1)} %get-tuple-element.49), channel_id=1, source_target_pairs={{0,32},{32,0},{1,33},{33,1},{2,34},{34,2},{3,35},{35,3},{4,36},{36... | collective-permute-start | bytes 36872 | tf_op jit(solution)/shard_map/ppermute | solution.py:48
  71.1 0.8 collective-permute-done.13.other
  71.9 3.6 %shard_map.63 = (bf16[1024,1024]{1,0:T(8,128)(2,1)S(1)}, bf16[256,1280]{1,0:T(8,128)(2,1)S(1)}, bf16[192,1280]{1,0:T(8,128)(2,1)S(1)}, bf16[32,1280]{1,0:T(8,128)(2,1)S(1)}) custom-call(s32[5]{0:T(128)S(1)} %stack.23.place, f32[1]{0:T(128)S(6)} %copy.6.scale, f32[1024,1024]{1,0:T(8,128)S(1)} %get-tuple-element.43.logits, ...), custom_call_target="tpu_custom_call" | custom-call | tf_op jit(solution)/shard_map/pallas_call | solution.py:358
  75.5 0.4 collective-permute-start.14
  75.9 0.2 collective-permute-start.15
  76.1 1.9 %shard_map.65 = (bf16[256,1280]{1,0:T(8,128)(2,1)S(1)}, bf16[64,1280]{1,0:T(8,128)(2,1)S(1)}) custom-call(f32[1]{0:T(128)S(6)} %copy.6.scale, bf16[1024,1024]{1,0:T(8,128)(2,1)S(1)} %get-tuple-element.51.weights, bf16[1024,1280]{1,0:T(8,128)(2,1)S(1)} %get-tuple-element.50.images), custom_call_target="tpu_custom_call" | custom-call | tf_op jit(solution)/shard_map/pallas_call | solution.py:382
  78.0 0.4 collective-permute-done.15.refs_3_.refs_1_
  78.4 0.2 shard_map.66.after
  78.6 1.1 collective-permute-start.22
  79.6 2.2 %shard_map.67 = (bf16[272,1280]{1,0:T(8,128)(2,1)S(1)}, bf16[272,1280]{1,0:T(8,128)(2,1)S(1)}, bf16[272,1280]{1,0:T(8,128)(2,1)S(1)}) custom-call(f32[1]{0:T(128)S(6)} %copy.6.scale, bf16[336,1280]{1,0:T(8,128)(2,1)S(1)} %shard_map.66.after, bf16[32,1280]{1,0:T(8,128)(2,1)S(1)} %get-tuple-element.58.refs_4_.digits.refs_3_.refs_6_, ...), custom_call_target="tpu_custom_call" | custom-call | tf_op jit(solution)/shard_map/pallas_call | solution.py:398
  81.8 0.6 collective-permute-start.16
  82.5 2.8 %collective-permute-start.17 = (bf16[272,1280]{1,0:T(8,128)(2,1)S(1)}, bf16[272,1280]{1,0:T(8,128)(2,1)S(1)}, u32[]{:S(2)}, u32[]{:S(2)}) collective-permute-start(bf16[272,1280]{1,0:T(8,128)(2,1)S(1)} %get-tuple-element.60), channel_id=1, source_target_pairs={{0,12},{1,13},{2,14},{3,15},{4,0},{5,1},{6,2},{7,3},{8,4},{9,5},{1... | collective-permute-start | bytes 2088968 | tf_op jit(solution)/shard_map/ppermute | solution.py:35
  85.3 0.0 collective-permute-start.18
  85.3 1.6 %shard_map.64 = (bf16[256,1280]{1,0:T(8,128)(2,1)S(1)}, bf16[256,1280]{1,0:T(8,128)(2,1)S(1)}) custom-call(f32[1]{0:T(128)S(6)} %copy.6.scale, bf16[1024,1024]{1,0:T(8,128)(2,1)S(1)} %get-tuple-element.51.weights, bf16[1024,1280]{1,0:T(8,128)(2,1)S(1)} %get-tuple-element.50.images, bf16[1024,1280]{1,0:T(8,128)(2,1)S(1)} %get-tuple-element.52.texts), custom_call_target="tpu_custom_call" | custom-call | tf_op jit(solution)/shard_map/pallas_call | solution.py:413
  86.9 15.2 %collective-permute-done.22.refs_2_ = bf16[336,1280]{1,0:T(8,128)(2,1)S(1)} collective-permute-done((bf16[336,1280]{1,0:T(8,128)(2,1)S(1)}, bf16[336,1280]{1,0:T(8,128)(2,1)S(1)}, u32[]{:S(2)}, u32[]{:S(2)}) %collective-permute-start.22) | collective-permute-done | bytes 860192 | tf_op jit(solution)/shard_map/ppermute | solution.py:44
  102.0 0.2 shard_map.69
  102.3 0.1 collective-permute-start.23
  102.4 0.0 collective-permute-done.16.refs_1_
  102.4 0.0 collective-permute-done.18.refs_3_
  102.4 0.4 shard_map.68
  102.8 2.4 %collective-permute-start.19 = (bf16[80,1280]{1,0:T(8,128)(2,1)S(1)}, bf16[80,1280]{1,0:T(8,128)(2,1)S(1)}, u32[]{:S(2)}, u32[]{:S(2)}) collective-permute-start(bf16[80,1280]{1,0:T(8,128)(2,1)S(1)} %get-tuple-element.63), channel_id=1, source_target_pairs={{0,2},{1,3},{2,0},{3,1},{4,6},{5,7},{6,4},{7,5},{8,10},{9,11},{10,... | collective-permute-start | bytes 614408 | tf_op jit(solution)/shard_map/ppermute | solution.py:35
  105.2 1.1 collective-permute-start.20
  106.3 0.7 collective-permute-start.24
  107.1 0.9 collective-permute-start.21
  108.0 1.9 %collective-permute-done.23.refs_1_ = bf16[144,1280]{1,0:T(8,128)(2,1)S(1)} collective-permute-done((bf16[144,1280]{1,0:T(8,128)(2,1)S(1)}, bf16[144,1280]{1,0:T(8,128)(2,1)S(1)}, u32[]{:S(2)}, u32[]{:S(2)}) %collective-permute-start.23) | collective-permute-done | bytes 368672 | tf_op jit(solution)/shard_map/ppermute | solution.py:44
  109.9 0.1 collective-permute-start.25
  110.0 5.4 %collective-permute-done.24.refs_2_ = bf16[80,1280]{1,0:T(8,128)(2,1)S(1)} collective-permute-done((bf16[80,1280]{1,0:T(8,128)(2,1)S(1)}, bf16[80,1280]{1,0:T(8,128)(2,1)S(1)}, u32[]{:S(2)}, u32[]{:S(2)}) %collective-permute-start.24) | collective-permute-done | bytes 204832 | tf_op jit(solution)/shard_map/ppermute | solution.py:44
  115.4 0.1 shard_map.70.refs_4_
  115.5 0.0 collective-permute-done.21.refs_3_
  115.5 0.0 collective-permute-done.25.refs_5_
  115.5 0.8 shard_map.72
  (9 shorter events, 0.1 us)
Async XLA Ops:
  0.6 1.7 %collective-permute-start = (bf16[64,1280]{1,0:T(8,128)(2,1)}, bf16[64,1280]{1,0:T(8,128)(2,1)S(1)}, u32[]{:S(2)}, u32[]{:S(2)}) collective-permute-start(bf16[64,1280]{1,0:T(8,128)(2,1)} %refs_0_.1), channel_id=1, source_target_pairs={{0,32},{32,0},{1,33},{33,1},{2,34},{34,2},{3,35},{35,3},{4,36},{36... | collective-permute-start | bytes 491528 | tf_op jit(solution)/shard_map/ppermute | solution.py:48
  2.3 0.9 copy-start
  3.2 0.9 copy-start.1
  4.2 18.9 %collective-permute-start.4 = (bf16[128,1280]{1,0:T(8,128)(2,1)S(1)}, bf16[128,1280]{1,0:T(8,128)(2,1)S(1)}, u32[]{:S(2)}, u32[]{:S(2)}) collective-permute-start(bf16[128,1280]{1,0:T(8,128)(2,1)S(1)} %get-tuple-element.39.refs_4_), channel_id=1, source_target_pairs={{0,208},{64,0},{128,64},{192,128},{16,192},{80,16},{144,80},{208,1... | collective-permute-start | bytes 983048 | tf_op jit(solution)/shard_map/ppermute | solution.py:44
  6.1 17.0 %collective-permute-start.5 = (bf16[64,1280]{1,0:T(8,128)(2,1)S(1)}, bf16[64,1280]{1,0:T(8,128)(2,1)S(1)}, u32[]{:S(2)}, u32[]{:S(2)}) collective-permute-start(bf16[64,1280]{1,0:T(8,128)(2,1)S(1)} %copy-done.1), channel_id=1, source_target_pairs={{0,16},{64,80},{128,144},{192,208},{16,0},{80,64},{144,128},{208,1... | collective-permute-start | bytes 491528 | tf_op jit(solution)/shard_map/ppermute | solution.py:44
  11.6 11.5 %collective-permute-start.3 = (bf16[64,1280]{1,0:T(8,128)(2,1)S(1)}, bf16[64,1280]{1,0:T(8,128)(2,1)S(1)}, u32[]{:S(2)}, u32[]{:S(2)}) collective-permute-start(bf16[64,1280]{1,0:T(8,128)(2,1)S(1)} %get-tuple-element.38.refs_0_), channel_id=1, source_target_pairs={{0,3},{1,0},{2,1},{3,2},{4,7},{5,4},{6,5},{7,6},{8,11},{9,8},{10,9... | collective-permute-start | bytes 491528 | tf_op jit(solution)/shard_map/ppermute | solution.py:35
  14.3 8.8 %collective-permute-start.2 = (bf16[64,1280]{1,0:T(8,128)(2,1)S(1)}, bf16[64,1280]{1,0:T(8,128)(2,1)S(1)}, u32[]{:S(2)}, u32[]{:S(2)}) collective-permute-start(bf16[64,1280]{1,0:T(8,128)(2,1)S(1)} %get-tuple-element.38.refs_0_), channel_id=1, source_target_pairs={{0,2},{1,3},{2,0},{3,1},{4,6},{5,7},{6,4},{7,5},{8,10},{9,11},{10,... | collective-permute-start | bytes 491528 | tf_op jit(solution)/shard_map/ppermute | solution.py:35
  15.1 8.0 %collective-permute-start.1 = (bf16[64,1280]{1,0:T(8,128)(2,1)S(1)}, bf16[64,1280]{1,0:T(8,128)(2,1)S(1)}, u32[]{:S(2)}, u32[]{:S(2)}) collective-permute-start(bf16[64,1280]{1,0:T(8,128)(2,1)S(1)} %get-tuple-element.38.refs_0_), channel_id=1, source_target_pairs={{0,1},{1,2},{2,3},{3,0},{4,5},{5,6},{6,7},{7,4},{8,9},{9,10},{10,1... | collective-permute-start | bytes 491528 | tf_op jit(solution)/shard_map/ppermute | solution.py:35
  24.0 17.4 %collective-permute-start.9 = (bf16[256,1280]{1,0:T(8,128)(2,1)S(1)}, bf16[256,1280]{1,0:T(8,128)(2,1)S(1)}, u32[]{:S(2)}, u32[]{:S(2)}) collective-permute-start(bf16[256,1280]{1,0:T(8,128)(2,1)S(1)} %get-tuple-element.41.refs_4_), channel_id=1, source_target_pairs={{0,144},{64,208},{128,0},{192,64},{16,128},{80,192},{144,16},{208,... | collective-permute-start | bytes 1966088 | tf_op jit(solution)/shard_map/ppermute | solution.py:44
  25.9 18.5 %collective-permute-start.8 = (bf16[256,1280]{1,0:T(8,128)(2,1)S(1)}, bf16[256,1280]{1,0:T(8,128)(2,1)S(1)}, u32[]{:S(2)}, u32[]{:S(2)}) collective-permute-start(bf16[256,1280]{1,0:T(8,128)(2,1)S(1)} %get-tuple-element.40.refs_0_), channel_id=1, source_target_pairs={{0,8},{1,9},{2,10},{3,11},{4,12},{5,13},{6,14},{7,15},{8,0},{9,1},... | collective-permute-start | bytes 1966088 | tf_op jit(solution)/shard_map/ppermute | solution.py:35
  29.1 16.3 %collective-permute-start.7 = (bf16[256,1280]{1,0:T(8,128)(2,1)S(1)}, bf16[256,1280]{1,0:T(8,128)(2,1)S(1)}, u32[]{:S(2)}, u32[]{:S(2)}) collective-permute-start(bf16[256,1280]{1,0:T(8,128)(2,1)S(1)} %get-tuple-element.40.refs_0_), channel_id=1, source_target_pairs={{0,12},{1,13},{2,14},{3,15},{4,0},{5,1},{6,2},{7,3},{8,4},{9,5},{1... | collective-permute-start | bytes 1966088 | tf_op jit(solution)/shard_map/ppermute | solution.py:35
  30.2 15.2 %collective-permute-start.6 = (bf16[256,1280]{1,0:T(8,128)(2,1)S(1)}, bf16[256,1280]{1,0:T(8,128)(2,1)}, u32[]{:S(2)}, u32[]{:S(2)}) collective-permute-start(bf16[256,1280]{1,0:T(8,128)(2,1)S(1)} %get-tuple-element.40.refs_0_), channel_id=1, source_target_pairs={{0,4},{1,5},{2,6},{3,7},{4,8},{5,9},{6,10},{7,11},{8,12},{9,13},{1... | collective-permute-start | bytes 1966088 | tf_op jit(solution)/shard_map/ppermute | solution.py:35
  41.5 4.0 %collective-permute-start.10 = (bf16[256,1280]{1,0:T(8,128)(2,1)S(1)}, bf16[256,1280]{1,0:T(8,128)(2,1)}, u32[]{:S(2)}, u32[]{:S(2)}) collective-permute-start(bf16[256,1280]{1,0:T(8,128)(2,1)S(1)} %collective-permute-done.9.refs_5_), channel_id=1, source_target_pairs={{0,32},{32,0},{1,33},{33,1},{2,34},{34,2},{3,35},{35,3},{4,36},{36... | collective-permute-start | bytes 1966088 | tf_op jit(solution)/shard_map/ppermute | solution.py:48
  41.5 2.9 %collective-permute-start.11 = (bf16[192,1280]{1,0:T(8,128)(2,1)}, bf16[192,1280]{1,0:T(8,128)(2,1)}, u32[]{:S(2)}, u32[]{:S(2)}) collective-permute-start(bf16[192,1280]{1,0:T(8,128)(2,1)} %get-tuple-element.42), channel_id=1, source_target_pairs={{0,32},{32,0},{1,33},{33,1},{2,34},{34,2},{3,35},{35,3},{4,36},{36... | collective-permute-start | bytes 1474568 | tf_op jit(solution)/shard_map/ppermute | solution.py:48
  51.2 1.4 %collective-permute-start.12 = (f32[24,128]{1,0:T(8,128)S(1)}, f32[24,128]{1,0:T(8,128)S(1)}, u32[]{:S(2)}, u32[]{:S(2)}) collective-permute-start(f32[24,128]{1,0:T(8,128)S(1)} %get-tuple-element.47), channel_id=1, source_target_pairs={{0,32},{32,0},{1,33},{33,1},{2,34},{34,2},{3,35},{35,3},{4,36},{36... | collective-permute-start | bytes 36872 | tf_op jit(solution)/shard_map/ppermute | solution.py:48
  68.9 3.0 %collective-permute-start.13 = (f32[24,128]{1,0:T(8,128)S(1)}, f32[24,128]{1,0:T(8,128)S(1)}, u32[]{:S(2)}, u32[]{:S(2)}) collective-permute-start(f32[24,128]{1,0:T(8,128)S(1)} %get-tuple-element.49), channel_id=1, source_target_pairs={{0,32},{32,0},{1,33},{33,1},{2,34},{34,2},{3,35},{35,3},{4,36},{36... | collective-permute-start | bytes 36872 | tf_op jit(solution)/shard_map/ppermute | solution.py:48
  75.5 2.9 %collective-permute-start.14 = (bf16[256,1280]{1,0:T(8,128)(2,1)S(1)}, bf16[256,1280]{1,0:T(8,128)(2,1)S(1)}, u32[]{:S(2)}, u32[]{:S(2)}) collective-permute-start(bf16[256,1280]{1,0:T(8,128)(2,1)S(1)} %get-tuple-element.55), channel_id=1, source_target_pairs={{0,32},{32,0},{1,33},{33,1},{2,34},{34,2},{3,35},{35,3},{4,36},{36... | collective-permute-start | bytes 1966088 | tf_op jit(solution)/shard_map/ppermute | solution.py:48
  75.9 2.5 %collective-permute-start.15 = (bf16[192,1280]{1,0:T(8,128)(2,1)S(1)}, bf16[192,1280]{1,0:T(8,128)(2,1)S(1)}, u32[]{:S(2)}, u32[]{:S(2)}) collective-permute-start(bf16[192,1280]{1,0:T(8,128)(2,1)S(1)} %get-tuple-element.57), channel_id=1, source_target_pairs={{0,32},{32,0},{1,33},{33,1},{2,34},{34,2},{3,35},{35,3},{4,36},{36... | collective-permute-start | bytes 1474568 | tf_op jit(solution)/shard_map/ppermute | solution.py:48
  78.6 23.5 %collective-permute-start.22 = (bf16[336,1280]{1,0:T(8,128)(2,1)S(1)}, bf16[336,1280]{1,0:T(8,128)(2,1)S(1)}, u32[]{:S(2)}, u32[]{:S(2)}) collective-permute-start(bf16[336,1280]{1,0:T(8,128)(2,1)S(1)} %shard_map.66.after), channel_id=1, source_target_pairs={{0,128},{64,192},{128,16},{192,80},{16,144},{80,208},{144,0},{208,... | collective-permute-start | bytes 2580488 | tf_op jit(solution)/shard_map/ppermute | solution.py:44
  81.8 20.5 %collective-permute-start.16 = (bf16[272,1280]{1,0:T(8,128)(2,1)S(1)}, bf16[272,1280]{1,0:T(8,128)(2,1)S(1)}, u32[]{:S(2)}, u32[]{:S(2)}) collective-permute-start(bf16[272,1280]{1,0:T(8,128)(2,1)S(1)} %get-tuple-element.59), channel_id=1, source_target_pairs={{0,8},{1,9},{2,10},{3,11},{4,12},{5,13},{6,14},{7,15},{8,0},{9,1},... | collective-permute-start | bytes 2088968 | tf_op jit(solution)/shard_map/ppermute | solution.py:35
  82.5 19.9 %collective-permute-start.17 = (bf16[272,1280]{1,0:T(8,128)(2,1)S(1)}, bf16[272,1280]{1,0:T(8,128)(2,1)S(1)}, u32[]{:S(2)}, u32[]{:S(2)}) collective-permute-start(bf16[272,1280]{1,0:T(8,128)(2,1)S(1)} %get-tuple-element.60), channel_id=1, source_target_pairs={{0,12},{1,13},{2,14},{3,15},{4,0},{5,1},{6,2},{7,3},{8,4},{9,5},{1... | collective-permute-start | bytes 2088968 | tf_op jit(solution)/shard_map/ppermute | solution.py:35
  85.3 17.1 %collective-permute-start.18 = (bf16[272,1280]{1,0:T(8,128)(2,1)S(1)}, bf16[272,1280]{1,0:T(8,128)(2,1)S(1)}, u32[]{:S(2)}, u32[]{:S(2)}) collective-permute-start(bf16[272,1280]{1,0:T(8,128)(2,1)S(1)} %get-tuple-element.61), channel_id=1, source_target_pairs={{0,4},{1,5},{2,6},{3,7},{4,8},{5,9},{6,10},{7,11},{8,12},{9,13},{1... | collective-permute-start | bytes 2088968 | tf_op jit(solution)/shard_map/ppermute | solution.py:35
  102.3 7.6 %collective-permute-start.23 = (bf16[144,1280]{1,0:T(8,128)(2,1)S(1)}, bf16[144,1280]{1,0:T(8,128)(2,1)S(1)}, u32[]{:S(2)}, u32[]{:S(2)}) collective-permute-start(bf16[144,1280]{1,0:T(8,128)(2,1)S(1)} %get-tuple-element.68), channel_id=1, source_target_pairs={{0,64},{64,128},{128,192},{192,16},{16,80},{80,144},{144,208},{208... | collective-permute-start | bytes 1105928 | tf_op jit(solution)/shard_map/ppermute | solution.py:44
  102.8 12.7 %collective-permute-start.19 = (bf16[80,1280]{1,0:T(8,128)(2,1)S(1)}, bf16[80,1280]{1,0:T(8,128)(2,1)S(1)}, u32[]{:S(2)}, u32[]{:S(2)}) collective-permute-start(bf16[80,1280]{1,0:T(8,128)(2,1)S(1)} %get-tuple-element.63), channel_id=1, source_target_pairs={{0,2},{1,3},{2,0},{3,1},{4,6},{5,7},{6,4},{7,5},{8,10},{9,11},{10,... | collective-permute-start | bytes 614408 | tf_op jit(solution)/shard_map/ppermute | solution.py:35
  105.2 10.3 %collective-permute-start.20 = (bf16[80,1280]{1,0:T(8,128)(2,1)S(1)}, bf16[80,1280]{1,0:T(8,128)(2,1)S(1)}, u32[]{:S(2)}, u32[]{:S(2)}) collective-permute-start(bf16[80,1280]{1,0:T(8,128)(2,1)S(1)} %get-tuple-element.64), channel_id=1, source_target_pairs={{0,3},{1,0},{2,1},{3,2},{4,7},{5,4},{6,5},{7,6},{8,11},{9,8},{10,9... | collective-permute-start | bytes 614408 | tf_op jit(solution)/shard_map/ppermute | solution.py:35
  106.3 9.1 %collective-permute-start.24 = (bf16[80,1280]{1,0:T(8,128)(2,1)S(1)}, bf16[80,1280]{1,0:T(8,128)(2,1)S(1)}, u32[]{:S(2)}, u32[]{:S(2)}) collective-permute-start(bf16[80,1280]{1,0:T(8,128)(2,1)S(1)} %get-tuple-element.69), channel_id=1, source_target_pairs={{0,128},{64,192},{128,16},{192,80},{16,144},{80,208},{144,0},{208,... | collective-permute-start | bytes 614408 | tf_op jit(solution)/shard_map/ppermute | solution.py:44
  107.1 8.5 %collective-permute-start.21 = (bf16[80,1280]{1,0:T(8,128)(2,1)S(1)}, bf16[80,1280]{1,0:T(8,128)(2,1)S(1)}, u32[]{:S(2)}, u32[]{:S(2)}) collective-permute-start(bf16[80,1280]{1,0:T(8,128)(2,1)S(1)} %get-tuple-element.65), channel_id=1, source_target_pairs={{0,1},{1,2},{2,3},{3,0},{4,5},{5,6},{6,7},{7,4},{8,9},{9,10},{10,1... | collective-permute-start | bytes 614408 | tf_op jit(solution)/shard_map/ppermute | solution.py:35
  109.9 5.6 %collective-permute-start.25 = (bf16[80,1280]{1,0:T(8,128)(2,1)S(1)}, bf16[80,1280]{1,0:T(8,128)(2,1)S(1)}, u32[]{:S(2)}, u32[]{:S(2)}) collective-permute-start(bf16[80,1280]{1,0:T(8,128)(2,1)S(1)} %shard_map.71), channel_id=1, source_target_pairs={{0,32},{32,0},{1,33},{33,1},{2,34},{34,2},{3,35},{35,3},{4,36},{36... | collective-permute-start | bytes 614408 | tf_op jit(solution)/shard_map/ppermute | solution.py:48

commit v10 on v9

--- a/solution.py
+++ b/solution.py
@@ -98,6 +98,8 @@
 PLANE_ORDER = (0, 1, 3, 2)
 PART = jax.ShapeDtypeStruct((CHUNK, EMBED), BF16)
 ALL = jax.ShapeDtypeStruct((BLOCK, EMBED), BF16)
+HALF = jax.ShapeDtypeStruct((BLOCK // 2, EMBED), BF16)
+HALF_LOGITS = jax.ShapeDtypeStruct((BLOCK, BLOCK // 2), F32)
 
 
 def pack_body(plan, n, *refs):
@@ -134,33 +136,64 @@
     return top + LOG2E * jnp.log(jnp.sum(total, axis=0, keepdims=True))
 
 
-def logits_body(place, scale, *refs):
-    images, texts = [refs[i] for i in PLANE_ORDER], refs[4:7]
-    logits, row_out, col_out, message, match_out, all_images, all_texts = refs[9:16]
-    row_wide = refs[16]
-    all_texts[3 * CHUNK : BLOCK - ROWS, :] = refs[7][...]
-    all_texts[BLOCK - ROWS :, :] = refs[8][...]
+def block_logits(multiplier, images, texts, logits):
+    for j in range(2):
+        for a in range(4):
+            logits[a * CHUNK : (a + 1) * CHUNK, j * CHUNK : (j + 1) * CHUNK] = multiplier * lax.dot_general(
+                images[a * CHUNK : (a + 1) * CHUNK, :],
+                texts[j * CHUNK : (j + 1) * CHUNK, :],
+                (((1,), (1,)), ((), ())),
+                preferred_element_type=F32,
+            )
+
+
+def first_body(scale, *refs):
+    images, texts = [refs[i] for i in PLANE_ORDER], refs[4:6]
+    logits, col_out, all_images, all_texts = refs[6:]
+    for a in range(4):
+        all_images[a * CHUNK : (a + 1) * CHUNK, :] = images[a][...]
+    for j in range(2):
+        all_texts[j * CHUNK : (j + 1) * CHUNK, :] = texts[j][:CHUNK, :]
+    block_logits(scale[0] * LOG2E, all_images, all_texts, logits)
+    for t in range(4):
+        top = jnp.max(fold(logits[:128, t * 128 : (t + 1) * 128]), axis=0)
+        for i in range(1, 8):
+            tile = logits[i * 128 : (i + 1) * 128, t * 128 : (t + 1) * 128]
+            top = jnp.maximum(top, jnp.max(fold(tile), axis=0))
+        col_out[t : t + 1, :] = column_part(logits, t, top)
+
+
+def first_call(scale, images, texts):
+    return pl.pallas_call(
+        first_body,
+        out_shape=(HALF_LOGITS, jax.ShapeDtypeStruct((8, 128), F32), ALL, HALF),
+        in_specs=[SMEM] + [VMEM] * 6,
+        out_specs=(VMEM,) * 4,
+        compiler_params=PARAMS,
+    )(scale, *images, *texts)
+
+
+def second_body(place, scale, logits_0, col_parts, images, text_1, text_2, side, *refs):
+    logits_1, row_out, col_out, message, match_out, all_texts, row_wide = refs
+    all_texts[:CHUNK, :] = text_2[:CHUNK, :]
+    all_texts[CHUNK : CHUNK + 2 * ROWS, :] = side[...]
+    all_texts[CHUNK + 2 * ROWS : CHUNK + 3 * ROWS, :] = text_2[CHUNK:, :]
+    all_texts[CHUNK + 3 * ROWS :, :] = text_1[CHUNK:, :]
     where = [place[i] for i in range(5)]
-    multiplier = scale[0] * LOG2E
-    for j in range(4):
-        if j < 3:
-            all_texts[j * CHUNK : (j + 1) * CHUNK, :] = texts[j][...]
-        all_images[j * CHUNK : (j + 1) * CHUNK, :] = images[j][...]
-        for a in range(4):
-            text = texts[j][...] if j < 3 else all_texts[3 * CHUNK :, :]
-            logits[a * CHUNK : (a + 1) * CHUNK, j * CHUNK : (j + 1) * CHUNK] = multiplier * lax.dot_general(
-                images[a][...], text, (((1,), (1,)), ((), ())), preferred_element_type=F32
-            )
+    block_logits(scale[0] * LOG2E, images, all_texts, logits_1)
+    halves = (logits_0, logits_1)
     cols = col_ids(where)
     step = 32
     matched = jnp.zeros((8, 128), F32)
-    col_top = [jnp.full((8, 128), -jnp.inf, F32) for _ in range(8)]
+    col_top = [jnp.full((8, 128), -jnp.inf, F32) for _ in range(4)]
     for a in range(4):
         ids = row_ids(where, a)
         for b in range(4):
             for half in range(ROWS // step):
                 at = a * CHUNK + b * ROWS + half * step
-                tiles = [logits[at : at + step, t * 128 : (t + 1) * 128] for t in range(8)]
+                tiles = [
+                    halves[t // 4][at : at + step, (t % 4) * 128 : (t % 4 + 1) * 128] for t in range(8)
+                ]
                 top = tiles[0]
                 for t in range(1, 8):
                     top = jnp.maximum(top, tiles[t])
@@ -169,7 +202,8 @@
                 total = jnp.zeros((step, 128), F32)
                 for t in range(8):
                     total += jnp.exp2(tiles[t] - top)
-                    col_top[t] = jnp.maximum(col_top[t], jnp.max(fold(tiles[t]), axis=0))
+                    if t > 3:
+                        col_top[t - 4] = jnp.maximum(col_top[t - 4], jnp.max(fold(tiles[t]), axis=0))
                     hit = jnp.where(mine == cols[t][0:1], tiles[t], 0.0)
                     matched += jnp.sum(fold(hit), axis=0)
                 part = top + LOG2E * jnp.log(jnp.sum(total, axis=1, keepdims=True))
@@ -178,7 +212,7 @@
     match_out[...] = matched
     message[16:24, :] = matched
     for t in range(8):
-        part = column_part(logits, t, col_top[t])
+        part = col_parts[t : t + 1, :] if t < 4 else column_part(logits_1, t - 4, col_top[t - 4])
         j, i = t // 2, (t % 2) * 2
         col_out[pl.ds(col_place(where, j, i)[0], 1), :] = part
         col_out[pl.ds(col_place(where, j, i + 1)[0], 1), :] = pltpu.roll(part, 64, 1)
@@ -188,23 +222,22 @@
     message[:16, :] = jnp.where(where[1] == 0, col_out[...], row_out[...])
 
 
-def logits_call(place, scale, images, texts):
-    return pl.pallas_call(
-        logits_body,
+def second_call(place, scale, *arrays):
+    return pl.pallas_call(
+        second_body,
         out_shape=(
-            jax.ShapeDtypeStruct((BLOCK, BLOCK), F32),
+            HALF_LOGITS,
             jax.ShapeDtypeStruct((16, 128), F32),
             jax.ShapeDtypeStruct((16, 128), F32),
             jax.ShapeDtypeStruct((24, 128), F32),
             jax.ShapeDtypeStruct((8, 128), F32),
-            ALL,
-            ALL,
+            HALF,
         ),
-        in_specs=[SMEM, SMEM] + [VMEM] * 9,
-        out_specs=(VMEM,) * 7,
+        in_specs=[SMEM, SMEM] + [VMEM] * 6,
+        out_specs=(VMEM,) * 6,
         scratch_shapes=[pltpu.VMEM((BLOCK, 128), F32)],
         compiler_params=PARAMS,
-    )(place, scale, *images, *texts)
+    )(place, scale, *arrays)
 
 
 def pair_up(rows):
@@ -293,7 +326,7 @@
     return jnp.sum(digits * units, axis=0, keepdims=True)
 
 
-def weights_body(place, scale, logits, mine, other, images, *refs):
+def weights_body(place, scale, logits_0, logits_1, mine, other, images, *refs):
     weights, outs = refs[0], refs[1:4]
     row_wide, row_lse, col_lse = refs[4:]
     first = place[1] == 0
@@ -324,7 +357,7 @@
             at = a * CHUNK + b * ROWS
             wide = row_wide[at : at + ROWS, :]
             for t in range(8):
-                tile = logits[at : at + ROWS, t * 128 : (t + 1) * 128]
+                tile = (logits_0, logits_1)[t // 4][at : at + ROWS, (t % 4) * 128 : (t % 4 + 1) * 128]
                 both = jnp.exp2(tile - wide) + jnp.exp2(tile - col_line[t])
                 both = both - jnp.where(ids[b] == cols[t][0:1], 1.0, 0.0)
                 weights[at : at + ROWS, t * 128 : (t + 1) * 128] = both.astype(BF16)
@@ -346,10 +379,13 @@
 def image_terms(multiplier, weights, texts, outs):
     for a, out in outs.items():
         for e in range(5):
-            term = jnp.dot(
-                weights[a * CHUNK : (a + 1) * CHUNK, :],
-                texts[:, e * 256 : (e + 1) * 256],
-                preferred_element_type=F32,
+            term = sum(
+                jnp.dot(
+                    weights[a * CHUNK : (a + 1) * CHUNK, h * BLOCK // 2 : (h + 1) * BLOCK // 2],
+                    texts[h][:, e * 256 : (e + 1) * 256],
+                    preferred_element_type=F32,
+                )
+                for h in range(2)
             )
             out[:CHUNK, e * 256 : (e + 1) * 256] = (multiplier * term).astype(BF16)
 
@@ -363,7 +399,7 @@
             jax.ShapeDtypeStruct((3 * ROWS, EMBED), BF16),
             jax.ShapeDtypeStruct((2 * TAIL, EMBED), BF16),
         ),
-        in_specs=[SMEM, SMEM] + [VMEM] * 4,
+        in_specs=[SMEM, SMEM] + [VMEM] * 5,
         out_specs=(VMEM,) * 4,
         scratch_shapes=[
             pltpu.VMEM((BLOCK, 128), F32),
@@ -371,7 +407,7 @@
             pltpu.VMEM((16, 128), F32),
         ],
         compiler_params=PARAMS,
-    )(place, scale, logits, mine, other, images)
+    )(place, scale, *logits, mine, other, images)
 
 
 def text_body(scale, weights, images, near, far):
@@ -388,8 +424,8 @@
     )(scale, weights, images)
 
 
-def image_body(scale, after, digits, weights, texts, *outs):
-    image_terms(scale[0], weights, texts, dict(zip((2, 1, 3), outs)))
+def image_body(scale, after, digits, weights, text_0, text_1, *outs):
+    image_terms(scale[0], weights, (text_0, text_1), dict(zip((2, 1, 3), outs)))
     for out in outs:
         out[CHUNK:, :] = digits[TAIL:, :]
 
@@ -398,25 +434,25 @@
     return pl.pallas_call(
         image_body,
         out_shape=(jax.ShapeDtypeStruct((CHUNK + TAIL, EMBED), BF16),) * 3,
-        in_specs=[SMEM] + [VMEM] * 4,
+        in_specs=[SMEM] + [VMEM] * 5,
         out_specs=(VMEM,) * 3,
         compiler_params=PARAMS,
-    )(scale, after, digits, weights, texts)
-
-
-def rest_body(scale, weights, images, texts, text_out, image_out):
+    )(scale, after, digits, weights, *texts)
+
+
+def rest_body(scale, weights, images, text_0, text_1, text_out, image_out):
     text_terms(scale[0], weights, images, ((0, text_out),))
-    image_terms(scale[0], weights, texts, {0: image_out})
+    image_terms(scale[0], weights, (text_0, text_1), {0: image_out})
 
 
 def rest_call(scale, weights, images, texts):
     return pl.pallas_call(
         rest_body,
         out_shape=(PART, PART),
-        in_specs=[SMEM] + [VMEM] * 3,
+        in_specs=[SMEM] + [VMEM] * 4,
         out_specs=(VMEM,) * 2,
         compiler_params=PARAMS,
-    )(scale, weights, images, texts)
+    )(scale, weights, images, *texts)
 
 
 def add_rows(refs, rows, terms, out, to):
@@ -473,19 +509,21 @@
     place = jnp.stack([lax.axis_index(n) for n in AXES]).astype(jnp.int32)
 
     chip, image = pack([text_emb, core_swap(text_emb), image_emb], ((0, 64), (1, 64)), ((2, 64),))
-    next_1, next_4 = z_shift(chip, -1), z_shift(text_emb, 4)
+    next_1, next_2 = z_shift(chip, -1), z_shift(text_emb, -2)
     near = [plane_shift(image, k, True) for k in (1, 2, 3)]
-    own, text_0, side = pack(
-        [image] + near + [chip, next_1, next_4],
+    own, text_0 = pack(
+        [image] + near + [chip, next_1, next_2],
         ((0, 64), (1, 64), (2, 64), (3, 64)),
-        ((4, 128), (5, 128)),
-        ((5, 128), (6, 64)),
+        ((4, 128), (5, 128), (6, 64)),
     )
     text_1 = z_shift(text_0, -2)
     near = [own] + [plane_shift(own, k, False) for k in PLANE_ORDER[1:]]
-    logits, row_part, col_part, message, matched, images, texts = logits_call(
-        place, logit_scale, near, [text_0, text_1, core_swap(text_1), core_swap(side), next_4]
-    )
+    (text_1,) = pack([text_1] + near[1:], ((0, CHUNK + ROWS),))
+    logits_0, col_parts, images, texts_0 = first_call(logit_scale, near, [text_0, text_1])
+    logits_1, row_part, col_part, message, matched, texts_1 = second_call(
+        place, logit_scale, logits_0, col_parts, images, text_1, core_swap(text_1), core_swap(next_1)
+    )
+    logits, texts = (logits_0, logits_1), (texts_0, texts_1)
 
     spread = spread_call(place, row_part, col_part, matched, core_swap(message))
     mine, message = join_call(place, exchange(spread, plane_or_ring()))
@@ -512,9 +550,10 @@
         ((80, ((2, 256),)),),
     )
     next_1, next_4 = z_shift(next_1, 1), z_shift(next_4, 2)
-    (other,) = sums([mine, next_1], ((64, ((0, 64), (1, 64))), (TAIL, ((0, 128), (1, 128)))))
-    (mine,) = sums(
-        [mine, next_1, next_4], ((64, ((0, 0), (1, 0), (2, 0))), (TAIL, ((0, 128), (1, 128), (2, 64))))
+    mine, other = sums(
+        [mine, next_1, next_4],
+        ((64, ((0, 0), (1, 0), (2, 0))), (TAIL, ((0, 128), (1, 128), (2, 64)))),
+        ((64, ((0, 64), (1, 64))), (TAIL, ((0, 128), (1, 128)))),
     )
 
     cols_tail = (TAIL, ((1, 256), (2, 256), (3, 256), (4, 16)))

time: 118 us -> 121 us (1.025); the launches traced: 116 us -> 121 us
  waiting for transfers between devices: 46.6 us -> 51.9 us
  blocking collectives: 14.9 us -> 12.7 us
    ppermute x12, waiting for transfers between devices: 1.03 us -> 21.2 us  [plane_shift(): return lax.ppermute(v, ('core', 'zh', 'y', 'x'), pairs)]
    ppermute x6, waiting for transfers between devices: 39.9 us -> 25.6 us  [z_shift(): return lax.ppermute(v, ('zl', 'core', 'zh'), pairs)]
    all_to_all x1, blocking collectives: 14.9 us -> 12.7 us  [exchange(): return lax.all_to_all(v, AXES, 0, 0, axis_index_groups=groups)]
    ppermute x8, starting transfers between devices: 3.7 us -> 5.15 us  [core_swap(): return lax.ppermute(v, 'core', [(0, 1), (1, 0)])]
    unnamed x4 -> x8, local copies, waits for them, and re-layouts: 1.83 us -> 2.98 us
    pallas_call x1 -> x2, Pallas kernels: 5.81 us -> 5.96 us  [the longest x1 4.08 us: second_call(): pl.pallas_call(second_body, out_shape=(HALF_LOGITS, jax.ShapeDtypeStruct(...]
  transfers between devices with their start and end apart: 26 -> 26, of which waited for: 11 -> 13; matrix products, arithmetic and copies ran while one was open for 0% -> 0% of each run, Pallas kernels for 6% -> 7%
where the time goes in v10:
time: 121 us
  waiting for transfers between devices  51.9 us (43%)
  starting transfers between devices  32.1 us (27%)
  Pallas kernels  19.6 us (16%)
  blocking collectives  12.7 us (10%)
  local copies, waits for them, and re-layouts  3.07 us (3%)
  between operations  1.47 us (1%)
    ppermute x6, waiting for transfers between devices, z_shift(): return lax.ppermute(v, ('zl', 'core', 'zh'), pairs)  25.6 us
    ppermute x12, waiting for transfers between devices, plane_shift(): return lax.ppermute(v, ('core', 'zh', 'y', 'x'), pairs)  21.2 us
    ppermute x12, starting transfers between devices, plane_shift(): return lax.ppermute(v, ('core', 'zh', 'y', 'x'), pairs)  16.9 us
    all_to_all x1, blocking collectives, exchange(): return lax.all_to_all(v, AXES, 0, 0, axis_index_groups=groups)  12.7 us
    ppermute x6, starting transfers between devices, z_shift(): return lax.ppermute(v, ('zl', 'core', 'zh'), pairs)  9.97 us
    ppermute x8, starting transfers between devices, core_swap(): return lax.ppermute(v, 'core', [(0, 1), (1, 0)])  5.15 us
    ppermute x8, waiting for transfers between devices, core_swap(): return lax.ppermute(v, 'core', [(0, 1), (1, 0)])  5.08 us
    pallas_call x1, Pallas kernels, second_call(): pl.pallas_call(second_body, out_shape=(HALF_LOGITS, jax.ShapeDtypeStruct(...  4.08 us
  transfers between devices with their start and end apart: 26, of which 13 were waited for; matrix products, arithmetic and copies ran while one was open for 0% of the time, Pallas kernels for 7%

profile of v10, /device:TPU:32, one launch (start us, length us, event | category | flops | bytes accessed | tf_op | source)
XLA Modules:
  0.0 120.8 jit_solution(11677334100932037973)
XLA Ops:
  0.6 0.1 collective-permute-start
  0.7 1.6 %collective-permute-done.refs_1_ = bf16[64,1280]{1,0:T(8,128)(2,1)S(1)} collective-permute-done((bf16[64,1280]{1,0:T(8,128)(2,1)}, bf16[64,1280]{1,0:T(8,128)(2,1)S(1)}, u32[]{:S(2)}, u32[]{:S(2)}) %collective-permute-start) | collective-permute-done | bytes 163872 | tf_op jit(solution)/shard_map/ppermute | solution.py:48
  2.3 0.9 copy-done.2
  3.2 0.9 copy-done.3
  4.2 1.9 %collective-permute-start.4 = (bf16[128,1280]{1,0:T(8,128)(2,1)S(1)}, bf16[128,1280]{1,0:T(8,128)(2,1)}, u32[]{:S(2)}, u32[]{:S(2)}) collective-permute-start(bf16[128,1280]{1,0:T(8,128)(2,1)S(1)} %get-tuple-element.43.refs_4_), channel_id=1, source_target_pairs={{0,208},{64,0},{128,64},{192,128},{16,192},{80,16},{144,80},{208,1... | collective-permute-start | bytes 983048 | tf_op jit(solution)/shard_map/ppermute | solution.py:44
  6.1 4.6 %collective-permute-start.5 = (bf16[64,1280]{1,0:T(8,128)(2,1)S(1)}, bf16[64,1280]{1,0:T(8,128)(2,1)S(1)}, u32[]{:S(2)}, u32[]{:S(2)}) collective-permute-start(bf16[64,1280]{1,0:T(8,128)(2,1)S(1)} %copy-done.3), channel_id=1, source_target_pairs={{0,144},{64,208},{128,0},{192,64},{16,128},{80,192},{144,16},{208,... | collective-permute-start | bytes 491528 | tf_op jit(solution)/shard_map/ppermute | solution.py:44
  10.7 2.8 %collective-permute-start.3 = (bf16[64,1280]{1,0:T(8,128)(2,1)S(1)}, bf16[64,1280]{1,0:T(8,128)(2,1)S(1)}, u32[]{:S(2)}, u32[]{:S(2)}) collective-permute-start(bf16[64,1280]{1,0:T(8,128)(2,1)S(1)} %get-tuple-element.42.refs_0_), channel_id=1, source_target_pairs={{0,3},{1,0},{2,1},{3,2},{4,7},{5,4},{6,5},{7,6},{8,11},{9,8},{10,9... | collective-permute-start | bytes 491528 | tf_op jit(solution)/shard_map/ppermute | solution.py:35
  13.4 0.8 collective-permute-start.2
  14.2 0.9 collective-permute-start.1
  15.1 0.0 collective-permute-done.5.refs_6_
  15.1 2.9 %collective-permute-done.3.refs_3_ = bf16[64,1280]{1,0:T(8,128)(2,1)S(1)} collective-permute-done((bf16[64,1280]{1,0:T(8,128)(2,1)S(1)}, bf16[64,1280]{1,0:T(8,128)(2,1)S(1)}, u32[]{:S(2)}, u32[]{:S(2)}) %collective-permute-start.3) | collective-permute-done | bytes 163872 | tf_op jit(solution)/shard_map/ppermute | solution.py:35
  18.1 2.3 %collective-permute-done.2.refs_2_ = bf16[64,1280]{1,0:T(8,128)(2,1)S(1)} collective-permute-done((bf16[64,1280]{1,0:T(8,128)(2,1)S(1)}, bf16[64,1280]{1,0:T(8,128)(2,1)S(1)}, u32[]{:S(2)}, u32[]{:S(2)}) %collective-permute-start.2) | collective-permute-done | bytes 163872 | tf_op jit(solution)/shard_map/ppermute | solution.py:35
  20.4 1.7 %collective-permute-done.1.refs_1_ = bf16[64,1280]{1,0:T(8,128)(2,1)S(1)} collective-permute-done((bf16[64,1280]{1,0:T(8,128)(2,1)S(1)}, bf16[64,1280]{1,0:T(8,128)(2,1)S(1)}, u32[]{:S(2)}, u32[]{:S(2)}) %collective-permute-start.1) | collective-permute-done | bytes 163872 | tf_op jit(solution)/shard_map/ppermute | solution.py:35
  22.0 1.1 shard_map.59
  23.1 1.5 %collective-permute-start.9 = (bf16[320,1280]{1,0:T(8,128)(2,1)S(1)}, bf16[320,1280]{1,0:T(8,128)(2,1)S(1)}, u32[]{:S(2)}, u32[]{:S(2)}) collective-permute-start(bf16[320,1280]{1,0:T(8,128)(2,1)S(1)} %get-tuple-element.45.refs_4_), channel_id=1, source_target_pairs={{0,144},{64,208},{128,0},{192,64},{16,128},{80,192},{144,16},{208,... | collective-permute-start | bytes 2457608 | tf_op jit(solution)/shard_map/ppermute | solution.py:44
  24.6 3.2 %collective-permute-start.8 = (bf16[256,1280]{1,0:T(8,128)(2,1)S(1)}, bf16[256,1280]{1,0:T(8,128)(2,1)S(1)}, u32[]{:S(2)}, u32[]{:S(2)}) collective-permute-start(bf16[256,1280]{1,0:T(8,128)(2,1)S(1)} %get-tuple-element.44.refs_0_), channel_id=1, source_target_pairs={{0,8},{1,9},{2,10},{3,11},{4,12},{5,13},{6,14},{7,15},{8,0},{9,1},... | collective-permute-start | bytes 1966088 | tf_op jit(solution)/shard_map/ppermute | solution.py:35
  27.8 1.1 collective-permute-start.7
  28.9 1.0 collective-permute-start.6
  29.9 7.0 %collective-permute-done.8.refs_3_ = bf16[256,1280]{1,0:T(8,128)(2,1)S(1)} collective-permute-done((bf16[256,1280]{1,0:T(8,128)(2,1)S(1)}, bf16[256,1280]{1,0:T(8,128)(2,1)S(1)}, u32[]{:S(2)}, u32[]{:S(2)}) %collective-permute-start.8) | collective-permute-done | bytes 655392 | tf_op jit(solution)/shard_map/ppermute | solution.py:35
  36.8 7.3 %collective-permute-done.7.refs_2_ = bf16[256,1280]{1,0:T(8,128)(2,1)S(1)} collective-permute-done((bf16[256,1280]{1,0:T(8,128)(2,1)S(1)}, bf16[256,1280]{1,0:T(8,128)(2,1)S(1)}, u32[]{:S(2)}, u32[]{:S(2)}) %collective-permute-start.7) | collective-permute-done | bytes 655392 | tf_op jit(solution)/shard_map/ppermute | solution.py:35
  44.1 0.0 collective-permute-done.6.refs_1_
  44.1 1.1 collective-permute-done.9.refs_0_
  45.2 0.1 shard_map.60.refs_5_.text_1
  45.3 0.1 collective-permute-start.10
  45.4 0.5 collective-permute-start.11
  46.6 0.1 stack.23.place
  46.6 1.1 copy-done.1
  47.8 1.9 %shard_map.61 = (f32[1024,512]{1,0:T(8,128)S(1)}, f32[8,128]{1,0:T(8,128)S(1)}, bf16[1024,1280]{1,0:T(8,128)(2,1)S(1)}, bf16[512,1280]{1,0:T(8,128)(2,1)S(1)}) custom-call(f32[1]{0:T(128)S(6)} %copy.6.scale, bf16[256,1280]{1,0:T(8,128)(2,1)S(1)} %get-tuple-element.44.refs_0_, bf16[256,1280]{1,0:T(8,128)(2,1)S(1)} %collective-permute-done.6.refs_1_, ...), custom_call_target="tpu_custom_call" | custom-call | tf_op jit(solution)/shard_map/pallas_call | solution.py:167
  49.7 0.0 collective-permute-done.11.side
  49.7 4.1 %shard_map.62 = (f32[1024,512]{1,0:T(8,128)S(1)}, f32[16,128]{1,0:T(8,128)S(1)}, f32[16,128]{1,0:T(8,128)S(1)}, f32[24,128]{1,0:T(8,128)S(1)}, f32[8,128]{1,0:T(8,128)S(1)}, /*index=5*/bf16[512,1280]{1,0:T(8,128)(2,1)S(1)}) custom-call(s32[5]{0:T(128)S(1)} %stack.23.place, f32[1]{0:T(128)S(6)} %copy.6.scale, f32[1024,512]{1,0:T(8,128)S(1)} %get-tuple-element.46.logits_0, ...), custom_call_target="tpu_custom_call" | custom-call | tf_op jit(solution)/shard_map/pallas_call | solution.py:226
  53.8 0.4 collective-permute-start.12
  54.1 0.9 collective-permute-done.12.got
  55.0 0.6 shard_map.63
  55.7 12.7 %all_to_all.5.got = f32[16,24,128]{2,1,0:T(8,128)S(1)} all-to-all(f32[16,24,128]{2,1,0:T(8,128)S(1)} %shard_map.63), channel_id=1, replica_groups={{0,1,2,3,4,5,6,7,8,9,10,11,12,13,14,15},{64,65,66,67,68,69,70,71,72,73,..., dimensions={0} | all-to-all | bytes 393216 | tf_op jit(solution)/shard_map/all_to_all | solution.py:63
  68.4 0.7 shard_map.64
  69.2 3.4 %collective-permute-start.13 = (f32[24,128]{1,0:T(8,128)S(1)}, f32[24,128]{1,0:T(8,128)S(1)}, u32[]{:S(2)}, u32[]{:S(2)}) collective-permute-start(f32[24,128]{1,0:T(8,128)S(1)} %get-tuple-element.55), channel_id=1, source_target_pairs={{0,32},{32,0},{1,33},{33,1},{2,34},{34,2},{3,35},{35,3},{4,36},{36... | collective-permute-start | bytes 36872 | tf_op jit(solution)/shard_map/ppermute | solution.py:48
  72.6 0.8 collective-permute-done.13.other
  73.4 3.7 %shard_map.65 = (bf16[1024,1024]{1,0:T(8,128)(2,1)S(1)}, bf16[256,1280]{1,0:T(8,128)(2,1)S(1)}, bf16[192,1280]{1,0:T(8,128)(2,1)S(1)}, bf16[32,1280]{1,0:T(8,128)(2,1)S(1)}) custom-call(s32[5]{0:T(128)S(1)} %stack.23.place, f32[1]{0:T(128)S(6)} %copy.6.scale, f32[1024,512]{1,0:T(8,128)S(1)} %get-tuple-element.46.logits_0, ...), custom_call_target="tpu_custom_call" | custom-call | tf_op jit(solution)/shard_map/pallas_call | solution.py:394
  77.1 0.4 collective-permute-start.14
  77.5 0.2 collective-permute-start.15
  77.7 2.0 %shard_map.67 = (bf16[256,1280]{1,0:T(8,128)(2,1)S(1)}, bf16[64,1280]{1,0:T(8,128)(2,1)S(1)}) custom-call(f32[1]{0:T(128)S(6)} %copy.6.scale, bf16[1024,1024]{1,0:T(8,128)(2,1)S(1)} %get-tuple-element.56.weights, bf16[1024,1280]{1,0:T(8,128)(2,1)S(1)} %get-tuple-element.48.images), custom_call_target="tpu_custom_call" | custom-call | tf_op jit(solution)/shard_map/pallas_call | solution.py:418
  79.6 0.3 collective-permute-done.15.refs_3_.refs_1_
  79.9 0.2 shard_map.68.after
  80.2 1.3 %collective-permute-start.22 = (bf16[336,1280]{1,0:T(8,128)(2,1)S(1)}, bf16[336,1280]{1,0:T(8,128)(2,1)S(1)}, u32[]{:S(2)}, u32[]{:S(2)}) collective-permute-start(bf16[336,1280]{1,0:T(8,128)(2,1)S(1)} %shard_map.68.after), channel_id=1, source_target_pairs={{0,128},{64,192},{128,16},{192,80},{16,144},{80,208},{144,0},{208,... | collective-permute-start | bytes 2580488 | tf_op jit(solution)/shard_map/ppermute | solution.py:44
  81.4 2.2 %shard_map.69 = (bf16[272,1280]{1,0:T(8,128)(2,1)S(1)}, bf16[272,1280]{1,0:T(8,128)(2,1)S(1)}, bf16[272,1280]{1,0:T(8,128)(2,1)S(1)}) custom-call(f32[1]{0:T(128)S(6)} %copy.6.scale, bf16[336,1280]{1,0:T(8,128)(2,1)S(1)} %shard_map.68.after, bf16[32,1280]{1,0:T(8,128)(2,1)S(1)} %get-tuple-element.64.refs_4_.digits.refs_3_.refs_6_, ...), custom_call_target="tpu_custom_call" | custom-call | tf_op jit(solution)/shard_map/pallas_call | solution.py:434
  83.6 0.6 collective-permute-start.16
  84.3 2.8 %collective-permute-start.17 = (bf16[272,1280]{1,0:T(8,128)(2,1)S(1)}, bf16[272,1280]{1,0:T(8,128)(2,1)S(1)}, u32[]{:S(2)}, u32[]{:S(2)}) collective-permute-start(bf16[272,1280]{1,0:T(8,128)(2,1)S(1)} %get-tuple-element.66), channel_id=1, source_target_pairs={{0,12},{1,13},{2,14},{3,15},{4,0},{5,1},{6,2},{7,3},{8,4},{9,5},{1... | collective-permute-start | bytes 2088968 | tf_op jit(solution)/shard_map/ppermute | solution.py:35
  87.1 0.0 collective-permute-start.18
  87.1 1.6 %shard_map.66 = (bf16[256,1280]{1,0:T(8,128)(2,1)S(1)}, bf16[256,1280]{1,0:T(8,128)(2,1)S(1)}) custom-call(f32[1]{0:T(128)S(6)} %copy.6.scale, bf16[1024,1024]{1,0:T(8,128)(2,1)S(1)} %get-tuple-element.56.weights, bf16[1024,1280]{1,0:T(8,128)(2,1)S(1)} %get-tuple-element.48.images, bf16[512,1280]{1,0:T(8,128)(2,1)S(1)} %get-tuple-element.57.text_0, ...), custom_call_target="tpu_custom_call" | custom-call | tf_op jit(solution)/shard_map/pallas_call | solution.py:449
  88.7 15.2 %collective-permute-done.22.refs_2_ = bf16[336,1280]{1,0:T(8,128)(2,1)S(1)} collective-permute-done((bf16[336,1280]{1,0:T(8,128)(2,1)S(1)}, bf16[336,1280]{1,0:T(8,128)(2,1)S(1)}, u32[]{:S(2)}, u32[]{:S(2)}) %collective-permute-start.22) | collective-permute-done | bytes 860192 | tf_op jit(solution)/shard_map/ppermute | solution.py:44
  103.9 0.2 shard_map.71
  104.1 0.1 collective-permute-start.23
  104.2 0.6 collective-permute-start.24
  104.8 0.0 collective-permute-done.18.refs_3_
  104.8 0.4 shard_map.70
  105.2 1.8 %collective-permute-start.19 = (bf16[80,1280]{1,0:T(8,128)(2,1)S(1)}, bf16[80,1280]{1,0:T(8,128)(2,1)S(1)}, u32[]{:S(2)}, u32[]{:S(2)}) collective-permute-start(bf16[80,1280]{1,0:T(8,128)(2,1)S(1)} %get-tuple-element.69), channel_id=1, source_target_pairs={{0,2},{1,3},{2,0},{3,1},{4,6},{5,7},{6,4},{7,5},{8,10},{9,11},{10,... | collective-permute-start | bytes 614408 | tf_op jit(solution)/shard_map/ppermute | solution.py:35
  107.0 1.2 collective-permute-start.20
  108.1 0.9 collective-permute-start.21
  109.0 9.3 %collective-permute-done.24.refs_2_ = bf16[80,1280]{1,0:T(8,128)(2,1)S(1)} collective-permute-done((bf16[80,1280]{1,0:T(8,128)(2,1)S(1)}, bf16[80,1280]{1,0:T(8,128)(2,1)S(1)}, u32[]{:S(2)}, u32[]{:S(2)}) %collective-permute-start.24) | collective-permute-done | bytes 204832 | tf_op jit(solution)/shard_map/ppermute | solution.py:44
  118.3 0.1 shard_map.72
  118.4 0.1 collective-permute-start.25
  118.5 0.0 collective-permute-done.20.refs_2_
  118.6 1.4 %collective-permute-done.25.refs_5_ = bf16[80,1280]{1,0:T(8,128)(2,1)S(1)} collective-permute-done((bf16[80,1280]{1,0:T(8,128)(2,1)S(1)}, bf16[80,1280]{1,0:T(8,128)(2,1)S(1)}, u32[]{:S(2)}, u32[]{:S(2)}) %collective-permute-start.25) | collective-permute-done | bytes 204832 | tf_op jit(solution)/shard_map/ppermute | solution.py:48
  120.0 0.8 shard_map.73
  (14 shorter events, 0.1 us)
Async XLA Ops:
  0.6 1.7 %collective-permute-start = (bf16[64,1280]{1,0:T(8,128)(2,1)}, bf16[64,1280]{1,0:T(8,128)(2,1)S(1)}, u32[]{:S(2)}, u32[]{:S(2)}) collective-permute-start(bf16[64,1280]{1,0:T(8,128)(2,1)} %refs_0_.1), channel_id=1, source_target_pairs={{0,32},{32,0},{1,33},{33,1},{2,34},{34,2},{3,35},{35,3},{4,36},{36... | collective-permute-start | bytes 491528 | tf_op jit(solution)/shard_map/ppermute | solution.py:48
  2.3 0.9 copy-start.2
  3.2 0.9 copy-start.3
  4.2 17.8 %collective-permute-start.4 = (bf16[128,1280]{1,0:T(8,128)(2,1)S(1)}, bf16[128,1280]{1,0:T(8,128)(2,1)}, u32[]{:S(2)}, u32[]{:S(2)}) collective-permute-start(bf16[128,1280]{1,0:T(8,128)(2,1)S(1)} %get-tuple-element.43.refs_4_), channel_id=1, source_target_pairs={{0,208},{64,0},{128,64},{192,128},{16,192},{80,16},{144,80},{208,1... | collective-permute-start | bytes 983048 | tf_op jit(solution)/shard_map/ppermute | solution.py:44
  6.1 9.0 %collective-permute-start.5 = (bf16[64,1280]{1,0:T(8,128)(2,1)S(1)}, bf16[64,1280]{1,0:T(8,128)(2,1)S(1)}, u32[]{:S(2)}, u32[]{:S(2)}) collective-permute-start(bf16[64,1280]{1,0:T(8,128)(2,1)S(1)} %copy-done.3), channel_id=1, source_target_pairs={{0,144},{64,208},{128,0},{192,64},{16,128},{80,192},{144,16},{208,... | collective-permute-start | bytes 491528 | tf_op jit(solution)/shard_map/ppermute | solution.py:44
  10.7 7.4 %collective-permute-start.3 = (bf16[64,1280]{1,0:T(8,128)(2,1)S(1)}, bf16[64,1280]{1,0:T(8,128)(2,1)S(1)}, u32[]{:S(2)}, u32[]{:S(2)}) collective-permute-start(bf16[64,1280]{1,0:T(8,128)(2,1)S(1)} %get-tuple-element.42.refs_0_), channel_id=1, source_target_pairs={{0,3},{1,0},{2,1},{3,2},{4,7},{5,4},{6,5},{7,6},{8,11},{9,8},{10,9... | collective-permute-start | bytes 491528 | tf_op jit(solution)/shard_map/ppermute | solution.py:35
  13.4 6.9 %collective-permute-start.2 = (bf16[64,1280]{1,0:T(8,128)(2,1)S(1)}, bf16[64,1280]{1,0:T(8,128)(2,1)S(1)}, u32[]{:S(2)}, u32[]{:S(2)}) collective-permute-start(bf16[64,1280]{1,0:T(8,128)(2,1)S(1)} %get-tuple-element.42.refs_0_), channel_id=1, source_target_pairs={{0,2},{1,3},{2,0},{3,1},{4,6},{5,7},{6,4},{7,5},{8,10},{9,11},{10,... | collective-permute-start | bytes 491528 | tf_op jit(solution)/shard_map/ppermute | solution.py:35
  14.2 7.8 %collective-permute-start.1 = (bf16[64,1280]{1,0:T(8,128)(2,1)S(1)}, bf16[64,1280]{1,0:T(8,128)(2,1)S(1)}, u32[]{:S(2)}, u32[]{:S(2)}) collective-permute-start(bf16[64,1280]{1,0:T(8,128)(2,1)S(1)} %get-tuple-element.42.refs_0_), channel_id=1, source_target_pairs={{0,1},{1,2},{2,3},{3,0},{4,5},{5,6},{6,7},{7,4},{8,9},{9,10},{10,1... | collective-permute-start | bytes 491528 | tf_op jit(solution)/shard_map/ppermute | solution.py:35
  23.1 22.2 %copy-start = (bf16[320,1280]{1,0:T(8,128)(2,1)}, bf16[320,1280]{1,0:T(8,128)(2,1)S(1)}, u32[]{:S(2)}) copy-start(bf16[320,1280]{1,0:T(8,128)(2,1)S(1)} %get-tuple-element.45.refs_4_) | copy-start | bytes 2457604
  23.1 22.1 %collective-permute-start.9 = (bf16[320,1280]{1,0:T(8,128)(2,1)S(1)}, bf16[320,1280]{1,0:T(8,128)(2,1)S(1)}, u32[]{:S(2)}, u32[]{:S(2)}) collective-permute-start(bf16[320,1280]{1,0:T(8,128)(2,1)S(1)} %get-tuple-element.45.refs_4_), channel_id=1, source_target_pairs={{0,144},{64,208},{128,0},{192,64},{16,128},{80,192},{144,16},{208,... | collective-permute-start | bytes 2457608 | tf_op jit(solution)/shard_map/ppermute | solution.py:44
  24.6 12.2 %collective-permute-start.8 = (bf16[256,1280]{1,0:T(8,128)(2,1)S(1)}, bf16[256,1280]{1,0:T(8,128)(2,1)S(1)}, u32[]{:S(2)}, u32[]{:S(2)}) collective-permute-start(bf16[256,1280]{1,0:T(8,128)(2,1)S(1)} %get-tuple-element.44.refs_0_), channel_id=1, source_target_pairs={{0,8},{1,9},{2,10},{3,11},{4,12},{5,13},{6,14},{7,15},{8,0},{9,1},... | collective-permute-start | bytes 1966088 | tf_op jit(solution)/shard_map/ppermute | solution.py:35
  27.8 16.3 %collective-permute-start.7 = (bf16[256,1280]{1,0:T(8,128)(2,1)S(1)}, bf16[256,1280]{1,0:T(8,128)(2,1)S(1)}, u32[]{:S(2)}, u32[]{:S(2)}) collective-permute-start(bf16[256,1280]{1,0:T(8,128)(2,1)S(1)} %get-tuple-element.44.refs_0_), channel_id=1, source_target_pairs={{0,12},{1,13},{2,14},{3,15},{4,0},{5,1},{6,2},{7,3},{8,4},{9,5},{1... | collective-permute-start | bytes 1966088 | tf_op jit(solution)/shard_map/ppermute | solution.py:35
  28.9 15.2 %collective-permute-start.6 = (bf16[256,1280]{1,0:T(8,128)(2,1)S(1)}, bf16[256,1280]{1,0:T(8,128)(2,1)S(1)}, u32[]{:S(2)}, u32[]{:S(2)}) collective-permute-start(bf16[256,1280]{1,0:T(8,128)(2,1)S(1)} %get-tuple-element.44.refs_0_), channel_id=1, source_target_pairs={{0,4},{1,5},{2,6},{3,7},{4,8},{5,9},{6,10},{7,11},{8,12},{9,13},{1... | collective-permute-start | bytes 1966088 | tf_op jit(solution)/shard_map/ppermute | solution.py:35
  45.3 4.4 %collective-permute-start.10 = (bf16[320,1280]{1,0:T(8,128)(2,1)S(1)}, bf16[320,1280]{1,0:T(8,128)(2,1)}, u32[]{:S(2)}, u32[]{:S(2)}) collective-permute-start(bf16[320,1280]{1,0:T(8,128)(2,1)S(1)} %shard_map.60.refs_5_.text_1), channel_id=1, source_target_pairs={{0,32},{32,0},{1,33},{33,1},{2,34},{34,2},{3,35},{35,3},{4,36},{36... | collective-permute-start | bytes 2457608 | tf_op jit(solution)/shard_map/ppermute | solution.py:48
  45.4 4.3 %collective-permute-start.11 = (bf16[128,1280]{1,0:T(8,128)(2,1)}, bf16[128,1280]{1,0:T(8,128)(2,1)}, u32[]{:S(2)}, u32[]{:S(2)}) collective-permute-start(bf16[128,1280]{1,0:T(8,128)(2,1)} %collective-permute-done.4.refs_5_), channel_id=1, source_target_pairs={{0,32},{32,0},{1,33},{33,1},{2,34},{34,2},{3,35},{35,3},{4,36},{36... | collective-permute-start | bytes 983048 | tf_op jit(solution)/shard_map/ppermute | solution.py:48
  46.6 1.1 copy-start.1
  53.8 1.3 %collective-permute-start.12 = (f32[24,128]{1,0:T(8,128)S(1)}, f32[24,128]{1,0:T(8,128)S(1)}, u32[]{:S(2)}, u32[]{:S(2)}) collective-permute-start(f32[24,128]{1,0:T(8,128)S(1)} %get-tuple-element.53), channel_id=1, source_target_pairs={{0,32},{32,0},{1,33},{33,1},{2,34},{34,2},{3,35},{35,3},{4,36},{36... | collective-permute-start | bytes 36872 | tf_op jit(solution)/shard_map/ppermute | solution.py:48
  69.2 4.2 %collective-permute-start.13 = (f32[24,128]{1,0:T(8,128)S(1)}, f32[24,128]{1,0:T(8,128)S(1)}, u32[]{:S(2)}, u32[]{:S(2)}) collective-permute-start(f32[24,128]{1,0:T(8,128)S(1)} %get-tuple-element.55), channel_id=1, source_target_pairs={{0,32},{32,0},{1,33},{33,1},{2,34},{34,2},{3,35},{35,3},{4,36},{36... | collective-permute-start | bytes 36872 | tf_op jit(solution)/shard_map/ppermute | solution.py:48
  77.1 2.9 %collective-permute-start.14 = (bf16[256,1280]{1,0:T(8,128)(2,1)S(1)}, bf16[256,1280]{1,0:T(8,128)(2,1)S(1)}, u32[]{:S(2)}, u32[]{:S(2)}) collective-permute-start(bf16[256,1280]{1,0:T(8,128)(2,1)S(1)} %get-tuple-element.61), channel_id=1, source_target_pairs={{0,32},{32,0},{1,33},{33,1},{2,34},{34,2},{3,35},{35,3},{4,36},{36... | collective-permute-start | bytes 1966088 | tf_op jit(solution)/shard_map/ppermute | solution.py:48
  77.5 2.5 %collective-permute-start.15 = (bf16[192,1280]{1,0:T(8,128)(2,1)S(1)}, bf16[192,1280]{1,0:T(8,128)(2,1)S(1)}, u32[]{:S(2)}, u32[]{:S(2)}) collective-permute-start(bf16[192,1280]{1,0:T(8,128)(2,1)S(1)} %get-tuple-element.63), channel_id=1, source_target_pairs={{0,32},{32,0},{1,33},{33,1},{2,34},{34,2},{3,35},{35,3},{4,36},{36... | collective-permute-start | bytes 1474568 | tf_op jit(solution)/shard_map/ppermute | solution.py:48
  80.2 23.7 %collective-permute-start.22 = (bf16[336,1280]{1,0:T(8,128)(2,1)S(1)}, bf16[336,1280]{1,0:T(8,128)(2,1)S(1)}, u32[]{:S(2)}, u32[]{:S(2)}) collective-permute-start(bf16[336,1280]{1,0:T(8,128)(2,1)S(1)} %shard_map.68.after), channel_id=1, source_target_pairs={{0,128},{64,192},{128,16},{192,80},{16,144},{80,208},{144,0},{208,... | collective-permute-start | bytes 2580488 | tf_op jit(solution)/shard_map/ppermute | solution.py:44
  83.6 21.1 %collective-permute-start.16 = (bf16[272,1280]{1,0:T(8,128)(2,1)S(1)}, bf16[272,1280]{1,0:T(8,128)(2,1)S(1)}, u32[]{:S(2)}, u32[]{:S(2)}) collective-permute-start(bf16[272,1280]{1,0:T(8,128)(2,1)S(1)} %get-tuple-element.65), channel_id=1, source_target_pairs={{0,8},{1,9},{2,10},{3,11},{4,12},{5,13},{6,14},{7,15},{8,0},{9,1},... | collective-permute-start | bytes 2088968 | tf_op jit(solution)/shard_map/ppermute | solution.py:35
  84.3 20.5 %collective-permute-start.17 = (bf16[272,1280]{1,0:T(8,128)(2,1)S(1)}, bf16[272,1280]{1,0:T(8,128)(2,1)S(1)}, u32[]{:S(2)}, u32[]{:S(2)}) collective-permute-start(bf16[272,1280]{1,0:T(8,128)(2,1)S(1)} %get-tuple-element.66), channel_id=1, source_target_pairs={{0,12},{1,13},{2,14},{3,15},{4,0},{5,1},{6,2},{7,3},{8,4},{9,5},{1... | collective-permute-start | bytes 2088968 | tf_op jit(solution)/shard_map/ppermute | solution.py:35
  87.1 17.7 %collective-permute-start.18 = (bf16[272,1280]{1,0:T(8,128)(2,1)S(1)}, bf16[272,1280]{1,0:T(8,128)(2,1)S(1)}, u32[]{:S(2)}, u32[]{:S(2)}) collective-permute-start(bf16[272,1280]{1,0:T(8,128)(2,1)S(1)} %get-tuple-element.67), channel_id=1, source_target_pairs={{0,4},{1,5},{2,6},{3,7},{4,8},{5,9},{6,10},{7,11},{8,12},{9,13},{1... | collective-permute-start | bytes 2088968 | tf_op jit(solution)/shard_map/ppermute | solution.py:35
  104.1 14.2 %collective-permute-start.23 = (bf16[144,1280]{1,0:T(8,128)(2,1)S(1)}, bf16[144,1280]{1,0:T(8,128)(2,1)S(1)}, u32[]{:S(2)}, u32[]{:S(2)}) collective-permute-start(bf16[144,1280]{1,0:T(8,128)(2,1)S(1)} %get-tuple-element.74), channel_id=1, source_target_pairs={{0,64},{64,128},{128,192},{192,16},{16,80},{80,144},{144,208},{208... | collective-permute-start | bytes 1105928 | tf_op jit(solution)/shard_map/ppermute | solution.py:44
  104.2 14.1 %collective-permute-start.24 = (bf16[80,1280]{1,0:T(8,128)(2,1)S(1)}, bf16[80,1280]{1,0:T(8,128)(2,1)S(1)}, u32[]{:S(2)}, u32[]{:S(2)}) collective-permute-start(bf16[80,1280]{1,0:T(8,128)(2,1)S(1)} %get-tuple-element.75), channel_id=1, source_target_pairs={{0,128},{64,192},{128,16},{192,80},{16,144},{80,208},{144,0},{208,... | collective-permute-start | bytes 614408 | tf_op jit(solution)/shard_map/ppermute | solution.py:44
  105.2 13.4 %collective-permute-start.19 = (bf16[80,1280]{1,0:T(8,128)(2,1)S(1)}, bf16[80,1280]{1,0:T(8,128)(2,1)S(1)}, u32[]{:S(2)}, u32[]{:S(2)}) collective-permute-start(bf16[80,1280]{1,0:T(8,128)(2,1)S(1)} %get-tuple-element.69), channel_id=1, source_target_pairs={{0,2},{1,3},{2,0},{3,1},{4,6},{5,7},{6,4},{7,5},{8,10},{9,11},{10,... | collective-permute-start | bytes 614408 | tf_op jit(solution)/shard_map/ppermute | solution.py:35
  107.0 11.6 %collective-permute-start.20 = (bf16[80,1280]{1,0:T(8,128)(2,1)S(1)}, bf16[80,1280]{1,0:T(8,128)(2,1)S(1)}, u32[]{:S(2)}, u32[]{:S(2)}) collective-permute-start(bf16[80,1280]{1,0:T(8,128)(2,1)S(1)} %get-tuple-element.70), channel_id=1, source_target_pairs={{0,3},{1,0},{2,1},{3,2},{4,7},{5,4},{6,5},{7,6},{8,11},{9,8},{10,9... | collective-permute-start | bytes 614408 | tf_op jit(solution)/shard_map/ppermute | solution.py:35
  108.1 10.4 %collective-permute-start.21 = (bf16[80,1280]{1,0:T(8,128)(2,1)S(1)}, bf16[80,1280]{1,0:T(8,128)(2,1)S(1)}, u32[]{:S(2)}, u32[]{:S(2)}) collective-permute-start(bf16[80,1280]{1,0:T(8,128)(2,1)S(1)} %get-tuple-element.71), channel_id=1, source_target_pairs={{0,1},{1,2},{2,3},{3,0},{4,5},{5,6},{6,7},{7,4},{8,9},{9,10},{10,1... | collective-permute-start | bytes 614408 | tf_op jit(solution)/shard_map/ppermute | solution.py:35
  118.4 1.5 %collective-permute-start.25 = (bf16[80,1280]{1,0:T(8,128)(2,1)S(1)}, bf16[80,1280]{1,0:T(8,128)(2,1)S(1)}, u32[]{:S(2)}, u32[]{:S(2)}) collective-permute-start(bf16[80,1280]{1,0:T(8,128)(2,1)S(1)} %get-tuple-element.77), channel_id=1, source_target_pairs={{0,32},{32,0},{1,33},{33,1},{2,34},{34,2},{3,35},{35,3},{4,36},{36... | collective-permute-start | bytes 614408 | tf_op jit(solution)/shard_map/ppermute | solution.py:48

commit v11 on v9

--- a/solution.py
+++ b/solution.py
@@ -298,7 +298,7 @@
     row_wide, row_lse, col_lse = refs[4:]
     first = place[1] == 0
     shares = jnp.where(first, mine[16:17, :], other[16:17, :]), jnp.where(first, other[16:17, :], mine[16:17, :])
-    for i, share in enumerate(shares):
+    for i, share in enumerate((*shares, jnp.where(first, shares[0], 0.0))):
         tail = digits_of(share).astype(BF16)
         for e in range(EMBED // 128):
             outs[2][i * TAIL : (i + 1) * TAIL, e * 128 : (e + 1) * 128] = tail
@@ -361,7 +361,7 @@
             jax.ShapeDtypeStruct((BLOCK, BLOCK), BF16),
             PART,
             jax.ShapeDtypeStruct((3 * ROWS, EMBED), BF16),
-            jax.ShapeDtypeStruct((2 * TAIL, EMBED), BF16),
+            jax.ShapeDtypeStruct((3 * TAIL, EMBED), BF16),
         ),
         in_specs=[SMEM, SMEM] + [VMEM] * 4,
         out_specs=(VMEM,) * 4,
@@ -391,7 +391,7 @@
 def image_body(scale, after, digits, weights, texts, *outs):
     image_terms(scale[0], weights, texts, dict(zip((2, 1, 3), outs)))
     for out in outs:
-        out[CHUNK:, :] = digits[TAIL:, :]
+        out[CHUNK:, :] = digits[TAIL : 2 * TAIL, :]
 
 
 def image_call(scale, after, digits, weights, texts):
@@ -495,26 +495,31 @@
 
     other_1, other_3 = core_swap(text_2), core_swap(text_3)
     text_1, far = text_call(logit_scale, weights, images)
-    pairs = sums(
+    pairs, far = sums(
         [text_1, other_1, far, other_3, digits],
-        ((256, ((0, 0), (1, 0))), (64, ((2, 0), (3, 128))), (TAIL, ((4, 0),))),
-    )[0]
+        ((256, ((0, 0), (1, 0))), (TAIL, ((4, 0),))),
+        ((64, ((2, 0), (3, 128))), (TAIL, ((4, 2 * TAIL),))),
+    )
     image_parts = image_call(logit_scale, pairs, digits, weights, texts)
-    pairs = z_shift(pairs, 2)
+    pairs, far = z_shift(pairs, 2), z_shift(far, 3)
     back = [plane_shift(v, -k, False) for v, k in zip(image_parts, (2, 1, 3))]
     text_0, image_0 = rest_call(logit_scale, weights, images, texts)
 
-    rows_tail = (TAIL, ((2, 320), (3, 0)))
-    next_1, mine, next_4 = sums(
-        [text_0, other_3, pairs, digits],
-        ((128, ((0, 128), (1, 0), (2, 128))), rows_tail),
-        ((128, ((0, 0), (2, 0))), rows_tail),
-        ((80, ((2, 256),)),),
-    )
-    next_1, next_4 = z_shift(next_1, 1), z_shift(next_4, 2)
-    (other,) = sums([mine, next_1], ((64, ((0, 64), (1, 64))), (TAIL, ((0, 128), (1, 128)))))
-    (mine,) = sums(
-        [mine, next_1, next_4], ((64, ((0, 0), (1, 0), (2, 0))), (TAIL, ((0, 128), (1, 128), (2, 64))))
+    next_1, mine = sums(
+        [text_0, other_3, pairs, far, digits],
+        (
+            (64, ((0, 128), (1, 0), (2, 128), (3, 0))),
+            (64, ((0, 192), (1, 64), (2, 192))),
+            (TAIL, ((2, 256), (3, 64), (4, 0))),
+        ),
+        ((128, ((0, 0), (2, 0))), (TAIL, ((2, 256), (4, 0)))),
+    )
+    next_1 = z_shift(next_1, 1)
+    rows_tail = (TAIL, ((0, 128), (1, 128)))
+    mine, other = sums(
+        [mine, next_1],
+        ((64, ((0, 0), (1, 0))), rows_tail),
+        ((64, ((0, 64), (1, 64))), rows_tail),
     )
 
     cols_tail = (TAIL, ((1, 256), (2, 256), (3, 256), (4, 16)))

time: 118 us -> 120 us (1.017); the launches traced: 116 us -> 120 us
  starting transfers between devices: 32.3 us -> 34.9 us
    ppermute x12, waiting for transfers between devices: 1.03 us -> 5.27 us  [plane_shift(): return lax.ppermute(v, ('core', 'zh', 'y', 'x'), pairs)]
    ppermute x6, waiting for transfers between devices: 39.9 us -> 36.1 us  [z_shift(): return lax.ppermute(v, ('zl', 'core', 'zh'), pairs)]
    ppermute x6, starting transfers between devices: 11.1 us -> 13.7 us  [z_shift(): return lax.ppermute(v, ('zl', 'core', 'zh'), pairs)]
  transfers between devices with their start and end apart: 26 -> 26, of which waited for: 11 -> 13; matrix products, arithmetic and copies ran while one was open for 0% -> 0% of each run, Pallas kernels for 6% -> 5%
where the time goes in v11:
time: 120 us
  waiting for transfers between devices  47 us (39%)
  starting transfers between devices  34.9 us (29%)
  Pallas kernels  19.5 us (16%)
  blocking collectives  14.9 us (12%)
  local copies, waits for them, and re-layouts  1.92 us (2%)
  between operations  1.4 us (1%)
    ppermute x6, waiting for transfers between devices, z_shift(): return lax.ppermute(v, ('zl', 'core', 'zh'), pairs)  36.1 us
    ppermute x12, starting transfers between devices, plane_shift(): return lax.ppermute(v, ('core', 'zh', 'y', 'x'), pairs)  17.5 us
    all_to_all x1, blocking collectives, exchange(): return lax.all_to_all(v, AXES, 0, 0, axis_index_groups=groups)  14.9 us
    ppermute x6, starting transfers between devices, z_shift(): return lax.ppermute(v, ('zl', 'core', 'zh'), pairs)  13.7 us
    pallas_call x1, Pallas kernels, logits_call(): pl.pallas_call(logits_body, out_shape=(jax.ShapeDtypeStruct((BLOCK, BLOCK...  6.13 us
    ppermute x8, waiting for transfers between devices, core_swap(): return lax.ppermute(v, 'core', [(0, 1), (1, 0)])  5.63 us
    ppermute x12, waiting for transfers between devices, plane_shift(): return lax.ppermute(v, ('core', 'zh', 'y', 'x'), pairs)  5.27 us
    ppermute x8, starting transfers between devices, core_swap(): return lax.ppermute(v, 'core', [(0, 1), (1, 0)])  3.71 us
  transfers between devices with their start and end apart: 26, of which 13 were waited for; matrix products, arithmetic and copies ran while one was open for 0% of the time, Pallas kernels for 5%

profile of v11, /device:TPU:32, one launch (start us, length us, event | category | flops | bytes accessed | tf_op | source)
XLA Modules:
  0.0 119.6 jit_solution(16064187281945553113)
XLA Ops:
  0.6 0.1 collective-permute-start
  0.7 1.6 %collective-permute-done.refs_1_ = bf16[64,1280]{1,0:T(8,128)(2,1)S(1)} collective-permute-done((bf16[64,1280]{1,0:T(8,128)(2,1)}, bf16[64,1280]{1,0:T(8,128)(2,1)S(1)}, u32[]{:S(2)}, u32[]{:S(2)}) %collective-permute-start) | collective-permute-done | bytes 163872 | tf_op jit(solution)/shard_map/ppermute | solution.py:48
  2.3 0.9 copy-done
  3.2 0.9 copy-done.1
  4.2 1.9 %collective-permute-start.4 = (bf16[128,1280]{1,0:T(8,128)(2,1)S(1)}, bf16[128,1280]{1,0:T(8,128)(2,1)S(1)}, u32[]{:S(2)}, u32[]{:S(2)}) collective-permute-start(bf16[128,1280]{1,0:T(8,128)(2,1)S(1)} %get-tuple-element.42.refs_4_), channel_id=1, source_target_pairs={{0,208},{64,0},{128,64},{192,128},{16,192},{80,16},{144,80},{208,1... | collective-permute-start | bytes 983048 | tf_op jit(solution)/shard_map/ppermute | solution.py:44
  6.1 5.5 %collective-permute-start.5 = (bf16[64,1280]{1,0:T(8,128)(2,1)S(1)}, bf16[64,1280]{1,0:T(8,128)(2,1)S(1)}, u32[]{:S(2)}, u32[]{:S(2)}) collective-permute-start(bf16[64,1280]{1,0:T(8,128)(2,1)S(1)} %copy-done.1), channel_id=1, source_target_pairs={{0,16},{64,80},{128,144},{192,208},{16,0},{80,64},{144,128},{208,1... | collective-permute-start | bytes 491528 | tf_op jit(solution)/shard_map/ppermute | solution.py:44
  11.6 2.8 %collective-permute-start.3 = (bf16[64,1280]{1,0:T(8,128)(2,1)S(1)}, bf16[64,1280]{1,0:T(8,128)(2,1)S(1)}, u32[]{:S(2)}, u32[]{:S(2)}) collective-permute-start(bf16[64,1280]{1,0:T(8,128)(2,1)S(1)} %get-tuple-element.41.refs_0_), channel_id=1, source_target_pairs={{0,3},{1,0},{2,1},{3,2},{4,7},{5,4},{6,5},{7,6},{8,11},{9,8},{10,9... | collective-permute-start | bytes 491528 | tf_op jit(solution)/shard_map/ppermute | solution.py:35
  14.3 0.8 collective-permute-start.2
  15.1 0.9 collective-permute-start.1
  16.0 7.1 %collective-permute-done.5.refs_6_.refs_8_ = bf16[64,1280]{1,0:T(8,128)(2,1)S(1)} collective-permute-done((bf16[64,1280]{1,0:T(8,128)(2,1)S(1)}, bf16[64,1280]{1,0:T(8,128)(2,1)S(1)}, u32[]{:S(2)}, u32[]{:S(2)}) %collective-permute-start.5) | collective-permute-done | bytes 163872 | tf_op jit(solution)/shard_map/ppermute | solution.py:44
  23.1 0.0 collective-permute-done.3.refs_3_
  23.1 0.0 collective-permute-done.2.refs_2_
  23.1 0.0 collective-permute-done.1.refs_1_
  23.1 0.0 collective-permute-done.4.refs_5_
  23.1 0.9 shard_map.59
  24.0 1.9 %collective-permute-start.9 = (bf16[256,1280]{1,0:T(8,128)(2,1)S(1)}, bf16[256,1280]{1,0:T(8,128)(2,1)S(1)}, u32[]{:S(2)}, u32[]{:S(2)}) collective-permute-start(bf16[256,1280]{1,0:T(8,128)(2,1)S(1)} %get-tuple-element.44.refs_4_), channel_id=1, source_target_pairs={{0,144},{64,208},{128,0},{192,64},{16,128},{80,192},{144,16},{208,... | collective-permute-start | bytes 1966088 | tf_op jit(solution)/shard_map/ppermute | solution.py:44
  25.9 3.2 %collective-permute-start.8 = (bf16[256,1280]{1,0:T(8,128)(2,1)S(1)}, bf16[256,1280]{1,0:T(8,128)(2,1)S(1)}, u32[]{:S(2)}, u32[]{:S(2)}) collective-permute-start(bf16[256,1280]{1,0:T(8,128)(2,1)S(1)} %get-tuple-element.43.refs_0_), channel_id=1, source_target_pairs={{0,8},{1,9},{2,10},{3,11},{4,12},{5,13},{6,14},{7,15},{8,0},{9,1},... | collective-permute-start | bytes 1966088 | tf_op jit(solution)/shard_map/ppermute | solution.py:35
  29.1 1.1 collective-permute-start.7
  30.1 1.0 collective-permute-start.6
  31.1 10.3 %collective-permute-done.9.refs_5_ = bf16[256,1280]{1,0:T(8,128)(2,1)S(1)} collective-permute-done((bf16[256,1280]{1,0:T(8,128)(2,1)S(1)}, bf16[256,1280]{1,0:T(8,128)(2,1)S(1)}, u32[]{:S(2)}, u32[]{:S(2)}) %collective-permute-start.9) | collective-permute-done | bytes 655392 | tf_op jit(solution)/shard_map/ppermute | solution.py:44
  41.4 0.0 collective-permute-start.10
  41.4 0.5 collective-permute-start.11
  42.6 0.1 stack.23.place
  42.7 1.7 %collective-permute-done.11.refs_7_ = bf16[192,1280]{1,0:T(8,128)(2,1)} collective-permute-done((bf16[192,1280]{1,0:T(8,128)(2,1)}, bf16[192,1280]{1,0:T(8,128)(2,1)}, u32[]{:S(2)}, u32[]{:S(2)}) %collective-permute-start.11) | collective-permute-done | bytes 491552 | tf_op jit(solution)/shard_map/ppermute | solution.py:48
  44.4 0.0 collective-permute-done.8.refs_3_
  44.4 1.0 collective-permute-done.7.refs_2_
  45.4 0.0 collective-permute-done.6.refs_1_
  45.4 0.0 collective-permute-done.10.refs_6_
  45.4 6.1 %shard_map.60 = (f32[1024,1024]{1,0:T(8,128)S(1)}, f32[16,128]{1,0:T(8,128)S(1)}, f32[16,128]{1,0:T(8,128)S(1)}, f32[24,128]{1,0:T(8,128)S(1)}, f32[8,128]{1,0:T...) custom-call(s32[5]{0:T(128)S(1)} %stack.23.place, f32[1]{0:T(128)S(6)} %copy.6.scale, ...), custom_call_target="tpu_custom_call" | custom-call | tf_op jit(solution)/shard_map/pallas_call | solution.py:192
  51.5 0.3 collective-permute-start.12
  51.8 1.2 collective-permute-done.12.got
  53.0 0.6 shard_map.61
  53.6 14.9 %all_to_all.5.got = f32[16,24,128]{2,1,0:T(8,128)S(1)} all-to-all(f32[16,24,128]{2,1,0:T(8,128)S(1)} %shard_map.61), channel_id=1, replica_groups={{0,1,2,3,4,5,6,7,8,9,10,11,12,13,14,15},{64,65,66,67,68,69,70,71,72,73,..., dimensions={0} | all-to-all | bytes 393216 | tf_op jit(solution)/shard_map/all_to_all | solution.py:63
  68.5 0.7 shard_map.62
  69.2 2.1 %collective-permute-start.13 = (f32[24,128]{1,0:T(8,128)S(1)}, f32[24,128]{1,0:T(8,128)S(1)}, u32[]{:S(2)}, u32[]{:S(2)}) collective-permute-start(f32[24,128]{1,0:T(8,128)S(1)} %get-tuple-element.52), channel_id=1, source_target_pairs={{0,32},{32,0},{1,33},{33,1},{2,34},{34,2},{3,35},{35,3},{4,36},{36... | collective-permute-start | bytes 36872 | tf_op jit(solution)/shard_map/ppermute | solution.py:48
  71.4 0.8 collective-permute-done.13.other
  72.2 3.7 %shard_map.63 = (bf16[1024,1024]{1,0:T(8,128)(2,1)S(1)}, bf16[256,1280]{1,0:T(8,128)(2,1)S(1)}, bf16[192,1280]{1,0:T(8,128)(2,1)S(1)}, bf16[48,1280]{1,0:T(8,128)(2,1)S(1)}) custom-call(s32[5]{0:T(128)S(1)} %stack.23.place, f32[1]{0:T(128)S(6)} %copy.6.scale, f32[1024,1024]{1,0:T(8,128)S(1)} %get-tuple-element.46.logits, ...), custom_call_target="tpu_custom_call" | custom-call | tf_op jit(solution)/shard_map/pallas_call | solution.py:358
  75.9 0.4 collective-permute-start.14
  76.3 0.2 collective-permute-start.15
  76.5 2.0 %shard_map.65 = (bf16[256,1280]{1,0:T(8,128)(2,1)S(1)}, bf16[64,1280]{1,0:T(8,128)(2,1)S(1)}) custom-call(f32[1]{0:T(128)S(6)} %copy.6.scale, bf16[1024,1024]{1,0:T(8,128)(2,1)S(1)} %get-tuple-element.54.weights, bf16[1024,1280]{1,0:T(8,128)(2,1)S(1)} %get-tuple-element.53.images), custom_call_target="tpu_custom_call" | custom-call | tf_op jit(solution)/shard_map/pallas_call | solution.py:382
  78.4 0.3 collective-permute-done.15.refs_3_.refs_1_
  78.8 0.2 shard_map.66
  79.0 1.1 collective-permute-start.22
  80.0 2.2 %shard_map.67 = (bf16[272,1280]{1,0:T(8,128)(2,1)S(1)}, bf16[272,1280]{1,0:T(8,128)(2,1)S(1)}, bf16[272,1280]{1,0:T(8,128)(2,1)S(1)}) custom-call(f32[1]{0:T(128)S(6)} %copy.6.scale, bf16[272,1280]{1,0:T(8,128)(2,1)S(1)} %get-tuple-element.62.after, bf16[48,1280]{1,0:T(8,128)(2,1)S(1)} %get-tuple-element.61.refs_4_.digits.refs_6_, ...), custom_call_target="tpu_custom_call" | custom-call | tf_op jit(solution)/shard_map/pallas_call | solution.py:398
  82.2 0.6 collective-permute-start.16
  82.9 2.8 %collective-permute-start.17 = (bf16[272,1280]{1,0:T(8,128)(2,1)S(1)}, bf16[272,1280]{1,0:T(8,128)(2,1)S(1)}, u32[]{:S(2)}, u32[]{:S(2)}) collective-permute-start(bf16[272,1280]{1,0:T(8,128)(2,1)S(1)} %get-tuple-element.64), channel_id=1, source_target_pairs={{0,12},{1,13},{2,14},{3,15},{4,0},{5,1},{6,2},{7,3},{8,4},{9,5},{1... | collective-permute-start | bytes 2088968 | tf_op jit(solution)/shard_map/ppermute | solution.py:35
  85.7 2.3 %collective-permute-start.23 = (bf16[80,1280]{1,0:T(8,128)(2,1)S(1)}, bf16[80,1280]{1,0:T(8,128)(2,1)S(1)}, u32[]{:S(2)}, u32[]{:S(2)}) collective-permute-start(bf16[80,1280]{1,0:T(8,128)(2,1)S(1)} %get-tuple-element.71), channel_id=1, source_target_pairs={{0,192},{64,16},{128,80},{192,144},{16,208},{80,0},{144,64},{208,1... | collective-permute-start | bytes 614408 | tf_op jit(solution)/shard_map/ppermute | solution.py:44
  87.9 1.6 %shard_map.64 = (bf16[256,1280]{1,0:T(8,128)(2,1)S(1)}, bf16[256,1280]{1,0:T(8,128)(2,1)S(1)}) custom-call(f32[1]{0:T(128)S(6)} %copy.6.scale, bf16[1024,1024]{1,0:T(8,128)(2,1)S(1)} %get-tuple-element.54.weights, bf16[1024,1280]{1,0:T(8,128)(2,1)S(1)} %get-tuple-element.53.images, bf16[1024,1280]{1,0:T(8,128)(2,1)S(1)} %get-tuple-element.55.texts), custom_call_target="tpu_custom_call" | custom-call | tf_op jit(solution)/shard_map/pallas_call | solution.py:413
  89.5 17.0 %collective-permute-done.23.refs_3_ = bf16[80,1280]{1,0:T(8,128)(2,1)S(1)} collective-permute-done((bf16[80,1280]{1,0:T(8,128)(2,1)S(1)}, bf16[80,1280]{1,0:T(8,128)(2,1)S(1)}, u32[]{:S(2)}, u32[]{:S(2)}) %collective-permute-start.23) | collective-permute-done | bytes 204832 | tf_op jit(solution)/shard_map/ppermute | solution.py:44
  106.6 0.2 shard_map.69
  106.8 1.1 collective-permute-start.24
  107.9 0.0 collective-permute-done.18.refs_3_
  107.9 0.4 shard_map.68
  108.3 2.4 %collective-permute-start.19 = (bf16[80,1280]{1,0:T(8,128)(2,1)S(1)}, bf16[80,1280]{1,0:T(8,128)(2,1)S(1)}, u32[]{:S(2)}, u32[]{:S(2)}) collective-permute-start(bf16[80,1280]{1,0:T(8,128)(2,1)S(1)} %get-tuple-element.67), channel_id=1, source_target_pairs={{0,2},{1,3},{2,0},{3,1},{4,6},{5,7},{6,4},{7,5},{8,10},{9,11},{10,... | collective-permute-start | bytes 614408 | tf_op jit(solution)/shard_map/ppermute | solution.py:35
  110.7 1.1 collective-permute-start.20
  111.9 0.9 collective-permute-start.21
  112.8 1.6 %collective-permute-done.24.refs_1_ = bf16[144,1280]{1,0:T(8,128)(2,1)S(1)} collective-permute-done((bf16[144,1280]{1,0:T(8,128)(2,1)S(1)}, bf16[144,1280]{1,0:T(8,128)(2,1)S(1)}, u32[]{:S(2)}, u32[]{:S(2)}) %collective-permute-start.24) | collective-permute-done | bytes 368672 | tf_op jit(solution)/shard_map/ppermute | solution.py:44
  114.4 0.1 shard_map.70
  114.5 0.1 collective-permute-start.25
  114.6 1.1 collective-permute-done.19.refs_1_
  115.7 1.6 %collective-permute-done.20.refs_2_ = bf16[80,1280]{1,0:T(8,128)(2,1)S(1)} collective-permute-done((bf16[80,1280]{1,0:T(8,128)(2,1)S(1)}, bf16[80,1280]{1,0:T(8,128)(2,1)S(1)}, u32[]{:S(2)}, u32[]{:S(2)}) %collective-permute-start.20) | collective-permute-done | bytes 204832 | tf_op jit(solution)/shard_map/ppermute | solution.py:35
  117.2 1.6 %collective-permute-done.21.refs_3_ = bf16[80,1280]{1,0:T(8,128)(2,1)S(1)} collective-permute-done((bf16[80,1280]{1,0:T(8,128)(2,1)S(1)}, bf16[80,1280]{1,0:T(8,128)(2,1)S(1)}, u32[]{:S(2)}, u32[]{:S(2)}) %collective-permute-start.21) | collective-permute-done | bytes 204832 | tf_op jit(solution)/shard_map/ppermute | solution.py:35
  118.8 0.0 collective-permute-done.25.refs_5_
  118.8 0.8 shard_map.71
  (8 shorter events, 0.0 us)
Async XLA Ops:
  0.6 1.7 %collective-permute-start = (bf16[64,1280]{1,0:T(8,128)(2,1)}, bf16[64,1280]{1,0:T(8,128)(2,1)S(1)}, u32[]{:S(2)}, u32[]{:S(2)}) collective-permute-start(bf16[64,1280]{1,0:T(8,128)(2,1)} %refs_0_.1), channel_id=1, source_target_pairs={{0,32},{32,0},{1,33},{33,1},{2,34},{34,2},{3,35},{35,3},{4,36},{36... | collective-permute-start | bytes 491528 | tf_op jit(solution)/shard_map/ppermute | solution.py:48
  2.3 0.9 copy-start
  3.2 0.9 copy-start.1
  4.2 18.9 %collective-permute-start.4 = (bf16[128,1280]{1,0:T(8,128)(2,1)S(1)}, bf16[128,1280]{1,0:T(8,128)(2,1)S(1)}, u32[]{:S(2)}, u32[]{:S(2)}) collective-permute-start(bf16[128,1280]{1,0:T(8,128)(2,1)S(1)} %get-tuple-element.42.refs_4_), channel_id=1, source_target_pairs={{0,208},{64,0},{128,64},{192,128},{16,192},{80,16},{144,80},{208,1... | collective-permute-start | bytes 983048 | tf_op jit(solution)/shard_map/ppermute | solution.py:44
  6.1 17.0 %collective-permute-start.5 = (bf16[64,1280]{1,0:T(8,128)(2,1)S(1)}, bf16[64,1280]{1,0:T(8,128)(2,1)S(1)}, u32[]{:S(2)}, u32[]{:S(2)}) collective-permute-start(bf16[64,1280]{1,0:T(8,128)(2,1)S(1)} %copy-done.1), channel_id=1, source_target_pairs={{0,16},{64,80},{128,144},{192,208},{16,0},{80,64},{144,128},{208,1... | collective-permute-start | bytes 491528 | tf_op jit(solution)/shard_map/ppermute | solution.py:44
  11.6 11.5 %collective-permute-start.3 = (bf16[64,1280]{1,0:T(8,128)(2,1)S(1)}, bf16[64,1280]{1,0:T(8,128)(2,1)S(1)}, u32[]{:S(2)}, u32[]{:S(2)}) collective-permute-start(bf16[64,1280]{1,0:T(8,128)(2,1)S(1)} %get-tuple-element.41.refs_0_), channel_id=1, source_target_pairs={{0,3},{1,0},{2,1},{3,2},{4,7},{5,4},{6,5},{7,6},{8,11},{9,8},{10,9... | collective-permute-start | bytes 491528 | tf_op jit(solution)/shard_map/ppermute | solution.py:35
  14.3 8.8 %collective-permute-start.2 = (bf16[64,1280]{1,0:T(8,128)(2,1)S(1)}, bf16[64,1280]{1,0:T(8,128)(2,1)S(1)}, u32[]{:S(2)}, u32[]{:S(2)}) collective-permute-start(bf16[64,1280]{1,0:T(8,128)(2,1)S(1)} %get-tuple-element.41.refs_0_), channel_id=1, source_target_pairs={{0,2},{1,3},{2,0},{3,1},{4,6},{5,7},{6,4},{7,5},{8,10},{9,11},{10,... | collective-permute-start | bytes 491528 | tf_op jit(solution)/shard_map/ppermute | solution.py:35
  15.1 8.0 %collective-permute-start.1 = (bf16[64,1280]{1,0:T(8,128)(2,1)S(1)}, bf16[64,1280]{1,0:T(8,128)(2,1)S(1)}, u32[]{:S(2)}, u32[]{:S(2)}) collective-permute-start(bf16[64,1280]{1,0:T(8,128)(2,1)S(1)} %get-tuple-element.41.refs_0_), channel_id=1, source_target_pairs={{0,1},{1,2},{2,3},{3,0},{4,5},{5,6},{6,7},{7,4},{8,9},{9,10},{10,1... | collective-permute-start | bytes 491528 | tf_op jit(solution)/shard_map/ppermute | solution.py:35
  24.0 17.4 %collective-permute-start.9 = (bf16[256,1280]{1,0:T(8,128)(2,1)S(1)}, bf16[256,1280]{1,0:T(8,128)(2,1)S(1)}, u32[]{:S(2)}, u32[]{:S(2)}) collective-permute-start(bf16[256,1280]{1,0:T(8,128)(2,1)S(1)} %get-tuple-element.44.refs_4_), channel_id=1, source_target_pairs={{0,144},{64,208},{128,0},{192,64},{16,128},{80,192},{144,16},{208,... | collective-permute-start | bytes 1966088 | tf_op jit(solution)/shard_map/ppermute | solution.py:44
  25.9 18.5 %collective-permute-start.8 = (bf16[256,1280]{1,0:T(8,128)(2,1)S(1)}, bf16[256,1280]{1,0:T(8,128)(2,1)S(1)}, u32[]{:S(2)}, u32[]{:S(2)}) collective-permute-start(bf16[256,1280]{1,0:T(8,128)(2,1)S(1)} %get-tuple-element.43.refs_0_), channel_id=1, source_target_pairs={{0,8},{1,9},{2,10},{3,11},{4,12},{5,13},{6,14},{7,15},{8,0},{9,1},... | collective-permute-start | bytes 1966088 | tf_op jit(solution)/shard_map/ppermute | solution.py:35
  29.1 16.3 %collective-permute-start.7 = (bf16[256,1280]{1,0:T(8,128)(2,1)S(1)}, bf16[256,1280]{1,0:T(8,128)(2,1)S(1)}, u32[]{:S(2)}, u32[]{:S(2)}) collective-permute-start(bf16[256,1280]{1,0:T(8,128)(2,1)S(1)} %get-tuple-element.43.refs_0_), channel_id=1, source_target_pairs={{0,12},{1,13},{2,14},{3,15},{4,0},{5,1},{6,2},{7,3},{8,4},{9,5},{1... | collective-permute-start | bytes 1966088 | tf_op jit(solution)/shard_map/ppermute | solution.py:35
  30.1 15.2 %collective-permute-start.6 = (bf16[256,1280]{1,0:T(8,128)(2,1)S(1)}, bf16[256,1280]{1,0:T(8,128)(2,1)}, u32[]{:S(2)}, u32[]{:S(2)}) collective-permute-start(bf16[256,1280]{1,0:T(8,128)(2,1)S(1)} %get-tuple-element.43.refs_0_), channel_id=1, source_target_pairs={{0,4},{1,5},{2,6},{3,7},{4,8},{5,9},{6,10},{7,11},{8,12},{9,13},{1... | collective-permute-start | bytes 1966088 | tf_op jit(solution)/shard_map/ppermute | solution.py:35
  41.4 4.0 %collective-permute-start.10 = (bf16[256,1280]{1,0:T(8,128)(2,1)S(1)}, bf16[256,1280]{1,0:T(8,128)(2,1)}, u32[]{:S(2)}, u32[]{:S(2)}) collective-permute-start(bf16[256,1280]{1,0:T(8,128)(2,1)S(1)} %collective-permute-done.9.refs_5_), channel_id=1, source_target_pairs={{0,32},{32,0},{1,33},{33,1},{2,34},{34,2},{3,35},{35,3},{4,36},{36... | collective-permute-start | bytes 1966088 | tf_op jit(solution)/shard_map/ppermute | solution.py:48
  41.4 2.9 %collective-permute-start.11 = (bf16[192,1280]{1,0:T(8,128)(2,1)}, bf16[192,1280]{1,0:T(8,128)(2,1)}, u32[]{:S(2)}, u32[]{:S(2)}) collective-permute-start(bf16[192,1280]{1,0:T(8,128)(2,1)} %get-tuple-element.45), channel_id=1, source_target_pairs={{0,32},{32,0},{1,33},{33,1},{2,34},{34,2},{3,35},{35,3},{4,36},{36... | collective-permute-start | bytes 1474568 | tf_op jit(solution)/shard_map/ppermute | solution.py:48
  51.5 1.4 %collective-permute-start.12 = (f32[24,128]{1,0:T(8,128)S(1)}, f32[24,128]{1,0:T(8,128)S(1)}, u32[]{:S(2)}, u32[]{:S(2)}) collective-permute-start(f32[24,128]{1,0:T(8,128)S(1)} %get-tuple-element.50), channel_id=1, source_target_pairs={{0,32},{32,0},{1,33},{33,1},{2,34},{34,2},{3,35},{35,3},{4,36},{36... | collective-permute-start | bytes 36872 | tf_op jit(solution)/shard_map/ppermute | solution.py:48
  69.2 3.0 %collective-permute-start.13 = (f32[24,128]{1,0:T(8,128)S(1)}, f32[24,128]{1,0:T(8,128)S(1)}, u32[]{:S(2)}, u32[]{:S(2)}) collective-permute-start(f32[24,128]{1,0:T(8,128)S(1)} %get-tuple-element.52), channel_id=1, source_target_pairs={{0,32},{32,0},{1,33},{33,1},{2,34},{34,2},{3,35},{35,3},{4,36},{36... | collective-permute-start | bytes 36872 | tf_op jit(solution)/shard_map/ppermute | solution.py:48
  75.9 2.9 %collective-permute-start.14 = (bf16[256,1280]{1,0:T(8,128)(2,1)S(1)}, bf16[256,1280]{1,0:T(8,128)(2,1)S(1)}, u32[]{:S(2)}, u32[]{:S(2)}) collective-permute-start(bf16[256,1280]{1,0:T(8,128)(2,1)S(1)} %get-tuple-element.58), channel_id=1, source_target_pairs={{0,32},{32,0},{1,33},{33,1},{2,34},{34,2},{3,35},{35,3},{4,36},{36... | collective-permute-start | bytes 1966088 | tf_op jit(solution)/shard_map/ppermute | solution.py:48
  76.3 2.5 %collective-permute-start.15 = (bf16[192,1280]{1,0:T(8,128)(2,1)S(1)}, bf16[192,1280]{1,0:T(8,128)(2,1)S(1)}, u32[]{:S(2)}, u32[]{:S(2)}) collective-permute-start(bf16[192,1280]{1,0:T(8,128)(2,1)S(1)} %get-tuple-element.60), channel_id=1, source_target_pairs={{0,32},{32,0},{1,33},{33,1},{2,34},{34,2},{3,35},{35,3},{4,36},{36... | collective-permute-start | bytes 1474568 | tf_op jit(solution)/shard_map/ppermute | solution.py:48
  79.0 27.6 %collective-permute-start.22 = (bf16[272,1280]{1,0:T(8,128)(2,1)S(1)}, bf16[272,1280]{1,0:T(8,128)(2,1)S(1)}, u32[]{:S(2)}, u32[]{:S(2)}) collective-permute-start(bf16[272,1280]{1,0:T(8,128)(2,1)S(1)} %get-tuple-element.62.after), channel_id=1, source_target_pairs={{0,128},{64,192},{128,16},{192,80},{16,144},{80,208},{144,0},{208,... | collective-permute-start | bytes 2088968 | tf_op jit(solution)/shard_map/ppermute | solution.py:44
  82.2 25.7 %collective-permute-start.16 = (bf16[272,1280]{1,0:T(8,128)(2,1)S(1)}, bf16[272,1280]{1,0:T(8,128)(2,1)S(1)}, u32[]{:S(2)}, u32[]{:S(2)}) collective-permute-start(bf16[272,1280]{1,0:T(8,128)(2,1)S(1)} %get-tuple-element.63), channel_id=1, source_target_pairs={{0,8},{1,9},{2,10},{3,11},{4,12},{5,13},{6,14},{7,15},{8,0},{9,1},... | collective-permute-start | bytes 2088968 | tf_op jit(solution)/shard_map/ppermute | solution.py:35
  82.9 25.0 %collective-permute-start.17 = (bf16[272,1280]{1,0:T(8,128)(2,1)S(1)}, bf16[272,1280]{1,0:T(8,128)(2,1)S(1)}, u32[]{:S(2)}, u32[]{:S(2)}) collective-permute-start(bf16[272,1280]{1,0:T(8,128)(2,1)S(1)} %get-tuple-element.64), channel_id=1, source_target_pairs={{0,12},{1,13},{2,14},{3,15},{4,0},{5,1},{6,2},{7,3},{8,4},{9,5},{1... | collective-permute-start | bytes 2088968 | tf_op jit(solution)/shard_map/ppermute | solution.py:35
  85.7 22.3 %collective-permute-start.18 = (bf16[272,1280]{1,0:T(8,128)(2,1)S(1)}, bf16[272,1280]{1,0:T(8,128)(2,1)S(1)}, u32[]{:S(2)}, u32[]{:S(2)}) collective-permute-start(bf16[272,1280]{1,0:T(8,128)(2,1)S(1)} %get-tuple-element.65), channel_id=1, source_target_pairs={{0,4},{1,5},{2,6},{3,7},{4,8},{5,9},{6,10},{7,11},{8,12},{9,13},{1... | collective-permute-start | bytes 2088968 | tf_op jit(solution)/shard_map/ppermute | solution.py:35
  85.7 20.9 %collective-permute-start.23 = (bf16[80,1280]{1,0:T(8,128)(2,1)S(1)}, bf16[80,1280]{1,0:T(8,128)(2,1)S(1)}, u32[]{:S(2)}, u32[]{:S(2)}) collective-permute-start(bf16[80,1280]{1,0:T(8,128)(2,1)S(1)} %get-tuple-element.71), channel_id=1, source_target_pairs={{0,192},{64,16},{128,80},{192,144},{16,208},{80,0},{144,64},{208,1... | collective-permute-start | bytes 614408 | tf_op jit(solution)/shard_map/ppermute | solution.py:44
  106.8 7.6 %collective-permute-start.24 = (bf16[144,1280]{1,0:T(8,128)(2,1)S(1)}, bf16[144,1280]{1,0:T(8,128)(2,1)S(1)}, u32[]{:S(2)}, u32[]{:S(2)}) collective-permute-start(bf16[144,1280]{1,0:T(8,128)(2,1)S(1)} %get-tuple-element.73), channel_id=1, source_target_pairs={{0,64},{64,128},{128,192},{192,16},{16,80},{80,144},{144,208},{208... | collective-permute-start | bytes 1105928 | tf_op jit(solution)/shard_map/ppermute | solution.py:44
  108.3 7.3 %collective-permute-start.19 = (bf16[80,1280]{1,0:T(8,128)(2,1)S(1)}, bf16[80,1280]{1,0:T(8,128)(2,1)S(1)}, u32[]{:S(2)}, u32[]{:S(2)}) collective-permute-start(bf16[80,1280]{1,0:T(8,128)(2,1)S(1)} %get-tuple-element.67), channel_id=1, source_target_pairs={{0,2},{1,3},{2,0},{3,1},{4,6},{5,7},{6,4},{7,5},{8,10},{9,11},{10,... | collective-permute-start | bytes 614408 | tf_op jit(solution)/shard_map/ppermute | solution.py:35
  110.7 6.5 %collective-permute-start.20 = (bf16[80,1280]{1,0:T(8,128)(2,1)S(1)}, bf16[80,1280]{1,0:T(8,128)(2,1)S(1)}, u32[]{:S(2)}, u32[]{:S(2)}) collective-permute-start(bf16[80,1280]{1,0:T(8,128)(2,1)S(1)} %get-tuple-element.68), channel_id=1, source_target_pairs={{0,3},{1,0},{2,1},{3,2},{4,7},{5,4},{6,5},{7,6},{8,11},{9,8},{10,9... | collective-permute-start | bytes 614408 | tf_op jit(solution)/shard_map/ppermute | solution.py:35
  111.9 7.0 %collective-permute-start.21 = (bf16[80,1280]{1,0:T(8,128)(2,1)S(1)}, bf16[80,1280]{1,0:T(8,128)(2,1)S(1)}, u32[]{:S(2)}, u32[]{:S(2)}) collective-permute-start(bf16[80,1280]{1,0:T(8,128)(2,1)S(1)} %get-tuple-element.69), channel_id=1, source_target_pairs={{0,1},{1,2},{2,3},{3,0},{4,5},{5,6},{6,7},{7,4},{8,9},{9,10},{10,1... | collective-permute-start | bytes 614408 | tf_op jit(solution)/shard_map/ppermute | solution.py:35
  114.5 4.4 %collective-permute-start.25 = (bf16[80,1280]{1,0:T(8,128)(2,1)S(1)}, bf16[80,1280]{1,0:T(8,128)(2,1)S(1)}, u32[]{:S(2)}, u32[]{:S(2)}) collective-permute-start(bf16[80,1280]{1,0:T(8,128)(2,1)S(1)} %get-tuple-element.75), channel_id=1, source_target_pairs={{0,32},{32,0},{1,33},{33,1},{2,34},{34,2},{3,35},{35,3},{4,36},{36... | collective-permute-start | bytes 614408 | tf_op jit(solution)/shard_map/ppermute | solution.py:48

commit v12 on v9

--- a/solution.py
+++ b/solution.py
@@ -55,7 +55,7 @@
 def plane_or_ring():
     out = [[device(0, y, x, z) for y in range(NY) for x in range(NX)] for z in range(NZ)]
     return out + [
-        [device(1, y + d, x, z) for z in range(NZ) for d in (0, 2)] for y in range(2) for x in range(NX)
+        [device(1, y + d, x, z) for z in range(NZ) for d in (0, 1)] for y in (0, 2) for x in range(NX)
     ]
 
 
@@ -142,20 +142,25 @@
     all_texts[BLOCK - ROWS :, :] = refs[8][...]
     where = [place[i] for i in range(5)]
     multiplier = scale[0] * LOG2E
-    for j in range(4):
-        if j < 3:
-            all_texts[j * CHUNK : (j + 1) * CHUNK, :] = texts[j][...]
-        all_images[j * CHUNK : (j + 1) * CHUNK, :] = images[j][...]
-        for a in range(4):
+    for j in range(3):
+        all_texts[j * CHUNK : (j + 1) * CHUNK, :] = texts[j][...]
+
+    def chunk_logits(a):
+        all_images[a * CHUNK : (a + 1) * CHUNK, :] = images[a][...]
+        for j in range(4):
             text = texts[j][...] if j < 3 else all_texts[3 * CHUNK :, :]
             logits[a * CHUNK : (a + 1) * CHUNK, j * CHUNK : (j + 1) * CHUNK] = multiplier * lax.dot_general(
                 images[a][...], text, (((1,), (1,)), ((), ())), preferred_element_type=F32
             )
+
+    chunk_logits(0)
     cols = col_ids(where)
     step = 32
     matched = jnp.zeros((8, 128), F32)
     col_top = [jnp.full((8, 128), -jnp.inf, F32) for _ in range(8)]
     for a in range(4):
+        if a < 3:
+            chunk_logits(a + 1)
         ids = row_ids(where, a)
         for b in range(4):
             for half in range(ROWS // step):
@@ -242,7 +247,7 @@
 
 def join_body(place, got, mine, message):
     first = place[1] == 0
-    counts = [jnp.logical_or(first, (place[3] >> 1) == i % 2) for i in range(16)]
+    counts = [jnp.logical_or(first, (place[3] & 1) == i % 2) for i in range(16)]
     parts = [jnp.where(counts[i], got[i, :16, :], -jnp.inf) for i in range(16)]
     top = parts[0]
     for p in parts[1:]:
@@ -294,14 +299,14 @@
 
 
 def weights_body(place, scale, logits, mine, other, images, *refs):
-    weights, outs = refs[0], refs[1:4]
-    row_wide, row_lse, col_lse = refs[4:]
+    weights, outs = refs[0], refs[1:5]
+    row_wide, row_lse, col_lse = refs[5:]
     first = place[1] == 0
     shares = jnp.where(first, mine[16:17, :], other[16:17, :]), jnp.where(first, other[16:17, :], mine[16:17, :])
     for i, share in enumerate(shares):
         tail = digits_of(share).astype(BF16)
         for e in range(EMBED // 128):
-            outs[2][i * TAIL : (i + 1) * TAIL, e * 128 : (e + 1) * 128] = tail
+            outs[3][i * TAIL : (i + 1) * TAIL, e * 128 : (e + 1) * 128] = tail
     row_lse[...] = jnp.where(first, mine[:16, :], other[:16, :]) + 1.0
     col_lse[...] = jnp.where(first, other[:16, :], mine[:16, :]) + 1.0
     where = [place[i] for i in range(5)]
@@ -328,30 +333,33 @@
                 both = jnp.exp2(tile - wide) + jnp.exp2(tile - col_line[t])
                 both = both - jnp.where(ids[b] == cols[t][0:1], 1.0, 0.0)
                 weights[at : at + ROWS, t * 128 : (t + 1) * 128] = both.astype(BF16)
-    text_terms(multiplier, weights, images, ((2 * CHUNK, outs[0]), (3 * CHUNK, outs[1])))
-
-
-def text_terms(multiplier, weights, images, outs):
-    for skip, out in outs:
-        for e in range(5):
-            term = lax.dot_general(
-                weights[:, skip : skip + out.shape[0]],
-                images[:, e * 256 : (e + 1) * 256],
-                (((0,), (0,)), ((), ())),
-                preferred_element_type=F32,
-            )
-            out[:, e * 256 : (e + 1) * 256] = (multiplier * term).astype(BF16)
-
-
-def image_terms(multiplier, weights, texts, outs):
-    for a, out in outs.items():
-        for e in range(5):
-            term = jnp.dot(
-                weights[a * CHUNK : (a + 1) * CHUNK, :],
-                texts[:, e * 256 : (e + 1) * 256],
-                preferred_element_type=F32,
-            )
-            out[:CHUNK, e * 256 : (e + 1) * 256] = (multiplier * term).astype(BF16)
+    text_terms(multiplier, weights, images, 2 * CHUNK, outs[:3])
+
+
+def text_terms(multiplier, weights, images, at, outs):
+    rows = sum(out.shape[0] for out in outs)
+    for e in range(5):
+        term = multiplier * lax.dot_general(
+            weights[:, at : at + rows],
+            images[:, e * 256 : (e + 1) * 256],
+            (((0,), (0,)), ((), ())),
+            preferred_element_type=F32,
+        )
+        skip = 0
+        for out in outs:
+            out[:, e * 256 : (e + 1) * 256] = term[skip : skip + out.shape[0]].astype(BF16)
+            skip += out.shape[0]
+
+
+def image_terms(multiplier, weights, texts, at, outs):
+    for e in range(5):
+        term = multiplier * jnp.dot(
+            weights[at * CHUNK : (at + len(outs)) * CHUNK, :],
+            texts[:, e * 256 : (e + 1) * 256],
+            preferred_element_type=F32,
+        )
+        for i, out in enumerate(outs):
+            out[:CHUNK, e * 256 : (e + 1) * 256] = term[i * CHUNK : (i + 1) * CHUNK].astype(BF16)
 
 
 def weights_call(place, scale, logits, mine, other, images):
@@ -361,10 +369,11 @@
             jax.ShapeDtypeStruct((BLOCK, BLOCK), BF16),
             PART,
             jax.ShapeDtypeStruct((3 * ROWS, EMBED), BF16),
+            jax.ShapeDtypeStruct((ROWS, EMBED), BF16),
             jax.ShapeDtypeStruct((2 * TAIL, EMBED), BF16),
         ),
         in_specs=[SMEM, SMEM] + [VMEM] * 4,
-        out_specs=(VMEM,) * 4,
+        out_specs=(VMEM,) * 5,
         scratch_shapes=[
             pltpu.VMEM((BLOCK, 128), F32),
             pltpu.VMEM((16, 128), F32),
@@ -374,22 +383,22 @@
     )(place, scale, logits, mine, other, images)
 
 
-def text_body(scale, weights, images, near, far):
-    text_terms(scale[0], weights, images, ((CHUNK, near), (BLOCK - ROWS, far)))
+def text_body(scale, weights, images, out):
+    text_terms(scale[0], weights, images, CHUNK, [out])
 
 
 def text_call(scale, weights, images):
     return pl.pallas_call(
         text_body,
-        out_shape=(PART, jax.ShapeDtypeStruct((ROWS, EMBED), BF16)),
+        out_shape=PART,
         in_specs=[SMEM] + [VMEM] * 2,
-        out_specs=(VMEM,) * 2,
+        out_specs=VMEM,
         compiler_params=PARAMS,
     )(scale, weights, images)
 
 
 def image_body(scale, after, digits, weights, texts, *outs):
-    image_terms(scale[0], weights, texts, dict(zip((2, 1, 3), outs)))
+    image_terms(scale[0], weights, texts, 1, outs)
     for out in outs:
         out[CHUNK:, :] = digits[TAIL:, :]
 
@@ -405,8 +414,8 @@
 
 
 def rest_body(scale, weights, images, texts, text_out, image_out):
-    text_terms(scale[0], weights, images, ((0, text_out),))
-    image_terms(scale[0], weights, texts, {0: image_out})
+    text_terms(scale[0], weights, images, 0, [text_out])
+    image_terms(scale[0], weights, texts, 0, [image_out])
 
 
 def rest_call(scale, weights, images, texts):
@@ -489,19 +498,19 @@
 
     spread = spread_call(place, row_part, col_part, matched, core_swap(message))
     mine, message = join_call(place, exchange(spread, plane_or_ring()))
-    weights, text_2, text_3, digits = weights_call(
+    weights, text_2, text_3, far, digits = weights_call(
         place, logit_scale, logits, mine, core_swap(message), images
     )
 
     other_1, other_3 = core_swap(text_2), core_swap(text_3)
-    text_1, far = text_call(logit_scale, weights, images)
+    text_1 = text_call(logit_scale, weights, images)
     pairs = sums(
         [text_1, other_1, far, other_3, digits],
         ((256, ((0, 0), (1, 0))), (64, ((2, 0), (3, 128))), (TAIL, ((4, 0),))),
     )[0]
     image_parts = image_call(logit_scale, pairs, digits, weights, texts)
     pairs = z_shift(pairs, 2)
-    back = [plane_shift(v, -k, False) for v, k in zip(image_parts, (2, 1, 3))]
+    back = [plane_shift(v, -k, False) for v, k in ((image_parts[k - 1], k) for k in (2, 1, 3))]
     text_0, image_0 = rest_call(logit_scale, weights, images, texts)
 
     rows_tail = (TAIL, ((2, 320), (3, 0)))

time: 118 us -> 116 us (0.983)
  starting transfers between devices: 32.3 us -> 29.8 us
  waiting for transfers between devices: 46.6 us -> 48.9 us
  Pallas kernels: 19.1 us -> 17.9 us
    ppermute x8, starting transfers between devices: 3.7 us -> 1.64 us  [core_swap(): return lax.ppermute(v, 'core', [(0, 1), (1, 0)])]
    ppermute x8, waiting for transfers between devices: 5.68 us -> 6.99 us  [core_swap(): return lax.ppermute(v, 'core', [(0, 1), (1, 0)])]
  transfers between devices with their start and end apart: 26 -> 26, of which waited for: 11 -> 11; matrix products, arithmetic and copies ran while one was open for 0% -> 0% of each run, Pallas kernels for 6% -> 5%
where the time goes in v12:
time: 116 us; the launch traced here: 115 us
  waiting for transfers between devices  48.9 us (42%)
  starting transfers between devices  29.8 us (26%)
  Pallas kernels  17.9 us (15%)
  blocking collectives  14.9 us (13%)
  local copies, waits for them, and re-layouts  1.92 us (2%)
  between operations  1.48 us (1%)
    ppermute x6, waiting for transfers between devices, z_shift(): return lax.ppermute(v, ('zl', 'core', 'zh'), pairs)  40.9 us
    ppermute x12, starting transfers between devices, plane_shift(): return lax.ppermute(v, ('core', 'zh', 'y', 'x'), pairs)  16.4 us
    all_to_all x1, blocking collectives, exchange(): return lax.all_to_all(v, AXES, 0, 0, axis_index_groups=groups)  14.9 us
    ppermute x6, starting transfers between devices, z_shift(): return lax.ppermute(v, ('zl', 'core', 'zh'), pairs)  11.7 us
    ppermute x8, waiting for transfers between devices, core_swap(): return lax.ppermute(v, 'core', [(0, 1), (1, 0)])  6.99 us
    pallas_call x1, Pallas kernels, logits_call(): pl.pallas_call(logits_body, out_shape=(jax.ShapeDtypeStruct((BLOCK, BLOCK...  5.63 us
    pallas_call x1, Pallas kernels, weights_call(): pl.pallas_call(weights_body, out_shape=(jax.ShapeDtypeStruct((BLOCK, BLOC...  3.55 us
  transfers between devices with their start and end apart: 26, of which 11 were waited for; matrix products, arithmetic and copies ran while one was open for 0% of the time, Pallas kernels for 5%

profile of v12, /device:TPU:32, one launch (start us, length us, event | category | flops | bytes accessed | tf_op | source)
XLA Modules:
  0.0 114.9 jit_solution(11843978628788436378)
XLA Ops:
  0.6 0.1 collective-permute-start
  0.7 1.6 %collective-permute-done.refs_1_ = bf16[64,1280]{1,0:T(8,128)(2,1)S(1)} collective-permute-done((bf16[64,1280]{1,0:T(8,128)(2,1)}, bf16[64,1280]{1,0:T(8,128)(2,1)S(1)}, u32[]{:S(2)}, u32[]{:S(2)}) %collective-permute-start) | collective-permute-done | bytes 163872 | tf_op jit(solution)/shard_map/ppermute | solution.py:48
  2.3 0.9 copy-done
  3.2 0.9 copy-done.1
  4.2 1.9 %collective-permute-start.4 = (bf16[128,1280]{1,0:T(8,128)(2,1)S(1)}, bf16[128,1280]{1,0:T(8,128)(2,1)S(1)}, u32[]{:S(2)}, u32[]{:S(2)}) collective-permute-start(bf16[128,1280]{1,0:T(8,128)(2,1)S(1)} %get-tuple-element.38.refs_4_), channel_id=1, source_target_pairs={{0,208},{64,0},{128,64},{192,128},{16,192},{80,16},{144,80},{208,1... | collective-permute-start | bytes 983048 | tf_op jit(solution)/shard_map/ppermute | solution.py:44
  6.1 5.5 %collective-permute-start.5 = (bf16[64,1280]{1,0:T(8,128)(2,1)S(1)}, bf16[64,1280]{1,0:T(8,128)(2,1)S(1)}, u32[]{:S(2)}, u32[]{:S(2)}) collective-permute-start(bf16[64,1280]{1,0:T(8,128)(2,1)S(1)} %copy-done.1), channel_id=1, source_target_pairs={{0,16},{64,80},{128,144},{192,208},{16,0},{80,64},{144,128},{208,1... | collective-permute-start | bytes 491528 | tf_op jit(solution)/shard_map/ppermute | solution.py:44
  11.6 2.8 %collective-permute-start.3 = (bf16[64,1280]{1,0:T(8,128)(2,1)S(1)}, bf16[64,1280]{1,0:T(8,128)(2,1)S(1)}, u32[]{:S(2)}, u32[]{:S(2)}) collective-permute-start(bf16[64,1280]{1,0:T(8,128)(2,1)S(1)} %get-tuple-element.37.refs_0_), channel_id=1, source_target_pairs={{0,3},{1,0},{2,1},{3,2},{4,7},{5,4},{6,5},{7,6},{8,11},{9,8},{10,9... | collective-permute-start | bytes 491528 | tf_op jit(solution)/shard_map/ppermute | solution.py:35
  14.3 0.8 collective-permute-start.2
  15.1 0.9 collective-permute-start.1
  16.0 7.1 %collective-permute-done.5.refs_6_.refs_8_ = bf16[64,1280]{1,0:T(8,128)(2,1)S(1)} collective-permute-done((bf16[64,1280]{1,0:T(8,128)(2,1)S(1)}, bf16[64,1280]{1,0:T(8,128)(2,1)S(1)}, u32[]{:S(2)}, u32[]{:S(2)}) %collective-permute-start.5) | collective-permute-done | bytes 163872 | tf_op jit(solution)/shard_map/ppermute | solution.py:44
  23.1 0.0 collective-permute-done.3.refs_3_
  23.1 0.0 collective-permute-done.2.refs_2_
  23.1 0.0 collective-permute-done.1.refs_1_
  23.1 0.0 collective-permute-done.4.refs_5_
  23.1 0.9 shard_map.59
  24.0 1.9 %collective-permute-start.9 = (bf16[256,1280]{1,0:T(8,128)(2,1)S(1)}, bf16[256,1280]{1,0:T(8,128)(2,1)S(1)}, u32[]{:S(2)}, u32[]{:S(2)}) collective-permute-start(bf16[256,1280]{1,0:T(8,128)(2,1)S(1)} %get-tuple-element.40.refs_4_), channel_id=1, source_target_pairs={{0,144},{64,208},{128,0},{192,64},{16,128},{80,192},{144,16},{208,... | collective-permute-start | bytes 1966088 | tf_op jit(solution)/shard_map/ppermute | solution.py:44
  25.9 3.2 %collective-permute-start.8 = (bf16[256,1280]{1,0:T(8,128)(2,1)S(1)}, bf16[256,1280]{1,0:T(8,128)(2,1)S(1)}, u32[]{:S(2)}, u32[]{:S(2)}) collective-permute-start(bf16[256,1280]{1,0:T(8,128)(2,1)S(1)} %get-tuple-element.39.refs_0_), channel_id=1, source_target_pairs={{0,8},{1,9},{2,10},{3,11},{4,12},{5,13},{6,14},{7,15},{8,0},{9,1},... | collective-permute-start | bytes 1966088 | tf_op jit(solution)/shard_map/ppermute | solution.py:35
  29.1 1.1 collective-permute-start.7
  30.2 1.0 collective-permute-start.6
  31.1 10.3 %collective-permute-done.9.refs_5_ = bf16[256,1280]{1,0:T(8,128)(2,1)S(1)} collective-permute-done((bf16[256,1280]{1,0:T(8,128)(2,1)S(1)}, bf16[256,1280]{1,0:T(8,128)(2,1)S(1)}, u32[]{:S(2)}, u32[]{:S(2)}) %collective-permute-start.9) | collective-permute-done | bytes 655392 | tf_op jit(solution)/shard_map/ppermute | solution.py:44
  41.5 0.0 collective-permute-start.10
  41.5 0.5 collective-permute-start.11
  42.6 0.1 stack.23.place
  42.7 1.7 %collective-permute-done.11.refs_7_ = bf16[192,1280]{1,0:T(8,128)(2,1)} collective-permute-done((bf16[192,1280]{1,0:T(8,128)(2,1)}, bf16[192,1280]{1,0:T(8,128)(2,1)}, u32[]{:S(2)}, u32[]{:S(2)}) %collective-permute-start.11) | collective-permute-done | bytes 491552 | tf_op jit(solution)/shard_map/ppermute | solution.py:48
  44.4 0.0 collective-permute-done.8.refs_3_
  44.4 1.0 collective-permute-done.7.refs_2_
  45.4 0.0 collective-permute-done.6.refs_1_
  45.4 5.6 %shard_map.60 = (f32[1024,1024]{1,0:T(8,128)S(1)}, f32[16,128]{1,0:T(8,128)S(1)}, f32[16,128]{1,0:T(8,128)S(1)}, f32[24,128]{1,0:T(8,128)S(1)}, f32[8,128]{1,0:T...) custom-call(s32[5]{0:T(128)S(1)} %stack.23.place, f32[1]{0:T(128)S(6)} %copy.6.scale, ...), custom_call_target="tpu_custom_call" | custom-call | tf_op jit(solution)/shard_map/pallas_call | solution.py:197
  51.0 0.3 collective-permute-start.12
  51.3 1.2 %collective-permute-done.12.got = f32[24,128]{1,0:T(8,128)S(1)} collective-permute-done((f32[24,128]{1,0:T(8,128)S(1)}, f32[24,128]{1,0:T(8,128)S(1)}, u32[]{:S(2)}, u32[]{:S(2)}) %collective-permute-start.12) | collective-permute-done | bytes 12320 | tf_op jit(solution)/shard_map/ppermute | solution.py:48
  52.5 0.6 shard_map.61
  53.1 14.9 %all_to_all.5.got = f32[16,24,128]{2,1,0:T(8,128)S(1)} all-to-all(f32[16,24,128]{2,1,0:T(8,128)S(1)} %shard_map.61), channel_id=1, replica_groups={{0,1,2,3,4,5,6,7,8,9,10,11,12,13,14,15},{64,65,66,67,68,69,70,71,72,73,..., dimensions={0} | all-to-all | bytes 393216 | tf_op jit(solution)/shard_map/all_to_all | solution.py:63
  68.0 0.7 shard_map.62
  68.8 0.1 collective-permute-start.13
  68.9 1.2 %collective-permute-done.13.other = f32[24,128]{1,0:T(8,128)S(1)} collective-permute-done((f32[24,128]{1,0:T(8,128)S(1)}, f32[24,128]{1,0:T(8,128)S(1)}, u32[]{:S(2)}, u32[]{:S(2)}) %collective-permute-start.13) | collective-permute-done | bytes 12320 | tf_op jit(solution)/shard_map/ppermute | solution.py:48
  70.0 3.6 %shard_map.63 = (bf16[1024,1024]{1,0:T(8,128)(2,1)S(1)}, bf16[256,1280]{1,0:T(8,128)(2,1)S(1)}, bf16[192,1280]{1,0:T(8,128)(2,1)S(1)}, bf16[64,1280]{1,0:T(8,128)(2,1)S(1)}, bf16[32,1280]{1,0:T(8,128)(2,1)S(1)}) custom-call(s32[5]{0:T(128)S(1)} %stack.23.place, f32[1]{0:T(128)S(6)} %copy.6.scale, f32[1024,1024]{1,0:T(8,128)S(1)} %get-tuple-element.42.logits, ...), custom_call_target="tpu_custom_call" | custom-call | tf_op jit(solution)/shard_map/pallas_call | solution.py:366
  73.6 0.3 collective-permute-start.14
  73.8 0.3 collective-permute-start.15
  74.2 0.9 shard_map.65.refs_0_
  75.1 1.4 %collective-permute-done.15.refs_3_.refs_1_ = bf16[192,1280]{1,0:T(8,128)(2,1)S(1)} collective-permute-done((bf16[192,1280]{1,0:T(8,128)(2,1)S(1)}, bf16[192,1280]{1,0:T(8,128)(2,1)S(1)}, u32[]{:S(2)}, u32[]{:S(2)}) %collective-permute-start.15) | collective-permute-done | bytes 491552 | tf_op jit(solution)/shard_map/ppermute | solution.py:48
  76.5 0.0 collective-permute-done.14.refs_1_
  76.5 0.2 shard_map.66.after
  76.7 1.3 %collective-permute-start.22 = (bf16[336,1280]{1,0:T(8,128)(2,1)S(1)}, bf16[336,1280]{1,0:T(8,128)(2,1)S(1)}, u32[]{:S(2)}, u32[]{:S(2)}) collective-permute-start(bf16[336,1280]{1,0:T(8,128)(2,1)S(1)} %shard_map.66.after), channel_id=1, source_target_pairs={{0,128},{64,192},{128,16},{192,80},{16,144},{80,208},{144,0},{208,... | collective-permute-start | bytes 2580488 | tf_op jit(solution)/shard_map/ppermute | solution.py:44
  77.9 2.2 %shard_map.67 = (bf16[272,1280]{1,0:T(8,128)(2,1)S(1)}, bf16[272,1280]{1,0:T(8,128)(2,1)S(1)}, bf16[272,1280]{1,0:T(8,128)(2,1)S(1)}) custom-call(f32[1]{0:T(128)S(6)} %copy.6.scale, bf16[336,1280]{1,0:T(8,128)(2,1)S(1)} %shard_map.66.after, bf16[32,1280]{1,0:T(8,128)(2,1)S(1)} %get-tuple-element.56.refs_4_.digits.refs_3_.refs_6_, ...), custom_call_target="tpu_custom_call" | custom-call | tf_op jit(solution)/shard_map/pallas_call | solution.py:407
  80.1 1.3 %collective-permute-start.16 = (bf16[272,1280]{1,0:T(8,128)(2,1)S(1)}, bf16[272,1280]{1,0:T(8,128)(2,1)S(1)}, u32[]{:S(2)}, u32[]{:S(2)}) collective-permute-start(bf16[272,1280]{1,0:T(8,128)(2,1)S(1)} %get-tuple-element.57), channel_id=1, source_target_pairs={{0,8},{1,9},{2,10},{3,11},{4,12},{5,13},{6,14},{7,15},{8,0},{9,1},... | collective-permute-start | bytes 2088968 | tf_op jit(solution)/shard_map/ppermute | solution.py:35
  81.5 1.4 %collective-permute-start.17 = (bf16[272,1280]{1,0:T(8,128)(2,1)S(1)}, bf16[272,1280]{1,0:T(8,128)(2,1)S(1)}, u32[]{:S(2)}, u32[]{:S(2)}) collective-permute-start(bf16[272,1280]{1,0:T(8,128)(2,1)S(1)} %get-tuple-element.58), channel_id=1, source_target_pairs={{0,12},{1,13},{2,14},{3,15},{4,0},{5,1},{6,2},{7,3},{8,4},{9,5},{1... | collective-permute-start | bytes 2088968 | tf_op jit(solution)/shard_map/ppermute | solution.py:35
  82.9 0.6 collective-permute-start.18
  83.5 1.6 %shard_map.64 = (bf16[256,1280]{1,0:T(8,128)(2,1)S(1)}, bf16[256,1280]{1,0:T(8,128)(2,1)S(1)}) custom-call(f32[1]{0:T(128)S(6)} %copy.6.scale, bf16[1024,1024]{1,0:T(8,128)(2,1)S(1)} %get-tuple-element.50.weights, bf16[1024,1280]{1,0:T(8,128)(2,1)S(1)} %get-tuple-element.49.images, bf16[1024,1280]{1,0:T(8,128)(2,1)S(1)} %get-tuple-element.51.texts), custom_call_target="tpu_custom_call" | custom-call | tf_op jit(solution)/shard_map/pallas_call | solution.py:422
  85.1 15.4 %collective-permute-done.22.refs_2_ = bf16[336,1280]{1,0:T(8,128)(2,1)S(1)} collective-permute-done((bf16[336,1280]{1,0:T(8,128)(2,1)S(1)}, bf16[336,1280]{1,0:T(8,128)(2,1)S(1)}, u32[]{:S(2)}, u32[]{:S(2)}) %collective-permute-start.22) | collective-permute-done | bytes 860192 | tf_op jit(solution)/shard_map/ppermute | solution.py:44
  100.5 0.2 shard_map.69
  100.7 0.1 collective-permute-start.23
  100.8 0.0 collective-permute-done.17.refs_2_
  100.8 0.0 collective-permute-done.18.refs_3_
  100.9 0.4 shard_map.68
  101.3 1.4 %collective-permute-start.19 = (bf16[80,1280]{1,0:T(8,128)(2,1)S(1)}, bf16[80,1280]{1,0:T(8,128)(2,1)S(1)}, u32[]{:S(2)}, u32[]{:S(2)}) collective-permute-start(bf16[80,1280]{1,0:T(8,128)(2,1)S(1)} %get-tuple-element.61), channel_id=1, source_target_pairs={{0,2},{1,3},{2,0},{3,1},{4,6},{5,7},{6,4},{7,5},{8,10},{9,11},{10,... | collective-permute-start | bytes 614408 | tf_op jit(solution)/shard_map/ppermute | solution.py:35
  102.7 1.9 %collective-permute-start.20 = (bf16[80,1280]{1,0:T(8,128)(2,1)S(1)}, bf16[80,1280]{1,0:T(8,128)(2,1)S(1)}, u32[]{:S(2)}, u32[]{:S(2)}) collective-permute-start(bf16[80,1280]{1,0:T(8,128)(2,1)S(1)} %get-tuple-element.62), channel_id=1, source_target_pairs={{0,3},{1,0},{2,1},{3,2},{4,7},{5,4},{6,5},{7,6},{8,11},{9,8},{10,9... | collective-permute-start | bytes 614408 | tf_op jit(solution)/shard_map/ppermute | solution.py:35
  104.6 1.1 collective-permute-start.24
  105.7 0.1 collective-permute-start.21
  105.8 2.5 %collective-permute-done.23.refs_1_ = bf16[144,1280]{1,0:T(8,128)(2,1)S(1)} collective-permute-done((bf16[144,1280]{1,0:T(8,128)(2,1)S(1)}, bf16[144,1280]{1,0:T(8,128)(2,1)S(1)}, u32[]{:S(2)}, u32[]{:S(2)}) %collective-permute-start.23) | collective-permute-done | bytes 368672 | tf_op jit(solution)/shard_map/ppermute | solution.py:44
  108.4 0.1 collective-permute-start.25
  108.5 5.5 %collective-permute-done.24.refs_2_ = bf16[80,1280]{1,0:T(8,128)(2,1)S(1)} collective-permute-done((bf16[80,1280]{1,0:T(8,128)(2,1)S(1)}, bf16[80,1280]{1,0:T(8,128)(2,1)S(1)}, u32[]{:S(2)}, u32[]{:S(2)}) %collective-permute-start.24) | collective-permute-done | bytes 204832 | tf_op jit(solution)/shard_map/ppermute | solution.py:44
  114.0 0.1 shard_map.70.refs_4_
  114.1 0.0 collective-permute-done.20.refs_2_
  114.1 0.8 shard_map.72
  (9 shorter events, 0.1 us)
Async XLA Ops:
  0.6 1.7 %collective-permute-start = (bf16[64,1280]{1,0:T(8,128)(2,1)}, bf16[64,1280]{1,0:T(8,128)(2,1)S(1)}, u32[]{:S(2)}, u32[]{:S(2)}) collective-permute-start(bf16[64,1280]{1,0:T(8,128)(2,1)} %refs_0_.1), channel_id=1, source_target_pairs={{0,32},{32,0},{1,33},{33,1},{2,34},{34,2},{3,35},{35,3},{4,36},{36... | collective-permute-start | bytes 491528 | tf_op jit(solution)/shard_map/ppermute | solution.py:48
  2.3 0.9 copy-start
  3.2 0.9 copy-start.1
  4.2 18.9 %collective-permute-start.4 = (bf16[128,1280]{1,0:T(8,128)(2,1)S(1)}, bf16[128,1280]{1,0:T(8,128)(2,1)S(1)}, u32[]{:S(2)}, u32[]{:S(2)}) collective-permute-start(bf16[128,1280]{1,0:T(8,128)(2,1)S(1)} %get-tuple-element.38.refs_4_), channel_id=1, source_target_pairs={{0,208},{64,0},{128,64},{192,128},{16,192},{80,16},{144,80},{208,1... | collective-permute-start | bytes 983048 | tf_op jit(solution)/shard_map/ppermute | solution.py:44
  6.1 17.0 %collective-permute-start.5 = (bf16[64,1280]{1,0:T(8,128)(2,1)S(1)}, bf16[64,1280]{1,0:T(8,128)(2,1)S(1)}, u32[]{:S(2)}, u32[]{:S(2)}) collective-permute-start(bf16[64,1280]{1,0:T(8,128)(2,1)S(1)} %copy-done.1), channel_id=1, source_target_pairs={{0,16},{64,80},{128,144},{192,208},{16,0},{80,64},{144,128},{208,1... | collective-permute-start | bytes 491528 | tf_op jit(solution)/shard_map/ppermute | solution.py:44
  11.6 11.5 %collective-permute-start.3 = (bf16[64,1280]{1,0:T(8,128)(2,1)S(1)}, bf16[64,1280]{1,0:T(8,128)(2,1)S(1)}, u32[]{:S(2)}, u32[]{:S(2)}) collective-permute-start(bf16[64,1280]{1,0:T(8,128)(2,1)S(1)} %get-tuple-element.37.refs_0_), channel_id=1, source_target_pairs={{0,3},{1,0},{2,1},{3,2},{4,7},{5,4},{6,5},{7,6},{8,11},{9,8},{10,9... | collective-permute-start | bytes 491528 | tf_op jit(solution)/shard_map/ppermute | solution.py:35
  14.3 8.8 %collective-permute-start.2 = (bf16[64,1280]{1,0:T(8,128)(2,1)S(1)}, bf16[64,1280]{1,0:T(8,128)(2,1)S(1)}, u32[]{:S(2)}, u32[]{:S(2)}) collective-permute-start(bf16[64,1280]{1,0:T(8,128)(2,1)S(1)} %get-tuple-element.37.refs_0_), channel_id=1, source_target_pairs={{0,2},{1,3},{2,0},{3,1},{4,6},{5,7},{6,4},{7,5},{8,10},{9,11},{10,... | collective-permute-start | bytes 491528 | tf_op jit(solution)/shard_map/ppermute | solution.py:35
  15.1 8.0 %collective-permute-start.1 = (bf16[64,1280]{1,0:T(8,128)(2,1)S(1)}, bf16[64,1280]{1,0:T(8,128)(2,1)S(1)}, u32[]{:S(2)}, u32[]{:S(2)}) collective-permute-start(bf16[64,1280]{1,0:T(8,128)(2,1)S(1)} %get-tuple-element.37.refs_0_), channel_id=1, source_target_pairs={{0,1},{1,2},{2,3},{3,0},{4,5},{5,6},{6,7},{7,4},{8,9},{9,10},{10,1... | collective-permute-start | bytes 491528 | tf_op jit(solution)/shard_map/ppermute | solution.py:35
  24.0 17.4 %collective-permute-start.9 = (bf16[256,1280]{1,0:T(8,128)(2,1)S(1)}, bf16[256,1280]{1,0:T(8,128)(2,1)S(1)}, u32[]{:S(2)}, u32[]{:S(2)}) collective-permute-start(bf16[256,1280]{1,0:T(8,128)(2,1)S(1)} %get-tuple-element.40.refs_4_), channel_id=1, source_target_pairs={{0,144},{64,208},{128,0},{192,64},{16,128},{80,192},{144,16},{208,... | collective-permute-start | bytes 1966088 | tf_op jit(solution)/shard_map/ppermute | solution.py:44
  25.9 18.5 %collective-permute-start.8 = (bf16[256,1280]{1,0:T(8,128)(2,1)S(1)}, bf16[256,1280]{1,0:T(8,128)(2,1)S(1)}, u32[]{:S(2)}, u32[]{:S(2)}) collective-permute-start(bf16[256,1280]{1,0:T(8,128)(2,1)S(1)} %get-tuple-element.39.refs_0_), channel_id=1, source_target_pairs={{0,8},{1,9},{2,10},{3,11},{4,12},{5,13},{6,14},{7,15},{8,0},{9,1},... | collective-permute-start | bytes 1966088 | tf_op jit(solution)/shard_map/ppermute | solution.py:35
  29.1 16.3 %collective-permute-start.7 = (bf16[256,1280]{1,0:T(8,128)(2,1)S(1)}, bf16[256,1280]{1,0:T(8,128)(2,1)S(1)}, u32[]{:S(2)}, u32[]{:S(2)}) collective-permute-start(bf16[256,1280]{1,0:T(8,128)(2,1)S(1)} %get-tuple-element.39.refs_0_), channel_id=1, source_target_pairs={{0,12},{1,13},{2,14},{3,15},{4,0},{5,1},{6,2},{7,3},{8,4},{9,5},{1... | collective-permute-start | bytes 1966088 | tf_op jit(solution)/shard_map/ppermute | solution.py:35
  30.2 15.2 %collective-permute-start.6 = (bf16[256,1280]{1,0:T(8,128)(2,1)S(1)}, bf16[256,1280]{1,0:T(8,128)(2,1)}, u32[]{:S(2)}, u32[]{:S(2)}) collective-permute-start(bf16[256,1280]{1,0:T(8,128)(2,1)S(1)} %get-tuple-element.39.refs_0_), channel_id=1, source_target_pairs={{0,4},{1,5},{2,6},{3,7},{4,8},{5,9},{6,10},{7,11},{8,12},{9,13},{1... | collective-permute-start | bytes 1966088 | tf_op jit(solution)/shard_map/ppermute | solution.py:35
  41.5 4.0 %collective-permute-start.10 = (bf16[256,1280]{1,0:T(8,128)(2,1)S(1)}, bf16[256,1280]{1,0:T(8,128)(2,1)}, u32[]{:S(2)}, u32[]{:S(2)}) collective-permute-start(bf16[256,1280]{1,0:T(8,128)(2,1)S(1)} %collective-permute-done.9.refs_5_), channel_id=1, source_target_pairs={{0,32},{32,0},{1,33},{33,1},{2,34},{34,2},{3,35},{35,3},{4,36},{36... | collective-permute-start | bytes 1966088 | tf_op jit(solution)/shard_map/ppermute | solution.py:48
  41.5 2.9 %collective-permute-start.11 = (bf16[192,1280]{1,0:T(8,128)(2,1)}, bf16[192,1280]{1,0:T(8,128)(2,1)}, u32[]{:S(2)}, u32[]{:S(2)}) collective-permute-start(bf16[192,1280]{1,0:T(8,128)(2,1)} %get-tuple-element.41), channel_id=1, source_target_pairs={{0,32},{32,0},{1,33},{33,1},{2,34},{34,2},{3,35},{35,3},{4,36},{36... | collective-permute-start | bytes 1474568 | tf_op jit(solution)/shard_map/ppermute | solution.py:48
  51.0 1.4 %collective-permute-start.12 = (f32[24,128]{1,0:T(8,128)S(1)}, f32[24,128]{1,0:T(8,128)S(1)}, u32[]{:S(2)}, u32[]{:S(2)}) collective-permute-start(f32[24,128]{1,0:T(8,128)S(1)} %get-tuple-element.46), channel_id=1, source_target_pairs={{0,32},{32,0},{1,33},{33,1},{2,34},{34,2},{3,35},{35,3},{4,36},{36... | collective-permute-start | bytes 36872 | tf_op jit(solution)/shard_map/ppermute | solution.py:48
  68.8 1.3 %collective-permute-start.13 = (f32[24,128]{1,0:T(8,128)S(1)}, f32[24,128]{1,0:T(8,128)S(1)}, u32[]{:S(2)}, u32[]{:S(2)}) collective-permute-start(f32[24,128]{1,0:T(8,128)S(1)} %get-tuple-element.48), channel_id=1, source_target_pairs={{0,32},{32,0},{1,33},{33,1},{2,34},{34,2},{3,35},{35,3},{4,36},{36... | collective-permute-start | bytes 36872 | tf_op jit(solution)/shard_map/ppermute | solution.py:48
  73.6 2.9 %collective-permute-start.14 = (bf16[256,1280]{1,0:T(8,128)(2,1)S(1)}, bf16[256,1280]{1,0:T(8,128)(2,1)S(1)}, u32[]{:S(2)}, u32[]{:S(2)}) collective-permute-start(bf16[256,1280]{1,0:T(8,128)(2,1)S(1)} %get-tuple-element.53), channel_id=1, source_target_pairs={{0,32},{32,0},{1,33},{33,1},{2,34},{34,2},{3,35},{35,3},{4,36},{36... | collective-permute-start | bytes 1966088 | tf_op jit(solution)/shard_map/ppermute | solution.py:48
  73.8 2.6 %collective-permute-start.15 = (bf16[192,1280]{1,0:T(8,128)(2,1)S(1)}, bf16[192,1280]{1,0:T(8,128)(2,1)S(1)}, u32[]{:S(2)}, u32[]{:S(2)}) collective-permute-start(bf16[192,1280]{1,0:T(8,128)(2,1)S(1)} %get-tuple-element.55), channel_id=1, source_target_pairs={{0,32},{32,0},{1,33},{33,1},{2,34},{34,2},{3,35},{35,3},{4,36},{36... | collective-permute-start | bytes 1474568 | tf_op jit(solution)/shard_map/ppermute | solution.py:48
  76.7 23.9 %collective-permute-start.22 = (bf16[336,1280]{1,0:T(8,128)(2,1)S(1)}, bf16[336,1280]{1,0:T(8,128)(2,1)S(1)}, u32[]{:S(2)}, u32[]{:S(2)}) collective-permute-start(bf16[336,1280]{1,0:T(8,128)(2,1)S(1)} %shard_map.66.after), channel_id=1, source_target_pairs={{0,128},{64,192},{128,16},{192,80},{16,144},{80,208},{144,0},{208,... | collective-permute-start | bytes 2580488 | tf_op jit(solution)/shard_map/ppermute | solution.py:44
  80.1 20.7 %collective-permute-start.16 = (bf16[272,1280]{1,0:T(8,128)(2,1)S(1)}, bf16[272,1280]{1,0:T(8,128)(2,1)S(1)}, u32[]{:S(2)}, u32[]{:S(2)}) collective-permute-start(bf16[272,1280]{1,0:T(8,128)(2,1)S(1)} %get-tuple-element.57), channel_id=1, source_target_pairs={{0,8},{1,9},{2,10},{3,11},{4,12},{5,13},{6,14},{7,15},{8,0},{9,1},... | collective-permute-start | bytes 2088968 | tf_op jit(solution)/shard_map/ppermute | solution.py:35
  81.5 19.4 %collective-permute-start.17 = (bf16[272,1280]{1,0:T(8,128)(2,1)S(1)}, bf16[272,1280]{1,0:T(8,128)(2,1)S(1)}, u32[]{:S(2)}, u32[]{:S(2)}) collective-permute-start(bf16[272,1280]{1,0:T(8,128)(2,1)S(1)} %get-tuple-element.58), channel_id=1, source_target_pairs={{0,12},{1,13},{2,14},{3,15},{4,0},{5,1},{6,2},{7,3},{8,4},{9,5},{1... | collective-permute-start | bytes 2088968 | tf_op jit(solution)/shard_map/ppermute | solution.py:35
  82.9 17.9 %collective-permute-start.18 = (bf16[272,1280]{1,0:T(8,128)(2,1)S(1)}, bf16[272,1280]{1,0:T(8,128)(2,1)S(1)}, u32[]{:S(2)}, u32[]{:S(2)}) collective-permute-start(bf16[272,1280]{1,0:T(8,128)(2,1)S(1)} %get-tuple-element.59), channel_id=1, source_target_pairs={{0,4},{1,5},{2,6},{3,7},{4,8},{5,9},{6,10},{7,11},{8,12},{9,13},{1... | collective-permute-start | bytes 2088968 | tf_op jit(solution)/shard_map/ppermute | solution.py:35
  100.7 7.6 %collective-permute-start.23 = (bf16[144,1280]{1,0:T(8,128)(2,1)S(1)}, bf16[144,1280]{1,0:T(8,128)(2,1)S(1)}, u32[]{:S(2)}, u32[]{:S(2)}) collective-permute-start(bf16[144,1280]{1,0:T(8,128)(2,1)S(1)} %get-tuple-element.66), channel_id=1, source_target_pairs={{0,64},{64,128},{128,192},{192,16},{16,80},{80,144},{144,208},{208... | collective-permute-start | bytes 1105928 | tf_op jit(solution)/shard_map/ppermute | solution.py:44
  101.3 12.8 %collective-permute-start.19 = (bf16[80,1280]{1,0:T(8,128)(2,1)S(1)}, bf16[80,1280]{1,0:T(8,128)(2,1)S(1)}, u32[]{:S(2)}, u32[]{:S(2)}) collective-permute-start(bf16[80,1280]{1,0:T(8,128)(2,1)S(1)} %get-tuple-element.61), channel_id=1, source_target_pairs={{0,2},{1,3},{2,0},{3,1},{4,6},{5,7},{6,4},{7,5},{8,10},{9,11},{10,... | collective-permute-start | bytes 614408 | tf_op jit(solution)/shard_map/ppermute | solution.py:35
  102.7 11.4 %collective-permute-start.20 = (bf16[80,1280]{1,0:T(8,128)(2,1)S(1)}, bf16[80,1280]{1,0:T(8,128)(2,1)S(1)}, u32[]{:S(2)}, u32[]{:S(2)}) collective-permute-start(bf16[80,1280]{1,0:T(8,128)(2,1)S(1)} %get-tuple-element.62), channel_id=1, source_target_pairs={{0,3},{1,0},{2,1},{3,2},{4,7},{5,4},{6,5},{7,6},{8,11},{9,8},{10,9... | collective-permute-start | bytes 614408 | tf_op jit(solution)/shard_map/ppermute | solution.py:35
  104.6 9.4 %collective-permute-start.24 = (bf16[80,1280]{1,0:T(8,128)(2,1)S(1)}, bf16[80,1280]{1,0:T(8,128)(2,1)S(1)}, u32[]{:S(2)}, u32[]{:S(2)}) collective-permute-start(bf16[80,1280]{1,0:T(8,128)(2,1)S(1)} %get-tuple-element.67), channel_id=1, source_target_pairs={{0,128},{64,192},{128,16},{192,80},{16,144},{80,208},{144,0},{208,... | collective-permute-start | bytes 614408 | tf_op jit(solution)/shard_map/ppermute | solution.py:44
  105.7 8.4 %collective-permute-start.21 = (bf16[80,1280]{1,0:T(8,128)(2,1)S(1)}, bf16[80,1280]{1,0:T(8,128)(2,1)S(1)}, u32[]{:S(2)}, u32[]{:S(2)}) collective-permute-start(bf16[80,1280]{1,0:T(8,128)(2,1)S(1)} %get-tuple-element.63), channel_id=1, source_target_pairs={{0,1},{1,2},{2,3},{3,0},{4,5},{5,6},{6,7},{7,4},{8,9},{9,10},{10,1... | collective-permute-start | bytes 614408 | tf_op jit(solution)/shard_map/ppermute | solution.py:35
  108.4 5.7 %collective-permute-start.25 = (bf16[80,1280]{1,0:T(8,128)(2,1)S(1)}, bf16[80,1280]{1,0:T(8,128)(2,1)S(1)}, u32[]{:S(2)}, u32[]{:S(2)}) collective-permute-start(bf16[80,1280]{1,0:T(8,128)(2,1)S(1)} %shard_map.71), channel_id=1, source_target_pairs={{0,32},{32,0},{1,33},{33,1},{2,34},{34,2},{3,35},{35,3},{4,36},{36... | collective-permute-start | bytes 614408 | tf_op jit(solution)/shard_map/ppermute | solution.py:48

commit v13 on v12

--- a/solution.py
+++ b/solution.py
@@ -397,20 +397,20 @@
     )(scale, weights, images)
 
 
-def image_body(scale, after, digits, weights, texts, *outs):
+def image_body(scale, digits, weights, texts, *outs):
     image_terms(scale[0], weights, texts, 1, outs)
     for out in outs:
         out[CHUNK:, :] = digits[TAIL:, :]
 
 
-def image_call(scale, after, digits, weights, texts):
+def image_call(scale, digits, weights, texts):
     return pl.pallas_call(
         image_body,
         out_shape=(jax.ShapeDtypeStruct((CHUNK + TAIL, EMBED), BF16),) * 3,
-        in_specs=[SMEM] + [VMEM] * 4,
+        in_specs=[SMEM] + [VMEM] * 3,
         out_specs=(VMEM,) * 3,
         compiler_params=PARAMS,
-    )(scale, after, digits, weights, texts)
+    )(scale, digits, weights, texts)
 
 
 def rest_body(scale, weights, images, texts, text_out, image_out):
@@ -504,11 +504,11 @@
 
     other_1, other_3 = core_swap(text_2), core_swap(text_3)
     text_1 = text_call(logit_scale, weights, images)
+    image_parts = image_call(logit_scale, digits, weights, texts)
     pairs = sums(
-        [text_1, other_1, far, other_3, digits],
+        [text_1, other_1, far, other_3, digits, image_parts[0]],
         ((256, ((0, 0), (1, 0))), (64, ((2, 0), (3, 128))), (TAIL, ((4, 0),))),
     )[0]
-    image_parts = image_call(logit_scale, pairs, digits, weights, texts)
     pairs = z_shift(pairs, 2)
     back = [plane_shift(v, -k, False) for v, k in ((image_parts[k - 1], k) for k in (2, 1, 3))]
     text_0, image_0 = rest_call(logit_scale, weights, images, texts)

time: 116 us -> 117 us (level)
    ppermute x8, waiting for transfers between devices: 6.99 us -> 5.63 us  [core_swap(): return lax.ppermute(v, 'core', [(0, 1), (1, 0)])]
    ppermute x6, waiting for transfers between devices: 40.9 us -> 42.2 us  [z_shift(): return lax.ppermute(v, ('zl', 'core', 'zh'), pairs)]
  transfers between devices with their start and end apart: 26 -> 26, of which waited for: 11 -> 10; matrix products, arithmetic and copies ran while one was open for 0% -> 0% of each run, Pallas kernels for 5% -> 5%
where the time goes in v13:
time: 117 us; the launch traced here: 116 us
  waiting for transfers between devices  48.9 us (42%)
  starting transfers between devices  30.6 us (26%)
  Pallas kernels  17.9 us (15%)
  blocking collectives  14.9 us (13%)
  local copies, waits for them, and re-layouts  1.92 us (2%)
  between operations  1.5 us (1%)
    ppermute x6, waiting for transfers between devices, z_shift(): return lax.ppermute(v, ('zl', 'core', 'zh'), pairs)  42.2 us
    ppermute x12, starting transfers between devices, plane_shift(): return lax.ppermute(v, ('core', 'zh', 'y', 'x'), pairs)  17.5 us
    all_to_all x1, blocking collectives, exchange(): return lax.all_to_all(v, AXES, 0, 0, axis_index_groups=groups)  14.9 us
    ppermute x6, starting transfers between devices, z_shift(): return lax.ppermute(v, ('zl', 'core', 'zh'), pairs)  11.5 us
    pallas_call x1, Pallas kernels, logits_call(): pl.pallas_call(logits_body, out_shape=(jax.ShapeDtypeStruct((BLOCK, BLOCK...  5.63 us
    ppermute x8, waiting for transfers between devices, core_swap(): return lax.ppermute(v, 'core', [(0, 1), (1, 0)])  5.63 us
    pallas_call x1, Pallas kernels, weights_call(): pl.pallas_call(weights_body, out_shape=(jax.ShapeDtypeStruct((BLOCK, BLOC...  3.55 us
  transfers between devices with their start and end apart: 26, of which 10 were waited for; matrix products, arithmetic and copies ran while one was open for 0% of the time, Pallas kernels for 5%

profile of v13, /device:TPU:32, one launch (start us, length us, event | category | flops | bytes accessed | tf_op | source)
XLA Modules:
  0.0 115.8 jit_solution(2183844377447193141)
XLA Ops:
  0.6 0.1 collective-permute-start
  0.7 1.6 %collective-permute-done.refs_1_ = bf16[64,1280]{1,0:T(8,128)(2,1)S(1)} collective-permute-done((bf16[64,1280]{1,0:T(8,128)(2,1)}, bf16[64,1280]{1,0:T(8,128)(2,1)S(1)}, u32[]{:S(2)}, u32[]{:S(2)}) %collective-permute-start) | collective-permute-done | bytes 163872 | tf_op jit(solution)/shard_map/ppermute | solution.py:48
  2.3 0.9 copy-done
  3.2 0.9 copy-done.1
  4.2 1.9 %collective-permute-start.4 = (bf16[128,1280]{1,0:T(8,128)(2,1)S(1)}, bf16[128,1280]{1,0:T(8,128)(2,1)S(1)}, u32[]{:S(2)}, u32[]{:S(2)}) collective-permute-start(bf16[128,1280]{1,0:T(8,128)(2,1)S(1)} %get-tuple-element.38.refs_4_), channel_id=1, source_target_pairs={{0,208},{64,0},{128,64},{192,128},{16,192},{80,16},{144,80},{208,1... | collective-permute-start | bytes 983048 | tf_op jit(solution)/shard_map/ppermute | solution.py:44
  6.1 5.5 %collective-permute-start.5 = (bf16[64,1280]{1,0:T(8,128)(2,1)S(1)}, bf16[64,1280]{1,0:T(8,128)(2,1)S(1)}, u32[]{:S(2)}, u32[]{:S(2)}) collective-permute-start(bf16[64,1280]{1,0:T(8,128)(2,1)S(1)} %copy-done.1), channel_id=1, source_target_pairs={{0,16},{64,80},{128,144},{192,208},{16,0},{80,64},{144,128},{208,1... | collective-permute-start | bytes 491528 | tf_op jit(solution)/shard_map/ppermute | solution.py:44
  11.6 2.8 %collective-permute-start.3 = (bf16[64,1280]{1,0:T(8,128)(2,1)S(1)}, bf16[64,1280]{1,0:T(8,128)(2,1)S(1)}, u32[]{:S(2)}, u32[]{:S(2)}) collective-permute-start(bf16[64,1280]{1,0:T(8,128)(2,1)S(1)} %get-tuple-element.37.refs_0_), channel_id=1, source_target_pairs={{0,3},{1,0},{2,1},{3,2},{4,7},{5,4},{6,5},{7,6},{8,11},{9,8},{10,9... | collective-permute-start | bytes 491528 | tf_op jit(solution)/shard_map/ppermute | solution.py:35
  14.3 0.8 collective-permute-start.2
  15.1 0.9 collective-permute-start.1
  16.0 7.1 %collective-permute-done.5.refs_6_.refs_8_ = bf16[64,1280]{1,0:T(8,128)(2,1)S(1)} collective-permute-done((bf16[64,1280]{1,0:T(8,128)(2,1)S(1)}, bf16[64,1280]{1,0:T(8,128)(2,1)S(1)}, u32[]{:S(2)}, u32[]{:S(2)}) %collective-permute-start.5) | collective-permute-done | bytes 163872 | tf_op jit(solution)/shard_map/ppermute | solution.py:44
  23.1 0.0 collective-permute-done.3.refs_3_
  23.1 0.0 collective-permute-done.1.refs_1_
  23.1 0.0 collective-permute-done.4.refs_5_
  23.1 0.9 shard_map.59
  24.0 1.9 %collective-permute-start.9 = (bf16[256,1280]{1,0:T(8,128)(2,1)S(1)}, bf16[256,1280]{1,0:T(8,128)(2,1)S(1)}, u32[]{:S(2)}, u32[]{:S(2)}) collective-permute-start(bf16[256,1280]{1,0:T(8,128)(2,1)S(1)} %get-tuple-element.40.refs_4_), channel_id=1, source_target_pairs={{0,144},{64,208},{128,0},{192,64},{16,128},{80,192},{144,16},{208,... | collective-permute-start | bytes 1966088 | tf_op jit(solution)/shard_map/ppermute | solution.py:44
  25.9 3.2 %collective-permute-start.8 = (bf16[256,1280]{1,0:T(8,128)(2,1)S(1)}, bf16[256,1280]{1,0:T(8,128)(2,1)S(1)}, u32[]{:S(2)}, u32[]{:S(2)}) collective-permute-start(bf16[256,1280]{1,0:T(8,128)(2,1)S(1)} %get-tuple-element.39.refs_0_), channel_id=1, source_target_pairs={{0,8},{1,9},{2,10},{3,11},{4,12},{5,13},{6,14},{7,15},{8,0},{9,1},... | collective-permute-start | bytes 1966088 | tf_op jit(solution)/shard_map/ppermute | solution.py:35
  29.1 1.1 collective-permute-start.7
  30.2 1.0 collective-permute-start.6
  31.1 10.3 %collective-permute-done.9.refs_5_ = bf16[256,1280]{1,0:T(8,128)(2,1)S(1)} collective-permute-done((bf16[256,1280]{1,0:T(8,128)(2,1)S(1)}, bf16[256,1280]{1,0:T(8,128)(2,1)S(1)}, u32[]{:S(2)}, u32[]{:S(2)}) %collective-permute-start.9) | collective-permute-done | bytes 655392 | tf_op jit(solution)/shard_map/ppermute | solution.py:44
  41.5 0.0 collective-permute-start.10
  41.5 0.5 collective-permute-start.11
  42.6 0.1 stack.23.place
  42.7 1.7 %collective-permute-done.11.refs_7_ = bf16[192,1280]{1,0:T(8,128)(2,1)} collective-permute-done((bf16[192,1280]{1,0:T(8,128)(2,1)}, bf16[192,1280]{1,0:T(8,128)(2,1)}, u32[]{:S(2)}, u32[]{:S(2)}) %collective-permute-start.11) | collective-permute-done | bytes 491552 | tf_op jit(solution)/shard_map/ppermute | solution.py:48
  44.4 0.0 collective-permute-done.8.refs_3_
  44.4 1.0 collective-permute-done.7.refs_2_
  45.4 0.0 collective-permute-done.6.refs_1_
  45.4 0.0 collective-permute-done.10.refs_6_
  45.4 5.6 %shard_map.60 = (f32[1024,1024]{1,0:T(8,128)S(1)}, f32[16,128]{1,0:T(8,128)S(1)}, f32[16,128]{1,0:T(8,128)S(1)}, f32[24,128]{1,0:T(8,128)S(1)}, f32[8,128]{1,0:T...) custom-call(s32[5]{0:T(128)S(1)} %stack.23.place, f32[1]{0:T(128)S(6)} %copy.6.scale, ...), custom_call_target="tpu_custom_call" | custom-call | tf_op jit(solution)/shard_map/pallas_call | solution.py:197
  51.0 0.3 collective-permute-start.12
  51.3 1.2 %collective-permute-done.12.got = f32[24,128]{1,0:T(8,128)S(1)} collective-permute-done((f32[24,128]{1,0:T(8,128)S(1)}, f32[24,128]{1,0:T(8,128)S(1)}, u32[]{:S(2)}, u32[]{:S(2)}) %collective-permute-start.12) | collective-permute-done | bytes 12320 | tf_op jit(solution)/shard_map/ppermute | solution.py:48
  52.5 0.6 shard_map.61
  53.1 14.9 %all_to_all.5.got = f32[16,24,128]{2,1,0:T(8,128)S(1)} all-to-all(f32[16,24,128]{2,1,0:T(8,128)S(1)} %shard_map.61), channel_id=1, replica_groups={{0,1,2,3,4,5,6,7,8,9,10,11,12,13,14,15},{64,65,66,67,68,69,70,71,72,73,..., dimensions={0} | all-to-all | bytes 393216 | tf_op jit(solution)/shard_map/all_to_all | solution.py:63
  68.0 0.7 shard_map.62
  68.8 0.1 collective-permute-start.13
  68.9 1.2 %collective-permute-done.13.other = f32[24,128]{1,0:T(8,128)S(1)} collective-permute-done((f32[24,128]{1,0:T(8,128)S(1)}, f32[24,128]{1,0:T(8,128)S(1)}, u32[]{:S(2)}, u32[]{:S(2)}) %collective-permute-start.13) | collective-permute-done | bytes 12320 | tf_op jit(solution)/shard_map/ppermute | solution.py:48
  70.0 3.6 %shard_map.63 = (bf16[1024,1024]{1,0:T(8,128)(2,1)S(1)}, bf16[256,1280]{1,0:T(8,128)(2,1)S(1)}, bf16[192,1280]{1,0:T(8,128)(2,1)S(1)}, bf16[64,1280]{1,0:T(8,128)(2,1)S(1)}, bf16[32,1280]{1,0:T(8,128)(2,1)S(1)}) custom-call(s32[5]{0:T(128)S(1)} %stack.23.place, f32[1]{0:T(128)S(6)} %copy.6.scale, f32[1024,1024]{1,0:T(8,128)S(1)} %get-tuple-element.42.logits, ...), custom_call_target="tpu_custom_call" | custom-call | tf_op jit(solution)/shard_map/pallas_call | solution.py:366
  73.6 0.3 collective-permute-start.21
  73.8 0.3 collective-permute-start.20
  74.2 0.9 shard_map.67.refs_0_
  75.1 2.2 %shard_map.65 = (bf16[272,1280]{1,0:T(8,128)(2,1)S(1)}, bf16[272,1280]{1,0:T(8,128)(2,1)S(1)}, bf16[272,1280]{1,0:T(8,128)(2,1)S(1)}) custom-call(f32[1]{0:T(128)S(6)} %copy.6.scale, bf16[32,1280]{1,0:T(8,128)(2,1)S(1)} %get-tuple-element.53.digits.refs_4_.refs_3_.refs_6_, bf16[1024,1024]{1,0:T(8,128)(2,1)S(1)} %get-tuple-element.50.weights, ...), custom_call_target="tpu_custom_call" | custom-call | tf_op jit(solution)/shard_map/pallas_call | solution.py:407
  77.3 0.0 collective-permute-done.20.refs_3_.refs_1_
  77.3 0.2 shard_map.68
  77.5 1.3 %collective-permute-start.22 = (bf16[336,1280]{1,0:T(8,128)(2,1)S(1)}, bf16[336,1280]{1,0:T(8,128)(2,1)S(1)}, u32[]{:S(2)}, u32[]{:S(2)}) collective-permute-start(bf16[336,1280]{1,0:T(8,128)(2,1)S(1)} %shard_map.68), channel_id=1, source_target_pairs={{0,128},{64,192},{128,16},{192,80},{16,144},{80,208},{144,0},{208,... | collective-permute-start | bytes 2580488 | tf_op jit(solution)/shard_map/ppermute | solution.py:44
  78.8 1.2 %collective-permute-start.14 = (bf16[272,1280]{1,0:T(8,128)(2,1)S(1)}, bf16[272,1280]{1,0:T(8,128)(2,1)S(1)}, u32[]{:S(2)}, u32[]{:S(2)}) collective-permute-start(bf16[272,1280]{1,0:T(8,128)(2,1)S(1)} %get-tuple-element.54), channel_id=1, source_target_pairs={{0,8},{1,9},{2,10},{3,11},{4,12},{5,13},{6,14},{7,15},{8,0},{9,1},... | collective-permute-start | bytes 2088968 | tf_op jit(solution)/shard_map/ppermute | solution.py:35
  80.1 0.6 collective-permute-start.16
  80.6 2.7 %collective-permute-start.15 = (bf16[272,1280]{1,0:T(8,128)(2,1)S(1)}, bf16[272,1280]{1,0:T(8,128)(2,1)S(1)}, u32[]{:S(2)}, u32[]{:S(2)}) collective-permute-start(bf16[272,1280]{1,0:T(8,128)(2,1)S(1)} %get-tuple-element.55.refs_5_), channel_id=1, source_target_pairs={{0,12},{1,13},{2,14},{3,15},{4,0},{5,1},{6,2},{7,3},{8,4},{9,5},{1... | collective-permute-start | bytes 2088968 | tf_op jit(solution)/shard_map/ppermute | solution.py:35
  83.3 1.6 %shard_map.64 = (bf16[256,1280]{1,0:T(8,128)(2,1)S(1)}, bf16[256,1280]{1,0:T(8,128)(2,1)S(1)}) custom-call(f32[1]{0:T(128)S(6)} %copy.6.scale, bf16[1024,1024]{1,0:T(8,128)(2,1)S(1)} %get-tuple-element.50.weights, bf16[1024,1280]{1,0:T(8,128)(2,1)S(1)} %get-tuple-element.49.images, bf16[1024,1280]{1,0:T(8,128)(2,1)S(1)} %get-tuple-element.51.texts), custom_call_target="tpu_custom_call" | custom-call | tf_op jit(solution)/shard_map/pallas_call | solution.py:422
  84.9 16.5 %collective-permute-done.22.refs_2_ = bf16[336,1280]{1,0:T(8,128)(2,1)S(1)} collective-permute-done((bf16[336,1280]{1,0:T(8,128)(2,1)S(1)}, bf16[336,1280]{1,0:T(8,128)(2,1)S(1)}, u32[]{:S(2)}, u32[]{:S(2)}) %collective-permute-start.22) | collective-permute-done | bytes 860192 | tf_op jit(solution)/shard_map/ppermute | solution.py:44
  101.4 0.2 shard_map.69
  101.6 0.1 collective-permute-start.23
  101.7 0.0 collective-permute-done.14.refs_1_
  101.7 0.0 collective-permute-done.15.refs_2_
  101.7 0.4 shard_map.66
  102.1 1.4 %collective-permute-start.17 = (bf16[80,1280]{1,0:T(8,128)(2,1)S(1)}, bf16[80,1280]{1,0:T(8,128)(2,1)S(1)}, u32[]{:S(2)}, u32[]{:S(2)}) collective-permute-start(bf16[80,1280]{1,0:T(8,128)(2,1)S(1)} %get-tuple-element.58), channel_id=1, source_target_pairs={{0,2},{1,3},{2,0},{3,1},{4,6},{5,7},{6,4},{7,5},{8,10},{9,11},{10,... | collective-permute-start | bytes 614408 | tf_op jit(solution)/shard_map/ppermute | solution.py:35
  103.6 1.9 %collective-permute-start.18 = (bf16[80,1280]{1,0:T(8,128)(2,1)S(1)}, bf16[80,1280]{1,0:T(8,128)(2,1)S(1)}, u32[]{:S(2)}, u32[]{:S(2)}) collective-permute-start(bf16[80,1280]{1,0:T(8,128)(2,1)S(1)} %get-tuple-element.59), channel_id=1, source_target_pairs={{0,3},{1,0},{2,1},{3,2},{4,7},{5,4},{6,5},{7,6},{8,11},{9,8},{10,9... | collective-permute-start | bytes 614408 | tf_op jit(solution)/shard_map/ppermute | solution.py:35
  105.5 0.9 collective-permute-start.24
  106.4 0.0 collective-permute-start.19
  106.4 2.8 %collective-permute-done.23.refs_1_ = bf16[144,1280]{1,0:T(8,128)(2,1)S(1)} collective-permute-done((bf16[144,1280]{1,0:T(8,128)(2,1)S(1)}, bf16[144,1280]{1,0:T(8,128)(2,1)S(1)}, u32[]{:S(2)}, u32[]{:S(2)}) %collective-permute-start.23) | collective-permute-done | bytes 368672 | tf_op jit(solution)/shard_map/ppermute | solution.py:44
  109.2 0.1 collective-permute-start.25
  109.3 5.5 %collective-permute-done.24.refs_2_ = bf16[80,1280]{1,0:T(8,128)(2,1)S(1)} collective-permute-done((bf16[80,1280]{1,0:T(8,128)(2,1)S(1)}, bf16[80,1280]{1,0:T(8,128)(2,1)S(1)}, u32[]{:S(2)}, u32[]{:S(2)}) %collective-permute-start.24) | collective-permute-done | bytes 204832 | tf_op jit(solution)/shard_map/ppermute | solution.py:44
  114.9 0.1 shard_map.70.refs_4_
  115.0 0.0 collective-permute-done.18.refs_2_
  115.0 0.0 collective-permute-done.19.refs_3_
  115.0 0.8 shard_map.72
  (9 shorter events, 0.1 us)
Async XLA Ops:
  0.6 1.7 %collective-permute-start = (bf16[64,1280]{1,0:T(8,128)(2,1)}, bf16[64,1280]{1,0:T(8,128)(2,1)S(1)}, u32[]{:S(2)}, u32[]{:S(2)}) collective-permute-start(bf16[64,1280]{1,0:T(8,128)(2,1)} %refs_0_.1), channel_id=1, source_target_pairs={{0,32},{32,0},{1,33},{33,1},{2,34},{34,2},{3,35},{35,3},{4,36},{36... | collective-permute-start | bytes 491528 | tf_op jit(solution)/shard_map/ppermute | solution.py:48
  2.3 0.9 copy-start
  3.2 0.9 copy-start.1
  4.2 18.9 %collective-permute-start.4 = (bf16[128,1280]{1,0:T(8,128)(2,1)S(1)}, bf16[128,1280]{1,0:T(8,128)(2,1)S(1)}, u32[]{:S(2)}, u32[]{:S(2)}) collective-permute-start(bf16[128,1280]{1,0:T(8,128)(2,1)S(1)} %get-tuple-element.38.refs_4_), channel_id=1, source_target_pairs={{0,208},{64,0},{128,64},{192,128},{16,192},{80,16},{144,80},{208,1... | collective-permute-start | bytes 983048 | tf_op jit(solution)/shard_map/ppermute | solution.py:44
  6.1 17.0 %collective-permute-start.5 = (bf16[64,1280]{1,0:T(8,128)(2,1)S(1)}, bf16[64,1280]{1,0:T(8,128)(2,1)S(1)}, u32[]{:S(2)}, u32[]{:S(2)}) collective-permute-start(bf16[64,1280]{1,0:T(8,128)(2,1)S(1)} %copy-done.1), channel_id=1, source_target_pairs={{0,16},{64,80},{128,144},{192,208},{16,0},{80,64},{144,128},{208,1... | collective-permute-start | bytes 491528 | tf_op jit(solution)/shard_map/ppermute | solution.py:44
  11.6 11.5 %collective-permute-start.3 = (bf16[64,1280]{1,0:T(8,128)(2,1)S(1)}, bf16[64,1280]{1,0:T(8,128)(2,1)S(1)}, u32[]{:S(2)}, u32[]{:S(2)}) collective-permute-start(bf16[64,1280]{1,0:T(8,128)(2,1)S(1)} %get-tuple-element.37.refs_0_), channel_id=1, source_target_pairs={{0,3},{1,0},{2,1},{3,2},{4,7},{5,4},{6,5},{7,6},{8,11},{9,8},{10,9... | collective-permute-start | bytes 491528 | tf_op jit(solution)/shard_map/ppermute | solution.py:35
  14.3 8.8 %collective-permute-start.2 = (bf16[64,1280]{1,0:T(8,128)(2,1)S(1)}, bf16[64,1280]{1,0:T(8,128)(2,1)S(1)}, u32[]{:S(2)}, u32[]{:S(2)}) collective-permute-start(bf16[64,1280]{1,0:T(8,128)(2,1)S(1)} %get-tuple-element.37.refs_0_), channel_id=1, source_target_pairs={{0,2},{1,3},{2,0},{3,1},{4,6},{5,7},{6,4},{7,5},{8,10},{9,11},{10,... | collective-permute-start | bytes 491528 | tf_op jit(solution)/shard_map/ppermute | solution.py:35
  15.1 8.0 %collective-permute-start.1 = (bf16[64,1280]{1,0:T(8,128)(2,1)S(1)}, bf16[64,1280]{1,0:T(8,128)(2,1)S(1)}, u32[]{:S(2)}, u32[]{:S(2)}) collective-permute-start(bf16[64,1280]{1,0:T(8,128)(2,1)S(1)} %get-tuple-element.37.refs_0_), channel_id=1, source_target_pairs={{0,1},{1,2},{2,3},{3,0},{4,5},{5,6},{6,7},{7,4},{8,9},{9,10},{10,1... | collective-permute-start | bytes 491528 | tf_op jit(solution)/shard_map/ppermute | solution.py:35
  24.0 17.4 %collective-permute-start.9 = (bf16[256,1280]{1,0:T(8,128)(2,1)S(1)}, bf16[256,1280]{1,0:T(8,128)(2,1)S(1)}, u32[]{:S(2)}, u32[]{:S(2)}) collective-permute-start(bf16[256,1280]{1,0:T(8,128)(2,1)S(1)} %get-tuple-element.40.refs_4_), channel_id=1, source_target_pairs={{0,144},{64,208},{128,0},{192,64},{16,128},{80,192},{144,16},{208,... | collective-permute-start | bytes 1966088 | tf_op jit(solution)/shard_map/ppermute | solution.py:44
  25.9 18.5 %collective-permute-start.8 = (bf16[256,1280]{1,0:T(8,128)(2,1)S(1)}, bf16[256,1280]{1,0:T(8,128)(2,1)S(1)}, u32[]{:S(2)}, u32[]{:S(2)}) collective-permute-start(bf16[256,1280]{1,0:T(8,128)(2,1)S(1)} %get-tuple-element.39.refs_0_), channel_id=1, source_target_pairs={{0,8},{1,9},{2,10},{3,11},{4,12},{5,13},{6,14},{7,15},{8,0},{9,1},... | collective-permute-start | bytes 1966088 | tf_op jit(solution)/shard_map/ppermute | solution.py:35
  29.1 16.3 %collective-permute-start.7 = (bf16[256,1280]{1,0:T(8,128)(2,1)S(1)}, bf16[256,1280]{1,0:T(8,128)(2,1)S(1)}, u32[]{:S(2)}, u32[]{:S(2)}) collective-permute-start(bf16[256,1280]{1,0:T(8,128)(2,1)S(1)} %get-tuple-element.39.refs_0_), channel_id=1, source_target_pairs={{0,12},{1,13},{2,14},{3,15},{4,0},{5,1},{6,2},{7,3},{8,4},{9,5},{1... | collective-permute-start | bytes 1966088 | tf_op jit(solution)/shard_map/ppermute | solution.py:35
  30.2 15.2 %collective-permute-start.6 = (bf16[256,1280]{1,0:T(8,128)(2,1)S(1)}, bf16[256,1280]{1,0:T(8,128)(2,1)}, u32[]{:S(2)}, u32[]{:S(2)}) collective-permute-start(bf16[256,1280]{1,0:T(8,128)(2,1)S(1)} %get-tuple-element.39.refs_0_), channel_id=1, source_target_pairs={{0,4},{1,5},{2,6},{3,7},{4,8},{5,9},{6,10},{7,11},{8,12},{9,13},{1... | collective-permute-start | bytes 1966088 | tf_op jit(solution)/shard_map/ppermute | solution.py:35
  41.5 4.0 %collective-permute-start.10 = (bf16[256,1280]{1,0:T(8,128)(2,1)S(1)}, bf16[256,1280]{1,0:T(8,128)(2,1)}, u32[]{:S(2)}, u32[]{:S(2)}) collective-permute-start(bf16[256,1280]{1,0:T(8,128)(2,1)S(1)} %collective-permute-done.9.refs_5_), channel_id=1, source_target_pairs={{0,32},{32,0},{1,33},{33,1},{2,34},{34,2},{3,35},{35,3},{4,36},{36... | collective-permute-start | bytes 1966088 | tf_op jit(solution)/shard_map/ppermute | solution.py:48
  41.5 2.9 %collective-permute-start.11 = (bf16[192,1280]{1,0:T(8,128)(2,1)}, bf16[192,1280]{1,0:T(8,128)(2,1)}, u32[]{:S(2)}, u32[]{:S(2)}) collective-permute-start(bf16[192,1280]{1,0:T(8,128)(2,1)} %get-tuple-element.41), channel_id=1, source_target_pairs={{0,32},{32,0},{1,33},{33,1},{2,34},{34,2},{3,35},{35,3},{4,36},{36... | collective-permute-start | bytes 1474568 | tf_op jit(solution)/shard_map/ppermute | solution.py:48
  51.0 1.4 %collective-permute-start.12 = (f32[24,128]{1,0:T(8,128)S(1)}, f32[24,128]{1,0:T(8,128)S(1)}, u32[]{:S(2)}, u32[]{:S(2)}) collective-permute-start(f32[24,128]{1,0:T(8,128)S(1)} %get-tuple-element.46), channel_id=1, source_target_pairs={{0,32},{32,0},{1,33},{33,1},{2,34},{34,2},{3,35},{35,3},{4,36},{36... | collective-permute-start | bytes 36872 | tf_op jit(solution)/shard_map/ppermute | solution.py:48
  68.8 1.3 %collective-permute-start.13 = (f32[24,128]{1,0:T(8,128)S(1)}, f32[24,128]{1,0:T(8,128)S(1)}, u32[]{:S(2)}, u32[]{:S(2)}) collective-permute-start(f32[24,128]{1,0:T(8,128)S(1)} %get-tuple-element.48), channel_id=1, source_target_pairs={{0,32},{32,0},{1,33},{33,1},{2,34},{34,2},{3,35},{35,3},{4,36},{36... | collective-permute-start | bytes 36872 | tf_op jit(solution)/shard_map/ppermute | solution.py:48
  73.6 3.7 %collective-permute-start.21 = (bf16[256,1280]{1,0:T(8,128)(2,1)S(1)}, bf16[256,1280]{1,0:T(8,128)(2,1)S(1)}, u32[]{:S(2)}, u32[]{:S(2)}) collective-permute-start(bf16[256,1280]{1,0:T(8,128)(2,1)S(1)} %get-tuple-element.63), channel_id=1, source_target_pairs={{0,32},{32,0},{1,33},{33,1},{2,34},{34,2},{3,35},{35,3},{4,36},{36... | collective-permute-start | bytes 1966088 | tf_op jit(solution)/shard_map/ppermute | solution.py:48
  73.8 3.5 %collective-permute-start.20 = (bf16[192,1280]{1,0:T(8,128)(2,1)S(1)}, bf16[192,1280]{1,0:T(8,128)(2,1)S(1)}, u32[]{:S(2)}, u32[]{:S(2)}) collective-permute-start(bf16[192,1280]{1,0:T(8,128)(2,1)S(1)} %get-tuple-element.62), channel_id=1, source_target_pairs={{0,32},{32,0},{1,33},{33,1},{2,34},{34,2},{3,35},{35,3},{4,36},{36... | collective-permute-start | bytes 1474568 | tf_op jit(solution)/shard_map/ppermute | solution.py:48
  77.5 23.8 %collective-permute-start.22 = (bf16[336,1280]{1,0:T(8,128)(2,1)S(1)}, bf16[336,1280]{1,0:T(8,128)(2,1)S(1)}, u32[]{:S(2)}, u32[]{:S(2)}) collective-permute-start(bf16[336,1280]{1,0:T(8,128)(2,1)S(1)} %shard_map.68), channel_id=1, source_target_pairs={{0,128},{64,192},{128,16},{192,80},{16,144},{80,208},{144,0},{208,... | collective-permute-start | bytes 2580488 | tf_op jit(solution)/shard_map/ppermute | solution.py:44
  78.8 22.9 %collective-permute-start.14 = (bf16[272,1280]{1,0:T(8,128)(2,1)S(1)}, bf16[272,1280]{1,0:T(8,128)(2,1)S(1)}, u32[]{:S(2)}, u32[]{:S(2)}) collective-permute-start(bf16[272,1280]{1,0:T(8,128)(2,1)S(1)} %get-tuple-element.54), channel_id=1, source_target_pairs={{0,8},{1,9},{2,10},{3,11},{4,12},{5,13},{6,14},{7,15},{8,0},{9,1},... | collective-permute-start | bytes 2088968 | tf_op jit(solution)/shard_map/ppermute | solution.py:35
  80.1 21.6 %collective-permute-start.16 = (bf16[272,1280]{1,0:T(8,128)(2,1)S(1)}, bf16[272,1280]{1,0:T(8,128)(2,1)S(1)}, u32[]{:S(2)}, u32[]{:S(2)}) collective-permute-start(bf16[272,1280]{1,0:T(8,128)(2,1)S(1)} %get-tuple-element.56), channel_id=1, source_target_pairs={{0,4},{1,5},{2,6},{3,7},{4,8},{5,9},{6,10},{7,11},{8,12},{9,13},{1... | collective-permute-start | bytes 2088968 | tf_op jit(solution)/shard_map/ppermute | solution.py:35
  80.6 21.1 %collective-permute-start.15 = (bf16[272,1280]{1,0:T(8,128)(2,1)S(1)}, bf16[272,1280]{1,0:T(8,128)(2,1)S(1)}, u32[]{:S(2)}, u32[]{:S(2)}) collective-permute-start(bf16[272,1280]{1,0:T(8,128)(2,1)S(1)} %get-tuple-element.55.refs_5_), channel_id=1, source_target_pairs={{0,12},{1,13},{2,14},{3,15},{4,0},{5,1},{6,2},{7,3},{8,4},{9,5},{1... | collective-permute-start | bytes 2088968 | tf_op jit(solution)/shard_map/ppermute | solution.py:35
  101.6 7.6 %collective-permute-start.23 = (bf16[144,1280]{1,0:T(8,128)(2,1)S(1)}, bf16[144,1280]{1,0:T(8,128)(2,1)S(1)}, u32[]{:S(2)}, u32[]{:S(2)}) collective-permute-start(bf16[144,1280]{1,0:T(8,128)(2,1)S(1)} %get-tuple-element.66), channel_id=1, source_target_pairs={{0,64},{64,128},{128,192},{192,16},{16,80},{80,144},{144,208},{208... | collective-permute-start | bytes 1105928 | tf_op jit(solution)/shard_map/ppermute | solution.py:44
  102.1 12.8 %collective-permute-start.17 = (bf16[80,1280]{1,0:T(8,128)(2,1)S(1)}, bf16[80,1280]{1,0:T(8,128)(2,1)S(1)}, u32[]{:S(2)}, u32[]{:S(2)}) collective-permute-start(bf16[80,1280]{1,0:T(8,128)(2,1)S(1)} %get-tuple-element.58), channel_id=1, source_target_pairs={{0,2},{1,3},{2,0},{3,1},{4,6},{5,7},{6,4},{7,5},{8,10},{9,11},{10,... | collective-permute-start | bytes 614408 | tf_op jit(solution)/shard_map/ppermute | solution.py:35
  103.6 11.4 %collective-permute-start.18 = (bf16[80,1280]{1,0:T(8,128)(2,1)S(1)}, bf16[80,1280]{1,0:T(8,128)(2,1)S(1)}, u32[]{:S(2)}, u32[]{:S(2)}) collective-permute-start(bf16[80,1280]{1,0:T(8,128)(2,1)S(1)} %get-tuple-element.59), channel_id=1, source_target_pairs={{0,3},{1,0},{2,1},{3,2},{4,7},{5,4},{6,5},{7,6},{8,11},{9,8},{10,9... | collective-permute-start | bytes 614408 | tf_op jit(solution)/shard_map/ppermute | solution.py:35
  105.5 9.4 %collective-permute-start.24 = (bf16[80,1280]{1,0:T(8,128)(2,1)S(1)}, bf16[80,1280]{1,0:T(8,128)(2,1)S(1)}, u32[]{:S(2)}, u32[]{:S(2)}) collective-permute-start(bf16[80,1280]{1,0:T(8,128)(2,1)S(1)} %get-tuple-element.67), channel_id=1, source_target_pairs={{0,128},{64,192},{128,16},{192,80},{16,144},{80,208},{144,0},{208,... | collective-permute-start | bytes 614408 | tf_op jit(solution)/shard_map/ppermute | solution.py:44
  106.4 8.6 %collective-permute-start.19 = (bf16[80,1280]{1,0:T(8,128)(2,1)S(1)}, bf16[80,1280]{1,0:T(8,128)(2,1)S(1)}, u32[]{:S(2)}, u32[]{:S(2)}) collective-permute-start(bf16[80,1280]{1,0:T(8,128)(2,1)S(1)} %get-tuple-element.60), channel_id=1, source_target_pairs={{0,1},{1,2},{2,3},{3,0},{4,5},{5,6},{6,7},{7,4},{8,9},{9,10},{10,1... | collective-permute-start | bytes 614408 | tf_op jit(solution)/shard_map/ppermute | solution.py:35
  109.2 5.7 %collective-permute-start.25 = (bf16[80,1280]{1,0:T(8,128)(2,1)S(1)}, bf16[80,1280]{1,0:T(8,128)(2,1)S(1)}, u32[]{:S(2)}, u32[]{:S(2)}) collective-permute-start(bf16[80,1280]{1,0:T(8,128)(2,1)S(1)} %shard_map.71), channel_id=1, source_target_pairs={{0,32},{32,0},{1,33},{33,1},{2,34},{34,2},{3,35},{35,3},{4,36},{36... | collective-permute-start | bytes 614408 | tf_op jit(solution)/shard_map/ppermute | solution.py:48

commit v14 on v12

--- a/solution.py
+++ b/solution.py
@@ -98,6 +98,7 @@
 PLANE_ORDER = (0, 1, 3, 2)
 PART = jax.ShapeDtypeStruct((CHUNK, EMBED), BF16)
 ALL = jax.ShapeDtypeStruct((BLOCK, EMBED), BF16)
+HALF_WEIGHTS = jax.ShapeDtypeStruct((BLOCK, BLOCK // 2), BF16)
 
 
 def pack_body(plan, n, *refs):
@@ -298,42 +299,78 @@
     return jnp.sum(digits * units, axis=0, keepdims=True)
 
 
-def weights_body(place, scale, logits, mine, other, images, *refs):
-    weights, outs = refs[0], refs[1:5]
-    row_wide, row_lse, col_lse = refs[5:]
+def half_weights(where, logits, at, row_wide, col_lines, weights):
+    cols = col_ids(where)
+    for a in range(4):
+        ids = row_ids(where, a)
+        for b in range(4):
+            rows = slice(a * CHUNK + b * ROWS, a * CHUNK + (b + 1) * ROWS)
+            wide = row_wide[rows, :]
+            for t in range(4):
+                tile = logits[rows, (at + t) * 128 : (at + t + 1) * 128]
+                both = jnp.exp2(tile - wide) + jnp.exp2(tile - col_lines[at + t : at + t + 1, :])
+                both = both - jnp.where(ids[b] == cols[at + t][0:1], 1.0, 0.0)
+                weights[rows, t * 128 : (t + 1) * 128] = both.astype(BF16)
+
+
+def high_body(place, scale, logits, mine, other, images, *refs):
+    weights, outs, digits, row_wide, col_lines = refs[0], refs[1:4], refs[4], refs[5], refs[6]
+    row_lse, col_lse = refs[7:]
+    where = [place[i] for i in range(5)]
     first = place[1] == 0
     shares = jnp.where(first, mine[16:17, :], other[16:17, :]), jnp.where(first, other[16:17, :], mine[16:17, :])
     for i, share in enumerate(shares):
         tail = digits_of(share).astype(BF16)
         for e in range(EMBED // 128):
-            outs[3][i * TAIL : (i + 1) * TAIL, e * 128 : (e + 1) * 128] = tail
+            digits[i * TAIL : (i + 1) * TAIL, e * 128 : (e + 1) * 128] = tail
     row_lse[...] = jnp.where(first, mine[:16, :], other[:16, :]) + 1.0
     col_lse[...] = jnp.where(first, other[:16, :], mine[:16, :]) + 1.0
-    where = [place[i] for i in range(5)]
-    multiplier = scale[0]
     lane = lax.broadcasted_iota(jnp.int32, (1, 128), 1)
-    cols = col_ids(where)
-    col_line = []
     for t in range(8):
         j, i = t // 2, (t % 2) * 2
         lo = col_lse[pl.ds(col_place(where, j, i)[0], 1), :]
         hi = col_lse[pl.ds(col_place(where, j, i + 1)[0], 1), :]
-        col_line.append(jnp.where(lane < ROWS, lo, pltpu.roll(hi, 64, 1)))
+        col_lines[t : t + 1, :] = jnp.where(lane < ROWS, lo, pltpu.roll(hi, 64, 1))
         lo = row_lse[pl.ds(row_place(where, j, i)[0], 1), :]
         hi = row_lse[pl.ds(row_place(where, j, i + 1)[0], 1), :]
         line = jnp.where(lane < ROWS, lo, pltpu.roll(hi, 64, 1))
         row_wide[t * 128 : (t + 1) * 128, :] = jnp.transpose(jnp.broadcast_to(line, (128, 128)))
-    for a in range(4):
-        ids = row_ids(where, a)
-        for b in range(4):
-            at = a * CHUNK + b * ROWS
-            wide = row_wide[at : at + ROWS, :]
-            for t in range(8):
-                tile = logits[at : at + ROWS, t * 128 : (t + 1) * 128]
-                both = jnp.exp2(tile - wide) + jnp.exp2(tile - col_line[t])
-                both = both - jnp.where(ids[b] == cols[t][0:1], 1.0, 0.0)
-                weights[at : at + ROWS, t * 128 : (t + 1) * 128] = both.astype(BF16)
-    text_terms(multiplier, weights, images, 2 * CHUNK, outs[:3])
+    half_weights(where, logits, 4, row_wide, col_lines, weights)
+    text_terms(scale[0], weights, images, 0, outs)
+
+
+def high_call(place, scale, logits, mine, other, images):
+    return pl.pallas_call(
+        high_body,
+        out_shape=(
+            HALF_WEIGHTS,
+            PART,
+            jax.ShapeDtypeStruct((3 * ROWS, EMBED), BF16),
+            jax.ShapeDtypeStruct((ROWS, EMBED), BF16),
+            jax.ShapeDtypeStruct((2 * TAIL, EMBED), BF16),
+            jax.ShapeDtypeStruct((BLOCK, 128), F32),
+            jax.ShapeDtypeStruct((8, 128), F32),
+        ),
+        in_specs=[SMEM, SMEM] + [VMEM] * 4,
+        out_specs=(VMEM,) * 7,
+        scratch_shapes=[pltpu.VMEM((16, 128), F32), pltpu.VMEM((16, 128), F32)],
+        compiler_params=PARAMS,
+    )(place, scale, logits, mine, other, images)
+
+
+def low_body(place, scale, logits, row_wide, col_lines, images, weights, out):
+    half_weights([place[i] for i in range(5)], logits, 0, row_wide, col_lines, weights)
+    text_terms(scale[0], weights, images, CHUNK, [out])
+
+
+def low_call(place, scale, logits, row_wide, col_lines, images):
+    return pl.pallas_call(
+        low_body,
+        out_shape=(HALF_WEIGHTS, PART),
+        in_specs=[SMEM, SMEM] + [VMEM] * 4,
+        out_specs=(VMEM,) * 2,
+        compiler_params=PARAMS,
+    )(place, scale, logits, row_wide, col_lines, images)
 
 
 def text_terms(multiplier, weights, images, at, outs):
@@ -353,52 +390,20 @@
 
 def image_terms(multiplier, weights, texts, at, outs):
     for e in range(5):
-        term = multiplier * jnp.dot(
-            weights[at * CHUNK : (at + len(outs)) * CHUNK, :],
-            texts[:, e * 256 : (e + 1) * 256],
-            preferred_element_type=F32,
+        term = multiplier * sum(
+            jnp.dot(
+                half[at * CHUNK : (at + len(outs)) * CHUNK, :],
+                texts[h * BLOCK // 2 : (h + 1) * BLOCK // 2, e * 256 : (e + 1) * 256],
+                preferred_element_type=F32,
+            )
+            for h, half in enumerate(weights)
         )
         for i, out in enumerate(outs):
             out[:CHUNK, e * 256 : (e + 1) * 256] = term[i * CHUNK : (i + 1) * CHUNK].astype(BF16)
 
 
-def weights_call(place, scale, logits, mine, other, images):
-    return pl.pallas_call(
-        weights_body,
-        out_shape=(
-            jax.ShapeDtypeStruct((BLOCK, BLOCK), BF16),
-            PART,
-            jax.ShapeDtypeStruct((3 * ROWS, EMBED), BF16),
-            jax.ShapeDtypeStruct((ROWS, EMBED), BF16),
-            jax.ShapeDtypeStruct((2 * TAIL, EMBED), BF16),
-        ),
-        in_specs=[SMEM, SMEM] + [VMEM] * 4,
-        out_specs=(VMEM,) * 5,
-        scratch_shapes=[
-            pltpu.VMEM((BLOCK, 128), F32),
-            pltpu.VMEM((16, 128), F32),
-            pltpu.VMEM((16, 128), F32),
-        ],
-        compiler_params=PARAMS,
-    )(place, scale, logits, mine, other, images)
-
-
-def text_body(scale, weights, images, out):
-    text_terms(scale[0], weights, images, CHUNK, [out])
-
-
-def text_call(scale, weights, images):
-    return pl.pallas_call(
-        text_body,
-        out_shape=PART,
-        in_specs=[SMEM] + [VMEM] * 2,
-        out_specs=VMEM,
-        compiler_params=PARAMS,
-    )(scale, weights, images)
-
-
-def image_body(scale, after, digits, weights, texts, *outs):
-    image_terms(scale[0], weights, texts, 1, outs)
+def image_body(scale, after, digits, low, high, texts, *outs):
+    image_terms(scale[0], (low, high), texts, 1, outs)
     for out in outs:
         out[CHUNK:, :] = digits[TAIL:, :]
 
@@ -407,25 +412,25 @@
     return pl.pallas_call(
         image_body,
         out_shape=(jax.ShapeDtypeStruct((CHUNK + TAIL, EMBED), BF16),) * 3,
-        in_specs=[SMEM] + [VMEM] * 4,
+        in_specs=[SMEM] + [VMEM] * 5,
         out_specs=(VMEM,) * 3,
         compiler_params=PARAMS,
-    )(scale, after, digits, weights, texts)
-
-
-def rest_body(scale, weights, images, texts, text_out, image_out):
-    text_terms(scale[0], weights, images, 0, [text_out])
-    image_terms(scale[0], weights, texts, 0, [image_out])
+    )(scale, after, digits, *weights, texts)
+
+
+def rest_body(scale, low, high, images, texts, text_out, image_out):
+    text_terms(scale[0], low, images, 0, [text_out])
+    image_terms(scale[0], (low, high), texts, 0, [image_out])
 
 
 def rest_call(scale, weights, images, texts):
     return pl.pallas_call(
         rest_body,
         out_shape=(PART, PART),
-        in_specs=[SMEM] + [VMEM] * 3,
+        in_specs=[SMEM] + [VMEM] * 4,
         out_specs=(VMEM,) * 2,
         compiler_params=PARAMS,
-    )(scale, weights, images, texts)
+    )(scale, *weights, images, texts)
 
 
 def add_rows(refs, rows, terms, out, to):
@@ -498,12 +503,13 @@
 
     spread = spread_call(place, row_part, col_part, matched, core_swap(message))
     mine, message = join_call(place, exchange(spread, plane_or_ring()))
-    weights, text_2, text_3, far, digits = weights_call(
+    high, text_2, text_3, far, digits, row_wide, col_lines = high_call(
         place, logit_scale, logits, mine, core_swap(message), images
     )
 
     other_1, other_3 = core_swap(text_2), core_swap(text_3)
-    text_1 = text_call(logit_scale, weights, images)
+    low, text_1 = low_call(place, logit_scale, logits, row_wide, col_lines, images)
+    weights = low, high
     pairs = sums(
         [text_1, other_1, far, other_3, digits],
         ((256, ((0, 0), (1, 0))), (64, ((2, 0), (3, 128))), (TAIL, ((4, 0),))),

time: 116 us -> 116 us (level)
    ppermute x8, waiting for transfers between devices: 6.99 us -> 5.82 us  [core_swap(): return lax.ppermute(v, 'core', [(0, 1), (1, 0)])]
  transfers between devices with their start and end apart: 26 -> 26, of which waited for: 11 -> 11; matrix products, arithmetic and copies ran while one was open for 0% -> 0% of each run, Pallas kernels for 5% -> 6%
where the time goes in v14:
time: 116 us; the launch traced here: 114 us
  waiting for transfers between devices  48 us (41%)
  starting transfers between devices  29.8 us (26%)
  Pallas kernels  18.4 us (16%)
  blocking collectives  14.9 us (13%)
  local copies, waits for them, and re-layouts  1.92 us (2%)
  between operations  1.48 us (1%)
    ppermute x6, waiting for transfers between devices, z_shift(): return lax.ppermute(v, ('zl', 'core', 'zh'), pairs)  41.1 us
    ppermute x12, starting transfers between devices, plane_shift(): return lax.ppermute(v, ('core', 'zh', 'y', 'x'), pairs)  16.4 us
    all_to_all x1, blocking collectives, exchange(): return lax.all_to_all(v, AXES, 0, 0, axis_index_groups=groups)  14.9 us
    ppermute x6, starting transfers between devices, z_shift(): return lax.ppermute(v, ('zl', 'core', 'zh'), pairs)  11.7 us
    ppermute x8, waiting for transfers between devices, core_swap(): return lax.ppermute(v, 'core', [(0, 1), (1, 0)])  5.82 us
    pallas_call x1, Pallas kernels, logits_call(): pl.pallas_call(logits_body, out_shape=(jax.ShapeDtypeStruct((BLOCK, BLOCK...  5.64 us
    pallas_call x1, Pallas kernels, high_call(): pl.pallas_call(high_body, out_shape=(HALF_WEIGHTS, PART, jax.ShapeDtypeSt...  2.85 us
  transfers between devices with their start and end apart: 26, of which 11 were waited for; matrix products, arithmetic and copies ran while one was open for 0% of the time, Pallas kernels for 6%

profile of v14, /device:TPU:32, one launch (start us, length us, event | category | flops | bytes accessed | tf_op | source)
XLA Modules:
  0.0 114.4 jit_solution(5304949822739126955)
XLA Ops:
  0.6 0.1 collective-permute-start
  0.7 1.6 %collective-permute-done.refs_1_ = bf16[64,1280]{1,0:T(8,128)(2,1)S(1)} collective-permute-done((bf16[64,1280]{1,0:T(8,128)(2,1)}, bf16[64,1280]{1,0:T(8,128)(2,1)S(1)}, u32[]{:S(2)}, u32[]{:S(2)}) %collective-permute-start) | collective-permute-done | bytes 163872 | tf_op jit(solution)/shard_map/ppermute | solution.py:48
  2.3 0.9 copy-done
  3.2 0.9 copy-done.1
  4.2 1.9 %collective-permute-start.4 = (bf16[128,1280]{1,0:T(8,128)(2,1)S(1)}, bf16[128,1280]{1,0:T(8,128)(2,1)S(1)}, u32[]{:S(2)}, u32[]{:S(2)}) collective-permute-start(bf16[128,1280]{1,0:T(8,128)(2,1)S(1)} %get-tuple-element.42.refs_4_), channel_id=1, source_target_pairs={{0,208},{64,0},{128,64},{192,128},{16,192},{80,16},{144,80},{208,1... | collective-permute-start | bytes 983048 | tf_op jit(solution)/shard_map/ppermute | solution.py:44
  6.1 5.5 %collective-permute-start.5 = (bf16[64,1280]{1,0:T(8,128)(2,1)S(1)}, bf16[64,1280]{1,0:T(8,128)(2,1)S(1)}, u32[]{:S(2)}, u32[]{:S(2)}) collective-permute-start(bf16[64,1280]{1,0:T(8,128)(2,1)S(1)} %copy-done.1), channel_id=1, source_target_pairs={{0,16},{64,80},{128,144},{192,208},{16,0},{80,64},{144,128},{208,1... | collective-permute-start | bytes 491528 | tf_op jit(solution)/shard_map/ppermute | solution.py:44
  11.6 2.8 %collective-permute-start.3 = (bf16[64,1280]{1,0:T(8,128)(2,1)S(1)}, bf16[64,1280]{1,0:T(8,128)(2,1)S(1)}, u32[]{:S(2)}, u32[]{:S(2)}) collective-permute-start(bf16[64,1280]{1,0:T(8,128)(2,1)S(1)} %get-tuple-element.41.refs_0_), channel_id=1, source_target_pairs={{0,3},{1,0},{2,1},{3,2},{4,7},{5,4},{6,5},{7,6},{8,11},{9,8},{10,9... | collective-permute-start | bytes 491528 | tf_op jit(solution)/shard_map/ppermute | solution.py:35
  14.3 0.8 collective-permute-start.2
  15.1 0.9 collective-permute-start.1
  16.0 7.1 %collective-permute-done.5.refs_6_.refs_8_ = bf16[64,1280]{1,0:T(8,128)(2,1)S(1)} collective-permute-done((bf16[64,1280]{1,0:T(8,128)(2,1)S(1)}, bf16[64,1280]{1,0:T(8,128)(2,1)S(1)}, u32[]{:S(2)}, u32[]{:S(2)}) %collective-permute-start.5) | collective-permute-done | bytes 163872 | tf_op jit(solution)/shard_map/ppermute | solution.py:44
  23.1 0.0 collective-permute-done.3.refs_3_
  23.1 0.0 collective-permute-done.2.refs_2_
  23.1 0.0 collective-permute-done.1.refs_1_
  23.1 0.0 collective-permute-done.4.refs_5_
  23.1 0.9 shard_map.59
  24.0 1.9 %collective-permute-start.9 = (bf16[256,1280]{1,0:T(8,128)(2,1)S(1)}, bf16[256,1280]{1,0:T(8,128)(2,1)S(1)}, u32[]{:S(2)}, u32[]{:S(2)}) collective-permute-start(bf16[256,1280]{1,0:T(8,128)(2,1)S(1)} %get-tuple-element.44.refs_4_), channel_id=1, source_target_pairs={{0,144},{64,208},{128,0},{192,64},{16,128},{80,192},{144,16},{208,... | collective-permute-start | bytes 1966088 | tf_op jit(solution)/shard_map/ppermute | solution.py:44
  25.9 3.2 %collective-permute-start.8 = (bf16[256,1280]{1,0:T(8,128)(2,1)S(1)}, bf16[256,1280]{1,0:T(8,128)(2,1)S(1)}, u32[]{:S(2)}, u32[]{:S(2)}) collective-permute-start(bf16[256,1280]{1,0:T(8,128)(2,1)S(1)} %get-tuple-element.43.refs_0_), channel_id=1, source_target_pairs={{0,8},{1,9},{2,10},{3,11},{4,12},{5,13},{6,14},{7,15},{8,0},{9,1},... | collective-permute-start | bytes 1966088 | tf_op jit(solution)/shard_map/ppermute | solution.py:35
  29.1 1.1 collective-permute-start.7
  30.2 1.0 collective-permute-start.6
  31.1 10.3 %collective-permute-done.9.refs_5_ = bf16[256,1280]{1,0:T(8,128)(2,1)S(1)} collective-permute-done((bf16[256,1280]{1,0:T(8,128)(2,1)S(1)}, bf16[256,1280]{1,0:T(8,128)(2,1)S(1)}, u32[]{:S(2)}, u32[]{:S(2)}) %collective-permute-start.9) | collective-permute-done | bytes 655392 | tf_op jit(solution)/shard_map/ppermute | solution.py:44
  41.5 0.5 collective-permute-start.11
  42.6 0.1 stack.23.place
  42.7 1.7 %collective-permute-done.11.refs_7_ = bf16[192,1280]{1,0:T(8,128)(2,1)} collective-permute-done((bf16[192,1280]{1,0:T(8,128)(2,1)}, bf16[192,1280]{1,0:T(8,128)(2,1)}, u32[]{:S(2)}, u32[]{:S(2)}) %collective-permute-start.11) | collective-permute-done | bytes 491552 | tf_op jit(solution)/shard_map/ppermute | solution.py:48
  44.4 1.0 collective-permute-done.7.refs_2_
  45.4 0.0 collective-permute-done.6.refs_1_
  45.4 0.0 collective-permute-done.10.refs_6_
  45.4 5.6 %shard_map.60 = (f32[1024,1024]{1,0:T(8,128)S(1)}, f32[16,128]{1,0:T(8,128)S(1)}, f32[16,128]{1,0:T(8,128)S(1)}, f32[24,128]{1,0:T(8,128)S(1)}, f32[8,128]{1,0:T...) custom-call(s32[5]{0:T(128)S(1)} %stack.23.place, f32[1]{0:T(128)S(6)} %copy.6.scale, ...), custom_call_target="tpu_custom_call" | custom-call | tf_op jit(solution)/shard_map/pallas_call | solution.py:198
  51.0 0.3 collective-permute-start.12
  51.3 1.2 %collective-permute-done.12.got = f32[24,128]{1,0:T(8,128)S(1)} collective-permute-done((f32[24,128]{1,0:T(8,128)S(1)}, f32[24,128]{1,0:T(8,128)S(1)}, u32[]{:S(2)}, u32[]{:S(2)}) %collective-permute-start.12) | collective-permute-done | bytes 12320 | tf_op jit(solution)/shard_map/ppermute | solution.py:48
  52.5 0.6 shard_map.61
  53.1 14.9 %all_to_all.5.got = f32[16,24,128]{2,1,0:T(8,128)S(1)} all-to-all(f32[16,24,128]{2,1,0:T(8,128)S(1)} %shard_map.61), channel_id=1, replica_groups={{0,1,2,3,4,5,6,7,8,9,10,11,12,13,14,15},{64,65,66,67,68,69,70,71,72,73,..., dimensions={0} | all-to-all | bytes 393216 | tf_op jit(solution)/shard_map/all_to_all | solution.py:63
  68.0 0.7 shard_map.62
  68.8 0.1 collective-permute-start.13
  68.9 1.2 %collective-permute-done.13.other = f32[24,128]{1,0:T(8,128)S(1)} collective-permute-done((f32[24,128]{1,0:T(8,128)S(1)}, f32[24,128]{1,0:T(8,128)S(1)}, u32[]{:S(2)}, u32[]{:S(2)}) %collective-permute-start.13) | collective-permute-done | bytes 12320 | tf_op jit(solution)/shard_map/ppermute | solution.py:48
  70.0 2.8 %shard_map.63 = (bf16[1024,512]{1,0:T(8,128)(2,1)S(1)}, bf16[256,1280]{1,0:T(8,128)(2,1)S(1)}, bf16[192,1280]{1,0:T(8,128)(2,1)S(1)}, bf16[64,1280]{1,0:T(8,128)...) custom-call(s32[5]{0:T(128)S(1)} %stack.23.place, f32[1]{0:T(128)S(6)} %copy.6.scale, ...), custom_call_target="tpu_custom_call" | custom-call | tf_op jit(solution)/shard_map/pallas_call | solution.py:343
  72.9 0.3 collective-permute-start.14
  73.1 0.3 collective-permute-start.15
  73.5 2.1 %shard_map.64 = (bf16[1024,512]{1,0:T(8,128)(2,1)S(1)}, bf16[256,1280]{1,0:T(8,128)(2,1)S(1)}) custom-call(s32[5]{0:T(128)S(1)} %stack.23.place, f32[1]{0:T(128)S(6)} %copy.6.scale, f32[1024,1024]{1,0:T(8,128)S(1)} %get-tuple-element.46.logits, f32[1024,128]{1,0:T(8,128)S(1)} %get-tuple-element.54.row_wide, f32[8,128]{1,0:T(8,128)S(1)} %get-tuple-element.55.col_lines, ...), custom_call_target="tpu_custom_call" | custom-call | tf_op jit(solution)/shard_map/pallas_call | solution.py:367
  75.6 0.2 collective-permute-done.15.refs_3_.refs_1_
  75.8 0.0 collective-permute-done.14.refs_1_
  75.8 0.2 shard_map.66.after
  76.0 1.3 %collective-permute-start.22 = (bf16[336,1280]{1,0:T(8,128)(2,1)S(1)}, bf16[336,1280]{1,0:T(8,128)(2,1)S(1)}, u32[]{:S(2)}, u32[]{:S(2)}) collective-permute-start(bf16[336,1280]{1,0:T(8,128)(2,1)S(1)} %shard_map.66.after), channel_id=1, source_target_pairs={{0,128},{64,192},{128,16},{192,80},{16,144},{80,208},{144,0},{208,... | collective-permute-start | bytes 2580488 | tf_op jit(solution)/shard_map/ppermute | solution.py:44
  77.2 2.2 %shard_map.67 = (bf16[272,1280]{1,0:T(8,128)(2,1)S(1)}, bf16[272,1280]{1,0:T(8,128)(2,1)S(1)}, bf16[272,1280]{1,0:T(8,128)(2,1)S(1)}) custom-call(f32[1]{0:T(128)S(6)} %copy.6.scale, bf16[336,1280]{1,0:T(8,128)(2,1)S(1)} %shard_map.66.after, bf16[32,1280]{1,0:T(8,128)(2,1)S(1)} %get-tuple-element.64.refs_4_.digits.refs_3_.refs_6_, ...), custom_call_target="tpu_custom_call" | custom-call | tf_op jit(solution)/shard_map/pallas_call | solution.py:412
  79.4 1.3 %collective-permute-start.16 = (bf16[272,1280]{1,0:T(8,128)(2,1)S(1)}, bf16[272,1280]{1,0:T(8,128)(2,1)S(1)}, u32[]{:S(2)}, u32[]{:S(2)}) collective-permute-start(bf16[272,1280]{1,0:T(8,128)(2,1)S(1)} %get-tuple-element.65), channel_id=1, source_target_pairs={{0,8},{1,9},{2,10},{3,11},{4,12},{5,13},{6,14},{7,15},{8,0},{9,1},... | collective-permute-start | bytes 2088968 | tf_op jit(solution)/shard_map/ppermute | solution.py:35
  80.8 1.5 %collective-permute-start.17 = (bf16[272,1280]{1,0:T(8,128)(2,1)S(1)}, bf16[272,1280]{1,0:T(8,128)(2,1)S(1)}, u32[]{:S(2)}, u32[]{:S(2)}) collective-permute-start(bf16[272,1280]{1,0:T(8,128)(2,1)S(1)} %get-tuple-element.66), channel_id=1, source_target_pairs={{0,12},{1,13},{2,14},{3,15},{4,0},{5,1},{6,2},{7,3},{8,4},{9,5},{1... | collective-permute-start | bytes 2088968 | tf_op jit(solution)/shard_map/ppermute | solution.py:35
  82.2 0.6 collective-permute-start.18
  82.8 1.6 %shard_map.65 = (bf16[256,1280]{1,0:T(8,128)(2,1)S(1)}, bf16[256,1280]{1,0:T(8,128)(2,1)S(1)}) custom-call(f32[1]{0:T(128)S(6)} %copy.6.scale, bf16[1024,512]{1,0:T(8,128)(2,1)S(1)} %get-tuple-element.56.low, bf16[1024,512]{1,0:T(8,128)(2,1)S(1)} %get-tuple-element.57.high, bf16[1024,1280]{1,0:T(8,128)(2,1)S(1)} %get-tuple-element.53.images, ...), custom_call_target="tpu_custom_call" | custom-call | tf_op jit(solution)/shard_map/pallas_call | solution.py:427
  84.4 15.4 %collective-permute-done.22.refs_2_ = bf16[336,1280]{1,0:T(8,128)(2,1)S(1)} collective-permute-done((bf16[336,1280]{1,0:T(8,128)(2,1)S(1)}, bf16[336,1280]{1,0:T(8,128)(2,1)S(1)}, u32[]{:S(2)}, u32[]{:S(2)}) %collective-permute-start.22) | collective-permute-done | bytes 860192 | tf_op jit(solution)/shard_map/ppermute | solution.py:44
  99.8 0.2 shard_map.69
  100.0 0.3 collective-permute-start.23
  100.4 0.0 collective-permute-done.16.refs_1_
  100.4 0.0 collective-permute-done.17.refs_2_
  100.4 0.4 shard_map.68
  100.8 1.4 %collective-permute-start.19 = (bf16[80,1280]{1,0:T(8,128)(2,1)S(1)}, bf16[80,1280]{1,0:T(8,128)(2,1)S(1)}, u32[]{:S(2)}, u32[]{:S(2)}) collective-permute-start(bf16[80,1280]{1,0:T(8,128)(2,1)S(1)} %get-tuple-element.69), channel_id=1, source_target_pairs={{0,2},{1,3},{2,0},{3,1},{4,6},{5,7},{6,4},{7,5},{8,10},{9,11},{10,... | collective-permute-start | bytes 614408 | tf_op jit(solution)/shard_map/ppermute | solution.py:35
  102.2 1.9 %collective-permute-start.20 = (bf16[80,1280]{1,0:T(8,128)(2,1)S(1)}, bf16[80,1280]{1,0:T(8,128)(2,1)S(1)}, u32[]{:S(2)}, u32[]{:S(2)}) collective-permute-start(bf16[80,1280]{1,0:T(8,128)(2,1)S(1)} %get-tuple-element.70), channel_id=1, source_target_pairs={{0,3},{1,0},{2,1},{3,2},{4,7},{5,4},{6,5},{7,6},{8,11},{9,8},{10,9... | collective-permute-start | bytes 614408 | tf_op jit(solution)/shard_map/ppermute | solution.py:35
  104.1 0.9 collective-permute-start.24
  105.0 0.1 collective-permute-start.21
  105.1 2.8 %collective-permute-done.23.refs_1_ = bf16[144,1280]{1,0:T(8,128)(2,1)S(1)} collective-permute-done((bf16[144,1280]{1,0:T(8,128)(2,1)S(1)}, bf16[144,1280]{1,0:T(8,128)(2,1)S(1)}, u32[]{:S(2)}, u32[]{:S(2)}) %collective-permute-start.23) | collective-permute-done | bytes 368672 | tf_op jit(solution)/shard_map/ppermute | solution.py:44
  107.9 0.1 collective-permute-start.25
  108.0 5.5 %collective-permute-done.24.refs_2_ = bf16[80,1280]{1,0:T(8,128)(2,1)S(1)} collective-permute-done((bf16[80,1280]{1,0:T(8,128)(2,1)S(1)}, bf16[80,1280]{1,0:T(8,128)(2,1)S(1)}, u32[]{:S(2)}, u32[]{:S(2)}) %collective-permute-start.24) | collective-permute-done | bytes 204832 | tf_op jit(solution)/shard_map/ppermute | solution.py:44
  113.5 0.1 shard_map.70.refs_4_
  113.6 0.0 collective-permute-done.19.refs_1_
  113.6 0.0 collective-permute-done.25.refs_5_
  113.6 0.8 shard_map.72
  (9 shorter events, 0.1 us)
Async XLA Ops:
  0.6 1.7 %collective-permute-start = (bf16[64,1280]{1,0:T(8,128)(2,1)}, bf16[64,1280]{1,0:T(8,128)(2,1)S(1)}, u32[]{:S(2)}, u32[]{:S(2)}) collective-permute-start(bf16[64,1280]{1,0:T(8,128)(2,1)} %refs_0_.1), channel_id=1, source_target_pairs={{0,32},{32,0},{1,33},{33,1},{2,34},{34,2},{3,35},{35,3},{4,36},{36... | collective-permute-start | bytes 491528 | tf_op jit(solution)/shard_map/ppermute | solution.py:48
  2.3 0.9 copy-start
  3.2 0.9 copy-start.1
  4.2 18.9 %collective-permute-start.4 = (bf16[128,1280]{1,0:T(8,128)(2,1)S(1)}, bf16[128,1280]{1,0:T(8,128)(2,1)S(1)}, u32[]{:S(2)}, u32[]{:S(2)}) collective-permute-start(bf16[128,1280]{1,0:T(8,128)(2,1)S(1)} %get-tuple-element.42.refs_4_), channel_id=1, source_target_pairs={{0,208},{64,0},{128,64},{192,128},{16,192},{80,16},{144,80},{208,1... | collective-permute-start | bytes 983048 | tf_op jit(solution)/shard_map/ppermute | solution.py:44
  6.1 17.0 %collective-permute-start.5 = (bf16[64,1280]{1,0:T(8,128)(2,1)S(1)}, bf16[64,1280]{1,0:T(8,128)(2,1)S(1)}, u32[]{:S(2)}, u32[]{:S(2)}) collective-permute-start(bf16[64,1280]{1,0:T(8,128)(2,1)S(1)} %copy-done.1), channel_id=1, source_target_pairs={{0,16},{64,80},{128,144},{192,208},{16,0},{80,64},{144,128},{208,1... | collective-permute-start | bytes 491528 | tf_op jit(solution)/shard_map/ppermute | solution.py:44
  11.6 11.5 %collective-permute-start.3 = (bf16[64,1280]{1,0:T(8,128)(2,1)S(1)}, bf16[64,1280]{1,0:T(8,128)(2,1)S(1)}, u32[]{:S(2)}, u32[]{:S(2)}) collective-permute-start(bf16[64,1280]{1,0:T(8,128)(2,1)S(1)} %get-tuple-element.41.refs_0_), channel_id=1, source_target_pairs={{0,3},{1,0},{2,1},{3,2},{4,7},{5,4},{6,5},{7,6},{8,11},{9,8},{10,9... | collective-permute-start | bytes 491528 | tf_op jit(solution)/shard_map/ppermute | solution.py:35
  14.3 8.8 %collective-permute-start.2 = (bf16[64,1280]{1,0:T(8,128)(2,1)S(1)}, bf16[64,1280]{1,0:T(8,128)(2,1)S(1)}, u32[]{:S(2)}, u32[]{:S(2)}) collective-permute-start(bf16[64,1280]{1,0:T(8,128)(2,1)S(1)} %get-tuple-element.41.refs_0_), channel_id=1, source_target_pairs={{0,2},{1,3},{2,0},{3,1},{4,6},{5,7},{6,4},{7,5},{8,10},{9,11},{10,... | collective-permute-start | bytes 491528 | tf_op jit(solution)/shard_map/ppermute | solution.py:35
  15.1 8.0 %collective-permute-start.1 = (bf16[64,1280]{1,0:T(8,128)(2,1)S(1)}, bf16[64,1280]{1,0:T(8,128)(2,1)S(1)}, u32[]{:S(2)}, u32[]{:S(2)}) collective-permute-start(bf16[64,1280]{1,0:T(8,128)(2,1)S(1)} %get-tuple-element.41.refs_0_), channel_id=1, source_target_pairs={{0,1},{1,2},{2,3},{3,0},{4,5},{5,6},{6,7},{7,4},{8,9},{9,10},{10,1... | collective-permute-start | bytes 491528 | tf_op jit(solution)/shard_map/ppermute | solution.py:35
  24.0 17.4 %collective-permute-start.9 = (bf16[256,1280]{1,0:T(8,128)(2,1)S(1)}, bf16[256,1280]{1,0:T(8,128)(2,1)S(1)}, u32[]{:S(2)}, u32[]{:S(2)}) collective-permute-start(bf16[256,1280]{1,0:T(8,128)(2,1)S(1)} %get-tuple-element.44.refs_4_), channel_id=1, source_target_pairs={{0,144},{64,208},{128,0},{192,64},{16,128},{80,192},{144,16},{208,... | collective-permute-start | bytes 1966088 | tf_op jit(solution)/shard_map/ppermute | solution.py:44
  25.9 18.5 %collective-permute-start.8 = (bf16[256,1280]{1,0:T(8,128)(2,1)S(1)}, bf16[256,1280]{1,0:T(8,128)(2,1)S(1)}, u32[]{:S(2)}, u32[]{:S(2)}) collective-permute-start(bf16[256,1280]{1,0:T(8,128)(2,1)S(1)} %get-tuple-element.43.refs_0_), channel_id=1, source_target_pairs={{0,8},{1,9},{2,10},{3,11},{4,12},{5,13},{6,14},{7,15},{8,0},{9,1},... | collective-permute-start | bytes 1966088 | tf_op jit(solution)/shard_map/ppermute | solution.py:35
  29.1 16.3 %collective-permute-start.7 = (bf16[256,1280]{1,0:T(8,128)(2,1)S(1)}, bf16[256,1280]{1,0:T(8,128)(2,1)S(1)}, u32[]{:S(2)}, u32[]{:S(2)}) collective-permute-start(bf16[256,1280]{1,0:T(8,128)(2,1)S(1)} %get-tuple-element.43.refs_0_), channel_id=1, source_target_pairs={{0,12},{1,13},{2,14},{3,15},{4,0},{5,1},{6,2},{7,3},{8,4},{9,5},{1... | collective-permute-start | bytes 1966088 | tf_op jit(solution)/shard_map/ppermute | solution.py:35
  30.2 15.2 %collective-permute-start.6 = (bf16[256,1280]{1,0:T(8,128)(2,1)S(1)}, bf16[256,1280]{1,0:T(8,128)(2,1)}, u32[]{:S(2)}, u32[]{:S(2)}) collective-permute-start(bf16[256,1280]{1,0:T(8,128)(2,1)S(1)} %get-tuple-element.43.refs_0_), channel_id=1, source_target_pairs={{0,4},{1,5},{2,6},{3,7},{4,8},{5,9},{6,10},{7,11},{8,12},{9,13},{1... | collective-permute-start | bytes 1966088 | tf_op jit(solution)/shard_map/ppermute | solution.py:35
  41.5 4.0 %collective-permute-start.10 = (bf16[256,1280]{1,0:T(8,128)(2,1)S(1)}, bf16[256,1280]{1,0:T(8,128)(2,1)}, u32[]{:S(2)}, u32[]{:S(2)}) collective-permute-start(bf16[256,1280]{1,0:T(8,128)(2,1)S(1)} %collective-permute-done.9.refs_5_), channel_id=1, source_target_pairs={{0,32},{32,0},{1,33},{33,1},{2,34},{34,2},{3,35},{35,3},{4,36},{36... | collective-permute-start | bytes 1966088 | tf_op jit(solution)/shard_map/ppermute | solution.py:48
  41.5 2.9 %collective-permute-start.11 = (bf16[192,1280]{1,0:T(8,128)(2,1)}, bf16[192,1280]{1,0:T(8,128)(2,1)}, u32[]{:S(2)}, u32[]{:S(2)}) collective-permute-start(bf16[192,1280]{1,0:T(8,128)(2,1)} %get-tuple-element.45), channel_id=1, source_target_pairs={{0,32},{32,0},{1,33},{33,1},{2,34},{34,2},{3,35},{35,3},{4,36},{36... | collective-permute-start | bytes 1474568 | tf_op jit(solution)/shard_map/ppermute | solution.py:48
  51.0 1.4 %collective-permute-start.12 = (f32[24,128]{1,0:T(8,128)S(1)}, f32[24,128]{1,0:T(8,128)S(1)}, u32[]{:S(2)}, u32[]{:S(2)}) collective-permute-start(f32[24,128]{1,0:T(8,128)S(1)} %get-tuple-element.50), channel_id=1, source_target_pairs={{0,32},{32,0},{1,33},{33,1},{2,34},{34,2},{3,35},{35,3},{4,36},{36... | collective-permute-start | bytes 36872 | tf_op jit(solution)/shard_map/ppermute | solution.py:48
  68.8 1.3 %collective-permute-start.13 = (f32[24,128]{1,0:T(8,128)S(1)}, f32[24,128]{1,0:T(8,128)S(1)}, u32[]{:S(2)}, u32[]{:S(2)}) collective-permute-start(f32[24,128]{1,0:T(8,128)S(1)} %get-tuple-element.52), channel_id=1, source_target_pairs={{0,32},{32,0},{1,33},{33,1},{2,34},{34,2},{3,35},{35,3},{4,36},{36... | collective-permute-start | bytes 36872 | tf_op jit(solution)/shard_map/ppermute | solution.py:48
  72.9 2.9 %collective-permute-start.14 = (bf16[256,1280]{1,0:T(8,128)(2,1)S(1)}, bf16[256,1280]{1,0:T(8,128)(2,1)S(1)}, u32[]{:S(2)}, u32[]{:S(2)}) collective-permute-start(bf16[256,1280]{1,0:T(8,128)(2,1)S(1)} %get-tuple-element.61), channel_id=1, source_target_pairs={{0,32},{32,0},{1,33},{33,1},{2,34},{34,2},{3,35},{35,3},{4,36},{36... | collective-permute-start | bytes 1966088 | tf_op jit(solution)/shard_map/ppermute | solution.py:48
  73.1 2.6 %collective-permute-start.15 = (bf16[192,1280]{1,0:T(8,128)(2,1)S(1)}, bf16[192,1280]{1,0:T(8,128)(2,1)S(1)}, u32[]{:S(2)}, u32[]{:S(2)}) collective-permute-start(bf16[192,1280]{1,0:T(8,128)(2,1)S(1)} %get-tuple-element.63), channel_id=1, source_target_pairs={{0,32},{32,0},{1,33},{33,1},{2,34},{34,2},{3,35},{35,3},{4,36},{36... | collective-permute-start | bytes 1474568 | tf_op jit(solution)/shard_map/ppermute | solution.py:48
  76.0 23.9 %collective-permute-start.22 = (bf16[336,1280]{1,0:T(8,128)(2,1)S(1)}, bf16[336,1280]{1,0:T(8,128)(2,1)S(1)}, u32[]{:S(2)}, u32[]{:S(2)}) collective-permute-start(bf16[336,1280]{1,0:T(8,128)(2,1)S(1)} %shard_map.66.after), channel_id=1, source_target_pairs={{0,128},{64,192},{128,16},{192,80},{16,144},{80,208},{144,0},{208,... | collective-permute-start | bytes 2580488 | tf_op jit(solution)/shard_map/ppermute | solution.py:44
  79.4 20.9 %collective-permute-start.16 = (bf16[272,1280]{1,0:T(8,128)(2,1)S(1)}, bf16[272,1280]{1,0:T(8,128)(2,1)S(1)}, u32[]{:S(2)}, u32[]{:S(2)}) collective-permute-start(bf16[272,1280]{1,0:T(8,128)(2,1)S(1)} %get-tuple-element.65), channel_id=1, source_target_pairs={{0,8},{1,9},{2,10},{3,11},{4,12},{5,13},{6,14},{7,15},{8,0},{9,1},... | collective-permute-start | bytes 2088968 | tf_op jit(solution)/shard_map/ppermute | solution.py:35
  80.8 19.6 %collective-permute-start.17 = (bf16[272,1280]{1,0:T(8,128)(2,1)S(1)}, bf16[272,1280]{1,0:T(8,128)(2,1)S(1)}, u32[]{:S(2)}, u32[]{:S(2)}) collective-permute-start(bf16[272,1280]{1,0:T(8,128)(2,1)S(1)} %get-tuple-element.66), channel_id=1, source_target_pairs={{0,12},{1,13},{2,14},{3,15},{4,0},{5,1},{6,2},{7,3},{8,4},{9,5},{1... | collective-permute-start | bytes 2088968 | tf_op jit(solution)/shard_map/ppermute | solution.py:35
  82.2 18.2 %collective-permute-start.18 = (bf16[272,1280]{1,0:T(8,128)(2,1)S(1)}, bf16[272,1280]{1,0:T(8,128)(2,1)S(1)}, u32[]{:S(2)}, u32[]{:S(2)}) collective-permute-start(bf16[272,1280]{1,0:T(8,128)(2,1)S(1)} %get-tuple-element.67), channel_id=1, source_target_pairs={{0,4},{1,5},{2,6},{3,7},{4,8},{5,9},{6,10},{7,11},{8,12},{9,13},{1... | collective-permute-start | bytes 2088968 | tf_op jit(solution)/shard_map/ppermute | solution.py:35
  100.0 7.8 %collective-permute-start.23 = (bf16[144,1280]{1,0:T(8,128)(2,1)S(1)}, bf16[144,1280]{1,0:T(8,128)(2,1)S(1)}, u32[]{:S(2)}, u32[]{:S(2)}) collective-permute-start(bf16[144,1280]{1,0:T(8,128)(2,1)S(1)} %get-tuple-element.74), channel_id=1, source_target_pairs={{0,64},{64,128},{128,192},{192,16},{16,80},{80,144},{144,208},{208... | collective-permute-start | bytes 1105928 | tf_op jit(solution)/shard_map/ppermute | solution.py:44
  100.8 12.8 %collective-permute-start.19 = (bf16[80,1280]{1,0:T(8,128)(2,1)S(1)}, bf16[80,1280]{1,0:T(8,128)(2,1)S(1)}, u32[]{:S(2)}, u32[]{:S(2)}) collective-permute-start(bf16[80,1280]{1,0:T(8,128)(2,1)S(1)} %get-tuple-element.69), channel_id=1, source_target_pairs={{0,2},{1,3},{2,0},{3,1},{4,6},{5,7},{6,4},{7,5},{8,10},{9,11},{10,... | collective-permute-start | bytes 614408 | tf_op jit(solution)/shard_map/ppermute | solution.py:35
  102.2 11.4 %collective-permute-start.20 = (bf16[80,1280]{1,0:T(8,128)(2,1)S(1)}, bf16[80,1280]{1,0:T(8,128)(2,1)S(1)}, u32[]{:S(2)}, u32[]{:S(2)}) collective-permute-start(bf16[80,1280]{1,0:T(8,128)(2,1)S(1)} %get-tuple-element.70), channel_id=1, source_target_pairs={{0,3},{1,0},{2,1},{3,2},{4,7},{5,4},{6,5},{7,6},{8,11},{9,8},{10,9... | collective-permute-start | bytes 614408 | tf_op jit(solution)/shard_map/ppermute | solution.py:35
  104.1 9.4 %collective-permute-start.24 = (bf16[80,1280]{1,0:T(8,128)(2,1)S(1)}, bf16[80,1280]{1,0:T(8,128)(2,1)S(1)}, u32[]{:S(2)}, u32[]{:S(2)}) collective-permute-start(bf16[80,1280]{1,0:T(8,128)(2,1)S(1)} %get-tuple-element.75), channel_id=1, source_target_pairs={{0,128},{64,192},{128,16},{192,80},{16,144},{80,208},{144,0},{208,... | collective-permute-start | bytes 614408 | tf_op jit(solution)/shard_map/ppermute | solution.py:44
  105.0 8.6 %collective-permute-start.21 = (bf16[80,1280]{1,0:T(8,128)(2,1)S(1)}, bf16[80,1280]{1,0:T(8,128)(2,1)S(1)}, u32[]{:S(2)}, u32[]{:S(2)}) collective-permute-start(bf16[80,1280]{1,0:T(8,128)(2,1)S(1)} %get-tuple-element.71), channel_id=1, source_target_pairs={{0,1},{1,2},{2,3},{3,0},{4,5},{5,6},{6,7},{7,4},{8,9},{9,10},{10,1... | collective-permute-start | bytes 614408 | tf_op jit(solution)/shard_map/ppermute | solution.py:35
  107.9 5.7 %collective-permute-start.25 = (bf16[80,1280]{1,0:T(8,128)(2,1)S(1)}, bf16[80,1280]{1,0:T(8,128)(2,1)S(1)}, u32[]{:S(2)}, u32[]{:S(2)}) collective-permute-start(bf16[80,1280]{1,0:T(8,128)(2,1)S(1)} %shard_map.71), channel_id=1, source_target_pairs={{0,32},{32,0},{1,33},{33,1},{2,34},{34,2},{3,35},{35,3},{4,36},{36... | collective-permute-start | bytes 614408 | tf_op jit(solution)/shard_map/ppermute | solution.py:48

commit v15 on v14

--- a/solution.py
+++ b/solution.py
@@ -122,6 +122,12 @@
 
 def fold(v):
     return v.reshape(v.shape[0] // 8, 8, 128)
+
+
+def two_sums(v):
+    coarse = 8.0 * jnp.floor(v * 0.125 + 0.5)
+    parts = [jnp.sum(p, keepdims=True) for p in (coarse, v - coarse)]
+    return jnp.where(lax.broadcasted_iota(jnp.int32, (8, 128), 0) < 4, *parts)
 
 
 def column_part(logits, t, top):
@@ -180,7 +186,7 @@
                     matched += jnp.sum(fold(hit), axis=0)
                 part = top + LOG2E * jnp.log(jnp.sum(total, axis=1, keepdims=True))
                 row_wide[at : at + step, :] = jnp.broadcast_to(part, (step, 128))
-    matched = jnp.broadcast_to(jnp.sum(matched, keepdims=True), (8, 128))
+    matched = two_sums(matched)
     match_out[...] = matched
     message[16:24, :] = matched
     for t in range(8):
@@ -261,8 +267,7 @@
     hits = got[0, 16:24, :]
     for i in range(1, 16):
         hits += got[i, 16:24, :]
-    both = low + jnp.where(first, high, 0.0)
-    share = jnp.sum(both, keepdims=True) - jnp.where(first, 2.0 * hits, 0.0)
+    share = two_sums(low) + jnp.where(first, two_sums(high) - 2.0 * hits, 0.0)
     for out, pairs in ((mine, low), (message, jnp.where(first, high, low))):
         for i in range(8):
             out[2 * i : 2 * i + 1, :] = pairs[i : i + 1]
@@ -292,11 +297,10 @@
 
 
 def value_of(digits):
-    place = lax.broadcasted_iota(jnp.int32, (16, 128), 0)
-    units = jnp.zeros((16, 128), F32)
-    for i in range(DIGITS):
-        units = jnp.where(place == i, 16.0 ** (7 - i), units)
-    return jnp.sum(digits * units, axis=0, keepdims=True)
+    total = digits[0:1] * 16.0**7
+    for i in range(1, DIGITS):
+        total = total + digits[i : i + 1] * 16.0 ** (7 - i)
+    return total
 
 
 def half_weights(where, logits, at, row_wide, col_lines, weights):
@@ -318,9 +322,10 @@
     row_lse, col_lse = refs[7:]
     where = [place[i] for i in range(5)]
     first = place[1] == 0
-    shares = jnp.where(first, mine[16:17, :], other[16:17, :]), jnp.where(first, other[16:17, :], mine[16:17, :])
-    for i, share in enumerate(shares):
-        tail = digits_of(share).astype(BF16)
+    for i, own in enumerate((first, jnp.logical_not(first))):
+        tail = sum(
+            digits_of(jnp.where(own, mine[r : r + 1, :], other[r : r + 1, :])) for r in (16, 20)
+        ).astype(BF16)
         for e in range(EMBED // 128):
             digits[i * TAIL : (i + 1) * TAIL, e * 128 : (e + 1) * 128] = tail
     row_lse[...] = jnp.where(first, mine[:16, :], other[:16, :]) + 1.0

time: 116 us -> 116 us (level)
  no operation moved by 1% of the time
where the time goes in v15:
time: 116 us; the launch traced here: 114 us
  waiting for transfers between devices  47.9 us (41%)
  starting transfers between devices  29.8 us (26%)
  Pallas kernels  18.3 us (16%)
  blocking collectives  14.9 us (13%)
  local copies, waits for them, and re-layouts  1.92 us (2%)
  between operations  1.48 us (1%)
    ppermute x6, waiting for transfers between devices, z_shift(): return lax.ppermute(v, ('zl', 'core', 'zh'), pairs)  41.1 us
    ppermute x12, starting transfers between devices, plane_shift(): return lax.ppermute(v, ('core', 'zh', 'y', 'x'), pairs)  16.5 us
    all_to_all x1, blocking collectives, exchange(): return lax.all_to_all(v, AXES, 0, 0, axis_index_groups=groups)  14.9 us
    ppermute x6, starting transfers between devices, z_shift(): return lax.ppermute(v, ('zl', 'core', 'zh'), pairs)  11.7 us
    ppermute x8, waiting for transfers between devices, core_swap(): return lax.ppermute(v, 'core', [(0, 1), (1, 0)])  5.82 us
    pallas_call x1, Pallas kernels, logits_call(): pl.pallas_call(logits_body, out_shape=(jax.ShapeDtypeStruct((BLOCK, BLOCK...  5.53 us
    pallas_call x1, Pallas kernels, high_call(): pl.pallas_call(high_body, out_shape=(HALF_WEIGHTS, PART, jax.ShapeDtypeSt...  2.84 us
  transfers between devices with their start and end apart: 26, of which 11 were waited for; matrix products, arithmetic and copies ran while one was open for 0% of the time, Pallas kernels for 6%

profile of v15, /device:TPU:32, one launch (start us, length us, event | category | flops | bytes accessed | tf_op | source)
XLA Modules:
  0.0 114.3 jit_solution(2975586096466482800)
XLA Ops:
  0.6 0.1 collective-permute-start
  0.7 1.6 %collective-permute-done.refs_1_ = bf16[64,1280]{1,0:T(8,128)(2,1)S(1)} collective-permute-done((bf16[64,1280]{1,0:T(8,128)(2,1)}, bf16[64,1280]{1,0:T(8,128)(2,1)S(1)}, u32[]{:S(2)}, u32[]{:S(2)}) %collective-permute-start) | collective-permute-done | bytes 163872 | tf_op jit(solution)/shard_map/ppermute | solution.py:48
  2.3 0.9 copy-done
  3.2 0.9 copy-done.1
  4.2 1.9 %collective-permute-start.4 = (bf16[128,1280]{1,0:T(8,128)(2,1)S(1)}, bf16[128,1280]{1,0:T(8,128)(2,1)S(1)}, u32[]{:S(2)}, u32[]{:S(2)}) collective-permute-start(bf16[128,1280]{1,0:T(8,128)(2,1)S(1)} %get-tuple-element.42.refs_4_), channel_id=1, source_target_pairs={{0,208},{64,0},{128,64},{192,128},{16,192},{80,16},{144,80},{208,1... | collective-permute-start | bytes 983048 | tf_op jit(solution)/shard_map/ppermute | solution.py:44
  6.1 5.5 %collective-permute-start.5 = (bf16[64,1280]{1,0:T(8,128)(2,1)S(1)}, bf16[64,1280]{1,0:T(8,128)(2,1)S(1)}, u32[]{:S(2)}, u32[]{:S(2)}) collective-permute-start(bf16[64,1280]{1,0:T(8,128)(2,1)S(1)} %copy-done.1), channel_id=1, source_target_pairs={{0,16},{64,80},{128,144},{192,208},{16,0},{80,64},{144,128},{208,1... | collective-permute-start | bytes 491528 | tf_op jit(solution)/shard_map/ppermute | solution.py:44
  11.6 2.8 %collective-permute-start.3 = (bf16[64,1280]{1,0:T(8,128)(2,1)S(1)}, bf16[64,1280]{1,0:T(8,128)(2,1)S(1)}, u32[]{:S(2)}, u32[]{:S(2)}) collective-permute-start(bf16[64,1280]{1,0:T(8,128)(2,1)S(1)} %get-tuple-element.41.refs_0_), channel_id=1, source_target_pairs={{0,3},{1,0},{2,1},{3,2},{4,7},{5,4},{6,5},{7,6},{8,11},{9,8},{10,9... | collective-permute-start | bytes 491528 | tf_op jit(solution)/shard_map/ppermute | solution.py:35
  14.3 0.8 collective-permute-start.2
  15.1 0.9 collective-permute-start.1
  16.0 7.1 %collective-permute-done.5.refs_6_.refs_8_ = bf16[64,1280]{1,0:T(8,128)(2,1)S(1)} collective-permute-done((bf16[64,1280]{1,0:T(8,128)(2,1)S(1)}, bf16[64,1280]{1,0:T(8,128)(2,1)S(1)}, u32[]{:S(2)}, u32[]{:S(2)}) %collective-permute-start.5) | collective-permute-done | bytes 163872 | tf_op jit(solution)/shard_map/ppermute | solution.py:44
  23.1 0.0 collective-permute-done.3.refs_3_
  23.1 0.0 collective-permute-done.2.refs_2_
  23.1 0.0 collective-permute-done.1.refs_1_
  23.1 0.0 collective-permute-done.4.refs_5_
  23.1 0.9 shard_map.59
  24.0 1.9 %collective-permute-start.9 = (bf16[256,1280]{1,0:T(8,128)(2,1)S(1)}, bf16[256,1280]{1,0:T(8,128)(2,1)S(1)}, u32[]{:S(2)}, u32[]{:S(2)}) collective-permute-start(bf16[256,1280]{1,0:T(8,128)(2,1)S(1)} %get-tuple-element.44.refs_4_), channel_id=1, source_target_pairs={{0,144},{64,208},{128,0},{192,64},{16,128},{80,192},{144,16},{208,... | collective-permute-start | bytes 1966088 | tf_op jit(solution)/shard_map/ppermute | solution.py:44
  25.9 3.2 %collective-permute-start.8 = (bf16[256,1280]{1,0:T(8,128)(2,1)S(1)}, bf16[256,1280]{1,0:T(8,128)(2,1)S(1)}, u32[]{:S(2)}, u32[]{:S(2)}) collective-permute-start(bf16[256,1280]{1,0:T(8,128)(2,1)S(1)} %get-tuple-element.43.refs_0_), channel_id=1, source_target_pairs={{0,8},{1,9},{2,10},{3,11},{4,12},{5,13},{6,14},{7,15},{8,0},{9,1},... | collective-permute-start | bytes 1966088 | tf_op jit(solution)/shard_map/ppermute | solution.py:35
  29.1 1.1 collective-permute-start.7
  30.2 1.0 collective-permute-start.6
  31.1 10.3 %collective-permute-done.9.refs_5_ = bf16[256,1280]{1,0:T(8,128)(2,1)S(1)} collective-permute-done((bf16[256,1280]{1,0:T(8,128)(2,1)S(1)}, bf16[256,1280]{1,0:T(8,128)(2,1)S(1)}, u32[]{:S(2)}, u32[]{:S(2)}) %collective-permute-start.9) | collective-permute-done | bytes 655392 | tf_op jit(solution)/shard_map/ppermute | solution.py:44
  41.5 0.5 collective-permute-start.11
  42.6 0.1 stack.23.place
  42.7 1.7 %collective-permute-done.11.refs_7_ = bf16[192,1280]{1,0:T(8,128)(2,1)} collective-permute-done((bf16[192,1280]{1,0:T(8,128)(2,1)}, bf16[192,1280]{1,0:T(8,128)(2,1)}, u32[]{:S(2)}, u32[]{:S(2)}) %collective-permute-start.11) | collective-permute-done | bytes 491552 | tf_op jit(solution)/shard_map/ppermute | solution.py:48
  44.4 0.0 collective-permute-done.8.refs_3_
  44.4 1.0 collective-permute-done.7.refs_2_
  45.4 0.0 collective-permute-done.6.refs_1_
  45.4 0.0 collective-permute-done.10.refs_6_
  45.4 5.5 %shard_map.60 = (f32[1024,1024]{1,0:T(8,128)S(1)}, f32[16,128]{1,0:T(8,128)S(1)}, f32[16,128]{1,0:T(8,128)S(1)}, f32[24,128]{1,0:T(8,128)S(1)}, f32[8,128]{1,0:T...) custom-call(s32[5]{0:T(128)S(1)} %stack.23.place, f32[1]{0:T(128)S(6)} %copy.6.scale, ...), custom_call_target="tpu_custom_call" | custom-call | tf_op jit(solution)/shard_map/pallas_call | solution.py:204
  50.9 0.2 collective-permute-start.12
  51.2 1.2 %collective-permute-done.12.got = f32[24,128]{1,0:T(8,128)S(1)} collective-permute-done((f32[24,128]{1,0:T(8,128)S(1)}, f32[24,128]{1,0:T(8,128)S(1)}, u32[]{:S(2)}, u32[]{:S(2)}) %collective-permute-start.12) | collective-permute-done | bytes 12320 | tf_op jit(solution)/shard_map/ppermute | solution.py:48
  52.4 0.6 shard_map.61
  53.0 14.9 %all_to_all.5.got = f32[16,24,128]{2,1,0:T(8,128)S(1)} all-to-all(f32[16,24,128]{2,1,0:T(8,128)S(1)} %shard_map.61), channel_id=1, replica_groups={{0,1,2,3,4,5,6,7,8,9,10,11,12,13,14,15},{64,65,66,67,68,69,70,71,72,73,..., dimensions={0} | all-to-all | bytes 393216 | tf_op jit(solution)/shard_map/all_to_all | solution.py:63
  67.9 0.7 shard_map.62
  68.6 0.1 collective-permute-start.13
  68.7 1.2 %collective-permute-done.13.other = f32[24,128]{1,0:T(8,128)S(1)} collective-permute-done((f32[24,128]{1,0:T(8,128)S(1)}, f32[24,128]{1,0:T(8,128)S(1)}, u32[]{:S(2)}, u32[]{:S(2)}) %collective-permute-start.13) | collective-permute-done | bytes 12320 | tf_op jit(solution)/shard_map/ppermute | solution.py:48
  69.9 2.8 %shard_map.63 = (bf16[1024,512]{1,0:T(8,128)(2,1)S(1)}, bf16[256,1280]{1,0:T(8,128)(2,1)S(1)}, bf16[192,1280]{1,0:T(8,128)(2,1)S(1)}, bf16[64,1280]{1,0:T(8,128)...) custom-call(s32[5]{0:T(128)S(1)} %stack.23.place, f32[1]{0:T(128)S(6)} %copy.6.scale, ...), custom_call_target="tpu_custom_call" | custom-call | tf_op jit(solution)/shard_map/pallas_call | solution.py:348
  72.7 0.3 collective-permute-start.14
  73.0 0.3 collective-permute-start.15
  73.3 2.1 %shard_map.64 = (bf16[1024,512]{1,0:T(8,128)(2,1)S(1)}, bf16[256,1280]{1,0:T(8,128)(2,1)S(1)}) custom-call(s32[5]{0:T(128)S(1)} %stack.23.place, f32[1]{0:T(128)S(6)} %copy.6.scale, f32[1024,1024]{1,0:T(8,128)S(1)} %get-tuple-element.46.logits, f32[1024,128]{1,0:T(8,128)S(1)} %get-tuple-element.54.row_wide, f32[8,128]{1,0:T(8,128)S(1)} %get-tuple-element.55.col_lines, ...), custom_call_target="tpu_custom_call" | custom-call | tf_op jit(solution)/shard_map/pallas_call | solution.py:372
  75.4 0.2 collective-permute-done.15.refs_3_.refs_1_
  75.6 0.0 collective-permute-done.14.refs_1_
  75.6 0.2 shard_map.66.after
  75.8 1.3 %collective-permute-start.22 = (bf16[336,1280]{1,0:T(8,128)(2,1)S(1)}, bf16[336,1280]{1,0:T(8,128)(2,1)S(1)}, u32[]{:S(2)}, u32[]{:S(2)}) collective-permute-start(bf16[336,1280]{1,0:T(8,128)(2,1)S(1)} %shard_map.66.after), channel_id=1, source_target_pairs={{0,128},{64,192},{128,16},{192,80},{16,144},{80,208},{144,0},{208,... | collective-permute-start | bytes 2580488 | tf_op jit(solution)/shard_map/ppermute | solution.py:44
  77.1 2.2 %shard_map.67 = (bf16[272,1280]{1,0:T(8,128)(2,1)S(1)}, bf16[272,1280]{1,0:T(8,128)(2,1)S(1)}, bf16[272,1280]{1,0:T(8,128)(2,1)S(1)}) custom-call(f32[1]{0:T(128)S(6)} %copy.6.scale, bf16[336,1280]{1,0:T(8,128)(2,1)S(1)} %shard_map.66.after, bf16[32,1280]{1,0:T(8,128)(2,1)S(1)} %get-tuple-element.64.refs_4_.digits.refs_3_.refs_6_, ...), custom_call_target="tpu_custom_call" | custom-call | tf_op jit(solution)/shard_map/pallas_call | solution.py:417
  79.3 1.4 %collective-permute-start.16 = (bf16[272,1280]{1,0:T(8,128)(2,1)S(1)}, bf16[272,1280]{1,0:T(8,128)(2,1)S(1)}, u32[]{:S(2)}, u32[]{:S(2)}) collective-permute-start(bf16[272,1280]{1,0:T(8,128)(2,1)S(1)} %get-tuple-element.65), channel_id=1, source_target_pairs={{0,8},{1,9},{2,10},{3,11},{4,12},{5,13},{6,14},{7,15},{8,0},{9,1},... | collective-permute-start | bytes 2088968 | tf_op jit(solution)/shard_map/ppermute | solution.py:35
  80.7 1.4 %collective-permute-start.17 = (bf16[272,1280]{1,0:T(8,128)(2,1)S(1)}, bf16[272,1280]{1,0:T(8,128)(2,1)S(1)}, u32[]{:S(2)}, u32[]{:S(2)}) collective-permute-start(bf16[272,1280]{1,0:T(8,128)(2,1)S(1)} %get-tuple-element.66), channel_id=1, source_target_pairs={{0,12},{1,13},{2,14},{3,15},{4,0},{5,1},{6,2},{7,3},{8,4},{9,5},{1... | collective-permute-start | bytes 2088968 | tf_op jit(solution)/shard_map/ppermute | solution.py:35
  82.1 0.6 collective-permute-start.18
  82.7 1.6 %shard_map.65 = (bf16[256,1280]{1,0:T(8,128)(2,1)S(1)}, bf16[256,1280]{1,0:T(8,128)(2,1)S(1)}) custom-call(f32[1]{0:T(128)S(6)} %copy.6.scale, bf16[1024,512]{1,0:T(8,128)(2,1)S(1)} %get-tuple-element.56.low, bf16[1024,512]{1,0:T(8,128)(2,1)S(1)} %get-tuple-element.57.high, bf16[1024,1280]{1,0:T(8,128)(2,1)S(1)} %get-tuple-element.53.images, ...), custom_call_target="tpu_custom_call" | custom-call | tf_op jit(solution)/shard_map/pallas_call | solution.py:432
  84.3 15.4 %collective-permute-done.22.refs_2_ = bf16[336,1280]{1,0:T(8,128)(2,1)S(1)} collective-permute-done((bf16[336,1280]{1,0:T(8,128)(2,1)S(1)}, bf16[336,1280]{1,0:T(8,128)(2,1)S(1)}, u32[]{:S(2)}, u32[]{:S(2)}) %collective-permute-start.22) | collective-permute-done | bytes 860192 | tf_op jit(solution)/shard_map/ppermute | solution.py:44
  99.7 0.2 shard_map.69
  99.9 0.3 collective-permute-start.23
  100.2 0.0 collective-permute-done.17.refs_2_
  100.2 0.0 collective-permute-done.18.refs_3_
  100.2 0.4 shard_map.68
  100.7 1.4 %collective-permute-start.19 = (bf16[80,1280]{1,0:T(8,128)(2,1)S(1)}, bf16[80,1280]{1,0:T(8,128)(2,1)S(1)}, u32[]{:S(2)}, u32[]{:S(2)}) collective-permute-start(bf16[80,1280]{1,0:T(8,128)(2,1)S(1)} %get-tuple-element.69), channel_id=1, source_target_pairs={{0,2},{1,3},{2,0},{3,1},{4,6},{5,7},{6,4},{7,5},{8,10},{9,11},{10,... | collective-permute-start | bytes 614408 | tf_op jit(solution)/shard_map/ppermute | solution.py:35
  102.1 1.9 %collective-permute-start.20 = (bf16[80,1280]{1,0:T(8,128)(2,1)S(1)}, bf16[80,1280]{1,0:T(8,128)(2,1)S(1)}, u32[]{:S(2)}, u32[]{:S(2)}) collective-permute-start(bf16[80,1280]{1,0:T(8,128)(2,1)S(1)} %get-tuple-element.70), channel_id=1, source_target_pairs={{0,3},{1,0},{2,1},{3,2},{4,7},{5,4},{6,5},{7,6},{8,11},{9,8},{10,9... | collective-permute-start | bytes 614408 | tf_op jit(solution)/shard_map/ppermute | solution.py:35
  104.0 0.9 collective-permute-start.24
  104.9 0.1 collective-permute-start.21
  105.0 2.8 %collective-permute-done.23.refs_1_ = bf16[144,1280]{1,0:T(8,128)(2,1)S(1)} collective-permute-done((bf16[144,1280]{1,0:T(8,128)(2,1)S(1)}, bf16[144,1280]{1,0:T(8,128)(2,1)S(1)}, u32[]{:S(2)}, u32[]{:S(2)}) %collective-permute-start.23) | collective-permute-done | bytes 368672 | tf_op jit(solution)/shard_map/ppermute | solution.py:44
  107.8 0.1 collective-permute-start.25
  107.9 5.5 %collective-permute-done.24.refs_2_ = bf16[80,1280]{1,0:T(8,128)(2,1)S(1)} collective-permute-done((bf16[80,1280]{1,0:T(8,128)(2,1)S(1)}, bf16[80,1280]{1,0:T(8,128)(2,1)S(1)}, u32[]{:S(2)}, u32[]{:S(2)}) %collective-permute-start.24) | collective-permute-done | bytes 204832 | tf_op jit(solution)/shard_map/ppermute | solution.py:44
  113.4 0.1 shard_map.70.refs_4_
  113.5 0.0 collective-permute-done.19.refs_1_
  113.5 0.8 shard_map.72
  (9 shorter events, 0.1 us)
Async XLA Ops:
  0.6 1.7 %collective-permute-start = (bf16[64,1280]{1,0:T(8,128)(2,1)}, bf16[64,1280]{1,0:T(8,128)(2,1)S(1)}, u32[]{:S(2)}, u32[]{:S(2)}) collective-permute-start(bf16[64,1280]{1,0:T(8,128)(2,1)} %refs_0_.1), channel_id=1, source_target_pairs={{0,32},{32,0},{1,33},{33,1},{2,34},{34,2},{3,35},{35,3},{4,36},{36... | collective-permute-start | bytes 491528 | tf_op jit(solution)/shard_map/ppermute | solution.py:48
  2.3 0.9 copy-start
  3.2 0.9 copy-start.1
  4.2 18.9 %collective-permute-start.4 = (bf16[128,1280]{1,0:T(8,128)(2,1)S(1)}, bf16[128,1280]{1,0:T(8,128)(2,1)S(1)}, u32[]{:S(2)}, u32[]{:S(2)}) collective-permute-start(bf16[128,1280]{1,0:T(8,128)(2,1)S(1)} %get-tuple-element.42.refs_4_), channel_id=1, source_target_pairs={{0,208},{64,0},{128,64},{192,128},{16,192},{80,16},{144,80},{208,1... | collective-permute-start | bytes 983048 | tf_op jit(solution)/shard_map/ppermute | solution.py:44
  6.1 17.0 %collective-permute-start.5 = (bf16[64,1280]{1,0:T(8,128)(2,1)S(1)}, bf16[64,1280]{1,0:T(8,128)(2,1)S(1)}, u32[]{:S(2)}, u32[]{:S(2)}) collective-permute-start(bf16[64,1280]{1,0:T(8,128)(2,1)S(1)} %copy-done.1), channel_id=1, source_target_pairs={{0,16},{64,80},{128,144},{192,208},{16,0},{80,64},{144,128},{208,1... | collective-permute-start | bytes 491528 | tf_op jit(solution)/shard_map/ppermute | solution.py:44
  11.6 11.5 %collective-permute-start.3 = (bf16[64,1280]{1,0:T(8,128)(2,1)S(1)}, bf16[64,1280]{1,0:T(8,128)(2,1)S(1)}, u32[]{:S(2)}, u32[]{:S(2)}) collective-permute-start(bf16[64,1280]{1,0:T(8,128)(2,1)S(1)} %get-tuple-element.41.refs_0_), channel_id=1, source_target_pairs={{0,3},{1,0},{2,1},{3,2},{4,7},{5,4},{6,5},{7,6},{8,11},{9,8},{10,9... | collective-permute-start | bytes 491528 | tf_op jit(solution)/shard_map/ppermute | solution.py:35
  14.3 8.8 %collective-permute-start.2 = (bf16[64,1280]{1,0:T(8,128)(2,1)S(1)}, bf16[64,1280]{1,0:T(8,128)(2,1)S(1)}, u32[]{:S(2)}, u32[]{:S(2)}) collective-permute-start(bf16[64,1280]{1,0:T(8,128)(2,1)S(1)} %get-tuple-element.41.refs_0_), channel_id=1, source_target_pairs={{0,2},{1,3},{2,0},{3,1},{4,6},{5,7},{6,4},{7,5},{8,10},{9,11},{10,... | collective-permute-start | bytes 491528 | tf_op jit(solution)/shard_map/ppermute | solution.py:35
  15.1 8.0 %collective-permute-start.1 = (bf16[64,1280]{1,0:T(8,128)(2,1)S(1)}, bf16[64,1280]{1,0:T(8,128)(2,1)S(1)}, u32[]{:S(2)}, u32[]{:S(2)}) collective-permute-start(bf16[64,1280]{1,0:T(8,128)(2,1)S(1)} %get-tuple-element.41.refs_0_), channel_id=1, source_target_pairs={{0,1},{1,2},{2,3},{3,0},{4,5},{5,6},{6,7},{7,4},{8,9},{9,10},{10,1... | collective-permute-start | bytes 491528 | tf_op jit(solution)/shard_map/ppermute | solution.py:35
  24.0 17.4 %collective-permute-start.9 = (bf16[256,1280]{1,0:T(8,128)(2,1)S(1)}, bf16[256,1280]{1,0:T(8,128)(2,1)S(1)}, u32[]{:S(2)}, u32[]{:S(2)}) collective-permute-start(bf16[256,1280]{1,0:T(8,128)(2,1)S(1)} %get-tuple-element.44.refs_4_), channel_id=1, source_target_pairs={{0,144},{64,208},{128,0},{192,64},{16,128},{80,192},{144,16},{208,... | collective-permute-start | bytes 1966088 | tf_op jit(solution)/shard_map/ppermute | solution.py:44
  25.9 18.5 %collective-permute-start.8 = (bf16[256,1280]{1,0:T(8,128)(2,1)S(1)}, bf16[256,1280]{1,0:T(8,128)(2,1)S(1)}, u32[]{:S(2)}, u32[]{:S(2)}) collective-permute-start(bf16[256,1280]{1,0:T(8,128)(2,1)S(1)} %get-tuple-element.43.refs_0_), channel_id=1, source_target_pairs={{0,8},{1,9},{2,10},{3,11},{4,12},{5,13},{6,14},{7,15},{8,0},{9,1},... | collective-permute-start | bytes 1966088 | tf_op jit(solution)/shard_map/ppermute | solution.py:35
  29.1 16.3 %collective-permute-start.7 = (bf16[256,1280]{1,0:T(8,128)(2,1)S(1)}, bf16[256,1280]{1,0:T(8,128)(2,1)S(1)}, u32[]{:S(2)}, u32[]{:S(2)}) collective-permute-start(bf16[256,1280]{1,0:T(8,128)(2,1)S(1)} %get-tuple-element.43.refs_0_), channel_id=1, source_target_pairs={{0,12},{1,13},{2,14},{3,15},{4,0},{5,1},{6,2},{7,3},{8,4},{9,5},{1... | collective-permute-start | bytes 1966088 | tf_op jit(solution)/shard_map/ppermute | solution.py:35
  30.2 15.2 %collective-permute-start.6 = (bf16[256,1280]{1,0:T(8,128)(2,1)S(1)}, bf16[256,1280]{1,0:T(8,128)(2,1)}, u32[]{:S(2)}, u32[]{:S(2)}) collective-permute-start(bf16[256,1280]{1,0:T(8,128)(2,1)S(1)} %get-tuple-element.43.refs_0_), channel_id=1, source_target_pairs={{0,4},{1,5},{2,6},{3,7},{4,8},{5,9},{6,10},{7,11},{8,12},{9,13},{1... | collective-permute-start | bytes 1966088 | tf_op jit(solution)/shard_map/ppermute | solution.py:35
  41.5 4.0 %collective-permute-start.10 = (bf16[256,1280]{1,0:T(8,128)(2,1)S(1)}, bf16[256,1280]{1,0:T(8,128)(2,1)}, u32[]{:S(2)}, u32[]{:S(2)}) collective-permute-start(bf16[256,1280]{1,0:T(8,128)(2,1)S(1)} %collective-permute-done.9.refs_5_), channel_id=1, source_target_pairs={{0,32},{32,0},{1,33},{33,1},{2,34},{34,2},{3,35},{35,3},{4,36},{36... | collective-permute-start | bytes 1966088 | tf_op jit(solution)/shard_map/ppermute | solution.py:48
  41.5 2.9 %collective-permute-start.11 = (bf16[192,1280]{1,0:T(8,128)(2,1)}, bf16[192,1280]{1,0:T(8,128)(2,1)}, u32[]{:S(2)}, u32[]{:S(2)}) collective-permute-start(bf16[192,1280]{1,0:T(8,128)(2,1)} %get-tuple-element.45), channel_id=1, source_target_pairs={{0,32},{32,0},{1,33},{33,1},{2,34},{34,2},{3,35},{35,3},{4,36},{36... | collective-permute-start | bytes 1474568 | tf_op jit(solution)/shard_map/ppermute | solution.py:48
  50.9 1.4 %collective-permute-start.12 = (f32[24,128]{1,0:T(8,128)S(1)}, f32[24,128]{1,0:T(8,128)S(1)}, u32[]{:S(2)}, u32[]{:S(2)}) collective-permute-start(f32[24,128]{1,0:T(8,128)S(1)} %get-tuple-element.50), channel_id=1, source_target_pairs={{0,32},{32,0},{1,33},{33,1},{2,34},{34,2},{3,35},{35,3},{4,36},{36... | collective-permute-start | bytes 36872 | tf_op jit(solution)/shard_map/ppermute | solution.py:48
  68.6 1.3 %collective-permute-start.13 = (f32[24,128]{1,0:T(8,128)S(1)}, f32[24,128]{1,0:T(8,128)S(1)}, u32[]{:S(2)}, u32[]{:S(2)}) collective-permute-start(f32[24,128]{1,0:T(8,128)S(1)} %get-tuple-element.52), channel_id=1, source_target_pairs={{0,32},{32,0},{1,33},{33,1},{2,34},{34,2},{3,35},{35,3},{4,36},{36... | collective-permute-start | bytes 36872 | tf_op jit(solution)/shard_map/ppermute | solution.py:48
  72.7 2.9 %collective-permute-start.14 = (bf16[256,1280]{1,0:T(8,128)(2,1)S(1)}, bf16[256,1280]{1,0:T(8,128)(2,1)S(1)}, u32[]{:S(2)}, u32[]{:S(2)}) collective-permute-start(bf16[256,1280]{1,0:T(8,128)(2,1)S(1)} %get-tuple-element.61), channel_id=1, source_target_pairs={{0,32},{32,0},{1,33},{33,1},{2,34},{34,2},{3,35},{35,3},{4,36},{36... | collective-permute-start | bytes 1966088 | tf_op jit(solution)/shard_map/ppermute | solution.py:48
  73.0 2.6 %collective-permute-start.15 = (bf16[192,1280]{1,0:T(8,128)(2,1)S(1)}, bf16[192,1280]{1,0:T(8,128)(2,1)S(1)}, u32[]{:S(2)}, u32[]{:S(2)}) collective-permute-start(bf16[192,1280]{1,0:T(8,128)(2,1)S(1)} %get-tuple-element.63), channel_id=1, source_target_pairs={{0,32},{32,0},{1,33},{33,1},{2,34},{34,2},{3,35},{35,3},{4,36},{36... | collective-permute-start | bytes 1474568 | tf_op jit(solution)/shard_map/ppermute | solution.py:48
  75.8 23.9 %collective-permute-start.22 = (bf16[336,1280]{1,0:T(8,128)(2,1)S(1)}, bf16[336,1280]{1,0:T(8,128)(2,1)S(1)}, u32[]{:S(2)}, u32[]{:S(2)}) collective-permute-start(bf16[336,1280]{1,0:T(8,128)(2,1)S(1)} %shard_map.66.after), channel_id=1, source_target_pairs={{0,128},{64,192},{128,16},{192,80},{16,144},{80,208},{144,0},{208,... | collective-permute-start | bytes 2580488 | tf_op jit(solution)/shard_map/ppermute | solution.py:44
  79.3 20.9 %collective-permute-start.16 = (bf16[272,1280]{1,0:T(8,128)(2,1)S(1)}, bf16[272,1280]{1,0:T(8,128)(2,1)S(1)}, u32[]{:S(2)}, u32[]{:S(2)}) collective-permute-start(bf16[272,1280]{1,0:T(8,128)(2,1)S(1)} %get-tuple-element.65), channel_id=1, source_target_pairs={{0,8},{1,9},{2,10},{3,11},{4,12},{5,13},{6,14},{7,15},{8,0},{9,1},... | collective-permute-start | bytes 2088968 | tf_op jit(solution)/shard_map/ppermute | solution.py:35
  80.7 19.6 %collective-permute-start.17 = (bf16[272,1280]{1,0:T(8,128)(2,1)S(1)}, bf16[272,1280]{1,0:T(8,128)(2,1)S(1)}, u32[]{:S(2)}, u32[]{:S(2)}) collective-permute-start(bf16[272,1280]{1,0:T(8,128)(2,1)S(1)} %get-tuple-element.66), channel_id=1, source_target_pairs={{0,12},{1,13},{2,14},{3,15},{4,0},{5,1},{6,2},{7,3},{8,4},{9,5},{1... | collective-permute-start | bytes 2088968 | tf_op jit(solution)/shard_map/ppermute | solution.py:35
  82.1 18.1 %collective-permute-start.18 = (bf16[272,1280]{1,0:T(8,128)(2,1)S(1)}, bf16[272,1280]{1,0:T(8,128)(2,1)S(1)}, u32[]{:S(2)}, u32[]{:S(2)}) collective-permute-start(bf16[272,1280]{1,0:T(8,128)(2,1)S(1)} %get-tuple-element.67), channel_id=1, source_target_pairs={{0,4},{1,5},{2,6},{3,7},{4,8},{5,9},{6,10},{7,11},{8,12},{9,13},{1... | collective-permute-start | bytes 2088968 | tf_op jit(solution)/shard_map/ppermute | solution.py:35
  99.9 7.8 %collective-permute-start.23 = (bf16[144,1280]{1,0:T(8,128)(2,1)S(1)}, bf16[144,1280]{1,0:T(8,128)(2,1)S(1)}, u32[]{:S(2)}, u32[]{:S(2)}) collective-permute-start(bf16[144,1280]{1,0:T(8,128)(2,1)S(1)} %get-tuple-element.74), channel_id=1, source_target_pairs={{0,64},{64,128},{128,192},{192,16},{16,80},{80,144},{144,208},{208... | collective-permute-start | bytes 1105928 | tf_op jit(solution)/shard_map/ppermute | solution.py:44
  100.7 12.8 %collective-permute-start.19 = (bf16[80,1280]{1,0:T(8,128)(2,1)S(1)}, bf16[80,1280]{1,0:T(8,128)(2,1)S(1)}, u32[]{:S(2)}, u32[]{:S(2)}) collective-permute-start(bf16[80,1280]{1,0:T(8,128)(2,1)S(1)} %get-tuple-element.69), channel_id=1, source_target_pairs={{0,2},{1,3},{2,0},{3,1},{4,6},{5,7},{6,4},{7,5},{8,10},{9,11},{10,... | collective-permute-start | bytes 614408 | tf_op jit(solution)/shard_map/ppermute | solution.py:35
  102.1 11.4 %collective-permute-start.20 = (bf16[80,1280]{1,0:T(8,128)(2,1)S(1)}, bf16[80,1280]{1,0:T(8,128)(2,1)S(1)}, u32[]{:S(2)}, u32[]{:S(2)}) collective-permute-start(bf16[80,1280]{1,0:T(8,128)(2,1)S(1)} %get-tuple-element.70), channel_id=1, source_target_pairs={{0,3},{1,0},{2,1},{3,2},{4,7},{5,4},{6,5},{7,6},{8,11},{9,8},{10,9... | collective-permute-start | bytes 614408 | tf_op jit(solution)/shard_map/ppermute | solution.py:35
  104.0 9.4 %collective-permute-start.24 = (bf16[80,1280]{1,0:T(8,128)(2,1)S(1)}, bf16[80,1280]{1,0:T(8,128)(2,1)S(1)}, u32[]{:S(2)}, u32[]{:S(2)}) collective-permute-start(bf16[80,1280]{1,0:T(8,128)(2,1)S(1)} %get-tuple-element.75), channel_id=1, source_target_pairs={{0,128},{64,192},{128,16},{192,80},{16,144},{80,208},{144,0},{208,... | collective-permute-start | bytes 614408 | tf_op jit(solution)/shard_map/ppermute | solution.py:44
  104.9 8.6 %collective-permute-start.21 = (bf16[80,1280]{1,0:T(8,128)(2,1)S(1)}, bf16[80,1280]{1,0:T(8,128)(2,1)S(1)}, u32[]{:S(2)}, u32[]{:S(2)}) collective-permute-start(bf16[80,1280]{1,0:T(8,128)(2,1)S(1)} %get-tuple-element.71), channel_id=1, source_target_pairs={{0,1},{1,2},{2,3},{3,0},{4,5},{5,6},{6,7},{7,4},{8,9},{9,10},{10,1... | collective-permute-start | bytes 614408 | tf_op jit(solution)/shard_map/ppermute | solution.py:35
  107.8 5.7 %collective-permute-start.25 = (bf16[80,1280]{1,0:T(8,128)(2,1)S(1)}, bf16[80,1280]{1,0:T(8,128)(2,1)S(1)}, u32[]{:S(2)}, u32[]{:S(2)}) collective-permute-start(bf16[80,1280]{1,0:T(8,128)(2,1)S(1)} %shard_map.71), channel_id=1, source_target_pairs={{0,32},{32,0},{1,33},{33,1},{2,34},{34,2},{3,35},{35,3},{4,36},{36... | collective-permute-start | bytes 614408 | tf_op jit(solution)/shard_map/ppermute | solution.py:48

commit v16 on v15

--- a/solution.py
+++ b/solution.py
@@ -491,15 +491,17 @@
 def local(image_emb, text_emb, logit_scale):
     place = jnp.stack([lax.axis_index(n) for n in AXES]).astype(jnp.int32)
 
-    chip, image = pack([text_emb, core_swap(text_emb), image_emb], ((0, 64), (1, 64)), ((2, 64),))
+    (text,) = pack([text_emb], ((0, 64),))
+    (image,) = pack([image_emb], ((0, 64),))
+    (chip,) = pack([text, core_swap(text_emb)], ((0, 64), (1, 64)))
     next_1, next_4 = z_shift(chip, -1), z_shift(text_emb, 4)
-    near = [plane_shift(image, k, True) for k in (1, 2, 3)]
-    own, text_0, side = pack(
+    near = [plane_shift(image_emb, k, True) for k in (1, 2, 3)]
+    own, text_0 = pack(
         [image] + near + [chip, next_1, next_4],
         ((0, 64), (1, 64), (2, 64), (3, 64)),
         ((4, 128), (5, 128)),
-        ((5, 128), (6, 64)),
-    )
+    )
+    (side,) = pack([next_1, next_4], ((0, 128), (1, 64)))
     text_1 = z_shift(text_0, -2)
     near = [own] + [plane_shift(own, k, False) for k in PLANE_ORDER[1:]]
     logits, row_part, col_part, message, matched, images, texts = logits_call(

time: 116 us -> 114 us (0.983)
  waiting for transfers between devices: 47.9 us -> 45.1 us
  Pallas kernels: 18.3 us -> 19.5 us
    ppermute x8, waiting for transfers between devices: 5.82 us -> 3.94 us  [core_swap(): return lax.ppermute(v, 'core', [(0, 1), (1, 0)])]
  transfers between devices with their start and end apart: 26 -> 26, of which waited for: 11 -> 10; matrix products, arithmetic and copies ran while one was open for 0% -> 0% of each run, Pallas kernels for 6% -> 7%
where the time goes in v16:
time: 114 us; the launch traced here: 112 us
  waiting for transfers between devices  45.1 us (40%)
  starting transfers between devices  30.8 us (27%)
  Pallas kernels  19.5 us (17%)
  blocking collectives  14.3 us (13%)
  between operations  1.49 us (1%)
    ppermute x6, waiting for transfers between devices, z_shift(): return lax.ppermute(v, ('zl', 'core', 'zh'), pairs)  41.2 us
    ppermute x12, starting transfers between devices, plane_shift(): return lax.ppermute(v, ('core', 'zh', 'y', 'x'), pairs)  16.8 us
    all_to_all x1, blocking collectives, exchange(): return lax.all_to_all(v, AXES, 0, 0, axis_index_groups=groups)  14.3 us
    ppermute x6, starting transfers between devices, z_shift(): return lax.ppermute(v, ('zl', 'core', 'zh'), pairs)  12 us
    pallas_call x1, Pallas kernels, logits_call(): pl.pallas_call(logits_body, out_shape=(jax.ShapeDtypeStruct((BLOCK, BLOCK...  5.79 us
    ppermute x8, waiting for transfers between devices, core_swap(): return lax.ppermute(v, 'core', [(0, 1), (1, 0)])  3.94 us
    pallas_call x1, Pallas kernels, high_call(): pl.pallas_call(high_body, out_shape=(HALF_WEIGHTS, PART, jax.ShapeDtypeSt...  2.89 us
  transfers between devices with their start and end apart: 26, of which 10 were waited for; matrix products, arithmetic and copies ran while one was open for 0% of the time, Pallas kernels for 7%

profile of v16, /device:TPU:32, one launch (start us, length us, event | category | flops | bytes accessed | tf_op | source)
XLA Modules:
  0.0 112.3 jit_solution(14241934928854904138)
XLA Ops:
  0.6 0.1 collective-permute-start.3
  0.7 0.9 shard_map.59.refs_0_
  1.7 0.7 collective-permute-done.3.refs_1_
  2.3 1.9 %collective-permute-start.4 = (bf16[128,1280]{1,0:T(8,128)(2,1)S(1)}, bf16[128,1280]{1,0:T(8,128)(2,1)S(1)}, u32[]{:S(2)}, u32[]{:S(2)}) collective-permute-start(bf16[128,1280]{1,0:T(8,128)(2,1)S(1)} %shard_map.60.refs_4_), channel_id=1, source_target_pairs={{0,208},{64,0},{128,64},{192,128},{16,192},{80,16},{144,80},{208,1... | collective-permute-start | bytes 983048 | tf_op jit(solution)/shard_map/ppermute | solution.py:44
  4.3 5.5 %collective-permute-start.5 = (bf16[64,1280]{1,0:T(8,128)(2,1)}, bf16[64,1280]{1,0:T(8,128)(2,1)S(1)}, u32[]{:S(2)}, u32[]{:S(2)}) collective-permute-start(bf16[64,1280]{1,0:T(8,128)(2,1)} %refs_0_.3), channel_id=1, source_target_pairs={{0,16},{64,80},{128,144},{192,208},{16,0},{80,64},{144,128},{208,1... | collective-permute-start | bytes 491528 | tf_op jit(solution)/shard_map/ppermute | solution.py:44
  9.7 1.5 %collective-permute-start = (bf16[64,1280]{1,0:T(8,128)(2,1)}, bf16[64,1280]{1,0:T(8,128)(2,1)S(1)}, u32[]{:S(2)}, u32[]{:S(2)}) collective-permute-start(bf16[64,1280]{1,0:T(8,128)(2,1)} %refs_0_.2), channel_id=1, source_target_pairs={{0,1},{1,2},{2,3},{3,0},{4,5},{5,6},{6,7},{7,4},{8,9},{9,10},{10,1... | collective-permute-start | bytes 491528 | tf_op jit(solution)/shard_map/ppermute | solution.py:35
  11.2 1.7 %collective-permute-start.2 = (bf16[64,1280]{1,0:T(8,128)(2,1)}, bf16[64,1280]{1,0:T(8,128)(2,1)S(1)}, u32[]{:S(2)}, u32[]{:S(2)}) collective-permute-start(bf16[64,1280]{1,0:T(8,128)(2,1)} %refs_0_.2), channel_id=1, source_target_pairs={{0,3},{1,0},{2,1},{3,2},{4,7},{5,4},{6,5},{7,6},{8,11},{9,8},{10,9... | collective-permute-start | bytes 491528 | tf_op jit(solution)/shard_map/ppermute | solution.py:35
  13.0 1.8 %collective-permute-start.1 = (bf16[64,1280]{1,0:T(8,128)(2,1)}, bf16[64,1280]{1,0:T(8,128)(2,1)S(1)}, u32[]{:S(2)}, u32[]{:S(2)}) collective-permute-start(bf16[64,1280]{1,0:T(8,128)(2,1)} %refs_0_.2), channel_id=1, source_target_pairs={{0,2},{1,3},{2,0},{3,1},{4,6},{5,7},{6,4},{7,5},{8,10},{9,11},{10,... | collective-permute-start | bytes 491528 | tf_op jit(solution)/shard_map/ppermute | solution.py:35
  14.8 0.9 copy-done
  15.7 5.7 %collective-permute-done.5.refs_6_.refs_1_.refs_8_ = bf16[64,1280]{1,0:T(8,128)(2,1)S(1)} collective-permute-done((bf16[64,1280]{1,0:T(8,128)(2,1)}, bf16[64,1280]{1,0:T(8,128)(2,1)S(1)}, u32[]{:S(2)}, u32[]{:S(2)}) %collective-permute-start.5) | collective-permute-done | bytes 163872 | tf_op jit(solution)/shard_map/ppermute | solution.py:44
  21.5 0.0 collective-permute-done.refs_1_
  21.5 0.0 collective-permute-done.2.refs_3_
  21.5 0.0 collective-permute-done.1.refs_2_
  21.5 0.0 collective-permute-done.4.refs_5_.refs_0_
  21.5 0.1 shard_map.61
  21.6 1.7 %collective-permute-start.9 = (bf16[256,1280]{1,0:T(8,128)(2,1)S(1)}, bf16[256,1280]{1,0:T(8,128)(2,1)S(1)}, u32[]{:S(2)}, u32[]{:S(2)}) collective-permute-start(bf16[256,1280]{1,0:T(8,128)(2,1)S(1)} %get-tuple-element.39.refs_4_), channel_id=1, source_target_pairs={{0,144},{64,208},{128,0},{192,64},{16,128},{80,192},{144,16},{208,... | collective-permute-start | bytes 1966088 | tf_op jit(solution)/shard_map/ppermute | solution.py:44
  23.3 3.2 %collective-permute-start.8 = (bf16[256,1280]{1,0:T(8,128)(2,1)S(1)}, bf16[256,1280]{1,0:T(8,128)(2,1)S(1)}, u32[]{:S(2)}, u32[]{:S(2)}) collective-permute-start(bf16[256,1280]{1,0:T(8,128)(2,1)S(1)} %get-tuple-element.38.refs_0_), channel_id=1, source_target_pairs={{0,8},{1,9},{2,10},{3,11},{4,12},{5,13},{6,14},{7,15},{8,0},{9,1},... | collective-permute-start | bytes 1966088 | tf_op jit(solution)/shard_map/ppermute | solution.py:35
  26.5 1.1 collective-permute-start.7
  27.5 1.0 collective-permute-start.6
  28.5 11.6 %collective-permute-done.9.refs_5_ = bf16[256,1280]{1,0:T(8,128)(2,1)S(1)} collective-permute-done((bf16[256,1280]{1,0:T(8,128)(2,1)S(1)}, bf16[256,1280]{1,0:T(8,128)(2,1)S(1)}, u32[]{:S(2)}, u32[]{:S(2)}) %collective-permute-start.9) | collective-permute-done | bytes 655392 | tf_op jit(solution)/shard_map/ppermute | solution.py:44
  40.2 0.0 collective-permute-start.10
  40.2 0.8 shard_map.62
  41.0 0.5 collective-permute-start.11
  42.2 0.1 stack.23.place
  42.2 1.1 collective-permute-done.11.refs_7_
  43.3 0.0 collective-permute-done.8.refs_3_
  43.3 0.0 collective-permute-done.6.refs_1_
  43.3 0.0 collective-permute-done.10.refs_6_
  43.4 5.8 %shard_map.63 = (f32[1024,1024]{1,0:T(8,128)S(1)}, f32[16,128]{1,0:T(8,128)S(1)}, f32[16,128]{1,0:T(8,128)S(1)}, f32[24,128]{1,0:T(8,128)S(1)}, f32[8,128]{1,0:T...) custom-call(s32[5]{0:T(128)S(1)} %stack.23.place, f32[1]{0:T(128)S(6)} %copy.6.scale, ...), custom_call_target="tpu_custom_call" | custom-call | tf_op jit(solution)/shard_map/pallas_call | solution.py:204
  49.1 0.6 collective-permute-start.12
  49.8 0.8 collective-permute-done.12.got
  50.6 0.6 shard_map.64
  51.2 14.3 %all_to_all.5.got = f32[16,24,128]{2,1,0:T(8,128)S(1)} all-to-all(f32[16,24,128]{2,1,0:T(8,128)S(1)} %shard_map.64), channel_id=1, replica_groups={{0,1,2,3,4,5,6,7,8,9,10,11,12,13,14,15},{64,65,66,67,68,69,70,71,72,73,..., dimensions={0} | all-to-all | bytes 393216 | tf_op jit(solution)/shard_map/all_to_all | solution.py:63
  65.5 0.7 shard_map.65
  66.3 0.1 collective-permute-start.13
  66.4 1.2 %collective-permute-done.13.other = f32[24,128]{1,0:T(8,128)S(1)} collective-permute-done((f32[24,128]{1,0:T(8,128)S(1)}, f32[24,128]{1,0:T(8,128)S(1)}, u32[]{:S(2)}, u32[]{:S(2)}) %collective-permute-start.13) | collective-permute-done | bytes 12320 | tf_op jit(solution)/shard_map/ppermute | solution.py:48
  67.5 2.9 %shard_map.66 = (bf16[1024,512]{1,0:T(8,128)(2,1)S(1)}, bf16[256,1280]{1,0:T(8,128)(2,1)S(1)}, bf16[192,1280]{1,0:T(8,128)(2,1)S(1)}, bf16[64,1280]{1,0:T(8,128)...) custom-call(s32[5]{0:T(128)S(1)} %stack.23.place, f32[1]{0:T(128)S(6)} %copy.6.scale, ...), custom_call_target="tpu_custom_call" | custom-call | tf_op jit(solution)/shard_map/pallas_call | solution.py:348
  70.4 0.3 collective-permute-start.14
  70.7 0.3 collective-permute-start.15
  71.0 2.1 %shard_map.67 = (bf16[1024,512]{1,0:T(8,128)(2,1)S(1)}, bf16[256,1280]{1,0:T(8,128)(2,1)S(1)}) custom-call(s32[5]{0:T(128)S(1)} %stack.23.place, f32[1]{0:T(128)S(6)} %copy.6.scale, f32[1024,1024]{1,0:T(8,128)S(1)} %get-tuple-element.40.logits, f32[1024,128]{1,0:T(8,128)S(1)} %get-tuple-element.48.row_wide, f32[8,128]{1,0:T(8,128)S(1)} %get-tuple-element.49.col_lines, ...), custom_call_target="tpu_custom_call" | custom-call | tf_op jit(solution)/shard_map/pallas_call | solution.py:372
  73.1 0.2 collective-permute-done.15.refs_3_.refs_1_
  73.3 0.0 collective-permute-done.14.refs_1_
  73.3 0.2 shard_map.69.after
  73.5 1.5 %collective-permute-start.22 = (bf16[336,1280]{1,0:T(8,128)(2,1)S(1)}, bf16[336,1280]{1,0:T(8,128)(2,1)S(1)}, u32[]{:S(2)}, u32[]{:S(2)}) collective-permute-start(bf16[336,1280]{1,0:T(8,128)(2,1)S(1)} %shard_map.69.after), channel_id=1, source_target_pairs={{0,128},{64,192},{128,16},{192,80},{16,144},{80,208},{144,0},{208,... | collective-permute-start | bytes 2580488 | tf_op jit(solution)/shard_map/ppermute | solution.py:44
  75.0 2.2 %shard_map.70 = (bf16[272,1280]{1,0:T(8,128)(2,1)S(1)}, bf16[272,1280]{1,0:T(8,128)(2,1)S(1)}, bf16[272,1280]{1,0:T(8,128)(2,1)S(1)}) custom-call(f32[1]{0:T(128)S(6)} %copy.6.scale, bf16[336,1280]{1,0:T(8,128)(2,1)S(1)} %shard_map.69.after, bf16[32,1280]{1,0:T(8,128)(2,1)S(1)} %get-tuple-element.58.refs_4_.digits.refs_3_.refs_6_, ...), custom_call_target="tpu_custom_call" | custom-call | tf_op jit(solution)/shard_map/pallas_call | solution.py:417
  77.2 1.1 collective-permute-start.16
  78.3 1.7 %collective-permute-start.17 = (bf16[272,1280]{1,0:T(8,128)(2,1)S(1)}, bf16[272,1280]{1,0:T(8,128)(2,1)S(1)}, u32[]{:S(2)}, u32[]{:S(2)}) collective-permute-start(bf16[272,1280]{1,0:T(8,128)(2,1)S(1)} %get-tuple-element.60), channel_id=1, source_target_pairs={{0,12},{1,13},{2,14},{3,15},{4,0},{5,1},{6,2},{7,3},{8,4},{9,5},{1... | collective-permute-start | bytes 2088968 | tf_op jit(solution)/shard_map/ppermute | solution.py:35
  80.0 0.3 collective-permute-start.18
  80.3 1.6 %shard_map.68 = (bf16[256,1280]{1,0:T(8,128)(2,1)S(1)}, bf16[256,1280]{1,0:T(8,128)(2,1)S(1)}) custom-call(f32[1]{0:T(128)S(6)} %copy.6.scale, bf16[1024,512]{1,0:T(8,128)(2,1)S(1)} %get-tuple-element.50.low, bf16[1024,512]{1,0:T(8,128)(2,1)S(1)} %get-tuple-element.51.high, bf16[1024,1280]{1,0:T(8,128)(2,1)S(1)} %get-tuple-element.47.images, ...), custom_call_target="tpu_custom_call" | custom-call | tf_op jit(solution)/shard_map/pallas_call | solution.py:432
  81.9 15.7 %collective-permute-done.22.refs_2_ = bf16[336,1280]{1,0:T(8,128)(2,1)S(1)} collective-permute-done((bf16[336,1280]{1,0:T(8,128)(2,1)S(1)}, bf16[336,1280]{1,0:T(8,128)(2,1)S(1)}, u32[]{:S(2)}, u32[]{:S(2)}) %collective-permute-start.22) | collective-permute-done | bytes 860192 | tf_op jit(solution)/shard_map/ppermute | solution.py:44
  97.6 0.2 shard_map.72
  97.8 0.3 collective-permute-start.23
  98.1 0.0 collective-permute-done.17.refs_2_
  98.2 0.4 shard_map.71
  98.6 1.6 %collective-permute-start.19 = (bf16[80,1280]{1,0:T(8,128)(2,1)S(1)}, bf16[80,1280]{1,0:T(8,128)(2,1)S(1)}, u32[]{:S(2)}, u32[]{:S(2)}) collective-permute-start(bf16[80,1280]{1,0:T(8,128)(2,1)S(1)} %get-tuple-element.63), channel_id=1, source_target_pairs={{0,2},{1,3},{2,0},{3,1},{4,6},{5,7},{6,4},{7,5},{8,10},{9,11},{10,... | collective-permute-start | bytes 614408 | tf_op jit(solution)/shard_map/ppermute | solution.py:35
  100.2 1.8 %collective-permute-start.20 = (bf16[80,1280]{1,0:T(8,128)(2,1)S(1)}, bf16[80,1280]{1,0:T(8,128)(2,1)S(1)}, u32[]{:S(2)}, u32[]{:S(2)}) collective-permute-start(bf16[80,1280]{1,0:T(8,128)(2,1)S(1)} %get-tuple-element.64), channel_id=1, source_target_pairs={{0,3},{1,0},{2,1},{3,2},{4,7},{5,4},{6,5},{7,6},{8,11},{9,8},{10,9... | collective-permute-start | bytes 614408 | tf_op jit(solution)/shard_map/ppermute | solution.py:35
  102.0 1.1 collective-permute-start.24
  103.1 2.5 %collective-permute-done.23.refs_1_ = bf16[144,1280]{1,0:T(8,128)(2,1)S(1)} collective-permute-done((bf16[144,1280]{1,0:T(8,128)(2,1)S(1)}, bf16[144,1280]{1,0:T(8,128)(2,1)S(1)}, u32[]{:S(2)}, u32[]{:S(2)}) %collective-permute-start.23) | collective-permute-done | bytes 368672 | tf_op jit(solution)/shard_map/ppermute | solution.py:44
  105.7 0.1 collective-permute-start.25
  105.8 5.6 %collective-permute-done.24.refs_2_ = bf16[80,1280]{1,0:T(8,128)(2,1)S(1)} collective-permute-done((bf16[80,1280]{1,0:T(8,128)(2,1)S(1)}, bf16[80,1280]{1,0:T(8,128)(2,1)S(1)}, u32[]{:S(2)}, u32[]{:S(2)}) %collective-permute-start.24) | collective-permute-done | bytes 204832 | tf_op jit(solution)/shard_map/ppermute | solution.py:44
  111.4 0.1 shard_map.73.refs_4_
  111.5 0.0 collective-permute-done.20.refs_2_
  111.5 0.0 collective-permute-done.21.refs_3_
  111.5 0.8 shard_map.75
  (10 shorter events, 0.1 us)
Async XLA Ops:
  0.6 1.7 %collective-permute-start.3 = (bf16[64,1280]{1,0:T(8,128)(2,1)}, bf16[64,1280]{1,0:T(8,128)(2,1)S(1)}, u32[]{:S(2)}, u32[]{:S(2)}) collective-permute-start(bf16[64,1280]{1,0:T(8,128)(2,1)} %refs_0_.3), channel_id=1, source_target_pairs={{0,32},{32,0},{1,33},{33,1},{2,34},{34,2},{3,35},{35,3},{4,36},{36... | collective-permute-start | bytes 491528 | tf_op jit(solution)/shard_map/ppermute | solution.py:48
  2.3 19.1 %collective-permute-start.4 = (bf16[128,1280]{1,0:T(8,128)(2,1)S(1)}, bf16[128,1280]{1,0:T(8,128)(2,1)S(1)}, u32[]{:S(2)}, u32[]{:S(2)}) collective-permute-start(bf16[128,1280]{1,0:T(8,128)(2,1)S(1)} %shard_map.60.refs_4_), channel_id=1, source_target_pairs={{0,208},{64,0},{128,64},{192,128},{16,192},{80,16},{144,80},{208,1... | collective-permute-start | bytes 983048 | tf_op jit(solution)/shard_map/ppermute | solution.py:44
  4.3 17.2 %collective-permute-start.5 = (bf16[64,1280]{1,0:T(8,128)(2,1)}, bf16[64,1280]{1,0:T(8,128)(2,1)S(1)}, u32[]{:S(2)}, u32[]{:S(2)}) collective-permute-start(bf16[64,1280]{1,0:T(8,128)(2,1)} %refs_0_.3), channel_id=1, source_target_pairs={{0,16},{64,80},{128,144},{192,208},{16,0},{80,64},{144,128},{208,1... | collective-permute-start | bytes 491528 | tf_op jit(solution)/shard_map/ppermute | solution.py:44
  9.7 11.7 %collective-permute-start = (bf16[64,1280]{1,0:T(8,128)(2,1)}, bf16[64,1280]{1,0:T(8,128)(2,1)S(1)}, u32[]{:S(2)}, u32[]{:S(2)}) collective-permute-start(bf16[64,1280]{1,0:T(8,128)(2,1)} %refs_0_.2), channel_id=1, source_target_pairs={{0,1},{1,2},{2,3},{3,0},{4,5},{5,6},{6,7},{7,4},{8,9},{9,10},{10,1... | collective-permute-start | bytes 491528 | tf_op jit(solution)/shard_map/ppermute | solution.py:35
  11.2 10.2 %collective-permute-start.2 = (bf16[64,1280]{1,0:T(8,128)(2,1)}, bf16[64,1280]{1,0:T(8,128)(2,1)S(1)}, u32[]{:S(2)}, u32[]{:S(2)}) collective-permute-start(bf16[64,1280]{1,0:T(8,128)(2,1)} %refs_0_.2), channel_id=1, source_target_pairs={{0,3},{1,0},{2,1},{3,2},{4,7},{5,4},{6,5},{7,6},{8,11},{9,8},{10,9... | collective-permute-start | bytes 491528 | tf_op jit(solution)/shard_map/ppermute | solution.py:35
  13.0 8.5 %collective-permute-start.1 = (bf16[64,1280]{1,0:T(8,128)(2,1)}, bf16[64,1280]{1,0:T(8,128)(2,1)S(1)}, u32[]{:S(2)}, u32[]{:S(2)}) collective-permute-start(bf16[64,1280]{1,0:T(8,128)(2,1)} %refs_0_.2), channel_id=1, source_target_pairs={{0,2},{1,3},{2,0},{3,1},{4,6},{5,7},{6,4},{7,5},{8,10},{9,11},{10,... | collective-permute-start | bytes 491528 | tf_op jit(solution)/shard_map/ppermute | solution.py:35
  14.8 0.9 copy-start
  21.6 18.6 %collective-permute-start.9 = (bf16[256,1280]{1,0:T(8,128)(2,1)S(1)}, bf16[256,1280]{1,0:T(8,128)(2,1)S(1)}, u32[]{:S(2)}, u32[]{:S(2)}) collective-permute-start(bf16[256,1280]{1,0:T(8,128)(2,1)S(1)} %get-tuple-element.39.refs_4_), channel_id=1, source_target_pairs={{0,144},{64,208},{128,0},{192,64},{16,128},{80,192},{144,16},{208,... | collective-permute-start | bytes 1966088 | tf_op jit(solution)/shard_map/ppermute | solution.py:44
  23.3 20.0 %collective-permute-start.8 = (bf16[256,1280]{1,0:T(8,128)(2,1)S(1)}, bf16[256,1280]{1,0:T(8,128)(2,1)S(1)}, u32[]{:S(2)}, u32[]{:S(2)}) collective-permute-start(bf16[256,1280]{1,0:T(8,128)(2,1)S(1)} %get-tuple-element.38.refs_0_), channel_id=1, source_target_pairs={{0,8},{1,9},{2,10},{3,11},{4,12},{5,13},{6,14},{7,15},{8,0},{9,1},... | collective-permute-start | bytes 1966088 | tf_op jit(solution)/shard_map/ppermute | solution.py:35
  26.5 16.8 %collective-permute-start.7 = (bf16[256,1280]{1,0:T(8,128)(2,1)S(1)}, bf16[256,1280]{1,0:T(8,128)(2,1)S(1)}, u32[]{:S(2)}, u32[]{:S(2)}) collective-permute-start(bf16[256,1280]{1,0:T(8,128)(2,1)S(1)} %get-tuple-element.38.refs_0_), channel_id=1, source_target_pairs={{0,12},{1,13},{2,14},{3,15},{4,0},{5,1},{6,2},{7,3},{8,4},{9,5},{1... | collective-permute-start | bytes 1966088 | tf_op jit(solution)/shard_map/ppermute | solution.py:35
  27.5 15.8 %collective-permute-start.6 = (bf16[256,1280]{1,0:T(8,128)(2,1)S(1)}, bf16[256,1280]{1,0:T(8,128)(2,1)}, u32[]{:S(2)}, u32[]{:S(2)}) collective-permute-start(bf16[256,1280]{1,0:T(8,128)(2,1)S(1)} %get-tuple-element.38.refs_0_), channel_id=1, source_target_pairs={{0,4},{1,5},{2,6},{3,7},{4,8},{5,9},{6,10},{7,11},{8,12},{9,13},{1... | collective-permute-start | bytes 1966088 | tf_op jit(solution)/shard_map/ppermute | solution.py:35
  40.2 3.2 %collective-permute-start.10 = (bf16[256,1280]{1,0:T(8,128)(2,1)S(1)}, bf16[256,1280]{1,0:T(8,128)(2,1)}, u32[]{:S(2)}, u32[]{:S(2)}) collective-permute-start(bf16[256,1280]{1,0:T(8,128)(2,1)S(1)} %collective-permute-done.9.refs_5_), channel_id=1, source_target_pairs={{0,32},{32,0},{1,33},{33,1},{2,34},{34,2},{3,35},{35,3},{4,36},{36... | collective-permute-start | bytes 1966088 | tf_op jit(solution)/shard_map/ppermute | solution.py:48
  41.0 2.3 %collective-permute-start.11 = (bf16[192,1280]{1,0:T(8,128)(2,1)}, bf16[192,1280]{1,0:T(8,128)(2,1)}, u32[]{:S(2)}, u32[]{:S(2)}) collective-permute-start(bf16[192,1280]{1,0:T(8,128)(2,1)} %shard_map.62), channel_id=1, source_target_pairs={{0,32},{32,0},{1,33},{33,1},{2,34},{34,2},{3,35},{35,3},{4,36},{36... | collective-permute-start | bytes 1474568 | tf_op jit(solution)/shard_map/ppermute | solution.py:48
  49.1 1.4 %collective-permute-start.12 = (f32[24,128]{1,0:T(8,128)S(1)}, f32[24,128]{1,0:T(8,128)S(1)}, u32[]{:S(2)}, u32[]{:S(2)}) collective-permute-start(f32[24,128]{1,0:T(8,128)S(1)} %get-tuple-element.44), channel_id=1, source_target_pairs={{0,32},{32,0},{1,33},{33,1},{2,34},{34,2},{3,35},{35,3},{4,36},{36... | collective-permute-start | bytes 36872 | tf_op jit(solution)/shard_map/ppermute | solution.py:48
  66.3 1.3 %collective-permute-start.13 = (f32[24,128]{1,0:T(8,128)S(1)}, f32[24,128]{1,0:T(8,128)S(1)}, u32[]{:S(2)}, u32[]{:S(2)}) collective-permute-start(f32[24,128]{1,0:T(8,128)S(1)} %get-tuple-element.46), channel_id=1, source_target_pairs={{0,32},{32,0},{1,33},{33,1},{2,34},{34,2},{3,35},{35,3},{4,36},{36... | collective-permute-start | bytes 36872 | tf_op jit(solution)/shard_map/ppermute | solution.py:48
  70.4 2.9 %collective-permute-start.14 = (bf16[256,1280]{1,0:T(8,128)(2,1)S(1)}, bf16[256,1280]{1,0:T(8,128)(2,1)S(1)}, u32[]{:S(2)}, u32[]{:S(2)}) collective-permute-start(bf16[256,1280]{1,0:T(8,128)(2,1)S(1)} %get-tuple-element.55), channel_id=1, source_target_pairs={{0,32},{32,0},{1,33},{33,1},{2,34},{34,2},{3,35},{35,3},{4,36},{36... | collective-permute-start | bytes 1966088 | tf_op jit(solution)/shard_map/ppermute | solution.py:48
  70.7 2.6 %collective-permute-start.15 = (bf16[192,1280]{1,0:T(8,128)(2,1)S(1)}, bf16[192,1280]{1,0:T(8,128)(2,1)S(1)}, u32[]{:S(2)}, u32[]{:S(2)}) collective-permute-start(bf16[192,1280]{1,0:T(8,128)(2,1)S(1)} %get-tuple-element.57), channel_id=1, source_target_pairs={{0,32},{32,0},{1,33},{33,1},{2,34},{34,2},{3,35},{35,3},{4,36},{36... | collective-permute-start | bytes 1474568 | tf_op jit(solution)/shard_map/ppermute | solution.py:48
  73.5 24.1 %collective-permute-start.22 = (bf16[336,1280]{1,0:T(8,128)(2,1)S(1)}, bf16[336,1280]{1,0:T(8,128)(2,1)S(1)}, u32[]{:S(2)}, u32[]{:S(2)}) collective-permute-start(bf16[336,1280]{1,0:T(8,128)(2,1)S(1)} %shard_map.69.after), channel_id=1, source_target_pairs={{0,128},{64,192},{128,16},{192,80},{16,144},{80,208},{144,0},{208,... | collective-permute-start | bytes 2580488 | tf_op jit(solution)/shard_map/ppermute | solution.py:44
  77.2 20.9 %collective-permute-start.16 = (bf16[272,1280]{1,0:T(8,128)(2,1)S(1)}, bf16[272,1280]{1,0:T(8,128)(2,1)S(1)}, u32[]{:S(2)}, u32[]{:S(2)}) collective-permute-start(bf16[272,1280]{1,0:T(8,128)(2,1)S(1)} %get-tuple-element.59), channel_id=1, source_target_pairs={{0,8},{1,9},{2,10},{3,11},{4,12},{5,13},{6,14},{7,15},{8,0},{9,1},... | collective-permute-start | bytes 2088968 | tf_op jit(solution)/shard_map/ppermute | solution.py:35
  78.3 19.8 %collective-permute-start.17 = (bf16[272,1280]{1,0:T(8,128)(2,1)S(1)}, bf16[272,1280]{1,0:T(8,128)(2,1)S(1)}, u32[]{:S(2)}, u32[]{:S(2)}) collective-permute-start(bf16[272,1280]{1,0:T(8,128)(2,1)S(1)} %get-tuple-element.60), channel_id=1, source_target_pairs={{0,12},{1,13},{2,14},{3,15},{4,0},{5,1},{6,2},{7,3},{8,4},{9,5},{1... | collective-permute-start | bytes 2088968 | tf_op jit(solution)/shard_map/ppermute | solution.py:35
  80.0 18.1 %collective-permute-start.18 = (bf16[272,1280]{1,0:T(8,128)(2,1)S(1)}, bf16[272,1280]{1,0:T(8,128)(2,1)S(1)}, u32[]{:S(2)}, u32[]{:S(2)}) collective-permute-start(bf16[272,1280]{1,0:T(8,128)(2,1)S(1)} %get-tuple-element.61), channel_id=1, source_target_pairs={{0,4},{1,5},{2,6},{3,7},{4,8},{5,9},{6,10},{7,11},{8,12},{9,13},{1... | collective-permute-start | bytes 2088968 | tf_op jit(solution)/shard_map/ppermute | solution.py:35
  97.8 7.8 %collective-permute-start.23 = (bf16[144,1280]{1,0:T(8,128)(2,1)S(1)}, bf16[144,1280]{1,0:T(8,128)(2,1)S(1)}, u32[]{:S(2)}, u32[]{:S(2)}) collective-permute-start(bf16[144,1280]{1,0:T(8,128)(2,1)S(1)} %get-tuple-element.68), channel_id=1, source_target_pairs={{0,64},{64,128},{128,192},{192,16},{16,80},{80,144},{144,208},{208... | collective-permute-start | bytes 1105928 | tf_op jit(solution)/shard_map/ppermute | solution.py:44
  98.6 12.9 %collective-permute-start.19 = (bf16[80,1280]{1,0:T(8,128)(2,1)S(1)}, bf16[80,1280]{1,0:T(8,128)(2,1)S(1)}, u32[]{:S(2)}, u32[]{:S(2)}) collective-permute-start(bf16[80,1280]{1,0:T(8,128)(2,1)S(1)} %get-tuple-element.63), channel_id=1, source_target_pairs={{0,2},{1,3},{2,0},{3,1},{4,6},{5,7},{6,4},{7,5},{8,10},{9,11},{10,... | collective-permute-start | bytes 614408 | tf_op jit(solution)/shard_map/ppermute | solution.py:35
  100.2 11.3 %collective-permute-start.20 = (bf16[80,1280]{1,0:T(8,128)(2,1)S(1)}, bf16[80,1280]{1,0:T(8,128)(2,1)S(1)}, u32[]{:S(2)}, u32[]{:S(2)}) collective-permute-start(bf16[80,1280]{1,0:T(8,128)(2,1)S(1)} %get-tuple-element.64), channel_id=1, source_target_pairs={{0,3},{1,0},{2,1},{3,2},{4,7},{5,4},{6,5},{7,6},{8,11},{9,8},{10,9... | collective-permute-start | bytes 614408 | tf_op jit(solution)/shard_map/ppermute | solution.py:35
  102.0 9.4 %collective-permute-start.24 = (bf16[80,1280]{1,0:T(8,128)(2,1)S(1)}, bf16[80,1280]{1,0:T(8,128)(2,1)S(1)}, u32[]{:S(2)}, u32[]{:S(2)}) collective-permute-start(bf16[80,1280]{1,0:T(8,128)(2,1)S(1)} %get-tuple-element.69), channel_id=1, source_target_pairs={{0,128},{64,192},{128,16},{192,80},{16,144},{80,208},{144,0},{208,... | collective-permute-start | bytes 614408 | tf_op jit(solution)/shard_map/ppermute | solution.py:44
  103.1 8.4 %collective-permute-start.21 = (bf16[80,1280]{1,0:T(8,128)(2,1)S(1)}, bf16[80,1280]{1,0:T(8,128)(2,1)S(1)}, u32[]{:S(2)}, u32[]{:S(2)}) collective-permute-start(bf16[80,1280]{1,0:T(8,128)(2,1)S(1)} %get-tuple-element.65), channel_id=1, source_target_pairs={{0,1},{1,2},{2,3},{3,0},{4,5},{5,6},{6,7},{7,4},{8,9},{9,10},{10,1... | collective-permute-start | bytes 614408 | tf_op jit(solution)/shard_map/ppermute | solution.py:35
  105.7 5.8 %collective-permute-start.25 = (bf16[80,1280]{1,0:T(8,128)(2,1)S(1)}, bf16[80,1280]{1,0:T(8,128)(2,1)S(1)}, u32[]{:S(2)}, u32[]{:S(2)}) collective-permute-start(bf16[80,1280]{1,0:T(8,128)(2,1)S(1)} %shard_map.74), channel_id=1, source_target_pairs={{0,32},{32,0},{1,33},{33,1},{2,34},{34,2},{3,35},{35,3},{4,36},{36... | collective-permute-start | bytes 614408 | tf_op jit(solution)/shard_map/ppermute | solution.py:48

commit v17 on v16

--- a/solution.py
+++ b/solution.py
@@ -146,7 +146,7 @@
     logits, row_out, col_out, message, match_out, all_images, all_texts = refs[9:16]
     row_wide = refs[16]
     all_texts[3 * CHUNK : BLOCK - ROWS, :] = refs[7][...]
-    all_texts[BLOCK - ROWS :, :] = refs[8][...]
+    all_texts[BLOCK - ROWS :, :] = refs[8][2 * ROWS :, :]
     where = [place[i] for i in range(5)]
     multiplier = scale[0] * LOG2E
     for j in range(3):
@@ -505,7 +505,7 @@
     text_1 = z_shift(text_0, -2)
     near = [own] + [plane_shift(own, k, False) for k in PLANE_ORDER[1:]]
     logits, row_part, col_part, message, matched, images, texts = logits_call(
-        place, logit_scale, near, [text_0, text_1, core_swap(text_1), core_swap(side), next_4]
+        place, logit_scale, near, [text_0, text_1, core_swap(text_1), core_swap(side), side]
     )
 
     spread = spread_call(place, row_part, col_part, matched, core_swap(message))

time: 114 us -> 114 us (level)
  no operation moved by 1% of the time
where the time goes in v17:
time: 114 us; the launch traced here: 112 us
  waiting for transfers between devices  45.9 us (40%)
  starting transfers between devices  30.3 us (27%)
  Pallas kernels  18.9 us (17%)
  blocking collectives  14.6 us (13%)
  between operations  1.5 us (1%)
    ppermute x6, waiting for transfers between devices, z_shift(): return lax.ppermute(v, ('zl', 'core', 'zh'), pairs)  41.2 us
    ppermute x12, starting transfers between devices, plane_shift(): return lax.ppermute(v, ('core', 'zh', 'y', 'x'), pairs)  16.8 us
    all_to_all x1, blocking collectives, exchange(): return lax.all_to_all(v, AXES, 0, 0, axis_index_groups=groups)  14.6 us
    ppermute x6, starting transfers between devices, z_shift(): return lax.ppermute(v, ('zl', 'core', 'zh'), pairs)  11.7 us
    pallas_call x1, Pallas kernels, logits_call(): pl.pallas_call(logits_body, out_shape=(jax.ShapeDtypeStruct((BLOCK, BLOCK...  5.99 us
    ppermute x8, waiting for transfers between devices, core_swap(): return lax.ppermute(v, 'core', [(0, 1), (1, 0)])  4.6 us
    pallas_call x1, Pallas kernels, high_call(): pl.pallas_call(high_body, out_shape=(HALF_WEIGHTS, PART, jax.ShapeDtypeSt...  2.89 us
  transfers between devices with their start and end apart: 26, of which 10 were waited for; matrix products, arithmetic and copies ran while one was open for 0% of the time, Pallas kernels for 7%

profile of v17, /device:TPU:32, one launch (start us, length us, event | category | flops | bytes accessed | tf_op | source)
XLA Modules:
  0.0 112.2 jit_solution(11557865174523982301)
XLA Ops:
  0.6 0.1 collective-permute-start.3
  0.7 0.9 shard_map.59.refs_0_
  1.7 0.7 collective-permute-done.3.refs_1_
  2.3 1.9 %collective-permute-start.4 = (bf16[128,1280]{1,0:T(8,128)(2,1)S(1)}, bf16[128,1280]{1,0:T(8,128)(2,1)S(1)}, u32[]{:S(2)}, u32[]{:S(2)}) collective-permute-start(bf16[128,1280]{1,0:T(8,128)(2,1)S(1)} %shard_map.60.refs_4_), channel_id=1, source_target_pairs={{0,208},{64,0},{128,64},{192,128},{16,192},{80,16},{144,80},{208,1... | collective-permute-start | bytes 983048 | tf_op jit(solution)/shard_map/ppermute | solution.py:44
  4.3 5.5 %collective-permute-start.5 = (bf16[64,1280]{1,0:T(8,128)(2,1)}, bf16[64,1280]{1,0:T(8,128)(2,1)S(1)}, u32[]{:S(2)}, u32[]{:S(2)}) collective-permute-start(bf16[64,1280]{1,0:T(8,128)(2,1)} %refs_0_.3), channel_id=1, source_target_pairs={{0,16},{64,80},{128,144},{192,208},{16,0},{80,64},{144,128},{208,1... | collective-permute-start | bytes 491528 | tf_op jit(solution)/shard_map/ppermute | solution.py:44
  9.7 1.5 %collective-permute-start = (bf16[64,1280]{1,0:T(8,128)(2,1)}, bf16[64,1280]{1,0:T(8,128)(2,1)S(1)}, u32[]{:S(2)}, u32[]{:S(2)}) collective-permute-start(bf16[64,1280]{1,0:T(8,128)(2,1)} %refs_0_.2), channel_id=1, source_target_pairs={{0,1},{1,2},{2,3},{3,0},{4,5},{5,6},{6,7},{7,4},{8,9},{9,10},{10,1... | collective-permute-start | bytes 491528 | tf_op jit(solution)/shard_map/ppermute | solution.py:35
  11.2 1.7 %collective-permute-start.2 = (bf16[64,1280]{1,0:T(8,128)(2,1)}, bf16[64,1280]{1,0:T(8,128)(2,1)S(1)}, u32[]{:S(2)}, u32[]{:S(2)}) collective-permute-start(bf16[64,1280]{1,0:T(8,128)(2,1)} %refs_0_.2), channel_id=1, source_target_pairs={{0,3},{1,0},{2,1},{3,2},{4,7},{5,4},{6,5},{7,6},{8,11},{9,8},{10,9... | collective-permute-start | bytes 491528 | tf_op jit(solution)/shard_map/ppermute | solution.py:35
  13.0 1.8 %collective-permute-start.1 = (bf16[64,1280]{1,0:T(8,128)(2,1)}, bf16[64,1280]{1,0:T(8,128)(2,1)S(1)}, u32[]{:S(2)}, u32[]{:S(2)}) collective-permute-start(bf16[64,1280]{1,0:T(8,128)(2,1)} %refs_0_.2), channel_id=1, source_target_pairs={{0,2},{1,3},{2,0},{3,1},{4,6},{5,7},{6,4},{7,5},{8,10},{9,11},{10,... | collective-permute-start | bytes 491528 | tf_op jit(solution)/shard_map/ppermute | solution.py:35
  14.8 0.9 copy-done
  15.7 5.7 %collective-permute-done.5.refs_6_.refs_1_ = bf16[64,1280]{1,0:T(8,128)(2,1)S(1)} collective-permute-done((bf16[64,1280]{1,0:T(8,128)(2,1)}, bf16[64,1280]{1,0:T(8,128)(2,1)S(1)}, u32[]{:S(2)}, u32[]{:S(2)}) %collective-permute-start.5) | collective-permute-done | bytes 163872 | tf_op jit(solution)/shard_map/ppermute | solution.py:44
  21.5 0.0 collective-permute-done.refs_1_
  21.5 0.0 collective-permute-done.2.refs_3_
  21.5 0.0 collective-permute-done.1.refs_2_
  21.5 0.0 collective-permute-done.4.refs_5_.refs_0_
  21.5 0.1 shard_map.61
  21.6 1.7 %collective-permute-start.9 = (bf16[256,1280]{1,0:T(8,128)(2,1)S(1)}, bf16[256,1280]{1,0:T(8,128)(2,1)S(1)}, u32[]{:S(2)}, u32[]{:S(2)}) collective-permute-start(bf16[256,1280]{1,0:T(8,128)(2,1)S(1)} %get-tuple-element.39.refs_4_), channel_id=1, source_target_pairs={{0,144},{64,208},{128,0},{192,64},{16,128},{80,192},{144,16},{208,... | collective-permute-start | bytes 1966088 | tf_op jit(solution)/shard_map/ppermute | solution.py:44
  23.3 3.2 %collective-permute-start.8 = (bf16[256,1280]{1,0:T(8,128)(2,1)S(1)}, bf16[256,1280]{1,0:T(8,128)(2,1)S(1)}, u32[]{:S(2)}, u32[]{:S(2)}) collective-permute-start(bf16[256,1280]{1,0:T(8,128)(2,1)S(1)} %get-tuple-element.38.refs_0_), channel_id=1, source_target_pairs={{0,8},{1,9},{2,10},{3,11},{4,12},{5,13},{6,14},{7,15},{8,0},{9,1},... | collective-permute-start | bytes 1966088 | tf_op jit(solution)/shard_map/ppermute | solution.py:35
  26.5 1.1 collective-permute-start.7
  27.5 1.0 collective-permute-start.6
  28.5 11.6 %collective-permute-done.9.refs_5_ = bf16[256,1280]{1,0:T(8,128)(2,1)S(1)} collective-permute-done((bf16[256,1280]{1,0:T(8,128)(2,1)S(1)}, bf16[256,1280]{1,0:T(8,128)(2,1)S(1)}, u32[]{:S(2)}, u32[]{:S(2)}) %collective-permute-start.9) | collective-permute-done | bytes 655392 | tf_op jit(solution)/shard_map/ppermute | solution.py:44
  40.2 0.0 collective-permute-start.10
  40.2 0.6 collective-permute-start.11
  41.4 0.1 stack.23.place
  41.5 1.6 %collective-permute-done.11.refs_7_ = bf16[192,1280]{1,0:T(8,128)(2,1)} collective-permute-done((bf16[192,1280]{1,0:T(8,128)(2,1)S(1)}, bf16[192,1280]{1,0:T(8,128)(2,1)}, u32[]{:S(2)}, u32[]{:S(2)}) %collective-permute-start.11) | collective-permute-done | bytes 491552 | tf_op jit(solution)/shard_map/ppermute | solution.py:48
  43.1 0.0 collective-permute-done.8.refs_3_
  43.1 0.0 collective-permute-done.7.refs_2_
  43.1 6.0 %shard_map.63 = (f32[1024,1024]{1,0:T(8,128)S(1)}, f32[16,128]{1,0:T(8,128)S(1)}, f32[16,128]{1,0:T(8,128)S(1)}, f32[24,128]{1,0:T(8,128)S(1)}, f32[8,128]{1,0:T...) custom-call(s32[5]{0:T(128)S(1)} %stack.23.place, f32[1]{0:T(128)S(6)} %copy.6.scale, ...), custom_call_target="tpu_custom_call" | custom-call | tf_op jit(solution)/shard_map/pallas_call | solution.py:204
  49.1 0.4 collective-permute-start.12
  49.5 1.0 collective-permute-done.12.got
  50.5 0.6 shard_map.64
  51.2 14.6 %all_to_all.5.got = f32[16,24,128]{2,1,0:T(8,128)S(1)} all-to-all(f32[16,24,128]{2,1,0:T(8,128)S(1)} %shard_map.64), channel_id=1, replica_groups={{0,1,2,3,4,5,6,7,8,9,10,11,12,13,14,15},{64,65,66,67,68,69,70,71,72,73,..., dimensions={0} | all-to-all | bytes 393216 | tf_op jit(solution)/shard_map/all_to_all | solution.py:63
  65.8 0.7 shard_map.65
  66.5 0.1 collective-permute-start.13
  66.6 1.2 %collective-permute-done.13.other = f32[24,128]{1,0:T(8,128)S(1)} collective-permute-done((f32[24,128]{1,0:T(8,128)S(1)}, f32[24,128]{1,0:T(8,128)S(1)}, u32[]{:S(2)}, u32[]{:S(2)}) %collective-permute-start.13) | collective-permute-done | bytes 12320 | tf_op jit(solution)/shard_map/ppermute | solution.py:48
  67.8 2.9 %shard_map.66 = (bf16[1024,512]{1,0:T(8,128)(2,1)S(1)}, bf16[256,1280]{1,0:T(8,128)(2,1)S(1)}, bf16[192,1280]{1,0:T(8,128)(2,1)S(1)}, bf16[64,1280]{1,0:T(8,128)...) custom-call(s32[5]{0:T(128)S(1)} %stack.23.place, f32[1]{0:T(128)S(6)} %copy.6.scale, ...), custom_call_target="tpu_custom_call" | custom-call | tf_op jit(solution)/shard_map/pallas_call | solution.py:348
  70.7 0.3 collective-permute-start.14
  70.9 0.3 collective-permute-start.15
  71.2 2.1 %shard_map.67 = (bf16[1024,512]{1,0:T(8,128)(2,1)S(1)}, bf16[256,1280]{1,0:T(8,128)(2,1)S(1)}) custom-call(s32[5]{0:T(128)S(1)} %stack.23.place, f32[1]{0:T(128)S(6)} %copy.6.scale, f32[1024,1024]{1,0:T(8,128)S(1)} %get-tuple-element.40.logits, f32[1024,128]{1,0:T(8,128)S(1)} %get-tuple-element.48.row_wide, f32[8,128]{1,0:T(8,128)S(1)} %get-tuple-element.49.col_lines, ...), custom_call_target="tpu_custom_call" | custom-call | tf_op jit(solution)/shard_map/pallas_call | solution.py:372
  73.4 0.2 collective-permute-done.15.refs_3_.refs_1_
  73.5 0.0 collective-permute-done.14.refs_1_
  73.5 0.2 shard_map.69.after
  73.7 1.3 %collective-permute-start.22 = (bf16[336,1280]{1,0:T(8,128)(2,1)S(1)}, bf16[336,1280]{1,0:T(8,128)(2,1)S(1)}, u32[]{:S(2)}, u32[]{:S(2)}) collective-permute-start(bf16[336,1280]{1,0:T(8,128)(2,1)S(1)} %shard_map.69.after), channel_id=1, source_target_pairs={{0,128},{64,192},{128,16},{192,80},{16,144},{80,208},{144,0},{208,... | collective-permute-start | bytes 2580488 | tf_op jit(solution)/shard_map/ppermute | solution.py:44
  75.1 2.2 %shard_map.70 = (bf16[272,1280]{1,0:T(8,128)(2,1)S(1)}, bf16[272,1280]{1,0:T(8,128)(2,1)S(1)}, bf16[272,1280]{1,0:T(8,128)(2,1)S(1)}) custom-call(f32[1]{0:T(128)S(6)} %copy.6.scale, bf16[336,1280]{1,0:T(8,128)(2,1)S(1)} %shard_map.69.after, bf16[32,1280]{1,0:T(8,128)(2,1)S(1)} %get-tuple-element.58.refs_4_.digits.refs_3_.refs_6_, ...), custom_call_target="tpu_custom_call" | custom-call | tf_op jit(solution)/shard_map/pallas_call | solution.py:417
  77.3 1.1 %collective-permute-start.16 = (bf16[272,1280]{1,0:T(8,128)(2,1)S(1)}, bf16[272,1280]{1,0:T(8,128)(2,1)S(1)}, u32[]{:S(2)}, u32[]{:S(2)}) collective-permute-start(bf16[272,1280]{1,0:T(8,128)(2,1)S(1)} %get-tuple-element.59), channel_id=1, source_target_pairs={{0,8},{1,9},{2,10},{3,11},{4,12},{5,13},{6,14},{7,15},{8,0},{9,1},... | collective-permute-start | bytes 2088968 | tf_op jit(solution)/shard_map/ppermute | solution.py:35
  78.4 1.9 %collective-permute-start.17 = (bf16[272,1280]{1,0:T(8,128)(2,1)S(1)}, bf16[272,1280]{1,0:T(8,128)(2,1)S(1)}, u32[]{:S(2)}, u32[]{:S(2)}) collective-permute-start(bf16[272,1280]{1,0:T(8,128)(2,1)S(1)} %get-tuple-element.60), channel_id=1, source_target_pairs={{0,12},{1,13},{2,14},{3,15},{4,0},{5,1},{6,2},{7,3},{8,4},{9,5},{1... | collective-permute-start | bytes 2088968 | tf_op jit(solution)/shard_map/ppermute | solution.py:35
  80.3 0.1 collective-permute-start.18
  80.4 1.6 %shard_map.68 = (bf16[256,1280]{1,0:T(8,128)(2,1)S(1)}, bf16[256,1280]{1,0:T(8,128)(2,1)S(1)}) custom-call(f32[1]{0:T(128)S(6)} %copy.6.scale, bf16[1024,512]{1,0:T(8,128)(2,1)S(1)} %get-tuple-element.50.low, bf16[1024,512]{1,0:T(8,128)(2,1)S(1)} %get-tuple-element.51.high, bf16[1024,1280]{1,0:T(8,128)(2,1)S(1)} %get-tuple-element.47.images, ...), custom_call_target="tpu_custom_call" | custom-call | tf_op jit(solution)/shard_map/pallas_call | solution.py:432
  82.0 15.7 %collective-permute-done.22.refs_2_ = bf16[336,1280]{1,0:T(8,128)(2,1)S(1)} collective-permute-done((bf16[336,1280]{1,0:T(8,128)(2,1)S(1)}, bf16[336,1280]{1,0:T(8,128)(2,1)S(1)}, u32[]{:S(2)}, u32[]{:S(2)}) %collective-permute-start.22) | collective-permute-done | bytes 860192 | tf_op jit(solution)/shard_map/ppermute | solution.py:44
  97.7 0.2 shard_map.72
  97.9 0.3 collective-permute-start.23
  98.2 0.0 collective-permute-done.16.refs_1_
  98.3 0.0 collective-permute-done.17.refs_2_
  98.3 0.4 shard_map.71
  98.7 1.3 %collective-permute-start.19 = (bf16[80,1280]{1,0:T(8,128)(2,1)S(1)}, bf16[80,1280]{1,0:T(8,128)(2,1)S(1)}, u32[]{:S(2)}, u32[]{:S(2)}) collective-permute-start(bf16[80,1280]{1,0:T(8,128)(2,1)S(1)} %get-tuple-element.63), channel_id=1, source_target_pairs={{0,2},{1,3},{2,0},{3,1},{4,6},{5,7},{6,4},{7,5},{8,10},{9,11},{10,... | collective-permute-start | bytes 614408 | tf_op jit(solution)/shard_map/ppermute | solution.py:35
  100.0 2.0 %collective-permute-start.20 = (bf16[80,1280]{1,0:T(8,128)(2,1)S(1)}, bf16[80,1280]{1,0:T(8,128)(2,1)S(1)}, u32[]{:S(2)}, u32[]{:S(2)}) collective-permute-start(bf16[80,1280]{1,0:T(8,128)(2,1)S(1)} %get-tuple-element.64), channel_id=1, source_target_pairs={{0,3},{1,0},{2,1},{3,2},{4,7},{5,4},{6,5},{7,6},{8,11},{9,8},{10,9... | collective-permute-start | bytes 614408 | tf_op jit(solution)/shard_map/ppermute | solution.py:35
  102.0 1.0 collective-permute-start.24
  103.0 0.0 collective-permute-start.21
  103.0 2.8 %collective-permute-done.23.refs_1_ = bf16[144,1280]{1,0:T(8,128)(2,1)S(1)} collective-permute-done((bf16[144,1280]{1,0:T(8,128)(2,1)S(1)}, bf16[144,1280]{1,0:T(8,128)(2,1)S(1)}, u32[]{:S(2)}, u32[]{:S(2)}) %collective-permute-start.23) | collective-permute-done | bytes 368672 | tf_op jit(solution)/shard_map/ppermute | solution.py:44
  105.8 0.1 collective-permute-start.25
  105.9 5.4 %collective-permute-done.24.refs_2_ = bf16[80,1280]{1,0:T(8,128)(2,1)S(1)} collective-permute-done((bf16[80,1280]{1,0:T(8,128)(2,1)S(1)}, bf16[80,1280]{1,0:T(8,128)(2,1)S(1)}, u32[]{:S(2)}, u32[]{:S(2)}) %collective-permute-start.24) | collective-permute-done | bytes 204832 | tf_op jit(solution)/shard_map/ppermute | solution.py:44
  111.3 0.1 shard_map.73.refs_4_
  111.4 0.0 collective-permute-done.20.refs_2_
  111.4 0.0 collective-permute-done.21.refs_3_
  111.4 0.8 shard_map.75
  (10 shorter events, 0.1 us)
Async XLA Ops:
  0.6 1.7 %collective-permute-start.3 = (bf16[64,1280]{1,0:T(8,128)(2,1)}, bf16[64,1280]{1,0:T(8,128)(2,1)S(1)}, u32[]{:S(2)}, u32[]{:S(2)}) collective-permute-start(bf16[64,1280]{1,0:T(8,128)(2,1)} %refs_0_.3), channel_id=1, source_target_pairs={{0,32},{32,0},{1,33},{33,1},{2,34},{34,2},{3,35},{35,3},{4,36},{36... | collective-permute-start | bytes 491528 | tf_op jit(solution)/shard_map/ppermute | solution.py:48
  2.3 19.1 %collective-permute-start.4 = (bf16[128,1280]{1,0:T(8,128)(2,1)S(1)}, bf16[128,1280]{1,0:T(8,128)(2,1)S(1)}, u32[]{:S(2)}, u32[]{:S(2)}) collective-permute-start(bf16[128,1280]{1,0:T(8,128)(2,1)S(1)} %shard_map.60.refs_4_), channel_id=1, source_target_pairs={{0,208},{64,0},{128,64},{192,128},{16,192},{80,16},{144,80},{208,1... | collective-permute-start | bytes 983048 | tf_op jit(solution)/shard_map/ppermute | solution.py:44
  4.3 17.2 %collective-permute-start.5 = (bf16[64,1280]{1,0:T(8,128)(2,1)}, bf16[64,1280]{1,0:T(8,128)(2,1)S(1)}, u32[]{:S(2)}, u32[]{:S(2)}) collective-permute-start(bf16[64,1280]{1,0:T(8,128)(2,1)} %refs_0_.3), channel_id=1, source_target_pairs={{0,16},{64,80},{128,144},{192,208},{16,0},{80,64},{144,128},{208,1... | collective-permute-start | bytes 491528 | tf_op jit(solution)/shard_map/ppermute | solution.py:44
  9.7 11.7 %collective-permute-start = (bf16[64,1280]{1,0:T(8,128)(2,1)}, bf16[64,1280]{1,0:T(8,128)(2,1)S(1)}, u32[]{:S(2)}, u32[]{:S(2)}) collective-permute-start(bf16[64,1280]{1,0:T(8,128)(2,1)} %refs_0_.2), channel_id=1, source_target_pairs={{0,1},{1,2},{2,3},{3,0},{4,5},{5,6},{6,7},{7,4},{8,9},{9,10},{10,1... | collective-permute-start | bytes 491528 | tf_op jit(solution)/shard_map/ppermute | solution.py:35
  11.2 10.2 %collective-permute-start.2 = (bf16[64,1280]{1,0:T(8,128)(2,1)}, bf16[64,1280]{1,0:T(8,128)(2,1)S(1)}, u32[]{:S(2)}, u32[]{:S(2)}) collective-permute-start(bf16[64,1280]{1,0:T(8,128)(2,1)} %refs_0_.2), channel_id=1, source_target_pairs={{0,3},{1,0},{2,1},{3,2},{4,7},{5,4},{6,5},{7,6},{8,11},{9,8},{10,9... | collective-permute-start | bytes 491528 | tf_op jit(solution)/shard_map/ppermute | solution.py:35
  13.0 8.5 %collective-permute-start.1 = (bf16[64,1280]{1,0:T(8,128)(2,1)}, bf16[64,1280]{1,0:T(8,128)(2,1)S(1)}, u32[]{:S(2)}, u32[]{:S(2)}) collective-permute-start(bf16[64,1280]{1,0:T(8,128)(2,1)} %refs_0_.2), channel_id=1, source_target_pairs={{0,2},{1,3},{2,0},{3,1},{4,6},{5,7},{6,4},{7,5},{8,10},{9,11},{10,... | collective-permute-start | bytes 491528 | tf_op jit(solution)/shard_map/ppermute | solution.py:35
  14.8 0.9 copy-start
  21.6 18.6 %collective-permute-start.9 = (bf16[256,1280]{1,0:T(8,128)(2,1)S(1)}, bf16[256,1280]{1,0:T(8,128)(2,1)S(1)}, u32[]{:S(2)}, u32[]{:S(2)}) collective-permute-start(bf16[256,1280]{1,0:T(8,128)(2,1)S(1)} %get-tuple-element.39.refs_4_), channel_id=1, source_target_pairs={{0,144},{64,208},{128,0},{192,64},{16,128},{80,192},{144,16},{208,... | collective-permute-start | bytes 1966088 | tf_op jit(solution)/shard_map/ppermute | solution.py:44
  23.3 19.8 %collective-permute-start.8 = (bf16[256,1280]{1,0:T(8,128)(2,1)S(1)}, bf16[256,1280]{1,0:T(8,128)(2,1)S(1)}, u32[]{:S(2)}, u32[]{:S(2)}) collective-permute-start(bf16[256,1280]{1,0:T(8,128)(2,1)S(1)} %get-tuple-element.38.refs_0_), channel_id=1, source_target_pairs={{0,8},{1,9},{2,10},{3,11},{4,12},{5,13},{6,14},{7,15},{8,0},{9,1},... | collective-permute-start | bytes 1966088 | tf_op jit(solution)/shard_map/ppermute | solution.py:35
  26.5 16.6 %collective-permute-start.7 = (bf16[256,1280]{1,0:T(8,128)(2,1)S(1)}, bf16[256,1280]{1,0:T(8,128)(2,1)}, u32[]{:S(2)}, u32[]{:S(2)}) collective-permute-start(bf16[256,1280]{1,0:T(8,128)(2,1)S(1)} %get-tuple-element.38.refs_0_), channel_id=1, source_target_pairs={{0,12},{1,13},{2,14},{3,15},{4,0},{5,1},{6,2},{7,3},{8,4},{9,5},{1... | collective-permute-start | bytes 1966088 | tf_op jit(solution)/shard_map/ppermute | solution.py:35
  27.5 15.5 %collective-permute-start.6 = (bf16[256,1280]{1,0:T(8,128)(2,1)S(1)}, bf16[256,1280]{1,0:T(8,128)(2,1)}, u32[]{:S(2)}, u32[]{:S(2)}) collective-permute-start(bf16[256,1280]{1,0:T(8,128)(2,1)S(1)} %get-tuple-element.38.refs_0_), channel_id=1, source_target_pairs={{0,4},{1,5},{2,6},{3,7},{4,8},{5,9},{6,10},{7,11},{8,12},{9,13},{1... | collective-permute-start | bytes 1966088 | tf_op jit(solution)/shard_map/ppermute | solution.py:35
  40.2 2.9 %collective-permute-start.10 = (bf16[256,1280]{1,0:T(8,128)(2,1)S(1)}, bf16[256,1280]{1,0:T(8,128)(2,1)}, u32[]{:S(2)}, u32[]{:S(2)}) collective-permute-start(bf16[256,1280]{1,0:T(8,128)(2,1)S(1)} %collective-permute-done.9.refs_5_), channel_id=1, source_target_pairs={{0,32},{32,0},{1,33},{33,1},{2,34},{34,2},{3,35},{35,3},{4,36},{36... | collective-permute-start | bytes 1966088 | tf_op jit(solution)/shard_map/ppermute | solution.py:48
  40.2 2.9 %collective-permute-start.11 = (bf16[192,1280]{1,0:T(8,128)(2,1)S(1)}, bf16[192,1280]{1,0:T(8,128)(2,1)}, u32[]{:S(2)}, u32[]{:S(2)}) collective-permute-start(bf16[192,1280]{1,0:T(8,128)(2,1)S(1)} %shard_map.62.refs_8_), channel_id=1, source_target_pairs={{0,32},{32,0},{1,33},{33,1},{2,34},{34,2},{3,35},{35,3},{4,36},{36... | collective-permute-start | bytes 1474568 | tf_op jit(solution)/shard_map/ppermute | solution.py:48
  49.1 1.4 %collective-permute-start.12 = (f32[24,128]{1,0:T(8,128)S(1)}, f32[24,128]{1,0:T(8,128)S(1)}, u32[]{:S(2)}, u32[]{:S(2)}) collective-permute-start(f32[24,128]{1,0:T(8,128)S(1)} %get-tuple-element.44), channel_id=1, source_target_pairs={{0,32},{32,0},{1,33},{33,1},{2,34},{34,2},{3,35},{35,3},{4,36},{36... | collective-permute-start | bytes 36872 | tf_op jit(solution)/shard_map/ppermute | solution.py:48
  66.5 1.3 %collective-permute-start.13 = (f32[24,128]{1,0:T(8,128)S(1)}, f32[24,128]{1,0:T(8,128)S(1)}, u32[]{:S(2)}, u32[]{:S(2)}) collective-permute-start(f32[24,128]{1,0:T(8,128)S(1)} %get-tuple-element.46), channel_id=1, source_target_pairs={{0,32},{32,0},{1,33},{33,1},{2,34},{34,2},{3,35},{35,3},{4,36},{36... | collective-permute-start | bytes 36872 | tf_op jit(solution)/shard_map/ppermute | solution.py:48
  70.7 2.9 %collective-permute-start.14 = (bf16[256,1280]{1,0:T(8,128)(2,1)S(1)}, bf16[256,1280]{1,0:T(8,128)(2,1)S(1)}, u32[]{:S(2)}, u32[]{:S(2)}) collective-permute-start(bf16[256,1280]{1,0:T(8,128)(2,1)S(1)} %get-tuple-element.55), channel_id=1, source_target_pairs={{0,32},{32,0},{1,33},{33,1},{2,34},{34,2},{3,35},{35,3},{4,36},{36... | collective-permute-start | bytes 1966088 | tf_op jit(solution)/shard_map/ppermute | solution.py:48
  70.9 2.6 %collective-permute-start.15 = (bf16[192,1280]{1,0:T(8,128)(2,1)S(1)}, bf16[192,1280]{1,0:T(8,128)(2,1)S(1)}, u32[]{:S(2)}, u32[]{:S(2)}) collective-permute-start(bf16[192,1280]{1,0:T(8,128)(2,1)S(1)} %get-tuple-element.57), channel_id=1, source_target_pairs={{0,32},{32,0},{1,33},{33,1},{2,34},{34,2},{3,35},{35,3},{4,36},{36... | collective-permute-start | bytes 1474568 | tf_op jit(solution)/shard_map/ppermute | solution.py:48
  73.7 24.0 %collective-permute-start.22 = (bf16[336,1280]{1,0:T(8,128)(2,1)S(1)}, bf16[336,1280]{1,0:T(8,128)(2,1)S(1)}, u32[]{:S(2)}, u32[]{:S(2)}) collective-permute-start(bf16[336,1280]{1,0:T(8,128)(2,1)S(1)} %shard_map.69.after), channel_id=1, source_target_pairs={{0,128},{64,192},{128,16},{192,80},{16,144},{80,208},{144,0},{208,... | collective-permute-start | bytes 2580488 | tf_op jit(solution)/shard_map/ppermute | solution.py:44
  77.3 21.0 %collective-permute-start.16 = (bf16[272,1280]{1,0:T(8,128)(2,1)S(1)}, bf16[272,1280]{1,0:T(8,128)(2,1)S(1)}, u32[]{:S(2)}, u32[]{:S(2)}) collective-permute-start(bf16[272,1280]{1,0:T(8,128)(2,1)S(1)} %get-tuple-element.59), channel_id=1, source_target_pairs={{0,8},{1,9},{2,10},{3,11},{4,12},{5,13},{6,14},{7,15},{8,0},{9,1},... | collective-permute-start | bytes 2088968 | tf_op jit(solution)/shard_map/ppermute | solution.py:35
  78.4 19.8 %collective-permute-start.17 = (bf16[272,1280]{1,0:T(8,128)(2,1)S(1)}, bf16[272,1280]{1,0:T(8,128)(2,1)S(1)}, u32[]{:S(2)}, u32[]{:S(2)}) collective-permute-start(bf16[272,1280]{1,0:T(8,128)(2,1)S(1)} %get-tuple-element.60), channel_id=1, source_target_pairs={{0,12},{1,13},{2,14},{3,15},{4,0},{5,1},{6,2},{7,3},{8,4},{9,5},{1... | collective-permute-start | bytes 2088968 | tf_op jit(solution)/shard_map/ppermute | solution.py:35
  80.3 17.9 %collective-permute-start.18 = (bf16[272,1280]{1,0:T(8,128)(2,1)S(1)}, bf16[272,1280]{1,0:T(8,128)(2,1)S(1)}, u32[]{:S(2)}, u32[]{:S(2)}) collective-permute-start(bf16[272,1280]{1,0:T(8,128)(2,1)S(1)} %get-tuple-element.61), channel_id=1, source_target_pairs={{0,4},{1,5},{2,6},{3,7},{4,8},{5,9},{6,10},{7,11},{8,12},{9,13},{1... | collective-permute-start | bytes 2088968 | tf_op jit(solution)/shard_map/ppermute | solution.py:35
  97.9 7.8 %collective-permute-start.23 = (bf16[144,1280]{1,0:T(8,128)(2,1)S(1)}, bf16[144,1280]{1,0:T(8,128)(2,1)S(1)}, u32[]{:S(2)}, u32[]{:S(2)}) collective-permute-start(bf16[144,1280]{1,0:T(8,128)(2,1)S(1)} %get-tuple-element.68), channel_id=1, source_target_pairs={{0,64},{64,128},{128,192},{192,16},{16,80},{80,144},{144,208},{208... | collective-permute-start | bytes 1105928 | tf_op jit(solution)/shard_map/ppermute | solution.py:44
  98.7 12.7 %collective-permute-start.19 = (bf16[80,1280]{1,0:T(8,128)(2,1)S(1)}, bf16[80,1280]{1,0:T(8,128)(2,1)S(1)}, u32[]{:S(2)}, u32[]{:S(2)}) collective-permute-start(bf16[80,1280]{1,0:T(8,128)(2,1)S(1)} %get-tuple-element.63), channel_id=1, source_target_pairs={{0,2},{1,3},{2,0},{3,1},{4,6},{5,7},{6,4},{7,5},{8,10},{9,11},{10,... | collective-permute-start | bytes 614408 | tf_op jit(solution)/shard_map/ppermute | solution.py:35
  100.0 11.4 %collective-permute-start.20 = (bf16[80,1280]{1,0:T(8,128)(2,1)S(1)}, bf16[80,1280]{1,0:T(8,128)(2,1)S(1)}, u32[]{:S(2)}, u32[]{:S(2)}) collective-permute-start(bf16[80,1280]{1,0:T(8,128)(2,1)S(1)} %get-tuple-element.64), channel_id=1, source_target_pairs={{0,3},{1,0},{2,1},{3,2},{4,7},{5,4},{6,5},{7,6},{8,11},{9,8},{10,9... | collective-permute-start | bytes 614408 | tf_op jit(solution)/shard_map/ppermute | solution.py:35
  102.0 9.3 %collective-permute-start.24 = (bf16[80,1280]{1,0:T(8,128)(2,1)S(1)}, bf16[80,1280]{1,0:T(8,128)(2,1)S(1)}, u32[]{:S(2)}, u32[]{:S(2)}) collective-permute-start(bf16[80,1280]{1,0:T(8,128)(2,1)S(1)} %get-tuple-element.69), channel_id=1, source_target_pairs={{0,128},{64,192},{128,16},{192,80},{16,144},{80,208},{144,0},{208,... | collective-permute-start | bytes 614408 | tf_op jit(solution)/shard_map/ppermute | solution.py:44
  103.0 8.4 %collective-permute-start.21 = (bf16[80,1280]{1,0:T(8,128)(2,1)S(1)}, bf16[80,1280]{1,0:T(8,128)(2,1)S(1)}, u32[]{:S(2)}, u32[]{:S(2)}) collective-permute-start(bf16[80,1280]{1,0:T(8,128)(2,1)S(1)} %get-tuple-element.65), channel_id=1, source_target_pairs={{0,1},{1,2},{2,3},{3,0},{4,5},{5,6},{6,7},{7,4},{8,9},{9,10},{10,1... | collective-permute-start | bytes 614408 | tf_op jit(solution)/shard_map/ppermute | solution.py:35
  105.8 5.6 %collective-permute-start.25 = (bf16[80,1280]{1,0:T(8,128)(2,1)S(1)}, bf16[80,1280]{1,0:T(8,128)(2,1)S(1)}, u32[]{:S(2)}, u32[]{:S(2)}) collective-permute-start(bf16[80,1280]{1,0:T(8,128)(2,1)S(1)} %shard_map.74), channel_id=1, source_target_pairs={{0,32},{32,0},{1,33},{33,1},{2,34},{34,2},{3,35},{35,3},{4,36},{36... | collective-permute-start | bytes 614408 | tf_op jit(solution)/shard_map/ppermute | solution.py:48

commit v18 on v16

--- a/solution.py
+++ b/solution.py
@@ -85,6 +85,11 @@
     return [row_place(where, a, b)[1] * ROWS + span for b in range(4)]
 
 
+def has_match(where, a, b):
+    block = row_place(where, a, b)[1]
+    return jnp.logical_and(((block >> 5) & 3) == where[3], ((block >> 3) & 3) == where[4])
+
+
 def col_ids(where):
     lane = lax.broadcasted_iota(jnp.int32, (8, 128), 1)
     out = []
@@ -163,12 +168,10 @@
     chunk_logits(0)
     cols = col_ids(where)
     step = 32
-    matched = jnp.zeros((8, 128), F32)
     col_top = [jnp.full((8, 128), -jnp.inf, F32) for _ in range(8)]
     for a in range(4):
         if a < 3:
             chunk_logits(a + 1)
-        ids = row_ids(where, a)
         for b in range(4):
             for half in range(ROWS // step):
                 at = a * CHUNK + b * ROWS + half * step
@@ -177,16 +180,25 @@
                 for t in range(1, 8):
                     top = jnp.maximum(top, tiles[t])
                 top = jnp.max(top, axis=1, keepdims=True)
-                mine = ids[b][half * step : (half + 1) * step]
                 total = jnp.zeros((step, 128), F32)
                 for t in range(8):
                     total += jnp.exp2(tiles[t] - top)
                     col_top[t] = jnp.maximum(col_top[t], jnp.max(fold(tiles[t]), axis=0))
-                    hit = jnp.where(mine == cols[t][0:1], tiles[t], 0.0)
-                    matched += jnp.sum(fold(hit), axis=0)
                 part = top + LOG2E * jnp.log(jnp.sum(total, axis=1, keepdims=True))
                 row_wide[at : at + step, :] = jnp.broadcast_to(part, (step, 128))
-    matched = two_sums(matched)
+    match_out[...] = jnp.zeros((8, 128), F32)
+    for a in range(4):
+        for b in range(4):
+
+            @pl.when(has_match(where, a, b))
+            def _(a=a, b=b):
+                at = a * CHUNK + b * ROWS
+                mine = row_ids(where, a)[b]
+                for t in range(8):
+                    hit = jnp.where(mine == cols[t][0:1], logits[at : at + ROWS, t * 128 : (t + 1) * 128], 0.0)
+                    match_out[...] += jnp.sum(fold(hit), axis=0)
+
+    matched = two_sums(match_out[...])
     match_out[...] = matched
     message[16:24, :] = matched
     for t in range(8):
@@ -305,16 +317,25 @@
 
 def half_weights(where, logits, at, row_wide, col_lines, weights):
     cols = col_ids(where)
-    for a in range(4):
-        ids = row_ids(where, a)
-        for b in range(4):
-            rows = slice(a * CHUNK + b * ROWS, a * CHUNK + (b + 1) * ROWS)
-            wide = row_wide[rows, :]
-            for t in range(4):
-                tile = logits[rows, (at + t) * 128 : (at + t + 1) * 128]
-                both = jnp.exp2(tile - wide) + jnp.exp2(tile - col_lines[at + t : at + t + 1, :])
-                both = both - jnp.where(ids[b] == cols[at + t][0:1], 1.0, 0.0)
-                weights[rows, t * 128 : (t + 1) * 128] = both.astype(BF16)
+
+    def block(a, b, labels):
+        rows = slice(a * CHUNK + b * ROWS, a * CHUNK + (b + 1) * ROWS)
+        wide = row_wide[rows, :]
+        for t in range(4):
+            tile = logits[rows, (at + t) * 128 : (at + t + 1) * 128]
+            both = jnp.exp2(tile - wide) + jnp.exp2(tile - col_lines[at + t : at + t + 1, :])
+            if labels is not None:
+                both = both - jnp.where(labels == cols[at + t][0:1], 1.0, 0.0)
+            weights[rows, t * 128 : (t + 1) * 128] = both.astype(BF16)
+
+    places = [(a, b) for a in range(4) for b in range(4)]
+    for a, b in places:
+        block(a, b, None)
+    for a, b in places:
+
+        @pl.when(has_match(where, a, b))
+        def _(a=a, b=b):
+            block(a, b, row_ids(where, a)[b])
 
 
 def high_body(place, scale, logits, mine, other, images, *refs):

time: 114 us -> 114 us (level)
  no operation moved by 1% of the time
where the time goes in v18:
time: 114 us; the launch traced here: 113 us
  waiting for transfers between devices  44.4 us (39%)
  starting transfers between devices  31.7 us (28%)
  Pallas kernels  19.8 us (17%)
  blocking collectives  14.3 us (13%)
  between operations  1.5 us (1%)
    ppermute x6, waiting for transfers between devices, z_shift(): return lax.ppermute(v, ('zl', 'core', 'zh'), pairs)  40.5 us
    ppermute x12, starting transfers between devices, plane_shift(): return lax.ppermute(v, ('core', 'zh', 'y', 'x'), pairs)  17.4 us
    all_to_all x1, blocking collectives, exchange(): return lax.all_to_all(v, AXES, 0, 0, axis_index_groups=groups)  14.3 us
    ppermute x6, starting transfers between devices, z_shift(): return lax.ppermute(v, ('zl', 'core', 'zh'), pairs)  12.6 us
    pallas_call x1, Pallas kernels, logits_call(): pl.pallas_call(logits_body, out_shape=(jax.ShapeDtypeStruct((BLOCK, BLOCK...  6.01 us
    ppermute x8, waiting for transfers between devices, core_swap(): return lax.ppermute(v, 'core', [(0, 1), (1, 0)])  3.9 us
    pallas_call x1, Pallas kernels, high_call(): pl.pallas_call(high_body, out_shape=(HALF_WEIGHTS, PART, jax.ShapeDtypeSt...  2.94 us
  transfers between devices with their start and end apart: 26, of which 10 were waited for; matrix products, arithmetic and copies ran while one was open for 0% of the time, Pallas kernels for 7%

profile of v18, /device:TPU:32, one launch (start us, length us, event | category | flops | bytes accessed | tf_op | source)
XLA Modules:
  0.0 112.8 jit_solution(4547199043097598063)
XLA Ops:
  0.6 0.1 collective-permute-start.3
  0.7 0.9 shard_map.59.refs_0_
  1.7 0.7 collective-permute-done.3.refs_1_
  2.3 1.9 %collective-permute-start.4 = (bf16[128,1280]{1,0:T(8,128)(2,1)S(1)}, bf16[128,1280]{1,0:T(8,128)(2,1)S(1)}, u32[]{:S(2)}, u32[]{:S(2)}) collective-permute-start(bf16[128,1280]{1,0:T(8,128)(2,1)S(1)} %shard_map.60.refs_4_), channel_id=1, source_target_pairs={{0,208},{64,0},{128,64},{192,128},{16,192},{80,16},{144,80},{208,1... | collective-permute-start | bytes 983048 | tf_op jit(solution)/shard_map/ppermute | solution.py:44
  4.3 5.5 %collective-permute-start.5 = (bf16[64,1280]{1,0:T(8,128)(2,1)}, bf16[64,1280]{1,0:T(8,128)(2,1)S(1)}, u32[]{:S(2)}, u32[]{:S(2)}) collective-permute-start(bf16[64,1280]{1,0:T(8,128)(2,1)} %refs_0_.3), channel_id=1, source_target_pairs={{0,16},{64,80},{128,144},{192,208},{16,0},{80,64},{144,128},{208,1... | collective-permute-start | bytes 491528 | tf_op jit(solution)/shard_map/ppermute | solution.py:44
  9.7 1.5 %collective-permute-start = (bf16[64,1280]{1,0:T(8,128)(2,1)}, bf16[64,1280]{1,0:T(8,128)(2,1)S(1)}, u32[]{:S(2)}, u32[]{:S(2)}) collective-permute-start(bf16[64,1280]{1,0:T(8,128)(2,1)} %refs_0_.2), channel_id=1, source_target_pairs={{0,1},{1,2},{2,3},{3,0},{4,5},{5,6},{6,7},{7,4},{8,9},{9,10},{10,1... | collective-permute-start | bytes 491528 | tf_op jit(solution)/shard_map/ppermute | solution.py:35
  11.2 1.7 %collective-permute-start.2 = (bf16[64,1280]{1,0:T(8,128)(2,1)}, bf16[64,1280]{1,0:T(8,128)(2,1)S(1)}, u32[]{:S(2)}, u32[]{:S(2)}) collective-permute-start(bf16[64,1280]{1,0:T(8,128)(2,1)} %refs_0_.2), channel_id=1, source_target_pairs={{0,3},{1,0},{2,1},{3,2},{4,7},{5,4},{6,5},{7,6},{8,11},{9,8},{10,9... | collective-permute-start | bytes 491528 | tf_op jit(solution)/shard_map/ppermute | solution.py:35
  13.0 1.8 %collective-permute-start.1 = (bf16[64,1280]{1,0:T(8,128)(2,1)}, bf16[64,1280]{1,0:T(8,128)(2,1)S(1)}, u32[]{:S(2)}, u32[]{:S(2)}) collective-permute-start(bf16[64,1280]{1,0:T(8,128)(2,1)} %refs_0_.2), channel_id=1, source_target_pairs={{0,2},{1,3},{2,0},{3,1},{4,6},{5,7},{6,4},{7,5},{8,10},{9,11},{10,... | collective-permute-start | bytes 491528 | tf_op jit(solution)/shard_map/ppermute | solution.py:35
  14.8 0.9 copy-done
  15.7 5.7 %collective-permute-done.5.refs_6_.refs_1_.refs_8_ = bf16[64,1280]{1,0:T(8,128)(2,1)S(1)} collective-permute-done((bf16[64,1280]{1,0:T(8,128)(2,1)}, bf16[64,1280]{1,0:T(8,128)(2,1)S(1)}, u32[]{:S(2)}, u32[]{:S(2)}) %collective-permute-start.5) | collective-permute-done | bytes 163872 | tf_op jit(solution)/shard_map/ppermute | solution.py:44
  21.5 0.0 collective-permute-done.refs_1_
  21.5 0.0 collective-permute-done.2.refs_3_
  21.5 0.0 collective-permute-done.1.refs_2_
  21.5 0.0 collective-permute-done.4.refs_5_.refs_0_
  21.5 0.1 shard_map.61
  21.6 1.7 %collective-permute-start.9 = (bf16[256,1280]{1,0:T(8,128)(2,1)S(1)}, bf16[256,1280]{1,0:T(8,128)(2,1)S(1)}, u32[]{:S(2)}, u32[]{:S(2)}) collective-permute-start(bf16[256,1280]{1,0:T(8,128)(2,1)S(1)} %get-tuple-element.39.refs_4_), channel_id=1, source_target_pairs={{0,144},{64,208},{128,0},{192,64},{16,128},{80,192},{144,16},{208,... | collective-permute-start | bytes 1966088 | tf_op jit(solution)/shard_map/ppermute | solution.py:44
  23.3 3.2 %collective-permute-start.8 = (bf16[256,1280]{1,0:T(8,128)(2,1)S(1)}, bf16[256,1280]{1,0:T(8,128)(2,1)S(1)}, u32[]{:S(2)}, u32[]{:S(2)}) collective-permute-start(bf16[256,1280]{1,0:T(8,128)(2,1)S(1)} %get-tuple-element.38.refs_0_), channel_id=1, source_target_pairs={{0,8},{1,9},{2,10},{3,11},{4,12},{5,13},{6,14},{7,15},{8,0},{9,1},... | collective-permute-start | bytes 1966088 | tf_op jit(solution)/shard_map/ppermute | solution.py:35
  26.5 1.1 collective-permute-start.7
  27.5 1.0 collective-permute-start.6
  28.5 11.6 %collective-permute-done.9.refs_5_ = bf16[256,1280]{1,0:T(8,128)(2,1)S(1)} collective-permute-done((bf16[256,1280]{1,0:T(8,128)(2,1)S(1)}, bf16[256,1280]{1,0:T(8,128)(2,1)S(1)}, u32[]{:S(2)}, u32[]{:S(2)}) %collective-permute-start.9) | collective-permute-done | bytes 655392 | tf_op jit(solution)/shard_map/ppermute | solution.py:44
  40.2 0.8 shard_map.62
  41.0 0.5 collective-permute-start.11
  42.2 0.1 stack.23.place
  42.2 1.1 collective-permute-done.11.refs_7_
  43.3 0.0 collective-permute-done.8.refs_3_
  43.3 0.0 collective-permute-done.7.refs_2_
  43.3 0.0 collective-permute-done.6.refs_1_
  43.4 6.0 %shard_map.63 = (f32[1024,1024]{1,0:T(8,128)S(1)}, f32[16,128]{1,0:T(8,128)S(1)}, f32[16,128]{1,0:T(8,128)S(1)}, f32[24,128]{1,0:T(8,128)S(1)}, f32[8,128]{1,0:T...) custom-call(s32[5]{0:T(128)S(1)} %stack.23.place, f32[1]{0:T(128)S(6)} %copy.6.scale, ...), custom_call_target="tpu_custom_call" | custom-call | tf_op jit(solution)/shard_map/pallas_call | solution.py:216
  49.4 0.4 collective-permute-start.12
  49.8 0.8 collective-permute-done.12.got
  50.6 0.6 shard_map.64
  51.3 14.3 %all_to_all.5.got = f32[16,24,128]{2,1,0:T(8,128)S(1)} all-to-all(f32[16,24,128]{2,1,0:T(8,128)S(1)} %shard_map.64), channel_id=1, replica_groups={{0,1,2,3,4,5,6,7,8,9,10,11,12,13,14,15},{64,65,66,67,68,69,70,71,72,73,..., dimensions={0} | all-to-all | bytes 393216 | tf_op jit(solution)/shard_map/all_to_all | solution.py:63
  65.6 0.7 shard_map.65
  66.3 0.1 collective-permute-start.13
  66.4 1.2 %collective-permute-done.13.other = f32[24,128]{1,0:T(8,128)S(1)} collective-permute-done((f32[24,128]{1,0:T(8,128)S(1)}, f32[24,128]{1,0:T(8,128)S(1)}, u32[]{:S(2)}, u32[]{:S(2)}) %collective-permute-start.13) | collective-permute-done | bytes 12320 | tf_op jit(solution)/shard_map/ppermute | solution.py:48
  67.6 2.9 %shard_map.66 = (bf16[1024,512]{1,0:T(8,128)(2,1)S(1)}, bf16[256,1280]{1,0:T(8,128)(2,1)S(1)}, bf16[192,1280]{1,0:T(8,128)(2,1)S(1)}, bf16[64,1280]{1,0:T(8,128)...) custom-call(s32[5]{0:T(128)S(1)} %stack.23.place, f32[1]{0:T(128)S(6)} %copy.6.scale, ...), custom_call_target="tpu_custom_call" | custom-call | tf_op jit(solution)/shard_map/pallas_call | solution.py:369
  70.5 0.3 collective-permute-start.14
  70.8 0.3 collective-permute-start.15
  71.1 2.1 %shard_map.67 = (bf16[1024,512]{1,0:T(8,128)(2,1)S(1)}, bf16[256,1280]{1,0:T(8,128)(2,1)S(1)}) custom-call(s32[5]{0:T(128)S(1)} %stack.23.place, f32[1]{0:T(128)S(6)} %copy.6.scale, f32[1024,1024]{1,0:T(8,128)S(1)} %get-tuple-element.40.logits, f32[1024,128]{1,0:T(8,128)S(1)} %get-tuple-element.48.row_wide, f32[8,128]{1,0:T(8,128)S(1)} %get-tuple-element.49.col_lines, ...), custom_call_target="tpu_custom_call" | custom-call | tf_op jit(solution)/shard_map/pallas_call | solution.py:393
  73.2 0.1 collective-permute-done.15.refs_3_.refs_1_
  73.4 0.0 collective-permute-done.14.refs_1_
  73.4 0.2 shard_map.69.after
  73.6 1.5 %collective-permute-start.22 = (bf16[336,1280]{1,0:T(8,128)(2,1)S(1)}, bf16[336,1280]{1,0:T(8,128)(2,1)S(1)}, u32[]{:S(2)}, u32[]{:S(2)}) collective-permute-start(bf16[336,1280]{1,0:T(8,128)(2,1)S(1)} %shard_map.69.after), channel_id=1, source_target_pairs={{0,128},{64,192},{128,16},{192,80},{16,144},{80,208},{144,0},{208,... | collective-permute-start | bytes 2580488 | tf_op jit(solution)/shard_map/ppermute | solution.py:44
  75.1 2.2 %shard_map.70 = (bf16[272,1280]{1,0:T(8,128)(2,1)S(1)}, bf16[272,1280]{1,0:T(8,128)(2,1)S(1)}, bf16[272,1280]{1,0:T(8,128)(2,1)S(1)}) custom-call(f32[1]{0:T(128)S(6)} %copy.6.scale, bf16[336,1280]{1,0:T(8,128)(2,1)S(1)} %shard_map.69.after, bf16[32,1280]{1,0:T(8,128)(2,1)S(1)} %get-tuple-element.58.refs_4_.digits.refs_3_.refs_6_, ...), custom_call_target="tpu_custom_call" | custom-call | tf_op jit(solution)/shard_map/pallas_call | solution.py:438
  77.3 1.7 %collective-permute-start.16 = (bf16[272,1280]{1,0:T(8,128)(2,1)S(1)}, bf16[272,1280]{1,0:T(8,128)(2,1)S(1)}, u32[]{:S(2)}, u32[]{:S(2)}) collective-permute-start(bf16[272,1280]{1,0:T(8,128)(2,1)S(1)} %get-tuple-element.59), channel_id=1, source_target_pairs={{0,8},{1,9},{2,10},{3,11},{4,12},{5,13},{6,14},{7,15},{8,0},{9,1},... | collective-permute-start | bytes 2088968 | tf_op jit(solution)/shard_map/ppermute | solution.py:35
  79.0 1.2 %collective-permute-start.17 = (bf16[272,1280]{1,0:T(8,128)(2,1)S(1)}, bf16[272,1280]{1,0:T(8,128)(2,1)S(1)}, u32[]{:S(2)}, u32[]{:S(2)}) collective-permute-start(bf16[272,1280]{1,0:T(8,128)(2,1)S(1)} %get-tuple-element.60), channel_id=1, source_target_pairs={{0,12},{1,13},{2,14},{3,15},{4,0},{5,1},{6,2},{7,3},{8,4},{9,5},{1... | collective-permute-start | bytes 2088968 | tf_op jit(solution)/shard_map/ppermute | solution.py:35
  80.1 0.9 collective-permute-start.18
  81.0 1.6 %shard_map.68 = (bf16[256,1280]{1,0:T(8,128)(2,1)S(1)}, bf16[256,1280]{1,0:T(8,128)(2,1)S(1)}) custom-call(f32[1]{0:T(128)S(6)} %copy.6.scale, bf16[1024,512]{1,0:T(8,128)(2,1)S(1)} %get-tuple-element.50.low, bf16[1024,512]{1,0:T(8,128)(2,1)S(1)} %get-tuple-element.51.high, bf16[1024,1280]{1,0:T(8,128)(2,1)S(1)} %get-tuple-element.47.images, ...), custom_call_target="tpu_custom_call" | custom-call | tf_op jit(solution)/shard_map/pallas_call | solution.py:453
  82.6 15.1 %collective-permute-done.22.refs_2_ = bf16[336,1280]{1,0:T(8,128)(2,1)S(1)} collective-permute-done((bf16[336,1280]{1,0:T(8,128)(2,1)S(1)}, bf16[336,1280]{1,0:T(8,128)(2,1)S(1)}, u32[]{:S(2)}, u32[]{:S(2)}) %collective-permute-start.22) | collective-permute-done | bytes 860192 | tf_op jit(solution)/shard_map/ppermute | solution.py:44
  97.7 0.2 shard_map.72
  97.9 0.1 collective-permute-start.23
  98.0 0.0 collective-permute-done.16.refs_1_
  98.0 0.4 shard_map.71
  98.5 0.7 collective-permute-start.19
  99.2 2.1 %collective-permute-start.20 = (bf16[80,1280]{1,0:T(8,128)(2,1)S(1)}, bf16[80,1280]{1,0:T(8,128)(2,1)S(1)}, u32[]{:S(2)}, u32[]{:S(2)}) collective-permute-start(bf16[80,1280]{1,0:T(8,128)(2,1)S(1)} %get-tuple-element.64), channel_id=1, source_target_pairs={{0,3},{1,0},{2,1},{3,2},{4,7},{5,4},{6,5},{7,6},{8,11},{9,8},{10,9... | collective-permute-start | bytes 614408 | tf_op jit(solution)/shard_map/ppermute | solution.py:35
  101.3 1.9 %collective-permute-start.24 = (bf16[80,1280]{1,0:T(8,128)(2,1)S(1)}, bf16[80,1280]{1,0:T(8,128)(2,1)S(1)}, u32[]{:S(2)}, u32[]{:S(2)}) collective-permute-start(bf16[80,1280]{1,0:T(8,128)(2,1)S(1)} %get-tuple-element.69), channel_id=1, source_target_pairs={{0,128},{64,192},{128,16},{192,80},{16,144},{80,208},{144,0},{208,... | collective-permute-start | bytes 614408 | tf_op jit(solution)/shard_map/ppermute | solution.py:44
  103.2 0.6 collective-permute-start.21
  103.7 1.8 %collective-permute-done.23.refs_1_ = bf16[144,1280]{1,0:T(8,128)(2,1)S(1)} collective-permute-done((bf16[144,1280]{1,0:T(8,128)(2,1)S(1)}, bf16[144,1280]{1,0:T(8,128)(2,1)S(1)}, u32[]{:S(2)}, u32[]{:S(2)}) %collective-permute-start.23) | collective-permute-done | bytes 368672 | tf_op jit(solution)/shard_map/ppermute | solution.py:44
  105.6 0.1 collective-permute-start.25
  105.7 6.2 %collective-permute-done.24.refs_2_ = bf16[80,1280]{1,0:T(8,128)(2,1)S(1)} collective-permute-done((bf16[80,1280]{1,0:T(8,128)(2,1)S(1)}, bf16[80,1280]{1,0:T(8,128)(2,1)S(1)}, u32[]{:S(2)}, u32[]{:S(2)}) %collective-permute-start.24) | collective-permute-done | bytes 204832 | tf_op jit(solution)/shard_map/ppermute | solution.py:44
  111.9 0.1 shard_map.73.refs_4_
  112.0 0.0 collective-permute-done.21.refs_3_
  112.0 0.0 collective-permute-done.25.refs_5_
  112.0 0.8 shard_map.75
  (10 shorter events, 0.1 us)
Async XLA Ops:
  0.6 1.7 %collective-permute-start.3 = (bf16[64,1280]{1,0:T(8,128)(2,1)}, bf16[64,1280]{1,0:T(8,128)(2,1)S(1)}, u32[]{:S(2)}, u32[]{:S(2)}) collective-permute-start(bf16[64,1280]{1,0:T(8,128)(2,1)} %refs_0_.3), channel_id=1, source_target_pairs={{0,32},{32,0},{1,33},{33,1},{2,34},{34,2},{3,35},{35,3},{4,36},{36... | collective-permute-start | bytes 491528 | tf_op jit(solution)/shard_map/ppermute | solution.py:48
  2.3 19.1 %collective-permute-start.4 = (bf16[128,1280]{1,0:T(8,128)(2,1)S(1)}, bf16[128,1280]{1,0:T(8,128)(2,1)S(1)}, u32[]{:S(2)}, u32[]{:S(2)}) collective-permute-start(bf16[128,1280]{1,0:T(8,128)(2,1)S(1)} %shard_map.60.refs_4_), channel_id=1, source_target_pairs={{0,208},{64,0},{128,64},{192,128},{16,192},{80,16},{144,80},{208,1... | collective-permute-start | bytes 983048 | tf_op jit(solution)/shard_map/ppermute | solution.py:44
  4.3 17.2 %collective-permute-start.5 = (bf16[64,1280]{1,0:T(8,128)(2,1)}, bf16[64,1280]{1,0:T(8,128)(2,1)S(1)}, u32[]{:S(2)}, u32[]{:S(2)}) collective-permute-start(bf16[64,1280]{1,0:T(8,128)(2,1)} %refs_0_.3), channel_id=1, source_target_pairs={{0,16},{64,80},{128,144},{192,208},{16,0},{80,64},{144,128},{208,1... | collective-permute-start | bytes 491528 | tf_op jit(solution)/shard_map/ppermute | solution.py:44
  9.7 11.7 %collective-permute-start = (bf16[64,1280]{1,0:T(8,128)(2,1)}, bf16[64,1280]{1,0:T(8,128)(2,1)S(1)}, u32[]{:S(2)}, u32[]{:S(2)}) collective-permute-start(bf16[64,1280]{1,0:T(8,128)(2,1)} %refs_0_.2), channel_id=1, source_target_pairs={{0,1},{1,2},{2,3},{3,0},{4,5},{5,6},{6,7},{7,4},{8,9},{9,10},{10,1... | collective-permute-start | bytes 491528 | tf_op jit(solution)/shard_map/ppermute | solution.py:35
  11.2 10.2 %collective-permute-start.2 = (bf16[64,1280]{1,0:T(8,128)(2,1)}, bf16[64,1280]{1,0:T(8,128)(2,1)S(1)}, u32[]{:S(2)}, u32[]{:S(2)}) collective-permute-start(bf16[64,1280]{1,0:T(8,128)(2,1)} %refs_0_.2), channel_id=1, source_target_pairs={{0,3},{1,0},{2,1},{3,2},{4,7},{5,4},{6,5},{7,6},{8,11},{9,8},{10,9... | collective-permute-start | bytes 491528 | tf_op jit(solution)/shard_map/ppermute | solution.py:35
  13.0 8.5 %collective-permute-start.1 = (bf16[64,1280]{1,0:T(8,128)(2,1)}, bf16[64,1280]{1,0:T(8,128)(2,1)S(1)}, u32[]{:S(2)}, u32[]{:S(2)}) collective-permute-start(bf16[64,1280]{1,0:T(8,128)(2,1)} %refs_0_.2), channel_id=1, source_target_pairs={{0,2},{1,3},{2,0},{3,1},{4,6},{5,7},{6,4},{7,5},{8,10},{9,11},{10,... | collective-permute-start | bytes 491528 | tf_op jit(solution)/shard_map/ppermute | solution.py:35
  14.8 0.9 copy-start
  21.6 18.6 %collective-permute-start.9 = (bf16[256,1280]{1,0:T(8,128)(2,1)S(1)}, bf16[256,1280]{1,0:T(8,128)(2,1)S(1)}, u32[]{:S(2)}, u32[]{:S(2)}) collective-permute-start(bf16[256,1280]{1,0:T(8,128)(2,1)S(1)} %get-tuple-element.39.refs_4_), channel_id=1, source_target_pairs={{0,144},{64,208},{128,0},{192,64},{16,128},{80,192},{144,16},{208,... | collective-permute-start | bytes 1966088 | tf_op jit(solution)/shard_map/ppermute | solution.py:44
  23.3 20.0 %collective-permute-start.8 = (bf16[256,1280]{1,0:T(8,128)(2,1)S(1)}, bf16[256,1280]{1,0:T(8,128)(2,1)S(1)}, u32[]{:S(2)}, u32[]{:S(2)}) collective-permute-start(bf16[256,1280]{1,0:T(8,128)(2,1)S(1)} %get-tuple-element.38.refs_0_), channel_id=1, source_target_pairs={{0,8},{1,9},{2,10},{3,11},{4,12},{5,13},{6,14},{7,15},{8,0},{9,1},... | collective-permute-start | bytes 1966088 | tf_op jit(solution)/shard_map/ppermute | solution.py:35
  26.5 16.8 %collective-permute-start.7 = (bf16[256,1280]{1,0:T(8,128)(2,1)S(1)}, bf16[256,1280]{1,0:T(8,128)(2,1)S(1)}, u32[]{:S(2)}, u32[]{:S(2)}) collective-permute-start(bf16[256,1280]{1,0:T(8,128)(2,1)S(1)} %get-tuple-element.38.refs_0_), channel_id=1, source_target_pairs={{0,12},{1,13},{2,14},{3,15},{4,0},{5,1},{6,2},{7,3},{8,4},{9,5},{1... | collective-permute-start | bytes 1966088 | tf_op jit(solution)/shard_map/ppermute | solution.py:35
  27.5 15.8 %collective-permute-start.6 = (bf16[256,1280]{1,0:T(8,128)(2,1)S(1)}, bf16[256,1280]{1,0:T(8,128)(2,1)}, u32[]{:S(2)}, u32[]{:S(2)}) collective-permute-start(bf16[256,1280]{1,0:T(8,128)(2,1)S(1)} %get-tuple-element.38.refs_0_), channel_id=1, source_target_pairs={{0,4},{1,5},{2,6},{3,7},{4,8},{5,9},{6,10},{7,11},{8,12},{9,13},{1... | collective-permute-start | bytes 1966088 | tf_op jit(solution)/shard_map/ppermute | solution.py:35
  40.2 3.2 %collective-permute-start.10 = (bf16[256,1280]{1,0:T(8,128)(2,1)S(1)}, bf16[256,1280]{1,0:T(8,128)(2,1)}, u32[]{:S(2)}, u32[]{:S(2)}) collective-permute-start(bf16[256,1280]{1,0:T(8,128)(2,1)S(1)} %collective-permute-done.9.refs_5_), channel_id=1, source_target_pairs={{0,32},{32,0},{1,33},{33,1},{2,34},{34,2},{3,35},{35,3},{4,36},{36... | collective-permute-start | bytes 1966088 | tf_op jit(solution)/shard_map/ppermute | solution.py:48
  41.0 2.3 %collective-permute-start.11 = (bf16[192,1280]{1,0:T(8,128)(2,1)}, bf16[192,1280]{1,0:T(8,128)(2,1)}, u32[]{:S(2)}, u32[]{:S(2)}) collective-permute-start(bf16[192,1280]{1,0:T(8,128)(2,1)} %shard_map.62), channel_id=1, source_target_pairs={{0,32},{32,0},{1,33},{33,1},{2,34},{34,2},{3,35},{35,3},{4,36},{36... | collective-permute-start | bytes 1474568 | tf_op jit(solution)/shard_map/ppermute | solution.py:48
  49.4 1.2 %collective-permute-start.12 = (f32[24,128]{1,0:T(8,128)S(1)}, f32[24,128]{1,0:T(8,128)S(1)}, u32[]{:S(2)}, u32[]{:S(2)}) collective-permute-start(f32[24,128]{1,0:T(8,128)S(1)} %get-tuple-element.44), channel_id=1, source_target_pairs={{0,32},{32,0},{1,33},{33,1},{2,34},{34,2},{3,35},{35,3},{4,36},{36... | collective-permute-start | bytes 36872 | tf_op jit(solution)/shard_map/ppermute | solution.py:48
  66.3 1.3 %collective-permute-start.13 = (f32[24,128]{1,0:T(8,128)S(1)}, f32[24,128]{1,0:T(8,128)S(1)}, u32[]{:S(2)}, u32[]{:S(2)}) collective-permute-start(f32[24,128]{1,0:T(8,128)S(1)} %get-tuple-element.46), channel_id=1, source_target_pairs={{0,32},{32,0},{1,33},{33,1},{2,34},{34,2},{3,35},{35,3},{4,36},{36... | collective-permute-start | bytes 36872 | tf_op jit(solution)/shard_map/ppermute | solution.py:48
  70.5 2.9 %collective-permute-start.14 = (bf16[256,1280]{1,0:T(8,128)(2,1)S(1)}, bf16[256,1280]{1,0:T(8,128)(2,1)S(1)}, u32[]{:S(2)}, u32[]{:S(2)}) collective-permute-start(bf16[256,1280]{1,0:T(8,128)(2,1)S(1)} %get-tuple-element.55), channel_id=1, source_target_pairs={{0,32},{32,0},{1,33},{33,1},{2,34},{34,2},{3,35},{35,3},{4,36},{36... | collective-permute-start | bytes 1966088 | tf_op jit(solution)/shard_map/ppermute | solution.py:48
  70.8 2.6 %collective-permute-start.15 = (bf16[192,1280]{1,0:T(8,128)(2,1)S(1)}, bf16[192,1280]{1,0:T(8,128)(2,1)S(1)}, u32[]{:S(2)}, u32[]{:S(2)}) collective-permute-start(bf16[192,1280]{1,0:T(8,128)(2,1)S(1)} %get-tuple-element.57), channel_id=1, source_target_pairs={{0,32},{32,0},{1,33},{33,1},{2,34},{34,2},{3,35},{35,3},{4,36},{36... | collective-permute-start | bytes 1474568 | tf_op jit(solution)/shard_map/ppermute | solution.py:48
  73.6 24.1 %collective-permute-start.22 = (bf16[336,1280]{1,0:T(8,128)(2,1)S(1)}, bf16[336,1280]{1,0:T(8,128)(2,1)S(1)}, u32[]{:S(2)}, u32[]{:S(2)}) collective-permute-start(bf16[336,1280]{1,0:T(8,128)(2,1)S(1)} %shard_map.69.after), channel_id=1, source_target_pairs={{0,128},{64,192},{128,16},{192,80},{16,144},{80,208},{144,0},{208,... | collective-permute-start | bytes 2580488 | tf_op jit(solution)/shard_map/ppermute | solution.py:44
  77.3 20.7 %collective-permute-start.16 = (bf16[272,1280]{1,0:T(8,128)(2,1)S(1)}, bf16[272,1280]{1,0:T(8,128)(2,1)S(1)}, u32[]{:S(2)}, u32[]{:S(2)}) collective-permute-start(bf16[272,1280]{1,0:T(8,128)(2,1)S(1)} %get-tuple-element.59), channel_id=1, source_target_pairs={{0,8},{1,9},{2,10},{3,11},{4,12},{5,13},{6,14},{7,15},{8,0},{9,1},... | collective-permute-start | bytes 2088968 | tf_op jit(solution)/shard_map/ppermute | solution.py:35
  79.0 19.1 %collective-permute-start.17 = (bf16[272,1280]{1,0:T(8,128)(2,1)S(1)}, bf16[272,1280]{1,0:T(8,128)(2,1)S(1)}, u32[]{:S(2)}, u32[]{:S(2)}) collective-permute-start(bf16[272,1280]{1,0:T(8,128)(2,1)S(1)} %get-tuple-element.60), channel_id=1, source_target_pairs={{0,12},{1,13},{2,14},{3,15},{4,0},{5,1},{6,2},{7,3},{8,4},{9,5},{1... | collective-permute-start | bytes 2088968 | tf_op jit(solution)/shard_map/ppermute | solution.py:35
  80.1 17.9 %collective-permute-start.18 = (bf16[272,1280]{1,0:T(8,128)(2,1)S(1)}, bf16[272,1280]{1,0:T(8,128)(2,1)S(1)}, u32[]{:S(2)}, u32[]{:S(2)}) collective-permute-start(bf16[272,1280]{1,0:T(8,128)(2,1)S(1)} %get-tuple-element.61), channel_id=1, source_target_pairs={{0,4},{1,5},{2,6},{3,7},{4,8},{5,9},{6,10},{7,11},{8,12},{9,13},{1... | collective-permute-start | bytes 2088968 | tf_op jit(solution)/shard_map/ppermute | solution.py:35
  97.9 7.6 %collective-permute-start.23 = (bf16[144,1280]{1,0:T(8,128)(2,1)S(1)}, bf16[144,1280]{1,0:T(8,128)(2,1)S(1)}, u32[]{:S(2)}, u32[]{:S(2)}) collective-permute-start(bf16[144,1280]{1,0:T(8,128)(2,1)S(1)} %get-tuple-element.68), channel_id=1, source_target_pairs={{0,64},{64,128},{128,192},{192,16},{16,80},{80,144},{144,208},{208... | collective-permute-start | bytes 1105928 | tf_op jit(solution)/shard_map/ppermute | solution.py:44
  98.5 13.5 %collective-permute-start.19 = (bf16[80,1280]{1,0:T(8,128)(2,1)S(1)}, bf16[80,1280]{1,0:T(8,128)(2,1)S(1)}, u32[]{:S(2)}, u32[]{:S(2)}) collective-permute-start(bf16[80,1280]{1,0:T(8,128)(2,1)S(1)} %get-tuple-element.63), channel_id=1, source_target_pairs={{0,2},{1,3},{2,0},{3,1},{4,6},{5,7},{6,4},{7,5},{8,10},{9,11},{10,... | collective-permute-start | bytes 614408 | tf_op jit(solution)/shard_map/ppermute | solution.py:35
  99.2 12.8 %collective-permute-start.20 = (bf16[80,1280]{1,0:T(8,128)(2,1)S(1)}, bf16[80,1280]{1,0:T(8,128)(2,1)S(1)}, u32[]{:S(2)}, u32[]{:S(2)}) collective-permute-start(bf16[80,1280]{1,0:T(8,128)(2,1)S(1)} %get-tuple-element.64), channel_id=1, source_target_pairs={{0,3},{1,0},{2,1},{3,2},{4,7},{5,4},{6,5},{7,6},{8,11},{9,8},{10,9... | collective-permute-start | bytes 614408 | tf_op jit(solution)/shard_map/ppermute | solution.py:35
  101.3 10.6 %collective-permute-start.24 = (bf16[80,1280]{1,0:T(8,128)(2,1)S(1)}, bf16[80,1280]{1,0:T(8,128)(2,1)S(1)}, u32[]{:S(2)}, u32[]{:S(2)}) collective-permute-start(bf16[80,1280]{1,0:T(8,128)(2,1)S(1)} %get-tuple-element.69), channel_id=1, source_target_pairs={{0,128},{64,192},{128,16},{192,80},{16,144},{80,208},{144,0},{208,... | collective-permute-start | bytes 614408 | tf_op jit(solution)/shard_map/ppermute | solution.py:44
  103.2 8.8 %collective-permute-start.21 = (bf16[80,1280]{1,0:T(8,128)(2,1)S(1)}, bf16[80,1280]{1,0:T(8,128)(2,1)S(1)}, u32[]{:S(2)}, u32[]{:S(2)}) collective-permute-start(bf16[80,1280]{1,0:T(8,128)(2,1)S(1)} %get-tuple-element.65), channel_id=1, source_target_pairs={{0,1},{1,2},{2,3},{3,0},{4,5},{5,6},{6,7},{7,4},{8,9},{9,10},{10,1... | collective-permute-start | bytes 614408 | tf_op jit(solution)/shard_map/ppermute | solution.py:35
  105.6 6.4 %collective-permute-start.25 = (bf16[80,1280]{1,0:T(8,128)(2,1)S(1)}, bf16[80,1280]{1,0:T(8,128)(2,1)S(1)}, u32[]{:S(2)}, u32[]{:S(2)}) collective-permute-start(bf16[80,1280]{1,0:T(8,128)(2,1)S(1)} %shard_map.74), channel_id=1, source_target_pairs={{0,32},{32,0},{1,33},{33,1},{2,34},{34,2},{3,35},{35,3},{4,36},{36... | collective-permute-start | bytes 614408 | tf_op jit(solution)/shard_map/ppermute | solution.py:48

commit v19 on v16

--- a/solution.py
+++ b/solution.py
@@ -534,9 +534,10 @@
         ((80, ((2, 256),)),),
     )
     next_1, next_4 = z_shift(next_1, 1), z_shift(next_4, 2)
-    (other,) = sums([mine, next_1], ((64, ((0, 64), (1, 64))), (TAIL, ((0, 128), (1, 128)))))
-    (mine,) = sums(
-        [mine, next_1, next_4], ((64, ((0, 0), (1, 0), (2, 0))), (TAIL, ((0, 128), (1, 128), (2, 64))))
+    mine, other = sums(
+        [mine, next_1, next_4],
+        ((64, ((0, 0), (1, 0), (2, 0))), (TAIL, ((0, 128), (1, 128), (2, 64)))),
+        ((64, ((0, 64), (1, 64))), (TAIL, ((0, 128), (1, 128)))),
     )
 
     cols_tail = (TAIL, ((1, 256), (2, 256), (3, 256), (4, 16)))

time: 114 us -> 114 us (level)
    ppermute x6, waiting for transfers between devices: 41.2 us -> 39 us  [z_shift(): return lax.ppermute(v, ('zl', 'core', 'zh'), pairs)]
  transfers between devices with their start and end apart: 26 -> 26, of which waited for: 10 -> 11; matrix products, arithmetic and copies ran while one was open for 0% -> 0% of each run, Pallas kernels for 7% -> 8%
where the time goes in v19:
time: 114 us; the launch traced here: 112 us
  waiting for transfers between devices  44.4 us (39%)
  starting transfers between devices  30.8 us (27%)
  Pallas kernels  19.5 us (17%)
  blocking collectives  14.3 us (13%)
  between operations  1.45 us (1%)
    ppermute x6, waiting for transfers between devices, z_shift(): return lax.ppermute(v, ('zl', 'core', 'zh'), pairs)  39 us
    ppermute x12, starting transfers between devices, plane_shift(): return lax.ppermute(v, ('core', 'zh', 'y', 'x'), pairs)  16.7 us
    all_to_all x1, blocking collectives, exchange(): return lax.all_to_all(v, AXES, 0, 0, axis_index_groups=groups)  14.3 us
    ppermute x6, starting transfers between devices, z_shift(): return lax.ppermute(v, ('zl', 'core', 'zh'), pairs)  12.1 us
    pallas_call x1, Pallas kernels, logits_call(): pl.pallas_call(logits_body, out_shape=(jax.ShapeDtypeStruct((BLOCK, BLOCK...  5.78 us
    ppermute x8, waiting for transfers between devices, core_swap(): return lax.ppermute(v, 'core', [(0, 1), (1, 0)])  4.62 us
    pallas_call x1, Pallas kernels, high_call(): pl.pallas_call(high_body, out_shape=(HALF_WEIGHTS, PART, jax.ShapeDtypeSt...  2.89 us
  transfers between devices with their start and end apart: 26, of which 11 were waited for; matrix products, arithmetic and copies ran while one was open for 0% of the time, Pallas kernels for 8%

profile of v19, /device:TPU:32, one launch (start us, length us, event | category | flops | bytes accessed | tf_op | source)
XLA Modules:
  0.0 111.5 jit_solution(9957229245359725471)
XLA Ops:
  0.6 0.1 collective-permute-start.3
  0.7 0.9 shard_map.59.refs_0_
  1.7 0.7 collective-permute-done.3.refs_1_
  2.3 1.9 %collective-permute-start.4 = (bf16[128,1280]{1,0:T(8,128)(2,1)S(1)}, bf16[128,1280]{1,0:T(8,128)(2,1)S(1)}, u32[]{:S(2)}, u32[]{:S(2)}) collective-permute-start(bf16[128,1280]{1,0:T(8,128)(2,1)S(1)} %shard_map.60.refs_4_), channel_id=1, source_target_pairs={{0,208},{64,0},{128,64},{192,128},{16,192},{80,16},{144,80},{208,1... | collective-permute-start | bytes 983048 | tf_op jit(solution)/shard_map/ppermute | solution.py:44
  4.3 5.5 %collective-permute-start.5 = (bf16[64,1280]{1,0:T(8,128)(2,1)}, bf16[64,1280]{1,0:T(8,128)(2,1)S(1)}, u32[]{:S(2)}, u32[]{:S(2)}) collective-permute-start(bf16[64,1280]{1,0:T(8,128)(2,1)} %refs_0_.3), channel_id=1, source_target_pairs={{0,16},{64,80},{128,144},{192,208},{16,0},{80,64},{144,128},{208,1... | collective-permute-start | bytes 491528 | tf_op jit(solution)/shard_map/ppermute | solution.py:44
  9.7 1.5 %collective-permute-start = (bf16[64,1280]{1,0:T(8,128)(2,1)}, bf16[64,1280]{1,0:T(8,128)(2,1)S(1)}, u32[]{:S(2)}, u32[]{:S(2)}) collective-permute-start(bf16[64,1280]{1,0:T(8,128)(2,1)} %refs_0_.2), channel_id=1, source_target_pairs={{0,1},{1,2},{2,3},{3,0},{4,5},{5,6},{6,7},{7,4},{8,9},{9,10},{10,1... | collective-permute-start | bytes 491528 | tf_op jit(solution)/shard_map/ppermute | solution.py:35
  11.2 1.7 %collective-permute-start.2 = (bf16[64,1280]{1,0:T(8,128)(2,1)}, bf16[64,1280]{1,0:T(8,128)(2,1)S(1)}, u32[]{:S(2)}, u32[]{:S(2)}) collective-permute-start(bf16[64,1280]{1,0:T(8,128)(2,1)} %refs_0_.2), channel_id=1, source_target_pairs={{0,3},{1,0},{2,1},{3,2},{4,7},{5,4},{6,5},{7,6},{8,11},{9,8},{10,9... | collective-permute-start | bytes 491528 | tf_op jit(solution)/shard_map/ppermute | solution.py:35
  13.0 1.8 %collective-permute-start.1 = (bf16[64,1280]{1,0:T(8,128)(2,1)}, bf16[64,1280]{1,0:T(8,128)(2,1)S(1)}, u32[]{:S(2)}, u32[]{:S(2)}) collective-permute-start(bf16[64,1280]{1,0:T(8,128)(2,1)} %refs_0_.2), channel_id=1, source_target_pairs={{0,2},{1,3},{2,0},{3,1},{4,6},{5,7},{6,4},{7,5},{8,10},{9,11},{10,... | collective-permute-start | bytes 491528 | tf_op jit(solution)/shard_map/ppermute | solution.py:35
  14.8 0.9 copy-done
  15.7 5.7 %collective-permute-done.5.refs_6_.refs_1_.refs_8_ = bf16[64,1280]{1,0:T(8,128)(2,1)S(1)} collective-permute-done((bf16[64,1280]{1,0:T(8,128)(2,1)}, bf16[64,1280]{1,0:T(8,128)(2,1)S(1)}, u32[]{:S(2)}, u32[]{:S(2)}) %collective-permute-start.5) | collective-permute-done | bytes 163872 | tf_op jit(solution)/shard_map/ppermute | solution.py:44
  21.5 0.0 collective-permute-done.refs_1_
  21.5 0.1 shard_map.61
  21.6 1.7 %collective-permute-start.9 = (bf16[256,1280]{1,0:T(8,128)(2,1)S(1)}, bf16[256,1280]{1,0:T(8,128)(2,1)S(1)}, u32[]{:S(2)}, u32[]{:S(2)}) collective-permute-start(bf16[256,1280]{1,0:T(8,128)(2,1)S(1)} %get-tuple-element.41.refs_4_), channel_id=1, source_target_pairs={{0,144},{64,208},{128,0},{192,64},{16,128},{80,192},{144,16},{208,... | collective-permute-start | bytes 1966088 | tf_op jit(solution)/shard_map/ppermute | solution.py:44
  23.3 3.2 %collective-permute-start.8 = (bf16[256,1280]{1,0:T(8,128)(2,1)S(1)}, bf16[256,1280]{1,0:T(8,128)(2,1)S(1)}, u32[]{:S(2)}, u32[]{:S(2)}) collective-permute-start(bf16[256,1280]{1,0:T(8,128)(2,1)S(1)} %get-tuple-element.40.refs_0_), channel_id=1, source_target_pairs={{0,8},{1,9},{2,10},{3,11},{4,12},{5,13},{6,14},{7,15},{8,0},{9,1},... | collective-permute-start | bytes 1966088 | tf_op jit(solution)/shard_map/ppermute | solution.py:35
  26.5 1.1 collective-permute-start.7
  27.5 1.0 collective-permute-start.6
  28.5 11.6 %collective-permute-done.9.refs_5_ = bf16[256,1280]{1,0:T(8,128)(2,1)S(1)} collective-permute-done((bf16[256,1280]{1,0:T(8,128)(2,1)S(1)}, bf16[256,1280]{1,0:T(8,128)(2,1)S(1)}, u32[]{:S(2)}, u32[]{:S(2)}) %collective-permute-start.9) | collective-permute-done | bytes 655392 | tf_op jit(solution)/shard_map/ppermute | solution.py:44
  40.2 0.0 collective-permute-start.10
  40.2 0.8 shard_map.62
  41.0 0.5 collective-permute-start.11
  42.1 0.1 stack.23.place
  42.2 1.1 collective-permute-done.11.refs_7_
  43.3 0.0 collective-permute-done.6.refs_1_
  43.3 0.0 collective-permute-done.10.refs_6_
  43.4 5.8 %shard_map.63 = (f32[1024,1024]{1,0:T(8,128)S(1)}, f32[16,128]{1,0:T(8,128)S(1)}, f32[16,128]{1,0:T(8,128)S(1)}, f32[24,128]{1,0:T(8,128)S(1)}, f32[8,128]{1,0:T...) custom-call(s32[5]{0:T(128)S(1)} %stack.23.place, f32[1]{0:T(128)S(6)} %copy.6.scale, ...), custom_call_target="tpu_custom_call" | custom-call | tf_op jit(solution)/shard_map/pallas_call | solution.py:204
  49.1 0.6 collective-permute-start.12
  49.8 0.8 collective-permute-done.12.got
  50.6 0.6 shard_map.64
  51.2 14.3 %all_to_all.5.got = f32[16,24,128]{2,1,0:T(8,128)S(1)} all-to-all(f32[16,24,128]{2,1,0:T(8,128)S(1)} %shard_map.64), channel_id=1, replica_groups={{0,1,2,3,4,5,6,7,8,9,10,11,12,13,14,15},{64,65,66,67,68,69,70,71,72,73,..., dimensions={0} | all-to-all | bytes 393216 | tf_op jit(solution)/shard_map/all_to_all | solution.py:63
  65.5 0.7 shard_map.65
  66.3 0.1 collective-permute-start.13
  66.4 1.2 %collective-permute-done.13.other = f32[24,128]{1,0:T(8,128)S(1)} collective-permute-done((f32[24,128]{1,0:T(8,128)S(1)}, f32[24,128]{1,0:T(8,128)S(1)}, u32[]{:S(2)}, u32[]{:S(2)}) %collective-permute-start.13) | collective-permute-done | bytes 12320 | tf_op jit(solution)/shard_map/ppermute | solution.py:48
  67.5 2.9 %shard_map.66 = (bf16[1024,512]{1,0:T(8,128)(2,1)S(1)}, bf16[256,1280]{1,0:T(8,128)(2,1)S(1)}, bf16[192,1280]{1,0:T(8,128)(2,1)S(1)}, bf16[64,1280]{1,0:T(8,128)...) custom-call(s32[5]{0:T(128)S(1)} %stack.23.place, f32[1]{0:T(128)S(6)} %copy.6.scale, ...), custom_call_target="tpu_custom_call" | custom-call | tf_op jit(solution)/shard_map/pallas_call | solution.py:348
  70.4 0.3 collective-permute-start.14
  70.7 0.3 collective-permute-start.15
  71.0 2.1 %shard_map.67 = (bf16[1024,512]{1,0:T(8,128)(2,1)S(1)}, bf16[256,1280]{1,0:T(8,128)(2,1)S(1)}) custom-call(s32[5]{0:T(128)S(1)} %stack.23.place, f32[1]{0:T(128)S(6)} %copy.6.scale, f32[1024,1024]{1,0:T(8,128)S(1)} %get-tuple-element.42.logits, f32[1024,128]{1,0:T(8,128)S(1)} %get-tuple-element.50.row_wide, f32[8,128]{1,0:T(8,128)S(1)} %get-tuple-element.51.col_lines, ...), custom_call_target="tpu_custom_call" | custom-call | tf_op jit(solution)/shard_map/pallas_call | solution.py:372
  73.1 0.2 collective-permute-done.15.refs_3_.refs_1_
  73.3 0.0 collective-permute-done.14.refs_1_
  73.3 0.2 shard_map.69.after
  73.5 1.5 %collective-permute-start.22 = (bf16[336,1280]{1,0:T(8,128)(2,1)S(1)}, bf16[336,1280]{1,0:T(8,128)(2,1)S(1)}, u32[]{:S(2)}, u32[]{:S(2)}) collective-permute-start(bf16[336,1280]{1,0:T(8,128)(2,1)S(1)} %shard_map.69.after), channel_id=1, source_target_pairs={{0,128},{64,192},{128,16},{192,80},{16,144},{80,208},{144,0},{208,... | collective-permute-start | bytes 2580488 | tf_op jit(solution)/shard_map/ppermute | solution.py:44
  75.0 2.2 %shard_map.70 = (bf16[272,1280]{1,0:T(8,128)(2,1)S(1)}, bf16[272,1280]{1,0:T(8,128)(2,1)S(1)}, bf16[272,1280]{1,0:T(8,128)(2,1)S(1)}) custom-call(f32[1]{0:T(128)S(6)} %copy.6.scale, bf16[336,1280]{1,0:T(8,128)(2,1)S(1)} %shard_map.69.after, bf16[32,1280]{1,0:T(8,128)(2,1)S(1)} %get-tuple-element.60.refs_4_.digits.refs_3_.refs_6_, ...), custom_call_target="tpu_custom_call" | custom-call | tf_op jit(solution)/shard_map/pallas_call | solution.py:417
  77.2 1.1 collective-permute-start.16
  78.3 1.7 %collective-permute-start.17 = (bf16[272,1280]{1,0:T(8,128)(2,1)S(1)}, bf16[272,1280]{1,0:T(8,128)(2,1)S(1)}, u32[]{:S(2)}, u32[]{:S(2)}) collective-permute-start(bf16[272,1280]{1,0:T(8,128)(2,1)S(1)} %get-tuple-element.62), channel_id=1, source_target_pairs={{0,12},{1,13},{2,14},{3,15},{4,0},{5,1},{6,2},{7,3},{8,4},{9,5},{1... | collective-permute-start | bytes 2088968 | tf_op jit(solution)/shard_map/ppermute | solution.py:35
  80.0 0.3 collective-permute-start.18
  80.3 1.6 %shard_map.68 = (bf16[256,1280]{1,0:T(8,128)(2,1)S(1)}, bf16[256,1280]{1,0:T(8,128)(2,1)S(1)}) custom-call(f32[1]{0:T(128)S(6)} %copy.6.scale, bf16[1024,512]{1,0:T(8,128)(2,1)S(1)} %get-tuple-element.52.low, bf16[1024,512]{1,0:T(8,128)(2,1)S(1)} %get-tuple-element.53.high, bf16[1024,1280]{1,0:T(8,128)(2,1)S(1)} %get-tuple-element.49.images, ...), custom_call_target="tpu_custom_call" | custom-call | tf_op jit(solution)/shard_map/pallas_call | solution.py:432
  81.9 15.7 %collective-permute-done.22.refs_2_ = bf16[336,1280]{1,0:T(8,128)(2,1)S(1)} collective-permute-done((bf16[336,1280]{1,0:T(8,128)(2,1)S(1)}, bf16[336,1280]{1,0:T(8,128)(2,1)S(1)}, u32[]{:S(2)}, u32[]{:S(2)}) %collective-permute-start.22) | collective-permute-done | bytes 860192 | tf_op jit(solution)/shard_map/ppermute | solution.py:44
  97.6 0.2 shard_map.72
  97.8 0.3 collective-permute-start.23
  98.1 1.2 %collective-permute-start.24 = (bf16[80,1280]{1,0:T(8,128)(2,1)S(1)}, bf16[80,1280]{1,0:T(8,128)(2,1)S(1)}, u32[]{:S(2)}, u32[]{:S(2)}) collective-permute-start(bf16[80,1280]{1,0:T(8,128)(2,1)S(1)} %get-tuple-element.71), channel_id=1, source_target_pairs={{0,128},{64,192},{128,16},{192,80},{16,144},{80,208},{144,0},{208,... | collective-permute-start | bytes 614408 | tf_op jit(solution)/shard_map/ppermute | solution.py:44
  99.3 0.0 collective-permute-done.16.refs_1_
  99.3 0.0 collective-permute-done.17.refs_2_
  99.3 0.0 collective-permute-done.18.refs_3_
  99.3 0.4 shard_map.71
  99.7 0.5 collective-permute-start.19
  100.3 2.8 %collective-permute-start.20 = (bf16[80,1280]{1,0:T(8,128)(2,1)S(1)}, bf16[80,1280]{1,0:T(8,128)(2,1)S(1)}, u32[]{:S(2)}, u32[]{:S(2)}) collective-permute-start(bf16[80,1280]{1,0:T(8,128)(2,1)S(1)} %get-tuple-element.66), channel_id=1, source_target_pairs={{0,3},{1,0},{2,1},{3,2},{4,7},{5,4},{6,5},{7,6},{8,11},{9,8},{10,9... | collective-permute-start | bytes 614408 | tf_op jit(solution)/shard_map/ppermute | solution.py:35
  103.1 6.0 %collective-permute-done.24.refs_2_ = bf16[80,1280]{1,0:T(8,128)(2,1)S(1)} collective-permute-done((bf16[80,1280]{1,0:T(8,128)(2,1)S(1)}, bf16[80,1280]{1,0:T(8,128)(2,1)S(1)}, u32[]{:S(2)}, u32[]{:S(2)}) %collective-permute-start.24) | collective-permute-done | bytes 204832 | tf_op jit(solution)/shard_map/ppermute | solution.py:44
  109.1 0.0 collective-permute-done.23.refs_1_
  109.1 0.1 shard_map.73
  109.2 0.1 collective-permute-start.25
  109.3 0.0 collective-permute-done.19.refs_1_
  109.3 0.0 collective-permute-done.20.refs_2_
  109.3 0.7 collective-permute-done.21.refs_3_
  110.0 0.7 collective-permute-done.25.refs_5_
  110.7 0.8 shard_map.74
  (9 shorter events, 0.1 us)
Async XLA Ops:
  0.6 1.7 %collective-permute-start.3 = (bf16[64,1280]{1,0:T(8,128)(2,1)}, bf16[64,1280]{1,0:T(8,128)(2,1)S(1)}, u32[]{:S(2)}, u32[]{:S(2)}) collective-permute-start(bf16[64,1280]{1,0:T(8,128)(2,1)} %refs_0_.3), channel_id=1, source_target_pairs={{0,32},{32,0},{1,33},{33,1},{2,34},{34,2},{3,35},{35,3},{4,36},{36... | collective-permute-start | bytes 491528 | tf_op jit(solution)/shard_map/ppermute | solution.py:48
  2.3 19.1 %collective-permute-start.4 = (bf16[128,1280]{1,0:T(8,128)(2,1)S(1)}, bf16[128,1280]{1,0:T(8,128)(2,1)S(1)}, u32[]{:S(2)}, u32[]{:S(2)}) collective-permute-start(bf16[128,1280]{1,0:T(8,128)(2,1)S(1)} %shard_map.60.refs_4_), channel_id=1, source_target_pairs={{0,208},{64,0},{128,64},{192,128},{16,192},{80,16},{144,80},{208,1... | collective-permute-start | bytes 983048 | tf_op jit(solution)/shard_map/ppermute | solution.py:44
  4.3 17.2 %collective-permute-start.5 = (bf16[64,1280]{1,0:T(8,128)(2,1)}, bf16[64,1280]{1,0:T(8,128)(2,1)S(1)}, u32[]{:S(2)}, u32[]{:S(2)}) collective-permute-start(bf16[64,1280]{1,0:T(8,128)(2,1)} %refs_0_.3), channel_id=1, source_target_pairs={{0,16},{64,80},{128,144},{192,208},{16,0},{80,64},{144,128},{208,1... | collective-permute-start | bytes 491528 | tf_op jit(solution)/shard_map/ppermute | solution.py:44
  9.7 11.7 %collective-permute-start = (bf16[64,1280]{1,0:T(8,128)(2,1)}, bf16[64,1280]{1,0:T(8,128)(2,1)S(1)}, u32[]{:S(2)}, u32[]{:S(2)}) collective-permute-start(bf16[64,1280]{1,0:T(8,128)(2,1)} %refs_0_.2), channel_id=1, source_target_pairs={{0,1},{1,2},{2,3},{3,0},{4,5},{5,6},{6,7},{7,4},{8,9},{9,10},{10,1... | collective-permute-start | bytes 491528 | tf_op jit(solution)/shard_map/ppermute | solution.py:35
  11.2 10.2 %collective-permute-start.2 = (bf16[64,1280]{1,0:T(8,128)(2,1)}, bf16[64,1280]{1,0:T(8,128)(2,1)S(1)}, u32[]{:S(2)}, u32[]{:S(2)}) collective-permute-start(bf16[64,1280]{1,0:T(8,128)(2,1)} %refs_0_.2), channel_id=1, source_target_pairs={{0,3},{1,0},{2,1},{3,2},{4,7},{5,4},{6,5},{7,6},{8,11},{9,8},{10,9... | collective-permute-start | bytes 491528 | tf_op jit(solution)/shard_map/ppermute | solution.py:35
  13.0 8.5 %collective-permute-start.1 = (bf16[64,1280]{1,0:T(8,128)(2,1)}, bf16[64,1280]{1,0:T(8,128)(2,1)S(1)}, u32[]{:S(2)}, u32[]{:S(2)}) collective-permute-start(bf16[64,1280]{1,0:T(8,128)(2,1)} %refs_0_.2), channel_id=1, source_target_pairs={{0,2},{1,3},{2,0},{3,1},{4,6},{5,7},{6,4},{7,5},{8,10},{9,11},{10,... | collective-permute-start | bytes 491528 | tf_op jit(solution)/shard_map/ppermute | solution.py:35
  14.8 0.9 copy-start
  21.6 18.6 %collective-permute-start.9 = (bf16[256,1280]{1,0:T(8,128)(2,1)S(1)}, bf16[256,1280]{1,0:T(8,128)(2,1)S(1)}, u32[]{:S(2)}, u32[]{:S(2)}) collective-permute-start(bf16[256,1280]{1,0:T(8,128)(2,1)S(1)} %get-tuple-element.41.refs_4_), channel_id=1, source_target_pairs={{0,144},{64,208},{128,0},{192,64},{16,128},{80,192},{144,16},{208,... | collective-permute-start | bytes 1966088 | tf_op jit(solution)/shard_map/ppermute | solution.py:44
  23.3 20.0 %collective-permute-start.8 = (bf16[256,1280]{1,0:T(8,128)(2,1)S(1)}, bf16[256,1280]{1,0:T(8,128)(2,1)S(1)}, u32[]{:S(2)}, u32[]{:S(2)}) collective-permute-start(bf16[256,1280]{1,0:T(8,128)(2,1)S(1)} %get-tuple-element.40.refs_0_), channel_id=1, source_target_pairs={{0,8},{1,9},{2,10},{3,11},{4,12},{5,13},{6,14},{7,15},{8,0},{9,1},... | collective-permute-start | bytes 1966088 | tf_op jit(solution)/shard_map/ppermute | solution.py:35
  26.5 16.8 %collective-permute-start.7 = (bf16[256,1280]{1,0:T(8,128)(2,1)S(1)}, bf16[256,1280]{1,0:T(8,128)(2,1)S(1)}, u32[]{:S(2)}, u32[]{:S(2)}) collective-permute-start(bf16[256,1280]{1,0:T(8,128)(2,1)S(1)} %get-tuple-element.40.refs_0_), channel_id=1, source_target_pairs={{0,12},{1,13},{2,14},{3,15},{4,0},{5,1},{6,2},{7,3},{8,4},{9,5},{1... | collective-permute-start | bytes 1966088 | tf_op jit(solution)/shard_map/ppermute | solution.py:35
  27.5 15.8 %collective-permute-start.6 = (bf16[256,1280]{1,0:T(8,128)(2,1)S(1)}, bf16[256,1280]{1,0:T(8,128)(2,1)}, u32[]{:S(2)}, u32[]{:S(2)}) collective-permute-start(bf16[256,1280]{1,0:T(8,128)(2,1)S(1)} %get-tuple-element.40.refs_0_), channel_id=1, source_target_pairs={{0,4},{1,5},{2,6},{3,7},{4,8},{5,9},{6,10},{7,11},{8,12},{9,13},{1... | collective-permute-start | bytes 1966088 | tf_op jit(solution)/shard_map/ppermute | solution.py:35
  40.2 3.2 %collective-permute-start.10 = (bf16[256,1280]{1,0:T(8,128)(2,1)S(1)}, bf16[256,1280]{1,0:T(8,128)(2,1)}, u32[]{:S(2)}, u32[]{:S(2)}) collective-permute-start(bf16[256,1280]{1,0:T(8,128)(2,1)S(1)} %collective-permute-done.9.refs_5_), channel_id=1, source_target_pairs={{0,32},{32,0},{1,33},{33,1},{2,34},{34,2},{3,35},{35,3},{4,36},{36... | collective-permute-start | bytes 1966088 | tf_op jit(solution)/shard_map/ppermute | solution.py:48
  41.0 2.3 %collective-permute-start.11 = (bf16[192,1280]{1,0:T(8,128)(2,1)}, bf16[192,1280]{1,0:T(8,128)(2,1)}, u32[]{:S(2)}, u32[]{:S(2)}) collective-permute-start(bf16[192,1280]{1,0:T(8,128)(2,1)} %shard_map.62), channel_id=1, source_target_pairs={{0,32},{32,0},{1,33},{33,1},{2,34},{34,2},{3,35},{35,3},{4,36},{36... | collective-permute-start | bytes 1474568 | tf_op jit(solution)/shard_map/ppermute | solution.py:48
  49.1 1.4 %collective-permute-start.12 = (f32[24,128]{1,0:T(8,128)S(1)}, f32[24,128]{1,0:T(8,128)S(1)}, u32[]{:S(2)}, u32[]{:S(2)}) collective-permute-start(f32[24,128]{1,0:T(8,128)S(1)} %get-tuple-element.46), channel_id=1, source_target_pairs={{0,32},{32,0},{1,33},{33,1},{2,34},{34,2},{3,35},{35,3},{4,36},{36... | collective-permute-start | bytes 36872 | tf_op jit(solution)/shard_map/ppermute | solution.py:48
  66.3 1.3 %collective-permute-start.13 = (f32[24,128]{1,0:T(8,128)S(1)}, f32[24,128]{1,0:T(8,128)S(1)}, u32[]{:S(2)}, u32[]{:S(2)}) collective-permute-start(f32[24,128]{1,0:T(8,128)S(1)} %get-tuple-element.48), channel_id=1, source_target_pairs={{0,32},{32,0},{1,33},{33,1},{2,34},{34,2},{3,35},{35,3},{4,36},{36... | collective-permute-start | bytes 36872 | tf_op jit(solution)/shard_map/ppermute | solution.py:48
  70.4 2.9 %collective-permute-start.14 = (bf16[256,1280]{1,0:T(8,128)(2,1)S(1)}, bf16[256,1280]{1,0:T(8,128)(2,1)S(1)}, u32[]{:S(2)}, u32[]{:S(2)}) collective-permute-start(bf16[256,1280]{1,0:T(8,128)(2,1)S(1)} %get-tuple-element.57), channel_id=1, source_target_pairs={{0,32},{32,0},{1,33},{33,1},{2,34},{34,2},{3,35},{35,3},{4,36},{36... | collective-permute-start | bytes 1966088 | tf_op jit(solution)/shard_map/ppermute | solution.py:48
  70.7 2.6 %collective-permute-start.15 = (bf16[192,1280]{1,0:T(8,128)(2,1)S(1)}, bf16[192,1280]{1,0:T(8,128)(2,1)S(1)}, u32[]{:S(2)}, u32[]{:S(2)}) collective-permute-start(bf16[192,1280]{1,0:T(8,128)(2,1)S(1)} %get-tuple-element.59), channel_id=1, source_target_pairs={{0,32},{32,0},{1,33},{33,1},{2,34},{34,2},{3,35},{35,3},{4,36},{36... | collective-permute-start | bytes 1474568 | tf_op jit(solution)/shard_map/ppermute | solution.py:48
  73.5 24.1 %collective-permute-start.22 = (bf16[336,1280]{1,0:T(8,128)(2,1)S(1)}, bf16[336,1280]{1,0:T(8,128)(2,1)S(1)}, u32[]{:S(2)}, u32[]{:S(2)}) collective-permute-start(bf16[336,1280]{1,0:T(8,128)(2,1)S(1)} %shard_map.69.after), channel_id=1, source_target_pairs={{0,128},{64,192},{128,16},{192,80},{16,144},{80,208},{144,0},{208,... | collective-permute-start | bytes 2580488 | tf_op jit(solution)/shard_map/ppermute | solution.py:44
  77.2 22.1 %collective-permute-start.16 = (bf16[272,1280]{1,0:T(8,128)(2,1)S(1)}, bf16[272,1280]{1,0:T(8,128)(2,1)S(1)}, u32[]{:S(2)}, u32[]{:S(2)}) collective-permute-start(bf16[272,1280]{1,0:T(8,128)(2,1)S(1)} %get-tuple-element.61), channel_id=1, source_target_pairs={{0,8},{1,9},{2,10},{3,11},{4,12},{5,13},{6,14},{7,15},{8,0},{9,1},... | collective-permute-start | bytes 2088968 | tf_op jit(solution)/shard_map/ppermute | solution.py:35
  78.3 21.0 %collective-permute-start.17 = (bf16[272,1280]{1,0:T(8,128)(2,1)S(1)}, bf16[272,1280]{1,0:T(8,128)(2,1)S(1)}, u32[]{:S(2)}, u32[]{:S(2)}) collective-permute-start(bf16[272,1280]{1,0:T(8,128)(2,1)S(1)} %get-tuple-element.62), channel_id=1, source_target_pairs={{0,12},{1,13},{2,14},{3,15},{4,0},{5,1},{6,2},{7,3},{8,4},{9,5},{1... | collective-permute-start | bytes 2088968 | tf_op jit(solution)/shard_map/ppermute | solution.py:35
  80.0 19.3 %collective-permute-start.18 = (bf16[272,1280]{1,0:T(8,128)(2,1)S(1)}, bf16[272,1280]{1,0:T(8,128)(2,1)S(1)}, u32[]{:S(2)}, u32[]{:S(2)}) collective-permute-start(bf16[272,1280]{1,0:T(8,128)(2,1)S(1)} %get-tuple-element.63), channel_id=1, source_target_pairs={{0,4},{1,5},{2,6},{3,7},{4,8},{5,9},{6,10},{7,11},{8,12},{9,13},{1... | collective-permute-start | bytes 2088968 | tf_op jit(solution)/shard_map/ppermute | solution.py:35
  97.8 11.2 %collective-permute-start.23 = (bf16[144,1280]{1,0:T(8,128)(2,1)S(1)}, bf16[144,1280]{1,0:T(8,128)(2,1)S(1)}, u32[]{:S(2)}, u32[]{:S(2)}) collective-permute-start(bf16[144,1280]{1,0:T(8,128)(2,1)S(1)} %get-tuple-element.70), channel_id=1, source_target_pairs={{0,64},{64,128},{128,192},{192,16},{16,80},{80,144},{144,208},{208... | collective-permute-start | bytes 1105928 | tf_op jit(solution)/shard_map/ppermute | solution.py:44
  98.1 10.9 %collective-permute-start.24 = (bf16[80,1280]{1,0:T(8,128)(2,1)S(1)}, bf16[80,1280]{1,0:T(8,128)(2,1)S(1)}, u32[]{:S(2)}, u32[]{:S(2)}) collective-permute-start(bf16[80,1280]{1,0:T(8,128)(2,1)S(1)} %get-tuple-element.71), channel_id=1, source_target_pairs={{0,128},{64,192},{128,16},{192,80},{16,144},{80,208},{144,0},{208,... | collective-permute-start | bytes 614408 | tf_op jit(solution)/shard_map/ppermute | solution.py:44
  99.7 9.5 %collective-permute-start.19 = (bf16[80,1280]{1,0:T(8,128)(2,1)S(1)}, bf16[80,1280]{1,0:T(8,128)(2,1)S(1)}, u32[]{:S(2)}, u32[]{:S(2)}) collective-permute-start(bf16[80,1280]{1,0:T(8,128)(2,1)S(1)} %get-tuple-element.65), channel_id=1, source_target_pairs={{0,2},{1,3},{2,0},{3,1},{4,6},{5,7},{6,4},{7,5},{8,10},{9,11},{10,... | collective-permute-start | bytes 614408 | tf_op jit(solution)/shard_map/ppermute | solution.py:35
  100.3 9.0 %collective-permute-start.20 = (bf16[80,1280]{1,0:T(8,128)(2,1)S(1)}, bf16[80,1280]{1,0:T(8,128)(2,1)S(1)}, u32[]{:S(2)}, u32[]{:S(2)}) collective-permute-start(bf16[80,1280]{1,0:T(8,128)(2,1)S(1)} %get-tuple-element.66), channel_id=1, source_target_pairs={{0,3},{1,0},{2,1},{3,2},{4,7},{5,4},{6,5},{7,6},{8,11},{9,8},{10,9... | collective-permute-start | bytes 614408 | tf_op jit(solution)/shard_map/ppermute | solution.py:35
  103.1 7.0 %collective-permute-start.21 = (bf16[80,1280]{1,0:T(8,128)(2,1)S(1)}, bf16[80,1280]{1,0:T(8,128)(2,1)S(1)}, u32[]{:S(2)}, u32[]{:S(2)}) collective-permute-start(bf16[80,1280]{1,0:T(8,128)(2,1)S(1)} %get-tuple-element.67), channel_id=1, source_target_pairs={{0,1},{1,2},{2,3},{3,0},{4,5},{5,6},{6,7},{7,4},{8,9},{9,10},{10,1... | collective-permute-start | bytes 614408 | tf_op jit(solution)/shard_map/ppermute | solution.py:35
  109.2 1.5 %collective-permute-start.25 = (bf16[80,1280]{1,0:T(8,128)(2,1)S(1)}, bf16[80,1280]{1,0:T(8,128)(2,1)S(1)}, u32[]{:S(2)}, u32[]{:S(2)}) collective-permute-start(bf16[80,1280]{1,0:T(8,128)(2,1)S(1)} %get-tuple-element.73), channel_id=1, source_target_pairs={{0,32},{32,0},{1,33},{33,1},{2,34},{34,2},{3,35},{35,3},{4,36},{36... | collective-permute-start | bytes 614408 | tf_op jit(solution)/shard_map/ppermute | solution.py:48
